TPU v7x, 32 devices: a whole 2x2x4 slice. The times are simulated.
32 devices in a mesh: sp: 8 (over z, x), win: 4 (over y, core).
Axes of the slice: x: 2, y: 2, z: 4, core: 2. Of those that a mesh axis runs over, the one named last changes fastest.
Arguments:
- features: bfloat16 [8192, 4096], P(('sp', 'win')), may hold values from -12 to 12
- proj_weight: bfloat16 [4096, 1024], replicated, may hold values from -0.09375 to 0.09375
- partner_offsets: int32 [8, 4], P('sp'), may hold values from 1 to 6, as said below
- ortholog_index: int32 [8192, 4], P(('sp', 'win')), may hold values from 0 to 255
Outputs:
- window_loss: float32 [8192], P(('sp', 'win'))
- weight_grad: float32 [4096, 1024], P(('sp', 'win'))
Inputs may be any that keep to these rules, and one draw needn't show every extreme that they name: `partner_offsets`: each row holds 4 different offsets; every offset from 1 to 6 occurs in some row.
All inputs are finite; a program needn't handle non-finite values.
Results may differ from a plain program's by a relative error of at most 0.00585.
The roundings to bfloat16 on the way count: a program that leaves them out, or rounds other values in their place, can miss the bound.
Values may be sent and summed in bfloat16 or wider, within the bound.
No kernel may reach another device: no remote copies, remote signals or barrier semaphores. Data moves between devices by JAX's collectives and lax.ppermute only.
A program may use at most 128 MiB of HBM per device.

v0:
```python
import jax
import jax.numpy as jnp
from jax import lax
from jax.sharding import PartitionSpec as P

PARTNERS = 4
MAXOFF = 6
ITERS = 3


logit_scale = 0.125


def from_behind(shard, axis, by):
    devices = lax.axis_size(axis)
    return lax.ppermute(shard, axis, [(i, (i + by) % devices) for i in range(devices)])


def newton_columns(full, scaled, identity_columns, first_column, share):
    highest = lax.Precision.HIGHEST
    columns = lax.dynamic_slice_in_dim(full, first_column, share, 1)
    moved = jnp.dot(scaled, columns, precision=highest, preferred_element_type=jnp.float32)
    quad = jnp.dot(full, moved, precision=highest, preferred_element_type=jnp.float32)
    return jnp.dot(
        full,
        0.5 * (3.0 * identity_columns - quad),
        precision=highest,
        preferred_element_type=jnp.float32,
    )


def shards(features, proj_weight, partner_offsets, ortholog_index):
    highest = lax.Precision.HIGHEST
    row_count = features.shape[0]
    embed_dim = proj_weight.shape[1]
    total_rows = row_count * lax.axis_size("sp") * lax.axis_size("win")
    projected = jnp.dot(features, proj_weight, preferred_element_type=jnp.float32).astype(
        jnp.bfloat16
    )
    projected_wide = projected.astype(jnp.float32)
    mean_row = lax.psum(jnp.sum(projected_wide, axis=0), ("sp", "win")) / total_rows
    centered_wide = projected_wide - mean_row
    covariance = (
        lax.psum(
            jnp.dot(
                centered_wide.T,
                centered_wide,
                precision=highest,
                preferred_element_type=jnp.float32,
            ),
            ("sp", "win"),
        )
        / total_rows
    )
    frobenius = jnp.sqrt(jnp.sum(covariance * covariance))
    scaled = covariance / frobenius
    identity = jnp.eye(embed_dim, dtype=jnp.float32)
    share = embed_dim // lax.axis_size("win")
    first_column = lax.axis_index("win") * share
    identity_columns = lax.dynamic_slice_in_dim(identity, first_column, share, 1)
    full = 0.5 * (3.0 * identity - scaled)
    columns = full
    for number in range(ITERS - 1):
        columns = newton_columns(full, scaled, identity_columns, first_column, share)
        if number < ITERS - 2:
            full = lax.all_gather(columns, "win", axis=1, tiled=True)
    whitener = lax.all_gather(
        (columns / jnp.sqrt(frobenius)).astype(jnp.bfloat16), "win", axis=1, tiled=True
    )
    centered = centered_wide.astype(jnp.bfloat16)
    white = jnp.dot(centered, whitener, preferred_element_type=jnp.float32).astype(jnp.bfloat16)
    blocks = []
    for number in range(MAXOFF):
        blocks.append(from_behind(white, "sp", -(number + 1)))
    stacked = jnp.stack(blocks)
    scores = (
        jnp.einsum("ie,dje->dij", white, stacked, preferred_element_type=jnp.float32) * logit_scale
    )
    choose = (
        partner_offsets[0][:, None] == jnp.arange(1, MAXOFF + 1, dtype=jnp.int32)[None, :]
    ).astype(jnp.float32)
    logits = jnp.sum(choose[:, :, None, None] * scores[None], axis=1)
    peak_value = jnp.max(logits, axis=-1, keepdims=True)
    log_total = peak_value + jnp.log(jnp.sum(jnp.exp(logits - peak_value), axis=-1, keepdims=True))
    hit_table = (
        jnp.arange(row_count, dtype=jnp.int32)[None, None, :] == ortholog_index.T[:, :, None]
    ).astype(jnp.float32)
    picked = jnp.sum(hit_table * logits, axis=-1)
    window_loss = jnp.sum(log_total[..., 0] - picked, axis=0) / PARTNERS
    probabilities = jnp.exp(logits - log_total)
    weights = ((probabilities - hit_table) / PARTNERS).astype(jnp.bfloat16)
    per_offset = jnp.sum(
        choose[:, :, None, None] * weights.astype(jnp.float32)[:, None], axis=0
    ).astype(jnp.bfloat16)
    grad_white = (
        jnp.einsum("dij,dje->ie", per_offset, stacked, preferred_element_type=jnp.float32)
        * logit_scale
    ).astype(jnp.bfloat16)
    grad_projected = jnp.dot(grad_white, whitener.T, preferred_element_type=jnp.float32).astype(
        jnp.bfloat16
    )
    local_term = lax.dot_general(
        features, grad_projected, (((0,), (0,)), ((), ())), preferred_element_type=jnp.float32
    )
    weight_grad = lax.psum_scatter(local_term, ("sp", "win"), scatter_dimension=0, tiled=True)
    return (window_loss, weight_grad)


def solution(mesh):
    return jax.shard_map(
        shards,
        mesh=mesh,
        in_specs=(P(("sp", "win"), None), P(), P("sp", None), P(("sp", "win"), None)),
        out_specs=(P(("sp", "win")), P(("sp", "win"), None)),
        check_vma=False,
    )
```

profile of v0, /device:TPU:0, one launch (start us, length us, event | category | flops | bytes accessed | tf_op | source)
XLA Modules:
  0.0 603.2 jit_solution(14104705535646263652)
XLA Ops:
  7.2 0.0 copy-start
  7.2 0.0 all-reduce.2.cloned.1.call-start
  7.2 1.5 copy-done
  8.8 5.7 convert_reduce_fusion
  14.5 0.0 copy-start.3
  14.5 42.0 %psum.14 = f32[1024]{0:T(1024)S(1)} all-reduce(f32[1024]{0:T(1024)S(1)} %get-tuple-element.10), channel_id=1, replica_groups=mesh['sp'=8,'win'=4] {'sp','win'}, use_global_device_ids=true, to_apply=%region_1.0 | all-reduce | flops 1024 | bytes 8192 | tf_op jit(solution)/shard_map/psum | solution.py:41
  56.5 5.2 fusion.5
  61.7 0.0 all-reduce.2.cloned.1.call-update
  61.7 0.0 copy-done.3
  61.7 0.2 all-gather.3.cloned.1.call-start
  62.0 0.3 iota_compare_fusion
  62.3 141.1 %all-reduce.2.cloned.1.call-done = f32[1024,1024]{1,0:T(8,128)} async-done(((f32[1024,1024]{1,0:T(8,128)}), f32[1024,1024]{1,0:T(8,128)}) %all-reduce.2.cloned.1.call-update) | async-done | bytes 4194320 | tf_op jit(solution)/shard_map/psum | solution.py:44
  203.4 3.9 multiply_reduce_fusion.2
  207.9 0.0 copy-start.1
  207.9 3.0 subtract_multiply_fusion
  210.9 0.4 copy-done.1
  211.4 3.4 fusion.9
  214.8 3.5 fusion.2
  218.3 4.7 fusion.19
  223.0 0.0 all-gather.3.cloned.1.call-update
  223.0 0.0 all-gather.5.cloned.1.call-start
  223.1 33.4 %all-gather.3.cloned.1.call-done = f32[1024,1024]{1,0:T(8,128)} async-done(((f32[1024,256]{1,0:T(8,128)}), f32[1024,1024]{1,0:T(8,128)}) %all-gather.3.cloned.1.call-update) | async-done | bytes 4194320 | tf_op jit(solution)/shard_map/all_gather | solution.py:66
  256.6 5.8 fusion.7
  262.4 0.0 copy-done.2
  262.4 3.5 fusion.1
  265.8 0.0 copy-start.4
  265.8 0.0 copy-start.8
  265.9 4.2 fusion.4
  270.1 0.0 all-gather.5.cloned.1.call-update
  270.1 0.0 reduce-scatter.2.cloned.1.call-start
  270.1 22.9 %all-gather.5.cloned.1.call-done = bf16[1024,1024]{1,0:T(8,128)(2,1)} async-done(((bf16[1024,256]{1,0:T(8,128)(2,1)}), bf16[1024,1024]{1,0:T(8,128)(2,1)}) %all-gather.5.cloned.1.call-update) | async-done | bytes 2097168 | tf_op jit(solution)/shard_map/all_gather | solution.py:67
  293.1 0.0 copy-done.4
  293.1 2.3 convolution_convert_fusion.2
  295.4 4.3 collective-permute-start
  299.7 0.5 collective-permute-start.1
  300.2 0.0 collective-permute-start.2
  300.2 0.0 copy-done.8
  300.2 0.1 compare_convert_fusion
  300.3 1.5 collective-permute-start.5
  301.8 2.9 collective-permute-start.4
  304.7 7.3 %collective-permute-done = bf16[256,1024]{1,0:T(8,128)(2,1)S(1)} collective-permute-done((bf16[256,1024]{1,0:T(8,128)(2,1)S(1)}, bf16[256,1024]{1,0:T(8,128)(2,1)S(1)}, u32[]{:S(2)}, u32[]{:S(2)}) %collective-permute-start) | collective-permute-done | bytes 524320 | tf_op jit(solution)/shard_map/ppermute | solution.py:16
  312.0 0.0 collective-permute-start.3
  312.1 11.2 %collective-permute-done.1 = bf16[256,1024]{1,0:T(8,128)(2,1)S(1)} collective-permute-done((bf16[256,1024]{1,0:T(8,128)(2,1)S(1)}, bf16[256,1024]{1,0:T(8,128)(2,1)S(1)}, u32[]{:S(2)}, u32[]{:S(2)}) %collective-permute-start.1) | collective-permute-done | bytes 524320 | tf_op jit(solution)/shard_map/ppermute | solution.py:16
  323.3 11.2 %collective-permute-done.2 = bf16[256,1024]{1,0:T(8,128)(2,1)S(1)} collective-permute-done((bf16[256,1024]{1,0:T(8,128)(2,1)S(1)}, bf16[256,1024]{1,0:T(8,128)(2,1)S(1)}, u32[]{:S(2)}, u32[]{:S(2)}) %collective-permute-start.2) | collective-permute-done | bytes 524320 | tf_op jit(solution)/shard_map/ppermute | solution.py:16
  334.5 55.5 %collective-permute-done.3 = bf16[256,1024]{1,0:T(8,128)(2,1)S(1)} collective-permute-done((bf16[256,1024]{1,0:T(8,128)(2,1)S(1)}, bf16[256,1024]{1,0:T(8,128)(2,1)S(1)}, u32[]{:S(2)}, u32[]{:S(2)}) %collective-permute-start.3) | collective-permute-done | bytes 524320 | tf_op jit(solution)/shard_map/ppermute | solution.py:16
  390.0 0.0 collective-permute-done.4
  390.1 0.0 collective-permute-done.5
  390.2 0.0 copy-start.5
  390.2 1.7 copy-done.5
  391.8 2.2 multiply_bitcast_fusion
  394.0 3.1 copy.8
  397.1 2.0 multiply_reduce_fusion.1
  399.1 0.2 reduce_max.9
  399.3 0.0 copy-start.6
  399.3 0.7 select_reduce_fusion
  400.0 0.3 fusion.12
  400.4 0.5 multiply_reduce_fusion
  400.9 0.3 copy-done.6
  401.2 1.0 fusion.3
  402.2 9.2 %convolution_bitcast_fusion = f32[4096,1024]{0,1:T(8,128)} fusion(bf16[256,4096]{1,0:T(8,128)(2,1)S(1)} %copy-done, bf16[256,1024]{1,0:T(8,128)(2,1)S(1)} %fusion.3, bf16[1024,1024]{1,0:T(8,128)(2,1)} %all-gather.5.cloned.1.call-done), kind=kOutput, calls=%fused_computation | convolution fusion | flops 2684616704 | bytes 21495808 | tf_op jit(solution)/shard_map/dot_general | solution.py:102
  411.4 0.0 reduce-scatter.2.cloned.1.call-update
  411.4 0.6 broadcast_multiply_fusion.1
  412.0 182.6 %reduce-scatter.2.cloned.1.call-done = f32[128,1024]{0,1:T(8,128)} async-done(((f32[4096,1024]{0,1:T(8,128)}), f32[128,1024]{0,1:T(8,128)}) %reduce-scatter.2.cloned.1.call-update) | async-done | bytes 524304 | tf_op jit(solution)/shard_map/reduce_scatter | solution.py:105
  594.6 2.0 copy.9
  (12 shorter events, 0.3 us)
Async XLA Ops:
  7.2 1.6 copy-start
  7.2 196.2 %all-reduce.2.cloned.1.call-start = ((), (), s32[]{:S(2)}) async-start(), calls=%async_computation.1 | async-start | bytes 8388608 | tf_op jit(solution)/shard_map/psum | solution.py:44
  14.5 47.2 %copy-start.3 = (bf16[256,1024]{1,0:T(8,128)(2,1)}, bf16[256,1024]{1,0:T(8,128)(2,1)S(1)}, u32[]{:S(2)}) copy-start(bf16[256,1024]{1,0:T(8,128)(2,1)S(1)} %get-tuple-element.11) | copy-start | bytes 1572868
  61.7 194.8 %all-gather.3.cloned.1.call-start = ((), (), s32[]{:S(2)}) async-start(), calls=%async_computation.2 | async-start | bytes 5242880 | tf_op jit(solution)/shard_map/all_gather | solution.py:66
  207.9 3.5 copy-start.1
  223.0 70.0 %all-gather.5.cloned.1.call-start = ((), (), s32[]{:S(2)}) async-start(), calls=%async_computation.3 | async-start | bytes 2621440 | tf_op jit(solution)/shard_map/all_gather | solution.py:67
  256.6 5.8 copy-start.2
  265.8 27.3 %copy-start.4 = (bf16[256,1024]{1,0:T(8,128)(2,1)S(1)}, bf16[256,1024]{1,0:T(8,128)(2,1)}, u32[]{:S(2)}) copy-start(bf16[256,1024]{1,0:T(8,128)(2,1)} %copy-done.3) | copy-start | bytes 1572868
  265.8 34.4 %copy-start.8 = (s32[1,4]{1,0:T(1,128)S(1)}, s32[1,4]{1,0:T(1,128)}, u32[]{:S(2)}) copy-start(s32[1,4]{1,0:T(1,128)} %param.6) | copy-start | bytes 52
  270.1 324.5 %reduce-scatter.2.cloned.1.call-start = ((), (), s32[]{:S(2)}) async-start(), calls=%async_computation.4 | async-start | bytes 17301504 | tf_op jit(solution)/shard_map/reduce_scatter | solution.py:105
  295.4 16.6 %collective-permute-start = (bf16[256,1024]{1,0:T(8,128)(2,1)S(1)}, bf16[256,1024]{1,0:T(8,128)(2,1)S(1)}, u32[]{:S(2)}, u32[]{:S(2)}) collective-permute-start(bf16[256,1024]{1,0:T(8,128)(2,1)S(1)} %convolution_convert_fusion.2), channel_id=1, source_target_pairs={{0,28},{4,0},{8,4},{12,8},{16,12},{20,16},{24,20},{28,24},{1,29},{... | collective-permute-start | bytes 1572872 | tf_op jit(solution)/shard_map/ppermute | solution.py:16
  299.7 23.6 %collective-permute-start.1 = (bf16[256,1024]{1,0:T(8,128)(2,1)S(1)}, bf16[256,1024]{1,0:T(8,128)(2,1)S(1)}, u32[]{:S(2)}, u32[]{:S(2)}) collective-permute-start(bf16[256,1024]{1,0:T(8,128)(2,1)S(1)} %convolution_convert_fusion.2), channel_id=1, source_target_pairs={{0,24},{4,28},{8,0},{12,4},{16,8},{20,12},{24,16},{28,20},{1,25},{... | collective-permute-start | bytes 1572872 | tf_op jit(solution)/shard_map/ppermute | solution.py:16
  300.2 34.3 %collective-permute-start.2 = (bf16[256,1024]{1,0:T(8,128)(2,1)S(1)}, bf16[256,1024]{1,0:T(8,128)(2,1)S(1)}, u32[]{:S(2)}, u32[]{:S(2)}) collective-permute-start(bf16[256,1024]{1,0:T(8,128)(2,1)S(1)} %convolution_convert_fusion.2), channel_id=1, source_target_pairs={{0,20},{4,24},{8,28},{12,0},{16,4},{20,8},{24,12},{28,16},{1,21},{... | collective-permute-start | bytes 1572872 | tf_op jit(solution)/shard_map/ppermute | solution.py:16
  300.3 89.8 %collective-permute-start.5 = (bf16[256,1024]{1,0:T(8,128)(2,1)S(1)}, bf16[256,1024]{1,0:T(8,128)(2,1)S(1)}, u32[]{:S(2)}, u32[]{:S(2)}) collective-permute-start(bf16[256,1024]{1,0:T(8,128)(2,1)S(1)} %convolution_convert_fusion.2), channel_id=1, source_target_pairs={{0,8},{4,12},{8,16},{12,20},{16,24},{20,28},{24,0},{28,4},{1,9},{5... | collective-permute-start | bytes 1572872 | tf_op jit(solution)/shard_map/ppermute | solution.py:16
  301.8 88.3 %collective-permute-start.4 = (bf16[256,1024]{1,0:T(8,128)(2,1)S(1)}, bf16[256,1024]{1,0:T(8,128)(2,1)S(1)}, u32[]{:S(2)}, u32[]{:S(2)}) collective-permute-start(bf16[256,1024]{1,0:T(8,128)(2,1)S(1)} %convolution_convert_fusion.2), channel_id=1, source_target_pairs={{0,12},{4,16},{8,20},{12,24},{16,28},{20,0},{24,4},{28,8},{1,13},{... | collective-permute-start | bytes 1572872 | tf_op jit(solution)/shard_map/ppermute | solution.py:16
  312.0 78.0 %collective-permute-start.3 = (bf16[256,1024]{1,0:T(8,128)(2,1)S(1)}, bf16[256,1024]{1,0:T(8,128)(2,1)S(1)}, u32[]{:S(2)}, u32[]{:S(2)}) collective-permute-start(bf16[256,1024]{1,0:T(8,128)(2,1)S(1)} %convolution_convert_fusion.2), channel_id=1, source_target_pairs={{0,16},{4,20},{8,24},{12,28},{16,0},{20,4},{24,8},{28,12},{1,17},{... | collective-permute-start | bytes 1572872 | tf_op jit(solution)/shard_map/ppermute | solution.py:16
  390.2 1.7 copy-start.5
  394.0 5.3 copy-start.7
  399.3 1.9 copy-start.6
Sparse Core Ops, SparseCore 0:
  61.8 141.4 all-reduce.1
  223.2 33.3 all-gather.2
  270.2 22.8 all-gather.4
  411.5 183.0 reduce-scatter.1
where the time goes:
time: 605 us; the launch traced here: 603 us
  waiting for transfers between devices  465 us (77%)
  matrix products  50.6 us (8%)
  blocking collectives  42 us (7%)
  between operations  14.7 us (2%)
  other arithmetic  11.6 us (2%)
  starting transfers between devices  9.58 us (2%)
  local copies, waits for them, and re-layouts  9.25 us (2%)
    reduce_scatter x1, waiting for transfers between devices, shards(): lax.psum_scatter(local_term, ('sp', 'win'), scatter_dimension=0, tiled=True)  183 us
    psum x1, waiting for transfers between devices, shards(): lax.psum(jnp.dot(centered_wide.T, centered_wide, precision=highest, prefe...  141 us
    ppermute x6, waiting for transfers between devices, from_behind(): lax.ppermute(shard, axis, [(i, (i + by) % devices) for i in range(devices)])  85.2 us
    psum x1, blocking collectives, shards(): lax.psum(jnp.sum(projected_wide, axis=0), ('sp', 'win')) / total_rows  42 us
    all_gather x1, waiting for transfers between devices, shards(): full = lax.all_gather(columns, 'win', axis=1, tiled=True)  33.4 us
    all_gather x1, waiting for transfers between devices, shards(): lax.all_gather((columns / jnp.sqrt(frobenius)).astype(jnp.bfloat16), 'win...  22.9 us
  transfers between devices with their start and end apart: 10, of which 8 were waited for; matrix products, arithmetic and copies ran while one was open for 0% of the time, Pallas kernels for 0%

commit v1 on v0

v1 whole, which is shorter than its diff:
```python
import jax
import jax.numpy as jnp
from jax import lax
from jax.experimental import pallas as pl
from jax.experimental.pallas import tpu as pltpu
from jax.sharding import PartitionSpec as P

PARTNERS = 4
LOGIT_SCALE = 0.125
AXES = ("sp", "win")
LANES = 128
F32 = jnp.float32
BF16 = jnp.bfloat16
VMEM_LIMIT = 60 * 2**20
HIGHEST = lax.Precision.HIGHEST


def dot(a, b, contract=(1, 0), precision=None):
    return lax.dot_general(
        a,
        b,
        (((contract[0],), (contract[1],)), ((), ())),
        precision=precision,
        preferred_element_type=F32,
    )


def params(semantics=None):
    return pltpu.CompilerParams(
        vmem_limit_bytes=VMEM_LIMIT, dimension_semantics=semantics
    )


def vmem():
    return pl.BlockSpec(memory_space=pltpu.VMEM)


def smem():
    return pl.BlockSpec(memory_space=pltpu.SMEM)


def xor_permute(piece, mask):
    devices = lax.axis_size(AXES)
    return lax.ppermute(piece, AXES, [(i, i ^ mask) for i in range(devices)])


def project_kernel(
    me_ref, features_ref, weight_ref, projected_ref, total_ref, send_ref, keep_ref, acc, wide
):
    step = pl.program_id(0)
    rows, embed = acc.shape
    packed = keep_ref.shape[1]
    blocks = embed // LANES

    @pl.when(step == 0)
    def _():
        acc[...] = jnp.zeros_like(acc)

    acc[...] += dot(features_ref[...], weight_ref[...])

    @pl.when(step == pl.num_programs(0) - 1)
    def _():
        projected = acc[...].astype(BF16)
        projected_ref[...] = projected
        total = jnp.sum(projected.astype(F32), axis=0, keepdims=True)
        total_ref[...] = total
        acc[0:8, :] = jnp.concatenate([total, jnp.zeros((7, embed), F32)], axis=0)
        wide[:, :embed] = projected
        wide[:, embed:] = projected[:, : packed - LANES]
        core = me_ref[0] & 1
        for side, out in ((0, keep_ref), (1, send_ref)):
            for r in range(blocks // 2):
                block = (core ^ side) * (blocks // 2) + r
                start = pl.multiple_of(block * LANES, LANES)
                gram = dot(wide[:, pl.ds(start, LANES)], wide[:, pl.ds(start, packed)], (0, 0))
                means = acc[0:8, pl.ds(start, LANES)] * (1.0 / rows)
                totals = jnp.concatenate(
                    [
                        acc[
                            0:8,
                            pl.ds(
                                pl.multiple_of((block + k) % blocks * LANES, LANES), LANES
                            ),
                        ]
                        for k in range(packed // LANES)
                    ],
                    axis=1,
                )
                gram = gram - dot(means, totals, (0, 0), HIGHEST)
                out[r * LANES : (r + 1) * LANES, :] = gram.astype(out.dtype)


def project(me, features, weight):
    rows, depth = features.shape
    embed = weight.shape[1]
    packed = embed // 2 + LANES
    tile = 512
    return pl.pallas_call(
        project_kernel,
        grid_spec=pltpu.PrefetchScalarGridSpec(
            num_scalar_prefetch=1,
            grid=(depth // tile,),
            in_specs=[
                pl.BlockSpec((rows, tile), lambda k, me: (0, k)),
                pl.BlockSpec((tile, embed), lambda k, me: (k, 0)),
            ],
            out_specs=[
                pl.BlockSpec((rows, embed), lambda k, me: (0, 0)),
                pl.BlockSpec((1, embed), lambda k, me: (0, 0)),
                pl.BlockSpec((embed // 2, packed), lambda k, me: (0, 0)),
                pl.BlockSpec((embed // 2, packed), lambda k, me: (0, 0)),
            ],
            scratch_shapes=[
                pltpu.VMEM((rows, embed), F32),
                pltpu.VMEM((rows, embed + packed - LANES), BF16),
            ],
        ),
        out_shape=[
            jax.ShapeDtypeStruct((rows, embed), BF16),
            jax.ShapeDtypeStruct((1, embed), F32),
            jax.ShapeDtypeStruct((embed // 2, packed), BF16),
            jax.ShapeDtypeStruct((embed // 2, packed), F32),
        ],
        compiler_params=params(("arbitrary",)),
        cost_estimate=pl.CostEstimate(
            flops=2 * rows * depth * embed, bytes_accessed=2 * depth * embed, transcendentals=0
        ),
        name="project",
    )(me, features, weight)


def split(value):
    high = value.astype(BF16)
    return high, (value - high.astype(F32)).astype(BF16)


def make_whiten_kernel(rows):
    def kernel(
        place_ref,
        totals_ref,
        packed_ref,
        whitener_ref,
        mean_ref,
        scaled,
        s_hi,
        s_lo,
        a_hi,
        a_lo,
        b_hi,
        b_lo,
        rest,
    ):
        place = place_ref[0]
        embed = scaled.shape[0]
        blocks = embed // LANES
        half = blocks // 2
        pieces, depth, packed = packed_ref.shape
        per_block = LANES // depth
        devices = totals_ref.shape[0]
        total_rows = rows * devices
        tile = 256
        tiles = embed // tile

        mean = jnp.sum(totals_ref[...], axis=0, keepdims=True) * (1.0 / total_rows)
        mean_ref[...] = mean
        shift = totals_ref[...] * (1.0 / rows) - mean

        for i in range(blocks):
            for part in range(per_block):
                piece = (i * per_block + part) ^ place
                wide = packed_ref[piece].astype(F32)
                lines = pl.ds(i * LANES + part * depth, depth)
                for k in range(half + 1):
                    if k == half and i >= half:
                        continue
                    j = (i + k) % blocks
                    scaled[lines, j * LANES : (j + 1) * LANES] = wide[
                        :, k * LANES : (k + 1) * LANES
                    ]
        for i in range(blocks):
            for k in range(1, half + 1):
                if k == half and i >= half:
                    continue
                j = (i + k) % blocks
                scaled[j * LANES : (j + 1) * LANES, i * LANES : (i + 1) * LANES] = scaled[
                    i * LANES : (i + 1) * LANES, j * LANES : (j + 1) * LANES
                ].T
        squares = jnp.zeros((1, 1), F32)
        for t in range(tiles):
            lines = slice(t * tile, (t + 1) * tile)
            between = dot(shift[:, lines], shift, (0, 0), HIGHEST)
            covariance = (scaled[lines, :] + rows * between) * (1.0 / total_rows)
            scaled[lines, :] = covariance
            squares = squares + jnp.sum(
                jnp.sum(covariance * covariance, axis=0, keepdims=True), axis=1, keepdims=True
            )
        frobenius = jnp.sqrt(squares)
        inverse = 1.0 / frobenius
        root = lax.rsqrt(frobenius)

        @pl.loop(0, tiles)
        def _(t):
            lines = pl.ds(pl.multiple_of(t * tile, tile), tile)
            value = scaled[lines, :] * inverse
            scaled[lines, :] = value
            s_hi[lines, :], s_lo[lines, :] = split(value)

        def product(left, right, finish):
            @pl.loop(0, tiles)
            def _(t):
                lines = pl.ds(pl.multiple_of(t * tile, tile), tile)
                left_hi = left[0][lines, :]
                value = dot(left_hi, right[0][...])
                value += dot(left_hi, right[1][...])
                value += dot(left[1][lines, :], right[0][...])
                finish(lines, value)

        def second(lines, value):
            rest[lines, :] = value
            a_hi[lines, :], a_lo[lines, :] = split(value)
            b_hi[lines, :], b_lo[lines, :] = split(value - 9.0 * scaled[lines, :])

        product((s_hi, s_lo), (s_hi, s_lo), second)

        def fourth(lines, value):
            value = (value + 27.0 * rest[lines, :] - 39.0 * scaled[lines, :]) * (1.0 / 16.0)
            rest[lines, :] = value

        product((a_hi, a_lo), (b_hi, b_lo), fourth)

        @pl.loop(0, tiles)
        def _(t):
            lines = pl.ds(pl.multiple_of(t * tile, tile), tile)
            a_hi[lines, :], a_lo[lines, :] = split(rest[lines, :])

        def moved(lines, value):
            scaled[lines, :] = 2.25 * 2.25 * scaled[lines, :] + 4.5 * value
            b_hi[lines, :], b_lo[lines, :] = split(value)

        product((s_hi, s_lo), (a_hi, a_lo), moved)

        def quad(lines, value):
            value = value + scaled[lines, :]
            scaled[lines, :] = value
            s_hi[lines, :], s_lo[lines, :] = split(value)

        product((a_hi, a_lo), (b_hi, b_lo), quad)

        def last(lines, value):
            at = lax.broadcasted_iota(jnp.int32, value.shape, 0) + lines.start
            eye = at == lax.broadcasted_iota(jnp.int32, value.shape, 1)
            value = 0.5 * (3.0 * rest[lines, :] - 2.25 * scaled[lines, :] - value)
            value = value + jnp.where(eye, 0.5 * 3.0 * 2.25, 0.0)
            whitener_ref[lines, :] = (value * root).astype(BF16)

        product((a_hi, a_lo), (s_hi, s_lo), last)

    return kernel


def whiten(place, totals, packed, rows):
    embed = totals.shape[1]
    square = (embed, embed)
    return pl.pallas_call(
        make_whiten_kernel(rows),
        in_specs=[smem(), vmem(), vmem()],
        out_specs=[vmem(), vmem()],
        out_shape=[
            jax.ShapeDtypeStruct(square, BF16),
            jax.ShapeDtypeStruct((1, embed), F32),
        ],
        scratch_shapes=[pltpu.VMEM(square, F32)]
        + [pltpu.VMEM(square, BF16)] * 6
        + [pltpu.VMEM(square, F32)],
        compiler_params=params(),
        cost_estimate=pl.CostEstimate(
            flops=15 * 2 * embed**3, bytes_accessed=2 * embed**2, transcendentals=0
        ),
        name="whiten",
    )(place, totals, packed)


def contrast_kernel(
    me_ref,
    offsets_ref,
    projected_ref,
    mean_ref,
    whitener_ref,
    features_ref,
    ortholog_ref,
    loss_ref,
    send_ref,
    keep_ref,
    white,
    total,
):
    groups, rows, embed = projected_ref.shape
    shares = send_ref.shape[0] + 1
    share = keep_ref.shape[0]
    group = me_ref[0] // shares
    window = me_ref[0] % shares

    @pl.loop(0, groups)
    def _(g):
        centered = (projected_ref[g].astype(F32) - mean_ref[...]).astype(BF16)
        white[g] = dot(centered, whitener_ref[...]).astype(BF16)

    total[...] = jnp.zeros_like(total)
    places = lax.broadcasted_iota(jnp.int32, (rows, rows), 0)

    @pl.loop(0, groups)
    def _(step):
        g = step ^ group
        own = white[g]
        loss = jnp.zeros((1, rows), F32)
        grad = jnp.zeros((rows, embed), F32)
        for k in range(PARTNERS):
            other = white[(g + offsets_ref[g, k]) % groups]
            logits = dot(other, own, (1, 1)) * LOGIT_SCALE
            peak = jnp.max(logits, axis=0, keepdims=True)
            powers = jnp.exp(logits - peak)
            sums = jnp.sum(powers, axis=0, keepdims=True)
            hit = places == ortholog_ref[g, k : k + 1, :]
            picked = jnp.sum(jnp.where(hit, logits, 0.0), axis=0, keepdims=True)
            loss = loss + (peak + jnp.log(sums) - picked)
            weights = (powers * (1.0 / sums) - hit.astype(F32)) * (1.0 / PARTNERS)
            grad = grad + dot(weights.astype(BF16), other, (0, 0))
        loss_ref[pl.ds(g, 1), :] = loss * (1.0 / PARTNERS)
        grad_white = (grad * LOGIT_SCALE).astype(BF16)
        total[...] += dot(features_ref[step], grad_white, (0, 0))

    for r in range(shares):
        piece = total[pl.ds(pl.multiple_of((window ^ r) * share, share), share), :]
        if r == 0:
            keep_ref[...] = piece
        else:
            send_ref[r - 1] = piece.astype(BF16)


def contrast(me, offsets, projected, mean, whitener, features, ortholog, shares):
    groups, rows, embed = projected.shape
    columns = features.shape[2]
    share = columns // shares
    return pl.pallas_call(
        contrast_kernel,
        in_specs=[smem(), smem()] + [vmem()] * 5,
        out_specs=[vmem()] * 3,
        out_shape=[
            jax.ShapeDtypeStruct((groups, rows), F32),
            jax.ShapeDtypeStruct((shares - 1, share, embed), BF16),
            jax.ShapeDtypeStruct((share, embed), F32),
        ],
        scratch_shapes=[
            pltpu.VMEM((groups, rows, embed), BF16),
            pltpu.VMEM((columns, embed), F32),
        ],
        compiler_params=params(),
        cost_estimate=pl.CostEstimate(
            flops=groups * rows * 2 * embed * (embed + 2 * PARTNERS * rows + columns),
            bytes_accessed=2 * groups * rows * embed,
            transcendentals=groups * PARTNERS * rows * rows,
        ),
        name="contrast",
    )(me, offsets, projected, mean, whitener, features, ortholog)


def shards(features, proj_weight, partner_offsets, ortholog_index):
    rows, depth = features.shape
    embed = proj_weight.shape[1]
    groups = lax.axis_size("sp")
    shares = lax.axis_size("win")
    devices = groups * shares
    group = lax.axis_index("sp")
    me = (group * shares + lax.axis_index("win")).astype(jnp.int32)
    me_scalar = me.reshape(1)

    table = jnp.concatenate(
        [ortholog_index.T, jnp.pad(partner_offsets.T, ((0, 0), (0, LANES - 1)))], axis=1
    )
    table = lax.all_gather(table, "sp")
    ortholog = table[:, :, :rows]
    offsets = table[:, :, rows]

    columns = depth // groups
    slices = [lax.dynamic_slice_in_dim(features, group * columns, columns, 1)]
    for k in range(1, groups):
        piece = lax.dynamic_slice_in_dim(features, (group ^ k) * columns, columns, 1)
        slices.append(xor_permute(piece, k * shares))
    feature_slices = jnp.stack(slices)

    projected, total, send, keep = project(me_scalar, features, proj_weight)
    projected_all = lax.all_gather(projected, "sp")
    totals = lax.all_gather(total[0], AXES)

    packed = keep.shape[1]
    part = keep + xor_permute(send, 1).astype(F32)
    stages = []
    low = 1
    place = me & 1
    while part.shape[0] > 32:
        bits = 2
        count = 1 << bits
        stages.append((low, count))
        pieces = part.reshape(count, part.shape[0] // count, packed)
        own = (me >> low) & (count - 1)
        part = lax.dynamic_index_in_dim(pieces, own, 0, keepdims=False)
        for r in range(1, count):
            sent = lax.dynamic_index_in_dim(pieces, own ^ r, 0, keepdims=False).astype(BF16)
            part = part + xor_permute(sent, r << low).astype(F32)
        place = place * count + own
        low += bits
    extra = devices >> low
    mine = part
    for r in range(1, extra):
        part = part + xor_permute(mine.astype(BF16), r << low).astype(F32)
    part = part.astype(BF16)
    depth_piece = part.shape[0]
    for low, count in reversed(stages):
        part = jnp.concatenate(
            [part] + [xor_permute(part, r << low) for r in range(1, count)], axis=0
        )
    part = jnp.concatenate([part, xor_permute(part, 1)], axis=0)
    part = part.reshape(embed // depth_piece, depth_piece, packed)

    whitener, mean = whiten(place.reshape(1), totals, part, rows)
    loss, send, keep = contrast(
        me_scalar, offsets, projected_all, mean, whitener, feature_slices, ortholog, shares
    )
    for r in range(1, shares):
        keep = keep + xor_permute(send[r - 1], r).astype(F32)
    high, low = split(keep)
    weight_grad = dot(high, whitener, (1, 1)) + dot(low, whitener, (1, 1))
    window_loss = lax.dynamic_index_in_dim(loss, group, 0, keepdims=False)
    return window_loss, weight_grad


def solution(mesh):
    return jax.shard_map(
        shards,
        mesh=mesh,
        in_specs=(P(("sp", "win"), None), P(), P("sp", None), P(("sp", "win"), None)),
        out_specs=(P(("sp", "win")), P(("sp", "win"), None)),
        check_vma=False,
    )
```

time: 605 us -> 275 us (0.45)
  waiting for transfers between devices: 465 us -> 25.5 us
  Pallas kernels: 0 us -> 90.8 us
  blocking collectives: 42 us -> 91.8 us
  matrix products: 50.6 us -> 3.5 us
  starting transfers between devices: 9.58 us -> 29.6 us
  other arithmetic: 11.6 us -> 1.36 us
  local copies, waits for them, and re-layouts: 9.25 us -> 17.8 us
    reduce_scatter x1 -> x0, waiting for transfers between devices: 183 us -> none  [shards(): lax.psum_scatter(local_term, ('sp', 'win'), scatter_dimension=0, tiled=True)]
    psum x1 -> x0, waiting for transfers between devices: 141 us -> none  [shards(): lax.psum(jnp.dot(centered_wide.T, centered_wide, precision=highest, prefe...]
    all_gather x0 -> x2, blocking collectives: none -> 91.8 us  [the longest x1 61.1 us: shards(): totals = lax.all_gather(total[0], AXES)]
    pallas_call x0 -> x3, Pallas kernels: none -> 90.8 us  [the longest x1 44.9 us: whiten(): pl.pallas_call(make_whiten_kernel(rows), in_specs=[smem(), vmem(), vmem()...]
    ppermute x6 -> x24, waiting for transfers between devices: 85.2 us -> 25.5 us  [xor_permute(): return lax.ppermute(piece, AXES, [(i, i ^ mask) for i in range(devices)])]
    all_gather x2 -> x1, waiting for transfers between devices: 56.4 us -> 0.01 us  [shards(): projected_all = lax.all_gather(projected, 'sp')]
    dot_general x12 -> x2, matrix products: 50.6 us -> 3.5 us  [dot(): lax.dot_general(a, b, (((contract[0],), (contract[1],)), ((), ())), preci...]
    psum x1 -> x0, blocking collectives: 42 us -> none  [shards(): lax.psum(jnp.sum(projected_wide, axis=0), ('sp', 'win')) / total_rows]
  transfers between devices with their start and end apart: 10 -> 25, of which waited for: 8 -> 10; matrix products, arithmetic and copies ran while one was open for 0% -> 6% of each run, Pallas kernels for 0% -> 16%
where the time goes in v1:
time: 275 us
  blocking collectives  91.8 us (33%)
  Pallas kernels  90.8 us (33%)
  starting transfers between devices  29.6 us (11%)
  waiting for transfers between devices  25.5 us (9%)
  local copies, waits for them, and re-layouts  17.8 us (6%)
  between operations  14.3 us (5%)
  matrix products  3.5 us (1%)
    all_gather x1, blocking collectives, shards(): totals = lax.all_gather(total[0], AXES)  61.1 us
    pallas_call x1, Pallas kernels, whiten(): pl.pallas_call(make_whiten_kernel(rows), in_specs=[smem(), vmem(), vmem()...  44.9 us
    pallas_call x1, Pallas kernels, contrast(): pl.pallas_call(contrast_kernel, in_specs=[smem(), smem()] + [vmem()] * 5,...  33.4 us
    all_gather x1, blocking collectives, shards(): table = lax.all_gather(table, 'sp')  30.7 us
    ppermute x24, starting transfers between devices, xor_permute(): return lax.ppermute(piece, AXES, [(i, i ^ mask) for i in range(devices)])  29.6 us
    ppermute x24, waiting for transfers between devices, xor_permute(): return lax.ppermute(piece, AXES, [(i, i ^ mask) for i in range(devices)])  25.5 us
    pallas_call x1, Pallas kernels, project(): pl.pallas_call(project_kernel, grid_spec=pltpu.PrefetchScalarGridSpec(num...  12.4 us
    unnamed x35, local copies, waits for them, and re-layouts  10.9 us
  transfers between devices with their start and end apart: 25, of which 10 were waited for; matrix products, arithmetic and copies ran while one was open for 6% of the time, Pallas kernels for 16%

profile of v1, /device:TPU:0, one launch (start us, length us, event | category | flops | bytes accessed | tf_op | source)
XLA Modules:
  0.0 274.7 jit_solution(18431226720842523779)
XLA Ops:
  7.2 0.0 all-gather.6.cloned.1.call-start
  7.2 12.4 %project.1 = (bf16[256,1024]{1,0:T(8,128)(2,1)}, f32[1,1024]{1,0:T(1,128)}, bf16[512,640]{1,0:T(8,128)(2,1)}, f32[512,640]{1,0:T(8,128)}) custom-call(s32[1]{0:T(128)} %bitcast.me_ref, bf16[256,4096]{1,0:T(8,128)(2,1)} %features_ref.1, bf16[4096,1024]{1,0:T(8,128)(2,1)} %weight_ref.1), custom_call_target="tpu_custom_call" | custom-call | flops 2147483648 | bytes 8388608 | tf_op jit(solution)/shard_map/project/pallas_call | solution.py:98
  19.6 0.0 all-gather.6.cloned.1.call-update
  19.7 0.0 copy-start.6
  19.8 1.3 constant_dynamic-slice_fusion.1
  21.0 3.0 %collective-permute-start.14 = (bf16[256,512]{1,0:T(8,128)(2,1)}, bf16[256,512]{1,0:T(8,128)(2,1)}, u32[]{:S(2)}, u32[]{:S(2)}) collective-permute-start(bf16[256,512]{1,0:T(8,128)(2,1)} %get-tuple-element.27), channel_id=1, source_target_pairs={{0,4},{1,5},{2,6},{3,7},{4,0},{5,1},{6,2},{7,3},{8,12},{9,13},{10,... | collective-permute-start | bytes 786440 | tf_op jit(solution)/shard_map/ppermute | solution.py:44
  24.0 1.6 collective-permute-start.15
  25.5 0.0 collective-permute-start.16
  25.5 3.0 %collective-permute-start.17 = (bf16[256,512]{1,0:T(8,128)(2,1)}, bf16[256,512]{1,0:T(8,128)(2,1)}, u32[]{:S(2)}, u32[]{:S(2)}) collective-permute-start(bf16[256,512]{1,0:T(8,128)(2,1)} %get-tuple-element.24), channel_id=1, source_target_pairs={{0,16},{1,17},{2,18},{3,19},{4,20},{5,21},{6,22},{7,23},{8,24},{9,... | collective-permute-start | bytes 786440 | tf_op jit(solution)/shard_map/ppermute | solution.py:44
  28.6 0.1 copy.13
  28.6 0.7 bitcast_dynamic-update-slice_fusion.7
  29.4 61.1 %all-gather.3 = f32[32,1,1024]{2,1,0:T(1,128)S(1)} all-gather(f32[1,1,1024]{2,1,0:T(1,128)S(1)} %bitcast.74), channel_id=1, replica_groups=mesh['sp'=8,'win'=4] {'sp','win'}, dimensions={0}, use_global_device_ids=true | all-gather | bytes 135168 | tf_op jit(solution)/shard_map/all_gather | solution.py:393
  90.5 30.7 %all-gather.2 = s32[8,4,384]{2,1,0:T(4,128)S(1)} all-gather(s32[1,4,384]{2,1,0:T(4,128)S(1)} %fusion.14), channel_id=2, replica_groups=mesh['sp'=8,'win'=4] {'sp'}, dimensions={0}, use_global_device_ids=true | all-gather | bytes 55296 | tf_op jit(solution)/shard_map/all_gather | solution.py:380
  121.2 0.6 slice.21.ortholog_ref
  121.8 0.7 copy.15
  122.5 0.1 copy.10
  122.6 0.7 copy.11.offsets_ref
  123.3 1.7 bitcast_dynamic-update-slice_fusion.6
  125.0 0.0 collective-permute-done.15
  125.0 1.7 bitcast_dynamic-update-slice_fusion.5
  126.7 1.2 convert_add_fusion
  127.9 0.1 fusion.3
  128.0 0.1 collective-permute-start.1
  128.1 0.1 collective-permute-start.2
  128.2 0.0 collective-permute-done.16
  128.2 3.4 %collective-permute-start.3 = (bf16[128,640]{1,0:T(8,128)(2,1)S(1)}, bf16[128,640]{1,0:T(8,128)(2,1)S(1)}, u32[]{:S(2)}, u32[]{:S(2)}) collective-permute-start(bf16[128,640]{1,0:T(8,128)(2,1)S(1)} %get-tuple-element.30), channel_id=1, source_target_pairs={{0,6},{1,7},{2,4},{3,5},{4,2},{5,3},{6,0},{7,1},{8,14},{9,15},{10,... | collective-permute-start | bytes 491528 | tf_op jit(solution)/shard_map/ppermute | solution.py:44
  131.6 1.7 bitcast_dynamic-update-slice_fusion.4
  133.2 0.3 collective-permute-done.1
  133.6 0.9 collective-permute-start.19
  134.4 2.5 collective-permute-done.3
  136.9 0.1 fusion.1
  137.0 0.3 collective-permute-start.4
  137.3 1.9 collective-permute-start.5
  139.2 2.2 collective-permute-start.6
  141.5 1.7 bitcast_dynamic-update-slice_fusion.3
  143.2 1.1 collective-permute-done.5
  144.2 0.9 collective-permute-done.6
  145.2 0.4 collective-permute-start.7
  145.6 2.9 %collective-permute-start.8 = (bf16[32,640]{1,0:T(8,128)(2,1)S(1)}, bf16[32,640]{1,0:T(8,128)(2,1)S(1)}, u32[]{:S(2)}, u32[]{:S(2)}) collective-permute-start(bf16[32,640]{1,0:T(8,128)(2,1)S(1)} %get-tuple-element.21), channel_id=1, source_target_pairs={{0,16},{1,17},{2,18},{3,19},{4,20},{5,21},{6,22},{7,23},{8,24},{9,... | collective-permute-start | bytes 122888 | tf_op jit(solution)/shard_map/ppermute | solution.py:44
  148.5 1.1 collective-permute-start.9
  149.6 4.1 %collective-permute-start.20 = (bf16[256,512]{1,0:T(8,128)(2,1)S(1)}, bf16[256,512]{1,0:T(8,128)(2,1)S(1)}, u32[]{:S(2)}, u32[]{:S(2)}) collective-permute-start(bf16[256,512]{1,0:T(8,128)(2,1)S(1)} %copy-done.4), channel_id=1, source_target_pairs={{0,28},{1,29},{2,30},{3,31},{4,24},{5,25},{6,26},{7,27},{8,20},{9,... | collective-permute-start | bytes 786440 | tf_op jit(solution)/shard_map/ppermute | solution.py:44
  153.7 1.2 collective-permute-done.9
  154.9 0.9 collective-permute-start.10
  155.8 0.7 collective-permute-start.11
  156.5 4.1 %collective-permute-done.10 = bf16[128,640]{1,0:T(8,128)(2,1)S(1)} collective-permute-done((bf16[128,640]{1,0:T(8,128)(2,1)S(1)}, bf16[128,640]{1,0:T(8,128)(2,1)S(1)}, u32[]{:S(2)}, u32[]{:S(2)}) %collective-permute-start.10) | collective-permute-done | bytes 163872 | tf_op jit(solution)/shard_map/ppermute | solution.py:44
  160.5 1.1 collective-permute-start.12
  161.7 0.4 collective-permute-done.11
  162.1 4.6 %collective-permute-done.12 = bf16[128,640]{1,0:T(8,128)(2,1)S(1)} collective-permute-done((bf16[128,640]{1,0:T(8,128)(2,1)S(1)}, bf16[128,640]{1,0:T(8,128)(2,1)S(1)}, u32[]{:S(2)}, u32[]{:S(2)}) %collective-permute-start.12) | collective-permute-done | bytes 163872 | tf_op jit(solution)/shard_map/ppermute | solution.py:44
  166.8 0.1 collective-permute-start.13
  166.9 0.7 bitcast_dynamic-update-slice_fusion.2
  167.6 0.7 bitcast_dynamic-update-slice_fusion.1
  168.3 0.7 bitcast_dynamic-update-slice_fusion.features_ref
  169.1 0.1 constant_dynamic-update-slice_fusion.7
  169.2 1.0 copy-done.8
  170.2 44.9 %whiten.1 = (bf16[1024,1024]{1,0:T(8,128)(2,1)}, f32[1,1024]{1,0:T(1,128)}) custom-call(s32[1]{0:T(128)} %bitcast.6.place_ref, f32[32,1024]{1,0:T(8,128)} %bitcast.71, bf16[32,32,640]{2,1,0:T(8,128)(2,1)} %bitcast.75), custom_call_target="tpu_custom_call" | custom-call | flops 32212254720 | bytes 2097152 | tf_op jit(solution)/shard_map/whiten/pallas_call | solution.py:264
  215.2 33.4 %contrast.1 = (f32[8,256]{1,0:T(8,128)}, bf16[3,128,1024]{2,1,0:T(8,128)(2,1)}, f32[128,1024]{1,0:T(8,128)}) custom-call(s32[1]{0:T(128)} %bitcast.me_ref, s32[8,4]{1,0:T(8,128)} %copy.11.offsets_ref, bf16[8,256,1024]{2,1,0:T(8,128)(2,1)} %bitcast.78, f32[1,1024]{1,0:T(1,128)} %get-tuple-element.15.mean_ref, ...), custom_call_target="tpu_custom_call" | custom-call | flops 15032385536 | bytes 4194304 | tf_op jit(solution)/shard_map/contrast/pallas_call | solution.py:344
  248.6 2.0 slice_bitcast_fusion.2
  250.7 0.5 collective-permute-start.21
  251.2 1.5 collective-permute-start.22
  252.6 1.3 constant_dynamic-slice_fusion
  253.9 6.6 %collective-permute-done.22 = bf16[128,1024]{1,0:T(8,128)(2,1)S(1)} collective-permute-done((bf16[128,1024]{1,0:T(8,128)(2,1)}, bf16[128,1024]{1,0:T(8,128)(2,1)S(1)}, u32[]{:S(2)}, u32[]{:S(2)}) %collective-permute-start.22) | collective-permute-done | bytes 262176 | tf_op jit(solution)/shard_map/ppermute | solution.py:44
  260.5 3.8 %collective-permute-done.23 = bf16[128,1024]{1,0:T(8,128)(2,1)S(1)} collective-permute-done((bf16[128,1024]{1,0:T(8,128)(2,1)}, bf16[128,1024]{1,0:T(8,128)(2,1)S(1)}, u32[]{:S(2)}, u32[]{:S(2)}) %collective-permute-start.23) | collective-permute-done | bytes 262176 | tf_op jit(solution)/shard_map/ppermute | solution.py:44
  264.3 1.9 fusion.2
  266.2 1.6 convolution_add_fusion
  (46 shorter events, 0.3 us)
Async XLA Ops:
  7.2 208.0 %all-gather.6.cloned.1.call-start = ((), (), s32[]{:S(2)}) async-start(), calls=%async_computation | async-start | bytes 4718592 | tf_op jit(solution)/shard_map/all_gather | solution.py:392
  7.2 12.5 %copy-start.1 = (bf16[256,4096]{1,0:T(8,128)(2,1)S(1)}, bf16[256,4096]{1,0:T(8,128)(2,1)}, u32[]{:S(2)}) copy-start(bf16[256,4096]{1,0:T(8,128)(2,1)} %features_ref.1) | copy-start | bytes 6291460
  19.6 8.9 %copy-start.9 = (s32[1,4]{1,0:T(1,128)S(1)}, s32[1,4]{1,0:T(1,128)}, u32[]{:S(2)}) copy-start(s32[1,4]{1,0:T(1,128)} %param.6) | copy-start | bytes 52
  19.7 9.7 %copy-start.6 = (s32[256,4]{0,1:T(4,128)S(1)}, s32[256,4]{0,1:T(4,128)}, u32[]{:S(2)}) copy-start(s32[256,4]{0,1:T(4,128)} %param.7) | copy-start | bytes 12292
  19.7 9.7 %copy-start.7 = (f32[1,1024]{1,0:T(1,128)S(1)}, f32[1,1024]{1,0:T(1,128)}, u32[]{:S(2)}) copy-start(f32[1,1024]{1,0:T(1,128)} %get-tuple-element.12) | copy-start | bytes 12292
  19.7 106.9 %copy-start.3 = (f32[512,640]{1,0:T(8,128)S(1)}, f32[512,640]{1,0:T(8,128)}, u32[]{:S(2)}) copy-start(f32[512,640]{1,0:T(8,128)} %get-tuple-element.13) | copy-start | bytes 3932164
  21.0 102.3 %collective-permute-start.14 = (bf16[256,512]{1,0:T(8,128)(2,1)}, bf16[256,512]{1,0:T(8,128)(2,1)}, u32[]{:S(2)}, u32[]{:S(2)}) collective-permute-start(bf16[256,512]{1,0:T(8,128)(2,1)} %get-tuple-element.27), channel_id=1, source_target_pairs={{0,4},{1,5},{2,6},{3,7},{4,0},{5,1},{6,2},{7,3},{8,12},{9,13},{10,... | collective-permute-start | bytes 786440 | tf_op jit(solution)/shard_map/ppermute | solution.py:44
  24.0 101.0 %collective-permute-start.15 = (bf16[256,512]{1,0:T(8,128)(2,1)}, bf16[256,512]{1,0:T(8,128)(2,1)}, u32[]{:S(2)}, u32[]{:S(2)}) collective-permute-start(bf16[256,512]{1,0:T(8,128)(2,1)} %get-tuple-element.26), channel_id=1, source_target_pairs={{0,8},{1,9},{2,10},{3,11},{4,12},{5,13},{6,14},{7,15},{8,0},{9,1},... | collective-permute-start | bytes 786440 | tf_op jit(solution)/shard_map/ppermute | solution.py:44
  25.5 102.6 %collective-permute-start.16 = (bf16[256,512]{1,0:T(8,128)(2,1)}, bf16[256,512]{1,0:T(8,128)(2,1)}, u32[]{:S(2)}, u32[]{:S(2)}) collective-permute-start(bf16[256,512]{1,0:T(8,128)(2,1)} %get-tuple-element.25), channel_id=1, source_target_pairs={{0,12},{1,13},{2,14},{3,15},{4,8},{5,9},{6,10},{7,11},{8,4},{9,5},... | collective-permute-start | bytes 786440 | tf_op jit(solution)/shard_map/ppermute | solution.py:44
  25.5 113.7 %collective-permute-start.17 = (bf16[256,512]{1,0:T(8,128)(2,1)}, bf16[256,512]{1,0:T(8,128)(2,1)}, u32[]{:S(2)}, u32[]{:S(2)}) collective-permute-start(bf16[256,512]{1,0:T(8,128)(2,1)} %get-tuple-element.24), channel_id=1, source_target_pairs={{0,16},{1,17},{2,18},{3,19},{4,20},{5,21},{6,22},{7,23},{8,24},{9,... | collective-permute-start | bytes 786440 | tf_op jit(solution)/shard_map/ppermute | solution.py:44
  28.6 98.1 %collective-permute-start = (bf16[512,640]{1,0:T(8,128)(2,1)}, bf16[512,640]{1,0:T(8,128)(2,1)}, u32[]{:S(2)}, u32[]{:S(2)}) collective-permute-start(bf16[512,640]{1,0:T(8,128)(2,1)} %get-tuple-element.14), channel_id=1, source_target_pairs={{0,1},{1,0},{2,3},{3,2},{4,5},{5,4},{6,7},{7,6},{8,9},{9,8},{10,11... | collective-permute-start | bytes 1966088 | tf_op jit(solution)/shard_map/ppermute | solution.py:44
  123.3 43.6 %collective-permute-start.18 = (bf16[256,512]{1,0:T(8,128)(2,1)}, bf16[256,512]{1,0:T(8,128)(2,1)S(1)}, u32[]{:S(2)}, u32[]{:S(2)}) collective-permute-start(bf16[256,512]{1,0:T(8,128)(2,1)} %get-tuple-element.23), channel_id=1, source_target_pairs={{0,20},{1,21},{2,22},{3,23},{4,16},{5,17},{6,18},{7,19},{8,28},{9,... | collective-permute-start | bytes 786440 | tf_op jit(solution)/shard_map/ppermute | solution.py:44
  126.7 6.9 %copy-start.5 = (bf16[256,512]{1,0:T(8,128)(2,1)S(1)}, bf16[256,512]{1,0:T(8,128)(2,1)}, u32[]{:S(2)}) copy-start(bf16[256,512]{1,0:T(8,128)(2,1)} %get-tuple-element.28) | copy-start | bytes 786436
  127.9 21.7 %copy-start.4 = (bf16[256,512]{1,0:T(8,128)(2,1)S(1)}, bf16[256,512]{1,0:T(8,128)(2,1)}, u32[]{:S(2)}) copy-start(bf16[256,512]{1,0:T(8,128)(2,1)} %get-tuple-element.22) | copy-start | bytes 786436
  128.0 5.5 %collective-permute-start.1 = (bf16[128,640]{1,0:T(8,128)(2,1)S(1)}, bf16[128,640]{1,0:T(8,128)(2,1)S(1)}, u32[]{:S(2)}, u32[]{:S(2)}) collective-permute-start(bf16[128,640]{1,0:T(8,128)(2,1)S(1)} %get-tuple-element.29), channel_id=1, source_target_pairs={{0,2},{1,3},{2,0},{3,1},{4,6},{5,7},{6,4},{7,5},{8,10},{9,11},{10,... | collective-permute-start | bytes 491528 | tf_op jit(solution)/shard_map/ppermute | solution.py:44
  128.1 6.4 %collective-permute-start.2 = (bf16[128,640]{1,0:T(8,128)(2,1)S(1)}, bf16[128,640]{1,0:T(8,128)(2,1)S(1)}, u32[]{:S(2)}, u32[]{:S(2)}) collective-permute-start(bf16[128,640]{1,0:T(8,128)(2,1)S(1)} %get-tuple-element.31), channel_id=1, source_target_pairs={{0,4},{1,5},{2,6},{3,7},{4,0},{5,1},{6,2},{7,3},{8,12},{9,13},{10,... | collective-permute-start | bytes 491528 | tf_op jit(solution)/shard_map/ppermute | solution.py:44
  128.2 8.7 %collective-permute-start.3 = (bf16[128,640]{1,0:T(8,128)(2,1)S(1)}, bf16[128,640]{1,0:T(8,128)(2,1)S(1)}, u32[]{:S(2)}, u32[]{:S(2)}) collective-permute-start(bf16[128,640]{1,0:T(8,128)(2,1)S(1)} %get-tuple-element.30), channel_id=1, source_target_pairs={{0,6},{1,7},{2,4},{3,5},{4,2},{5,3},{6,0},{7,1},{8,14},{9,15},{10,... | collective-permute-start | bytes 491528 | tf_op jit(solution)/shard_map/ppermute | solution.py:44
  133.6 34.1 %collective-permute-start.19 = (bf16[256,512]{1,0:T(8,128)(2,1)S(1)}, bf16[256,512]{1,0:T(8,128)(2,1)S(1)}, u32[]{:S(2)}, u32[]{:S(2)}) collective-permute-start(bf16[256,512]{1,0:T(8,128)(2,1)S(1)} %copy-done.5), channel_id=1, source_target_pairs={{0,24},{1,25},{2,26},{3,27},{4,28},{5,29},{6,30},{7,31},{8,16},{9,... | collective-permute-start | bytes 786440 | tf_op jit(solution)/shard_map/ppermute | solution.py:44
  137.0 6.1 %collective-permute-start.4 = (bf16[32,640]{1,0:T(8,128)(2,1)S(1)}, bf16[32,640]{1,0:T(8,128)(2,1)S(1)}, u32[]{:S(2)}, u32[]{:S(2)}) collective-permute-start(bf16[32,640]{1,0:T(8,128)(2,1)S(1)} %get-tuple-element.35), channel_id=1, source_target_pairs={{0,8},{1,9},{2,10},{3,11},{4,12},{5,13},{6,14},{7,15},{8,0},{9,1},... | collective-permute-start | bytes 122888 | tf_op jit(solution)/shard_map/ppermute | solution.py:44
  137.3 6.9 %collective-permute-start.5 = (bf16[32,640]{1,0:T(8,128)(2,1)S(1)}, bf16[32,640]{1,0:T(8,128)(2,1)S(1)}, u32[]{:S(2)}, u32[]{:S(2)}) collective-permute-start(bf16[32,640]{1,0:T(8,128)(2,1)S(1)} %get-tuple-element.37), channel_id=1, source_target_pairs={{0,16},{1,17},{2,18},{3,19},{4,20},{5,21},{6,22},{7,23},{8,24},{9,... | collective-permute-start | bytes 122888 | tf_op jit(solution)/shard_map/ppermute | solution.py:44
  139.2 5.9 %collective-permute-start.6 = (bf16[32,640]{1,0:T(8,128)(2,1)S(1)}, bf16[32,640]{1,0:T(8,128)(2,1)S(1)}, u32[]{:S(2)}, u32[]{:S(2)}) collective-permute-start(bf16[32,640]{1,0:T(8,128)(2,1)S(1)} %get-tuple-element.36), channel_id=1, source_target_pairs={{0,24},{1,25},{2,26},{3,27},{4,28},{5,29},{6,30},{7,31},{8,16},{9,... | collective-permute-start | bytes 122888 | tf_op jit(solution)/shard_map/ppermute | solution.py:44
  145.2 4.5 %collective-permute-start.7 = (bf16[32,640]{1,0:T(8,128)(2,1)S(1)}, bf16[32,640]{1,0:T(8,128)(2,1)S(1)}, u32[]{:S(2)}, u32[]{:S(2)}) collective-permute-start(bf16[32,640]{1,0:T(8,128)(2,1)S(1)} %get-tuple-element.21), channel_id=1, source_target_pairs={{0,8},{1,9},{2,10},{3,11},{4,12},{5,13},{6,14},{7,15},{8,0},{9,1},... | collective-permute-start | bytes 122888 | tf_op jit(solution)/shard_map/ppermute | solution.py:44
  145.6 8.1 %collective-permute-start.8 = (bf16[32,640]{1,0:T(8,128)(2,1)S(1)}, bf16[32,640]{1,0:T(8,128)(2,1)S(1)}, u32[]{:S(2)}, u32[]{:S(2)}) collective-permute-start(bf16[32,640]{1,0:T(8,128)(2,1)S(1)} %get-tuple-element.21), channel_id=1, source_target_pairs={{0,16},{1,17},{2,18},{3,19},{4,20},{5,21},{6,22},{7,23},{8,24},{9,... | collective-permute-start | bytes 122888 | tf_op jit(solution)/shard_map/ppermute | solution.py:44
  148.5 6.4 %collective-permute-start.9 = (bf16[32,640]{1,0:T(8,128)(2,1)S(1)}, bf16[32,640]{1,0:T(8,128)(2,1)S(1)}, u32[]{:S(2)}, u32[]{:S(2)}) collective-permute-start(bf16[32,640]{1,0:T(8,128)(2,1)S(1)} %get-tuple-element.21), channel_id=1, source_target_pairs={{0,24},{1,25},{2,26},{3,27},{4,28},{5,29},{6,30},{7,31},{8,16},{9,... | collective-permute-start | bytes 122888 | tf_op jit(solution)/shard_map/ppermute | solution.py:44
  149.6 18.7 %collective-permute-start.20 = (bf16[256,512]{1,0:T(8,128)(2,1)S(1)}, bf16[256,512]{1,0:T(8,128)(2,1)S(1)}, u32[]{:S(2)}, u32[]{:S(2)}) collective-permute-start(bf16[256,512]{1,0:T(8,128)(2,1)S(1)} %copy-done.4), channel_id=1, source_target_pairs={{0,28},{1,29},{2,30},{3,31},{4,24},{5,25},{6,26},{7,27},{8,20},{9,... | collective-permute-start | bytes 786440 | tf_op jit(solution)/shard_map/ppermute | solution.py:44
  154.9 5.6 %collective-permute-start.10 = (bf16[128,640]{1,0:T(8,128)(2,1)S(1)}, bf16[128,640]{1,0:T(8,128)(2,1)S(1)}, u32[]{:S(2)}, u32[]{:S(2)}) collective-permute-start(bf16[128,640]{1,0:T(8,128)(2,1)S(1)} %pad_maximum_fusion), channel_id=1, source_target_pairs={{0,2},{1,3},{2,0},{3,1},{4,6},{5,7},{6,4},{7,5},{8,10},{9,11},{10,... | collective-permute-start | bytes 491528 | tf_op jit(solution)/shard_map/ppermute | solution.py:44
  155.8 6.3 %collective-permute-start.11 = (bf16[128,640]{1,0:T(8,128)(2,1)S(1)}, bf16[128,640]{1,0:T(8,128)(2,1)S(1)}, u32[]{:S(2)}, u32[]{:S(2)}) collective-permute-start(bf16[128,640]{1,0:T(8,128)(2,1)S(1)} %pad_maximum_fusion), channel_id=1, source_target_pairs={{0,4},{1,5},{2,6},{3,7},{4,0},{5,1},{6,2},{7,3},{8,12},{9,13},{10,... | collective-permute-start | bytes 491528 | tf_op jit(solution)/shard_map/ppermute | solution.py:44
  160.5 6.2 %collective-permute-start.12 = (bf16[128,640]{1,0:T(8,128)(2,1)S(1)}, bf16[128,640]{1,0:T(8,128)(2,1)S(1)}, u32[]{:S(2)}, u32[]{:S(2)}) collective-permute-start(bf16[128,640]{1,0:T(8,128)(2,1)S(1)} %pad_maximum_fusion), channel_id=1, source_target_pairs={{0,6},{1,7},{2,4},{3,5},{4,2},{5,3},{6,0},{7,1},{8,14},{9,15},{10,... | collective-permute-start | bytes 491528 | tf_op jit(solution)/shard_map/ppermute | solution.py:44
  166.8 2.3 collective-permute-start.13
  169.2 1.1 copy-start.8
  215.2 49.1 %copy-start = (bf16[1024,1024]{1,0:T(8,128)(2,1)S(1)}, bf16[1024,1024]{1,0:T(8,128)(2,1)}, u32[]{:S(2)}) copy-start(bf16[1024,1024]{1,0:T(8,128)(2,1)} %get-tuple-element.16.whitener_ref) | copy-start | bytes 6291460
  250.7 15.5 %copy-start.2 = (f32[128,1024]{1,0:T(8,128)S(1)}, f32[128,1024]{1,0:T(8,128)}, u32[]{:S(2)}) copy-start(f32[128,1024]{1,0:T(8,128)} %get-tuple-element.18) | copy-start | bytes 1572868
  250.7 3.2 %collective-permute-start.21 = (bf16[128,1024]{1,0:T(8,128)(2,1)}, bf16[128,1024]{1,0:T(8,128)(2,1)S(1)}, u32[]{:S(2)}, u32[]{:S(2)}) collective-permute-start(bf16[128,1024]{1,0:T(8,128)(2,1)} %get-tuple-element.32), channel_id=1, source_target_pairs={{0,1},{1,0},{2,3},{3,2},{4,5},{5,4},{6,7},{7,6},{8,9},{9,8},{10,11... | collective-permute-start | bytes 786440 | tf_op jit(solution)/shard_map/ppermute | solution.py:44
  251.2 9.4 %collective-permute-start.22 = (bf16[128,1024]{1,0:T(8,128)(2,1)}, bf16[128,1024]{1,0:T(8,128)(2,1)S(1)}, u32[]{:S(2)}, u32[]{:S(2)}) collective-permute-start(bf16[128,1024]{1,0:T(8,128)(2,1)} %get-tuple-element.34), channel_id=1, source_target_pairs={{0,2},{1,3},{2,0},{3,1},{4,6},{5,7},{6,4},{7,5},{8,10},{9,11},{10,... | collective-permute-start | bytes 786440 | tf_op jit(solution)/shard_map/ppermute | solution.py:44
  252.6 11.7 %collective-permute-start.23 = (bf16[128,1024]{1,0:T(8,128)(2,1)}, bf16[128,1024]{1,0:T(8,128)(2,1)S(1)}, u32[]{:S(2)}, u32[]{:S(2)}) collective-permute-start(bf16[128,1024]{1,0:T(8,128)(2,1)} %get-tuple-element.33), channel_id=1, source_target_pairs={{0,3},{1,2},{2,1},{3,0},{4,7},{5,6},{6,5},{7,4},{8,11},{9,10},{10,... | collective-permute-start | bytes 786440 | tf_op jit(solution)/shard_map/ppermute | solution.py:44
Sparse Core Ops, SparseCore 0:
  19.8 86.1 all-gather.5

commit v2 on v1

v2 whole, which is shorter than its diff:
```python
import jax
import jax.numpy as jnp
from jax import lax
from jax.experimental import pallas as pl
from jax.experimental.pallas import tpu as pltpu
from jax.sharding import PartitionSpec as P

PARTNERS = 4
LOGIT_SCALE = 0.125
AXES = ("sp", "win")
LANES = 128
F32 = jnp.float32
BF16 = jnp.bfloat16
HIGHEST = lax.Precision.HIGHEST


def dot(a, b, contract=(1, 0), precision=None):
    return lax.dot_general(
        a,
        b,
        (((contract[0],), (contract[1],)), ((), ())),
        precision=precision,
        preferred_element_type=F32,
    )


def params(mebibytes, semantics=None):
    return pltpu.CompilerParams(
        vmem_limit_bytes=mebibytes * 2**20, dimension_semantics=semantics
    )


def vmem():
    return pl.BlockSpec(memory_space=pltpu.VMEM)


def smem():
    return pl.BlockSpec(memory_space=pltpu.SMEM)


def xor_permute(piece, mask):
    devices = lax.axis_size(AXES)
    return lax.ppermute(piece, AXES, [(i, i ^ mask) for i in range(devices)])


def project_kernel(
    me_ref, features_ref, weight_ref, projected_ref, total_ref, send_ref, keep_ref, acc, wide
):
    step = pl.program_id(0)
    rows, embed = acc.shape
    packed = keep_ref.shape[1]
    blocks = embed // LANES

    @pl.when(step == 0)
    def _():
        acc[...] = jnp.zeros_like(acc)

    acc[...] += dot(features_ref[...], weight_ref[...])

    @pl.when(step == pl.num_programs(0) - 1)
    def _():
        projected = acc[...].astype(BF16)
        projected_ref[...] = projected
        total = jnp.sum(projected.astype(F32), axis=0, keepdims=True)
        total_ref[...] = total
        wide[:, :embed] = projected
        wide[:, embed:] = projected[:, : packed - LANES]
        ones = jnp.ones((rows, LANES), BF16)
        means = total * (1.0 / rows)
        acc[0:8, :] = jnp.broadcast_to(means, (8, embed))
        core = me_ref[0] & 1
        for side, out in ((0, keep_ref), (1, send_ref)):
            for r in range(blocks // 2):
                block = (core ^ side) * (blocks // 2) + r
                start = pl.multiple_of(block * LANES, LANES)
                own = wide[:, pl.ds(start, LANES)]
                gram = dot(own, wide[:, pl.ds(start, packed)], (0, 0))
                sums = dot(own, ones, (0, 0))
                for k in range(packed // LANES):
                    other = pl.multiple_of((block + k) % blocks * LANES, LANES)
                    at = slice(k * LANES, (k + 1) * LANES)
                    value = gram[:, at] - sums * acc[0:1, pl.ds(other, LANES)]
                    out[r * LANES : (r + 1) * LANES, at] = value.astype(out.dtype)


def project(me, features, weight):
    rows, depth = features.shape
    embed = weight.shape[1]
    packed = embed // 2 + LANES
    tile = 512
    return pl.pallas_call(
        project_kernel,
        grid_spec=pltpu.PrefetchScalarGridSpec(
            num_scalar_prefetch=1,
            grid=(depth // tile,),
            in_specs=[
                pl.BlockSpec((rows, tile), lambda k, me: (0, k)),
                pl.BlockSpec((tile, embed), lambda k, me: (k, 0)),
            ],
            out_specs=[
                pl.BlockSpec((rows, embed), lambda k, me: (0, 0)),
                pl.BlockSpec((1, embed), lambda k, me: (0, 0)),
                pl.BlockSpec((embed // 2, packed), lambda k, me: (0, 0)),
                pl.BlockSpec((embed // 2, packed), lambda k, me: (0, 0)),
            ],
            scratch_shapes=[
                pltpu.VMEM((rows, embed), F32),
                pltpu.VMEM((rows, embed + packed - LANES), BF16),
            ],
        ),
        out_shape=[
            jax.ShapeDtypeStruct((rows, embed), BF16),
            jax.ShapeDtypeStruct((1, embed), F32),
            jax.ShapeDtypeStruct((embed // 2, packed), BF16),
            jax.ShapeDtypeStruct((embed // 2, packed), F32),
        ],
        compiler_params=params(16, ("arbitrary",)),
        cost_estimate=pl.CostEstimate(
            flops=2 * rows * depth * embed, bytes_accessed=2 * depth * embed, transcendentals=0
        ),
        name="project",
    )(me, features, weight)


def split(value):
    high = value.astype(BF16)
    return high, (value - high.astype(F32)).astype(BF16)


def make_whiten_kernel(rows):
    def kernel(
        place_ref, totals_ref, packed_ref, whitener_ref, mean_ref, scaled, rest, first, left, right
    ):
        place = place_ref[0]
        embed = scaled.shape[0]
        blocks = embed // LANES
        half = blocks // 2
        depth = packed_ref.shape[1]
        per_block = LANES // depth
        total_rows = rows * totals_ref.shape[0]
        tile = 256
        tiles = embed // tile

        mean = jnp.sum(totals_ref[...], axis=0, keepdims=True) * (1.0 / total_rows)
        mean_ref[...] = mean
        shift_high, shift_low = split(totals_ref[...] * (1.0 / rows) - mean)
        shift_left = jnp.concatenate([shift_high, shift_high, shift_low], axis=0)
        shift_right = jnp.concatenate([shift_high, shift_low, shift_high], axis=0)

        for i in range(blocks):
            for part in range(per_block):
                piece = (i * per_block + part) ^ place
                wide = packed_ref[piece].astype(F32)
                lines = pl.ds(i * LANES + part * depth, depth)
                for k in range(half + 1):
                    if k == half and i >= half:
                        continue
                    j = (i + k) % blocks
                    scaled[lines, j * LANES : (j + 1) * LANES] = wide[
                        :, k * LANES : (k + 1) * LANES
                    ]
        for i in range(blocks):
            for k in range(1, half + 1):
                if k == half and i >= half:
                    continue
                j = (i + k) % blocks
                scaled[j * LANES : (j + 1) * LANES, i * LANES : (i + 1) * LANES] = scaled[
                    i * LANES : (i + 1) * LANES, j * LANES : (j + 1) * LANES
                ].T
        squares = jnp.zeros((1, embed), F32)
        for t in range(tiles):
            lines = slice(t * tile, (t + 1) * tile)
            between = dot(shift_left[:, lines], shift_right, (0, 0))
            covariance = (scaled[lines, :] + rows * between) * (1.0 / total_rows)
            scaled[lines, :] = covariance
            first[lines, :] = covariance.astype(BF16)
            squares = squares + jnp.sum(covariance * covariance, axis=0, keepdims=True)
        frobenius = jnp.sqrt(jnp.sum(squares, axis=1, keepdims=True))
        inverse = 1.0 / frobenius
        root = lax.rsqrt(frobenius)

        def product(one, two, finish):
            @pl.loop(0, tiles)
            def _(t):
                lines = pl.ds(pl.multiple_of(t * tile, tile), tile)
                finish(lines, dot(one[lines, :], two[...]))

        def second(lines, value):
            value = value * (inverse * inverse)
            own = scaled[lines, :] * inverse
            scaled[lines, :] = own
            rest[lines, :] = 27.0 * value - 39.0 * own
            left[lines, :] = value.astype(BF16)
            right[lines, :] = (value - 9.0 * own).astype(BF16)

        product(first, first, second)

        def fourth(lines, value):
            value = (value + rest[lines, :]) * (1.0 / 16.0)
            rest[lines, :] = value
            whitener_ref[lines, :] = value.astype(BF16)

        product(left, right, fourth)

        def moved(lines, value):
            value = value * inverse
            scaled[lines, :] = 2.25 * 2.25 * scaled[lines, :] + 4.5 * value
            right[lines, :] = value.astype(BF16)

        product(first, whitener_ref, moved)

        def quad(lines, value):
            value = value + scaled[lines, :]
            rest[lines, :] = 3.0 * rest[lines, :] - 2.25 * value
            left[lines, :] = value.astype(BF16)

        product(whitener_ref, right, quad)
        first[...] = whitener_ref[...]

        def last(lines, value):
            at = lax.broadcasted_iota(jnp.int32, value.shape, 0) + lines.start
            eye = at == lax.broadcasted_iota(jnp.int32, value.shape, 1)
            value = 0.5 * (rest[lines, :] - value)
            value = value + jnp.where(eye, 0.5 * 3.0 * 2.25, 0.0)
            whitener_ref[lines, :] = (value * root).astype(BF16)

        product(first, left, last)

    return kernel


def whiten(place, totals, packed, rows):
    embed = totals.shape[1]
    square = (embed, embed)
    return pl.pallas_call(
        make_whiten_kernel(rows),
        in_specs=[smem(), vmem(), vmem()],
        out_specs=[vmem(), vmem()],
        out_shape=[
            jax.ShapeDtypeStruct(square, BF16),
            jax.ShapeDtypeStruct((1, embed), F32),
        ],
        scratch_shapes=[pltpu.VMEM(square, F32)] * 2 + [pltpu.VMEM(square, BF16)] * 3,
        compiler_params=params(24),
        cost_estimate=pl.CostEstimate(
            flops=5 * 2 * embed**3, bytes_accessed=2 * embed**2, transcendentals=0
        ),
        name="whiten",
    )(place, totals, packed)


def contrast_kernel(
    group_ref, offsets_ref, projected_ref, mean_ref, whitener_ref, ortholog_ref, loss_ref, grad_ref, white
):
    groups, rows, embed = projected_ref.shape
    group = group_ref[0]

    @pl.loop(0, groups)
    def _(g):
        centered = (projected_ref[g].astype(F32) - mean_ref[...]).astype(BF16)
        white[g] = dot(centered, whitener_ref[...]).astype(BF16)

    places = lax.broadcasted_iota(jnp.int32, (rows, rows), 0)

    @pl.loop(0, groups)
    def _(step):
        g = step ^ group
        own = white[g]
        loss = jnp.zeros((1, rows), F32)
        grad = jnp.zeros((rows, embed), F32)
        for k in range(PARTNERS):
            other = white[(g + offsets_ref[step, k]) % groups]
            logits = dot(other, own, (1, 1)) * LOGIT_SCALE
            peak = jnp.max(logits, axis=0, keepdims=True)
            powers = jnp.exp(logits - peak)
            sums = jnp.sum(powers, axis=0, keepdims=True)
            hit = places == ortholog_ref[step, k : k + 1, :]
            picked = jnp.sum(jnp.where(hit, logits, 0.0), axis=0, keepdims=True)
            loss = loss + (peak + jnp.log(sums) - picked)
            weights = (powers * (1.0 / sums) - hit.astype(F32)) * (1.0 / PARTNERS)
            grad = grad + dot(weights.astype(BF16), other, (0, 0))
        grad_ref[step] = (grad * LOGIT_SCALE).astype(BF16)

        @pl.when(step == 0)
        def _():
            loss_ref[...] = loss * (1.0 / PARTNERS)


def contrast(group, offsets, projected, mean, whitener, ortholog):
    groups, rows, embed = projected.shape
    return pl.pallas_call(
        contrast_kernel,
        in_specs=[smem(), smem()] + [vmem()] * 4,
        out_specs=[vmem()] * 2,
        out_shape=[
            jax.ShapeDtypeStruct((1, rows), F32),
            jax.ShapeDtypeStruct((groups, rows, embed), BF16),
        ],
        scratch_shapes=[pltpu.VMEM((groups, rows, embed), BF16)],
        compiler_params=params(12 + 6 * groups * rows * embed // 2**20),
        cost_estimate=pl.CostEstimate(
            flops=groups * rows * 2 * embed * (embed + 2 * PARTNERS * rows),
            bytes_accessed=4 * groups * rows * embed,
            transcendentals=groups * PARTNERS * rows * rows,
        ),
        name="contrast",
    )(group, offsets, projected, mean, whitener, ortholog)


def gather_kernel(window_ref, grad_ref, *refs):
    groups = grad_ref.shape[0]
    feature_refs = refs[:groups]
    outs, total = refs[groups:-1], refs[-1]
    share = outs[0].shape[0]
    window = window_ref[0]

    def columns(at):
        value = dot(feature_refs[0][:, at], grad_ref[0], (0, 0))
        for k in range(1, groups):
            value = value + dot(feature_refs[k][:, at], grad_ref[k], (0, 0))
        return value

    if share % LANES:
        total[...] = columns(slice(None))
    for r, out in enumerate(outs):
        at = pl.ds(pl.multiple_of((window ^ r) * share, share), share)
        value = total[at, :] if share % LANES else columns(at)
        out[...] = value.astype(out.dtype)


def weight_pieces(window, grad, feature_slices, shares):
    groups, rows, embed = grad.shape
    columns = feature_slices[0].shape[1]
    share = columns // shares
    return pl.pallas_call(
        gather_kernel,
        in_specs=[smem()] + [vmem()] * (1 + groups),
        out_specs=[vmem()] * shares,
        out_shape=[
            jax.ShapeDtypeStruct((share, embed), BF16 if r else F32) for r in range(shares)
        ],
        scratch_shapes=[pltpu.VMEM((columns if share % LANES else 8, embed), F32)],
        compiler_params=params(24),
        cost_estimate=pl.CostEstimate(
            flops=groups * rows * 2 * embed * columns,
            bytes_accessed=2 * groups * rows * (embed + columns),
            transcendentals=0,
        ),
        name="weight_pieces",
    )(window, grad, *feature_slices)


def finish_kernel(*refs):
    keep_ref, whitener_ref, out_ref = refs[0], refs[-2], refs[-1]
    value = keep_ref[...]
    for ref in refs[1:-2]:
        value = value + ref[...].astype(F32)
    high, low = split(value)
    out_ref[...] = dot(high, whitener_ref[...], (1, 1)) + dot(low, whitener_ref[...], (1, 1))


def finish(pieces, whitener):
    return pl.pallas_call(
        finish_kernel,
        in_specs=[vmem()] * (len(pieces) + 1),
        out_specs=vmem(),
        out_shape=jax.ShapeDtypeStruct(pieces[0].shape, F32),
        compiler_params=params(12),
        name="finish",
    )(*pieces, whitener)


def shards(features, proj_weight, partner_offsets, ortholog_index):
    rows, depth = features.shape
    embed = proj_weight.shape[1]
    groups = lax.axis_size("sp")
    shares = lax.axis_size("win")
    devices = groups * shares
    group = lax.axis_index("sp")
    me = (group * shares + lax.axis_index("win")).astype(jnp.int32)
    me_scalar = me.reshape(1)

    table = jnp.concatenate(
        [ortholog_index.T, jnp.pad(partner_offsets.T, ((0, 0), (0, LANES - 1)))], axis=1
    )
    table = jnp.stack([table] + [xor_permute(table, k * shares) for k in range(1, groups)])
    ortholog = table[:, :, :rows]
    offsets = table[:, :, rows]

    projected, total, send, keep = project(me_scalar, features, proj_weight)
    projected_all = lax.all_gather(projected, "sp")

    packed = keep.shape[1]
    totals = total
    part = keep + xor_permute(send, 1).astype(F32)
    totals = jnp.concatenate([totals, xor_permute(totals, 1)], axis=0)
    stages = []
    low = 1
    place = me & 1
    while part.shape[0] > 32:
        bits = 2
        count = 1 << bits
        stages.append((low, count))
        pieces = part.reshape(count, part.shape[0] // count, packed)
        own = (me >> low) & (count - 1)
        part = lax.dynamic_index_in_dim(pieces, own, 0, keepdims=False)
        for r in range(1, count):
            sent = lax.dynamic_index_in_dim(pieces, own ^ r, 0, keepdims=False).astype(BF16)
            part = part + xor_permute(sent, r << low).astype(F32)
        totals = jnp.concatenate(
            [totals] + [xor_permute(totals, r << low) for r in range(1, count)], axis=0
        )
        place = place * count + own
        low += bits
    extra = devices >> low
    mine = part
    for r in range(1, extra):
        part = part + xor_permute(mine.astype(BF16), r << low).astype(F32)
    totals = jnp.concatenate(
        [totals] + [xor_permute(totals, r << low) for r in range(1, extra)], axis=0
    )
    part = part.astype(BF16)
    depth_piece = part.shape[0]
    for low, count in reversed(stages):
        part = jnp.concatenate(
            [part] + [xor_permute(part, r << low) for r in range(1, count)], axis=0
        )
    part = jnp.concatenate([part, xor_permute(part, 1)], axis=0)
    part = part.reshape(embed // depth_piece, depth_piece, packed)

    columns = depth // groups
    slices = [
        lax.dynamic_slice_in_dim(features, (group ^ k) * columns, columns, 1) for k in range(groups)
    ]
    part, *slices = lax.optimization_barrier((part, *slices))
    for k in range(1, groups):
        slices[k] = xor_permute(slices[k], k * shares)

    whitener, mean = whiten(place.reshape(1), totals, part, rows)
    loss, grad = contrast(group.reshape(1), offsets, projected_all, mean, whitener, ortholog)
    window = lax.axis_index("win").reshape(1)
    pieces = weight_pieces(window, grad, slices, shares)
    pieces = [pieces[0]] + [xor_permute(pieces[r], r) for r in range(1, shares)]
    return loss[0], finish(pieces, whitener)


def solution(mesh):
    return jax.shard_map(
        shards,
        mesh=mesh,
        in_specs=(P(("sp", "win"), None), P(), P("sp", None), P(("sp", "win"), None)),
        out_specs=(P(("sp", "win")), P(("sp", "win"), None)),
        check_vma=False,
    )
```

time: 275 us -> 183 us (0.67)
  blocking collectives: 91.8 us -> 0 us
  Pallas kernels: 90.8 us -> 53.8 us
  starting transfers between devices: 29.6 us -> 57.2 us
  waiting for transfers between devices: 25.5 us -> 38.5 us
  matrix products: 3.5 us -> 0 us
    all_gather x2 -> x0, blocking collectives: 91.8 us -> none  [the longest x1 61.1 us: shards(): totals = lax.all_gather(total[0], AXES)]
    pallas_call x1, Pallas kernels: 44.9 us -> 16.5 us  [whiten(): pl.pallas_call(make_whiten_kernel(rows), in_specs=[smem(), vmem(), vmem()...]
    ppermute x24 -> x38, starting transfers between devices: 29.6 us -> 57.2 us  [xor_permute(): return lax.ppermute(piece, AXES, [(i, i ^ mask) for i in range(devices)])]
    ppermute x24 -> x38, waiting for transfers between devices: 25.5 us -> 38.5 us  [xor_permute(): return lax.ppermute(piece, AXES, [(i, i ^ mask) for i in range(devices)])]
    pallas_call x1, Pallas kernels: 12.4 us -> 4.82 us  [project(): pl.pallas_call(project_kernel, grid_spec=pltpu.PrefetchScalarGridSpec(num...]
    unnamed x35 -> x34, local copies, waits for them, and re-layouts: 10.9 us -> 14.5 us
    dot_general x2 -> x0, matrix products: 3.5 us -> none  [dot(): lax.dot_general(a, b, (((contract[0],), (contract[1],)), ((), ())), preci...]
    pallas_call x1 -> x3, Pallas kernels: 33.4 us -> 32.4 us  [the longest x1 26.7 us: contrast(): pl.pallas_call(contrast_kernel, in_specs=[smem(), smem()] + [vmem()] * 4,...]
  transfers between devices with their start and end apart: 25 -> 39, of which waited for: 10 -> 16; matrix products, arithmetic and copies ran while one was open for 6% -> 4% of each run, Pallas kernels for 16% -> 24%
where the time goes in v2:
time: 183 us
  starting transfers between devices  57.2 us (31%)
  Pallas kernels  53.8 us (29%)
  waiting for transfers between devices  38.5 us (21%)
  local copies, waits for them, and re-layouts  17.2 us (9%)
  between operations  14.3 us (8%)
  other arithmetic  1.96 us (1%)
    ppermute x38, starting transfers between devices, xor_permute(): return lax.ppermute(piece, AXES, [(i, i ^ mask) for i in range(devices)])  57.2 us
    ppermute x38, waiting for transfers between devices, xor_permute(): return lax.ppermute(piece, AXES, [(i, i ^ mask) for i in range(devices)])  38.5 us
    pallas_call x1, Pallas kernels, contrast(): pl.pallas_call(contrast_kernel, in_specs=[smem(), smem()] + [vmem()] * 4,...  26.7 us
    pallas_call x1, Pallas kernels, whiten(): pl.pallas_call(make_whiten_kernel(rows), in_specs=[smem(), vmem(), vmem()...  16.5 us
    unnamed x34, local copies, waits for them, and re-layouts  14.5 us
    pallas_call x1, Pallas kernels, project(): pl.pallas_call(project_kernel, grid_spec=pltpu.PrefetchScalarGridSpec(num...  4.82 us
  transfers between devices with their start and end apart: 39, of which 16 were waited for; matrix products, arithmetic and copies ran while one was open for 4% of the time, Pallas kernels for 24%

profile of v2, /device:TPU:0, one launch (start us, length us, event | category | flops | bytes accessed | tf_op | source)
XLA Modules:
  0.0 182.9 jit_solution(7637607006456984146)
XLA Ops:
  7.2 3.4 %copy-done = bf16[4096,1024]{1,0:T(8,128)(2,1)S(1)} copy-done((bf16[4096,1024]{1,0:T(8,128)(2,1)S(1)}, bf16[4096,1024]{1,0:T(8,128)(2,1)}, u32[]{:S(2)}) %copy-start) | copy-done | bytes 8388632
  10.6 1.6 copy-done.1
  12.2 4.8 %project.1 = (bf16[256,1024]{1,0:T(8,128)(2,1)S(1)}, f32[1,1024]{1,0:T(1,128)S(1)}, bf16[512,640]{1,0:T(8,128)(2,1)S(1)}, f32[512,640]{1,0:T(8,128)S(1)}) custom-call(s32[1]{0:T(128)} %bitcast.12.me_ref, bf16[256,4096]{1,0:T(8,128)(2,1)S(1)} %copy-done.1, bf16[4096,1024]{1,0:T(8,128)(2,1)S(1)} %copy-done), custom_call_target="tpu_custom_call" | custom-call | flops 2147483648 | bytes 8388608 | tf_op jit(solution)/shard_map/project/pallas_call | solution.py:91
  17.0 0.8 copy-done.3
  17.8 0.9 copy-done.8
  18.8 5.1 %collective-permute-start.5 = (s32[4,384]{1,0:T(4,128)S(1)}, s32[4,384]{1,0:T(4,128)S(1)}, u32[]{:S(2)}, u32[]{:S(2)}) collective-permute-start(s32[4,384]{1,0:T(4,128)S(1)} %pad_add_fusion), channel_id=1, source_target_pairs={{0,24},{1,25},{2,26},{3,27},{4,28},{5,29},{6,30},{7,31},{8,16},{9,... | collective-permute-start | bytes 18440 | tf_op jit(solution)/shard_map/ppermute | solution.py:43
  24.3 1.2 collective-permute-start.2
  25.5 0.5 collective-permute-start.14
  26.0 1.4 constant_dynamic-slice_fusion
  27.4 1.7 collective-permute-start
  29.1 2.0 %collective-permute-done = s32[4,384]{1,0:T(4,128)S(1)} collective-permute-done((s32[4,384]{1,0:T(4,128)S(1)}, s32[4,384]{1,0:T(4,128)S(1)}, u32[]{:S(2)}, u32[]{:S(2)}) %collective-permute-start) | collective-permute-done | bytes 6176 | tf_op jit(solution)/shard_map/ppermute | solution.py:43
  31.1 1.4 collective-permute-start.1
  32.5 2.4 %collective-permute-done.1 = s32[4,384]{1,0:T(4,128)S(1)} collective-permute-done((s32[4,384]{1,0:T(4,128)S(1)}, s32[4,384]{1,0:T(4,128)S(1)}, u32[]{:S(2)}, u32[]{:S(2)}) %collective-permute-start.1) | collective-permute-done | bytes 6176 | tf_op jit(solution)/shard_map/ppermute | solution.py:43
  34.9 1.2 convert_add_fusion
  36.2 1.6 collective-permute-start.15
  37.8 1.4 collective-permute-start.17
  39.2 0.5 collective-permute-start.16
  39.8 2.8 %collective-permute-done.15 = bf16[128,640]{1,0:T(8,128)(2,1)S(1)} collective-permute-done((bf16[128,640]{1,0:T(8,128)(2,1)S(1)}, bf16[128,640]{1,0:T(8,128)(2,1)S(1)}, u32[]{:S(2)}, u32[]{:S(2)}) %collective-permute-start.15) | collective-permute-done | bytes 163872 | tf_op jit(solution)/shard_map/ppermute | solution.py:43
  42.6 2.8 %collective-permute-start.3 = (s32[4,384]{1,0:T(4,128)S(1)}, s32[4,384]{1,0:T(4,128)S(1)}, u32[]{:S(2)}, u32[]{:S(2)}) collective-permute-start(s32[4,384]{1,0:T(4,128)S(1)} %pad_add_fusion), channel_id=1, source_target_pairs={{0,16},{1,17},{2,18},{3,19},{4,20},{5,21},{6,22},{7,23},{8,24},{9,... | collective-permute-start | bytes 18440 | tf_op jit(solution)/shard_map/ppermute | solution.py:43
  45.6 1.8 %collective-permute-start.18 = (bf16[32,640]{1,0:T(8,128)(2,1)S(1)}, bf16[32,640]{1,0:T(8,128)(2,1)S(1)}, u32[]{:S(2)}, u32[]{:S(2)}) collective-permute-start(bf16[32,640]{1,0:T(8,128)(2,1)S(1)} %get-tuple-element.57), channel_id=1, source_target_pairs={{0,8},{1,9},{2,10},{3,11},{4,12},{5,13},{6,14},{7,15},{8,0},{9,1},... | collective-permute-start | bytes 122888 | tf_op jit(solution)/shard_map/ppermute | solution.py:43
  47.4 1.8 collective-permute-start.20
  49.2 0.9 collective-permute-start.19
  50.5 3.4 %collective-permute-done.20 = bf16[32,640]{1,0:T(8,128)(2,1)S(1)} collective-permute-done((bf16[32,640]{1,0:T(8,128)(2,1)S(1)}, bf16[32,640]{1,0:T(8,128)(2,1)S(1)}, u32[]{:S(2)}, u32[]{:S(2)}) %collective-permute-start.20) | collective-permute-done | bytes 40992 | tf_op jit(solution)/shard_map/ppermute | solution.py:43
  53.8 0.9 collective-permute-done.19
  54.7 0.7 constant_dynamic-update-slice_fusion.14
  55.3 2.8 %collective-permute-start.23 = (bf16[32,640]{1,0:T(8,128)(2,1)S(1)}, bf16[32,640]{1,0:T(8,128)(2,1)S(1)}, u32[]{:S(2)}, u32[]{:S(2)}) collective-permute-start(bf16[32,640]{1,0:T(8,128)(2,1)S(1)} %get-tuple-element.45), channel_id=1, source_target_pairs={{0,24},{1,25},{2,26},{3,27},{4,28},{5,29},{6,30},{7,31},{8,16},{9,... | collective-permute-start | bytes 122888 | tf_op jit(solution)/shard_map/ppermute | solution.py:43
  58.1 1.6 collective-permute-start.21
  59.7 1.6 collective-permute-done.23
  61.3 4.7 %collective-permute-start.6 = (s32[4,384]{1,0:T(4,128)S(1)}, s32[4,384]{1,0:T(4,128)S(1)}, u32[]{:S(2)}, u32[]{:S(2)}) collective-permute-start(s32[4,384]{1,0:T(4,128)S(1)} %pad_add_fusion), channel_id=1, source_target_pairs={{0,28},{1,29},{2,30},{3,31},{4,24},{5,25},{6,26},{7,27},{8,20},{9,... | collective-permute-start | bytes 18440 | tf_op jit(solution)/shard_map/ppermute | solution.py:43
  66.4 1.8 %collective-permute-start.24 = (bf16[128,640]{1,0:T(8,128)(2,1)S(1)}, bf16[128,640]{1,0:T(8,128)(2,1)S(1)}, u32[]{:S(2)}, u32[]{:S(2)}) collective-permute-start(bf16[128,640]{1,0:T(8,128)(2,1)S(1)} %pad_maximum_fusion), channel_id=1, source_target_pairs={{0,2},{1,3},{2,0},{3,1},{4,6},{5,7},{6,4},{7,5},{8,10},{9,11},{10,... | collective-permute-start | bytes 491528 | tf_op jit(solution)/shard_map/ppermute | solution.py:43
  68.3 0.6 constant_dynamic-update-slice_fusion.13
  68.9 0.6 constant_dynamic-update-slice_fusion.12
  69.5 0.6 constant_dynamic-update-slice_fusion.11
  70.1 2.3 %collective-permute-done.24 = bf16[128,640]{1,0:T(8,128)(2,1)S(1)} collective-permute-done((bf16[128,640]{1,0:T(8,128)(2,1)S(1)}, bf16[128,640]{1,0:T(8,128)(2,1)S(1)}, u32[]{:S(2)}, u32[]{:S(2)}) %collective-permute-start.24) | collective-permute-done | bytes 163872 | tf_op jit(solution)/shard_map/ppermute | solution.py:43
  72.4 2.7 %collective-permute-start.26 = (bf16[128,640]{1,0:T(8,128)(2,1)S(1)}, bf16[128,640]{1,0:T(8,128)(2,1)S(1)}, u32[]{:S(2)}, u32[]{:S(2)}) collective-permute-start(bf16[128,640]{1,0:T(8,128)(2,1)S(1)} %pad_maximum_fusion), channel_id=1, source_target_pairs={{0,6},{1,7},{2,4},{3,5},{4,2},{5,3},{6,0},{7,1},{8,14},{9,15},{10,... | collective-permute-start | bytes 491528 | tf_op jit(solution)/shard_map/ppermute | solution.py:43
  75.1 0.7 constant_dynamic-update-slice_fusion.10
  75.8 0.5 collective-permute-done.25
  76.3 1.5 collective-permute-start.10
  77.8 0.7 constant_dynamic-update-slice_fusion.9
  78.5 4.1 %collective-permute-done.26 = bf16[128,640]{1,0:T(8,128)(2,1)S(1)} collective-permute-done((bf16[128,640]{1,0:T(8,128)(2,1)S(1)}, bf16[128,640]{1,0:T(8,128)(2,1)S(1)}, u32[]{:S(2)}, u32[]{:S(2)}) %collective-permute-start.26) | collective-permute-done | bytes 163872 | tf_op jit(solution)/shard_map/ppermute | solution.py:43
  82.6 1.3 collective-permute-start.9
  83.9 0.7 constant_dynamic-update-slice_fusion.8
  84.6 1.7 collective-permute-start.8
  86.3 1.9 %collective-permute-done.8 = f32[2,1024]{1,0:T(2,128)S(1)} collective-permute-done((f32[2,1024]{1,0:T(2,128)S(1)}, f32[2,1024]{1,0:T(2,128)S(1)}, u32[]{:S(2)}, u32[]{:S(2)}) %collective-permute-start.8) | collective-permute-done | bytes 8224 | tf_op jit(solution)/shard_map/ppermute | solution.py:43
  88.3 2.1 %collective-permute-start.13 = (f32[8,1024]{1,0:T(8,128)S(1)}, f32[8,1024]{1,0:T(8,128)S(1)}, u32[]{:S(2)}, u32[]{:S(2)}) collective-permute-start(f32[8,1024]{1,0:T(8,128)S(1)} %concatenate.27), channel_id=1, source_target_pairs={{0,24},{1,25},{2,26},{3,27},{4,28},{5,29},{6,30},{7,31},{8,16},{9,... | collective-permute-start | bytes 98312 | tf_op jit(solution)/shard_map/ppermute | solution.py:43
  90.4 2.4 %collective-permute-start.11 = (f32[8,1024]{1,0:T(8,128)S(1)}, f32[8,1024]{1,0:T(8,128)S(1)}, u32[]{:S(2)}, u32[]{:S(2)}) collective-permute-start(f32[8,1024]{1,0:T(8,128)S(1)} %concatenate.27), channel_id=1, source_target_pairs={{0,8},{1,9},{2,10},{3,11},{4,12},{5,13},{6,14},{7,15},{8,0},{9,1},... | collective-permute-start | bytes 98312 | tf_op jit(solution)/shard_map/ppermute | solution.py:43
  93.0 1.5 collective-permute-done.13
  94.5 2.6 %collective-permute-done.12 = f32[8,1024]{1,0:T(8,128)S(1)} collective-permute-done((f32[8,1024]{1,0:T(8,128)S(1)}, f32[8,1024]{1,0:T(8,128)S(1)}, u32[]{:S(2)}, u32[]{:S(2)}) %collective-permute-start.12) | collective-permute-done | bytes 32800 | tf_op jit(solution)/shard_map/ppermute | solution.py:43
  97.3 1.1 copy-done.5
  98.4 0.6 collective-permute-start.28
  99.4 2.5 %collective-permute-start.30 = (bf16[256,512]{1,0:T(8,128)(2,1)}, bf16[256,512]{1,0:T(8,128)(2,1)S(1)}, u32[]{:S(2)}, u32[]{:S(2)}) collective-permute-start(bf16[256,512]{1,0:T(8,128)(2,1)} %get-tuple-element.35), channel_id=1, source_target_pairs={{0,12},{1,13},{2,14},{3,15},{4,8},{5,9},{6,10},{7,11},{8,4},{9,5},... | collective-permute-start | bytes 786440 | tf_op jit(solution)/shard_map/ppermute | solution.py:43
  101.8 0.8 collective-permute-start.31
  102.7 2.2 %collective-permute-start.32 = (bf16[256,512]{1,0:T(8,128)(2,1)}, bf16[256,512]{1,0:T(8,128)(2,1)}, u32[]{:S(2)}, u32[]{:S(2)}) collective-permute-start(bf16[256,512]{1,0:T(8,128)(2,1)} %get-tuple-element.37), channel_id=1, source_target_pairs={{0,20},{1,21},{2,22},{3,23},{4,16},{5,17},{6,18},{7,19},{8,28},{9,... | collective-permute-start | bytes 786440 | tf_op jit(solution)/shard_map/ppermute | solution.py:43
  104.9 1.3 copy-done.6
  106.2 16.5 %whiten.1 = (bf16[1024,1024]{1,0:T(8,128)(2,1)S(1)}, f32[1,1024]{1,0:T(1,128)S(1)}) custom-call(s32[1]{0:T(128)} %bitcast.14.place_ref, f32[32,1024]{1,0:T(8,128)S(1)} %concatenate.28.totals_ref, bf16[32,32,640]{2,1,0:T(8,128)(2,1)S(1)} %bitcast.55), custom_call_target="tpu_custom_call" | custom-call | flops 10737418240 | bytes 2097152 | tf_op jit(solution)/shard_map/whiten/pallas_call | solution.py:235
  122.7 2.2 %collective-permute-start.33 = (bf16[256,512]{1,0:T(8,128)(2,1)}, bf16[256,512]{1,0:T(8,128)(2,1)}, u32[]{:S(2)}, u32[]{:S(2)}) collective-permute-start(bf16[256,512]{1,0:T(8,128)(2,1)} %get-tuple-element.38), channel_id=1, source_target_pairs={{0,24},{1,25},{2,26},{3,27},{4,28},{5,29},{6,30},{7,31},{8,16},{9,... | collective-permute-start | bytes 786440 | tf_op jit(solution)/shard_map/ppermute | solution.py:43
  125.0 2.5 %collective-permute-start.34 = (bf16[256,512]{1,0:T(8,128)(2,1)}, bf16[256,512]{1,0:T(8,128)(2,1)}, u32[]{:S(2)}, u32[]{:S(2)}) collective-permute-start(bf16[256,512]{1,0:T(8,128)(2,1)} %get-tuple-element.39), channel_id=1, source_target_pairs={{0,28},{1,29},{2,30},{3,31},{4,24},{5,25},{6,26},{7,27},{8,20},{9,... | collective-permute-start | bytes 786440 | tf_op jit(solution)/shard_map/ppermute | solution.py:43
  127.4 2.2 %copy-done.7 = bf16[2048,1024]{1,0:T(8,128)(2,1)S(1)} copy-done((bf16[2048,1024]{1,0:T(8,128)(2,1)S(1)}, bf16[2048,1024]{1,0:T(8,128)(2,1)}, u32[]{:S(2)}) %copy-start.7) | copy-done | bytes 4194328
  129.6 26.7 %contrast.1 = (f32[1,256]{1,0:T(1,128)}, bf16[8,256,1024]{2,1,0:T(8,128)(2,1)S(1)}) custom-call(s32[1]{0:T(128)} %bitcast.group_ref, s32[8,4]{1,0:T(8,128)S(1)} %copy.8.offsets_ref, bf16[8,256,1024]{2,1,0:T(8,128)(2,1)S(1)} %bitcast.56, f32[1,1024]{1,0:T(1,128)S(1)} %get-tuple-element.28.mean_ref, ...), custom_call_target="tpu_custom_call" | custom-call | flops 12884901888 | bytes 8388608 | tf_op jit(solution)/shard_map/contrast/pallas_call | solution.py:291
  156.3 3.5 %weight_pieces.1 = (f32[128,1024]{1,0:T(8,128)S(1)}, bf16[128,1024]{1,0:T(8,128)(2,1)S(1)}, bf16[128,1024]{1,0:T(8,128)(2,1)S(1)}, bf16[128,1024]{1,0:T(8,128)(2,1)S(1)}) custom-call(s32[1]{0:T(128)} %bitcast.27.window_ref, bf16[8,256,1024]{2,1,0:T(8,128)(2,1)S(1)} %get-tuple-element.31.grad_ref, bf16[256,512]{1,0:T(8,128)(2,1)S(1)} %copy-done.4, ...), custom_call_target="tpu_custom_call" | custom-call | flops 2147483648 | bytes 6291456 | tf_op jit(solution)/shard_map/weight_pieces/pallas_call | solution.py:335
  159.9 1.6 collective-permute-start.36
  161.8 7.3 %collective-permute-done.36.refs_2_ = bf16[128,1024]{1,0:T(8,128)(2,1)S(1)} collective-permute-done((bf16[128,1024]{1,0:T(8,128)(2,1)S(1)}, bf16[128,1024]{1,0:T(8,128)(2,1)S(1)}, u32[]{:S(2)}, u32[]{:S(2)}) %collective-permute-start.36) | collective-permute-done | bytes 262176 | tf_op jit(solution)/shard_map/ppermute | solution.py:43
  169.1 4.7 %collective-permute-done.37.refs_3_ = bf16[128,1024]{1,0:T(8,128)(2,1)S(1)} collective-permute-done((bf16[128,1024]{1,0:T(8,128)(2,1)S(1)}, bf16[128,1024]{1,0:T(8,128)(2,1)S(1)}, u32[]{:S(2)}, u32[]{:S(2)}) %collective-permute-start.37) | collective-permute-done | bytes 262176 | tf_op jit(solution)/shard_map/ppermute | solution.py:43
  173.8 2.3 %finish.1 = f32[128,1024]{1,0:T(8,128)} custom-call(f32[128,1024]{1,0:T(8,128)S(1)} %get-tuple-element.40.refs_0_, bf16[128,1024]{1,0:T(8,128)(2,1)S(1)} %collective-permute-done.35.refs_1_, bf16[128,1024]{1,0:T(8,128)(2,1)S(1)} %collective-permute-done.36.refs_2_, bf16[128,1024]{1,0:T(8,128)(2,1)S(1)} %collective-permute-done.37.refs_3_, ...), custom_call_target="tpu_custom_call" | custom-call | tf_op jit(solution)/shard_map/finish/pallas_call | solution.py:363
  (74 shorter events, 2.8 us)
Async XLA Ops:
  7.2 120.3 %all-gather.3.cloned.1.call-start = ((), (), s32[]{:S(2)}) async-start(), calls=%async_computation | async-start | bytes 4718592 | tf_op jit(solution)/shard_map/all_gather | solution.py:391
  7.2 3.4 %copy-start = (bf16[4096,1024]{1,0:T(8,128)(2,1)S(1)}, bf16[4096,1024]{1,0:T(8,128)(2,1)}, u32[]{:S(2)}) copy-start(bf16[4096,1024]{1,0:T(8,128)(2,1)} %weight_ref.1) | copy-start | bytes 25165828
  10.6 1.6 copy-start.1
  12.2 6.5 %copy-start.10 = (s32[1,4]{1,0:T(1,128)S(1)}, s32[1,4]{1,0:T(1,128)}, u32[]{:S(2)}) copy-start(s32[1,4]{1,0:T(1,128)} %param.6) | copy-start | bytes 52
  12.2 6.6 %copy-start.9 = (s32[256,4]{0,1:T(4,128)S(1)}, s32[256,4]{0,1:T(4,128)}, u32[]{:S(2)}) copy-start(s32[256,4]{0,1:T(4,128)} %param.7) | copy-start | bytes 12292
  12.2 13.8 %copy-start.2 = (bf16[256,4096]{1,0:T(8,128)(2,1)S(1)}, bf16[256,4096]{1,0:T(8,128)(2,1)}, u32[]{:S(2)}) copy-start(bf16[256,4096]{1,0:T(8,128)(2,1)} %features_ref.1) | copy-start | bytes 6291460
  17.0 0.8 copy-start.3
  17.8 0.9 copy-start.8
  18.8 65.7 %collective-permute-start.5 = (s32[4,384]{1,0:T(4,128)S(1)}, s32[4,384]{1,0:T(4,128)S(1)}, u32[]{:S(2)}, u32[]{:S(2)}) collective-permute-start(s32[4,384]{1,0:T(4,128)S(1)} %pad_add_fusion), channel_id=1, source_target_pairs={{0,24},{1,25},{2,26},{3,27},{4,28},{5,29},{6,30},{7,31},{8,16},{9,... | collective-permute-start | bytes 18440 | tf_op jit(solution)/shard_map/ppermute | solution.py:43
  23.9 60.6 %collective-permute-start.4 = (s32[4,384]{1,0:T(4,128)S(1)}, s32[4,384]{1,0:T(4,128)S(1)}, u32[]{:S(2)}, u32[]{:S(2)}) collective-permute-start(s32[4,384]{1,0:T(4,128)S(1)} %pad_add_fusion), channel_id=1, source_target_pairs={{0,20},{1,21},{2,22},{3,23},{4,16},{5,17},{6,18},{7,19},{8,28},{9,... | collective-permute-start | bytes 18440 | tf_op jit(solution)/shard_map/ppermute | solution.py:43
  24.3 14.9 %collective-permute-start.2 = (s32[4,384]{1,0:T(4,128)S(1)}, s32[4,384]{1,0:T(4,128)S(1)}, u32[]{:S(2)}, u32[]{:S(2)}) collective-permute-start(s32[4,384]{1,0:T(4,128)S(1)} %pad_add_fusion), channel_id=1, source_target_pairs={{0,12},{1,13},{2,14},{3,15},{4,8},{5,9},{6,10},{7,11},{8,4},{9,5},... | collective-permute-start | bytes 18440 | tf_op jit(solution)/shard_map/ppermute | solution.py:43
  25.5 1.9 %collective-permute-start.7 = (f32[1,1024]{1,0:T(1,128)S(1)}, f32[1,1024]{1,0:T(1,128)S(1)}, u32[]{:S(2)}, u32[]{:S(2)}) collective-permute-start(f32[1,1024]{1,0:T(1,128)S(1)} %get-tuple-element.24), channel_id=1, source_target_pairs={{0,1},{1,0},{2,3},{3,2},{4,5},{5,4},{6,7},{7,6},{8,9},{9,8},{10,11... | collective-permute-start | bytes 12296 | tf_op jit(solution)/shard_map/ppermute | solution.py:43
  25.5 9.5 %collective-permute-start.14 = (bf16[512,640]{1,0:T(8,128)(2,1)}, bf16[512,640]{1,0:T(8,128)(2,1)}, u32[]{:S(2)}, u32[]{:S(2)}) collective-permute-start(bf16[512,640]{1,0:T(8,128)(2,1)} %copy-done.8), channel_id=1, source_target_pairs={{0,1},{1,0},{2,3},{3,2},{4,5},{5,4},{6,7},{7,6},{8,9},{9,8},{10,11... | collective-permute-start | bytes 1966088 | tf_op jit(solution)/shard_map/ppermute | solution.py:43
  27.4 3.7 %collective-permute-start = (s32[4,384]{1,0:T(4,128)S(1)}, s32[4,384]{1,0:T(4,128)S(1)}, u32[]{:S(2)}, u32[]{:S(2)}) collective-permute-start(s32[4,384]{1,0:T(4,128)S(1)} %pad_add_fusion), channel_id=1, source_target_pairs={{0,4},{1,5},{2,6},{3,7},{4,0},{5,1},{6,2},{7,3},{8,12},{9,13},{10,... | collective-permute-start | bytes 18440 | tf_op jit(solution)/shard_map/ppermute | solution.py:43
  31.1 3.8 %collective-permute-start.1 = (s32[4,384]{1,0:T(4,128)S(1)}, s32[4,384]{1,0:T(4,128)S(1)}, u32[]{:S(2)}, u32[]{:S(2)}) collective-permute-start(s32[4,384]{1,0:T(4,128)S(1)} %pad_add_fusion), channel_id=1, source_target_pairs={{0,8},{1,9},{2,10},{3,11},{4,12},{5,13},{6,14},{7,15},{8,0},{9,1},... | collective-permute-start | bytes 18440 | tf_op jit(solution)/shard_map/ppermute | solution.py:43
  36.2 6.4 %collective-permute-start.15 = (bf16[128,640]{1,0:T(8,128)(2,1)S(1)}, bf16[128,640]{1,0:T(8,128)(2,1)S(1)}, u32[]{:S(2)}, u32[]{:S(2)}) collective-permute-start(bf16[128,640]{1,0:T(8,128)(2,1)S(1)} %get-tuple-element.54), channel_id=1, source_target_pairs={{0,2},{1,3},{2,0},{3,1},{4,6},{5,7},{6,4},{7,5},{8,10},{9,11},{10,... | collective-permute-start | bytes 491528 | tf_op jit(solution)/shard_map/ppermute | solution.py:43
  37.8 7.6 %collective-permute-start.17 = (bf16[128,640]{1,0:T(8,128)(2,1)S(1)}, bf16[128,640]{1,0:T(8,128)(2,1)S(1)}, u32[]{:S(2)}, u32[]{:S(2)}) collective-permute-start(bf16[128,640]{1,0:T(8,128)(2,1)S(1)} %get-tuple-element.55), channel_id=1, source_target_pairs={{0,6},{1,7},{2,4},{3,5},{4,2},{5,3},{6,0},{7,1},{8,14},{9,15},{10,... | collective-permute-start | bytes 491528 | tf_op jit(solution)/shard_map/ppermute | solution.py:43
  39.2 6.2 %collective-permute-start.16 = (bf16[128,640]{1,0:T(8,128)(2,1)S(1)}, bf16[128,640]{1,0:T(8,128)(2,1)S(1)}, u32[]{:S(2)}, u32[]{:S(2)}) collective-permute-start(bf16[128,640]{1,0:T(8,128)(2,1)S(1)} %get-tuple-element.56), channel_id=1, source_target_pairs={{0,4},{1,5},{2,6},{3,7},{4,0},{5,1},{6,2},{7,3},{8,12},{9,13},{10,... | collective-permute-start | bytes 491528 | tf_op jit(solution)/shard_map/ppermute | solution.py:43
  42.6 6.6 %collective-permute-start.3 = (s32[4,384]{1,0:T(4,128)S(1)}, s32[4,384]{1,0:T(4,128)S(1)}, u32[]{:S(2)}, u32[]{:S(2)}) collective-permute-start(s32[4,384]{1,0:T(4,128)S(1)} %pad_add_fusion), channel_id=1, source_target_pairs={{0,16},{1,17},{2,18},{3,19},{4,20},{5,21},{6,22},{7,23},{8,24},{9,... | collective-permute-start | bytes 18440 | tf_op jit(solution)/shard_map/ppermute | solution.py:43
  45.6 4.9 %collective-permute-start.18 = (bf16[32,640]{1,0:T(8,128)(2,1)S(1)}, bf16[32,640]{1,0:T(8,128)(2,1)S(1)}, u32[]{:S(2)}, u32[]{:S(2)}) collective-permute-start(bf16[32,640]{1,0:T(8,128)(2,1)S(1)} %get-tuple-element.57), channel_id=1, source_target_pairs={{0,8},{1,9},{2,10},{3,11},{4,12},{5,13},{6,14},{7,15},{8,0},{9,1},... | collective-permute-start | bytes 122888 | tf_op jit(solution)/shard_map/ppermute | solution.py:43
  47.4 6.4 %collective-permute-start.20 = (bf16[32,640]{1,0:T(8,128)(2,1)S(1)}, bf16[32,640]{1,0:T(8,128)(2,1)S(1)}, u32[]{:S(2)}, u32[]{:S(2)}) collective-permute-start(bf16[32,640]{1,0:T(8,128)(2,1)S(1)} %get-tuple-element.58), channel_id=1, source_target_pairs={{0,24},{1,25},{2,26},{3,27},{4,28},{5,29},{6,30},{7,31},{8,16},{9,... | collective-permute-start | bytes 122888 | tf_op jit(solution)/shard_map/ppermute | solution.py:43
  49.2 5.5 %collective-permute-start.19 = (bf16[32,640]{1,0:T(8,128)(2,1)S(1)}, bf16[32,640]{1,0:T(8,128)(2,1)S(1)}, u32[]{:S(2)}, u32[]{:S(2)}) collective-permute-start(bf16[32,640]{1,0:T(8,128)(2,1)S(1)} %get-tuple-element.59), channel_id=1, source_target_pairs={{0,16},{1,17},{2,18},{3,19},{4,20},{5,21},{6,22},{7,23},{8,24},{9,... | collective-permute-start | bytes 122888 | tf_op jit(solution)/shard_map/ppermute | solution.py:43
  55.3 6.0 %collective-permute-start.23 = (bf16[32,640]{1,0:T(8,128)(2,1)S(1)}, bf16[32,640]{1,0:T(8,128)(2,1)S(1)}, u32[]{:S(2)}, u32[]{:S(2)}) collective-permute-start(bf16[32,640]{1,0:T(8,128)(2,1)S(1)} %get-tuple-element.45), channel_id=1, source_target_pairs={{0,24},{1,25},{2,26},{3,27},{4,28},{5,29},{6,30},{7,31},{8,16},{9,... | collective-permute-start | bytes 122888 | tf_op jit(solution)/shard_map/ppermute | solution.py:43
  58.1 8.0 %collective-permute-start.22 = (bf16[32,640]{1,0:T(8,128)(2,1)S(1)}, bf16[32,640]{1,0:T(8,128)(2,1)S(1)}, u32[]{:S(2)}, u32[]{:S(2)}) collective-permute-start(bf16[32,640]{1,0:T(8,128)(2,1)S(1)} %get-tuple-element.45), channel_id=1, source_target_pairs={{0,16},{1,17},{2,18},{3,19},{4,20},{5,21},{6,22},{7,23},{8,24},{9,... | collective-permute-start | bytes 122888 | tf_op jit(solution)/shard_map/ppermute | solution.py:43
  58.1 8.0 %collective-permute-start.21 = (bf16[32,640]{1,0:T(8,128)(2,1)S(1)}, bf16[32,640]{1,0:T(8,128)(2,1)S(1)}, u32[]{:S(2)}, u32[]{:S(2)}) collective-permute-start(bf16[32,640]{1,0:T(8,128)(2,1)S(1)} %get-tuple-element.45), channel_id=1, source_target_pairs={{0,8},{1,9},{2,10},{3,11},{4,12},{5,13},{6,14},{7,15},{8,0},{9,1},... | collective-permute-start | bytes 122888 | tf_op jit(solution)/shard_map/ppermute | solution.py:43
  61.3 31.5 %collective-permute-start.6 = (s32[4,384]{1,0:T(4,128)S(1)}, s32[4,384]{1,0:T(4,128)S(1)}, u32[]{:S(2)}, u32[]{:S(2)}) collective-permute-start(s32[4,384]{1,0:T(4,128)S(1)} %pad_add_fusion), channel_id=1, source_target_pairs={{0,28},{1,29},{2,30},{3,31},{4,24},{5,25},{6,26},{7,27},{8,20},{9,... | collective-permute-start | bytes 18440 | tf_op jit(solution)/shard_map/ppermute | solution.py:43
  66.1 10.3 %collective-permute-start.25 = (bf16[128,640]{1,0:T(8,128)(2,1)S(1)}, bf16[128,640]{1,0:T(8,128)(2,1)S(1)}, u32[]{:S(2)}, u32[]{:S(2)}) collective-permute-start(bf16[128,640]{1,0:T(8,128)(2,1)S(1)} %pad_maximum_fusion), channel_id=1, source_target_pairs={{0,4},{1,5},{2,6},{3,7},{4,0},{5,1},{6,2},{7,3},{8,12},{9,13},{10,... | collective-permute-start | bytes 491528 | tf_op jit(solution)/shard_map/ppermute | solution.py:43
  66.4 6.0 %collective-permute-start.24 = (bf16[128,640]{1,0:T(8,128)(2,1)S(1)}, bf16[128,640]{1,0:T(8,128)(2,1)S(1)}, u32[]{:S(2)}, u32[]{:S(2)}) collective-permute-start(bf16[128,640]{1,0:T(8,128)(2,1)S(1)} %pad_maximum_fusion), channel_id=1, source_target_pairs={{0,2},{1,3},{2,0},{3,1},{4,6},{5,7},{6,4},{7,5},{8,10},{9,11},{10,... | collective-permute-start | bytes 491528 | tf_op jit(solution)/shard_map/ppermute | solution.py:43
  72.4 10.2 %collective-permute-start.26 = (bf16[128,640]{1,0:T(8,128)(2,1)S(1)}, bf16[128,640]{1,0:T(8,128)(2,1)S(1)}, u32[]{:S(2)}, u32[]{:S(2)}) collective-permute-start(bf16[128,640]{1,0:T(8,128)(2,1)S(1)} %pad_maximum_fusion), channel_id=1, source_target_pairs={{0,6},{1,7},{2,4},{3,5},{4,2},{5,3},{6,0},{7,1},{8,14},{9,15},{10,... | collective-permute-start | bytes 491528 | tf_op jit(solution)/shard_map/ppermute | solution.py:43
  76.3 9.9 %collective-permute-start.10 = (f32[2,1024]{1,0:T(2,128)S(1)}, f32[2,1024]{1,0:T(2,128)S(1)}, u32[]{:S(2)}, u32[]{:S(2)}) collective-permute-start(f32[2,1024]{1,0:T(2,128)S(1)} %pad_maximum_fusion.1), channel_id=1, source_target_pairs={{0,6},{1,7},{2,4},{3,5},{4,2},{5,3},{6,0},{7,1},{8,14},{9,15},{10,... | collective-permute-start | bytes 24584 | tf_op jit(solution)/shard_map/ppermute | solution.py:43
  82.6 3.8 %collective-permute-start.9 = (f32[2,1024]{1,0:T(2,128)S(1)}, f32[2,1024]{1,0:T(2,128)S(1)}, u32[]{:S(2)}, u32[]{:S(2)}) collective-permute-start(f32[2,1024]{1,0:T(2,128)S(1)} %pad_maximum_fusion.1), channel_id=1, source_target_pairs={{0,4},{1,5},{2,6},{3,7},{4,0},{5,1},{6,2},{7,3},{8,12},{9,13},{10,... | collective-permute-start | bytes 24584 | tf_op jit(solution)/shard_map/ppermute | solution.py:43
  84.5 12.6 %collective-permute-start.27 = (bf16[512,640]{1,0:T(8,128)(2,1)}, bf16[512,640]{1,0:T(8,128)(2,1)S(1)}, u32[]{:S(2)}, u32[]{:S(2)}) collective-permute-start(bf16[512,640]{1,0:T(8,128)(2,1)} %get-tuple-element.60), channel_id=1, source_target_pairs={{0,1},{1,0},{2,3},{3,2},{4,5},{5,4},{6,7},{7,6},{8,9},{9,8},{10,11... | collective-permute-start | bytes 1966088 | tf_op jit(solution)/shard_map/ppermute | solution.py:43
  84.6 3.7 %collective-permute-start.8 = (f32[2,1024]{1,0:T(2,128)S(1)}, f32[2,1024]{1,0:T(2,128)S(1)}, u32[]{:S(2)}, u32[]{:S(2)}) collective-permute-start(f32[2,1024]{1,0:T(2,128)S(1)} %pad_maximum_fusion.1), channel_id=1, source_target_pairs={{0,2},{1,3},{2,0},{3,1},{4,6},{5,7},{6,4},{7,5},{8,10},{9,11},{10,... | collective-permute-start | bytes 24584 | tf_op jit(solution)/shard_map/ppermute | solution.py:43
  88.3 6.2 %collective-permute-start.13 = (f32[8,1024]{1,0:T(8,128)S(1)}, f32[8,1024]{1,0:T(8,128)S(1)}, u32[]{:S(2)}, u32[]{:S(2)}) collective-permute-start(f32[8,1024]{1,0:T(8,128)S(1)} %concatenate.27), channel_id=1, source_target_pairs={{0,24},{1,25},{2,26},{3,27},{4,28},{5,29},{6,30},{7,31},{8,16},{9,... | collective-permute-start | bytes 98312 | tf_op jit(solution)/shard_map/ppermute | solution.py:43
  90.4 6.7 %collective-permute-start.12 = (f32[8,1024]{1,0:T(8,128)S(1)}, f32[8,1024]{1,0:T(8,128)S(1)}, u32[]{:S(2)}, u32[]{:S(2)}) collective-permute-start(f32[8,1024]{1,0:T(8,128)S(1)} %concatenate.27), channel_id=1, source_target_pairs={{0,16},{1,17},{2,18},{3,19},{4,20},{5,21},{6,22},{7,23},{8,24},{9,... | collective-permute-start | bytes 98312 | tf_op jit(solution)/shard_map/ppermute | solution.py:43
  90.4 6.7 %collective-permute-start.11 = (f32[8,1024]{1,0:T(8,128)S(1)}, f32[8,1024]{1,0:T(8,128)S(1)}, u32[]{:S(2)}, u32[]{:S(2)}) collective-permute-start(f32[8,1024]{1,0:T(8,128)S(1)} %concatenate.27), channel_id=1, source_target_pairs={{0,8},{1,9},{2,10},{3,11},{4,12},{5,13},{6,14},{7,15},{8,0},{9,1},... | collective-permute-start | bytes 98312 | tf_op jit(solution)/shard_map/ppermute | solution.py:43
  97.2 1.1 copy-start.5
  98.4 24.4 %collective-permute-start.28 = (bf16[256,512]{1,0:T(8,128)(2,1)}, bf16[256,512]{1,0:T(8,128)(2,1)S(1)}, u32[]{:S(2)}, u32[]{:S(2)}) collective-permute-start(bf16[256,512]{1,0:T(8,128)(2,1)} %get-tuple-element.33), channel_id=1, source_target_pairs={{0,4},{1,5},{2,6},{3,7},{4,0},{5,1},{6,2},{7,3},{8,12},{9,13},{10,... | collective-permute-start | bytes 786440 | tf_op jit(solution)/shard_map/ppermute | solution.py:43
  99.0 26.0 %collective-permute-start.29 = (bf16[256,512]{1,0:T(8,128)(2,1)}, bf16[256,512]{1,0:T(8,128)(2,1)S(1)}, u32[]{:S(2)}, u32[]{:S(2)}) collective-permute-start(bf16[256,512]{1,0:T(8,128)(2,1)} %get-tuple-element.34), channel_id=1, source_target_pairs={{0,8},{1,9},{2,10},{3,11},{4,12},{5,13},{6,14},{7,15},{8,0},{9,1},... | collective-permute-start | bytes 786440 | tf_op jit(solution)/shard_map/ppermute | solution.py:43
  99.4 56.9 %collective-permute-start.30 = (bf16[256,512]{1,0:T(8,128)(2,1)}, bf16[256,512]{1,0:T(8,128)(2,1)S(1)}, u32[]{:S(2)}, u32[]{:S(2)}) collective-permute-start(bf16[256,512]{1,0:T(8,128)(2,1)} %get-tuple-element.35), channel_id=1, source_target_pairs={{0,12},{1,13},{2,14},{3,15},{4,8},{5,9},{6,10},{7,11},{8,4},{9,5},... | collective-permute-start | bytes 786440 | tf_op jit(solution)/shard_map/ppermute | solution.py:43
  101.8 54.4 %collective-permute-start.31 = (bf16[256,512]{1,0:T(8,128)(2,1)}, bf16[256,512]{1,0:T(8,128)(2,1)S(1)}, u32[]{:S(2)}, u32[]{:S(2)}) collective-permute-start(bf16[256,512]{1,0:T(8,128)(2,1)} %get-tuple-element.36), channel_id=1, source_target_pairs={{0,16},{1,17},{2,18},{3,19},{4,20},{5,21},{6,22},{7,23},{8,24},{9,... | collective-permute-start | bytes 786440 | tf_op jit(solution)/shard_map/ppermute | solution.py:43
  102.7 53.6 %collective-permute-start.32 = (bf16[256,512]{1,0:T(8,128)(2,1)}, bf16[256,512]{1,0:T(8,128)(2,1)}, u32[]{:S(2)}, u32[]{:S(2)}) collective-permute-start(bf16[256,512]{1,0:T(8,128)(2,1)} %get-tuple-element.37), channel_id=1, source_target_pairs={{0,20},{1,21},{2,22},{3,23},{4,16},{5,17},{6,18},{7,19},{8,28},{9,... | collective-permute-start | bytes 786440 | tf_op jit(solution)/shard_map/ppermute | solution.py:43
  104.8 1.3 copy-start.6
  122.7 33.6 %collective-permute-start.33 = (bf16[256,512]{1,0:T(8,128)(2,1)}, bf16[256,512]{1,0:T(8,128)(2,1)}, u32[]{:S(2)}, u32[]{:S(2)}) collective-permute-start(bf16[256,512]{1,0:T(8,128)(2,1)} %get-tuple-element.38), channel_id=1, source_target_pairs={{0,24},{1,25},{2,26},{3,27},{4,28},{5,29},{6,30},{7,31},{8,16},{9,... | collective-permute-start | bytes 786440 | tf_op jit(solution)/shard_map/ppermute | solution.py:43
  125.0 31.3 %collective-permute-start.34 = (bf16[256,512]{1,0:T(8,128)(2,1)}, bf16[256,512]{1,0:T(8,128)(2,1)}, u32[]{:S(2)}, u32[]{:S(2)}) collective-permute-start(bf16[256,512]{1,0:T(8,128)(2,1)} %get-tuple-element.39), channel_id=1, source_target_pairs={{0,28},{1,29},{2,30},{3,31},{4,24},{5,25},{6,26},{7,27},{8,20},{9,... | collective-permute-start | bytes 786440 | tf_op jit(solution)/shard_map/ppermute | solution.py:43
  127.4 2.2 %copy-start.7 = (bf16[2048,1024]{1,0:T(8,128)(2,1)S(1)}, bf16[2048,1024]{1,0:T(8,128)(2,1)}, u32[]{:S(2)}) copy-start(bf16[2048,1024]{1,0:T(8,128)(2,1)} %all-gather.3.cloned.1.call-done) | copy-start | bytes 12582916
  129.6 26.7 %copy-start.4 = (bf16[256,512]{1,0:T(8,128)(2,1)S(1)}, bf16[256,512]{1,0:T(8,128)(2,1)}, u32[]{:S(2)}) copy-start(bf16[256,512]{1,0:T(8,128)(2,1)} %get-tuple-element.32.refs_0_) | copy-start | bytes 786436
  159.8 1.9 %collective-permute-start.35 = (bf16[128,1024]{1,0:T(8,128)(2,1)S(1)}, bf16[128,1024]{1,0:T(8,128)(2,1)S(1)}, u32[]{:S(2)}, u32[]{:S(2)}) collective-permute-start(bf16[128,1024]{1,0:T(8,128)(2,1)S(1)} %get-tuple-element.41), channel_id=1, source_target_pairs={{0,1},{1,0},{2,3},{3,2},{4,5},{5,4},{6,7},{7,6},{8,9},{9,8},{10,11... | collective-permute-start | bytes 786440 | tf_op jit(solution)/shard_map/ppermute | solution.py:43
  159.9 9.2 %collective-permute-start.36 = (bf16[128,1024]{1,0:T(8,128)(2,1)S(1)}, bf16[128,1024]{1,0:T(8,128)(2,1)S(1)}, u32[]{:S(2)}, u32[]{:S(2)}) collective-permute-start(bf16[128,1024]{1,0:T(8,128)(2,1)S(1)} %get-tuple-element.42), channel_id=1, source_target_pairs={{0,2},{1,3},{2,0},{3,1},{4,6},{5,7},{6,4},{7,5},{8,10},{9,11},{10,... | collective-permute-start | bytes 786440 | tf_op jit(solution)/shard_map/ppermute | solution.py:43
  161.5 12.3 %collective-permute-start.37 = (bf16[128,1024]{1,0:T(8,128)(2,1)S(1)}, bf16[128,1024]{1,0:T(8,128)(2,1)S(1)}, u32[]{:S(2)}, u32[]{:S(2)}) collective-permute-start(bf16[128,1024]{1,0:T(8,128)(2,1)S(1)} %get-tuple-element.43), channel_id=1, source_target_pairs={{0,3},{1,2},{2,1},{3,0},{4,7},{5,6},{6,5},{7,4},{8,11},{9,10},{10,... | collective-permute-start | bytes 786440 | tf_op jit(solution)/shard_map/ppermute | solution.py:43
Sparse Core Ops, SparseCore 0:
  18.8 100.2 all-gather.2

commit v3 on v2

v3 whole, which is shorter than its diff:
```python
import jax
import jax.numpy as jnp
from jax import lax
from jax.experimental import pallas as pl
from jax.experimental.pallas import tpu as pltpu
from jax.sharding import PartitionSpec as P

PARTNERS = 4
LOGIT_SCALE = 0.125
AXES = ("sp", "win")
LANES = 128
TAIL = 16
F32 = jnp.float32
BF16 = jnp.bfloat16
HIGHEST = lax.Precision.HIGHEST


def dot(a, b, contract=(1, 0), precision=None):
    return lax.dot_general(
        a,
        b,
        (((contract[0],), (contract[1],)), ((), ())),
        precision=precision,
        preferred_element_type=F32,
    )


def params(mebibytes, semantics=None):
    return pltpu.CompilerParams(
        vmem_limit_bytes=mebibytes * 2**20, dimension_semantics=semantics
    )


def vmem():
    return pl.BlockSpec(memory_space=pltpu.VMEM)


def smem():
    return pl.BlockSpec(memory_space=pltpu.SMEM)


def xor_permute(piece, mask):
    devices = lax.axis_size(AXES)
    return lax.ppermute(piece, AXES, [(i, i ^ mask) for i in range(devices)])


def split(value):
    high = value.astype(BF16)
    return high, (value - high.astype(F32)).astype(BF16)


def pack_sums(sums, packed, rows):
    high = sums.astype(BF16).astype(F32)
    pad = jnp.zeros((sums.shape[0], 2 * packed - sums.shape[1]), F32)
    lines = []
    for half in (high, sums - high):
        lines += [half[:, :packed], jnp.concatenate([half[:, packed:], pad], axis=1)]
    if rows > 4 * sums.shape[0]:
        lines.append(jnp.zeros((rows - 4 * sums.shape[0], packed), F32))
    return jnp.concatenate(lines, axis=0).astype(BF16)


def unpack_sums(block, count, embed):
    wide = block.astype(F32)
    packed = wide.shape[1]
    low = 2 * count
    left = wide[0:count] + wide[low : low + count]
    right = wide[count:low] + wide[low + count : low + 2 * count]
    return jnp.concatenate([left, right[:, : embed - packed]], axis=1)


def project_kernel(
    me_ref,
    offsets_ref,
    features_ref,
    weight_ref,
    ortholog_ref,
    block_ref,
    slices_ref,
    send_ref,
    keep_ref,
    acc,
    wide,
):
    step = pl.program_id(0)
    rows, embed = acc.shape
    half, packed = keep_ref.shape
    blocks = embed // LANES

    @pl.when(step == 0)
    def _():
        acc[...] = jnp.zeros_like(acc)

    slices_ref[0] = features_ref[...]
    acc[...] += dot(features_ref[...], weight_ref[...])

    @pl.when(step == pl.num_programs(0) - 1)
    def _():
        projected = acc[...].astype(BF16)
        block_ref[0:rows, :] = projected
        line = lax.broadcasted_iota(jnp.int32, (TAIL, embed), 0)
        lane = lax.broadcasted_iota(jnp.int32, (TAIL, embed), 1)
        table = jnp.zeros((TAIL, embed), F32)
        for k in range(PARTNERS):
            table = jnp.where((line == 1) & (lane == k), offsets_ref[0, k].astype(F32), table)
        hits = jnp.concatenate(
            [ortholog_ref[k : k + 1, :].astype(F32) for k in range(PARTNERS)]
            + ([jnp.zeros((1, embed - PARTNERS * rows), F32)] if embed > PARTNERS * rows else []),
            axis=1,
        )
        block_ref[rows:, :] = jnp.where(line == 0, hits, table).astype(BF16)

        total = jnp.sum(projected.astype(F32), axis=0, keepdims=True)
        send_ref[half:, :] = pack_sums(total, packed, TAIL)
        wide[:, :embed] = projected
        wide[:, embed:] = projected[:, : packed - LANES]
        ones = jnp.ones((rows, LANES), BF16)
        acc[0:8, :] = jnp.broadcast_to(total * (1.0 / rows), (8, embed))
        core = me_ref[0] & 1
        for side, out in ((0, keep_ref), (1, send_ref)):
            for r in range(blocks // 2):
                block = (core ^ side) * (blocks // 2) + r
                start = pl.multiple_of(block * LANES, LANES)
                own = wide[:, pl.ds(start, LANES)]
                gram = dot(own, wide[:, pl.ds(start, packed)], (0, 0))
                sums = dot(own, ones, (0, 0))
                for k in range(packed // LANES):
                    other = pl.multiple_of((block + k) % blocks * LANES, LANES)
                    at = slice(k * LANES, (k + 1) * LANES)
                    value = gram[:, at] - sums * acc[0:1, pl.ds(other, LANES)]
                    out[r * LANES : (r + 1) * LANES, at] = value.astype(out.dtype)


def project(me, offsets, features, weight, ortholog, groups):
    rows, depth = features.shape
    embed = weight.shape[1]
    packed = embed // 2 + LANES
    tile = depth // groups
    fixed = lambda k, *_: (0, 0)
    return pl.pallas_call(
        project_kernel,
        grid_spec=pltpu.PrefetchScalarGridSpec(
            num_scalar_prefetch=2,
            grid=(groups,),
            in_specs=[
                pl.BlockSpec((rows, tile), lambda k, *_: (0, k)),
                pl.BlockSpec((tile, embed), lambda k, *_: (k, 0)),
                pl.BlockSpec((PARTNERS, rows), fixed),
            ],
            out_specs=[
                pl.BlockSpec((rows + TAIL, embed), fixed),
                pl.BlockSpec((1, rows, tile), lambda k, *_: (k, 0, 0)),
                pl.BlockSpec((embed // 2 + TAIL, packed), fixed),
                pl.BlockSpec((embed // 2, packed), fixed),
            ],
            scratch_shapes=[
                pltpu.VMEM((rows, embed), F32),
                pltpu.VMEM((rows, embed + packed - LANES), BF16),
            ],
        ),
        out_shape=[
            jax.ShapeDtypeStruct((rows + TAIL, embed), BF16),
            jax.ShapeDtypeStruct((groups, rows, tile), BF16),
            jax.ShapeDtypeStruct((embed // 2 + TAIL, packed), BF16),
            jax.ShapeDtypeStruct((embed // 2, packed), F32),
        ],
        compiler_params=params(40, ("arbitrary",)),
        cost_estimate=pl.CostEstimate(
            flops=2 * rows * depth * embed, bytes_accessed=2 * depth * embed, transcendentals=0
        ),
        name="project",
    )(me, offsets, features, weight, ortholog)


def make_stage_kernel(seen, arrivals, count, embed):
    def kernel(own_ref, keep_ref, sent_ref, *refs):
        arrived, next_keep, outs = refs[:arrivals], refs[arrivals], refs[arrivals + 1 :]
        full, packed = keep_ref.shape
        share = full // count
        own = own_ref[0]
        sums = [unpack_sums(ref[full:, :], seen, embed) for ref in (sent_ref, *arrived)]
        block = pack_sums(jnp.concatenate(sums, axis=0), packed, outs[0].shape[0] - share)
        for r in range(count):
            at = pl.ds(pl.multiple_of((own ^ r) * share, share), share)
            value = keep_ref[at, :]
            for ref in arrived:
                value = value + ref[at, :].astype(F32)
            if r == 0:
                next_keep[...] = value
            else:
                outs[r - 1][:share, :] = value.astype(BF16)
                outs[r - 1][share:, :] = block

    return kernel


def stage(own, keep, sent, arrived, seen, count, embed):
    full, packed = keep.shape
    share = full // count
    held = seen * (1 + len(arrived))
    tail = -(-4 * held // TAIL) * TAIL
    out = pl.pallas_call(
        make_stage_kernel(seen, len(arrived), count, embed),
        in_specs=[smem()] + [vmem()] * (2 + len(arrived)),
        out_specs=[vmem()] * count,
        out_shape=[jax.ShapeDtypeStruct((share, packed), F32)]
        + [jax.ShapeDtypeStruct((share + tail, packed), BF16)] * (count - 1),
        compiler_params=params(16),
        cost_estimate=pl.CostEstimate(
            flops=full * packed, bytes_accessed=4 * full * packed, transcendentals=0
        ),
        name="stage",
    )(own.reshape(1), keep, sent, *arrived)
    return out[0], out[1:], held


def make_whiten_kernel(rows):
    def kernel(
        place_ref,
        sums_ref,
        near_ref,
        far_ref,
        whitener_ref,
        mean_ref,
        scaled,
        rest,
        first,
        left,
        right,
    ):
        place = place_ref[0]
        embed = scaled.shape[0]
        blocks = embed // LANES
        half = blocks // 2
        pieces, depth = near_ref.shape[:2]
        per_block = LANES // depth
        count = sums_ref.shape[1] // 4
        totals = jnp.concatenate(
            [unpack_sums(sums_ref[k], count, embed) for k in range(sums_ref.shape[0])], axis=0
        )
        total_rows = rows * totals.shape[0]
        tile = 256
        tiles = embed // tile

        mean = jnp.sum(totals, axis=0, keepdims=True) * (1.0 / total_rows)
        mean_ref[...] = mean
        shift_high, shift_low = split(totals * (1.0 / rows) - mean)
        shift_left = jnp.concatenate([shift_high, shift_high, shift_low], axis=0)
        shift_right = jnp.concatenate([shift_high, shift_low, shift_high], axis=0)

        def unpack(source_ref, side):
            for i in range(side * half, (side + 1) * half):
                for part in range(per_block):
                    piece = ((i - side * half) * per_block + part) ^ (place & (pieces - 1))
                    wide = source_ref[piece].astype(F32)
                    lines = pl.ds(i * LANES + part * depth, depth)
                    for k in range(half + 1):
                        if k == half and side:
                            continue
                        j = (i + k) % blocks
                        scaled[lines, j * LANES : (j + 1) * LANES] = wide[
                            :, k * LANES : (k + 1) * LANES
                        ]

        for core in range(2):

            @pl.when(place // pieces == core)
            def _():
                unpack(near_ref, core)
                unpack(far_ref, 1 - core)

        for i in range(blocks):
            for k in range(1, half + 1):
                if k == half and i >= half:
                    continue
                j = (i + k) % blocks
                scaled[j * LANES : (j + 1) * LANES, i * LANES : (i + 1) * LANES] = scaled[
                    i * LANES : (i + 1) * LANES, j * LANES : (j + 1) * LANES
                ].T
        squares = jnp.zeros((1, embed), F32)
        for t in range(tiles):
            lines = slice(t * tile, (t + 1) * tile)
            between = dot(shift_left[:, lines], shift_right, (0, 0))
            covariance = (scaled[lines, :] + rows * between) * (1.0 / total_rows)
            scaled[lines, :] = covariance
            first[lines, :] = covariance.astype(BF16)
            squares = squares + jnp.sum(covariance * covariance, axis=0, keepdims=True)
        frobenius = jnp.sqrt(jnp.sum(squares, axis=1, keepdims=True))
        inverse = 1.0 / frobenius
        root = lax.rsqrt(frobenius)

        def product(one, two, finish):
            @pl.loop(0, tiles)
            def _(t):
                lines = pl.ds(pl.multiple_of(t * tile, tile), tile)
                finish(lines, dot(one[lines, :], two[...]))

        def second(lines, value):
            value = value * (inverse * inverse)
            own = scaled[lines, :] * inverse
            scaled[lines, :] = own
            rest[lines, :] = 27.0 * value - 39.0 * own
            left[lines, :] = value.astype(BF16)
            right[lines, :] = (value - 9.0 * own).astype(BF16)

        product(first, first, second)

        def fourth(lines, value):
            value = (value + rest[lines, :]) * (1.0 / 16.0)
            rest[lines, :] = value
            whitener_ref[lines, :] = value.astype(BF16)

        product(left, right, fourth)

        def moved(lines, value):
            value = value * inverse
            scaled[lines, :] = 2.25 * 2.25 * scaled[lines, :] + 4.5 * value
            right[lines, :] = value.astype(BF16)

        product(first, whitener_ref, moved)

        def quad(lines, value):
            value = value + scaled[lines, :]
            rest[lines, :] = 3.0 * rest[lines, :] - 2.25 * value
            left[lines, :] = value.astype(BF16)

        product(whitener_ref, right, quad)
        first[...] = whitener_ref[...]

        def last(lines, value):
            at = lax.broadcasted_iota(jnp.int32, value.shape, 0) + lines.start
            eye = at == lax.broadcasted_iota(jnp.int32, value.shape, 1)
            value = 0.5 * (rest[lines, :] - value)
            value = value + jnp.where(eye, 0.5 * 3.0 * 2.25, 0.0)
            whitener_ref[lines, :] = (value * root).astype(BF16)

        product(first, left, last)

    return kernel


def whiten(place, sums, near, far, rows, embed):
    square = (embed, embed)
    return pl.pallas_call(
        make_whiten_kernel(rows),
        in_specs=[smem()] + [vmem()] * 3,
        out_specs=[vmem(), vmem()],
        out_shape=[
            jax.ShapeDtypeStruct(square, BF16),
            jax.ShapeDtypeStruct((1, embed), F32),
        ],
        scratch_shapes=[pltpu.VMEM(square, F32)] * 2 + [pltpu.VMEM(square, BF16)] * 3,
        compiler_params=params(24),
        cost_estimate=pl.CostEstimate(
            flops=5 * 2 * embed**3, bytes_accessed=2 * embed**2, transcendentals=0
        ),
        name="whiten",
    )(place, sums, near, far)


def contrast_kernel(
    group_ref, offsets_ref, blocks_ref, mean_ref, whitener_ref, loss_ref, grad_ref, white
):
    groups, rows, embed = white.shape
    group = group_ref[0]

    @pl.loop(0, groups)
    def _(g):
        centered = (blocks_ref[g, 0:rows, :].astype(F32) - mean_ref[...]).astype(BF16)
        white[g] = dot(centered, whitener_ref[...]).astype(BF16)

    places = lax.broadcasted_iota(jnp.int32, (rows, rows), 0).astype(F32)

    @pl.loop(0, groups)
    def _(g):
        own = white[g]
        table = blocks_ref[g, rows:, :].astype(F32)
        loss = jnp.zeros((1, rows), F32)
        grad = jnp.zeros((rows, embed), F32)
        for k in range(PARTNERS):
            other = white[(g + offsets_ref[g, k]) % groups]
            logits = dot(other, own, (1, 1)) * LOGIT_SCALE
            peak = jnp.max(logits, axis=0, keepdims=True)
            powers = jnp.exp(logits - peak)
            sums = jnp.sum(powers, axis=0, keepdims=True)
            hit = places == table[0:1, k * rows : (k + 1) * rows]
            picked = jnp.sum(jnp.where(hit, logits, 0.0), axis=0, keepdims=True)
            loss = loss + (peak + jnp.log(sums) - picked)
            weights = (powers * (1.0 / sums) - hit.astype(F32)) * (1.0 / PARTNERS)
            grad = grad + dot(weights.astype(BF16), other, (0, 0))
        grad_ref[g] = (grad * LOGIT_SCALE).astype(BF16)

        @pl.when(g == group)
        def _():
            loss_ref[...] = loss * (1.0 / PARTNERS)


def contrast(group, offsets, blocks, mean, whitener):
    groups, rows, embed = blocks.shape
    rows -= TAIL
    return pl.pallas_call(
        contrast_kernel,
        in_specs=[smem(), smem()] + [vmem()] * 3,
        out_specs=[vmem()] * 2,
        out_shape=[
            jax.ShapeDtypeStruct((1, rows), F32),
            jax.ShapeDtypeStruct((groups, rows, embed), BF16),
        ],
        scratch_shapes=[pltpu.VMEM((groups, rows, embed), BF16)],
        compiler_params=params(12 + 6 * groups * rows * embed // 2**20),
        cost_estimate=pl.CostEstimate(
            flops=groups * rows * 2 * embed * (embed + 2 * PARTNERS * rows),
            bytes_accessed=4 * groups * rows * embed,
            transcendentals=groups * PARTNERS * rows * rows,
        ),
        name="contrast",
    )(group, offsets, blocks, mean, whitener)


def gather_kernel(window_ref, grad_ref, features_ref, *refs):
    groups = grad_ref.shape[0]
    outs, total = refs[:-1], refs[-1]
    share = outs[0].shape[0]
    window = window_ref[0]

    def columns(at):
        value = dot(features_ref[0, :, at], grad_ref[0], (0, 0))
        for k in range(1, groups):
            value = value + dot(features_ref[k, :, at], grad_ref[k], (0, 0))
        return value

    if share % LANES:
        total[...] = columns(slice(None))
    for r, out in enumerate(outs):
        at = pl.ds(pl.multiple_of((window ^ r) * share, share), share)
        value = total[at, :] if share % LANES else columns(at)
        out[...] = value.astype(out.dtype)


def weight_pieces(window, grad, feature_slices, shares):
    groups, rows, embed = grad.shape
    columns = feature_slices.shape[2]
    share = columns // shares
    return pl.pallas_call(
        gather_kernel,
        in_specs=[smem()] + [vmem()] * 2,
        out_specs=[vmem()] * shares,
        out_shape=[
            jax.ShapeDtypeStruct((share, embed), BF16 if r else F32) for r in range(shares)
        ],
        scratch_shapes=[pltpu.VMEM((columns if share % LANES else 8, embed), F32)],
        compiler_params=params(24),
        cost_estimate=pl.CostEstimate(
            flops=groups * rows * 2 * embed * columns,
            bytes_accessed=2 * groups * rows * (embed + columns),
            transcendentals=0,
        ),
        name="weight_pieces",
    )(window, grad, feature_slices)


def finish_kernel(*refs):
    keep_ref, whitener_ref, out_ref = refs[0], refs[-2], refs[-1]
    value = keep_ref[...]
    for ref in refs[1:-2]:
        value = value + ref[...].astype(F32)
    high, low = split(value)
    out_ref[...] = dot(high, whitener_ref[...], (1, 1)) + dot(low, whitener_ref[...], (1, 1))


def finish(pieces, whitener):
    return pl.pallas_call(
        finish_kernel,
        in_specs=[vmem()] * (len(pieces) + 1),
        out_specs=vmem(),
        out_shape=jax.ShapeDtypeStruct(pieces[0].shape, F32),
        compiler_params=params(12),
        name="finish",
    )(*pieces, whitener)


def shards(features, proj_weight, partner_offsets, ortholog_index):
    rows, depth = features.shape
    embed = proj_weight.shape[1]
    groups = lax.axis_size("sp")
    shares = lax.axis_size("win")
    devices = groups * shares
    group = lax.axis_index("sp").astype(jnp.int32)
    window = lax.axis_index("win").astype(jnp.int32)
    me = group * shares + window

    block, slices, send, keep = project(
        me.reshape(1), partner_offsets, features, proj_weight, ortholog_index.T, groups
    )
    blocks = lax.all_gather(block, "sp")

    arrived = [xor_permute(send, 1)]
    sent = send
    seen = 1
    stages = []
    low = 1
    place = me & 1
    while keep.shape[0] > 32:
        count = 4
        own = (me >> low) & (count - 1)
        keep, sends, seen = stage(own, keep, sent, arrived, seen, count, embed)
        arrived = [xor_permute(piece, (r + 1) << low) for r, piece in enumerate(sends)]
        sent = sends[0]
        stages.append((low, count))
        place = place * count + own
        low += 2
    size = keep.shape[0]
    part = keep
    for piece in arrived:
        part = part + piece[:size].astype(F32)
    sums = jnp.stack([sent[size:]] + [piece[size:] for piece in arrived])
    extra = devices >> low
    if extra > 1:
        mine = jnp.concatenate([part.astype(BF16), sums.reshape(-1, sums.shape[2])])
        others = [xor_permute(mine, r << low) for r in range(1, extra)]
        for piece in others:
            part = part + piece[:size].astype(F32)
        sums = jnp.concatenate([sums] + [piece[size:].reshape(sums.shape) for piece in others])
    part = part.astype(BF16)
    for low, count in reversed(stages):
        part = jnp.concatenate(
            [part] + [xor_permute(part, r << low) for r in range(1, count)], axis=0
        )
    part = part.reshape(-1, size, part.shape[1])
    other = xor_permute(part, 1)

    other, slices = lax.optimization_barrier((other, slices))
    slices = lax.all_to_all(slices, "sp", 0, 0)

    whitener, mean = whiten(place.reshape(1), sums, part, other, rows, embed)
    offsets = blocks[:, rows + 1, :PARTNERS].astype(jnp.int32)
    loss, grad = contrast(group.reshape(1), offsets, blocks, mean, whitener)
    pieces = weight_pieces(window.reshape(1), grad, slices, shares)
    pieces = [pieces[0]] + [xor_permute(pieces[r], r) for r in range(1, shares)]
    return loss[0], finish(pieces, whitener)


def solution(mesh):
    return jax.shard_map(
        shards,
        mesh=mesh,
        in_specs=(P(("sp", "win"), None), P(), P("sp", None), P(("sp", "win"), None)),
        out_specs=(P(("sp", "win")), P(("sp", "win"), None)),
        check_vma=False,
    )
```

time: 183 us -> 207 us (1.13)
  waiting for transfers between devices: 38.5 us -> 89.5 us
  starting transfers between devices: 57.2 us -> 27.2 us
  Pallas kernels: 53.8 us -> 59.7 us
  local copies, waits for them, and re-layouts: 17.2 us -> 12.4 us
    all_gather x1, waiting for transfers between devices: 0.01 us -> 37 us  [shards(): blocks = lax.all_gather(block, 'sp')]
    ppermute x38 -> x17, starting transfers between devices: 57.2 us -> 22.7 us  [xor_permute(): return lax.ppermute(piece, AXES, [(i, i ^ mask) for i in range(devices)])]
    ppermute x38 -> x17, waiting for transfers between devices: 38.5 us -> 52.5 us  [xor_permute(): return lax.ppermute(piece, AXES, [(i, i ^ mask) for i in range(devices)])]
    pallas_call x1, Pallas kernels: 4.82 us -> 10.4 us  [project(): pl.pallas_call(project_kernel, grid_spec=pltpu.PrefetchScalarGridSpec(num...]
    all_to_all x0 -> x1, starting transfers between devices: none -> 4.44 us  [shards(): slices = lax.all_to_all(slices, 'sp', 0, 0)]
    unnamed x34 -> x23, local copies, waits for them, and re-layouts: 14.5 us -> 12.4 us
    pallas_call x3 -> x5, Pallas kernels: 46.7 us -> 47 us  [the longest x1 26.3 us: contrast(): pl.pallas_call(contrast_kernel, in_specs=[smem(), smem()] + [vmem()] * 3,...]
  transfers between devices with their start and end apart: 39 -> 19, of which waited for: 16 -> 13; matrix products, arithmetic and copies ran while one was open for 4% -> 1% of each run, Pallas kernels for 24% -> 22%
where the time goes in v3:
time: 207 us; the launch traced here: 205 us
  waiting for transfers between devices  89.5 us (43%)
  Pallas kernels  59.7 us (29%)
  starting transfers between devices  27.2 us (13%)
  between operations  14.1 us (7%)
  local copies, waits for them, and re-layouts  12.4 us (6%)
  other arithmetic  2.22 us (1%)
    ppermute x17, waiting for transfers between devices, xor_permute(): return lax.ppermute(piece, AXES, [(i, i ^ mask) for i in range(devices)])  52.5 us
    all_gather x1, waiting for transfers between devices, shards(): blocks = lax.all_gather(block, 'sp')  37 us
    pallas_call x1, Pallas kernels, contrast(): pl.pallas_call(contrast_kernel, in_specs=[smem(), smem()] + [vmem()] * 3,...  26.3 us
    ppermute x17, starting transfers between devices, xor_permute(): return lax.ppermute(piece, AXES, [(i, i ^ mask) for i in range(devices)])  22.7 us
    pallas_call x1, Pallas kernels, whiten(): pl.pallas_call(make_whiten_kernel(rows), in_specs=[smem()] + [vmem()] * 3...  17.3 us
    unnamed x23, local copies, waits for them, and re-layouts  12.4 us
    pallas_call x1, Pallas kernels, project(): pl.pallas_call(project_kernel, grid_spec=pltpu.PrefetchScalarGridSpec(num...  10.4 us
    all_to_all x1, starting transfers between devices, shards(): slices = lax.all_to_all(slices, 'sp', 0, 0)  4.44 us
  transfers between devices with their start and end apart: 19, of which 13 were waited for; matrix products, arithmetic and copies ran while one was open for 1% of the time, Pallas kernels for 22%

profile of v3, /device:TPU:0, one launch (start us, length us, event | category | flops | bytes accessed | tf_op | source)
XLA Modules:
  0.0 205.2 jit_solution(8986542716383767777)
XLA Ops:
  7.2 0.0 all-gather.3.cloned.1.call-start
  7.2 0.0 copy-start
  7.2 1.6 copy-done
  8.8 0.0 copy-start.4
  8.8 0.7 copy-done.4
  9.5 0.0 copy-start.5
  9.5 0.7 copy-done.5
  10.2 10.4 %project.1 = (bf16[272,1024]{1,0:T(8,128)(2,1)}, bf16[8,256,512]{2,1,0:T(8,128)(2,1)}, bf16[528,640]{1,0:T(8,128)(2,1)S(1)}, f32[512,640]{1,0:T(8,128)S(1)}) custom-call(s32[1]{0:T(128)} %bitcast.1.me_ref, s32[1,4]{1,0:T(1,128)S(1)} %copy-done.5, bf16[256,4096]{1,0:T(8,128)(2,1)S(1)} %copy-done, bf16[4096,1024]{1,0:T(8,128)(2,1)} %weight_ref.1, ...), custom_call_target="tpu_custom_call" | custom-call | flops 2147483648 | bytes 8388608 | tf_op jit(solution)/shard_map/project/pallas_call | solution.py:140
  20.6 0.0 all-gather.3.cloned.1.call-update
  20.6 0.5 collective-permute-start
  21.1 1.8 collective-permute-done.refs_0_
  22.9 0.8 stage.2
  23.7 2.9 %collective-permute-start.2 = (bf16[144,640]{1,0:T(8,128)(2,1)}, bf16[144,640]{1,0:T(8,128)(2,1)S(1)}, u32[]{:S(2)}, u32[]{:S(2)}) collective-permute-start(bf16[144,640]{1,0:T(8,128)(2,1)} %get-tuple-element.29), channel_id=1, source_target_pairs={{0,4},{1,5},{2,6},{3,7},{4,0},{5,1},{6,2},{7,3},{8,12},{9,13},{10,... | collective-permute-start | bytes 552968 | tf_op jit(solution)/shard_map/ppermute | solution.py:44
  26.5 1.5 collective-permute-start.3
  28.0 0.0 collective-permute-start.1
  28.1 4.1 %collective-permute-done.2.refs_1_ = bf16[144,640]{1,0:T(8,128)(2,1)S(1)} collective-permute-done((bf16[144,640]{1,0:T(8,128)(2,1)}, bf16[144,640]{1,0:T(8,128)(2,1)S(1)}, u32[]{:S(2)}, u32[]{:S(2)}) %collective-permute-start.2) | collective-permute-done | bytes 184352 | tf_op jit(solution)/shard_map/ppermute | solution.py:44
  32.2 7.1 %collective-permute-done.3.refs_2_ = bf16[144,640]{1,0:T(8,128)(2,1)S(1)} collective-permute-done((bf16[144,640]{1,0:T(8,128)(2,1)S(1)}, bf16[144,640]{1,0:T(8,128)(2,1)S(1)}, u32[]{:S(2)}, u32[]{:S(2)}) %collective-permute-start.3) | collective-permute-done | bytes 184352 | tf_op jit(solution)/shard_map/ppermute | solution.py:44
  39.3 0.0 collective-permute-done.1.refs_0_
  39.3 0.1 stage.3
  39.4 2.8 %collective-permute-start.5 = (bf16[64,640]{1,0:T(8,128)(2,1)S(1)}, bf16[64,640]{1,0:T(8,128)(2,1)S(1)}, u32[]{:S(2)}, u32[]{:S(2)}) collective-permute-start(bf16[64,640]{1,0:T(8,128)(2,1)S(1)} %get-tuple-element.32), channel_id=1, source_target_pairs={{0,16},{1,17},{2,18},{3,19},{4,20},{5,21},{6,22},{7,23},{8,24},{9,... | collective-permute-start | bytes 245768 | tf_op jit(solution)/shard_map/ppermute | solution.py:44
  42.2 1.3 collective-permute-start.6
  43.5 0.4 collective-permute-start.4
  43.9 8.6 %collective-permute-done.5 = bf16[64,640]{1,0:T(8,128)(2,1)S(1)} collective-permute-done((bf16[64,640]{1,0:T(8,128)(2,1)S(1)}, bf16[64,640]{1,0:T(8,128)(2,1)S(1)}, u32[]{:S(2)}, u32[]{:S(2)}) %collective-permute-start.5) | collective-permute-done | bytes 81952 | tf_op jit(solution)/shard_map/ppermute | solution.py:44
  52.5 0.0 collective-permute-done.6
  52.5 1.0 collective-permute-done.4
  53.5 0.6 constant_dynamic-update-slice_fusion.6
  54.2 2.8 %collective-permute-start.9 = (bf16[32,640]{1,0:T(8,128)(2,1)S(1)}, bf16[32,640]{1,0:T(8,128)(2,1)S(1)}, u32[]{:S(2)}, u32[]{:S(2)}) collective-permute-start(bf16[32,640]{1,0:T(8,128)(2,1)S(1)} %get-tuple-element.47), channel_id=1, source_target_pairs={{0,24},{1,25},{2,26},{3,27},{4,28},{5,29},{6,30},{7,31},{8,16},{9,... | collective-permute-start | bytes 122888 | tf_op jit(solution)/shard_map/ppermute | solution.py:44
  57.0 4.1 %collective-permute-start.8 = (bf16[32,640]{1,0:T(8,128)(2,1)S(1)}, bf16[32,640]{1,0:T(8,128)(2,1)S(1)}, u32[]{:S(2)}, u32[]{:S(2)}) collective-permute-start(bf16[32,640]{1,0:T(8,128)(2,1)S(1)} %get-tuple-element.47), channel_id=1, source_target_pairs={{0,16},{1,17},{2,18},{3,19},{4,20},{5,21},{6,22},{7,23},{8,24},{9,... | collective-permute-start | bytes 122888 | tf_op jit(solution)/shard_map/ppermute | solution.py:44
  61.1 0.2 collective-permute-start.7
  61.3 0.0 collective-permute-done.9
  61.3 2.7 %collective-permute-done.8 = bf16[32,640]{1,0:T(8,128)(2,1)S(1)} collective-permute-done((bf16[32,640]{1,0:T(8,128)(2,1)S(1)}, bf16[32,640]{1,0:T(8,128)(2,1)S(1)}, u32[]{:S(2)}, u32[]{:S(2)}) %collective-permute-start.8) | collective-permute-done | bytes 40992 | tf_op jit(solution)/shard_map/ppermute | solution.py:44
  64.0 1.1 collective-permute-done.7
  65.1 2.4 %collective-permute-start.12 = (bf16[128,640]{1,0:T(8,128)(2,1)S(1)}, bf16[128,640]{1,0:T(8,128)(2,1)S(1)}, u32[]{:S(2)}, u32[]{:S(2)}) collective-permute-start(bf16[128,640]{1,0:T(8,128)(2,1)S(1)} %pad_maximum_fusion.1), channel_id=1, source_target_pairs={{0,6},{1,7},{2,4},{3,5},{4,2},{5,3},{6,0},{7,1},{8,14},{9,15},{10,... | collective-permute-start | bytes 491528 | tf_op jit(solution)/shard_map/ppermute | solution.py:44
  67.6 0.3 collective-permute-start.11
  67.9 1.4 collective-permute-start.10
  69.3 4.8 %collective-permute-done.10 = bf16[128,640]{1,0:T(8,128)(2,1)S(1)} collective-permute-done((bf16[128,640]{1,0:T(8,128)(2,1)S(1)}, bf16[128,640]{1,0:T(8,128)(2,1)S(1)}, u32[]{:S(2)}, u32[]{:S(2)}) %collective-permute-start.10) | collective-permute-done | bytes 163872 | tf_op jit(solution)/shard_map/ppermute | solution.py:44
  74.1 7.1 %collective-permute-done.11 = bf16[128,640]{1,0:T(8,128)(2,1)S(1)} collective-permute-done((bf16[128,640]{1,0:T(8,128)(2,1)S(1)}, bf16[128,640]{1,0:T(8,128)(2,1)S(1)}, u32[]{:S(2)}, u32[]{:S(2)}) %collective-permute-start.11) | collective-permute-done | bytes 163872 | tf_op jit(solution)/shard_map/ppermute | solution.py:44
  81.3 0.0 collective-permute-done.12
  81.3 0.1 collective-permute-start.13
  81.4 2.1 %collective-permute-done.13.far_ref = bf16[16,32,640]{2,1,0:T(8,128)(2,1)S(1)} collective-permute-done((bf16[16,32,640]{2,1,0:T(8,128)(2,1)S(1)}, bf16[16,32,640]{2,1,0:T(8,128)(2,1)S(1)}, u32[]{:S(2)}, u32[]{:S(2)}) %collective-permute-start.13) | collective-permute-done | bytes 655392 | tf_op jit(solution)/shard_map/ppermute | solution.py:44
  83.5 4.4 %all-to-all-start = ((bf16[8,256,512]{2,1,0:T(8,128)(2,1)}), bf16[8,256,512]{2,1,0:T(8,128)(2,1)S(1)}, u32[]{:S(2)}, u32[]{:S(2)}) async-start(bf16[8,256,512]{2,1,0:T(8,128)(2,1)} %get-tuple-element.41), calls=%async_computation | async-start | bytes 4194304 | tf_op jit(solution)/shard_map/all_to_all | solution.py:533
  87.9 0.8 pad_maximum_fusion.sums_ref
  88.8 17.3 %whiten.1 = (bf16[1024,1024]{1,0:T(8,128)(2,1)S(1)}, f32[1,1024]{1,0:T(1,128)S(1)}) custom-call(s32[1]{0:T(128)} %bitcast.5.place_ref, bf16[4,32,640]{2,1,0:T(8,128)(2,1)S(1)} %pad_maximum_fusion.sums_ref, bf16[16,32,640]{2,1,0:T(8,128)(2,1)S(1)} %bitcast.22, bf16[16,32,640]{2,1,0:T(8,128)(2,1)S(1)} %collective-permute-done.13.far_ref), custom_call_target="tpu_custom_call" | custom-call | flops 10737418240 | bytes 2097152 | tf_op jit(solution)/shard_map/whiten/pallas_call | solution.py:344
  106.1 0.0 copy-start.1
  106.1 1.4 copy-done.1
  107.5 37.0 %all-gather.3.cloned.1.call-done = bf16[2176,1024]{1,0:T(8,128)(2,1)} async-done(((bf16[272,1024]{1,0:T(8,128)(2,1)}), bf16[2176,1024]{1,0:T(8,128)(2,1)}) %all-gather.3.cloned.1.call-update) | async-done | bytes 4456464 | tf_op jit(solution)/shard_map/all_gather | solution.py:495
  144.5 0.7 slice_convert_fusion
  145.3 0.0 copy-start.2
  145.3 1.6 copy-done.2
  146.9 0.0 copy-start.6
  146.9 2.3 %copy-done.6 = bf16[2176,1024]{1,0:T(8,128)(2,1)S(1)} copy-done((bf16[2176,1024]{1,0:T(8,128)(2,1)S(1)}, bf16[2176,1024]{1,0:T(8,128)(2,1)}, u32[]{:S(2)}) %copy-start.6) | copy-done | bytes 4456472
  149.1 26.3 %contrast.1 = (f32[1,256]{1,0:T(1,128)}, bf16[8,256,1024]{2,1,0:T(8,128)(2,1)S(1)}) custom-call(s32[1]{0:T(128)} %bitcast.group_ref, s32[8,4]{1,0:T(8,128)S(1)} %bitcast.20, bf16[8,272,1024]{2,1,0:T(8,128)(2,1)S(1)} %bitcast.24, f32[1,1024]{1,0:T(1,128)S(1)} %get-tuple-element.37.mean_ref, bf16[1024,1024]{1,0:T(8,128)(2,1)S(1)} %copy-done.2), custom_call_target="tpu_custom_call" | custom-call | flops 12884901888 | bytes 8388608 | tf_op jit(solution)/shard_map/contrast/pallas_call | solution.py:401
  175.4 2.0 copy-done.7
  177.4 0.0 all-to-all-done.features_ref
  177.4 2.2 %copy-done.8 = bf16[8,256,1024]{2,1,0:T(8,128)(2,1)S(1)} copy-done((bf16[8,256,1024]{2,1,0:T(8,128)(2,1)S(1)}, bf16[8,256,1024]{2,1,0:T(8,128)(2,1)}, u32[]{:S(2)}) %copy-start.8) | copy-done | bytes 4194328
  179.6 2.4 %weight_pieces.1 = (f32[128,1024]{1,0:T(8,128)S(1)}, bf16[128,1024]{1,0:T(8,128)(2,1)S(1)}, bf16[128,1024]{1,0:T(8,128)(2,1)S(1)}, bf16[128,1024]{1,0:T(8,128)(2,1)S(1)}) custom-call(s32[1]{0:T(128)} %bitcast.14.window_ref, bf16[8,256,1024]{2,1,0:T(8,128)(2,1)S(1)} %copy-done.8, bf16[8,256,512]{2,1,0:T(8,128)(2,1)S(1)} %all-to-all-done.features_ref), custom_call_target="tpu_custom_call" | custom-call | flops 2147483648 | bytes 6291456 | tf_op jit(solution)/shard_map/weight_pieces/pallas_call | solution.py:444
  182.0 0.1 collective-permute-start.14
  182.1 1.8 collective-permute-start.15
  183.9 0.1 collective-permute-start.16
  184.0 0.0 collective-permute-done.14.refs_1_
  184.0 7.3 %collective-permute-done.15.refs_2_ = bf16[128,1024]{1,0:T(8,128)(2,1)S(1)} collective-permute-done((bf16[128,1024]{1,0:T(8,128)(2,1)S(1)}, bf16[128,1024]{1,0:T(8,128)(2,1)S(1)}, u32[]{:S(2)}, u32[]{:S(2)}) %collective-permute-start.15) | collective-permute-done | bytes 262176 | tf_op jit(solution)/shard_map/ppermute | solution.py:44
  191.3 4.7 %collective-permute-done.16.refs_3_ = bf16[128,1024]{1,0:T(8,128)(2,1)S(1)} collective-permute-done((bf16[128,1024]{1,0:T(8,128)(2,1)S(1)}, bf16[128,1024]{1,0:T(8,128)(2,1)S(1)}, u32[]{:S(2)}, u32[]{:S(2)}) %collective-permute-start.16) | collective-permute-done | bytes 262176 | tf_op jit(solution)/shard_map/ppermute | solution.py:44
  196.0 0.0 copy-done.3
  196.0 2.3 %finish.1 = f32[128,1024]{1,0:T(8,128)} custom-call(f32[128,1024]{1,0:T(8,128)S(1)} %get-tuple-element.42.refs_0_, bf16[128,1024]{1,0:T(8,128)(2,1)S(1)} %collective-permute-done.14.refs_1_, bf16[128,1024]{1,0:T(8,128)(2,1)S(1)} %collective-permute-done.15.refs_2_, bf16[128,1024]{1,0:T(8,128)(2,1)S(1)} %collective-permute-done.16.refs_3_, ...), custom_call_target="tpu_custom_call" | custom-call | tf_op jit(solution)/shard_map/finish/pallas_call | solution.py:472
  (11 shorter events, 0.1 us)
Async XLA Ops:
  7.2 137.4 %all-gather.3.cloned.1.call-start = ((), (), s32[]{:S(2)}) async-start(), calls=%async_computation.1 | async-start | bytes 5013504 | tf_op jit(solution)/shard_map/all_gather | solution.py:495
  7.2 1.6 copy-start
  8.8 0.7 copy-start.4
  9.5 0.7 copy-start.5
  20.6 2.3 %collective-permute-start = (bf16[528,640]{1,0:T(8,128)(2,1)S(1)}, bf16[528,640]{1,0:T(8,128)(2,1)S(1)}, u32[]{:S(2)}, u32[]{:S(2)}) collective-permute-start(bf16[528,640]{1,0:T(8,128)(2,1)S(1)} %get-tuple-element.26.sent_ref), channel_id=1, source_target_pairs={{0,1},{1,0},{2,3},{3,2},{4,5},{5,4},{6,7},{7,6},{8,9},{9,8},{10,11... | collective-permute-start | bytes 2027528 | tf_op jit(solution)/shard_map/ppermute | solution.py:44
  23.7 8.5 %collective-permute-start.2 = (bf16[144,640]{1,0:T(8,128)(2,1)}, bf16[144,640]{1,0:T(8,128)(2,1)S(1)}, u32[]{:S(2)}, u32[]{:S(2)}) collective-permute-start(bf16[144,640]{1,0:T(8,128)(2,1)} %get-tuple-element.29), channel_id=1, source_target_pairs={{0,4},{1,5},{2,6},{3,7},{4,0},{5,1},{6,2},{7,3},{8,12},{9,13},{10,... | collective-permute-start | bytes 552968 | tf_op jit(solution)/shard_map/ppermute | solution.py:44
  26.5 12.7 %collective-permute-start.3 = (bf16[144,640]{1,0:T(8,128)(2,1)S(1)}, bf16[144,640]{1,0:T(8,128)(2,1)S(1)}, u32[]{:S(2)}, u32[]{:S(2)}) collective-permute-start(bf16[144,640]{1,0:T(8,128)(2,1)S(1)} %get-tuple-element.30), channel_id=1, source_target_pairs={{0,6},{1,7},{2,4},{3,5},{4,2},{5,3},{6,0},{7,1},{8,14},{9,15},{10,... | collective-permute-start | bytes 552968 | tf_op jit(solution)/shard_map/ppermute | solution.py:44
  28.0 11.2 %collective-permute-start.1 = (bf16[144,640]{1,0:T(8,128)(2,1)S(1)}, bf16[144,640]{1,0:T(8,128)(2,1)S(1)}, u32[]{:S(2)}, u32[]{:S(2)}) collective-permute-start(bf16[144,640]{1,0:T(8,128)(2,1)S(1)} %get-tuple-element.28.sent_ref), channel_id=1, source_target_pairs={{0,2},{1,3},{2,0},{3,1},{4,6},{5,7},{6,4},{7,5},{8,10},{9,11},{10,... | collective-permute-start | bytes 552968 | tf_op jit(solution)/shard_map/ppermute | solution.py:44
  39.4 13.1 %collective-permute-start.5 = (bf16[64,640]{1,0:T(8,128)(2,1)S(1)}, bf16[64,640]{1,0:T(8,128)(2,1)S(1)}, u32[]{:S(2)}, u32[]{:S(2)}) collective-permute-start(bf16[64,640]{1,0:T(8,128)(2,1)S(1)} %get-tuple-element.32), channel_id=1, source_target_pairs={{0,16},{1,17},{2,18},{3,19},{4,20},{5,21},{6,22},{7,23},{8,24},{9,... | collective-permute-start | bytes 245768 | tf_op jit(solution)/shard_map/ppermute | solution.py:44
  42.2 10.3 %collective-permute-start.6 = (bf16[64,640]{1,0:T(8,128)(2,1)S(1)}, bf16[64,640]{1,0:T(8,128)(2,1)S(1)}, u32[]{:S(2)}, u32[]{:S(2)}) collective-permute-start(bf16[64,640]{1,0:T(8,128)(2,1)S(1)} %get-tuple-element.33), channel_id=1, source_target_pairs={{0,24},{1,25},{2,26},{3,27},{4,28},{5,29},{6,30},{7,31},{8,16},{9,... | collective-permute-start | bytes 245768 | tf_op jit(solution)/shard_map/ppermute | solution.py:44
  43.5 10.1 %collective-permute-start.4 = (bf16[64,640]{1,0:T(8,128)(2,1)S(1)}, bf16[64,640]{1,0:T(8,128)(2,1)S(1)}, u32[]{:S(2)}, u32[]{:S(2)}) collective-permute-start(bf16[64,640]{1,0:T(8,128)(2,1)S(1)} %get-tuple-element.31), channel_id=1, source_target_pairs={{0,8},{1,9},{2,10},{3,11},{4,12},{5,13},{6,14},{7,15},{8,0},{9,1},... | collective-permute-start | bytes 245768 | tf_op jit(solution)/shard_map/ppermute | solution.py:44
  54.2 7.1 %collective-permute-start.9 = (bf16[32,640]{1,0:T(8,128)(2,1)S(1)}, bf16[32,640]{1,0:T(8,128)(2,1)S(1)}, u32[]{:S(2)}, u32[]{:S(2)}) collective-permute-start(bf16[32,640]{1,0:T(8,128)(2,1)S(1)} %get-tuple-element.47), channel_id=1, source_target_pairs={{0,24},{1,25},{2,26},{3,27},{4,28},{5,29},{6,30},{7,31},{8,16},{9,... | collective-permute-start | bytes 122888 | tf_op jit(solution)/shard_map/ppermute | solution.py:44
  57.0 7.0 %collective-permute-start.8 = (bf16[32,640]{1,0:T(8,128)(2,1)S(1)}, bf16[32,640]{1,0:T(8,128)(2,1)S(1)}, u32[]{:S(2)}, u32[]{:S(2)}) collective-permute-start(bf16[32,640]{1,0:T(8,128)(2,1)S(1)} %get-tuple-element.47), channel_id=1, source_target_pairs={{0,16},{1,17},{2,18},{3,19},{4,20},{5,21},{6,22},{7,23},{8,24},{9,... | collective-permute-start | bytes 122888 | tf_op jit(solution)/shard_map/ppermute | solution.py:44
  61.1 4.0 %collective-permute-start.7 = (bf16[32,640]{1,0:T(8,128)(2,1)S(1)}, bf16[32,640]{1,0:T(8,128)(2,1)S(1)}, u32[]{:S(2)}, u32[]{:S(2)}) collective-permute-start(bf16[32,640]{1,0:T(8,128)(2,1)S(1)} %get-tuple-element.47), channel_id=1, source_target_pairs={{0,8},{1,9},{2,10},{3,11},{4,12},{5,13},{6,14},{7,15},{8,0},{9,1},... | collective-permute-start | bytes 122888 | tf_op jit(solution)/shard_map/ppermute | solution.py:44
  65.1 16.2 %collective-permute-start.12 = (bf16[128,640]{1,0:T(8,128)(2,1)S(1)}, bf16[128,640]{1,0:T(8,128)(2,1)S(1)}, u32[]{:S(2)}, u32[]{:S(2)}) collective-permute-start(bf16[128,640]{1,0:T(8,128)(2,1)S(1)} %pad_maximum_fusion.1), channel_id=1, source_target_pairs={{0,6},{1,7},{2,4},{3,5},{4,2},{5,3},{6,0},{7,1},{8,14},{9,15},{10,... | collective-permute-start | bytes 491528 | tf_op jit(solution)/shard_map/ppermute | solution.py:44
  67.6 13.7 %collective-permute-start.11 = (bf16[128,640]{1,0:T(8,128)(2,1)S(1)}, bf16[128,640]{1,0:T(8,128)(2,1)S(1)}, u32[]{:S(2)}, u32[]{:S(2)}) collective-permute-start(bf16[128,640]{1,0:T(8,128)(2,1)S(1)} %pad_maximum_fusion.1), channel_id=1, source_target_pairs={{0,4},{1,5},{2,6},{3,7},{4,0},{5,1},{6,2},{7,3},{8,12},{9,13},{10,... | collective-permute-start | bytes 491528 | tf_op jit(solution)/shard_map/ppermute | solution.py:44
  67.9 6.2 %collective-permute-start.10 = (bf16[128,640]{1,0:T(8,128)(2,1)S(1)}, bf16[128,640]{1,0:T(8,128)(2,1)S(1)}, u32[]{:S(2)}, u32[]{:S(2)}) collective-permute-start(bf16[128,640]{1,0:T(8,128)(2,1)S(1)} %pad_maximum_fusion.1), channel_id=1, source_target_pairs={{0,2},{1,3},{2,0},{3,1},{4,6},{5,7},{6,4},{7,5},{8,10},{9,11},{10,... | collective-permute-start | bytes 491528 | tf_op jit(solution)/shard_map/ppermute | solution.py:44
  81.3 2.2 %collective-permute-start.13 = (bf16[16,32,640]{2,1,0:T(8,128)(2,1)S(1)}, bf16[16,32,640]{2,1,0:T(8,128)(2,1)S(1)}, u32[]{:S(2)}, u32[]{:S(2)}) collective-permute-start(bf16[16,32,640]{2,1,0:T(8,128)(2,1)S(1)} %bitcast.21), channel_id=1, source_target_pairs={{0,1},{1,0},{2,3},{3,2},{4,5},{5,4},{6,7},{7,6},{8,9},{9,8},{10,11... | collective-permute-start | bytes 1966088 | tf_op jit(solution)/shard_map/ppermute | solution.py:44
  83.5 93.9 %all-to-all-start = ((bf16[8,256,512]{2,1,0:T(8,128)(2,1)}), bf16[8,256,512]{2,1,0:T(8,128)(2,1)S(1)}, u32[]{:S(2)}, u32[]{:S(2)}) async-start(bf16[8,256,512]{2,1,0:T(8,128)(2,1)} %get-tuple-element.41), calls=%async_computation | async-start | bytes 4194304 | tf_op jit(solution)/shard_map/all_to_all | solution.py:533
  106.1 1.4 copy-start.1
  145.3 1.6 copy-start.2
  146.9 2.3 %copy-start.6 = (bf16[2176,1024]{1,0:T(8,128)(2,1)S(1)}, bf16[2176,1024]{1,0:T(8,128)(2,1)}, u32[]{:S(2)}) copy-start(bf16[2176,1024]{1,0:T(8,128)(2,1)} %all-gather.3.cloned.1.call-done) | copy-start | bytes 13369348
  175.4 2.0 copy-start.7
  177.4 2.2 %copy-start.8 = (bf16[8,256,1024]{2,1,0:T(8,128)(2,1)S(1)}, bf16[8,256,1024]{2,1,0:T(8,128)(2,1)}, u32[]{:S(2)}) copy-start(bf16[8,256,1024]{2,1,0:T(8,128)(2,1)} %copy-done.7) | copy-start | bytes 12582916
  179.6 16.4 %copy-start.3 = (bf16[1024,1024]{1,0:T(8,128)(2,1)S(1)}, bf16[1024,1024]{1,0:T(8,128)(2,1)}, u32[]{:S(2)}) copy-start(bf16[1024,1024]{1,0:T(8,128)(2,1)} %copy-done.1) | copy-start | bytes 6291460
  182.0 2.0 collective-permute-start.14
  182.1 9.1 %collective-permute-start.15 = (bf16[128,1024]{1,0:T(8,128)(2,1)S(1)}, bf16[128,1024]{1,0:T(8,128)(2,1)S(1)}, u32[]{:S(2)}, u32[]{:S(2)}) collective-permute-start(bf16[128,1024]{1,0:T(8,128)(2,1)S(1)} %get-tuple-element.44), channel_id=1, source_target_pairs={{0,2},{1,3},{2,0},{3,1},{4,6},{5,7},{6,4},{7,5},{8,10},{9,11},{10,... | collective-permute-start | bytes 786440 | tf_op jit(solution)/shard_map/ppermute | solution.py:44
  183.9 12.1 %collective-permute-start.16 = (bf16[128,1024]{1,0:T(8,128)(2,1)S(1)}, bf16[128,1024]{1,0:T(8,128)(2,1)S(1)}, u32[]{:S(2)}, u32[]{:S(2)}) collective-permute-start(bf16[128,1024]{1,0:T(8,128)(2,1)S(1)} %get-tuple-element.45), channel_id=1, source_target_pairs={{0,3},{1,2},{2,1},{3,0},{4,7},{5,6},{6,5},{7,4},{8,11},{9,10},{10,... | collective-permute-start | bytes 786440 | tf_op jit(solution)/shard_map/ppermute | solution.py:44
Sparse Core Ops, SparseCore 0:
  20.7 123.7 all-gather.2

commit v4 on v3

--- a/solution.py
+++ b/solution.py
@@ -10,6 +10,7 @@
 AXES = ("sp", "win")
 LANES = 128
 TAIL = 16
+STREAMS = 4
 F32 = jnp.float32
 BF16 = jnp.bfloat16
 HIGHEST = lax.Precision.HIGHEST
@@ -73,15 +74,11 @@
     me_ref,
     offsets_ref,
     features_ref,
-    weight_ref,
     ortholog_ref,
-    block_ref,
-    slices_ref,
-    send_ref,
-    keep_ref,
-    acc,
-    wide,
+    *refs,
 ):
+    weight_refs = refs[:STREAMS]
+    block_ref, send_ref, keep_ref, acc, wide = refs[STREAMS:]
     step = pl.program_id(0)
     rows, embed = acc.shape
     half, packed = keep_ref.shape
@@ -91,8 +88,11 @@
     def _():
         acc[...] = jnp.zeros_like(acc)
 
-    slices_ref[0] = features_ref[...]
-    acc[...] += dot(features_ref[...], weight_ref[...])
+    part = features_ref.shape[1] // STREAMS
+    value = acc[...]
+    for k, weight_ref in enumerate(weight_refs):
+        value += dot(features_ref[:, k * part : (k + 1) * part], weight_ref[...])
+    acc[...] = value
 
     @pl.when(step == pl.num_programs(0) - 1)
     def _():
@@ -131,25 +131,29 @@
                     out[r * LANES : (r + 1) * LANES, at] = value.astype(out.dtype)
 
 
-def project(me, offsets, features, weight, ortholog, groups):
+def project(me, offsets, features, weight, ortholog):
     rows, depth = features.shape
     embed = weight.shape[1]
     packed = embed // 2 + LANES
-    tile = depth // groups
+    steps = 4
+    tile = depth // steps
     fixed = lambda k, *_: (0, 0)
+    streams = [
+        pl.BlockSpec((tile // STREAMS, embed), lambda k, *_, j=j: (STREAMS * k + j, 0))
+        for j in range(STREAMS)
+    ]
     return pl.pallas_call(
         project_kernel,
         grid_spec=pltpu.PrefetchScalarGridSpec(
             num_scalar_prefetch=2,
-            grid=(groups,),
+            grid=(steps,),
             in_specs=[
                 pl.BlockSpec((rows, tile), lambda k, *_: (0, k)),
-                pl.BlockSpec((tile, embed), lambda k, *_: (k, 0)),
                 pl.BlockSpec((PARTNERS, rows), fixed),
-            ],
+            ]
+            + streams,
             out_specs=[
                 pl.BlockSpec((rows + TAIL, embed), fixed),
-                pl.BlockSpec((1, rows, tile), lambda k, *_: (k, 0, 0)),
                 pl.BlockSpec((embed // 2 + TAIL, packed), fixed),
                 pl.BlockSpec((embed // 2, packed), fixed),
             ],
@@ -160,16 +164,15 @@
         ),
         out_shape=[
             jax.ShapeDtypeStruct((rows + TAIL, embed), BF16),
-            jax.ShapeDtypeStruct((groups, rows, tile), BF16),
             jax.ShapeDtypeStruct((embed // 2 + TAIL, packed), BF16),
             jax.ShapeDtypeStruct((embed // 2, packed), F32),
         ],
-        compiler_params=params(40, ("arbitrary",)),
+        compiler_params=params(48, ("arbitrary",)),
         cost_estimate=pl.CostEstimate(
             flops=2 * rows * depth * embed, bytes_accessed=2 * depth * embed, transcendentals=0
         ),
         name="project",
-    )(me, offsets, features, weight, ortholog)
+    )(me, offsets, features, ortholog, *([weight] * STREAMS))
 
 
 def make_stage_kernel(seen, arrivals, count, embed):
@@ -239,7 +242,7 @@
             [unpack_sums(sums_ref[k], count, embed) for k in range(sums_ref.shape[0])], axis=0
         )
         total_rows = rows * totals.shape[0]
-        tile = 256
+        tile = 512
         tiles = embed // tile
 
         mean = jnp.sum(totals, axis=0, keepdims=True) * (1.0 / total_rows)
@@ -350,7 +353,7 @@
             jax.ShapeDtypeStruct((1, embed), F32),
         ],
         scratch_shapes=[pltpu.VMEM(square, F32)] * 2 + [pltpu.VMEM(square, BF16)] * 3,
-        compiler_params=params(24),
+        compiler_params=params(32),
         cost_estimate=pl.CostEstimate(
             flops=5 * 2 * embed**3, bytes_accessed=2 * embed**2, transcendentals=0
         ),
@@ -359,35 +362,42 @@
 
 
 def contrast_kernel(
-    group_ref, offsets_ref, blocks_ref, mean_ref, whitener_ref, loss_ref, grad_ref, white
+    group_ref, offsets_ref, blocks_ref, mean_ref, whitener_ref, loss_ref, grad_ref, white, others
 ):
     groups, rows, embed = white.shape
     group = group_ref[0]
 
+    @pl.loop(0, groups // 2)
+    def _(pair):
+        centered = [
+            (blocks_ref[2 * pair + side, 0:rows, :].astype(F32) - mean_ref[...]).astype(BF16)
+            for side in range(2)
+        ]
+        value = dot(jnp.concatenate(centered, axis=0), whitener_ref[...]).astype(BF16)
+        for side in range(2):
+            white[2 * pair + side] = value[side * rows : (side + 1) * rows]
+
+    places = lax.broadcasted_iota(jnp.int32, (rows, rows), 0).astype(F32)
+
     @pl.loop(0, groups)
     def _(g):
-        centered = (blocks_ref[g, 0:rows, :].astype(F32) - mean_ref[...]).astype(BF16)
-        white[g] = dot(centered, whitener_ref[...]).astype(BF16)
-
-    places = lax.broadcasted_iota(jnp.int32, (rows, rows), 0).astype(F32)
-
-    @pl.loop(0, groups)
-    def _(g):
-        own = white[g]
         table = blocks_ref[g, rows:, :].astype(F32)
+        for k in range(PARTNERS):
+            others[k * rows : (k + 1) * rows, :] = white[(g + offsets_ref[g, k]) % groups]
+        logits = dot(others[...], white[g], (1, 1)) * LOGIT_SCALE
         loss = jnp.zeros((1, rows), F32)
-        grad = jnp.zeros((rows, embed), F32)
+        weights = []
         for k in range(PARTNERS):
-            other = white[(g + offsets_ref[g, k]) % groups]
-            logits = dot(other, own, (1, 1)) * LOGIT_SCALE
-            peak = jnp.max(logits, axis=0, keepdims=True)
-            powers = jnp.exp(logits - peak)
+            own = logits[k * rows : (k + 1) * rows]
+            peak = jnp.max(own, axis=0, keepdims=True)
+            powers = jnp.exp(own - peak)
             sums = jnp.sum(powers, axis=0, keepdims=True)
             hit = places == table[0:1, k * rows : (k + 1) * rows]
-            picked = jnp.sum(jnp.where(hit, logits, 0.0), axis=0, keepdims=True)
+            picked = jnp.sum(jnp.where(hit, own, 0.0), axis=0, keepdims=True)
             loss = loss + (peak + jnp.log(sums) - picked)
-            weights = (powers * (1.0 / sums) - hit.astype(F32)) * (1.0 / PARTNERS)
-            grad = grad + dot(weights.astype(BF16), other, (0, 0))
+            share = powers * (1.0 / (PARTNERS * sums))
+            weights.append(jnp.where(hit, share - 1.0 / PARTNERS, share).astype(BF16))
+        grad = dot(jnp.concatenate(weights, axis=0), others[...], (0, 0))
         grad_ref[g] = (grad * LOGIT_SCALE).astype(BF16)
 
         @pl.when(g == group)
@@ -406,8 +416,11 @@
             jax.ShapeDtypeStruct((1, rows), F32),
             jax.ShapeDtypeStruct((groups, rows, embed), BF16),
         ],
-        scratch_shapes=[pltpu.VMEM((groups, rows, embed), BF16)],
-        compiler_params=params(12 + 6 * groups * rows * embed // 2**20),
+        scratch_shapes=[
+            pltpu.VMEM((groups, rows, embed), BF16),
+            pltpu.VMEM((PARTNERS * rows, embed), BF16),
+        ],
+        compiler_params=params(20 + 6 * groups * rows * embed // 2**20),
         cost_estimate=pl.CostEstimate(
             flops=groups * rows * 2 * embed * (embed + 2 * PARTNERS * rows),
             bytes_accessed=4 * groups * rows * embed,
@@ -489,8 +502,12 @@
     window = lax.axis_index("win").astype(jnp.int32)
     me = group * shares + window
 
-    block, slices, send, keep = project(
-        me.reshape(1), partner_offsets, features, proj_weight, ortholog_index.T, groups
+    slices = features.reshape(rows, groups, depth // groups).transpose(1, 0, 2)
+    slices, me_scalar = lax.optimization_barrier((slices, me.reshape(1)))
+    slices = lax.all_to_all(slices, "sp", 0, 0)
+
+    block, send, keep = project(
+        me_scalar, partner_offsets, features, proj_weight, ortholog_index.T
     )
     blocks = lax.all_gather(block, "sp")
 
@@ -530,8 +547,6 @@
     other = xor_permute(part, 1)
 
     other, slices = lax.optimization_barrier((other, slices))
-    slices = lax.all_to_all(slices, "sp", 0, 0)
-
     whitener, mean = whiten(place.reshape(1), sums, part, other, rows, embed)
     offsets = blocks[:, rows + 1, :PARTNERS].astype(jnp.int32)
     loss, grad = contrast(group.reshape(1), offsets, blocks, mean, whitener)

time: 207 us -> 222 us (1.072)
  waiting for transfers between devices: 89.5 us -> 102 us
  local copies, waits for them, and re-layouts: 12.4 us -> 18.1 us
    ppermute x17, waiting for transfers between devices: 52.5 us -> 102 us  [xor_permute(): return lax.ppermute(piece, AXES, [(i, i ^ mask) for i in range(devices)])]
    all_gather x1, waiting for transfers between devices: 37 us -> 0.01 us  [shards(): blocks = lax.all_gather(block, 'sp')]
    reshape x0 -> x1, local copies, waits for them, and re-layouts: none -> 4.07 us  [shards(): slices = features.reshape(rows, groups, depth // groups).transpose(1, 0, 2)]
    pallas_call x1, Pallas kernels: 10.4 us -> 7.16 us  [project(): pl.pallas_call(project_kernel, grid_spec=pltpu.PrefetchScalarGridSpec(num...]
    all_to_all x1, starting transfers between devices: 4.44 us -> 7.26 us  [shards(): slices = lax.all_to_all(slices, 'sp', 0, 0)]
    unnamed x23 -> x28, local copies, waits for them, and re-layouts: 12.4 us -> 14 us
  transfers between devices with their start and end apart: 19 -> 19, of which waited for: 13 -> 11; matrix products, arithmetic and copies ran while one was open for 1% -> 0% of each run, Pallas kernels for 22% -> 9%
where the time goes in v4:
time: 222 us
  waiting for transfers between devices  102 us (46%)
  Pallas kernels  58.4 us (26%)
  starting transfers between devices  27.9 us (13%)
  local copies, waits for them, and re-layouts  18.1 us (8%)
  between operations  14.2 us (6%)
    ppermute x17, waiting for transfers between devices, xor_permute(): return lax.ppermute(piece, AXES, [(i, i ^ mask) for i in range(devices)])  102 us
    pallas_call x1, Pallas kernels, contrast(): pl.pallas_call(contrast_kernel, in_specs=[smem(), smem()] + [vmem()] * 3,...  27.3 us
    ppermute x17, starting transfers between devices, xor_permute(): return lax.ppermute(piece, AXES, [(i, i ^ mask) for i in range(devices)])  20.6 us
    pallas_call x1, Pallas kernels, whiten(): pl.pallas_call(make_whiten_kernel(rows), in_specs=[smem()] + [vmem()] * 3...  16.3 us
    unnamed x28, local copies, waits for them, and re-layouts  14 us
    all_to_all x1, starting transfers between devices, shards(): slices = lax.all_to_all(slices, 'sp', 0, 0)  7.26 us
    pallas_call x1, Pallas kernels, project(): pl.pallas_call(project_kernel, grid_spec=pltpu.PrefetchScalarGridSpec(num...  7.16 us
  transfers between devices with their start and end apart: 19, of which 11 were waited for; matrix products, arithmetic and copies ran while one was open for 0% of the time, Pallas kernels for 9%

profile of v4, /device:TPU:0, one launch (start us, length us, event | category | flops | bytes accessed | tf_op | source)
XLA Modules:
  0.0 221.6 jit_solution(15954349993593421660)
XLA Ops:
  7.2 0.0 all-gather.3.cloned.1.call-start
  7.2 4.1 %copy.12 = bf16[256,4096]{0,1:T(8,128)(2,1)} copy(bf16[256,4096]{1,0:T(8,128)(2,1)} %features_ref.1) | data formatting | bytes 4194304 | tf_op args[0]
  11.3 0.0 copy-start
  11.3 0.0 copy-start.8
  11.3 4.1 %copy.13 = bf16[256,8,512]{2,0,1:T(8,128)(2,1)} copy(bf16[256,8,512]{0,2,1:T(8,128)(2,1)} %bitcast.28) | data formatting | bytes 4194304 | tf_op jit(solution)/shard_map/reshape | solution.py:505
  15.4 0.0 copy-done
  15.4 0.0 copy-done.8
  15.4 0.0 copy-done.9
  15.4 7.2 %project.1 = (bf16[272,1024]{1,0:T(8,128)(2,1)S(1)}, bf16[528,640]{1,0:T(8,128)(2,1)S(1)}, f32[512,640]{1,0:T(8,128)S(1)}) custom-call(s32[1]{0:T(128)} %bitcast.3.me_ref, s32[1,4]{1,0:T(1,128)S(1)} %copy-done.9, bf16[256,4096]{1,0:T(8,128)(2,1)S(1)} %copy-done, s32[4,256]{1,0:T(4,128)S(1)} %bitcast.22, bf16[4096,1024]{1,0:T(8,128)(2,1)} %refs_3_.1, ...), custom_call_target="tpu_custom_call" | custom-call | flops 2147483648 | bytes 8388608 | tf_op jit(solution)/shard_map/project/pallas_call | solution.py:145
  22.5 0.0 copy-start.3
  22.6 0.9 copy-done.3
  23.5 0.8 copy-done.5
  24.3 0.0 all-gather.3.cloned.1.call-update
  24.3 7.3 %all-to-all-start = ((bf16[8,256,512]{2,1,0:T(8,128)(2,1)}), bf16[8,256,512]{2,1,0:T(8,128)(2,1)S(1)}, u32[]{:S(2)}, u32[]{:S(2)}) async-start(bf16[8,256,512]{2,1,0:T(8,128)(2,1)} %bitcast.27), calls=%async_computation | async-start | bytes 4194304 | tf_op jit(solution)/shard_map/all_to_all | solution.py:507
  31.6 0.0 collective-permute-start
  31.6 2.5 %collective-permute-done.refs_0_ = bf16[528,640]{1,0:T(8,128)(2,1)} collective-permute-done((bf16[528,640]{1,0:T(8,128)(2,1)}, bf16[528,640]{1,0:T(8,128)(2,1)}, u32[]{:S(2)}, u32[]{:S(2)}) %collective-permute-start) | collective-permute-done | bytes 675872 | tf_op jit(solution)/shard_map/ppermute | solution.py:45
  34.1 1.1 copy-done.4
  35.2 2.0 stage.2
  37.2 0.7 copy-done.6
  37.9 2.0 collective-permute-start.2
  40.0 1.0 collective-permute-start.3
  41.0 0.6 collective-permute-start.1
  41.5 18.2 %collective-permute-done.2.refs_1_ = bf16[144,640]{1,0:T(8,128)(2,1)S(1)} collective-permute-done((bf16[144,640]{1,0:T(8,128)(2,1)}, bf16[144,640]{1,0:T(8,128)(2,1)S(1)}, u32[]{:S(2)}, u32[]{:S(2)}) %collective-permute-start.2) | collective-permute-done | bytes 184352 | tf_op jit(solution)/shard_map/ppermute | solution.py:45
  59.8 3.3 %collective-permute-done.3.refs_2_ = bf16[144,640]{1,0:T(8,128)(2,1)S(1)} collective-permute-done((bf16[144,640]{1,0:T(8,128)(2,1)}, bf16[144,640]{1,0:T(8,128)(2,1)S(1)}, u32[]{:S(2)}, u32[]{:S(2)}) %collective-permute-start.3) | collective-permute-done | bytes 184352 | tf_op jit(solution)/shard_map/ppermute | solution.py:45
  63.1 0.0 collective-permute-done.1.refs_0_
  63.1 1.0 copy-done.7
  64.0 1.0 stage.3
  65.1 2.2 collective-permute-start.5
  67.3 1.5 collective-permute-start.6
  68.7 0.0 collective-permute-start.4
  68.8 52.2 %collective-permute-done.5 = bf16[64,640]{1,0:T(8,128)(2,1)S(1)} collective-permute-done((bf16[64,640]{1,0:T(8,128)(2,1)S(1)}, bf16[64,640]{1,0:T(8,128)(2,1)S(1)}, u32[]{:S(2)}, u32[]{:S(2)}) %collective-permute-start.5) | collective-permute-done | bytes 81952 | tf_op jit(solution)/shard_map/ppermute | solution.py:45
  121.0 0.0 collective-permute-done.6
  121.0 0.0 collective-permute-done.4
  121.0 0.1 collective-permute-start.9
  121.1 6.5 %collective-permute-start.8 = (bf16[32,640]{1,0:T(8,128)(2,1)S(1)}, bf16[32,640]{1,0:T(8,128)(2,1)S(1)}, u32[]{:S(2)}, u32[]{:S(2)}) collective-permute-start(bf16[32,640]{1,0:T(8,128)(2,1)S(1)} %get-tuple-element.49), channel_id=1, source_target_pairs={{0,16},{1,17},{2,18},{3,19},{4,20},{5,21},{6,22},{7,23},{8,24},{9,... | collective-permute-start | bytes 122888 | tf_op jit(solution)/shard_map/ppermute | solution.py:45
  127.7 0.0 collective-permute-start.7
  127.7 0.3 collective-permute-done.9
  127.9 6.1 %collective-permute-done.8 = bf16[32,640]{1,0:T(8,128)(2,1)S(1)} collective-permute-done((bf16[32,640]{1,0:T(8,128)(2,1)S(1)}, bf16[32,640]{1,0:T(8,128)(2,1)S(1)}, u32[]{:S(2)}, u32[]{:S(2)}) %collective-permute-start.8) | collective-permute-done | bytes 40992 | tf_op jit(solution)/shard_map/ppermute | solution.py:45
  134.1 0.2 collective-permute-done.7
  134.3 1.6 collective-permute-start.12
  135.9 3.1 %collective-permute-start.11 = (bf16[128,640]{1,0:T(8,128)(2,1)S(1)}, bf16[128,640]{1,0:T(8,128)(2,1)S(1)}, u32[]{:S(2)}, u32[]{:S(2)}) collective-permute-start(bf16[128,640]{1,0:T(8,128)(2,1)S(1)} %pad_maximum_fusion.1), channel_id=1, source_target_pairs={{0,4},{1,5},{2,6},{3,7},{4,0},{5,1},{6,2},{7,3},{8,12},{9,13},{10,... | collective-permute-start | bytes 491528 | tf_op jit(solution)/shard_map/ppermute | solution.py:45
  139.0 0.0 collective-permute-start.10
  139.1 5.3 %collective-permute-done.10 = bf16[128,640]{1,0:T(8,128)(2,1)S(1)} collective-permute-done((bf16[128,640]{1,0:T(8,128)(2,1)S(1)}, bf16[128,640]{1,0:T(8,128)(2,1)S(1)}, u32[]{:S(2)}, u32[]{:S(2)}) %collective-permute-start.10) | collective-permute-done | bytes 163872 | tf_op jit(solution)/shard_map/ppermute | solution.py:45
  144.4 0.0 collective-permute-done.11
  144.4 0.0 collective-permute-done.12
  144.5 0.1 collective-permute-start.13
  144.6 2.2 collective-permute-done.13.far_ref
  146.7 0.0 all-to-all-done.features_ref
  146.8 16.3 %whiten.1 = (bf16[1024,1024]{1,0:T(8,128)(2,1)S(1)}, f32[1,1024]{1,0:T(1,128)S(1)}) custom-call(s32[1]{0:T(128)} %bitcast.7.place_ref, bf16[4,32,640]{2,1,0:T(8,128)(2,1)S(1)} %pad_maximum_fusion.sums_ref, bf16[16,32,640]{2,1,0:T(8,128)(2,1)S(1)} %bitcast.24, bf16[16,32,640]{2,1,0:T(8,128)(2,1)} %collective-permute-done.13.far_ref), custom_call_target="tpu_custom_call" | custom-call | flops 10737418240 | bytes 2097152 | tf_op jit(solution)/shard_map/whiten/pallas_call | solution.py:347
  163.0 0.0 copy-start.1
  163.0 1.4 copy-done.1
  164.4 0.7 slice_convert_fusion
  165.1 0.0 copy-start.2
  165.1 1.6 copy-done.2
  166.7 2.3 %copy-done.10 = bf16[2176,1024]{1,0:T(8,128)(2,1)S(1)} copy-done((bf16[2176,1024]{1,0:T(8,128)(2,1)S(1)}, bf16[2176,1024]{1,0:T(8,128)(2,1)}, u32[]{:S(2)}) %copy-start.10) | copy-done | bytes 4456472
  169.0 27.3 %contrast.1 = (f32[1,256]{1,0:T(1,128)}, bf16[8,256,1024]{2,1,0:T(8,128)(2,1)S(1)}) custom-call(s32[1]{0:T(128)} %bitcast.group_ref, s32[8,4]{1,0:T(8,128)S(1)} %bitcast.21, bf16[8,272,1024]{2,1,0:T(8,128)(2,1)S(1)} %bitcast.26, f32[1,1024]{1,0:T(1,128)S(1)} %get-tuple-element.39.mean_ref, bf16[1024,1024]{1,0:T(8,128)(2,1)S(1)} %copy-done.2), custom_call_target="tpu_custom_call" | custom-call | flops 12884901888 | bytes 8388608 | tf_op jit(solution)/shard_map/contrast/pallas_call | solution.py:411
  196.2 2.4 %weight_pieces.1 = (f32[128,1024]{1,0:T(8,128)S(1)}, bf16[128,1024]{1,0:T(8,128)(2,1)S(1)}, bf16[128,1024]{1,0:T(8,128)(2,1)S(1)}, bf16[128,1024]{1,0:T(8,128)(2,1)S(1)}) custom-call(s32[1]{0:T(128)} %bitcast.16.window_ref, bf16[8,256,1024]{2,1,0:T(8,128)(2,1)S(1)} %get-tuple-element.42.grad_ref, bf16[8,256,512]{2,1,0:T(8,128)(2,1)S(1)} %all-to-all-done.features_ref), custom_call_target="tpu_custom_call" | custom-call | flops 2147483648 | bytes 6291456 | tf_op jit(solution)/shard_map/weight_pieces/pallas_call | solution.py:457
  198.7 0.2 collective-permute-start.14
  198.9 1.2 collective-permute-start.15
  200.1 0.5 collective-permute-start.16
  200.6 0.0 collective-permute-done.14.refs_1_
  200.6 7.4 %collective-permute-done.15.refs_2_ = bf16[128,1024]{1,0:T(8,128)(2,1)S(1)} collective-permute-done((bf16[128,1024]{1,0:T(8,128)(2,1)S(1)}, bf16[128,1024]{1,0:T(8,128)(2,1)S(1)}, u32[]{:S(2)}, u32[]{:S(2)}) %collective-permute-start.15) | collective-permute-done | bytes 262176 | tf_op jit(solution)/shard_map/ppermute | solution.py:45
  208.0 4.5 %collective-permute-done.16.refs_3_ = bf16[128,1024]{1,0:T(8,128)(2,1)S(1)} collective-permute-done((bf16[128,1024]{1,0:T(8,128)(2,1)S(1)}, bf16[128,1024]{1,0:T(8,128)(2,1)S(1)}, u32[]{:S(2)}, u32[]{:S(2)}) %collective-permute-start.16) | collective-permute-done | bytes 262176 | tf_op jit(solution)/shard_map/ppermute | solution.py:45
  212.5 2.3 %finish.1 = f32[128,1024]{1,0:T(8,128)} custom-call(f32[128,1024]{1,0:T(8,128)S(1)} %get-tuple-element.44.refs_0_, bf16[128,1024]{1,0:T(8,128)(2,1)S(1)} %collective-permute-done.14.refs_1_, bf16[128,1024]{1,0:T(8,128)(2,1)S(1)} %collective-permute-done.15.refs_2_, bf16[128,1024]{1,0:T(8,128)(2,1)S(1)} %collective-permute-done.16.refs_3_, ...), custom_call_target="tpu_custom_call" | custom-call | tf_op jit(solution)/shard_map/finish/pallas_call | solution.py:485
  (17 shorter events, 0.2 us)
Async XLA Ops:
  7.2 157.2 %all-gather.3.cloned.1.call-start = ((), (), s32[]{:S(2)}) async-start(), calls=%async_computation.1 | async-start | bytes 5013504 | tf_op jit(solution)/shard_map/all_gather | solution.py:512
  11.3 4.1 %copy-start = (bf16[256,4096]{1,0:T(8,128)(2,1)S(1)}, bf16[256,4096]{1,0:T(8,128)(2,1)}, u32[]{:S(2)}) copy-start(bf16[256,4096]{1,0:T(8,128)(2,1)} %features_ref.1) | copy-start | bytes 6291460
  11.3 4.1 %copy-start.8 = (s32[256,4]{0,1:T(4,128)S(1)}, s32[256,4]{0,1:T(4,128)}, u32[]{:S(2)}) copy-start(s32[256,4]{0,1:T(4,128)} %param.7) | copy-start | bytes 12292
  11.3 4.1 %copy-start.9 = (s32[1,4]{1,0:T(1,128)S(1)}, s32[1,4]{1,0:T(1,128)}, u32[]{:S(2)}) copy-start(s32[1,4]{1,0:T(1,128)} %offsets_ref.1) | copy-start | bytes 52
  22.5 0.9 copy-start.3
  23.5 0.8 copy-start.5
  24.3 122.4 %all-to-all-start = ((bf16[8,256,512]{2,1,0:T(8,128)(2,1)}), bf16[8,256,512]{2,1,0:T(8,128)(2,1)S(1)}, u32[]{:S(2)}, u32[]{:S(2)}) async-start(bf16[8,256,512]{2,1,0:T(8,128)(2,1)} %bitcast.27), calls=%async_computation | async-start | bytes 4194304 | tf_op jit(solution)/shard_map/all_to_all | solution.py:507
  31.6 2.5 %collective-permute-start = (bf16[528,640]{1,0:T(8,128)(2,1)}, bf16[528,640]{1,0:T(8,128)(2,1)}, u32[]{:S(2)}, u32[]{:S(2)}) collective-permute-start(bf16[528,640]{1,0:T(8,128)(2,1)} %copy-done.3), channel_id=1, source_target_pairs={{0,1},{1,0},{2,3},{3,2},{4,5},{5,4},{6,7},{7,6},{8,9},{9,8},{10,11... | collective-permute-start | bytes 2027528 | tf_op jit(solution)/shard_map/ppermute | solution.py:45
  34.0 1.1 copy-start.4
  37.2 0.7 copy-start.6
  37.9 21.8 %collective-permute-start.2 = (bf16[144,640]{1,0:T(8,128)(2,1)}, bf16[144,640]{1,0:T(8,128)(2,1)S(1)}, u32[]{:S(2)}, u32[]{:S(2)}) collective-permute-start(bf16[144,640]{1,0:T(8,128)(2,1)} %get-tuple-element.31), channel_id=1, source_target_pairs={{0,4},{1,5},{2,6},{3,7},{4,0},{5,1},{6,2},{7,3},{8,12},{9,13},{10,... | collective-permute-start | bytes 552968 | tf_op jit(solution)/shard_map/ppermute | solution.py:45
  40.0 23.1 %collective-permute-start.3 = (bf16[144,640]{1,0:T(8,128)(2,1)}, bf16[144,640]{1,0:T(8,128)(2,1)S(1)}, u32[]{:S(2)}, u32[]{:S(2)}) collective-permute-start(bf16[144,640]{1,0:T(8,128)(2,1)} %get-tuple-element.32), channel_id=1, source_target_pairs={{0,6},{1,7},{2,4},{3,5},{4,2},{5,3},{6,0},{7,1},{8,14},{9,15},{10,... | collective-permute-start | bytes 552968 | tf_op jit(solution)/shard_map/ppermute | solution.py:45
  41.0 22.1 %collective-permute-start.1 = (bf16[144,640]{1,0:T(8,128)(2,1)}, bf16[144,640]{1,0:T(8,128)(2,1)S(1)}, u32[]{:S(2)}, u32[]{:S(2)}) collective-permute-start(bf16[144,640]{1,0:T(8,128)(2,1)} %get-tuple-element.30.sent_ref), channel_id=1, source_target_pairs={{0,2},{1,3},{2,0},{3,1},{4,6},{5,7},{6,4},{7,5},{8,10},{9,11},{10,... | collective-permute-start | bytes 552968 | tf_op jit(solution)/shard_map/ppermute | solution.py:45
  63.1 1.0 copy-start.7
  65.1 55.9 %collective-permute-start.5 = (bf16[64,640]{1,0:T(8,128)(2,1)S(1)}, bf16[64,640]{1,0:T(8,128)(2,1)S(1)}, u32[]{:S(2)}, u32[]{:S(2)}) collective-permute-start(bf16[64,640]{1,0:T(8,128)(2,1)S(1)} %get-tuple-element.34), channel_id=1, source_target_pairs={{0,16},{1,17},{2,18},{3,19},{4,20},{5,21},{6,22},{7,23},{8,24},{9,... | collective-permute-start | bytes 245768 | tf_op jit(solution)/shard_map/ppermute | solution.py:45
  67.3 53.7 %collective-permute-start.6 = (bf16[64,640]{1,0:T(8,128)(2,1)S(1)}, bf16[64,640]{1,0:T(8,128)(2,1)S(1)}, u32[]{:S(2)}, u32[]{:S(2)}) collective-permute-start(bf16[64,640]{1,0:T(8,128)(2,1)S(1)} %get-tuple-element.35), channel_id=1, source_target_pairs={{0,24},{1,25},{2,26},{3,27},{4,28},{5,29},{6,30},{7,31},{8,16},{9,... | collective-permute-start | bytes 245768 | tf_op jit(solution)/shard_map/ppermute | solution.py:45
  68.7 52.3 %collective-permute-start.4 = (bf16[64,640]{1,0:T(8,128)(2,1)S(1)}, bf16[64,640]{1,0:T(8,128)(2,1)S(1)}, u32[]{:S(2)}, u32[]{:S(2)}) collective-permute-start(bf16[64,640]{1,0:T(8,128)(2,1)S(1)} %get-tuple-element.33), channel_id=1, source_target_pairs={{0,8},{1,9},{2,10},{3,11},{4,12},{5,13},{6,14},{7,15},{8,0},{9,1},... | collective-permute-start | bytes 245768 | tf_op jit(solution)/shard_map/ppermute | solution.py:45
  121.0 6.9 %collective-permute-start.9 = (bf16[32,640]{1,0:T(8,128)(2,1)S(1)}, bf16[32,640]{1,0:T(8,128)(2,1)S(1)}, u32[]{:S(2)}, u32[]{:S(2)}) collective-permute-start(bf16[32,640]{1,0:T(8,128)(2,1)S(1)} %get-tuple-element.49), channel_id=1, source_target_pairs={{0,24},{1,25},{2,26},{3,27},{4,28},{5,29},{6,30},{7,31},{8,16},{9,... | collective-permute-start | bytes 122888 | tf_op jit(solution)/shard_map/ppermute | solution.py:45
  121.1 13.0 %collective-permute-start.8 = (bf16[32,640]{1,0:T(8,128)(2,1)S(1)}, bf16[32,640]{1,0:T(8,128)(2,1)S(1)}, u32[]{:S(2)}, u32[]{:S(2)}) collective-permute-start(bf16[32,640]{1,0:T(8,128)(2,1)S(1)} %get-tuple-element.49), channel_id=1, source_target_pairs={{0,16},{1,17},{2,18},{3,19},{4,20},{5,21},{6,22},{7,23},{8,24},{9,... | collective-permute-start | bytes 122888 | tf_op jit(solution)/shard_map/ppermute | solution.py:45
  127.7 6.6 %collective-permute-start.7 = (bf16[32,640]{1,0:T(8,128)(2,1)S(1)}, bf16[32,640]{1,0:T(8,128)(2,1)S(1)}, u32[]{:S(2)}, u32[]{:S(2)}) collective-permute-start(bf16[32,640]{1,0:T(8,128)(2,1)S(1)} %get-tuple-element.49), channel_id=1, source_target_pairs={{0,8},{1,9},{2,10},{3,11},{4,12},{5,13},{6,14},{7,15},{8,0},{9,1},... | collective-permute-start | bytes 122888 | tf_op jit(solution)/shard_map/ppermute | solution.py:45
  134.3 10.1 %collective-permute-start.12 = (bf16[128,640]{1,0:T(8,128)(2,1)S(1)}, bf16[128,640]{1,0:T(8,128)(2,1)S(1)}, u32[]{:S(2)}, u32[]{:S(2)}) collective-permute-start(bf16[128,640]{1,0:T(8,128)(2,1)S(1)} %pad_maximum_fusion.1), channel_id=1, source_target_pairs={{0,6},{1,7},{2,4},{3,5},{4,2},{5,3},{6,0},{7,1},{8,14},{9,15},{10,... | collective-permute-start | bytes 491528 | tf_op jit(solution)/shard_map/ppermute | solution.py:45
  135.9 8.4 %collective-permute-start.11 = (bf16[128,640]{1,0:T(8,128)(2,1)S(1)}, bf16[128,640]{1,0:T(8,128)(2,1)S(1)}, u32[]{:S(2)}, u32[]{:S(2)}) collective-permute-start(bf16[128,640]{1,0:T(8,128)(2,1)S(1)} %pad_maximum_fusion.1), channel_id=1, source_target_pairs={{0,4},{1,5},{2,6},{3,7},{4,0},{5,1},{6,2},{7,3},{8,12},{9,13},{10,... | collective-permute-start | bytes 491528 | tf_op jit(solution)/shard_map/ppermute | solution.py:45
  139.0 5.3 %collective-permute-start.10 = (bf16[128,640]{1,0:T(8,128)(2,1)S(1)}, bf16[128,640]{1,0:T(8,128)(2,1)S(1)}, u32[]{:S(2)}, u32[]{:S(2)}) collective-permute-start(bf16[128,640]{1,0:T(8,128)(2,1)S(1)} %pad_maximum_fusion.1), channel_id=1, source_target_pairs={{0,2},{1,3},{2,0},{3,1},{4,6},{5,7},{6,4},{7,5},{8,10},{9,11},{10,... | collective-permute-start | bytes 491528 | tf_op jit(solution)/shard_map/ppermute | solution.py:45
  144.5 2.3 %collective-permute-start.13 = (bf16[16,32,640]{2,1,0:T(8,128)(2,1)S(1)}, bf16[16,32,640]{2,1,0:T(8,128)(2,1)}, u32[]{:S(2)}, u32[]{:S(2)}) collective-permute-start(bf16[16,32,640]{2,1,0:T(8,128)(2,1)S(1)} %bitcast.23), channel_id=1, source_target_pairs={{0,1},{1,0},{2,3},{3,2},{4,5},{5,4},{6,7},{7,6},{8,9},{9,8},{10,11... | collective-permute-start | bytes 1966088 | tf_op jit(solution)/shard_map/ppermute | solution.py:45
  163.0 1.4 copy-start.1
  165.1 1.6 copy-start.2
  166.7 2.3 %copy-start.10 = (bf16[2176,1024]{1,0:T(8,128)(2,1)S(1)}, bf16[2176,1024]{1,0:T(8,128)(2,1)}, u32[]{:S(2)}) copy-start(bf16[2176,1024]{1,0:T(8,128)(2,1)} %all-gather.3.cloned.1.call-done) | copy-start | bytes 13369348
  198.7 1.9 collective-permute-start.14
  198.9 9.1 %collective-permute-start.15 = (bf16[128,1024]{1,0:T(8,128)(2,1)S(1)}, bf16[128,1024]{1,0:T(8,128)(2,1)S(1)}, u32[]{:S(2)}, u32[]{:S(2)}) collective-permute-start(bf16[128,1024]{1,0:T(8,128)(2,1)S(1)} %get-tuple-element.46), channel_id=1, source_target_pairs={{0,2},{1,3},{2,0},{3,1},{4,6},{5,7},{6,4},{7,5},{8,10},{9,11},{10,... | collective-permute-start | bytes 786440 | tf_op jit(solution)/shard_map/ppermute | solution.py:45
  200.1 12.5 %collective-permute-start.16 = (bf16[128,1024]{1,0:T(8,128)(2,1)S(1)}, bf16[128,1024]{1,0:T(8,128)(2,1)S(1)}, u32[]{:S(2)}, u32[]{:S(2)}) collective-permute-start(bf16[128,1024]{1,0:T(8,128)(2,1)S(1)} %get-tuple-element.47), channel_id=1, source_target_pairs={{0,3},{1,2},{2,1},{3,0},{4,7},{5,6},{6,5},{7,4},{8,11},{9,10},{10,... | collective-permute-start | bytes 786440 | tf_op jit(solution)/shard_map/ppermute | solution.py:45
Sparse Core Ops, SparseCore 0:
  24.4 120.4 all-gather.2

commit v5 on v4

--- a/solution.py
+++ b/solution.py
@@ -1,3 +1,5 @@
+import functools
+
 import jax
 import jax.numpy as jnp
 from jax import lax
@@ -10,6 +12,7 @@
 AXES = ("sp", "win")
 LANES = 128
 TAIL = 16
+SHARED = 4
 STREAMS = 4
 F32 = jnp.float32
 BF16 = jnp.bfloat16
@@ -71,6 +74,7 @@
 
 
 def project_kernel(
+    chunk,
     me_ref,
     offsets_ref,
     features_ref,
@@ -78,7 +82,9 @@
     *refs,
 ):
     weight_refs = refs[:STREAMS]
-    block_ref, send_ref, keep_ref, acc, wide = refs[STREAMS:]
+    block_ref, send_ref, keep_ref = refs[STREAMS : STREAMS + 3]
+    slice_refs = refs[STREAMS + 3 : -2]
+    acc, wide = refs[-2:]
     step = pl.program_id(0)
     rows, embed = acc.shape
     half, packed = keep_ref.shape
@@ -87,6 +93,17 @@
     @pl.when(step == 0)
     def _():
         acc[...] = jnp.zeros_like(acc)
+
+    tile = features_ref.shape[1]
+    chunks = tile // chunk
+    for number in range(chunks):
+        target = step * chunks + number
+        at = pl.ds(pl.multiple_of(target // SHARED * chunk, chunk), chunk)
+        for k, slice_ref in enumerate(slice_refs):
+
+            @pl.when((target ^ me_ref[1]) % SHARED == k)
+            def _():
+                slice_ref[:, at] = features_ref[:, number * chunk : (number + 1) * chunk]
 
     part = features_ref.shape[1] // STREAMS
     value = acc[...]
@@ -131,7 +148,7 @@
                     out[r * LANES : (r + 1) * LANES, at] = value.astype(out.dtype)
 
 
-def project(me, offsets, features, weight, ortholog):
+def project(me, offsets, features, weight, ortholog, groups):
     rows, depth = features.shape
     embed = weight.shape[1]
     packed = embed // 2 + LANES
@@ -143,7 +160,7 @@
         for j in range(STREAMS)
     ]
     return pl.pallas_call(
-        project_kernel,
+        functools.partial(project_kernel, depth // groups),
         grid_spec=pltpu.PrefetchScalarGridSpec(
             num_scalar_prefetch=2,
             grid=(steps,),
@@ -156,7 +173,8 @@
                 pl.BlockSpec((rows + TAIL, embed), fixed),
                 pl.BlockSpec((embed // 2 + TAIL, packed), fixed),
                 pl.BlockSpec((embed // 2, packed), fixed),
-            ],
+            ]
+            + [pl.BlockSpec((rows, depth // SHARED), fixed)] * SHARED,
             scratch_shapes=[
                 pltpu.VMEM((rows, embed), F32),
                 pltpu.VMEM((rows, embed + packed - LANES), BF16),
@@ -166,8 +184,9 @@
             jax.ShapeDtypeStruct((rows + TAIL, embed), BF16),
             jax.ShapeDtypeStruct((embed // 2 + TAIL, packed), BF16),
             jax.ShapeDtypeStruct((embed // 2, packed), F32),
-        ],
-        compiler_params=params(48, ("arbitrary",)),
+        ]
+        + [jax.ShapeDtypeStruct((rows, depth // SHARED), BF16)] * SHARED,
+        compiler_params=params(24, ("arbitrary",)),
         cost_estimate=pl.CostEstimate(
             flops=2 * rows * depth * embed, bytes_accessed=2 * depth * embed, transcendentals=0
         ),
@@ -379,8 +398,9 @@
 
     places = lax.broadcasted_iota(jnp.int32, (rows, rows), 0).astype(F32)
 
-    @pl.loop(0, groups)
-    def _(g):
+    @pl.loop(0, SHARED)
+    def _(step):
+        g = step ^ group
         table = blocks_ref[g, rows:, :].astype(F32)
         for k in range(PARTNERS):
             others[k * rows : (k + 1) * rows, :] = white[(g + offsets_ref[g, k]) % groups]
@@ -398,9 +418,9 @@
             share = powers * (1.0 / (PARTNERS * sums))
             weights.append(jnp.where(hit, share - 1.0 / PARTNERS, share).astype(BF16))
         grad = dot(jnp.concatenate(weights, axis=0), others[...], (0, 0))
-        grad_ref[g] = (grad * LOGIT_SCALE).astype(BF16)
-
-        @pl.when(g == group)
+        grad_ref[step] = (grad * LOGIT_SCALE).astype(BF16)
+
+        @pl.when(step == 0)
         def _():
             loss_ref[...] = loss * (1.0 / PARTNERS)
 
@@ -414,7 +434,7 @@
         out_specs=[vmem()] * 2,
         out_shape=[
             jax.ShapeDtypeStruct((1, rows), F32),
-            jax.ShapeDtypeStruct((groups, rows, embed), BF16),
+            jax.ShapeDtypeStruct((SHARED, rows, embed), BF16),
         ],
         scratch_shapes=[
             pltpu.VMEM((groups, rows, embed), BF16),
@@ -422,54 +442,81 @@
         ],
         compiler_params=params(20 + 6 * groups * rows * embed // 2**20),
         cost_estimate=pl.CostEstimate(
-            flops=groups * rows * 2 * embed * (embed + 2 * PARTNERS * rows),
+            flops=rows * 2 * embed * (groups * embed + SHARED * 2 * PARTNERS * rows),
             bytes_accessed=4 * groups * rows * embed,
-            transcendentals=groups * PARTNERS * rows * rows,
+            transcendentals=SHARED * PARTNERS * rows * rows,
         ),
         name="contrast",
     )(group, offsets, blocks, mean, whitener)
 
 
-def gather_kernel(window_ref, grad_ref, features_ref, *refs):
-    groups = grad_ref.shape[0]
-    outs, total = refs[:-1], refs[-1]
-    share = outs[0].shape[0]
-    window = window_ref[0]
+def pieces_kernel(bits, shares, place_ref, grad_ref, *refs):
+    feature_refs = refs[:SHARED]
+    keep_ref, send_ref, total = refs[SHARED:]
+    count = 1 << len(bits)
+    share = 2 * keep_ref.shape[0] // count
 
     def columns(at):
-        value = dot(features_ref[0, :, at], grad_ref[0], (0, 0))
-        for k in range(1, groups):
-            value = value + dot(features_ref[k, :, at], grad_ref[k], (0, 0))
+        value = dot(feature_refs[0][:, at], grad_ref[0], (0, 0))
+        for k in range(1, SHARED):
+            value = value + dot(feature_refs[k][:, at], grad_ref[k], (0, 0))
         return value
 
     if share % LANES:
         total[...] = columns(slice(None))
-    for r, out in enumerate(outs):
-        at = pl.ds(pl.multiple_of((window ^ r) * share, share), share)
+    for t in reversed(range(count)):
+        mask = sum(bit for s, bit in enumerate(bits) if t >> (len(bits) - 1 - s) & 1)
+        at = pl.ds(pl.multiple_of((place_ref[0] ^ mask) * share, share), share)
         value = total[at, :] if share % LANES else columns(at)
-        out[...] = value.astype(out.dtype)
-
-
-def weight_pieces(window, grad, feature_slices, shares):
-    groups, rows, embed = grad.shape
-    columns = feature_slices.shape[2]
-    share = columns // shares
+        if t < count // 2:
+            keep_ref[t * share : (t + 1) * share, :] = value
+        else:
+            line = t - count // 2
+            send_ref[line * share : (line + 1) * share, :] = value.astype(BF16)
+
+
+def weight_pieces(place, grad, slices, bits, shares):
+    embed = grad.shape[2]
+    rows, columns = slices[0].shape
+    aligned = (columns >> len(bits)) % LANES == 0
     return pl.pallas_call(
-        gather_kernel,
-        in_specs=[smem()] + [vmem()] * 2,
-        out_specs=[vmem()] * shares,
+        functools.partial(pieces_kernel, bits, shares),
+        in_specs=[smem()] + [vmem()] * (1 + SHARED),
+        out_specs=[vmem()] * 2,
         out_shape=[
-            jax.ShapeDtypeStruct((share, embed), BF16 if r else F32) for r in range(shares)
+            jax.ShapeDtypeStruct((columns // 2, embed), F32),
+            jax.ShapeDtypeStruct((columns // 2, embed), BF16),
         ],
-        scratch_shapes=[pltpu.VMEM((columns if share % LANES else 8, embed), F32)],
+        scratch_shapes=[pltpu.VMEM((8 if aligned else columns, embed), F32)],
         compiler_params=params(24),
         cost_estimate=pl.CostEstimate(
-            flops=groups * rows * 2 * embed * columns,
-            bytes_accessed=2 * groups * rows * (embed + columns),
+            flops=SHARED * rows * 2 * embed * columns,
+            bytes_accessed=2 * SHARED * rows * (embed + columns),
             transcendentals=0,
         ),
         name="weight_pieces",
-    )(window, grad, feature_slices)
+    )(place, grad, *slices)
+
+
+def halve_kernel(keep_ref, arrived_ref, next_ref, send_ref):
+    half = next_ref.shape[0]
+    next_ref[...] = keep_ref[:half, :] + arrived_ref[:half, :].astype(F32)
+    send_ref[...] = (keep_ref[half:, :] + arrived_ref[half:, :].astype(F32)).astype(BF16)
+
+
+def halve(keep, arrived):
+    rows, embed = keep.shape
+    return pl.pallas_call(
+        halve_kernel,
+        in_specs=[vmem()] * 2,
+        out_specs=[vmem()] * 2,
+        out_shape=[
+            jax.ShapeDtypeStruct((rows // 2, embed), F32),
+            jax.ShapeDtypeStruct((rows // 2, embed), BF16),
+        ],
+        compiler_params=params(16),
+        name="halve",
+    )(keep, arrived)
 
 
 def finish_kernel(*refs):
@@ -502,12 +549,8 @@
     window = lax.axis_index("win").astype(jnp.int32)
     me = group * shares + window
 
-    slices = features.reshape(rows, groups, depth // groups).transpose(1, 0, 2)
-    slices, me_scalar = lax.optimization_barrier((slices, me.reshape(1)))
-    slices = lax.all_to_all(slices, "sp", 0, 0)
-
-    block, send, keep = project(
-        me_scalar, partner_offsets, features, proj_weight, ortholog_index.T
+    block, send, keep, *slices = project(
+        jnp.stack([me, group]), partner_offsets, features, proj_weight, ortholog_index.T, groups
     )
     blocks = lax.all_gather(block, "sp")
 
@@ -539,20 +582,30 @@
             part = part + piece[:size].astype(F32)
         sums = jnp.concatenate([sums] + [piece[size:].reshape(sums.shape) for piece in others])
     part = part.astype(BF16)
-    for low, count in reversed(stages):
+    for number, (low, count) in enumerate(reversed(stages)):
+        if number == len(stages) - 1:
+            part, *slices = lax.optimization_barrier((part, *slices))
+            for k in range(1, SHARED):
+                slices[k] = xor_permute(slices[k], k * shares)
         part = jnp.concatenate(
             [part] + [xor_permute(part, r << low) for r in range(1, count)], axis=0
         )
     part = part.reshape(-1, size, part.shape[1])
     other = xor_permute(part, 1)
 
-    other, slices = lax.optimization_barrier((other, slices))
     whitener, mean = whiten(place.reshape(1), sums, part, other, rows, embed)
     offsets = blocks[:, rows + 1, :PARTNERS].astype(jnp.int32)
     loss, grad = contrast(group.reshape(1), offsets, blocks, mean, whitener)
-    pieces = weight_pieces(window.reshape(1), grad, slices, shares)
-    pieces = [pieces[0]] + [xor_permute(pieces[r], r) for r in range(1, shares)]
-    return loss[0], finish(pieces, whitener)
+    bits = [bit for bit in (1 << n for n in range(devices.bit_length() - 1))]
+    bits = [bit for bit in bits if bit < shares or bit >= SHARED * shares]
+    far = group // SHARED * shares + window
+    inner = [bit if bit < shares else bit // SHARED for bit in bits]
+    keep, send = weight_pieces(far.reshape(1), grad, slices, inner, shares)
+    for number, bit in enumerate(bits):
+        arrived = xor_permute(send, bit)
+        if number < len(bits) - 1:
+            keep, send = halve(keep, arrived)
+    return loss[0], finish([keep, arrived], whitener)
 
 
 def solution(mesh):

time: 222 us -> 199 us (0.90)
  Pallas kernels: 58.4 us -> 44.7 us
  local copies, waits for them, and re-layouts: 18.1 us -> 11 us
  waiting for transfers between devices: 102 us -> 99.3 us
    ppermute x17 -> x20, waiting for transfers between devices: 102 us -> 65.7 us  [xor_permute(): return lax.ppermute(piece, AXES, [(i, i ^ mask) for i in range(devices)])]
    all_gather x1, waiting for transfers between devices: 0.01 us -> 33.6 us  [shards(): blocks = lax.all_gather(block, 'sp')]
    pallas_call x1, Pallas kernels: 27.3 us -> 16.7 us  [contrast(): pl.pallas_call(contrast_kernel, in_specs=[smem(), smem()] + [vmem()] * 3,...]
    ppermute x17 -> x20, starting transfers between devices: 20.6 us -> 28.4 us  [xor_permute(): return lax.ppermute(piece, AXES, [(i, i ^ mask) for i in range(devices)])]
    all_to_all x1 -> x0, starting transfers between devices: 7.26 us -> none  [shards(): slices = lax.all_to_all(slices, 'sp', 0, 0)]
    reshape x1 -> x0, local copies, waits for them, and re-layouts: 4.07 us -> none  [shards(): slices = features.reshape(rows, groups, depth // groups).transpose(1, 0, 2)]
    unnamed x28 -> x22, local copies, waits for them, and re-layouts: 14 us -> 11 us
    pallas_call x2, Pallas kernels: 3.06 us -> 0.27 us  [stage(): pl.pallas_call(make_stage_kernel(seen, len(arrived), count, embed), in_sp...]
  transfers between devices with their start and end apart: 19 -> 21, of which waited for: 11 -> 12; matrix products, arithmetic and copies ran while one was open for 0% -> 0% of each run, Pallas kernels for 9% -> 16%
where the time goes in v5:
time: 199 us
  waiting for transfers between devices  99.3 us (50%)
  Pallas kernels  44.7 us (22%)
  starting transfers between devices  28.5 us (14%)
  between operations  14.2 us (7%)
  local copies, waits for them, and re-layouts  11 us (6%)
    ppermute x20, waiting for transfers between devices, xor_permute(): return lax.ppermute(piece, AXES, [(i, i ^ mask) for i in range(devices)])  65.7 us
    all_gather x1, waiting for transfers between devices, shards(): blocks = lax.all_gather(block, 'sp')  33.6 us
    ppermute x20, starting transfers between devices, xor_permute(): return lax.ppermute(piece, AXES, [(i, i ^ mask) for i in range(devices)])  28.4 us
    pallas_call x1, Pallas kernels, contrast(): pl.pallas_call(contrast_kernel, in_specs=[smem(), smem()] + [vmem()] * 3,...  16.7 us
    pallas_call x1, Pallas kernels, whiten(): pl.pallas_call(make_whiten_kernel(rows), in_specs=[smem()] + [vmem()] * 3...  15.2 us
    unnamed x22, local copies, waits for them, and re-layouts  11 us
    pallas_call x1, Pallas kernels, project(): pl.pallas_call(functools.partial(project_kernel, depth // groups), grid_s...  6.17 us
  transfers between devices with their start and end apart: 21, of which 12 were waited for; matrix products, arithmetic and copies ran while one was open for 0% of the time, Pallas kernels for 16%

profile of v5, /device:TPU:0, one launch (start us, length us, event | category | flops | bytes accessed | tf_op | source)
XLA Modules:
  0.0 198.6 jit_solution(18443737829459486984)
XLA Ops:
  7.2 0.0 all-gather.3.cloned.1.call-start
  7.2 0.1 pad_add_fusion.me_ref
  7.3 3.4 %copy-done = bf16[4096,1024]{1,0:T(8,128)(2,1)S(1)} copy-done((bf16[4096,1024]{1,0:T(8,128)(2,1)S(1)}, bf16[4096,1024]{1,0:T(8,128)(2,1)}, u32[]{:S(2)}) %copy-start) | copy-done | bytes 8388632
  10.7 1.6 copy-done.1
  12.3 0.7 copy-done.2
  13.0 0.7 copy-done.3
  13.6 6.2 %project.1 = (bf16[272,1024]{1,0:T(8,128)(2,1)}, bf16[528,640]{1,0:T(8,128)(2,1)S(1)}, f32[512,640]{1,0:T(8,128)S(1)}, bf16[256,1024]{1,0:T(8,128)(2,1)S(1)}, bf...) custom-call(s32[2]{0:T(128)S(1)} %pad_add_fusion.me_ref, ...), custom_call_target="tpu_custom_call" | custom-call | flops 2147483648 | bytes 8388608 | tf_op jit(solution)/shard_map/project/pallas_call | solution.py:162
  19.8 0.8 copy-done.5
  20.6 0.8 copy-done.7
  21.4 0.8 copy-done.9
  22.2 0.0 all-gather.3.cloned.1.call-update
  22.2 0.5 collective-permute-start
  22.7 1.8 collective-permute-done.refs_0_
  24.5 0.2 stage.2
  24.6 2.9 %collective-permute-start.2 = (bf16[144,640]{1,0:T(8,128)(2,1)S(1)}, bf16[144,640]{1,0:T(8,128)(2,1)S(1)}, u32[]{:S(2)}, u32[]{:S(2)}) collective-permute-start(bf16[144,640]{1,0:T(8,128)(2,1)S(1)} %get-tuple-element.37), channel_id=1, source_target_pairs={{0,4},{1,5},{2,6},{3,7},{4,0},{5,1},{6,2},{7,3},{8,12},{9,13},{10,... | collective-permute-start | bytes 552968 | tf_op jit(solution)/shard_map/ppermute | solution.py:48
  27.6 1.5 collective-permute-start.3
  29.1 0.0 collective-permute-start.1
  29.1 3.9 %collective-permute-done.2.refs_1_ = bf16[144,640]{1,0:T(8,128)(2,1)S(1)} collective-permute-done((bf16[144,640]{1,0:T(8,128)(2,1)S(1)}, bf16[144,640]{1,0:T(8,128)(2,1)S(1)}, u32[]{:S(2)}, u32[]{:S(2)}) %collective-permute-start.2) | collective-permute-done | bytes 184352 | tf_op jit(solution)/shard_map/ppermute | solution.py:48
  33.0 6.3 %collective-permute-done.3.refs_2_ = bf16[144,640]{1,0:T(8,128)(2,1)S(1)} collective-permute-done((bf16[144,640]{1,0:T(8,128)(2,1)S(1)}, bf16[144,640]{1,0:T(8,128)(2,1)S(1)}, u32[]{:S(2)}, u32[]{:S(2)}) %collective-permute-start.3) | collective-permute-done | bytes 184352 | tf_op jit(solution)/shard_map/ppermute | solution.py:48
  39.3 0.0 collective-permute-done.1.refs_0_
  39.3 0.1 stage.3
  39.5 2.8 %collective-permute-start.5 = (bf16[64,640]{1,0:T(8,128)(2,1)S(1)}, bf16[64,640]{1,0:T(8,128)(2,1)S(1)}, u32[]{:S(2)}, u32[]{:S(2)}) collective-permute-start(bf16[64,640]{1,0:T(8,128)(2,1)S(1)} %get-tuple-element.40), channel_id=1, source_target_pairs={{0,16},{1,17},{2,18},{3,19},{4,20},{5,21},{6,22},{7,23},{8,24},{9,... | collective-permute-start | bytes 245768 | tf_op jit(solution)/shard_map/ppermute | solution.py:48
  42.3 1.3 collective-permute-start.6
  43.6 0.4 collective-permute-start.4
  44.0 8.6 %collective-permute-done.5 = bf16[64,640]{1,0:T(8,128)(2,1)S(1)} collective-permute-done((bf16[64,640]{1,0:T(8,128)(2,1)S(1)}, bf16[64,640]{1,0:T(8,128)(2,1)S(1)}, u32[]{:S(2)}, u32[]{:S(2)}) %collective-permute-start.5) | collective-permute-done | bytes 81952 | tf_op jit(solution)/shard_map/ppermute | solution.py:48
  52.6 0.0 collective-permute-done.6
  52.6 0.7 collective-permute-done.4
  53.3 3.3 %collective-permute-start.9 = (bf16[32,640]{1,0:T(8,128)(2,1)S(1)}, bf16[32,640]{1,0:T(8,128)(2,1)S(1)}, u32[]{:S(2)}, u32[]{:S(2)}) collective-permute-start(bf16[32,640]{1,0:T(8,128)(2,1)S(1)} %add_convert_fusion), channel_id=1, source_target_pairs={{0,24},{1,25},{2,26},{3,27},{4,28},{5,29},{6,30},{7,31},{8,16},{9,... | collective-permute-start | bytes 122888 | tf_op jit(solution)/shard_map/ppermute | solution.py:48
  56.6 4.1 %collective-permute-start.8 = (bf16[32,640]{1,0:T(8,128)(2,1)S(1)}, bf16[32,640]{1,0:T(8,128)(2,1)S(1)}, u32[]{:S(2)}, u32[]{:S(2)}) collective-permute-start(bf16[32,640]{1,0:T(8,128)(2,1)S(1)} %add_convert_fusion), channel_id=1, source_target_pairs={{0,16},{1,17},{2,18},{3,19},{4,20},{5,21},{6,22},{7,23},{8,24},{9,... | collective-permute-start | bytes 122888 | tf_op jit(solution)/shard_map/ppermute | solution.py:48
  60.7 0.5 collective-permute-start.7
  61.2 0.0 collective-permute-done.9
  61.2 4.5 %collective-permute-done.8 = bf16[32,640]{1,0:T(8,128)(2,1)S(1)} collective-permute-done((bf16[32,640]{1,0:T(8,128)(2,1)S(1)}, bf16[32,640]{1,0:T(8,128)(2,1)S(1)}, u32[]{:S(2)}, u32[]{:S(2)}) %collective-permute-start.8) | collective-permute-done | bytes 40992 | tf_op jit(solution)/shard_map/ppermute | solution.py:48
  65.7 0.0 collective-permute-done.7
  65.7 2.4 %collective-permute-start.12 = (bf16[128,640]{1,0:T(8,128)(2,1)S(1)}, bf16[128,640]{1,0:T(8,128)(2,1)S(1)}, u32[]{:S(2)}, u32[]{:S(2)}) collective-permute-start(bf16[128,640]{1,0:T(8,128)(2,1)S(1)} %pad_maximum_fusion.2), channel_id=1, source_target_pairs={{0,6},{1,7},{2,4},{3,5},{4,2},{5,3},{6,0},{7,1},{8,14},{9,15},{10,... | collective-permute-start | bytes 491528 | tf_op jit(solution)/shard_map/ppermute | solution.py:48
  68.1 0.6 collective-permute-start.11
  68.7 0.6 collective-permute-start.10
  69.2 6.7 %collective-permute-done.12 = bf16[128,640]{1,0:T(8,128)(2,1)S(1)} collective-permute-done((bf16[128,640]{1,0:T(8,128)(2,1)S(1)}, bf16[128,640]{1,0:T(8,128)(2,1)S(1)}, u32[]{:S(2)}, u32[]{:S(2)}) %collective-permute-start.12) | collective-permute-done | bytes 163872 | tf_op jit(solution)/shard_map/ppermute | solution.py:48
  75.9 5.7 %collective-permute-done.11 = bf16[128,640]{1,0:T(8,128)(2,1)S(1)} collective-permute-done((bf16[128,640]{1,0:T(8,128)(2,1)S(1)}, bf16[128,640]{1,0:T(8,128)(2,1)S(1)}, u32[]{:S(2)}, u32[]{:S(2)}) %collective-permute-start.11) | collective-permute-done | bytes 163872 | tf_op jit(solution)/shard_map/ppermute | solution.py:48
  81.6 0.0 collective-permute-done.10
  81.6 0.1 pad_maximum_fusion
  81.7 0.1 collective-permute-start.13
  81.9 2.5 %collective-permute-start.14 = (bf16[256,1024]{1,0:T(8,128)(2,1)}, bf16[256,1024]{1,0:T(8,128)(2,1)}, u32[]{:S(2)}, u32[]{:S(2)}) collective-permute-start(bf16[256,1024]{1,0:T(8,128)(2,1)} %get-tuple-element.53), channel_id=1, source_target_pairs={{0,4},{1,5},{2,6},{3,7},{4,0},{5,1},{6,2},{7,3},{8,12},{9,13},{10,... | collective-permute-start | bytes 1572872 | tf_op jit(solution)/shard_map/ppermute | solution.py:48
  84.4 0.0 copy-done.10
  84.4 0.0 collective-permute-start.15
  84.4 1.5 collective-permute-start.16
  86.0 0.0 collective-permute-done.13.far_ref
  86.0 15.2 %whiten.1 = (bf16[1024,1024]{1,0:T(8,128)(2,1)S(1)}, f32[1,1024]{1,0:T(1,128)S(1)}) custom-call(s32[1]{0:T(128)} %bitcast.5.place_ref, bf16[4,32,640]{2,1,0:T(8,128)(2,1)S(1)} %pad_maximum_fusion.1.sums_ref, bf16[16,32,640]{2,1,0:T(8,128)(2,1)S(1)} %bitcast.20, bf16[16,32,640]{2,1,0:T(8,128)(2,1)S(1)} %collective-permute-done.13.far_ref), custom_call_target="tpu_custom_call" | custom-call | flops 10737418240 | bytes 2097152 | tf_op jit(solution)/shard_map/whiten/pallas_call | solution.py:366
  101.1 33.6 %all-gather.3.cloned.1.call-done = bf16[2176,1024]{1,0:T(8,128)(2,1)} async-done(((bf16[272,1024]{1,0:T(8,128)(2,1)}), bf16[2176,1024]{1,0:T(8,128)(2,1)}) %all-gather.3.cloned.1.call-update) | async-done | bytes 4456464 | tf_op jit(solution)/shard_map/all_gather | solution.py:555
  134.8 0.7 slice_convert_fusion
  135.5 2.3 %copy-done.4 = bf16[2176,1024]{1,0:T(8,128)(2,1)S(1)} copy-done((bf16[2176,1024]{1,0:T(8,128)(2,1)S(1)}, bf16[2176,1024]{1,0:T(8,128)(2,1)}, u32[]{:S(2)}) %copy-start.4) | copy-done | bytes 4456472
  137.8 16.7 %contrast.1 = (f32[1,256]{1,0:T(1,128)}, bf16[4,256,1024]{2,1,0:T(8,128)(2,1)S(1)}) custom-call(s32[1]{0:T(128)} %bitcast.group_ref, s32[8,4]{1,0:T(8,128)S(1)} %bitcast.21, bf16[8,272,1024]{2,1,0:T(8,128)(2,1)S(1)} %bitcast.24, f32[1,1024]{1,0:T(1,128)S(1)} %get-tuple-element.48.mean_ref, bf16[1024,1024]{1,0:T(8,128)(2,1)S(1)} %get-tuple-element.49.whitener_ref.refs_2_), custom_call_target="tpu_custom_call" | custom-call | flops 8589934592 | bytes 8388608 | tf_op jit(solution)/shard_map/contrast/pallas_call | solution.py:431
  154.5 0.0 collective-permute-done.14.refs_1_
  154.5 0.0 collective-permute-done.15.refs_2_
  154.5 0.0 collective-permute-done.16.refs_3_
  154.5 3.8 %weight_pieces.1 = (f32[512,1024]{1,0:T(8,128)S(1)}, bf16[512,1024]{1,0:T(8,128)(2,1)S(1)}) custom-call(s32[1]{0:T(128)} %bitcast.14.place_ref, bf16[4,256,1024]{2,1,0:T(8,128)(2,1)S(1)} %get-tuple-element.51.grad_ref, bf16[256,1024]{1,0:T(8,128)(2,1)S(1)} %copy-done.6, bf16[256,1024]{1,0:T(8,128)(2,1)} %collective-permute-done.14.refs_1_, ...), custom_call_target="tpu_custom_call" | custom-call | flops 2147483648 | bytes 4194304 | tf_op jit(solution)/shard_map/weight_pieces/pallas_call | solution.py:482
  158.3 0.1 collective-permute-start.17
  158.4 2.6 %collective-permute-done.17.arrived_ref = bf16[512,1024]{1,0:T(8,128)(2,1)S(1)} collective-permute-done((bf16[512,1024]{1,0:T(8,128)(2,1)S(1)}, bf16[512,1024]{1,0:T(8,128)(2,1)S(1)}, u32[]{:S(2)}, u32[]{:S(2)}) %collective-permute-start.17) | collective-permute-done | bytes 1048608 | tf_op jit(solution)/shard_map/ppermute | solution.py:48
  161.0 0.2 halve.2
  161.2 0.9 collective-permute-start.18
  162.1 13.1 %collective-permute-done.18.arrived_ref = bf16[256,1024]{1,0:T(8,128)(2,1)S(1)} collective-permute-done((bf16[256,1024]{1,0:T(8,128)(2,1)S(1)}, bf16[256,1024]{1,0:T(8,128)(2,1)S(1)}, u32[]{:S(2)}, u32[]{:S(2)}) %collective-permute-start.18) | collective-permute-done | bytes 524320 | tf_op jit(solution)/shard_map/ppermute | solution.py:48
  175.2 0.1 halve.3
  175.3 2.4 %collective-permute-start.19 = (bf16[128,1024]{1,0:T(8,128)(2,1)S(1)}, bf16[128,1024]{1,0:T(8,128)(2,1)S(1)}, u32[]{:S(2)}, u32[]{:S(2)}) collective-permute-start(bf16[128,1024]{1,0:T(8,128)(2,1)S(1)} %get-tuple-element.61), channel_id=1, source_target_pairs={{0,16},{1,17},{2,18},{3,19},{4,20},{5,21},{6,22},{7,23},{8,24},{9,... | collective-permute-start | bytes 786440 | tf_op jit(solution)/shard_map/ppermute | solution.py:48
  177.7 11.7 %collective-permute-done.19.refs_1_ = bf16[128,1024]{1,0:T(8,128)(2,1)S(1)} collective-permute-done((bf16[128,1024]{1,0:T(8,128)(2,1)S(1)}, bf16[128,1024]{1,0:T(8,128)(2,1)S(1)}, u32[]{:S(2)}, u32[]{:S(2)}) %collective-permute-start.19) | collective-permute-done | bytes 262176 | tf_op jit(solution)/shard_map/ppermute | solution.py:48
  189.4 2.3 %finish.1 = f32[128,1024]{1,0:T(8,128)} custom-call(f32[128,1024]{1,0:T(8,128)S(1)} %get-tuple-element.60.refs_0_, bf16[128,1024]{1,0:T(8,128)(2,1)S(1)} %collective-permute-done.19.refs_1_, bf16[1024,1024]{1,0:T(8,128)(2,1)S(1)} %get-tuple-element.49.whitener_ref.refs_2_), custom_call_target="tpu_custom_call" | custom-call | tf_op jit(solution)/shard_map/finish/pallas_call | solution.py:532
  (20 shorter events, 0.1 us)
Async XLA Ops:
  7.2 127.6 %all-gather.3.cloned.1.call-start = ((), (), s32[]{:S(2)}) async-start(), calls=%async_computation | async-start | bytes 5013504 | tf_op jit(solution)/shard_map/all_gather | solution.py:555
  7.3 3.4 %copy-start = (bf16[4096,1024]{1,0:T(8,128)(2,1)S(1)}, bf16[4096,1024]{1,0:T(8,128)(2,1)}, u32[]{:S(2)}) copy-start(bf16[4096,1024]{1,0:T(8,128)(2,1)} %refs_3_.1) | copy-start | bytes 25165828
  10.7 1.6 copy-start.1
  12.3 0.7 copy-start.2
  13.0 0.7 copy-start.3
  19.8 0.8 copy-start.5
  20.6 0.8 copy-start.7
  21.4 0.8 copy-start.9
  22.2 2.3 %collective-permute-start = (bf16[528,640]{1,0:T(8,128)(2,1)S(1)}, bf16[528,640]{1,0:T(8,128)(2,1)S(1)}, u32[]{:S(2)}, u32[]{:S(2)}) collective-permute-start(bf16[528,640]{1,0:T(8,128)(2,1)S(1)} %get-tuple-element.34.sent_ref), channel_id=1, source_target_pairs={{0,1},{1,0},{2,3},{3,2},{4,5},{5,4},{6,7},{7,6},{8,9},{9,8},{10,11... | collective-permute-start | bytes 2027528 | tf_op jit(solution)/shard_map/ppermute | solution.py:48
  24.6 8.3 %collective-permute-start.2 = (bf16[144,640]{1,0:T(8,128)(2,1)S(1)}, bf16[144,640]{1,0:T(8,128)(2,1)S(1)}, u32[]{:S(2)}, u32[]{:S(2)}) collective-permute-start(bf16[144,640]{1,0:T(8,128)(2,1)S(1)} %get-tuple-element.37), channel_id=1, source_target_pairs={{0,4},{1,5},{2,6},{3,7},{4,0},{5,1},{6,2},{7,3},{8,12},{9,13},{10,... | collective-permute-start | bytes 552968 | tf_op jit(solution)/shard_map/ppermute | solution.py:48
  27.6 11.8 %collective-permute-start.3 = (bf16[144,640]{1,0:T(8,128)(2,1)S(1)}, bf16[144,640]{1,0:T(8,128)(2,1)S(1)}, u32[]{:S(2)}, u32[]{:S(2)}) collective-permute-start(bf16[144,640]{1,0:T(8,128)(2,1)S(1)} %get-tuple-element.38), channel_id=1, source_target_pairs={{0,6},{1,7},{2,4},{3,5},{4,2},{5,3},{6,0},{7,1},{8,14},{9,15},{10,... | collective-permute-start | bytes 552968 | tf_op jit(solution)/shard_map/ppermute | solution.py:48
  29.1 10.3 %collective-permute-start.1 = (bf16[144,640]{1,0:T(8,128)(2,1)S(1)}, bf16[144,640]{1,0:T(8,128)(2,1)S(1)}, u32[]{:S(2)}, u32[]{:S(2)}) collective-permute-start(bf16[144,640]{1,0:T(8,128)(2,1)S(1)} %get-tuple-element.36.sent_ref), channel_id=1, source_target_pairs={{0,2},{1,3},{2,0},{3,1},{4,6},{5,7},{6,4},{7,5},{8,10},{9,11},{10,... | collective-permute-start | bytes 552968 | tf_op jit(solution)/shard_map/ppermute | solution.py:48
  39.4 45.0 %copy-start.10 = (bf16[256,1024]{1,0:T(8,128)(2,1)S(1)}, bf16[256,1024]{1,0:T(8,128)(2,1)}, u32[]{:S(2)}) copy-start(bf16[256,1024]{1,0:T(8,128)(2,1)} %copy-done.9) | copy-start | bytes 1572868
  39.4 45.0 %copy-start.8 = (bf16[256,1024]{1,0:T(8,128)(2,1)S(1)}, bf16[256,1024]{1,0:T(8,128)(2,1)}, u32[]{:S(2)}) copy-start(bf16[256,1024]{1,0:T(8,128)(2,1)} %copy-done.7) | copy-start | bytes 1572868
  39.5 13.2 %collective-permute-start.5 = (bf16[64,640]{1,0:T(8,128)(2,1)S(1)}, bf16[64,640]{1,0:T(8,128)(2,1)S(1)}, u32[]{:S(2)}, u32[]{:S(2)}) collective-permute-start(bf16[64,640]{1,0:T(8,128)(2,1)S(1)} %get-tuple-element.40), channel_id=1, source_target_pairs={{0,16},{1,17},{2,18},{3,19},{4,20},{5,21},{6,22},{7,23},{8,24},{9,... | collective-permute-start | bytes 245768 | tf_op jit(solution)/shard_map/ppermute | solution.py:48
  42.3 10.3 %collective-permute-start.6 = (bf16[64,640]{1,0:T(8,128)(2,1)S(1)}, bf16[64,640]{1,0:T(8,128)(2,1)S(1)}, u32[]{:S(2)}, u32[]{:S(2)}) collective-permute-start(bf16[64,640]{1,0:T(8,128)(2,1)S(1)} %get-tuple-element.41), channel_id=1, source_target_pairs={{0,24},{1,25},{2,26},{3,27},{4,28},{5,29},{6,30},{7,31},{8,16},{9,... | collective-permute-start | bytes 245768 | tf_op jit(solution)/shard_map/ppermute | solution.py:48
  43.6 9.7 %collective-permute-start.4 = (bf16[64,640]{1,0:T(8,128)(2,1)S(1)}, bf16[64,640]{1,0:T(8,128)(2,1)S(1)}, u32[]{:S(2)}, u32[]{:S(2)}) collective-permute-start(bf16[64,640]{1,0:T(8,128)(2,1)S(1)} %get-tuple-element.39), channel_id=1, source_target_pairs={{0,8},{1,9},{2,10},{3,11},{4,12},{5,13},{6,14},{7,15},{8,0},{9,1},... | collective-permute-start | bytes 245768 | tf_op jit(solution)/shard_map/ppermute | solution.py:48
  53.3 7.9 %collective-permute-start.9 = (bf16[32,640]{1,0:T(8,128)(2,1)S(1)}, bf16[32,640]{1,0:T(8,128)(2,1)S(1)}, u32[]{:S(2)}, u32[]{:S(2)}) collective-permute-start(bf16[32,640]{1,0:T(8,128)(2,1)S(1)} %add_convert_fusion), channel_id=1, source_target_pairs={{0,24},{1,25},{2,26},{3,27},{4,28},{5,29},{6,30},{7,31},{8,16},{9,... | collective-permute-start | bytes 122888 | tf_op jit(solution)/shard_map/ppermute | solution.py:48
  56.6 9.1 %collective-permute-start.8 = (bf16[32,640]{1,0:T(8,128)(2,1)S(1)}, bf16[32,640]{1,0:T(8,128)(2,1)S(1)}, u32[]{:S(2)}, u32[]{:S(2)}) collective-permute-start(bf16[32,640]{1,0:T(8,128)(2,1)S(1)} %add_convert_fusion), channel_id=1, source_target_pairs={{0,16},{1,17},{2,18},{3,19},{4,20},{5,21},{6,22},{7,23},{8,24},{9,... | collective-permute-start | bytes 122888 | tf_op jit(solution)/shard_map/ppermute | solution.py:48
  60.7 5.0 %collective-permute-start.7 = (bf16[32,640]{1,0:T(8,128)(2,1)S(1)}, bf16[32,640]{1,0:T(8,128)(2,1)S(1)}, u32[]{:S(2)}, u32[]{:S(2)}) collective-permute-start(bf16[32,640]{1,0:T(8,128)(2,1)S(1)} %add_convert_fusion), channel_id=1, source_target_pairs={{0,8},{1,9},{2,10},{3,11},{4,12},{5,13},{6,14},{7,15},{8,0},{9,1},... | collective-permute-start | bytes 122888 | tf_op jit(solution)/shard_map/ppermute | solution.py:48
  65.7 10.2 %collective-permute-start.12 = (bf16[128,640]{1,0:T(8,128)(2,1)S(1)}, bf16[128,640]{1,0:T(8,128)(2,1)S(1)}, u32[]{:S(2)}, u32[]{:S(2)}) collective-permute-start(bf16[128,640]{1,0:T(8,128)(2,1)S(1)} %pad_maximum_fusion.2), channel_id=1, source_target_pairs={{0,6},{1,7},{2,4},{3,5},{4,2},{5,3},{6,0},{7,1},{8,14},{9,15},{10,... | collective-permute-start | bytes 491528 | tf_op jit(solution)/shard_map/ppermute | solution.py:48
  68.1 13.5 %collective-permute-start.11 = (bf16[128,640]{1,0:T(8,128)(2,1)S(1)}, bf16[128,640]{1,0:T(8,128)(2,1)S(1)}, u32[]{:S(2)}, u32[]{:S(2)}) collective-permute-start(bf16[128,640]{1,0:T(8,128)(2,1)S(1)} %pad_maximum_fusion.2), channel_id=1, source_target_pairs={{0,4},{1,5},{2,6},{3,7},{4,0},{5,1},{6,2},{7,3},{8,12},{9,13},{10,... | collective-permute-start | bytes 491528 | tf_op jit(solution)/shard_map/ppermute | solution.py:48
  68.7 13.0 %collective-permute-start.10 = (bf16[128,640]{1,0:T(8,128)(2,1)S(1)}, bf16[128,640]{1,0:T(8,128)(2,1)S(1)}, u32[]{:S(2)}, u32[]{:S(2)}) collective-permute-start(bf16[128,640]{1,0:T(8,128)(2,1)S(1)} %pad_maximum_fusion.2), channel_id=1, source_target_pairs={{0,2},{1,3},{2,0},{3,1},{4,6},{5,7},{6,4},{7,5},{8,10},{9,11},{10,... | collective-permute-start | bytes 491528 | tf_op jit(solution)/shard_map/ppermute | solution.py:48
  81.7 4.3 %collective-permute-start.13 = (bf16[16,32,640]{2,1,0:T(8,128)(2,1)S(1)}, bf16[16,32,640]{2,1,0:T(8,128)(2,1)S(1)}, u32[]{:S(2)}, u32[]{:S(2)}) collective-permute-start(bf16[16,32,640]{2,1,0:T(8,128)(2,1)S(1)} %bitcast.19), channel_id=1, source_target_pairs={{0,1},{1,0},{2,3},{3,2},{4,5},{5,4},{6,7},{7,6},{8,9},{9,8},{10,11... | collective-permute-start | bytes 1966088 | tf_op jit(solution)/shard_map/ppermute | solution.py:48
  81.9 72.6 %collective-permute-start.14 = (bf16[256,1024]{1,0:T(8,128)(2,1)}, bf16[256,1024]{1,0:T(8,128)(2,1)}, u32[]{:S(2)}, u32[]{:S(2)}) collective-permute-start(bf16[256,1024]{1,0:T(8,128)(2,1)} %get-tuple-element.53), channel_id=1, source_target_pairs={{0,4},{1,5},{2,6},{3,7},{4,0},{5,1},{6,2},{7,3},{8,12},{9,13},{10,... | collective-permute-start | bytes 1572872 | tf_op jit(solution)/shard_map/ppermute | solution.py:48
  84.4 70.1 %collective-permute-start.15 = (bf16[256,1024]{1,0:T(8,128)(2,1)S(1)}, bf16[256,1024]{1,0:T(8,128)(2,1)}, u32[]{:S(2)}, u32[]{:S(2)}) collective-permute-start(bf16[256,1024]{1,0:T(8,128)(2,1)S(1)} %copy-done.10), channel_id=1, source_target_pairs={{0,8},{1,9},{2,10},{3,11},{4,12},{5,13},{6,14},{7,15},{8,0},{9,1},... | collective-permute-start | bytes 1572872 | tf_op jit(solution)/shard_map/ppermute | solution.py:48
  84.4 70.1 %collective-permute-start.16 = (bf16[256,1024]{1,0:T(8,128)(2,1)S(1)}, bf16[256,1024]{1,0:T(8,128)(2,1)}, u32[]{:S(2)}, u32[]{:S(2)}) collective-permute-start(bf16[256,1024]{1,0:T(8,128)(2,1)S(1)} %copy-done.8), channel_id=1, source_target_pairs={{0,12},{1,13},{2,14},{3,15},{4,8},{5,9},{6,10},{7,11},{8,4},{9,5},... | collective-permute-start | bytes 1572872 | tf_op jit(solution)/shard_map/ppermute | solution.py:48
  135.5 2.3 %copy-start.4 = (bf16[2176,1024]{1,0:T(8,128)(2,1)S(1)}, bf16[2176,1024]{1,0:T(8,128)(2,1)}, u32[]{:S(2)}) copy-start(bf16[2176,1024]{1,0:T(8,128)(2,1)} %all-gather.3.cloned.1.call-done) | copy-start | bytes 13369348
  137.8 16.8 %copy-start.6 = (bf16[256,1024]{1,0:T(8,128)(2,1)S(1)}, bf16[256,1024]{1,0:T(8,128)(2,1)}, u32[]{:S(2)}) copy-start(bf16[256,1024]{1,0:T(8,128)(2,1)} %copy-done.5) | copy-start | bytes 1572868
  158.3 2.7 %collective-permute-start.17 = (bf16[512,1024]{1,0:T(8,128)(2,1)S(1)}, bf16[512,1024]{1,0:T(8,128)(2,1)S(1)}, u32[]{:S(2)}, u32[]{:S(2)}) collective-permute-start(bf16[512,1024]{1,0:T(8,128)(2,1)S(1)} %get-tuple-element.57), channel_id=1, source_target_pairs={{0,1},{1,0},{2,3},{3,2},{4,5},{5,4},{6,7},{7,6},{8,9},{9,8},{10,11... | collective-permute-start | bytes 3145736 | tf_op jit(solution)/shard_map/ppermute | solution.py:48
  161.2 14.0 %collective-permute-start.18 = (bf16[256,1024]{1,0:T(8,128)(2,1)S(1)}, bf16[256,1024]{1,0:T(8,128)(2,1)S(1)}, u32[]{:S(2)}, u32[]{:S(2)}) collective-permute-start(bf16[256,1024]{1,0:T(8,128)(2,1)S(1)} %get-tuple-element.59), channel_id=1, source_target_pairs={{0,2},{1,3},{2,0},{3,1},{4,6},{5,7},{6,4},{7,5},{8,10},{9,11},{10,... | collective-permute-start | bytes 1572872 | tf_op jit(solution)/shard_map/ppermute | solution.py:48
  175.3 14.1 %collective-permute-start.19 = (bf16[128,1024]{1,0:T(8,128)(2,1)S(1)}, bf16[128,1024]{1,0:T(8,128)(2,1)S(1)}, u32[]{:S(2)}, u32[]{:S(2)}) collective-permute-start(bf16[128,1024]{1,0:T(8,128)(2,1)S(1)} %get-tuple-element.61), channel_id=1, source_target_pairs={{0,16},{1,17},{2,18},{3,19},{4,20},{5,21},{6,22},{7,23},{8,24},{9,... | collective-permute-start | bytes 786440 | tf_op jit(solution)/shard_map/ppermute | solution.py:48
Sparse Core Ops, SparseCore 0:
  22.3 112.4 all-gather.2

commit v6 on v3

--- a/solution.py
+++ b/solution.py
@@ -10,6 +10,7 @@
 AXES = ("sp", "win")
 LANES = 128
 TAIL = 16
+CHUNKS = 8
 F32 = jnp.float32
 BF16 = jnp.bfloat16
 HIGHEST = lax.Precision.HIGHEST
@@ -72,99 +73,109 @@
 def project_kernel(
     me_ref,
     offsets_ref,
-    features_ref,
-    weight_ref,
-    ortholog_ref,
+    features_hbm,
+    weight_hbm,
+    ortholog_hbm,
     block_ref,
     slices_ref,
     send_ref,
     keep_ref,
-    acc,
+    features_ref,
+    weight_ref,
+    ortholog_ref,
+    means,
     wide,
+    sems,
 ):
-    step = pl.program_id(0)
-    rows, embed = acc.shape
+    groups, rows, columns = slices_ref.shape
+    depth, embed = weight_ref.shape
     half, packed = keep_ref.shape
     blocks = embed // LANES
-
-    @pl.when(step == 0)
-    def _():
-        acc[...] = jnp.zeros_like(acc)
-
-    slices_ref[0] = features_ref[...]
-    acc[...] += dot(features_ref[...], weight_ref[...])
-
-    @pl.when(step == pl.num_programs(0) - 1)
-    def _():
-        projected = acc[...].astype(BF16)
-        block_ref[0:rows, :] = projected
-        line = lax.broadcasted_iota(jnp.int32, (TAIL, embed), 0)
-        lane = lax.broadcasted_iota(jnp.int32, (TAIL, embed), 1)
-        table = jnp.zeros((TAIL, embed), F32)
-        for k in range(PARTNERS):
-            table = jnp.where((line == 1) & (lane == k), offsets_ref[0, k].astype(F32), table)
-        hits = jnp.concatenate(
-            [ortholog_ref[k : k + 1, :].astype(F32) for k in range(PARTNERS)]
-            + ([jnp.zeros((1, embed - PARTNERS * rows), F32)] if embed > PARTNERS * rows else []),
-            axis=1,
+    tile = depth // CHUNKS
+
+    copies = []
+    for n in range(CHUNKS):
+        at = pl.ds(n * tile, tile)
+        copies.append(
+            (
+                pltpu.make_async_copy(features_hbm.at[:, at], features_ref.at[:, at], sems.at[0, n]),
+                pltpu.make_async_copy(weight_hbm.at[at, :], weight_ref.at[at, :], sems.at[1, n]),
+            )
         )
-        block_ref[rows:, :] = jnp.where(line == 0, hits, table).astype(BF16)
-
-        total = jnp.sum(projected.astype(F32), axis=0, keepdims=True)
-        send_ref[half:, :] = pack_sums(total, packed, TAIL)
-        wide[:, :embed] = projected
-        wide[:, embed:] = projected[:, : packed - LANES]
-        ones = jnp.ones((rows, LANES), BF16)
-        acc[0:8, :] = jnp.broadcast_to(total * (1.0 / rows), (8, embed))
-        core = me_ref[0] & 1
-        for side, out in ((0, keep_ref), (1, send_ref)):
-            for r in range(blocks // 2):
-                block = (core ^ side) * (blocks // 2) + r
-                start = pl.multiple_of(block * LANES, LANES)
-                own = wide[:, pl.ds(start, LANES)]
-                gram = dot(own, wide[:, pl.ds(start, packed)], (0, 0))
-                sums = dot(own, ones, (0, 0))
-                for k in range(packed // LANES):
-                    other = pl.multiple_of((block + k) % blocks * LANES, LANES)
-                    at = slice(k * LANES, (k + 1) * LANES)
-                    value = gram[:, at] - sums * acc[0:1, pl.ds(other, LANES)]
-                    out[r * LANES : (r + 1) * LANES, at] = value.astype(out.dtype)
+        for copy in copies[-1]:
+            copy.start()
+    table_copy = pltpu.make_async_copy(ortholog_hbm, ortholog_ref, sems.at[0, CHUNKS])
+    table_copy.start()
+
+    total = jnp.zeros((rows, embed), F32)
+    for n in range(CHUNKS):
+        for copy in copies[n]:
+            copy.wait()
+        at = slice(n * tile, (n + 1) * tile)
+        total = total + dot(features_ref[:, at], weight_ref[at, :])
+    for g in range(groups):
+        slices_ref[g] = features_ref[:, g * columns : (g + 1) * columns]
+    projected = total.astype(BF16)
+    block_ref[0:rows, :] = projected
+
+    table_copy.wait()
+    line = lax.broadcasted_iota(jnp.int32, (TAIL, embed), 0)
+    lane = lax.broadcasted_iota(jnp.int32, (TAIL, embed), 1)
+    table = jnp.zeros((TAIL, embed), F32)
+    for k in range(PARTNERS):
+        table = jnp.where((line == 1) & (lane == k), offsets_ref[0, k].astype(F32), table)
+    hits = jnp.concatenate(
+        [ortholog_ref[k : k + 1, :].astype(F32) for k in range(PARTNERS)]
+        + ([jnp.zeros((1, embed - PARTNERS * rows), F32)] if embed > PARTNERS * rows else []),
+        axis=1,
+    )
+    block_ref[rows:, :] = jnp.where(line == 0, hits, table).astype(BF16)
+
+    sums = jnp.sum(projected.astype(F32), axis=0, keepdims=True)
+    send_ref[half:, :] = pack_sums(sums, packed, TAIL)
+    wide[:, :embed] = projected
+    wide[:, embed:] = projected[:, : packed - LANES]
+    ones = jnp.ones((rows, LANES), BF16)
+    means[...] = jnp.broadcast_to(sums * (1.0 / rows), means.shape)
+    core = me_ref[0] & 1
+    for side, out in ((1, send_ref), (0, keep_ref)):
+        for r in range(blocks // 2):
+            block = (core ^ side) * (blocks // 2) + r
+            start = pl.multiple_of(block * LANES, LANES)
+            own = wide[:, pl.ds(start, LANES)]
+            gram = dot(own, wide[:, pl.ds(start, packed)], (0, 0))
+            sums = dot(own, ones, (0, 0))
+            for k in range(packed // LANES):
+                other = pl.multiple_of((block + k) % blocks * LANES, LANES)
+                at = slice(k * LANES, (k + 1) * LANES)
+                value = gram[:, at] - sums * means[0:1, pl.ds(other, LANES)]
+                out[r * LANES : (r + 1) * LANES, at] = value.astype(out.dtype)
 
 
 def project(me, offsets, features, weight, ortholog, groups):
     rows, depth = features.shape
     embed = weight.shape[1]
     packed = embed // 2 + LANES
-    tile = depth // groups
-    fixed = lambda k, *_: (0, 0)
+    hbm = pl.BlockSpec(memory_space=pltpu.HBM)
     return pl.pallas_call(
         project_kernel,
-        grid_spec=pltpu.PrefetchScalarGridSpec(
-            num_scalar_prefetch=2,
-            grid=(groups,),
-            in_specs=[
-                pl.BlockSpec((rows, tile), lambda k, *_: (0, k)),
-                pl.BlockSpec((tile, embed), lambda k, *_: (k, 0)),
-                pl.BlockSpec((PARTNERS, rows), fixed),
-            ],
-            out_specs=[
-                pl.BlockSpec((rows + TAIL, embed), fixed),
-                pl.BlockSpec((1, rows, tile), lambda k, *_: (k, 0, 0)),
-                pl.BlockSpec((embed // 2 + TAIL, packed), fixed),
-                pl.BlockSpec((embed // 2, packed), fixed),
-            ],
-            scratch_shapes=[
-                pltpu.VMEM((rows, embed), F32),
-                pltpu.VMEM((rows, embed + packed - LANES), BF16),
-            ],
-        ),
+        in_specs=[smem(), smem(), hbm, hbm, hbm],
+        out_specs=[vmem()] * 4,
         out_shape=[
             jax.ShapeDtypeStruct((rows + TAIL, embed), BF16),
-            jax.ShapeDtypeStruct((groups, rows, tile), BF16),
+            jax.ShapeDtypeStruct((groups, rows, depth // groups), BF16),
             jax.ShapeDtypeStruct((embed // 2 + TAIL, packed), BF16),
             jax.ShapeDtypeStruct((embed // 2, packed), F32),
         ],
-        compiler_params=params(40, ("arbitrary",)),
+        scratch_shapes=[
+            pltpu.VMEM((rows, depth), BF16),
+            pltpu.VMEM((depth, embed), BF16),
+            pltpu.VMEM((PARTNERS, rows), jnp.int32),
+            pltpu.VMEM((8, embed), F32),
+            pltpu.VMEM((rows, embed + packed - LANES), BF16),
+            pltpu.SemaphoreType.DMA((2, CHUNKS + 1)),
+        ],
+        compiler_params=params(49),
         cost_estimate=pl.CostEstimate(
             flops=2 * rows * depth * embed, bytes_accessed=2 * depth * embed, transcendentals=0
         ),
@@ -239,7 +250,7 @@
             [unpack_sums(sums_ref[k], count, embed) for k in range(sums_ref.shape[0])], axis=0
         )
         total_rows = rows * totals.shape[0]
-        tile = 256
+        tile = 512
         tiles = embed // tile
 
         mean = jnp.sum(totals, axis=0, keepdims=True) * (1.0 / total_rows)
@@ -251,7 +262,8 @@
         def unpack(source_ref, side):
             for i in range(side * half, (side + 1) * half):
                 for part in range(per_block):
-                    piece = ((i - side * half) * per_block + part) ^ (place & (pieces - 1))
+                    column = (i - side * half) ^ (place % pieces // per_block)
+                    piece = (part ^ (place % per_block)) * half + column
                     wide = source_ref[piece].astype(F32)
                     lines = pl.ds(i * LANES + part * depth, depth)
                     for k in range(half + 1):
@@ -358,36 +370,45 @@
     )(place, sums, near, far)
 
 
-def contrast_kernel(
-    group_ref, offsets_ref, blocks_ref, mean_ref, whitener_ref, loss_ref, grad_ref, white
-):
+def contrast_kernel(group_ref, mean_ref, whitener_ref, *refs):
+    loss_ref, grad_ref, white, others, tables, numbers, offsets_ref, sem = refs[-8:]
+    block_refs = refs[:-8]
     groups, rows, embed = white.shape
     group = group_ref[0]
 
+    for k in range(0, groups, 2):
+        pair = block_refs[k : k + 2]
+        centered = [(ref[0:rows, :].astype(F32) - mean_ref[...]).astype(BF16) for ref in pair]
+        value = dot(jnp.concatenate(centered, axis=0), whitener_ref[...]).astype(BF16)
+        for side, ref in enumerate(pair):
+            white[group ^ (k + side)] = value[side * rows : (side + 1) * rows]
+            table = ref[rows:, :].astype(F32)[0:8]
+            tables[group ^ (k + side)] = table
+            numbers[group ^ (k + side)] = table[:, 0:LANES].astype(jnp.int32)
+    copy = pltpu.make_async_copy(numbers, offsets_ref, sem)
+    copy.start()
+    copy.wait()
+
+    places = lax.broadcasted_iota(jnp.int32, (rows, rows), 0).astype(F32)
+
     @pl.loop(0, groups)
     def _(g):
-        centered = (blocks_ref[g, 0:rows, :].astype(F32) - mean_ref[...]).astype(BF16)
-        white[g] = dot(centered, whitener_ref[...]).astype(BF16)
-
-    places = lax.broadcasted_iota(jnp.int32, (rows, rows), 0).astype(F32)
-
-    @pl.loop(0, groups)
-    def _(g):
-        own = white[g]
-        table = blocks_ref[g, rows:, :].astype(F32)
+        for k in range(PARTNERS):
+            others[k * rows : (k + 1) * rows, :] = white[(g + offsets_ref[g, 1, k]) % groups]
+        logits = dot(others[...], white[g], (1, 1)) * LOGIT_SCALE
         loss = jnp.zeros((1, rows), F32)
-        grad = jnp.zeros((rows, embed), F32)
+        weights = []
         for k in range(PARTNERS):
-            other = white[(g + offsets_ref[g, k]) % groups]
-            logits = dot(other, own, (1, 1)) * LOGIT_SCALE
-            peak = jnp.max(logits, axis=0, keepdims=True)
-            powers = jnp.exp(logits - peak)
+            own = logits[k * rows : (k + 1) * rows]
+            peak = jnp.max(own, axis=0, keepdims=True)
+            powers = jnp.exp(own - peak)
             sums = jnp.sum(powers, axis=0, keepdims=True)
-            hit = places == table[0:1, k * rows : (k + 1) * rows]
-            picked = jnp.sum(jnp.where(hit, logits, 0.0), axis=0, keepdims=True)
+            hit = places == tables[g, 0:1, k * rows : (k + 1) * rows]
+            picked = jnp.sum(jnp.where(hit, own, 0.0), axis=0, keepdims=True)
             loss = loss + (peak + jnp.log(sums) - picked)
-            weights = (powers * (1.0 / sums) - hit.astype(F32)) * (1.0 / PARTNERS)
-            grad = grad + dot(weights.astype(BF16), other, (0, 0))
+            share = powers * (1.0 / (PARTNERS * sums))
+            weights.append(jnp.where(hit, share - 1.0 / PARTNERS, share).astype(BF16))
+        grad = dot(jnp.concatenate(weights, axis=0), others[...], (0, 0))
         grad_ref[g] = (grad * LOGIT_SCALE).astype(BF16)
 
         @pl.when(g == group)
@@ -395,26 +416,34 @@
             loss_ref[...] = loss * (1.0 / PARTNERS)
 
 
-def contrast(group, offsets, blocks, mean, whitener):
-    groups, rows, embed = blocks.shape
+def contrast(group, blocks, mean, whitener):
+    groups = len(blocks)
+    rows, embed = blocks[0].shape
     rows -= TAIL
     return pl.pallas_call(
         contrast_kernel,
-        in_specs=[smem(), smem()] + [vmem()] * 3,
+        in_specs=[smem()] + [vmem()] * (2 + groups),
         out_specs=[vmem()] * 2,
         out_shape=[
             jax.ShapeDtypeStruct((1, rows), F32),
             jax.ShapeDtypeStruct((groups, rows, embed), BF16),
         ],
-        scratch_shapes=[pltpu.VMEM((groups, rows, embed), BF16)],
-        compiler_params=params(12 + 6 * groups * rows * embed // 2**20),
+        scratch_shapes=[
+            pltpu.VMEM((groups, rows, embed), BF16),
+            pltpu.VMEM((PARTNERS * rows, embed), BF16),
+            pltpu.VMEM((groups, 8, embed), F32),
+            pltpu.VMEM((groups, 8, LANES), jnp.int32),
+            pltpu.SMEM((groups, 8, LANES), jnp.int32),
+            pltpu.SemaphoreType.DMA,
+        ],
+        compiler_params=params(min(58, 12 + 6 * groups * rows * embed // 2**20)),
         cost_estimate=pl.CostEstimate(
             flops=groups * rows * 2 * embed * (embed + 2 * PARTNERS * rows),
             bytes_accessed=4 * groups * rows * embed,
             transcendentals=groups * PARTNERS * rows * rows,
         ),
         name="contrast",
-    )(group, offsets, blocks, mean, whitener)
+    )(group, mean, whitener, *blocks)
 
 
 def gather_kernel(window_ref, grad_ref, features_ref, *refs):
@@ -492,7 +521,16 @@
     block, slices, send, keep = project(
         me.reshape(1), partner_offsets, features, proj_weight, ortholog_index.T, groups
     )
-    blocks = lax.all_gather(block, "sp")
+
+    direct = groups == 8
+    blocks = {0: block}
+    if direct:
+        blocks[4] = xor_permute(block, 4 * shares)
+        blocks[2] = xor_permute(block, 2 * shares)
+    else:
+        gathered = lax.all_gather(block, "sp")
+        for k in range(groups):
+            blocks[k] = lax.dynamic_index_in_dim(gathered, group ^ k, 0, keepdims=False)
 
     arrived = [xor_permute(send, 1)]
     sent = send
@@ -504,6 +542,9 @@
         count = 4
         own = (me >> low) & (count - 1)
         keep, sends, seen = stage(own, keep, sent, arrived, seen, count, embed)
+        if direct and low == 1:
+            *sends, block = lax.optimization_barrier((*sends, block))
+            blocks[1] = xor_permute(block, shares)
         arrived = [xor_permute(piece, (r + 1) << low) for r, piece in enumerate(sends)]
         sent = sends[0]
         stages.append((low, count))
@@ -522,19 +563,27 @@
             part = part + piece[:size].astype(F32)
         sums = jnp.concatenate([sums] + [piece[size:].reshape(sums.shape) for piece in others])
     part = part.astype(BF16)
-    for low, count in reversed(stages):
+    for number, (low, count) in enumerate(stages):
+        if direct and number == 0:
+            part, blocks[4], blocks[2] = lax.optimization_barrier((part, blocks[4], blocks[2]))
+            blocks[6] = xor_permute(blocks[4], 2 * shares)
+            blocks[5] = xor_permute(blocks[4], shares)
+            blocks[3] = xor_permute(blocks[2], shares)
         part = jnp.concatenate(
             [part] + [xor_permute(part, r << low) for r in range(1, count)], axis=0
         )
     part = part.reshape(-1, size, part.shape[1])
+    if direct:
+        part, blocks[6] = lax.optimization_barrier((part, blocks[6]))
+        blocks[7] = xor_permute(blocks[6], shares)
     other = xor_permute(part, 1)
 
     other, slices = lax.optimization_barrier((other, slices))
     slices = lax.all_to_all(slices, "sp", 0, 0)
 
     whitener, mean = whiten(place.reshape(1), sums, part, other, rows, embed)
-    offsets = blocks[:, rows + 1, :PARTNERS].astype(jnp.int32)
-    loss, grad = contrast(group.reshape(1), offsets, blocks, mean, whitener)
+    blocks = [blocks[k] for k in range(groups)]
+    loss, grad = contrast(group.reshape(1), blocks, mean, whitener)
     pieces = weight_pieces(window.reshape(1), grad, slices, shares)
     pieces = [pieces[0]] + [xor_permute(pieces[r], r) for r in range(1, shares)]
     return loss[0], finish(pieces, whitener)

time: 207 us -> 209 us (level)
  waiting for transfers between devices: 89.5 us -> 107 us
  between operations: 14.1 us -> 0.84 us
  starting transfers between devices: 27.2 us -> 33.9 us
  local copies, waits for them, and re-layouts: 12.4 us -> 9.35 us
  Pallas kernels: 59.7 us -> 57.2 us
  other arithmetic: 2.22 us -> 0.06 us
    ppermute x17 -> x24, waiting for transfers between devices: 52.5 us -> 107 us  [xor_permute(): return lax.ppermute(piece, AXES, [(i, i ^ mask) for i in range(devices)])]
    all_gather x1 -> x0, waiting for transfers between devices: 37 us -> none  [shards(): blocks = lax.all_gather(block, 'sp')]
    ppermute x17 -> x24, starting transfers between devices: 22.7 us -> 29.6 us  [xor_permute(): return lax.ppermute(piece, AXES, [(i, i ^ mask) for i in range(devices)])]
    unnamed x23 -> x27, local copies, waits for them, and re-layouts: 12.4 us -> 6.97 us
    another operation x1 -> x4, local copies, waits for them, and re-layouts: 0.01 us -> 2.35 us  [shards(): sums = jnp.stack([sent[size:]] + [piece[size:] for piece in arrived])]
  transfers between devices with their start and end apart: 19 -> 25, of which waited for: 13 -> 13; matrix products, arithmetic and copies ran while one was open for 1% -> 1% of each run, Pallas kernels for 22% -> 22%
where the time goes in v6:
time: 209 us; the launch traced here: 208 us
  waiting for transfers between devices  107 us (51%)
  Pallas kernels  57.2 us (27%)
  starting transfers between devices  33.9 us (16%)
  local copies, waits for them, and re-layouts  9.35 us (4%)
    ppermute x24, waiting for transfers between devices, xor_permute(): return lax.ppermute(piece, AXES, [(i, i ^ mask) for i in range(devices)])  107 us
    ppermute x24, starting transfers between devices, xor_permute(): return lax.ppermute(piece, AXES, [(i, i ^ mask) for i in range(devices)])  29.6 us
    pallas_call x1, Pallas kernels, contrast(): pl.pallas_call(contrast_kernel, in_specs=[smem()] + [vmem()] * (2 + group...  28.7 us
    pallas_call x1, Pallas kernels, whiten(): pl.pallas_call(make_whiten_kernel(rows), in_specs=[smem()] + [vmem()] * 3...  15.3 us
    pallas_call x1, Pallas kernels, project(): pl.pallas_call(project_kernel, in_specs=[smem(), smem(), hbm, hbm, hbm],...  7.59 us
    unnamed x27, local copies, waits for them, and re-layouts  6.97 us
    all_to_all x1, starting transfers between devices, shards(): slices = lax.all_to_all(slices, 'sp', 0, 0)  4.28 us
  transfers between devices with their start and end apart: 25, of which 13 were waited for; matrix products, arithmetic and copies ran while one was open for 1% of the time, Pallas kernels for 22%

profile of v6, /device:TPU:0, one launch (start us, length us, event | category | flops | bytes accessed | tf_op | source)
XLA Modules:
  0.0 208.4 jit_solution(13845610409982711785)
XLA Ops:
  0.7 0.7 copy-done.2
  1.3 0.7 copy-done.3
  2.0 7.6 %project.1 = (bf16[272,1024]{1,0:T(8,128)(2,1)}, bf16[8,256,512]{2,1,0:T(8,128)(2,1)}, bf16[528,640]{1,0:T(8,128)(2,1)S(1)}, f32[512,640]{1,0:T(8,128)S(1)}) custom-call(s32[1]{0:T(128)} %bitcast.4.me_ref, s32[1,4]{1,0:T(1,128)S(1)} %copy-done.3, bf16[256,4096]{1,0:T(8,128)(2,1)} %features_hbm.1, bf16[4096,1024]{1,0:T(8,128)(2,1)} %weight_hbm.1, ...), custom_call_target="tpu_custom_call" | custom-call | flops 2147483648 | bytes 8388608 | tf_op jit(solution)/shard_map/project/pallas_call | solution.py:160
  9.6 0.5 collective-permute-start
  10.1 2.6 %collective-permute-start.8 = (bf16[272,1024]{1,0:T(8,128)(2,1)}, bf16[272,1024]{1,0:T(8,128)(2,1)}, u32[]{:S(2)}, u32[]{:S(2)}) collective-permute-start(bf16[272,1024]{1,0:T(8,128)(2,1)} %get-tuple-element.54.refs_0_), channel_id=1, source_target_pairs={{0,8},{1,9},{2,10},{3,11},{4,12},{5,13},{6,14},{7,15},{8,0},{9,1},... | collective-permute-start | bytes 1671176 | tf_op jit(solution)/shard_map/ppermute | solution.py:45
  12.7 2.6 %collective-permute-start.7 = (bf16[272,1024]{1,0:T(8,128)(2,1)}, bf16[272,1024]{1,0:T(8,128)(2,1)}, u32[]{:S(2)}, u32[]{:S(2)}) collective-permute-start(bf16[272,1024]{1,0:T(8,128)(2,1)} %get-tuple-element.54.refs_0_), channel_id=1, source_target_pairs={{0,16},{1,17},{2,18},{3,19},{4,20},{5,21},{6,22},{7,23},{8,24},{9,... | collective-permute-start | bytes 1671176 | tf_op jit(solution)/shard_map/ppermute | solution.py:45
  15.3 0.0 collective-permute-done.refs_0_
  15.3 0.8 stage.2
  16.1 1.5 collective-permute-start.2
  17.6 1.5 collective-permute-start.3
  19.1 0.5 collective-permute-start.1
  19.6 4.2 %collective-permute-done.2.refs_1_ = bf16[144,640]{1,0:T(8,128)(2,1)S(1)} collective-permute-done((bf16[144,640]{1,0:T(8,128)(2,1)}, bf16[144,640]{1,0:T(8,128)(2,1)S(1)}, u32[]{:S(2)}, u32[]{:S(2)}) %collective-permute-start.2) | collective-permute-done | bytes 184352 | tf_op jit(solution)/shard_map/ppermute | solution.py:45
  23.9 3.9 %collective-permute-done.3.refs_2_ = bf16[144,640]{1,0:T(8,128)(2,1)S(1)} collective-permute-done((bf16[144,640]{1,0:T(8,128)(2,1)S(1)}, bf16[144,640]{1,0:T(8,128)(2,1)S(1)}, u32[]{:S(2)}, u32[]{:S(2)}) %collective-permute-start.3) | collective-permute-done | bytes 184352 | tf_op jit(solution)/shard_map/ppermute | solution.py:45
  27.8 1.2 collective-permute-done.1.refs_0_
  28.9 0.1 stage.3
  29.0 0.8 collective-permute-start.5
  29.8 2.1 %collective-permute-start.6 = (bf16[64,640]{1,0:T(8,128)(2,1)S(1)}, bf16[64,640]{1,0:T(8,128)(2,1)S(1)}, u32[]{:S(2)}, u32[]{:S(2)}) collective-permute-start(bf16[64,640]{1,0:T(8,128)(2,1)S(1)} %get-tuple-element.45), channel_id=1, source_target_pairs={{0,24},{1,25},{2,26},{3,27},{4,28},{5,29},{6,30},{7,31},{8,16},{9,... | collective-permute-start | bytes 245768 | tf_op jit(solution)/shard_map/ppermute | solution.py:45
  31.9 0.7 collective-permute-start.4
  32.6 13.3 %collective-permute-done.5 = bf16[64,640]{1,0:T(8,128)(2,1)S(1)} collective-permute-done((bf16[64,640]{1,0:T(8,128)(2,1)S(1)}, bf16[64,640]{1,0:T(8,128)(2,1)S(1)}, u32[]{:S(2)}, u32[]{:S(2)}) %collective-permute-start.5) | collective-permute-done | bytes 81952 | tf_op jit(solution)/shard_map/ppermute | solution.py:45
  45.9 0.0 collective-permute-done.6
  45.9 0.0 collective-permute-done.4
  45.9 0.0 collective-permute-done.8.refs_2_
  46.0 0.0 collective-permute-done.7.refs_4_
  46.0 2.5 %collective-permute-start.11 = (bf16[32,640]{1,0:T(8,128)(2,1)S(1)}, bf16[32,640]{1,0:T(8,128)(2,1)S(1)}, u32[]{:S(2)}, u32[]{:S(2)}) collective-permute-start(bf16[32,640]{1,0:T(8,128)(2,1)S(1)} %add_convert_fusion), channel_id=1, source_target_pairs={{0,6},{1,7},{2,4},{3,5},{4,2},{5,3},{6,0},{7,1},{8,14},{9,15},{10,... | collective-permute-start | bytes 122888 | tf_op jit(solution)/shard_map/ppermute | solution.py:45
  48.5 0.5 collective-permute-start.10
  49.0 0.5 collective-permute-start.9
  49.5 2.3 %collective-permute-start.15 = (bf16[272,1024]{1,0:T(8,128)(2,1)}, bf16[272,1024]{1,0:T(8,128)(2,1)S(1)}, u32[]{:S(2)}, u32[]{:S(2)}) collective-permute-start(bf16[272,1024]{1,0:T(8,128)(2,1)} %collective-permute-done.7.refs_4_), channel_id=1, source_target_pairs={{0,8},{1,9},{2,10},{3,11},{4,12},{5,13},{6,14},{7,15},{8,0},{9,1},... | collective-permute-start | bytes 1671176 | tf_op jit(solution)/shard_map/ppermute | solution.py:45
  51.8 1.2 collective-permute-done.9
  53.0 0.0 collective-permute-done.10
  53.1 0.0 collective-permute-done.11
  53.1 2.3 %collective-permute-start.12 = (bf16[128,640]{1,0:T(8,128)(2,1)S(1)}, bf16[128,640]{1,0:T(8,128)(2,1)S(1)}, u32[]{:S(2)}, u32[]{:S(2)}) collective-permute-start(bf16[128,640]{1,0:T(8,128)(2,1)S(1)} %get-tuple-element.64), channel_id=1, source_target_pairs={{0,8},{1,9},{2,10},{3,11},{4,12},{5,13},{6,14},{7,15},{8,0},{9,1},... | collective-permute-start | bytes 491528 | tf_op jit(solution)/shard_map/ppermute | solution.py:45
  55.4 1.5 collective-permute-start.13
  56.9 1.0 collective-permute-start.14
  57.9 14.3 %collective-permute-done.12 = bf16[128,640]{1,0:T(8,128)(2,1)S(1)} collective-permute-done((bf16[128,640]{1,0:T(8,128)(2,1)S(1)}, bf16[128,640]{1,0:T(8,128)(2,1)S(1)}, u32[]{:S(2)}, u32[]{:S(2)}) %collective-permute-start.12) | collective-permute-done | bytes 163872 | tf_op jit(solution)/shard_map/ppermute | solution.py:45
  72.2 0.0 collective-permute-done.13
  72.2 3.8 %collective-permute-done.14 = bf16[128,640]{1,0:T(8,128)(2,1)S(1)} collective-permute-done((bf16[128,640]{1,0:T(8,128)(2,1)S(1)}, bf16[128,640]{1,0:T(8,128)(2,1)S(1)}, u32[]{:S(2)}, u32[]{:S(2)}) %collective-permute-start.14) | collective-permute-done | bytes 163872 | tf_op jit(solution)/shard_map/ppermute | solution.py:45
  76.1 0.0 collective-permute-done.15.refs_6_
  76.1 0.1 collective-permute-start.16
  76.2 2.1 %collective-permute-done.16.far_ref = bf16[16,32,640]{2,1,0:T(8,128)(2,1)S(1)} collective-permute-done((bf16[16,32,640]{2,1,0:T(8,128)(2,1)S(1)}, bf16[16,32,640]{2,1,0:T(8,128)(2,1)S(1)}, u32[]{:S(2)}, u32[]{:S(2)}) %collective-permute-start.16) | collective-permute-done | bytes 655392 | tf_op jit(solution)/shard_map/ppermute | solution.py:45
  78.3 4.3 %all-to-all-start = ((bf16[8,256,512]{2,1,0:T(8,128)(2,1)}), bf16[8,256,512]{2,1,0:T(8,128)(2,1)S(1)}, u32[]{:S(2)}, u32[]{:S(2)}) async-start(bf16[8,256,512]{2,1,0:T(8,128)(2,1)} %get-tuple-element.59), calls=%async_computation | async-start | bytes 4194304 | tf_op jit(solution)/shard_map/all_to_all | solution.py:582
  82.5 2.0 collective-permute-start.17
  84.6 0.1 collective-permute-start.19
  84.6 2.0 collective-permute-start.18
  86.6 0.8 slice_bitcast_fusion.1
  87.4 0.8 slice_bitcast_fusion
  88.2 0.8 slice_bitcast_fusion.2
  89.0 0.1 collective-permute-start.20
  89.1 15.3 %whiten.1 = (bf16[1024,1024]{1,0:T(8,128)(2,1)S(1)}, f32[1,1024]{1,0:T(1,128)S(1)}) custom-call(s32[1]{0:T(128)} %bitcast.1.place_ref, bf16[4,32,640]{2,1,0:T(8,128)(2,1)S(1)} %pad_maximum_fusion.sums_ref, bf16[16,32,640]{2,1,0:T(8,128)(2,1)S(1)} %bitcast.19, bf16[16,32,640]{2,1,0:T(8,128)(2,1)S(1)} %collective-permute-done.16.far_ref), custom_call_target="tpu_custom_call" | custom-call | flops 10737418240 | bytes 2097152 | tf_op jit(solution)/shard_map/whiten/pallas_call | solution.py:356
  104.4 16.3 %collective-permute-done.17.refs_1_ = bf16[272,1024]{1,0:T(8,128)(2,1)S(1)} collective-permute-done((bf16[272,1024]{1,0:T(8,128)(2,1)}, bf16[272,1024]{1,0:T(8,128)(2,1)S(1)}, u32[]{:S(2)}, u32[]{:S(2)}) %collective-permute-start.17) | collective-permute-done | bytes 557088 | tf_op jit(solution)/shard_map/ppermute | solution.py:45
  120.7 23.9 %collective-permute-done.18.refs_3_ = bf16[272,1024]{1,0:T(8,128)(2,1)S(1)} collective-permute-done((bf16[272,1024]{1,0:T(8,128)(2,1)}, bf16[272,1024]{1,0:T(8,128)(2,1)S(1)}, u32[]{:S(2)}, u32[]{:S(2)}) %collective-permute-start.18) | collective-permute-done | bytes 557088 | tf_op jit(solution)/shard_map/ppermute | solution.py:45
  144.6 10.8 %collective-permute-done.20.refs_7_ = bf16[272,1024]{1,0:T(8,128)(2,1)S(1)} collective-permute-done((bf16[272,1024]{1,0:T(8,128)(2,1)}, bf16[272,1024]{1,0:T(8,128)(2,1)S(1)}, u32[]{:S(2)}, u32[]{:S(2)}) %collective-permute-start.20) | collective-permute-done | bytes 557088 | tf_op jit(solution)/shard_map/ppermute | solution.py:45
  155.4 28.7 %contrast.1 = (f32[1,256]{1,0:T(1,128)}, bf16[8,256,1024]{2,1,0:T(8,128)(2,1)S(1)}) custom-call(s32[1]{0:T(128)} %bitcast.group_ref, f32[1,1024]{1,0:T(1,128)S(1)} %get-tuple-element.52.mean_ref, bf16[1024,1024]{1,0:T(8,128)(2,1)S(1)} %get-tuple-element.53.whitener_ref.refs_4_, bf16[272,1024]{1,0:T(8,128)(2,1)} %get-tuple-element.54.refs_0_, ...), custom_call_target="tpu_custom_call" | custom-call | flops 12884901888 | bytes 8388608 | tf_op jit(solution)/shard_map/contrast/pallas_call | solution.py:423
  184.2 1.4 copy-done
  185.5 2.0 copy-done.6
  187.5 0.0 all-to-all-done.features_ref
  187.5 2.2 %copy-done.7 = bf16[8,256,1024]{2,1,0:T(8,128)(2,1)S(1)} copy-done((bf16[8,256,1024]{2,1,0:T(8,128)(2,1)S(1)}, bf16[8,256,1024]{2,1,0:T(8,128)(2,1)}, u32[]{:S(2)}) %copy-start.7) | copy-done | bytes 4194328
  189.7 2.4 %weight_pieces.1 = (f32[128,1024]{1,0:T(8,128)S(1)}, bf16[128,1024]{1,0:T(8,128)(2,1)S(1)}, bf16[128,1024]{1,0:T(8,128)(2,1)S(1)}, bf16[128,1024]{1,0:T(8,128)(2,1)S(1)}) custom-call(s32[1]{0:T(128)} %bitcast.12.window_ref, bf16[8,256,1024]{2,1,0:T(8,128)(2,1)S(1)} %copy-done.7, bf16[8,256,512]{2,1,0:T(8,128)(2,1)S(1)} %all-to-all-done.features_ref), custom_call_target="tpu_custom_call" | custom-call | flops 2147483648 | bytes 6291456 | tf_op jit(solution)/shard_map/weight_pieces/pallas_call | solution.py:473
  192.1 0.1 collective-permute-start.21
  192.2 1.6 collective-permute-start.22
  193.8 0.3 collective-permute-start.23
  194.0 0.0 collective-permute-done.21.refs_1_
  194.1 7.3 %collective-permute-done.22.refs_2_ = bf16[128,1024]{1,0:T(8,128)(2,1)S(1)} collective-permute-done((bf16[128,1024]{1,0:T(8,128)(2,1)S(1)}, bf16[128,1024]{1,0:T(8,128)(2,1)S(1)}, u32[]{:S(2)}, u32[]{:S(2)}) %collective-permute-start.22) | collective-permute-done | bytes 262176 | tf_op jit(solution)/shard_map/ppermute | solution.py:45
  201.4 4.7 %collective-permute-done.23.refs_3_ = bf16[128,1024]{1,0:T(8,128)(2,1)S(1)} collective-permute-done((bf16[128,1024]{1,0:T(8,128)(2,1)S(1)}, bf16[128,1024]{1,0:T(8,128)(2,1)S(1)}, u32[]{:S(2)}, u32[]{:S(2)}) %collective-permute-start.23) | collective-permute-done | bytes 262176 | tf_op jit(solution)/shard_map/ppermute | solution.py:45
  206.1 2.3 %finish.1 = f32[128,1024]{1,0:T(8,128)} custom-call(f32[128,1024]{1,0:T(8,128)S(1)} %get-tuple-element.60.refs_0_, bf16[128,1024]{1,0:T(8,128)(2,1)S(1)} %collective-permute-done.21.refs_1_, bf16[128,1024]{1,0:T(8,128)(2,1)S(1)} %collective-permute-done.22.refs_2_, bf16[128,1024]{1,0:T(8,128)(2,1)S(1)} %collective-permute-done.23.refs_3_, ...), custom_call_target="tpu_custom_call" | custom-call | tf_op jit(solution)/shard_map/finish/pallas_call | solution.py:501
  (28 shorter events, 0.2 us)
Async XLA Ops:
  0.6 0.7 copy-start.2
  1.3 0.7 copy-start.3
  9.6 5.8 %collective-permute-start = (bf16[528,640]{1,0:T(8,128)(2,1)S(1)}, bf16[528,640]{1,0:T(8,128)(2,1)S(1)}, u32[]{:S(2)}, u32[]{:S(2)}) collective-permute-start(bf16[528,640]{1,0:T(8,128)(2,1)S(1)} %get-tuple-element.34.sent_ref), channel_id=1, source_target_pairs={{0,1},{1,0},{2,3},{3,2},{4,5},{5,4},{6,7},{7,6},{8,9},{9,8},{10,11... | collective-permute-start | bytes 2027528 | tf_op jit(solution)/shard_map/ppermute | solution.py:45
  10.1 35.8 %collective-permute-start.8 = (bf16[272,1024]{1,0:T(8,128)(2,1)}, bf16[272,1024]{1,0:T(8,128)(2,1)}, u32[]{:S(2)}, u32[]{:S(2)}) collective-permute-start(bf16[272,1024]{1,0:T(8,128)(2,1)} %get-tuple-element.54.refs_0_), channel_id=1, source_target_pairs={{0,8},{1,9},{2,10},{3,11},{4,12},{5,13},{6,14},{7,15},{8,0},{9,1},... | collective-permute-start | bytes 1671176 | tf_op jit(solution)/shard_map/ppermute | solution.py:45
  12.7 33.2 %collective-permute-start.7 = (bf16[272,1024]{1,0:T(8,128)(2,1)}, bf16[272,1024]{1,0:T(8,128)(2,1)}, u32[]{:S(2)}, u32[]{:S(2)}) collective-permute-start(bf16[272,1024]{1,0:T(8,128)(2,1)} %get-tuple-element.54.refs_0_), channel_id=1, source_target_pairs={{0,16},{1,17},{2,18},{3,19},{4,20},{5,21},{6,22},{7,23},{8,24},{9,... | collective-permute-start | bytes 1671176 | tf_op jit(solution)/shard_map/ppermute | solution.py:45
  16.1 7.7 %collective-permute-start.2 = (bf16[144,640]{1,0:T(8,128)(2,1)}, bf16[144,640]{1,0:T(8,128)(2,1)S(1)}, u32[]{:S(2)}, u32[]{:S(2)}) collective-permute-start(bf16[144,640]{1,0:T(8,128)(2,1)} %get-tuple-element.41), channel_id=1, source_target_pairs={{0,4},{1,5},{2,6},{3,7},{4,0},{5,1},{6,2},{7,3},{8,12},{9,13},{10,... | collective-permute-start | bytes 552968 | tf_op jit(solution)/shard_map/ppermute | solution.py:45
  17.6 10.2 %collective-permute-start.3 = (bf16[144,640]{1,0:T(8,128)(2,1)S(1)}, bf16[144,640]{1,0:T(8,128)(2,1)S(1)}, u32[]{:S(2)}, u32[]{:S(2)}) collective-permute-start(bf16[144,640]{1,0:T(8,128)(2,1)S(1)} %get-tuple-element.42), channel_id=1, source_target_pairs={{0,6},{1,7},{2,4},{3,5},{4,2},{5,3},{6,0},{7,1},{8,14},{9,15},{10,... | collective-permute-start | bytes 552968 | tf_op jit(solution)/shard_map/ppermute | solution.py:45
  19.1 9.8 %collective-permute-start.1 = (bf16[144,640]{1,0:T(8,128)(2,1)S(1)}, bf16[144,640]{1,0:T(8,128)(2,1)S(1)}, u32[]{:S(2)}, u32[]{:S(2)}) collective-permute-start(bf16[144,640]{1,0:T(8,128)(2,1)S(1)} %get-tuple-element.40.sent_ref), channel_id=1, source_target_pairs={{0,2},{1,3},{2,0},{3,1},{4,6},{5,7},{6,4},{7,5},{8,10},{9,11},{10,... | collective-permute-start | bytes 552968 | tf_op jit(solution)/shard_map/ppermute | solution.py:45
  29.0 16.8 %collective-permute-start.5 = (bf16[64,640]{1,0:T(8,128)(2,1)S(1)}, bf16[64,640]{1,0:T(8,128)(2,1)S(1)}, u32[]{:S(2)}, u32[]{:S(2)}) collective-permute-start(bf16[64,640]{1,0:T(8,128)(2,1)S(1)} %get-tuple-element.44), channel_id=1, source_target_pairs={{0,16},{1,17},{2,18},{3,19},{4,20},{5,21},{6,22},{7,23},{8,24},{9,... | collective-permute-start | bytes 245768 | tf_op jit(solution)/shard_map/ppermute | solution.py:45
  29.8 16.1 %collective-permute-start.6 = (bf16[64,640]{1,0:T(8,128)(2,1)S(1)}, bf16[64,640]{1,0:T(8,128)(2,1)S(1)}, u32[]{:S(2)}, u32[]{:S(2)}) collective-permute-start(bf16[64,640]{1,0:T(8,128)(2,1)S(1)} %get-tuple-element.45), channel_id=1, source_target_pairs={{0,24},{1,25},{2,26},{3,27},{4,28},{5,29},{6,30},{7,31},{8,16},{9,... | collective-permute-start | bytes 245768 | tf_op jit(solution)/shard_map/ppermute | solution.py:45
  31.9 14.0 %collective-permute-start.4 = (bf16[64,640]{1,0:T(8,128)(2,1)S(1)}, bf16[64,640]{1,0:T(8,128)(2,1)S(1)}, u32[]{:S(2)}, u32[]{:S(2)}) collective-permute-start(bf16[64,640]{1,0:T(8,128)(2,1)S(1)} %get-tuple-element.43), channel_id=1, source_target_pairs={{0,8},{1,9},{2,10},{3,11},{4,12},{5,13},{6,14},{7,15},{8,0},{9,1},... | collective-permute-start | bytes 245768 | tf_op jit(solution)/shard_map/ppermute | solution.py:45
  45.9 3.6 %copy-start.8 = (bf16[64,640]{1,0:T(8,128)(2,1)}, bf16[64,640]{1,0:T(8,128)(2,1)S(1)}, u32[]{:S(2)}) copy-start(bf16[64,640]{1,0:T(8,128)(2,1)S(1)} %collective-permute-done.5) | copy-start | bytes 245764
  45.9 3.6 %copy-start.9 = (bf16[64,640]{1,0:T(8,128)(2,1)}, bf16[64,640]{1,0:T(8,128)(2,1)S(1)}, u32[]{:S(2)}) copy-start(bf16[64,640]{1,0:T(8,128)(2,1)S(1)} %collective-permute-done.6) | copy-start | bytes 245764
  45.9 3.6 %copy-start.10 = (bf16[64,640]{1,0:T(8,128)(2,1)}, bf16[64,640]{1,0:T(8,128)(2,1)S(1)}, u32[]{:S(2)}) copy-start(bf16[64,640]{1,0:T(8,128)(2,1)S(1)} %collective-permute-done.4) | copy-start | bytes 245764
  46.0 7.1 %collective-permute-start.11 = (bf16[32,640]{1,0:T(8,128)(2,1)S(1)}, bf16[32,640]{1,0:T(8,128)(2,1)S(1)}, u32[]{:S(2)}, u32[]{:S(2)}) collective-permute-start(bf16[32,640]{1,0:T(8,128)(2,1)S(1)} %add_convert_fusion), channel_id=1, source_target_pairs={{0,6},{1,7},{2,4},{3,5},{4,2},{5,3},{6,0},{7,1},{8,14},{9,15},{10,... | collective-permute-start | bytes 122888 | tf_op jit(solution)/shard_map/ppermute | solution.py:45
  48.5 4.6 %collective-permute-start.10 = (bf16[32,640]{1,0:T(8,128)(2,1)S(1)}, bf16[32,640]{1,0:T(8,128)(2,1)S(1)}, u32[]{:S(2)}, u32[]{:S(2)}) collective-permute-start(bf16[32,640]{1,0:T(8,128)(2,1)S(1)} %add_convert_fusion), channel_id=1, source_target_pairs={{0,4},{1,5},{2,6},{3,7},{4,0},{5,1},{6,2},{7,3},{8,12},{9,13},{10,... | collective-permute-start | bytes 122888 | tf_op jit(solution)/shard_map/ppermute | solution.py:45
  49.0 4.0 %collective-permute-start.9 = (bf16[32,640]{1,0:T(8,128)(2,1)S(1)}, bf16[32,640]{1,0:T(8,128)(2,1)S(1)}, u32[]{:S(2)}, u32[]{:S(2)}) collective-permute-start(bf16[32,640]{1,0:T(8,128)(2,1)S(1)} %add_convert_fusion), channel_id=1, source_target_pairs={{0,2},{1,3},{2,0},{3,1},{4,6},{5,7},{6,4},{7,5},{8,10},{9,11},{10,... | collective-permute-start | bytes 122888 | tf_op jit(solution)/shard_map/ppermute | solution.py:45
  49.5 26.5 %collective-permute-start.15 = (bf16[272,1024]{1,0:T(8,128)(2,1)}, bf16[272,1024]{1,0:T(8,128)(2,1)S(1)}, u32[]{:S(2)}, u32[]{:S(2)}) collective-permute-start(bf16[272,1024]{1,0:T(8,128)(2,1)} %collective-permute-done.7.refs_4_), channel_id=1, source_target_pairs={{0,8},{1,9},{2,10},{3,11},{4,12},{5,13},{6,14},{7,15},{8,0},{9,1},... | collective-permute-start | bytes 1671176 | tf_op jit(solution)/shard_map/ppermute | solution.py:45
  53.1 19.0 %collective-permute-start.12 = (bf16[128,640]{1,0:T(8,128)(2,1)S(1)}, bf16[128,640]{1,0:T(8,128)(2,1)S(1)}, u32[]{:S(2)}, u32[]{:S(2)}) collective-permute-start(bf16[128,640]{1,0:T(8,128)(2,1)S(1)} %get-tuple-element.64), channel_id=1, source_target_pairs={{0,8},{1,9},{2,10},{3,11},{4,12},{5,13},{6,14},{7,15},{8,0},{9,1},... | collective-permute-start | bytes 491528 | tf_op jit(solution)/shard_map/ppermute | solution.py:45
  55.4 16.8 %collective-permute-start.13 = (bf16[128,640]{1,0:T(8,128)(2,1)S(1)}, bf16[128,640]{1,0:T(8,128)(2,1)S(1)}, u32[]{:S(2)}, u32[]{:S(2)}) collective-permute-start(bf16[128,640]{1,0:T(8,128)(2,1)S(1)} %get-tuple-element.64), channel_id=1, source_target_pairs={{0,16},{1,17},{2,18},{3,19},{4,20},{5,21},{6,22},{7,23},{8,24},{9,... | collective-permute-start | bytes 491528 | tf_op jit(solution)/shard_map/ppermute | solution.py:45
  56.9 19.2 %collective-permute-start.14 = (bf16[128,640]{1,0:T(8,128)(2,1)S(1)}, bf16[128,640]{1,0:T(8,128)(2,1)S(1)}, u32[]{:S(2)}, u32[]{:S(2)}) collective-permute-start(bf16[128,640]{1,0:T(8,128)(2,1)S(1)} %get-tuple-element.64), channel_id=1, source_target_pairs={{0,24},{1,25},{2,26},{3,27},{4,28},{5,29},{6,30},{7,31},{8,16},{9,... | collective-permute-start | bytes 491528 | tf_op jit(solution)/shard_map/ppermute | solution.py:45
  76.1 2.2 %copy-start.4 = (bf16[272,1024]{1,0:T(8,128)(2,1)}, bf16[272,1024]{1,0:T(8,128)(2,1)S(1)}, u32[]{:S(2)}) copy-start(bf16[272,1024]{1,0:T(8,128)(2,1)S(1)} %collective-permute-done.15.refs_6_) | copy-start | bytes 1671172
  76.1 2.2 %collective-permute-start.16 = (bf16[16,32,640]{2,1,0:T(8,128)(2,1)S(1)}, bf16[16,32,640]{2,1,0:T(8,128)(2,1)S(1)}, u32[]{:S(2)}, u32[]{:S(2)}) collective-permute-start(bf16[16,32,640]{2,1,0:T(8,128)(2,1)S(1)} %bitcast.18), channel_id=1, source_target_pairs={{0,1},{1,0},{2,3},{3,2},{4,5},{5,4},{6,7},{7,6},{8,9},{9,8},{10,11... | collective-permute-start | bytes 1966088 | tf_op jit(solution)/shard_map/ppermute | solution.py:45
  78.3 109.2 %all-to-all-start = ((bf16[8,256,512]{2,1,0:T(8,128)(2,1)}), bf16[8,256,512]{2,1,0:T(8,128)(2,1)S(1)}, u32[]{:S(2)}, u32[]{:S(2)}) async-start(bf16[8,256,512]{2,1,0:T(8,128)(2,1)} %get-tuple-element.59), calls=%async_computation | async-start | bytes 4194304 | tf_op jit(solution)/shard_map/all_to_all | solution.py:582
  82.5 38.2 %collective-permute-start.17 = (bf16[272,1024]{1,0:T(8,128)(2,1)}, bf16[272,1024]{1,0:T(8,128)(2,1)S(1)}, u32[]{:S(2)}, u32[]{:S(2)}) collective-permute-start(bf16[272,1024]{1,0:T(8,128)(2,1)} %get-tuple-element.54.refs_0_), channel_id=1, source_target_pairs={{0,4},{1,5},{2,6},{3,7},{4,0},{5,1},{6,2},{7,3},{8,12},{9,13},{10,... | collective-permute-start | bytes 1671176 | tf_op jit(solution)/shard_map/ppermute | solution.py:45
  84.6 60.0 %collective-permute-start.19 = (bf16[272,1024]{1,0:T(8,128)(2,1)}, bf16[272,1024]{1,0:T(8,128)(2,1)S(1)}, u32[]{:S(2)}, u32[]{:S(2)}) collective-permute-start(bf16[272,1024]{1,0:T(8,128)(2,1)} %collective-permute-done.7.refs_4_), channel_id=1, source_target_pairs={{0,4},{1,5},{2,6},{3,7},{4,0},{5,1},{6,2},{7,3},{8,12},{9,13},{10,... | collective-permute-start | bytes 1671176 | tf_op jit(solution)/shard_map/ppermute | solution.py:45
  84.6 60.0 %collective-permute-start.18 = (bf16[272,1024]{1,0:T(8,128)(2,1)}, bf16[272,1024]{1,0:T(8,128)(2,1)S(1)}, u32[]{:S(2)}, u32[]{:S(2)}) collective-permute-start(bf16[272,1024]{1,0:T(8,128)(2,1)} %collective-permute-done.8.refs_2_), channel_id=1, source_target_pairs={{0,4},{1,5},{2,6},{3,7},{4,0},{5,1},{6,2},{7,3},{8,12},{9,13},{10,... | collective-permute-start | bytes 1671176 | tf_op jit(solution)/shard_map/ppermute | solution.py:45
  89.0 66.4 %collective-permute-start.20 = (bf16[272,1024]{1,0:T(8,128)(2,1)}, bf16[272,1024]{1,0:T(8,128)(2,1)S(1)}, u32[]{:S(2)}, u32[]{:S(2)}) collective-permute-start(bf16[272,1024]{1,0:T(8,128)(2,1)} %copy-done.4), channel_id=1, source_target_pairs={{0,4},{1,5},{2,6},{3,7},{4,0},{5,1},{6,2},{7,3},{8,12},{9,13},{10,... | collective-permute-start | bytes 1671176 | tf_op jit(solution)/shard_map/ppermute | solution.py:45
  89.1 66.3 %copy-start.5 = (bf16[272,1024]{1,0:T(8,128)(2,1)S(1)}, bf16[272,1024]{1,0:T(8,128)(2,1)}, u32[]{:S(2)}) copy-start(bf16[272,1024]{1,0:T(8,128)(2,1)} %copy-done.4) | copy-start | bytes 1671172
  184.2 1.4 copy-start
  185.5 2.0 copy-start.6
  187.5 2.2 %copy-start.7 = (bf16[8,256,1024]{2,1,0:T(8,128)(2,1)S(1)}, bf16[8,256,1024]{2,1,0:T(8,128)(2,1)}, u32[]{:S(2)}) copy-start(bf16[8,256,1024]{2,1,0:T(8,128)(2,1)} %copy-done.6) | copy-start | bytes 12582916
  189.7 16.4 %copy-start.1 = (bf16[1024,1024]{1,0:T(8,128)(2,1)S(1)}, bf16[1024,1024]{1,0:T(8,128)(2,1)}, u32[]{:S(2)}) copy-start(bf16[1024,1024]{1,0:T(8,128)(2,1)} %copy-done) | copy-start | bytes 6291460
  192.1 1.9 collective-permute-start.21
  192.2 9.2 %collective-permute-start.22 = (bf16[128,1024]{1,0:T(8,128)(2,1)S(1)}, bf16[128,1024]{1,0:T(8,128)(2,1)S(1)}, u32[]{:S(2)}, u32[]{:S(2)}) collective-permute-start(bf16[128,1024]{1,0:T(8,128)(2,1)S(1)} %get-tuple-element.62), channel_id=1, source_target_pairs={{0,2},{1,3},{2,0},{3,1},{4,6},{5,7},{6,4},{7,5},{8,10},{9,11},{10,... | collective-permute-start | bytes 786440 | tf_op jit(solution)/shard_map/ppermute | solution.py:45
  193.8 12.3 %collective-permute-start.23 = (bf16[128,1024]{1,0:T(8,128)(2,1)S(1)}, bf16[128,1024]{1,0:T(8,128)(2,1)S(1)}, u32[]{:S(2)}, u32[]{:S(2)}) collective-permute-start(bf16[128,1024]{1,0:T(8,128)(2,1)S(1)} %get-tuple-element.63), channel_id=1, source_target_pairs={{0,3},{1,2},{2,1},{3,0},{4,7},{5,6},{6,5},{7,4},{8,11},{9,10},{10,... | collective-permute-start | bytes 786440 | tf_op jit(solution)/shard_map/ppermute | solution.py:45

commit v7 on v6

--- a/solution.py
+++ b/solution.py
@@ -1,3 +1,5 @@
+import functools
+
 import jax
 import jax.numpy as jnp
 from jax import lax
@@ -50,6 +52,35 @@
     return high, (value - high.astype(F32)).astype(BF16)
 
 
+def cut_kernel(group_ref, features_hbm, near_ref, far_ref, sems):
+    halves, _, columns = near_ref.shape
+    copies = []
+    for r in range(halves):
+        for side, out in ((1, far_ref), (0, near_ref)):
+            start = pl.multiple_of((group_ref[0] ^ (2 * r + side)) * columns, columns)
+            copy = pltpu.make_async_copy(
+                features_hbm.at[:, pl.ds(start, columns)], out.at[r], sems.at[side, r]
+            )
+            copy.start()
+            copies.append(copy)
+    for copy in copies:
+        copy.wait()
+
+
+def cut(group, features, groups):
+    rows, depth = features.shape
+    half = jax.ShapeDtypeStruct((groups // 2, rows, depth // groups), BF16)
+    return pl.pallas_call(
+        cut_kernel,
+        in_specs=[smem(), pl.BlockSpec(memory_space=pltpu.HBM)],
+        out_specs=[vmem()] * 2,
+        out_shape=[half, half],
+        scratch_shapes=[pltpu.SemaphoreType.DMA((2, groups // 2))],
+        compiler_params=params(56),
+        name="cut",
+    )(group, features)
+
+
 def pack_sums(sums, packed, rows):
     high = sums.astype(BF16).astype(F32)
     pad = jnp.zeros((sums.shape[0], 2 * packed - sums.shape[1]), F32)
@@ -77,7 +108,6 @@
     weight_hbm,
     ortholog_hbm,
     block_ref,
-    slices_ref,
     send_ref,
     keep_ref,
     features_ref,
@@ -87,7 +117,7 @@
     wide,
     sems,
 ):
-    groups, rows, columns = slices_ref.shape
+    rows = features_ref.shape[0]
     depth, embed = weight_ref.shape
     half, packed = keep_ref.shape
     blocks = embed // LANES
@@ -113,8 +143,6 @@
             copy.wait()
         at = slice(n * tile, (n + 1) * tile)
         total = total + dot(features_ref[:, at], weight_ref[at, :])
-    for g in range(groups):
-        slices_ref[g] = features_ref[:, g * columns : (g + 1) * columns]
     projected = total.astype(BF16)
     block_ref[0:rows, :] = projected
 
@@ -152,7 +180,7 @@
                 out[r * LANES : (r + 1) * LANES, at] = value.astype(out.dtype)
 
 
-def project(me, offsets, features, weight, ortholog, groups):
+def project(me, offsets, features, weight, ortholog):
     rows, depth = features.shape
     embed = weight.shape[1]
     packed = embed // 2 + LANES
@@ -160,10 +188,9 @@
     return pl.pallas_call(
         project_kernel,
         in_specs=[smem(), smem(), hbm, hbm, hbm],
-        out_specs=[vmem()] * 4,
+        out_specs=[vmem()] * 3,
         out_shape=[
             jax.ShapeDtypeStruct((rows + TAIL, embed), BF16),
-            jax.ShapeDtypeStruct((groups, rows, depth // groups), BF16),
             jax.ShapeDtypeStruct((embed // 2 + TAIL, packed), BF16),
             jax.ShapeDtypeStruct((embed // 2, packed), F32),
         ],
@@ -225,29 +252,28 @@
     return out[0], out[1:], held
 
 
-def make_whiten_kernel(rows):
+def make_whiten_kernel(rows, count):
     def kernel(
         place_ref,
-        sums_ref,
         near_ref,
         far_ref,
-        whitener_ref,
-        mean_ref,
-        scaled,
-        rest,
-        first,
-        left,
-        right,
+        *refs,
     ):
+        sums_refs = refs[:-7]
+        whitener_ref, mean_ref, scaled, rest, first, left, right = refs[-7:]
         place = place_ref[0]
         embed = scaled.shape[0]
         blocks = embed // LANES
         half = blocks // 2
         pieces, depth = near_ref.shape[:2]
         per_block = LANES // depth
-        count = sums_ref.shape[1] // 4
         totals = jnp.concatenate(
-            [unpack_sums(sums_ref[k], count, embed) for k in range(sums_ref.shape[0])], axis=0
+            [
+                unpack_sums(ref[start : start + 4 * count, :], count, embed)
+                for ref in sums_refs
+                for start in range(depth, ref.shape[0], 4 * count)
+            ],
+            axis=0,
         )
         total_rows = rows * totals.shape[0]
         tile = 512
@@ -262,8 +288,7 @@
         def unpack(source_ref, side):
             for i in range(side * half, (side + 1) * half):
                 for part in range(per_block):
-                    column = (i - side * half) ^ (place % pieces // per_block)
-                    piece = (part ^ (place % per_block)) * half + column
+                    piece = ((i - side * half) * per_block + part) ^ (place % pieces)
                     wide = source_ref[piece].astype(F32)
                     lines = pl.ds(i * LANES + part * depth, depth)
                     for k in range(half + 1):
@@ -351,11 +376,11 @@
     return kernel
 
 
-def whiten(place, sums, near, far, rows, embed):
+def whiten(place, near, far, sums, count, rows, embed):
     square = (embed, embed)
     return pl.pallas_call(
-        make_whiten_kernel(rows),
-        in_specs=[smem()] + [vmem()] * 3,
+        make_whiten_kernel(rows, count),
+        in_specs=[smem()] + [vmem()] * (2 + len(sums)),
         out_specs=[vmem(), vmem()],
         out_shape=[
             jax.ShapeDtypeStruct(square, BF16),
@@ -367,12 +392,13 @@
             flops=5 * 2 * embed**3, bytes_accessed=2 * embed**2, transcendentals=0
         ),
         name="whiten",
-    )(place, sums, near, far)
-
-
-def contrast_kernel(group_ref, mean_ref, whitener_ref, *refs):
+    )(place, near, far, *sums)
+
+
+def contrast_kernel(order, group_ref, mean_ref, whitener_ref, *refs):
     loss_ref, grad_ref, white, others, tables, numbers, offsets_ref, sem = refs[-8:]
-    block_refs = refs[:-8]
+    block_refs = [ref.at[i] for ref in refs[:-8] for i in range(ref.shape[0])]
+    block_refs = [block_refs[order.index(k)] for k in range(len(order))]
     groups, rows, embed = white.shape
     group = group_ref[0]
 
@@ -416,13 +442,13 @@
             loss_ref[...] = loss * (1.0 / PARTNERS)
 
 
-def contrast(group, blocks, mean, whitener):
-    groups = len(blocks)
-    rows, embed = blocks[0].shape
+def contrast(group, blocks, order, mean, whitener):
+    groups = len(order)
+    rows, embed = blocks[0].shape[1:]
     rows -= TAIL
     return pl.pallas_call(
-        contrast_kernel,
-        in_specs=[smem()] + [vmem()] * (2 + groups),
+        functools.partial(contrast_kernel, order),
+        in_specs=[smem()] + [vmem()] * (2 + len(blocks)),
         out_specs=[vmem()] * 2,
         out_shape=[
             jax.ShapeDtypeStruct((1, rows), F32),
@@ -446,33 +472,33 @@
     )(group, mean, whitener, *blocks)
 
 
-def gather_kernel(window_ref, grad_ref, features_ref, *refs):
-    groups = grad_ref.shape[0]
-    outs, total = refs[:-1], refs[-1]
+def pieces_kernel(shares, group_ref, window_ref, grad_ref, *refs):
+    groups, _, embed = grad_ref.shape
+    outs, total = refs[-1 - shares : -1], refs[-1]
+    features = [ref.at[i] for ref in refs[: -1 - shares] for i in range(ref.shape[0])]
     share = outs[0].shape[0]
-    window = window_ref[0]
 
     def columns(at):
-        value = dot(features_ref[0, :, at], grad_ref[0], (0, 0))
+        value = dot(features[0][:, at], grad_ref[group_ref[0]], (0, 0))
         for k in range(1, groups):
-            value = value + dot(features_ref[k, :, at], grad_ref[k], (0, 0))
+            value = value + dot(features[k][:, at], grad_ref[group_ref[0] ^ k], (0, 0))
         return value
 
     if share % LANES:
         total[...] = columns(slice(None))
     for r, out in enumerate(outs):
-        at = pl.ds(pl.multiple_of((window ^ r) * share, share), share)
+        at = pl.ds(pl.multiple_of((window_ref[0] ^ r) * share, share), share)
         value = total[at, :] if share % LANES else columns(at)
         out[...] = value.astype(out.dtype)
 
 
-def weight_pieces(window, grad, feature_slices, shares):
+def weight_pieces(group, window, grad, slices, shares):
     groups, rows, embed = grad.shape
-    columns = feature_slices.shape[2]
+    columns = slices[0].shape[2]
     share = columns // shares
     return pl.pallas_call(
-        gather_kernel,
-        in_specs=[smem()] + [vmem()] * 2,
+        functools.partial(pieces_kernel, shares),
+        in_specs=[smem(), smem()] + [vmem()] * (1 + len(slices)),
         out_specs=[vmem()] * shares,
         out_shape=[
             jax.ShapeDtypeStruct((share, embed), BF16 if r else F32) for r in range(shares)
@@ -485,7 +511,7 @@
             transcendentals=0,
         ),
         name="weight_pieces",
-    )(window, grad, feature_slices)
+    )(group, window, grad, *slices)
 
 
 def finish_kernel(*refs):
@@ -518,21 +544,33 @@
     window = lax.axis_index("win").astype(jnp.int32)
     me = group * shares + window
 
-    block, slices, send, keep = project(
-        me.reshape(1), partner_offsets, features, proj_weight, ortholog_index.T, groups
+    direct = groups == 8
+    by_x, by_near, by_far = shares, 2 * shares, 4 * shares
+    me_scalar = me.reshape(1)
+    if direct:
+        own_slices, x_slices = cut(group.reshape(1), features, groups)
+        own_slices, x_slices, me_scalar = lax.optimization_barrier((own_slices, x_slices, me_scalar))
+        x_slices = xor_permute(x_slices, by_x)
+    else:
+        slices = features.reshape(rows, groups, depth // groups).transpose(1, 0, 2)
+        slices = lax.all_to_all(slices, "sp", 0, 0)
+        slices = [
+            lax.dynamic_index_in_dim(slices, group ^ k, 0, keepdims=True) for k in range(groups)
+        ]
+
+    block, send, keep = project(
+        me_scalar, partner_offsets, features, proj_weight, ortholog_index.T
     )
-
-    direct = groups == 8
-    blocks = {0: block}
+    block = block[None]
     if direct:
-        blocks[4] = xor_permute(block, 4 * shares)
-        blocks[2] = xor_permute(block, 2 * shares)
+        block_far = xor_permute(block, by_far)
+        block_near = xor_permute(block, by_near)
     else:
-        gathered = lax.all_gather(block, "sp")
-        for k in range(groups):
-            blocks[k] = lax.dynamic_index_in_dim(gathered, group ^ k, 0, keepdims=False)
+        gathered = lax.all_gather(block, "sp", tiled=True)
 
     arrived = [xor_permute(send, 1)]
+    if direct:
+        arrived[0], x_slices = lax.optimization_barrier((arrived[0], x_slices))
     sent = send
     seen = 1
     stages = []
@@ -542,9 +580,11 @@
         count = 4
         own = (me >> low) & (count - 1)
         keep, sends, seen = stage(own, keep, sent, arrived, seen, count, embed)
-        if direct and low == 1:
-            *sends, block = lax.optimization_barrier((*sends, block))
-            blocks[1] = xor_permute(block, shares)
+        if direct and stages:
+            *sends, block_far, block_near = lax.optimization_barrier(
+                (*sends, block_far, block_near)
+            )
+            pair_x = xor_permute(jnp.concatenate([block, block_near]), by_x)
         arrived = [xor_permute(piece, (r + 1) << low) for r, piece in enumerate(sends)]
         sent = sends[0]
         stages.append((low, count))
@@ -554,37 +594,44 @@
     part = keep
     for piece in arrived:
         part = part + piece[:size].astype(F32)
-    sums = jnp.stack([sent[size:]] + [piece[size:] for piece in arrived])
+    sums = [sent, *arrived]
     extra = devices >> low
     if extra > 1:
-        mine = jnp.concatenate([part.astype(BF16), sums.reshape(-1, sums.shape[2])])
+        mine = jnp.concatenate([part.astype(BF16)] + [piece[size:] for piece in sums])
         others = [xor_permute(mine, r << low) for r in range(1, extra)]
         for piece in others:
             part = part + piece[:size].astype(F32)
-        sums = jnp.concatenate([sums] + [piece[size:].reshape(sums.shape) for piece in others])
+        sums = [mine, *others]
     part = part.astype(BF16)
-    for number, (low, count) in enumerate(stages):
-        if direct and number == 0:
-            part, blocks[4], blocks[2] = lax.optimization_barrier((part, blocks[4], blocks[2]))
-            blocks[6] = xor_permute(blocks[4], 2 * shares)
-            blocks[5] = xor_permute(blocks[4], shares)
-            blocks[3] = xor_permute(blocks[2], shares)
+    for number, (low, count) in enumerate(reversed(stages)):
+        if direct and number == 1:
+            part, pair_x, block_far = lax.optimization_barrier((part, pair_x, block_far))
+            block_far_near = xor_permute(block_far, by_near)
         part = jnp.concatenate(
             [part] + [xor_permute(part, r << low) for r in range(1, count)], axis=0
         )
     part = part.reshape(-1, size, part.shape[1])
     if direct:
-        part, blocks[6] = lax.optimization_barrier((part, blocks[6]))
-        blocks[7] = xor_permute(blocks[6], shares)
+        part, block_far_near, own_slices, x_slices = lax.optimization_barrier(
+            (part, block_far_near, own_slices, x_slices)
+        )
+        far_x = xor_permute(jnp.concatenate([block_far, block_far_near]), by_x)
+        blocks = [block, block_near, pair_x, block_far, block_far_near, far_x]
+        order = [0, 2, 1, 3, 4, 6, 5, 7]
+        slices = [own_slices[:1], x_slices[:1]]
+        for r in range(1, groups // 2):
+            pair = jnp.stack([own_slices[r], x_slices[r]])
+            slices.append(xor_permute(pair, 2 * r * shares))
+    else:
+        order = list(range(groups))
+        blocks = [
+            lax.dynamic_index_in_dim(gathered, group ^ k, 0, keepdims=True) for k in order
+        ]
     other = xor_permute(part, 1)
 
-    other, slices = lax.optimization_barrier((other, slices))
-    slices = lax.all_to_all(slices, "sp", 0, 0)
-
-    whitener, mean = whiten(place.reshape(1), sums, part, other, rows, embed)
-    blocks = [blocks[k] for k in range(groups)]
-    loss, grad = contrast(group.reshape(1), blocks, mean, whitener)
-    pieces = weight_pieces(window.reshape(1), grad, slices, shares)
+    whitener, mean = whiten(place.reshape(1), part, other, sums, seen, rows, embed)
+    loss, grad = contrast(group.reshape(1), blocks, order, mean, whitener)
+    pieces = weight_pieces(group.reshape(1), window.reshape(1), grad, slices, shares)
     pieces = [pieces[0]] + [xor_permute(pieces[r], r) for r in range(1, shares)]
     return loss[0], finish(pieces, whitener)
 

time: 209 us -> 161 us (0.77)
  waiting for transfers between devices: 107 us -> 58.7 us
  local copies, waits for them, and re-layouts: 9.35 us -> 3.04 us
  Pallas kernels: 57.2 us -> 60.3 us
  other arithmetic: 0.06 us -> 2.58 us
    ppermute x24 -> x26, waiting for transfers between devices: 107 us -> 58.7 us  [xor_permute(): return lax.ppermute(piece, AXES, [(i, i ^ mask) for i in range(devices)])]
    ppermute x24 -> x26, starting transfers between devices: 29.6 us -> 35 us  [xor_permute(): return lax.ppermute(piece, AXES, [(i, i ^ mask) for i in range(devices)])]
    unnamed x27 -> x12, local copies, waits for them, and re-layouts: 6.97 us -> 1.71 us
    all_to_all x1 -> x0, starting transfers between devices: 4.28 us -> none  [shards(): slices = lax.all_to_all(slices, 'sp', 0, 0)]
    pallas_call x3 -> x4, Pallas kernels: 46.4 us -> 49.2 us  [the longest x1 28.5 us: contrast(): pl.pallas_call(functools.partial(contrast_kernel, order), in_specs=[smem(...]
    concatenate x0 -> x4, other arithmetic: none -> 2.41 us  [the longest x1 1.16 us: shards(): pair_x = xor_permute(jnp.concatenate([block, block_near]), by_x)]
    another operation x4 -> x0, local copies, waits for them, and re-layouts: 2.35 us -> none  [shards(): sums = jnp.stack([sent[size:]] + [piece[size:] for piece in arrived])]
  transfers between devices with their start and end apart: 25 -> 26, of which waited for: 13 -> 16; matrix products, arithmetic and copies ran while one was open for 1% -> 2% of each run, Pallas kernels for 22% -> 33%
where the time goes in v7:
time: 161 us; the launch traced here: 160 us
  Pallas kernels  60.3 us (37%)
  waiting for transfers between devices  58.7 us (36%)
  starting transfers between devices  35 us (22%)
  local copies, waits for them, and re-layouts  3.04 us (2%)
  other arithmetic  2.58 us (2%)
    ppermute x26, waiting for transfers between devices, xor_permute(): return lax.ppermute(piece, AXES, [(i, i ^ mask) for i in range(devices)])  58.7 us
    ppermute x26, starting transfers between devices, xor_permute(): return lax.ppermute(piece, AXES, [(i, i ^ mask) for i in range(devices)])  35 us
    pallas_call x1, Pallas kernels, contrast(): pl.pallas_call(functools.partial(contrast_kernel, order), in_specs=[smem(...  28.5 us
    pallas_call x1, Pallas kernels, whiten(): pl.pallas_call(make_whiten_kernel(rows, count), in_specs=[smem()] + [vmem...  15.3 us
    pallas_call x1, Pallas kernels, project(): pl.pallas_call(project_kernel, in_specs=[smem(), smem(), hbm, hbm, hbm],...  6.79 us
  transfers between devices with their start and end apart: 26, of which 16 were waited for; matrix products, arithmetic and copies ran while one was open for 2% of the time, Pallas kernels for 33%

profile of v7, /device:TPU:0, one launch (start us, length us, event | category | flops | bytes accessed | tf_op | source)
XLA Modules:
  0.0 160.5 jit_solution(8957264115478377745)
XLA Ops:
  0.7 3.0 %cut.1 = (bf16[4,256,512]{2,1,0:T(8,128)(2,1)}, bf16[4,256,512]{2,1,0:T(8,128)(2,1)}) custom-call(s32[1]{0:T(128)} %bitcast.group_ref, bf16[256,4096]{1,0:T(8,128)(2,1)} %features_hbm.3), custom_call_target="tpu_custom_call" | custom-call | tf_op jit(solution)/shard_map/cut/pallas_call | solution.py:73
  3.7 3.0 %collective-permute-start.1 = (bf16[4,256,512]{2,1,0:T(8,128)(2,1)}, bf16[4,256,512]{2,1,0:T(8,128)(2,1)}, u32[]{:S(2)}, u32[]{:S(2)}) collective-permute-start(bf16[4,256,512]{2,1,0:T(8,128)(2,1)} %get-tuple-element.45), channel_id=1, source_target_pairs={{0,4},{1,5},{2,6},{3,7},{4,0},{5,1},{6,2},{7,3},{8,12},{9,13},{10,... | collective-permute-start | bytes 3145736 | tf_op jit(solution)/shard_map/ppermute | solution.py:47
  6.7 6.8 %project.1 = (bf16[272,1024]{1,0:T(8,128)(2,1)}, bf16[528,640]{1,0:T(8,128)(2,1)}, f32[512,640]{1,0:T(8,128)S(1)}) custom-call(s32[1]{0:T(128)} %bitcast.4.me_ref, s32[1,4]{1,0:T(1,128)S(1)} %copy-done.4, bf16[256,4096]{1,0:T(8,128)(2,1)S(1)} %copy-done, bf16[4096,1024]{1,0:T(8,128)(2,1)} %weight_hbm.1, s32[4,256]{1,0:T(4,128)S(1)} %bitcast.12), custom_call_target="tpu_custom_call" | custom-call | flops 2147483648 | bytes 8388608 | tf_op jit(solution)/shard_map/project/pallas_call | solution.py:188
  13.5 0.1 collective-permute-start
  13.6 1.6 %collective-permute-start.6 = (bf16[1,272,1024]{2,1,0:T(8,128)(2,1)}, bf16[1,272,1024]{2,1,0:T(8,128)(2,1)S(1)}, u32[]{:S(2)}, u32[]{:S(2)}) collective-permute-start(bf16[1,272,1024]{2,1,0:T(8,128)(2,1)} %bitcast.6.refs_0_), channel_id=1, source_target_pairs={{0,8},{1,9},{2,10},{3,11},{4,12},{5,13},{6,14},{7,15},{8,0},{9,1},... | collective-permute-start | bytes 1671176 | tf_op jit(solution)/shard_map/ppermute | solution.py:47
  15.3 2.6 %collective-permute-start.5 = (bf16[1,272,1024]{2,1,0:T(8,128)(2,1)}, bf16[1,272,1024]{2,1,0:T(8,128)(2,1)S(1)}, u32[]{:S(2)}, u32[]{:S(2)}) collective-permute-start(bf16[1,272,1024]{2,1,0:T(8,128)(2,1)} %bitcast.6.refs_0_), channel_id=1, source_target_pairs={{0,16},{1,17},{2,18},{3,19},{4,20},{5,21},{6,22},{7,23},{8,24},{9,... | collective-permute-start | bytes 1671176 | tf_op jit(solution)/shard_map/ppermute | solution.py:47
  17.8 0.0 collective-permute-done.refs_0_
  17.8 12.4 %collective-permute-done.1 = bf16[4,256,512]{2,1,0:T(8,128)(2,1)} collective-permute-done((bf16[4,256,512]{2,1,0:T(8,128)(2,1)}, bf16[4,256,512]{2,1,0:T(8,128)(2,1)}, u32[]{:S(2)}, u32[]{:S(2)}) %collective-permute-start.1) | collective-permute-done | bytes 1048608 | tf_op jit(solution)/shard_map/ppermute | solution.py:47
  30.2 1.9 %stage.2 = (f32[128,640]{1,0:T(8,128)S(1)}, bf16[144,640]{1,0:T(8,128)(2,1)S(1)}, bf16[144,640]{1,0:T(8,128)(2,1)}, bf16[144,640]{1,0:T(8,128)(2,1)}) custom-call(s32[1]{0:T(128)} %bitcast.3.own_ref, f32[512,640]{1,0:T(8,128)S(1)} %get-tuple-element.43.keep_ref, bf16[528,640]{1,0:T(8,128)(2,1)} %get-tuple-element.44.sent_ref, ...), custom_call_target="tpu_custom_call" | custom-call | flops 327680 | bytes 1310720 | tf_op jit(solution)/shard_map/stage/pallas_call | solution.py:240
  32.1 0.7 copy-done.1
  32.9 1.7 %collective-permute-start.3 = (bf16[144,640]{1,0:T(8,128)(2,1)}, bf16[144,640]{1,0:T(8,128)(2,1)S(1)}, u32[]{:S(2)}, u32[]{:S(2)}) collective-permute-start(bf16[144,640]{1,0:T(8,128)(2,1)} %get-tuple-element.49), channel_id=1, source_target_pairs={{0,4},{1,5},{2,6},{3,7},{4,0},{5,1},{6,2},{7,3},{8,12},{9,13},{10,... | collective-permute-start | bytes 552968 | tf_op jit(solution)/shard_map/ppermute | solution.py:47
  34.6 1.5 collective-permute-start.4
  36.1 0.3 collective-permute-start.2
  36.4 4.3 %collective-permute-done.3.refs_1_ = bf16[144,640]{1,0:T(8,128)(2,1)S(1)} collective-permute-done((bf16[144,640]{1,0:T(8,128)(2,1)}, bf16[144,640]{1,0:T(8,128)(2,1)S(1)}, u32[]{:S(2)}, u32[]{:S(2)}) %collective-permute-start.3) | collective-permute-done | bytes 184352 | tf_op jit(solution)/shard_map/ppermute | solution.py:47
  40.6 3.1 %collective-permute-done.4.refs_2_ = bf16[144,640]{1,0:T(8,128)(2,1)S(1)} collective-permute-done((bf16[144,640]{1,0:T(8,128)(2,1)}, bf16[144,640]{1,0:T(8,128)(2,1)S(1)}, u32[]{:S(2)}, u32[]{:S(2)}) %collective-permute-start.4) | collective-permute-done | bytes 184352 | tf_op jit(solution)/shard_map/ppermute | solution.py:47
  43.8 1.2 collective-permute-done.2.refs_0_
  45.0 1.0 copy-done.2
  46.0 0.1 stage.3
  46.1 0.0 collective-permute-done.6.refs_1_
  46.1 0.0 collective-permute-done.5.refs_3_
  46.1 1.2 pad_maximum_fusion
  47.3 1.6 collective-permute-start.13
  48.8 2.6 %collective-permute-start.8 = (bf16[64,640]{1,0:T(8,128)(2,1)S(1)}, bf16[64,640]{1,0:T(8,128)(2,1)S(1)}, u32[]{:S(2)}, u32[]{:S(2)}) collective-permute-start(bf16[64,640]{1,0:T(8,128)(2,1)S(1)} %get-tuple-element.57), channel_id=1, source_target_pairs={{0,16},{1,17},{2,18},{3,19},{4,20},{5,21},{6,22},{7,23},{8,24},{9,... | collective-permute-start | bytes 245768 | tf_op jit(solution)/shard_map/ppermute | solution.py:47
  51.4 1.3 collective-permute-start.9
  52.8 0.2 collective-permute-start.7
  53.0 1.2 collective-permute-done.8.refs_2_
  54.2 4.0 %collective-permute-done.9.refs_3_ = bf16[64,640]{1,0:T(8,128)(2,1)S(1)} collective-permute-done((bf16[64,640]{1,0:T(8,128)(2,1)S(1)}, bf16[64,640]{1,0:T(8,128)(2,1)S(1)}, u32[]{:S(2)}, u32[]{:S(2)}) %collective-permute-start.9) | collective-permute-done | bytes 81952 | tf_op jit(solution)/shard_map/ppermute | solution.py:47
  58.1 0.6 collective-permute-done.7.refs_1_
  58.7 2.2 %collective-permute-start.12 = (bf16[32,640]{1,0:T(8,128)(2,1)S(1)}, bf16[32,640]{1,0:T(8,128)(2,1)S(1)}, u32[]{:S(2)}, u32[]{:S(2)}) collective-permute-start(bf16[32,640]{1,0:T(8,128)(2,1)S(1)} %add_convert_fusion), channel_id=1, source_target_pairs={{0,24},{1,25},{2,26},{3,27},{4,28},{5,29},{6,30},{7,31},{8,16},{9,... | collective-permute-start | bytes 122888 | tf_op jit(solution)/shard_map/ppermute | solution.py:47
  60.9 0.4 collective-permute-start.11
  61.3 1.9 %collective-permute-start.10 = (bf16[32,640]{1,0:T(8,128)(2,1)S(1)}, bf16[32,640]{1,0:T(8,128)(2,1)S(1)}, u32[]{:S(2)}, u32[]{:S(2)}) collective-permute-start(bf16[32,640]{1,0:T(8,128)(2,1)S(1)} %add_convert_fusion), channel_id=1, source_target_pairs={{0,8},{1,9},{2,10},{3,11},{4,12},{5,13},{6,14},{7,15},{8,0},{9,1},... | collective-permute-start | bytes 122888 | tf_op jit(solution)/shard_map/ppermute | solution.py:47
  63.2 1.4 collective-permute-done.12
  64.6 1.7 %collective-permute-done.11 = bf16[32,640]{1,0:T(8,128)(2,1)S(1)} collective-permute-done((bf16[32,640]{1,0:T(8,128)(2,1)S(1)}, bf16[32,640]{1,0:T(8,128)(2,1)S(1)}, u32[]{:S(2)}, u32[]{:S(2)}) %collective-permute-start.11) | collective-permute-done | bytes 40992 | tf_op jit(solution)/shard_map/ppermute | solution.py:47
  66.3 0.0 collective-permute-done.10
  66.3 4.3 %collective-permute-done.13.refs_2_ = bf16[2,272,1024]{2,1,0:T(8,128)(2,1)S(1)} collective-permute-done((bf16[2,272,1024]{2,1,0:T(8,128)(2,1)S(1)}, bf16[2,272,1024]{2,1,0:T(8,128)(2,1)S(1)}, u32[]{:S(2)}, u32[]{:S(2)}) %collective-permute-start.13) | collective-permute-done | bytes 1114144 | tf_op jit(solution)/shard_map/ppermute | solution.py:47
  70.6 2.2 %collective-permute-start.17 = (bf16[1,272,1024]{2,1,0:T(8,128)(2,1)S(1)}, bf16[1,272,1024]{2,1,0:T(8,128)(2,1)S(1)}, u32[]{:S(2)}, u32[]{:S(2)}) collective-permute-start(bf16[1,272,1024]{2,1,0:T(8,128)(2,1)S(1)} %collective-permute-done.5.refs_3_), channel_id=1, source_target_pairs={{0,8},{1,9},{2,10},{3,11},{4,12},{5,13},{6,14},{7,15},{8,0},{9,1},... | collective-permute-start | bytes 1671176 | tf_op jit(solution)/shard_map/ppermute | solution.py:47
  72.8 1.1 collective-permute-start.16
  73.9 1.1 collective-permute-start.15
  75.1 1.2 collective-permute-start.14
  76.3 2.9 %collective-permute-done.16 = bf16[128,640]{1,0:T(8,128)(2,1)} collective-permute-done((bf16[128,640]{1,0:T(8,128)(2,1)S(1)}, bf16[128,640]{1,0:T(8,128)(2,1)}, u32[]{:S(2)}, u32[]{:S(2)}) %collective-permute-start.16) | collective-permute-done | bytes 163872 | tf_op jit(solution)/shard_map/ppermute | solution.py:47
  79.2 1.0 collective-permute-done.15
  80.2 0.7 collective-permute-done.14
  80.9 1.1 pad_maximum_fusion.2
  82.0 0.1 collective-permute-start.18
  82.1 1.3 fusion
  83.4 0.1 pad_maximum_fusion.3
  83.5 0.5 collective-permute-start.20
  84.0 0.1 pad_maximum_fusion.4
  84.1 2.7 %collective-permute-start.21 = (bf16[2,256,512]{2,1,0:T(8,128)(2,1)S(1)}, bf16[2,256,512]{2,1,0:T(8,128)(2,1)S(1)}, u32[]{:S(2)}, u32[]{:S(2)}) collective-permute-start(bf16[2,256,512]{2,1,0:T(8,128)(2,1)S(1)} %pad_maximum_fusion.4), channel_id=1, source_target_pairs={{0,16},{1,17},{2,18},{3,19},{4,20},{5,21},{6,22},{7,23},{8,24},{9,... | collective-permute-start | bytes 1572872 | tf_op jit(solution)/shard_map/ppermute | solution.py:47
  86.7 0.1 pad_maximum_fusion.1
  86.8 1.6 %collective-permute-start.19 = (bf16[2,272,1024]{2,1,0:T(8,128)(2,1)S(1)}, bf16[2,272,1024]{2,1,0:T(8,128)(2,1)S(1)}, u32[]{:S(2)}, u32[]{:S(2)}) collective-permute-start(bf16[2,272,1024]{2,1,0:T(8,128)(2,1)S(1)} %pad_maximum_fusion.1), channel_id=1, source_target_pairs={{0,4},{1,5},{2,6},{3,7},{4,0},{5,1},{6,2},{7,3},{8,12},{9,13},{10,... | collective-permute-start | bytes 3342344 | tf_op jit(solution)/shard_map/ppermute | solution.py:47
  88.5 0.1 pad_maximum_fusion.5
  88.5 1.5 collective-permute-start.22
  90.0 15.3 %whiten.1 = (bf16[1024,1024]{1,0:T(8,128)(2,1)S(1)}, f32[1,1024]{1,0:T(1,128)S(1)}) custom-call(s32[1]{0:T(128)} %bitcast.1.place_ref, bf16[16,32,640]{2,1,0:T(8,128)(2,1)S(1)} %bitcast.11, bf16[16,32,640]{2,1,0:T(8,128)(2,1)S(1)} %collective-permute-done.18.far_ref, bf16[64,640]{1,0:T(8,128)(2,1)S(1)} %get-tuple-element.56.refs_0_, ...), custom_call_target="tpu_custom_call" | custom-call | flops 10737418240 | bytes 2097152 | tf_op jit(solution)/shard_map/whiten/pallas_call | solution.py:381
  105.3 8.0 %collective-permute-done.19.refs_5_ = bf16[2,272,1024]{2,1,0:T(8,128)(2,1)S(1)} collective-permute-done((bf16[2,272,1024]{2,1,0:T(8,128)(2,1)S(1)}, bf16[2,272,1024]{2,1,0:T(8,128)(2,1)S(1)}, u32[]{:S(2)}, u32[]{:S(2)}) %collective-permute-start.19) | collective-permute-done | bytes 1114144 | tf_op jit(solution)/shard_map/ppermute | solution.py:47
  113.3 28.5 %contrast.1 = (f32[1,256]{1,0:T(1,128)}, bf16[8,256,1024]{2,1,0:T(8,128)(2,1)S(1)}) custom-call(s32[1]{0:T(128)} %bitcast.group_ref, f32[1,1024]{1,0:T(1,128)S(1)} %get-tuple-element.66.mean_ref, bf16[1024,1024]{1,0:T(8,128)(2,1)S(1)} %get-tuple-element.67.whitener_ref.refs_4_, bf16[1,272,1024]{2,1,0:T(8,128)(2,1)} %bitcast.6.refs_0_, ...), custom_call_target="tpu_custom_call" | custom-call | flops 12884901888 | bytes 8388608 | tf_op jit(solution)/shard_map/contrast/pallas_call | solution.py:449
  141.8 0.0 collective-permute-done.22.refs_4_
  141.8 2.4 %weight_pieces.1 = (f32[128,1024]{1,0:T(8,128)S(1)}, bf16[128,1024]{1,0:T(8,128)(2,1)S(1)}, bf16[128,1024]{1,0:T(8,128)(2,1)S(1)}, bf16[128,1024]{1,0:T(8,128)(2,1)S(1)}) custom-call(s32[1]{0:T(128)} %bitcast.group_ref, s32[1]{0:T(128)} %bitcast.9.window_ref, bf16[8,256,1024]{2,1,0:T(8,128)(2,1)S(1)} %get-tuple-element.71.grad_ref, ...), custom_call_target="tpu_custom_call" | custom-call | flops 2147483648 | bytes 6291456 | tf_op jit(solution)/shard_map/weight_pieces/pallas_call | solution.py:499
  144.2 0.1 collective-permute-start.23
  144.3 1.2 collective-permute-start.24
  145.5 0.7 collective-permute-start.25
  146.1 7.3 %collective-permute-done.24.refs_2_ = bf16[128,1024]{1,0:T(8,128)(2,1)S(1)} collective-permute-done((bf16[128,1024]{1,0:T(8,128)(2,1)S(1)}, bf16[128,1024]{1,0:T(8,128)(2,1)S(1)}, u32[]{:S(2)}, u32[]{:S(2)}) %collective-permute-start.24) | collective-permute-done | bytes 262176 | tf_op jit(solution)/shard_map/ppermute | solution.py:47
  153.5 4.7 %collective-permute-done.25.refs_3_ = bf16[128,1024]{1,0:T(8,128)(2,1)S(1)} collective-permute-done((bf16[128,1024]{1,0:T(8,128)(2,1)S(1)}, bf16[128,1024]{1,0:T(8,128)(2,1)S(1)}, u32[]{:S(2)}, u32[]{:S(2)}) %collective-permute-start.25) | collective-permute-done | bytes 262176 | tf_op jit(solution)/shard_map/ppermute | solution.py:47
  158.2 2.3 %finish.1 = f32[128,1024]{1,0:T(8,128)} custom-call(f32[128,1024]{1,0:T(8,128)S(1)} %get-tuple-element.74.refs_0_, bf16[128,1024]{1,0:T(8,128)(2,1)S(1)} %collective-permute-done.23.refs_1_, bf16[128,1024]{1,0:T(8,128)(2,1)S(1)} %collective-permute-done.24.refs_2_, bf16[128,1024]{1,0:T(8,128)(2,1)S(1)} %collective-permute-done.25.refs_3_, ...), custom_call_target="tpu_custom_call" | custom-call | tf_op jit(solution)/shard_map/finish/pallas_call | solution.py:527
  (17 shorter events, 0.1 us)
Async XLA Ops:
  0.6 6.1 %copy-start = (bf16[256,4096]{1,0:T(8,128)(2,1)S(1)}, bf16[256,4096]{1,0:T(8,128)(2,1)}, u32[]{:S(2)}) copy-start(bf16[256,4096]{1,0:T(8,128)(2,1)} %features_hbm.3) | copy-start | bytes 6291460
  0.6 6.1 %copy-start.3 = (s32[256,4]{0,1:T(4,128)S(1)}, s32[256,4]{0,1:T(4,128)}, u32[]{:S(2)}) copy-start(s32[256,4]{0,1:T(4,128)} %param.7) | copy-start | bytes 12292
  0.6 6.1 %copy-start.4 = (s32[1,4]{1,0:T(1,128)S(1)}, s32[1,4]{1,0:T(1,128)}, u32[]{:S(2)}) copy-start(s32[1,4]{1,0:T(1,128)} %offsets_ref.1) | copy-start | bytes 52
  3.7 26.5 %collective-permute-start.1 = (bf16[4,256,512]{2,1,0:T(8,128)(2,1)}, bf16[4,256,512]{2,1,0:T(8,128)(2,1)}, u32[]{:S(2)}, u32[]{:S(2)}) collective-permute-start(bf16[4,256,512]{2,1,0:T(8,128)(2,1)} %get-tuple-element.45), channel_id=1, source_target_pairs={{0,4},{1,5},{2,6},{3,7},{4,0},{5,1},{6,2},{7,3},{8,12},{9,13},{10,... | collective-permute-start | bytes 3145736 | tf_op jit(solution)/shard_map/ppermute | solution.py:47
  13.5 4.3 %collective-permute-start = (bf16[528,640]{1,0:T(8,128)(2,1)}, bf16[528,640]{1,0:T(8,128)(2,1)S(1)}, u32[]{:S(2)}, u32[]{:S(2)}) collective-permute-start(bf16[528,640]{1,0:T(8,128)(2,1)} %get-tuple-element.44.sent_ref), channel_id=1, source_target_pairs={{0,1},{1,0},{2,3},{3,2},{4,5},{5,4},{6,7},{7,6},{8,9},{9,8},{10,11... | collective-permute-start | bytes 2027528 | tf_op jit(solution)/shard_map/ppermute | solution.py:47
  13.6 32.5 %collective-permute-start.6 = (bf16[1,272,1024]{2,1,0:T(8,128)(2,1)}, bf16[1,272,1024]{2,1,0:T(8,128)(2,1)S(1)}, u32[]{:S(2)}, u32[]{:S(2)}) collective-permute-start(bf16[1,272,1024]{2,1,0:T(8,128)(2,1)} %bitcast.6.refs_0_), channel_id=1, source_target_pairs={{0,8},{1,9},{2,10},{3,11},{4,12},{5,13},{6,14},{7,15},{8,0},{9,1},... | collective-permute-start | bytes 1671176 | tf_op jit(solution)/shard_map/ppermute | solution.py:47
  15.3 30.8 %collective-permute-start.5 = (bf16[1,272,1024]{2,1,0:T(8,128)(2,1)}, bf16[1,272,1024]{2,1,0:T(8,128)(2,1)S(1)}, u32[]{:S(2)}, u32[]{:S(2)}) collective-permute-start(bf16[1,272,1024]{2,1,0:T(8,128)(2,1)} %bitcast.6.refs_0_), channel_id=1, source_target_pairs={{0,16},{1,17},{2,18},{3,19},{4,20},{5,21},{6,22},{7,23},{8,24},{9,... | collective-permute-start | bytes 1671176 | tf_op jit(solution)/shard_map/ppermute | solution.py:47
  32.1 0.7 copy-start.1
  32.9 7.8 %collective-permute-start.3 = (bf16[144,640]{1,0:T(8,128)(2,1)}, bf16[144,640]{1,0:T(8,128)(2,1)S(1)}, u32[]{:S(2)}, u32[]{:S(2)}) collective-permute-start(bf16[144,640]{1,0:T(8,128)(2,1)} %get-tuple-element.49), channel_id=1, source_target_pairs={{0,4},{1,5},{2,6},{3,7},{4,0},{5,1},{6,2},{7,3},{8,12},{9,13},{10,... | collective-permute-start | bytes 552968 | tf_op jit(solution)/shard_map/ppermute | solution.py:47
  34.6 9.2 %collective-permute-start.4 = (bf16[144,640]{1,0:T(8,128)(2,1)}, bf16[144,640]{1,0:T(8,128)(2,1)S(1)}, u32[]{:S(2)}, u32[]{:S(2)}) collective-permute-start(bf16[144,640]{1,0:T(8,128)(2,1)} %get-tuple-element.50), channel_id=1, source_target_pairs={{0,6},{1,7},{2,4},{3,5},{4,2},{5,3},{6,0},{7,1},{8,14},{9,15},{10,... | collective-permute-start | bytes 552968 | tf_op jit(solution)/shard_map/ppermute | solution.py:47
  36.1 8.9 %collective-permute-start.2 = (bf16[144,640]{1,0:T(8,128)(2,1)S(1)}, bf16[144,640]{1,0:T(8,128)(2,1)S(1)}, u32[]{:S(2)}, u32[]{:S(2)}) collective-permute-start(bf16[144,640]{1,0:T(8,128)(2,1)S(1)} %get-tuple-element.48.sent_ref), channel_id=1, source_target_pairs={{0,2},{1,3},{2,0},{3,1},{4,6},{5,7},{6,4},{7,5},{8,10},{9,11},{10,... | collective-permute-start | bytes 552968 | tf_op jit(solution)/shard_map/ppermute | solution.py:47
  45.0 1.0 copy-start.2
  47.3 23.3 %collective-permute-start.13 = (bf16[2,272,1024]{2,1,0:T(8,128)(2,1)S(1)}, bf16[2,272,1024]{2,1,0:T(8,128)(2,1)S(1)}, u32[]{:S(2)}, u32[]{:S(2)}) collective-permute-start(bf16[2,272,1024]{2,1,0:T(8,128)(2,1)S(1)} %pad_maximum_fusion), channel_id=1, source_target_pairs={{0,4},{1,5},{2,6},{3,7},{4,0},{5,1},{6,2},{7,3},{8,12},{9,13},{10,... | collective-permute-start | bytes 3342344 | tf_op jit(solution)/shard_map/ppermute | solution.py:47
  48.8 5.3 %collective-permute-start.8 = (bf16[64,640]{1,0:T(8,128)(2,1)S(1)}, bf16[64,640]{1,0:T(8,128)(2,1)S(1)}, u32[]{:S(2)}, u32[]{:S(2)}) collective-permute-start(bf16[64,640]{1,0:T(8,128)(2,1)S(1)} %get-tuple-element.57), channel_id=1, source_target_pairs={{0,16},{1,17},{2,18},{3,19},{4,20},{5,21},{6,22},{7,23},{8,24},{9,... | collective-permute-start | bytes 245768 | tf_op jit(solution)/shard_map/ppermute | solution.py:47
  51.4 6.7 %collective-permute-start.9 = (bf16[64,640]{1,0:T(8,128)(2,1)S(1)}, bf16[64,640]{1,0:T(8,128)(2,1)S(1)}, u32[]{:S(2)}, u32[]{:S(2)}) collective-permute-start(bf16[64,640]{1,0:T(8,128)(2,1)S(1)} %get-tuple-element.58), channel_id=1, source_target_pairs={{0,24},{1,25},{2,26},{3,27},{4,28},{5,29},{6,30},{7,31},{8,16},{9,... | collective-permute-start | bytes 245768 | tf_op jit(solution)/shard_map/ppermute | solution.py:47
  52.8 6.0 %collective-permute-start.7 = (bf16[64,640]{1,0:T(8,128)(2,1)S(1)}, bf16[64,640]{1,0:T(8,128)(2,1)S(1)}, u32[]{:S(2)}, u32[]{:S(2)}) collective-permute-start(bf16[64,640]{1,0:T(8,128)(2,1)S(1)} %get-tuple-element.56.refs_0_), channel_id=1, source_target_pairs={{0,8},{1,9},{2,10},{3,11},{4,12},{5,13},{6,14},{7,15},{8,0},{9,1},... | collective-permute-start | bytes 245768 | tf_op jit(solution)/shard_map/ppermute | solution.py:47
  58.7 5.9 %collective-permute-start.12 = (bf16[32,640]{1,0:T(8,128)(2,1)S(1)}, bf16[32,640]{1,0:T(8,128)(2,1)S(1)}, u32[]{:S(2)}, u32[]{:S(2)}) collective-permute-start(bf16[32,640]{1,0:T(8,128)(2,1)S(1)} %add_convert_fusion), channel_id=1, source_target_pairs={{0,24},{1,25},{2,26},{3,27},{4,28},{5,29},{6,30},{7,31},{8,16},{9,... | collective-permute-start | bytes 122888 | tf_op jit(solution)/shard_map/ppermute | solution.py:47
  60.9 5.3 %collective-permute-start.11 = (bf16[32,640]{1,0:T(8,128)(2,1)S(1)}, bf16[32,640]{1,0:T(8,128)(2,1)S(1)}, u32[]{:S(2)}, u32[]{:S(2)}) collective-permute-start(bf16[32,640]{1,0:T(8,128)(2,1)S(1)} %add_convert_fusion), channel_id=1, source_target_pairs={{0,16},{1,17},{2,18},{3,19},{4,20},{5,21},{6,22},{7,23},{8,24},{9,... | collective-permute-start | bytes 122888 | tf_op jit(solution)/shard_map/ppermute | solution.py:47
  61.3 5.0 %collective-permute-start.10 = (bf16[32,640]{1,0:T(8,128)(2,1)S(1)}, bf16[32,640]{1,0:T(8,128)(2,1)S(1)}, u32[]{:S(2)}, u32[]{:S(2)}) collective-permute-start(bf16[32,640]{1,0:T(8,128)(2,1)S(1)} %add_convert_fusion), channel_id=1, source_target_pairs={{0,8},{1,9},{2,10},{3,11},{4,12},{5,13},{6,14},{7,15},{8,0},{9,1},... | collective-permute-start | bytes 122888 | tf_op jit(solution)/shard_map/ppermute | solution.py:47
  70.6 11.4 %collective-permute-start.17 = (bf16[1,272,1024]{2,1,0:T(8,128)(2,1)S(1)}, bf16[1,272,1024]{2,1,0:T(8,128)(2,1)S(1)}, u32[]{:S(2)}, u32[]{:S(2)}) collective-permute-start(bf16[1,272,1024]{2,1,0:T(8,128)(2,1)S(1)} %collective-permute-done.5.refs_3_), channel_id=1, source_target_pairs={{0,8},{1,9},{2,10},{3,11},{4,12},{5,13},{6,14},{7,15},{8,0},{9,1},... | collective-permute-start | bytes 1671176 | tf_op jit(solution)/shard_map/ppermute | solution.py:47
  72.8 6.4 %collective-permute-start.16 = (bf16[128,640]{1,0:T(8,128)(2,1)S(1)}, bf16[128,640]{1,0:T(8,128)(2,1)}, u32[]{:S(2)}, u32[]{:S(2)}) collective-permute-start(bf16[128,640]{1,0:T(8,128)(2,1)S(1)} %pad_maximum_fusion.6), channel_id=1, source_target_pairs={{0,6},{1,7},{2,4},{3,5},{4,2},{5,3},{6,0},{7,1},{8,14},{9,15},{10,... | collective-permute-start | bytes 491528 | tf_op jit(solution)/shard_map/ppermute | solution.py:47
  73.9 6.3 %collective-permute-start.15 = (bf16[128,640]{1,0:T(8,128)(2,1)S(1)}, bf16[128,640]{1,0:T(8,128)(2,1)}, u32[]{:S(2)}, u32[]{:S(2)}) collective-permute-start(bf16[128,640]{1,0:T(8,128)(2,1)S(1)} %pad_maximum_fusion.6), channel_id=1, source_target_pairs={{0,4},{1,5},{2,6},{3,7},{4,0},{5,1},{6,2},{7,3},{8,12},{9,13},{10,... | collective-permute-start | bytes 491528 | tf_op jit(solution)/shard_map/ppermute | solution.py:47
  75.1 5.8 %collective-permute-start.14 = (bf16[128,640]{1,0:T(8,128)(2,1)S(1)}, bf16[128,640]{1,0:T(8,128)(2,1)}, u32[]{:S(2)}, u32[]{:S(2)}) collective-permute-start(bf16[128,640]{1,0:T(8,128)(2,1)S(1)} %pad_maximum_fusion.6), channel_id=1, source_target_pairs={{0,2},{1,3},{2,0},{3,1},{4,6},{5,7},{6,4},{7,5},{8,10},{9,11},{10,... | collective-permute-start | bytes 491528 | tf_op jit(solution)/shard_map/ppermute | solution.py:47
  76.3 5.8 %copy-start.5 = (bf16[4,256,512]{2,1,0:T(8,128)(2,1)S(1)}, bf16[4,256,512]{2,1,0:T(8,128)(2,1)}, u32[]{:S(2)}) copy-start(bf16[4,256,512]{2,1,0:T(8,128)(2,1)} %get-tuple-element.72) | copy-start | bytes 3145732
  82.0 8.0 %collective-permute-start.18 = (bf16[16,32,640]{2,1,0:T(8,128)(2,1)S(1)}, bf16[16,32,640]{2,1,0:T(8,128)(2,1)S(1)}, u32[]{:S(2)}, u32[]{:S(2)}) collective-permute-start(bf16[16,32,640]{2,1,0:T(8,128)(2,1)S(1)} %bitcast.10), channel_id=1, source_target_pairs={{0,1},{1,0},{2,3},{3,2},{4,5},{5,4},{6,7},{7,6},{8,9},{9,8},{10,11... | collective-permute-start | bytes 1966088 | tf_op jit(solution)/shard_map/ppermute | solution.py:47
  83.5 58.3 %collective-permute-start.20 = (bf16[2,256,512]{2,1,0:T(8,128)(2,1)S(1)}, bf16[2,256,512]{2,1,0:T(8,128)(2,1)S(1)}, u32[]{:S(2)}, u32[]{:S(2)}) collective-permute-start(bf16[2,256,512]{2,1,0:T(8,128)(2,1)S(1)} %pad_maximum_fusion.3), channel_id=1, source_target_pairs={{0,8},{1,9},{2,10},{3,11},{4,12},{5,13},{6,14},{7,15},{8,0},{9,1},... | collective-permute-start | bytes 1572872 | tf_op jit(solution)/shard_map/ppermute | solution.py:47
  84.1 57.7 %collective-permute-start.21 = (bf16[2,256,512]{2,1,0:T(8,128)(2,1)S(1)}, bf16[2,256,512]{2,1,0:T(8,128)(2,1)S(1)}, u32[]{:S(2)}, u32[]{:S(2)}) collective-permute-start(bf16[2,256,512]{2,1,0:T(8,128)(2,1)S(1)} %pad_maximum_fusion.4), channel_id=1, source_target_pairs={{0,16},{1,17},{2,18},{3,19},{4,20},{5,21},{6,22},{7,23},{8,24},{9,... | collective-permute-start | bytes 1572872 | tf_op jit(solution)/shard_map/ppermute | solution.py:47
  86.8 26.5 %collective-permute-start.19 = (bf16[2,272,1024]{2,1,0:T(8,128)(2,1)S(1)}, bf16[2,272,1024]{2,1,0:T(8,128)(2,1)S(1)}, u32[]{:S(2)}, u32[]{:S(2)}) collective-permute-start(bf16[2,272,1024]{2,1,0:T(8,128)(2,1)S(1)} %pad_maximum_fusion.1), channel_id=1, source_target_pairs={{0,4},{1,5},{2,6},{3,7},{4,0},{5,1},{6,2},{7,3},{8,12},{9,13},{10,... | collective-permute-start | bytes 3342344 | tf_op jit(solution)/shard_map/ppermute | solution.py:47
  88.5 53.3 %collective-permute-start.22 = (bf16[2,256,512]{2,1,0:T(8,128)(2,1)S(1)}, bf16[2,256,512]{2,1,0:T(8,128)(2,1)S(1)}, u32[]{:S(2)}, u32[]{:S(2)}) collective-permute-start(bf16[2,256,512]{2,1,0:T(8,128)(2,1)S(1)} %pad_maximum_fusion.5), channel_id=1, source_target_pairs={{0,24},{1,25},{2,26},{3,27},{4,28},{5,29},{6,30},{7,31},{8,16},{9,... | collective-permute-start | bytes 1572872 | tf_op jit(solution)/shard_map/ppermute | solution.py:47
  144.2 1.9 %collective-permute-start.23 = (bf16[128,1024]{1,0:T(8,128)(2,1)S(1)}, bf16[128,1024]{1,0:T(8,128)(2,1)S(1)}, u32[]{:S(2)}, u32[]{:S(2)}) collective-permute-start(bf16[128,1024]{1,0:T(8,128)(2,1)S(1)} %get-tuple-element.75), channel_id=1, source_target_pairs={{0,1},{1,0},{2,3},{3,2},{4,5},{5,4},{6,7},{7,6},{8,9},{9,8},{10,11... | collective-permute-start | bytes 786440 | tf_op jit(solution)/shard_map/ppermute | solution.py:47
  144.3 9.2 %collective-permute-start.24 = (bf16[128,1024]{1,0:T(8,128)(2,1)S(1)}, bf16[128,1024]{1,0:T(8,128)(2,1)S(1)}, u32[]{:S(2)}, u32[]{:S(2)}) collective-permute-start(bf16[128,1024]{1,0:T(8,128)(2,1)S(1)} %get-tuple-element.76), channel_id=1, source_target_pairs={{0,2},{1,3},{2,0},{3,1},{4,6},{5,7},{6,4},{7,5},{8,10},{9,11},{10,... | collective-permute-start | bytes 786440 | tf_op jit(solution)/shard_map/ppermute | solution.py:47
  145.5 12.7 %collective-permute-start.25 = (bf16[128,1024]{1,0:T(8,128)(2,1)S(1)}, bf16[128,1024]{1,0:T(8,128)(2,1)S(1)}, u32[]{:S(2)}, u32[]{:S(2)}) collective-permute-start(bf16[128,1024]{1,0:T(8,128)(2,1)S(1)} %get-tuple-element.77), channel_id=1, source_target_pairs={{0,3},{1,2},{2,1},{3,0},{4,7},{5,6},{6,5},{7,4},{8,11},{9,10},{10,... | collective-permute-start | bytes 786440 | tf_op jit(solution)/shard_map/ppermute | solution.py:47

commit v8 on v7

--- a/solution.py
+++ b/solution.py
@@ -52,31 +52,29 @@
     return high, (value - high.astype(F32)).astype(BF16)
 
 
-def cut_kernel(group_ref, features_hbm, near_ref, far_ref, sems):
-    halves, _, columns = near_ref.shape
+def cut_kernel(group_ref, features_hbm, *refs):
+    outs, sems = refs[:-1], refs[-1]
+    columns = outs[0].shape[1]
     copies = []
-    for r in range(halves):
-        for side, out in ((1, far_ref), (0, near_ref)):
-            start = pl.multiple_of((group_ref[0] ^ (2 * r + side)) * columns, columns)
-            copy = pltpu.make_async_copy(
-                features_hbm.at[:, pl.ds(start, columns)], out.at[r], sems.at[side, r]
-            )
-            copy.start()
-            copies.append(copy)
+    for k, out in enumerate(outs):
+        start = pl.multiple_of((group_ref[0] ^ k) * columns, columns)
+        copies.append(
+            pltpu.make_async_copy(features_hbm.at[:, pl.ds(start, columns)], out, sems.at[k])
+        )
+        copies[k].start()
     for copy in copies:
         copy.wait()
 
 
 def cut(group, features, groups):
     rows, depth = features.shape
-    half = jax.ShapeDtypeStruct((groups // 2, rows, depth // groups), BF16)
     return pl.pallas_call(
         cut_kernel,
         in_specs=[smem(), pl.BlockSpec(memory_space=pltpu.HBM)],
-        out_specs=[vmem()] * 2,
-        out_shape=[half, half],
-        scratch_shapes=[pltpu.SemaphoreType.DMA((2, groups // 2))],
-        compiler_params=params(56),
+        out_specs=[vmem()] * groups,
+        out_shape=[jax.ShapeDtypeStruct((rows, depth // groups), BF16)] * groups,
+        scratch_shapes=[pltpu.SemaphoreType.DMA((groups,))],
+        compiler_params=params(8),
         name="cut",
     )(group, features)
 
@@ -396,8 +394,9 @@
 
 
 def contrast_kernel(order, group_ref, mean_ref, whitener_ref, *refs):
-    loss_ref, grad_ref, white, others, tables, numbers, offsets_ref, sem = refs[-8:]
-    block_refs = [ref.at[i] for ref in refs[:-8] for i in range(ref.shape[0])]
+    loss_ref, grad_ref, white, tables, numbers, offsets_ref, sem = refs[-11:-4]
+    even, odd = (refs[-4], refs[-3]), (refs[-2], refs[-1])
+    block_refs = [ref.at[i] for ref in refs[:-11] for i in range(ref.shape[0])]
     block_refs = [block_refs[order.index(k)] for k in range(len(order))]
     groups, rows, embed = white.shape
     group = group_ref[0]
@@ -416,30 +415,53 @@
     copy.wait()
 
     places = lax.broadcasted_iota(jnp.int32, (rows, rows), 0).astype(F32)
-
-    @pl.loop(0, groups)
-    def _(g):
+    log2e = 1.4426950408889634
+
+    def partner(g, k):
+        return white[(g + offsets_ref[g, 1, k]) % groups]
+
+    def scores(g, buffers):
+        own = white[g]
         for k in range(PARTNERS):
-            others[k * rows : (k + 1) * rows, :] = white[(g + offsets_ref[g, 1, k]) % groups]
-        logits = dot(others[...], white[g], (1, 1)) * LOGIT_SCALE
+            buffers[0][k * rows : (k + 1) * rows, :] = dot(partner(g, k), own, (1, 1))
+
+    def softmax(g, buffers):
         loss = jnp.zeros((1, rows), F32)
-        weights = []
         for k in range(PARTNERS):
-            own = logits[k * rows : (k + 1) * rows]
+            at = slice(k * rows, (k + 1) * rows)
+            own = buffers[0][at, :]
             peak = jnp.max(own, axis=0, keepdims=True)
-            powers = jnp.exp(own - peak)
+            powers = jnp.exp2((own - peak) * (LOGIT_SCALE * log2e))
             sums = jnp.sum(powers, axis=0, keepdims=True)
-            hit = places == tables[g, 0:1, k * rows : (k + 1) * rows]
+            hit = places == tables[g, 0:1, at]
             picked = jnp.sum(jnp.where(hit, own, 0.0), axis=0, keepdims=True)
-            loss = loss + (peak + jnp.log(sums) - picked)
+            loss = loss + ((peak - picked) * LOGIT_SCALE + jnp.log(sums))
             share = powers * (1.0 / (PARTNERS * sums))
-            weights.append(jnp.where(hit, share - 1.0 / PARTNERS, share).astype(BF16))
-        grad = dot(jnp.concatenate(weights, axis=0), others[...], (0, 0))
+            weights = share - jnp.where(hit, 1.0 / PARTNERS, 0.0)
+            buffers[1][at, :] = weights.astype(BF16)
+        return loss * (1.0 / PARTNERS)
+
+    def gradient(g, buffers):
+        grad = dot(buffers[1][0:rows, :], partner(g, 0), (0, 0))
+        for k in range(1, PARTNERS):
+            grad = grad + dot(buffers[1][k * rows : (k + 1) * rows, :], partner(g, k), (0, 0))
         grad_ref[g] = (grad * LOGIT_SCALE).astype(BF16)
 
-        @pl.when(g == group)
+    scores(0, even)
+
+    @pl.loop(0, groups // 2)
+    def _(pair):
+        g = 2 * pair
+        scores(g + 1, odd)
+        first = softmax(g, even)
+        gradient(g, even)
+        second = softmax(g + 1, odd)
+        scores(lax.rem(g + 2, groups), even)
+        gradient(g + 1, odd)
+
+        @pl.when(pair == group // 2)
         def _():
-            loss_ref[...] = loss * (1.0 / PARTNERS)
+            loss_ref[...] = jnp.where(group % 2 == 0, first, second)
 
 
 def contrast(group, blocks, order, mean, whitener):
@@ -456,12 +478,12 @@
         ],
         scratch_shapes=[
             pltpu.VMEM((groups, rows, embed), BF16),
-            pltpu.VMEM((PARTNERS * rows, embed), BF16),
             pltpu.VMEM((groups, 8, embed), F32),
             pltpu.VMEM((groups, 8, LANES), jnp.int32),
             pltpu.SMEM((groups, 8, LANES), jnp.int32),
             pltpu.SemaphoreType.DMA,
-        ],
+        ]
+        + [pltpu.VMEM((PARTNERS * rows, rows), F32), pltpu.VMEM((PARTNERS * rows, rows), BF16)] * 2,
         compiler_params=params(min(58, 12 + 6 * groups * rows * embed // 2**20)),
         cost_estimate=pl.CostEstimate(
             flops=groups * rows * 2 * embed * (embed + 2 * PARTNERS * rows),
@@ -472,11 +494,9 @@
     )(group, mean, whitener, *blocks)
 
 
-def pieces_kernel(shares, group_ref, window_ref, grad_ref, *refs):
-    groups, _, embed = grad_ref.shape
-    outs, total = refs[-1 - shares : -1], refs[-1]
-    features = [ref.at[i] for ref in refs[: -1 - shares] for i in range(ref.shape[0])]
-    share = outs[0].shape[0]
+def pieces_kernel(share, masks, group_ref, window_ref, grad_ref, *refs):
+    groups = grad_ref.shape[0]
+    features, (keep_ref, send_ref, total) = refs[:groups], refs[groups:]
 
     def columns(at):
         value = dot(features[0][:, at], grad_ref[group_ref[0]], (0, 0))
@@ -486,32 +506,50 @@
 
     if share % LANES:
         total[...] = columns(slice(None))
-    for r, out in enumerate(outs):
-        at = pl.ds(pl.multiple_of((window_ref[0] ^ r) * share, share), share)
+    for n, mask in enumerate(masks):
+        at = pl.ds(pl.multiple_of((window_ref[0] ^ mask) * share, share), share)
         value = total[at, :] if share % LANES else columns(at)
-        out[...] = value.astype(out.dtype)
-
-
-def weight_pieces(group, window, grad, slices, shares):
+        out, n = (send_ref, n - len(masks) // 2) if n >= len(masks) // 2 else (keep_ref, n)
+        out[n * share : (n + 1) * share, :] = value.astype(out.dtype)
+
+
+def weight_pieces(group, window, grad, slices, shares, masks):
     groups, rows, embed = grad.shape
-    columns = slices[0].shape[2]
+    columns = slices[0].shape[1]
     share = columns // shares
+    half = len(masks) // 2 * share
     return pl.pallas_call(
-        functools.partial(pieces_kernel, shares),
+        functools.partial(pieces_kernel, share, masks),
         in_specs=[smem(), smem()] + [vmem()] * (1 + len(slices)),
-        out_specs=[vmem()] * shares,
+        out_specs=[vmem()] * 2,
         out_shape=[
-            jax.ShapeDtypeStruct((share, embed), BF16 if r else F32) for r in range(shares)
+            jax.ShapeDtypeStruct((half, embed), F32),
+            jax.ShapeDtypeStruct((half, embed), BF16),
         ],
         scratch_shapes=[pltpu.VMEM((columns if share % LANES else 8, embed), F32)],
         compiler_params=params(24),
         cost_estimate=pl.CostEstimate(
-            flops=groups * rows * 2 * embed * columns,
+            flops=groups * rows * 2 * embed * share * len(masks),
             bytes_accessed=2 * groups * rows * (embed + columns),
             transcendentals=0,
         ),
         name="weight_pieces",
     )(group, window, grad, *slices)
+
+
+def join_kernel(keep_ref, arrived_ref, out_ref):
+    out_ref[...] = (keep_ref[...] + arrived_ref[...].astype(F32)).astype(BF16)
+
+
+def join(keep, arrived):
+    return pl.pallas_call(
+        join_kernel,
+        in_specs=[vmem()] * 2,
+        out_specs=vmem(),
+        out_shape=jax.ShapeDtypeStruct(keep.shape, BF16),
+        compiler_params=params(8),
+        name="join",
+    )(keep, arrived)
 
 
 def finish_kernel(*refs):
@@ -520,7 +558,8 @@
     for ref in refs[1:-2]:
         value = value + ref[...].astype(F32)
     high, low = split(value)
-    out_ref[...] = dot(high, whitener_ref[...], (1, 1)) + dot(low, whitener_ref[...], (1, 1))
+    both = dot(jnp.concatenate([high, low], axis=0), whitener_ref[...], (1, 1))
+    out_ref[...] = both[: value.shape[0]] + both[value.shape[0] :]
 
 
 def finish(pieces, whitener):
@@ -546,20 +585,15 @@
 
     direct = groups == 8
     by_x, by_near, by_far = shares, 2 * shares, 4 * shares
-    me_scalar = me.reshape(1)
-    if direct:
-        own_slices, x_slices = cut(group.reshape(1), features, groups)
-        own_slices, x_slices, me_scalar = lax.optimization_barrier((own_slices, x_slices, me_scalar))
-        x_slices = xor_permute(x_slices, by_x)
-    else:
+    if not direct:
         slices = features.reshape(rows, groups, depth // groups).transpose(1, 0, 2)
         slices = lax.all_to_all(slices, "sp", 0, 0)
         slices = [
-            lax.dynamic_index_in_dim(slices, group ^ k, 0, keepdims=True) for k in range(groups)
+            lax.dynamic_index_in_dim(slices, group ^ k, 0, keepdims=False) for k in range(groups)
         ]
 
     block, send, keep = project(
-        me_scalar, partner_offsets, features, proj_weight, ortholog_index.T
+        me.reshape(1), partner_offsets, features, proj_weight, ortholog_index.T
     )
     block = block[None]
     if direct:
@@ -569,8 +603,6 @@
         gathered = lax.all_gather(block, "sp", tiled=True)
 
     arrived = [xor_permute(send, 1)]
-    if direct:
-        arrived[0], x_slices = lax.optimization_barrier((arrived[0], x_slices))
     sent = send
     seen = 1
     stages = []
@@ -581,9 +613,11 @@
         own = (me >> low) & (count - 1)
         keep, sends, seen = stage(own, keep, sent, arrived, seen, count, embed)
         if direct and stages:
-            *sends, block_far, block_near = lax.optimization_barrier(
-                (*sends, block_far, block_near)
+            group_scalar = group.reshape(1)
+            *sends, block_far, block_near, group_scalar = lax.optimization_barrier(
+                (*sends, block_far, block_near, group_scalar)
             )
+            slices = cut(group_scalar, features, groups)
             pair_x = xor_permute(jnp.concatenate([block, block_near]), by_x)
         arrived = [xor_permute(piece, (r + 1) << low) for r, piece in enumerate(sends)]
         sent = sends[0]
@@ -612,16 +646,13 @@
         )
     part = part.reshape(-1, size, part.shape[1])
     if direct:
-        part, block_far_near, own_slices, x_slices = lax.optimization_barrier(
-            (part, block_far_near, own_slices, x_slices)
-        )
+        part, block_far_near, *slices = lax.optimization_barrier((part, block_far_near, *slices))
         far_x = xor_permute(jnp.concatenate([block_far, block_far_near]), by_x)
         blocks = [block, block_near, pair_x, block_far, block_far_near, far_x]
         order = [0, 2, 1, 3, 4, 6, 5, 7]
-        slices = [own_slices[:1], x_slices[:1]]
-        for r in range(1, groups // 2):
-            pair = jnp.stack([own_slices[r], x_slices[r]])
-            slices.append(xor_permute(pair, 2 * r * shares))
+        slices = list(slices)
+        for k in (2, 4, 6, 1, 3, 5, 7):
+            slices[k] = xor_permute(slices[k], k * shares)
     else:
         order = list(range(groups))
         blocks = [
@@ -631,8 +662,15 @@
 
     whitener, mean = whiten(place.reshape(1), part, other, sums, seen, rows, embed)
     loss, grad = contrast(group.reshape(1), blocks, order, mean, whitener)
-    pieces = weight_pieces(group.reshape(1), window.reshape(1), grad, slices, shares)
-    pieces = [pieces[0]] + [xor_permute(pieces[r], r) for r in range(1, shares)]
+    group, window = group.reshape(1), window.reshape(1)
+    pieces = []
+    for mask in reversed(range(0, shares, 2)):
+        keep, send = weight_pieces(group, window, grad, slices, shares, (mask, mask + 1))
+        arrived = xor_permute(send, 1)
+        if mask:
+            pieces.append(xor_permute(join(keep, arrived), mask))
+        else:
+            pieces = [keep, arrived] + pieces
     return loss[0], finish(pieces, whitener)
 
 

time: 161 us -> 171 us (1.062)
  the two profiles are of different devices: /device:TPU:0 before, /device:TPU:20 now
where the time goes in v8:
time: 171 us; the launch traced here: 170 us
  waiting for transfers between devices  78.3 us (46%)
  Pallas kernels  48 us (28%)
  starting transfers between devices  32.2 us (19%)
  local copies, waits for them, and re-layouts  7.54 us (4%)
  other arithmetic  3.56 us (2%)
    ppermute x29, waiting for transfers between devices, xor_permute(): return lax.ppermute(piece, AXES, [(i, i ^ mask) for i in range(devices)])  78.3 us
    ppermute x29, starting transfers between devices, xor_permute(): return lax.ppermute(piece, AXES, [(i, i ^ mask) for i in range(devices)])  32.2 us
    pallas_call x1, Pallas kernels, contrast(): pl.pallas_call(functools.partial(contrast_kernel, order), in_specs=[smem(...  20.6 us
    pallas_call x1, Pallas kernels, whiten(): pl.pallas_call(make_whiten_kernel(rows, count), in_specs=[smem()] + [vmem...  15.3 us
    unnamed x24, local copies, waits for them, and re-layouts  7.54 us
    pallas_call x1, Pallas kernels, project(): pl.pallas_call(project_kernel, in_specs=[smem(), smem(), hbm, hbm, hbm],...  5.82 us
  transfers between devices with their start and end apart: 29, of which 21 were waited for; matrix products, arithmetic and copies ran while one was open for 1% of the time, Pallas kernels for 23%

profile of v8, /device:TPU:20, one launch (start us, length us, event | category | flops | bytes accessed | tf_op | source)
XLA Modules:
  0.0 170.4 jit_solution(7538871135936290137)
XLA Ops:
  0.6 1.6 copy-done
  2.2 0.7 copy-done.2
  2.9 0.7 copy-done.3
  3.6 5.8 %project.1 = (bf16[272,1024]{1,0:T(8,128)(2,1)S(1)}, bf16[528,640]{1,0:T(8,128)(2,1)S(1)}, f32[512,640]{1,0:T(8,128)S(1)}) custom-call(s32[1]{0:T(128)} %bitcast.4.me_ref, s32[1,4]{1,0:T(1,128)S(1)} %copy-done.3, bf16[256,4096]{1,0:T(8,128)(2,1)S(1)} %copy-done, bf16[4096,1024]{1,0:T(8,128)(2,1)} %weight_hbm.1, s32[4,256]{1,0:T(4,128)S(1)} %bitcast.16), custom_call_target="tpu_custom_call" | custom-call | flops 2147483648 | bytes 8388608 | tf_op jit(solution)/shard_map/project/pallas_call | solution.py:186
  9.5 1.6 collective-permute-start.5
  11.1 0.3 collective-permute-start.4
  11.6 0.9 stage.2
  12.5 1.5 collective-permute-start.2
  14.0 0.5 collective-permute-start.3
  14.4 1.5 collective-permute-start.1
  16.0 4.2 %collective-permute-done.2.refs_1_ = bf16[144,640]{1,0:T(8,128)(2,1)S(1)} collective-permute-done((bf16[144,640]{1,0:T(8,128)(2,1)}, bf16[144,640]{1,0:T(8,128)(2,1)S(1)}, u32[]{:S(2)}, u32[]{:S(2)}) %collective-permute-start.2) | collective-permute-done | bytes 184352 | tf_op jit(solution)/shard_map/ppermute | solution.py:47
  20.2 3.2 %collective-permute-done.3.refs_2_ = bf16[144,640]{1,0:T(8,128)(2,1)S(1)} collective-permute-done((bf16[144,640]{1,0:T(8,128)(2,1)}, bf16[144,640]{1,0:T(8,128)(2,1)S(1)}, u32[]{:S(2)}, u32[]{:S(2)}) %collective-permute-start.3) | collective-permute-done | bytes 184352 | tf_op jit(solution)/shard_map/ppermute | solution.py:47
  23.4 1.4 collective-permute-done.1.refs_0_
  24.7 1.0 stage.3
  25.8 8.6 %collective-permute-done.5.refs_1_ = bf16[1,272,1024]{2,1,0:T(8,128)(2,1)} collective-permute-done((bf16[1,272,1024]{2,1,0:T(8,128)(2,1)S(1)}, bf16[1,272,1024]{2,1,0:T(8,128)(2,1)}, u32[]{:S(2)}, u32[]{:S(2)}) %collective-permute-start.5) | collective-permute-done | bytes 557088 | tf_op jit(solution)/shard_map/ppermute | solution.py:47
  34.3 2.2 %collective-permute-done.4.refs_3_ = bf16[1,272,1024]{2,1,0:T(8,128)(2,1)} collective-permute-done((bf16[1,272,1024]{2,1,0:T(8,128)(2,1)S(1)}, bf16[1,272,1024]{2,1,0:T(8,128)(2,1)}, u32[]{:S(2)}, u32[]{:S(2)}) %collective-permute-start.4) | collective-permute-done | bytes 557088 | tf_op jit(solution)/shard_map/ppermute | solution.py:47
  36.6 1.3 pad_maximum_fusion
  37.9 1.6 collective-permute-start.12
  39.4 2.6 %collective-permute-start.7 = (bf16[64,640]{1,0:T(8,128)(2,1)S(1)}, bf16[64,640]{1,0:T(8,128)(2,1)S(1)}, u32[]{:S(2)}, u32[]{:S(2)}) collective-permute-start(bf16[64,640]{1,0:T(8,128)(2,1)S(1)} %get-tuple-element.60), channel_id=1, source_target_pairs={{0,16},{1,17},{2,18},{3,19},{4,20},{5,21},{6,22},{7,23},{8,24},{9,... | collective-permute-start | bytes 245768 | tf_op jit(solution)/shard_map/ppermute | solution.py:47
  42.0 1.6 collective-permute-start.8
  43.8 3.0 %collective-permute-done.7.refs_2_ = bf16[64,640]{1,0:T(8,128)(2,1)S(1)} collective-permute-done((bf16[64,640]{1,0:T(8,128)(2,1)S(1)}, bf16[64,640]{1,0:T(8,128)(2,1)S(1)}, u32[]{:S(2)}, u32[]{:S(2)}) %collective-permute-start.7) | collective-permute-done | bytes 81952 | tf_op jit(solution)/shard_map/ppermute | solution.py:47
  46.8 2.5 %collective-permute-done.8.refs_3_ = bf16[64,640]{1,0:T(8,128)(2,1)S(1)} collective-permute-done((bf16[64,640]{1,0:T(8,128)(2,1)S(1)}, bf16[64,640]{1,0:T(8,128)(2,1)S(1)}, u32[]{:S(2)}, u32[]{:S(2)}) %collective-permute-start.8) | collective-permute-done | bytes 81952 | tf_op jit(solution)/shard_map/ppermute | solution.py:47
  49.4 0.9 collective-permute-start.11
  50.3 2.2 %collective-permute-start.10 = (bf16[32,640]{1,0:T(8,128)(2,1)S(1)}, bf16[32,640]{1,0:T(8,128)(2,1)S(1)}, u32[]{:S(2)}, u32[]{:S(2)}) collective-permute-start(bf16[32,640]{1,0:T(8,128)(2,1)S(1)} %add_convert_fusion), channel_id=1, source_target_pairs={{0,16},{1,17},{2,18},{3,19},{4,20},{5,21},{6,22},{7,23},{8,24},{9,... | collective-permute-start | bytes 122888 | tf_op jit(solution)/shard_map/ppermute | solution.py:47
  52.4 0.5 collective-permute-start.9
  52.9 0.6 collective-permute-done.11
  53.5 1.6 collective-permute-done.10
  55.2 1.3 collective-permute-done.9
  56.4 7.6 %collective-permute-done.12.refs_2_ = bf16[2,272,1024]{2,1,0:T(8,128)(2,1)S(1)} collective-permute-done((bf16[2,272,1024]{2,1,0:T(8,128)(2,1)S(1)}, bf16[2,272,1024]{2,1,0:T(8,128)(2,1)S(1)}, u32[]{:S(2)}, u32[]{:S(2)}) %collective-permute-start.12) | collective-permute-done | bytes 1114144 | tf_op jit(solution)/shard_map/ppermute | solution.py:47
  64.0 1.0 copy-done.4
  65.0 2.4 %collective-permute-start.16 = (bf16[1,272,1024]{2,1,0:T(8,128)(2,1)}, bf16[1,272,1024]{2,1,0:T(8,128)(2,1)S(1)}, u32[]{:S(2)}, u32[]{:S(2)}) collective-permute-start(bf16[1,272,1024]{2,1,0:T(8,128)(2,1)} %collective-permute-done.4.refs_3_), channel_id=1, source_target_pairs={{0,8},{1,9},{2,10},{3,11},{4,12},{5,13},{6,14},{7,15},{8,0},{9,1},... | collective-permute-start | bytes 1671176 | tf_op jit(solution)/shard_map/ppermute | solution.py:47
  67.5 1.4 collective-permute-start.15
  68.9 0.5 collective-permute-start.14
  69.4 1.5 collective-permute-start.13
  71.0 0.3 cut.1
  71.2 0.7 copy-done.6
  72.0 0.7 copy-done.8
  72.7 0.7 copy-done.9
  73.4 0.7 copy-done.10
  74.1 0.7 copy-done.11
  74.8 0.3 collective-permute-done.14
  75.2 1.0 collective-permute-done.13
  76.2 2.7 %collective-permute-done.16.refs_4_ = bf16[1,272,1024]{2,1,0:T(8,128)(2,1)S(1)} collective-permute-done((bf16[1,272,1024]{2,1,0:T(8,128)(2,1)}, bf16[1,272,1024]{2,1,0:T(8,128)(2,1)S(1)}, u32[]{:S(2)}, u32[]{:S(2)}) %collective-permute-start.16) | collective-permute-done | bytes 557088 | tf_op jit(solution)/shard_map/ppermute | solution.py:47
  78.9 2.2 %pad_maximum_fusion.1 = bf16[2,272,1024]{2,1,0:T(8,128)(2,1)} fusion(bf16[1,272,1024]{2,1,0:T(8,128)(2,1)S(1)} %collective-permute-done.16.refs_4_, bf16[1,272,1024]{2,1,0:T(8,128)(2,1)} %collective-permute-done.4.refs_3_), kind=kLoop, calls=%fused_computation.1 | loop fusion | flops 557056 | bytes 2228224 | tf_op jit(solution)/shard_map/concatenate | solution.py:650
  81.0 1.5 collective-permute-start.18
  82.5 0.5 collective-permute-start.19
  83.1 1.7 %collective-permute-start.20 = (bf16[256,512]{1,0:T(8,128)(2,1)}, bf16[256,512]{1,0:T(8,128)(2,1)S(1)}, u32[]{:S(2)}, u32[]{:S(2)}) collective-permute-start(bf16[256,512]{1,0:T(8,128)(2,1)} %copy-done.10), channel_id=1, source_target_pairs={{0,8},{1,9},{2,10},{3,11},{4,12},{5,13},{6,14},{7,15},{8,0},{9,1},... | collective-permute-start | bytes 786440 | tf_op jit(solution)/shard_map/ppermute | solution.py:47
  84.8 1.2 collective-permute-start.21
  86.0 0.9 collective-permute-start.22
  86.9 15.3 %whiten.1 = (bf16[1024,1024]{1,0:T(8,128)(2,1)S(1)}, f32[1,1024]{1,0:T(1,128)S(1)}) custom-call(s32[1]{0:T(128)} %bitcast.1.place_ref, bf16[16,32,640]{2,1,0:T(8,128)(2,1)S(1)} %bitcast.11, bf16[16,32,640]{2,1,0:T(8,128)(2,1)S(1)} %collective-permute-done.17.far_ref, bf16[64,640]{1,0:T(8,128)(2,1)S(1)} %get-tuple-element.59.refs_0_, ...), custom_call_target="tpu_custom_call" | custom-call | flops 10737418240 | bytes 2097152 | tf_op jit(solution)/shard_map/whiten/pallas_call | solution.py:379
  102.2 17.3 %collective-permute-done.19.refs_1_ = bf16[256,512]{1,0:T(8,128)(2,1)S(1)} collective-permute-done((bf16[256,512]{1,0:T(8,128)(2,1)}, bf16[256,512]{1,0:T(8,128)(2,1)S(1)}, u32[]{:S(2)}, u32[]{:S(2)}) %collective-permute-start.19) | collective-permute-done | bytes 262176 | tf_op jit(solution)/shard_map/ppermute | solution.py:47
  119.5 1.8 %collective-permute-start.23 = (bf16[256,512]{1,0:T(8,128)(2,1)S(1)}, bf16[256,512]{1,0:T(8,128)(2,1)S(1)}, u32[]{:S(2)}, u32[]{:S(2)}) collective-permute-start(bf16[256,512]{1,0:T(8,128)(2,1)S(1)} %copy-done.7), channel_id=1, source_target_pairs={{0,20},{1,21},{2,22},{3,23},{4,16},{5,17},{6,18},{7,19},{8,28},{9,... | collective-permute-start | bytes 786440 | tf_op jit(solution)/shard_map/ppermute | solution.py:47
  121.3 2.3 %collective-permute-start.24 = (bf16[256,512]{1,0:T(8,128)(2,1)S(1)}, bf16[256,512]{1,0:T(8,128)(2,1)S(1)}, u32[]{:S(2)}, u32[]{:S(2)}) collective-permute-start(bf16[256,512]{1,0:T(8,128)(2,1)S(1)} %get-tuple-element.88), channel_id=1, source_target_pairs={{0,24},{1,25},{2,26},{3,27},{4,28},{5,29},{6,30},{7,31},{8,16},{9,... | collective-permute-start | bytes 786440 | tf_op jit(solution)/shard_map/ppermute | solution.py:47
  123.6 20.6 %contrast.1 = (f32[1,256]{1,0:T(1,128)}, bf16[8,256,1024]{2,1,0:T(8,128)(2,1)S(1)}) custom-call(s32[1]{0:T(128)} %bitcast.group_ref, f32[1,1024]{1,0:T(1,128)S(1)} %get-tuple-element.76.mean_ref, bf16[1024,1024]{1,0:T(8,128)(2,1)S(1)} %get-tuple-element.77.whitener_ref.refs_3_, bf16[1,272,1024]{2,1,0:T(8,128)(2,1)S(1)} %bitcast.15, ...), custom_call_target="tpu_custom_call" | custom-call | flops 12884901888 | bytes 8388608 | tf_op jit(solution)/shard_map/contrast/pallas_call | solution.py:471
  144.3 0.6 collective-permute-done.23.refs_5_
  144.8 6.9 %collective-permute-done.24.refs_6_ = bf16[256,512]{1,0:T(8,128)(2,1)S(1)} collective-permute-done((bf16[256,512]{1,0:T(8,128)(2,1)S(1)}, bf16[256,512]{1,0:T(8,128)(2,1)S(1)}, u32[]{:S(2)}, u32[]{:S(2)}) %collective-permute-start.24) | collective-permute-done | bytes 262176 | tf_op jit(solution)/shard_map/ppermute | solution.py:47
  151.8 5.5 %collective-permute-done.25.refs_7_ = bf16[256,512]{1,0:T(8,128)(2,1)S(1)} collective-permute-done((bf16[256,512]{1,0:T(8,128)(2,1)S(1)}, bf16[256,512]{1,0:T(8,128)(2,1)S(1)}, u32[]{:S(2)}, u32[]{:S(2)}) %collective-permute-start.25) | collective-permute-done | bytes 262176 | tf_op jit(solution)/shard_map/ppermute | solution.py:47
  157.3 1.3 weight_pieces.3
  158.7 1.3 weight_pieces.2
  160.0 0.5 collective-permute-start.26
  160.6 0.6 collective-permute-start.28
  161.1 0.5 collective-permute-done.26.refs_1_
  161.7 7.2 %collective-permute-done.28.refs_2_ = bf16[128,1024]{1,0:T(8,128)(2,1)S(1)} collective-permute-done((bf16[128,1024]{1,0:T(8,128)(2,1)S(1)}, bf16[128,1024]{1,0:T(8,128)(2,1)S(1)}, u32[]{:S(2)}, u32[]{:S(2)}) %collective-permute-start.28) | collective-permute-done | bytes 262176 | tf_op jit(solution)/shard_map/ppermute | solution.py:47
  168.9 1.5 finish.1
  (33 shorter events, 0.8 us)
Async XLA Ops:
  0.6 1.6 copy-start
  2.2 0.7 copy-start.2
  2.9 0.7 copy-start.3
  9.4 2.2 %collective-permute-start = (bf16[528,640]{1,0:T(8,128)(2,1)S(1)}, bf16[528,640]{1,0:T(8,128)(2,1)S(1)}, u32[]{:S(2)}, u32[]{:S(2)}) collective-permute-start(bf16[528,640]{1,0:T(8,128)(2,1)S(1)} %get-tuple-element.49.sent_ref), channel_id=1, source_target_pairs={{0,1},{1,0},{2,3},{3,2},{4,5},{5,4},{6,7},{7,6},{8,9},{9,8},{10,11... | collective-permute-start | bytes 2027528 | tf_op jit(solution)/shard_map/ppermute | solution.py:47
  9.5 24.8 %collective-permute-start.5 = (bf16[1,272,1024]{2,1,0:T(8,128)(2,1)S(1)}, bf16[1,272,1024]{2,1,0:T(8,128)(2,1)}, u32[]{:S(2)}, u32[]{:S(2)}) collective-permute-start(bf16[1,272,1024]{2,1,0:T(8,128)(2,1)S(1)} %bitcast.12), channel_id=1, source_target_pairs={{0,8},{1,9},{2,10},{3,11},{4,12},{5,13},{6,14},{7,15},{8,0},{9,1},... | collective-permute-start | bytes 1671176 | tf_op jit(solution)/shard_map/ppermute | solution.py:47
  11.1 25.4 %collective-permute-start.4 = (bf16[1,272,1024]{2,1,0:T(8,128)(2,1)S(1)}, bf16[1,272,1024]{2,1,0:T(8,128)(2,1)}, u32[]{:S(2)}, u32[]{:S(2)}) collective-permute-start(bf16[1,272,1024]{2,1,0:T(8,128)(2,1)S(1)} %bitcast.13), channel_id=1, source_target_pairs={{0,16},{1,17},{2,18},{3,19},{4,20},{5,21},{6,22},{7,23},{8,24},{9,... | collective-permute-start | bytes 1671176 | tf_op jit(solution)/shard_map/ppermute | solution.py:47
  12.5 7.7 %collective-permute-start.2 = (bf16[144,640]{1,0:T(8,128)(2,1)}, bf16[144,640]{1,0:T(8,128)(2,1)S(1)}, u32[]{:S(2)}, u32[]{:S(2)}) collective-permute-start(bf16[144,640]{1,0:T(8,128)(2,1)} %get-tuple-element.52), channel_id=1, source_target_pairs={{0,4},{1,5},{2,6},{3,7},{4,0},{5,1},{6,2},{7,3},{8,12},{9,13},{10,... | collective-permute-start | bytes 552968 | tf_op jit(solution)/shard_map/ppermute | solution.py:47
  14.0 9.4 %collective-permute-start.3 = (bf16[144,640]{1,0:T(8,128)(2,1)}, bf16[144,640]{1,0:T(8,128)(2,1)S(1)}, u32[]{:S(2)}, u32[]{:S(2)}) collective-permute-start(bf16[144,640]{1,0:T(8,128)(2,1)} %get-tuple-element.53), channel_id=1, source_target_pairs={{0,6},{1,7},{2,4},{3,5},{4,2},{5,3},{6,0},{7,1},{8,14},{9,15},{10,... | collective-permute-start | bytes 552968 | tf_op jit(solution)/shard_map/ppermute | solution.py:47
  14.4 10.3 %collective-permute-start.1 = (bf16[144,640]{1,0:T(8,128)(2,1)}, bf16[144,640]{1,0:T(8,128)(2,1)S(1)}, u32[]{:S(2)}, u32[]{:S(2)}) collective-permute-start(bf16[144,640]{1,0:T(8,128)(2,1)} %get-tuple-element.51.sent_ref), channel_id=1, source_target_pairs={{0,2},{1,3},{2,0},{3,1},{4,6},{5,7},{6,4},{7,5},{8,10},{9,11},{10,... | collective-permute-start | bytes 552968 | tf_op jit(solution)/shard_map/ppermute | solution.py:47
  36.6 34.4 %copy-start.1 = (bf16[256,4096]{1,0:T(8,128)(2,1)S(1)}, bf16[256,4096]{1,0:T(8,128)(2,1)}, u32[]{:S(2)}) copy-start(bf16[256,4096]{1,0:T(8,128)(2,1)} %features_hbm.3) | copy-start | bytes 6291460
  37.9 26.1 %collective-permute-start.12 = (bf16[2,272,1024]{2,1,0:T(8,128)(2,1)S(1)}, bf16[2,272,1024]{2,1,0:T(8,128)(2,1)S(1)}, u32[]{:S(2)}, u32[]{:S(2)}) collective-permute-start(bf16[2,272,1024]{2,1,0:T(8,128)(2,1)S(1)} %pad_maximum_fusion), channel_id=1, source_target_pairs={{0,4},{1,5},{2,6},{3,7},{4,0},{5,1},{6,2},{7,3},{8,12},{9,13},{10,... | collective-permute-start | bytes 3342344 | tf_op jit(solution)/shard_map/ppermute | solution.py:47
  39.4 7.4 %collective-permute-start.7 = (bf16[64,640]{1,0:T(8,128)(2,1)S(1)}, bf16[64,640]{1,0:T(8,128)(2,1)S(1)}, u32[]{:S(2)}, u32[]{:S(2)}) collective-permute-start(bf16[64,640]{1,0:T(8,128)(2,1)S(1)} %get-tuple-element.60), channel_id=1, source_target_pairs={{0,16},{1,17},{2,18},{3,19},{4,20},{5,21},{6,22},{7,23},{8,24},{9,... | collective-permute-start | bytes 245768 | tf_op jit(solution)/shard_map/ppermute | solution.py:47
  42.0 7.3 %collective-permute-start.8 = (bf16[64,640]{1,0:T(8,128)(2,1)S(1)}, bf16[64,640]{1,0:T(8,128)(2,1)S(1)}, u32[]{:S(2)}, u32[]{:S(2)}) collective-permute-start(bf16[64,640]{1,0:T(8,128)(2,1)S(1)} %get-tuple-element.61), channel_id=1, source_target_pairs={{0,24},{1,25},{2,26},{3,27},{4,28},{5,29},{6,30},{7,31},{8,16},{9,... | collective-permute-start | bytes 245768 | tf_op jit(solution)/shard_map/ppermute | solution.py:47
  43.6 5.8 %collective-permute-start.6 = (bf16[64,640]{1,0:T(8,128)(2,1)S(1)}, bf16[64,640]{1,0:T(8,128)(2,1)S(1)}, u32[]{:S(2)}, u32[]{:S(2)}) collective-permute-start(bf16[64,640]{1,0:T(8,128)(2,1)S(1)} %get-tuple-element.59.refs_0_), channel_id=1, source_target_pairs={{0,8},{1,9},{2,10},{3,11},{4,12},{5,13},{6,14},{7,15},{8,0},{9,1},... | collective-permute-start | bytes 245768 | tf_op jit(solution)/shard_map/ppermute | solution.py:47
  49.4 4.1 %collective-permute-start.11 = (bf16[32,640]{1,0:T(8,128)(2,1)S(1)}, bf16[32,640]{1,0:T(8,128)(2,1)S(1)}, u32[]{:S(2)}, u32[]{:S(2)}) collective-permute-start(bf16[32,640]{1,0:T(8,128)(2,1)S(1)} %add_convert_fusion), channel_id=1, source_target_pairs={{0,24},{1,25},{2,26},{3,27},{4,28},{5,29},{6,30},{7,31},{8,16},{9,... | collective-permute-start | bytes 122888 | tf_op jit(solution)/shard_map/ppermute | solution.py:47
  50.3 4.9 %collective-permute-start.10 = (bf16[32,640]{1,0:T(8,128)(2,1)S(1)}, bf16[32,640]{1,0:T(8,128)(2,1)S(1)}, u32[]{:S(2)}, u32[]{:S(2)}) collective-permute-start(bf16[32,640]{1,0:T(8,128)(2,1)S(1)} %add_convert_fusion), channel_id=1, source_target_pairs={{0,16},{1,17},{2,18},{3,19},{4,20},{5,21},{6,22},{7,23},{8,24},{9,... | collective-permute-start | bytes 122888 | tf_op jit(solution)/shard_map/ppermute | solution.py:47
  52.4 4.0 %collective-permute-start.9 = (bf16[32,640]{1,0:T(8,128)(2,1)S(1)}, bf16[32,640]{1,0:T(8,128)(2,1)S(1)}, u32[]{:S(2)}, u32[]{:S(2)}) collective-permute-start(bf16[32,640]{1,0:T(8,128)(2,1)S(1)} %add_convert_fusion), channel_id=1, source_target_pairs={{0,8},{1,9},{2,10},{3,11},{4,12},{5,13},{6,14},{7,15},{8,0},{9,1},... | collective-permute-start | bytes 122888 | tf_op jit(solution)/shard_map/ppermute | solution.py:47
  64.0 1.0 copy-start.4
  65.0 13.8 %collective-permute-start.16 = (bf16[1,272,1024]{2,1,0:T(8,128)(2,1)}, bf16[1,272,1024]{2,1,0:T(8,128)(2,1)S(1)}, u32[]{:S(2)}, u32[]{:S(2)}) collective-permute-start(bf16[1,272,1024]{2,1,0:T(8,128)(2,1)} %collective-permute-done.4.refs_3_), channel_id=1, source_target_pairs={{0,8},{1,9},{2,10},{3,11},{4,12},{5,13},{6,14},{7,15},{8,0},{9,1},... | collective-permute-start | bytes 1671176 | tf_op jit(solution)/shard_map/ppermute | solution.py:47
  67.5 7.4 %collective-permute-start.15 = (bf16[128,640]{1,0:T(8,128)(2,1)S(1)}, bf16[128,640]{1,0:T(8,128)(2,1)S(1)}, u32[]{:S(2)}, u32[]{:S(2)}) collective-permute-start(bf16[128,640]{1,0:T(8,128)(2,1)S(1)} %pad_maximum_fusion.3), channel_id=1, source_target_pairs={{0,6},{1,7},{2,4},{3,5},{4,2},{5,3},{6,0},{7,1},{8,14},{9,15},{10,... | collective-permute-start | bytes 491528 | tf_op jit(solution)/shard_map/ppermute | solution.py:47
  68.9 6.3 %collective-permute-start.14 = (bf16[128,640]{1,0:T(8,128)(2,1)S(1)}, bf16[128,640]{1,0:T(8,128)(2,1)S(1)}, u32[]{:S(2)}, u32[]{:S(2)}) collective-permute-start(bf16[128,640]{1,0:T(8,128)(2,1)S(1)} %pad_maximum_fusion.3), channel_id=1, source_target_pairs={{0,4},{1,5},{2,6},{3,7},{4,0},{5,1},{6,2},{7,3},{8,12},{9,13},{10,... | collective-permute-start | bytes 491528 | tf_op jit(solution)/shard_map/ppermute | solution.py:47
  69.4 6.7 %collective-permute-start.13 = (bf16[128,640]{1,0:T(8,128)(2,1)S(1)}, bf16[128,640]{1,0:T(8,128)(2,1)S(1)}, u32[]{:S(2)}, u32[]{:S(2)}) collective-permute-start(bf16[128,640]{1,0:T(8,128)(2,1)S(1)} %pad_maximum_fusion.3), channel_id=1, source_target_pairs={{0,2},{1,3},{2,0},{3,1},{4,6},{5,7},{6,4},{7,5},{8,10},{9,11},{10,... | collective-permute-start | bytes 491528 | tf_op jit(solution)/shard_map/ppermute | solution.py:47
  71.2 0.7 copy-start.6
  72.0 0.7 copy-start.8
  72.7 0.7 copy-start.9
  73.4 0.7 copy-start.10
  74.1 0.7 copy-start.11
  78.9 7.1 %collective-permute-start.17 = (bf16[16,32,640]{2,1,0:T(8,128)(2,1)S(1)}, bf16[16,32,640]{2,1,0:T(8,128)(2,1)S(1)}, u32[]{:S(2)}, u32[]{:S(2)}) collective-permute-start(bf16[16,32,640]{2,1,0:T(8,128)(2,1)S(1)} %bitcast.10), channel_id=1, source_target_pairs={{0,1},{1,0},{2,3},{3,2},{4,5},{5,4},{6,7},{7,6},{8,9},{9,8},{10,11... | collective-permute-start | bytes 1966088 | tf_op jit(solution)/shard_map/ppermute | solution.py:47
  81.0 42.6 %collective-permute-start.18 = (bf16[2,272,1024]{2,1,0:T(8,128)(2,1)}, bf16[2,272,1024]{2,1,0:T(8,128)(2,1)}, u32[]{:S(2)}, u32[]{:S(2)}) collective-permute-start(bf16[2,272,1024]{2,1,0:T(8,128)(2,1)} %pad_maximum_fusion.1), channel_id=1, source_target_pairs={{0,4},{1,5},{2,6},{3,7},{4,0},{5,1},{6,2},{7,3},{8,12},{9,13},{10,... | collective-permute-start | bytes 3342344 | tf_op jit(solution)/shard_map/ppermute | solution.py:47
  82.5 36.9 %collective-permute-start.19 = (bf16[256,512]{1,0:T(8,128)(2,1)}, bf16[256,512]{1,0:T(8,128)(2,1)S(1)}, u32[]{:S(2)}, u32[]{:S(2)}) collective-permute-start(bf16[256,512]{1,0:T(8,128)(2,1)} %copy-done.11), channel_id=1, source_target_pairs={{0,4},{1,5},{2,6},{3,7},{4,0},{5,1},{6,2},{7,3},{8,12},{9,13},{10,... | collective-permute-start | bytes 786440 | tf_op jit(solution)/shard_map/ppermute | solution.py:47
  83.1 38.2 %collective-permute-start.20 = (bf16[256,512]{1,0:T(8,128)(2,1)}, bf16[256,512]{1,0:T(8,128)(2,1)S(1)}, u32[]{:S(2)}, u32[]{:S(2)}) collective-permute-start(bf16[256,512]{1,0:T(8,128)(2,1)} %copy-done.10), channel_id=1, source_target_pairs={{0,8},{1,9},{2,10},{3,11},{4,12},{5,13},{6,14},{7,15},{8,0},{9,1},... | collective-permute-start | bytes 786440 | tf_op jit(solution)/shard_map/ppermute | solution.py:47
  84.8 59.5 %collective-permute-start.21 = (bf16[256,512]{1,0:T(8,128)(2,1)}, bf16[256,512]{1,0:T(8,128)(2,1)S(1)}, u32[]{:S(2)}, u32[]{:S(2)}) collective-permute-start(bf16[256,512]{1,0:T(8,128)(2,1)} %copy-done.9), channel_id=1, source_target_pairs={{0,12},{1,13},{2,14},{3,15},{4,8},{5,9},{6,10},{7,11},{8,4},{9,5},... | collective-permute-start | bytes 786440 | tf_op jit(solution)/shard_map/ppermute | solution.py:47
  86.0 58.3 %collective-permute-start.22 = (bf16[256,512]{1,0:T(8,128)(2,1)}, bf16[256,512]{1,0:T(8,128)(2,1)S(1)}, u32[]{:S(2)}, u32[]{:S(2)}) collective-permute-start(bf16[256,512]{1,0:T(8,128)(2,1)} %copy-done.8), channel_id=1, source_target_pairs={{0,16},{1,17},{2,18},{3,19},{4,20},{5,21},{6,22},{7,23},{8,24},{9,... | collective-permute-start | bytes 786440 | tf_op jit(solution)/shard_map/ppermute | solution.py:47
  86.9 32.5 %copy-start.7 = (bf16[256,512]{1,0:T(8,128)(2,1)S(1)}, bf16[256,512]{1,0:T(8,128)(2,1)}, u32[]{:S(2)}) copy-start(bf16[256,512]{1,0:T(8,128)(2,1)} %copy-done.6) | copy-start | bytes 786436
  86.9 36.7 %copy-start.5 = (bf16[2,272,1024]{2,1,0:T(8,128)(2,1)S(1)}, bf16[2,272,1024]{2,1,0:T(8,128)(2,1)}, u32[]{:S(2)}) copy-start(bf16[2,272,1024]{2,1,0:T(8,128)(2,1)} %copy-done.4) | copy-start | bytes 3342340
  119.5 25.4 %collective-permute-start.23 = (bf16[256,512]{1,0:T(8,128)(2,1)S(1)}, bf16[256,512]{1,0:T(8,128)(2,1)S(1)}, u32[]{:S(2)}, u32[]{:S(2)}) collective-permute-start(bf16[256,512]{1,0:T(8,128)(2,1)S(1)} %copy-done.7), channel_id=1, source_target_pairs={{0,20},{1,21},{2,22},{3,23},{4,16},{5,17},{6,18},{7,19},{8,28},{9,... | collective-permute-start | bytes 786440 | tf_op jit(solution)/shard_map/ppermute | solution.py:47
  121.3 30.5 %collective-permute-start.24 = (bf16[256,512]{1,0:T(8,128)(2,1)S(1)}, bf16[256,512]{1,0:T(8,128)(2,1)S(1)}, u32[]{:S(2)}, u32[]{:S(2)}) collective-permute-start(bf16[256,512]{1,0:T(8,128)(2,1)S(1)} %get-tuple-element.88), channel_id=1, source_target_pairs={{0,24},{1,25},{2,26},{3,27},{4,28},{5,29},{6,30},{7,31},{8,16},{9,... | collective-permute-start | bytes 786440 | tf_op jit(solution)/shard_map/ppermute | solution.py:47
  123.6 33.7 %collective-permute-start.25 = (bf16[256,512]{1,0:T(8,128)(2,1)S(1)}, bf16[256,512]{1,0:T(8,128)(2,1)S(1)}, u32[]{:S(2)}, u32[]{:S(2)}) collective-permute-start(bf16[256,512]{1,0:T(8,128)(2,1)S(1)} %get-tuple-element.89), channel_id=1, source_target_pairs={{0,28},{1,29},{2,30},{3,31},{4,24},{5,25},{6,26},{7,27},{8,20},{9,... | collective-permute-start | bytes 786440 | tf_op jit(solution)/shard_map/ppermute | solution.py:47
  158.6 2.0 %collective-permute-start.27 = (bf16[128,1024]{1,0:T(8,128)(2,1)S(1)}, bf16[128,1024]{1,0:T(8,128)(2,1)S(1)}, u32[]{:S(2)}, u32[]{:S(2)}) collective-permute-start(bf16[128,1024]{1,0:T(8,128)(2,1)S(1)} %get-tuple-element.93), channel_id=1, source_target_pairs={{0,1},{1,0},{2,3},{3,2},{4,5},{5,4},{6,7},{7,6},{8,9},{9,8},{10,11... | collective-permute-start | bytes 786440 | tf_op jit(solution)/shard_map/ppermute | solution.py:47
  160.0 1.7 collective-permute-start.26
  160.6 8.3 %collective-permute-start.28 = (bf16[128,1024]{1,0:T(8,128)(2,1)S(1)}, bf16[128,1024]{1,0:T(8,128)(2,1)S(1)}, u32[]{:S(2)}, u32[]{:S(2)}) collective-permute-start(bf16[128,1024]{1,0:T(8,128)(2,1)S(1)} %join.1), channel_id=1, source_target_pairs={{0,2},{1,3},{2,0},{3,1},{4,6},{5,7},{6,4},{7,5},{8,10},{9,11},{10,... | collective-permute-start | bytes 786440 | tf_op jit(solution)/shard_map/ppermute | solution.py:47

commit v9 on v8

--- a/solution.py
+++ b/solution.py
@@ -71,7 +71,7 @@
     return pl.pallas_call(
         cut_kernel,
         in_specs=[smem(), pl.BlockSpec(memory_space=pltpu.HBM)],
-        out_specs=[vmem()] * groups,
+        out_specs=[pl.BlockSpec(memory_space=pltpu.HBM)] * groups,
         out_shape=[jax.ShapeDtypeStruct((rows, depth // groups), BF16)] * groups,
         scratch_shapes=[pltpu.SemaphoreType.DMA((groups,))],
         compiler_params=params(8),
@@ -200,7 +200,7 @@
             pltpu.VMEM((rows, embed + packed - LANES), BF16),
             pltpu.SemaphoreType.DMA((2, CHUNKS + 1)),
         ],
-        compiler_params=params(49),
+        compiler_params=params(51),
         cost_estimate=pl.CostEstimate(
             flops=2 * rows * depth * embed, bytes_accessed=2 * depth * embed, transcendentals=0
         ),
@@ -274,14 +274,16 @@
             axis=0,
         )
         total_rows = rows * totals.shape[0]
-        tile = 512
-        tiles = embed // tile
+        tile = 256
 
         mean = jnp.sum(totals, axis=0, keepdims=True) * (1.0 / total_rows)
         mean_ref[...] = mean
         shift_high, shift_low = split(totals * (1.0 / rows) - mean)
         shift_left = jnp.concatenate([shift_high, shift_high, shift_low], axis=0)
         shift_right = jnp.concatenate([shift_high, shift_low, shift_high], axis=0)
+
+        def block_at(i, j):
+            return slice(i * LANES, (i + 1) * LANES), slice(j * LANES, (j + 1) * LANES)
 
         def unpack(source_ref, side):
             for i in range(side * half, (side + 1) * half):
@@ -305,69 +307,81 @@
                 unpack(far_ref, 1 - core)
 
         for i in range(blocks):
-            for k in range(1, half + 1):
-                if k == half and i >= half:
-                    continue
-                j = (i + k) % blocks
-                scaled[j * LANES : (j + 1) * LANES, i * LANES : (i + 1) * LANES] = scaled[
-                    i * LANES : (i + 1) * LANES, j * LANES : (j + 1) * LANES
-                ].T
-        squares = jnp.zeros((1, embed), F32)
-        for t in range(tiles):
-            lines = slice(t * tile, (t + 1) * tile)
-            between = dot(shift_left[:, lines], shift_right, (0, 0))
-            covariance = (scaled[lines, :] + rows * between) * (1.0 / total_rows)
-            scaled[lines, :] = covariance
-            first[lines, :] = covariance.astype(BF16)
-            squares = squares + jnp.sum(covariance * covariance, axis=0, keepdims=True)
+            for j in range(blocks):
+                held = (j - i) % blocks < half or ((j - i) % blocks == half and i < half)
+                if not held and i * LANES // tile <= j * LANES // tile:
+                    scaled[block_at(i, j)] = scaled[block_at(j, i)].T
+
+        panels = []
+        for t in range(embed // tile):
+            panels.append((slice(0, (t + 1) * tile), slice(t * tile, (t + 1) * tile)))
+
+        def mirror(out, panel, value):
+            rows_at, columns_at = panel
+            value = value.astype(BF16)
+            out[panel] = value
+            above = columns_at.start
+            if above:
+                out[columns_at, 0:above] = value[0:above].T
+
+        squares = jnp.zeros((1, tile), F32)
+        for panel in panels:
+            rows_at, columns_at = panel
+            between = dot(shift_left[:, rows_at], shift_right[:, columns_at], (0, 0))
+            covariance = (scaled[panel] + rows * between) * (1.0 / total_rows)
+            scaled[panel] = covariance
+            mirror(first, panel, covariance)
+            above = columns_at.start
+            square = covariance * covariance
+            squares = squares + jnp.sum(square[above:], axis=0, keepdims=True)
+            if above:
+                squares = squares + 2.0 * jnp.sum(square[:above], axis=0, keepdims=True)
         frobenius = jnp.sqrt(jnp.sum(squares, axis=1, keepdims=True))
         inverse = 1.0 / frobenius
         root = lax.rsqrt(frobenius)
 
         def product(one, two, finish):
-            @pl.loop(0, tiles)
-            def _(t):
-                lines = pl.ds(pl.multiple_of(t * tile, tile), tile)
-                finish(lines, dot(one[lines, :], two[...]))
-
-        def second(lines, value):
+            for panel in panels:
+                finish(panel, dot(one[panel[0], :], two[:, panel[1]]))
+
+        def second(panel, value):
             value = value * (inverse * inverse)
-            own = scaled[lines, :] * inverse
-            scaled[lines, :] = own
-            rest[lines, :] = 27.0 * value - 39.0 * own
-            left[lines, :] = value.astype(BF16)
-            right[lines, :] = (value - 9.0 * own).astype(BF16)
+            own = scaled[panel] * inverse
+            scaled[panel] = own
+            rest[panel] = 27.0 * value - 39.0 * own
+            mirror(left, panel, value)
+            mirror(right, panel, value - 9.0 * own)
 
         product(first, first, second)
 
-        def fourth(lines, value):
-            value = (value + rest[lines, :]) * (1.0 / 16.0)
-            rest[lines, :] = value
-            whitener_ref[lines, :] = value.astype(BF16)
+        def fourth(panel, value):
+            value = (value + rest[panel]) * (1.0 / 16.0)
+            rest[panel] = value
+            mirror(whitener_ref, panel, value)
 
         product(left, right, fourth)
 
-        def moved(lines, value):
+        def moved(panel, value):
             value = value * inverse
-            scaled[lines, :] = 2.25 * 2.25 * scaled[lines, :] + 4.5 * value
-            right[lines, :] = value.astype(BF16)
+            scaled[panel] = 2.25 * 2.25 * scaled[panel] + 4.5 * value
+            mirror(right, panel, value)
 
         product(first, whitener_ref, moved)
 
-        def quad(lines, value):
-            value = value + scaled[lines, :]
-            rest[lines, :] = 3.0 * rest[lines, :] - 2.25 * value
-            left[lines, :] = value.astype(BF16)
+        def quad(panel, value):
+            value = value + scaled[panel]
+            rest[panel] = 3.0 * rest[panel] - 2.25 * value
+            mirror(left, panel, value)
 
         product(whitener_ref, right, quad)
         first[...] = whitener_ref[...]
 
-        def last(lines, value):
-            at = lax.broadcasted_iota(jnp.int32, value.shape, 0) + lines.start
-            eye = at == lax.broadcasted_iota(jnp.int32, value.shape, 1)
-            value = 0.5 * (rest[lines, :] - value)
+        def last(panel, value):
+            at = lax.broadcasted_iota(jnp.int32, value.shape, 0)
+            eye = at == lax.broadcasted_iota(jnp.int32, value.shape, 1) + panel[1].start
+            value = 0.5 * (rest[panel] - value)
             value = value + jnp.where(eye, 0.5 * 3.0 * 2.25, 0.0)
-            whitener_ref[lines, :] = (value * root).astype(BF16)
+            mirror(whitener_ref, panel, value * root)
 
         product(first, left, last)
 
@@ -494,14 +508,15 @@
     )(group, mean, whitener, *blocks)
 
 
-def pieces_kernel(share, masks, group_ref, window_ref, grad_ref, *refs):
+def pieces_kernel(share, masks, order, group_ref, window_ref, grad_ref, *refs):
     groups = grad_ref.shape[0]
     features, (keep_ref, send_ref, total) = refs[:groups], refs[groups:]
 
     def columns(at):
-        value = dot(features[0][:, at], grad_ref[group_ref[0]], (0, 0))
-        for k in range(1, groups):
-            value = value + dot(features[k][:, at], grad_ref[group_ref[0] ^ k], (0, 0))
+        value = None
+        for k, feature_ref in zip(order, features):
+            term = dot(feature_ref[:, at], grad_ref[group_ref[0] ^ k], (0, 0))
+            value = term if value is None else value + term
         return value
 
     if share % LANES:
@@ -513,13 +528,13 @@
         out[n * share : (n + 1) * share, :] = value.astype(out.dtype)
 
 
-def weight_pieces(group, window, grad, slices, shares, masks):
+def weight_pieces(group, window, grad, slices, order, shares, masks):
     groups, rows, embed = grad.shape
     columns = slices[0].shape[1]
     share = columns // shares
     half = len(masks) // 2 * share
     return pl.pallas_call(
-        functools.partial(pieces_kernel, share, masks),
+        functools.partial(pieces_kernel, share, masks, order),
         in_specs=[smem(), smem()] + [vmem()] * (1 + len(slices)),
         out_specs=[vmem()] * 2,
         out_shape=[
@@ -597,12 +612,15 @@
     )
     block = block[None]
     if direct:
+        block_x = xor_permute(block, by_x)
         block_far = xor_permute(block, by_far)
         block_near = xor_permute(block, by_near)
     else:
         gathered = lax.all_gather(block, "sp", tiled=True)
 
     arrived = [xor_permute(send, 1)]
+    if direct:
+        arrived[0], block_x = lax.optimization_barrier((arrived[0], block_x))
     sent = send
     seen = 1
     stages = []
@@ -618,7 +636,7 @@
                 (*sends, block_far, block_near, group_scalar)
             )
             slices = cut(group_scalar, features, groups)
-            pair_x = xor_permute(jnp.concatenate([block, block_near]), by_x)
+            pair_x = xor_permute(jnp.concatenate([block_far, block_near]), by_x)
         arrived = [xor_permute(piece, (r + 1) << low) for r, piece in enumerate(sends)]
         sent = sends[0]
         stages.append((low, count))
@@ -639,33 +657,37 @@
     part = part.astype(BF16)
     for number, (low, count) in enumerate(reversed(stages)):
         if direct and number == 1:
-            part, pair_x, block_far = lax.optimization_barrier((part, pair_x, block_far))
+            part, block_far = lax.optimization_barrier((part, block_far))
             block_far_near = xor_permute(block_far, by_near)
+            part, pair_x = lax.optimization_barrier((part, pair_x))
         part = jnp.concatenate(
             [part] + [xor_permute(part, r << low) for r in range(1, count)], axis=0
         )
     part = part.reshape(-1, size, part.shape[1])
     if direct:
-        part, block_far_near, *slices = lax.optimization_barrier((part, block_far_near, *slices))
-        far_x = xor_permute(jnp.concatenate([block_far, block_far_near]), by_x)
-        blocks = [block, block_near, pair_x, block_far, block_far_near, far_x]
-        order = [0, 2, 1, 3, 4, 6, 5, 7]
-        slices = list(slices)
-        for k in (2, 4, 6, 1, 3, 5, 7):
-            slices[k] = xor_permute(slices[k], k * shares)
+        part, block_far_near = lax.optimization_barrier((part, block_far_near))
+        far_near_x = xor_permute(block_far_near, by_x)
+        blocks = [block, block_x, block_near, block_far, pair_x, block_far_near, far_near_x]
+        order = [0, 1, 2, 4, 5, 3, 6, 7]
     else:
-        order = list(range(groups))
+        order = slice_order = list(range(groups))
         blocks = [
             lax.dynamic_index_in_dim(gathered, group ^ k, 0, keepdims=True) for k in order
         ]
     other = xor_permute(part, 1)
+    if direct:
+        other, *slices = lax.optimization_barrier((other, *slices))
+        slice_order = [0, 2, 4, 6, 1, 3, 5, 7]
+        slices = [xor_permute(slices[k], k * shares) if k else slices[k] for k in slice_order]
 
     whitener, mean = whiten(place.reshape(1), part, other, sums, seen, rows, embed)
     loss, grad = contrast(group.reshape(1), blocks, order, mean, whitener)
     group, window = group.reshape(1), window.reshape(1)
     pieces = []
     for mask in reversed(range(0, shares, 2)):
-        keep, send = weight_pieces(group, window, grad, slices, shares, (mask, mask + 1))
+        keep, send = weight_pieces(
+            group, window, grad, slices, slice_order, shares, (mask, mask + 1)
+        )
         arrived = xor_permute(send, 1)
         if mask:
             pieces.append(xor_permute(join(keep, arrived), mask))

time: 171 us -> 141 us (0.82)
  the two profiles are of different devices: /device:TPU:20 before, /device:TPU:0 now
where the time goes in v9:
time: 141 us; the launch traced here: 139 us
  waiting for transfers between devices  44.8 us (32%)
  Pallas kernels  43.6 us (31%)
  starting transfers between devices  42.7 us (30%)
  local copies, waits for them, and re-layouts  5.65 us (4%)
    ppermute x30, waiting for transfers between devices, xor_permute(): return lax.ppermute(piece, AXES, [(i, i ^ mask) for i in range(devices)])  44.8 us
    ppermute x30, starting transfers between devices, xor_permute(): return lax.ppermute(piece, AXES, [(i, i ^ mask) for i in range(devices)])  42.7 us
    pallas_call x1, Pallas kernels, contrast(): pl.pallas_call(functools.partial(contrast_kernel, order), in_specs=[smem(...  20.5 us
    pallas_call x1, Pallas kernels, whiten(): pl.pallas_call(make_whiten_kernel(rows, count), in_specs=[smem()] + [vmem...  10.8 us
    pallas_call x1, Pallas kernels, project(): pl.pallas_call(project_kernel, in_specs=[smem(), smem(), hbm, hbm, hbm],...  6.82 us
    unnamed x22, local copies, waits for them, and re-layouts  5.65 us
  transfers between devices with their start and end apart: 30, of which 17 were waited for; matrix products, arithmetic and copies ran while one was open for 0% of the time, Pallas kernels for 24%

profile of v9, /device:TPU:0, one launch (start us, length us, event | category | flops | bytes accessed | tf_op | source)
XLA Modules:
  0.0 139.0 jit_solution(10316129624832484003)
XLA Ops:
  0.6 0.7 copy-done.3
  1.3 0.7 copy-done.4
  2.0 6.8 %project.1 = (bf16[272,1024]{1,0:T(8,128)(2,1)}, bf16[528,640]{1,0:T(8,128)(2,1)S(1)}, f32[512,640]{1,0:T(8,128)S(1)}) custom-call(s32[1]{0:T(128)} %bitcast.4.me_ref, s32[1,4]{1,0:T(1,128)S(1)} %copy-done.4, bf16[256,4096]{1,0:T(8,128)(2,1)} %features_hbm.3, bf16[4096,1024]{1,0:T(8,128)(2,1)} %weight_hbm.1, s32[4,256]{1,0:T(4,128)S(1)} %bitcast.12), custom_call_target="tpu_custom_call" | custom-call | flops 2147483648 | bytes 8388608 | tf_op jit(solution)/shard_map/project/pallas_call | solution.py:186
  8.8 0.5 collective-permute-start
  9.3 2.6 %collective-permute-start.1 = (bf16[1,272,1024]{2,1,0:T(8,128)(2,1)}, bf16[1,272,1024]{2,1,0:T(8,128)(2,1)}, u32[]{:S(2)}, u32[]{:S(2)}) collective-permute-start(bf16[1,272,1024]{2,1,0:T(8,128)(2,1)} %bitcast.6.refs_0_), channel_id=1, source_target_pairs={{0,4},{1,5},{2,6},{3,7},{4,0},{5,1},{6,2},{7,3},{8,12},{9,13},{10,... | collective-permute-start | bytes 1671176 | tf_op jit(solution)/shard_map/ppermute | solution.py:47
  11.9 1.6 %collective-permute-start.6 = (bf16[1,272,1024]{2,1,0:T(8,128)(2,1)}, bf16[1,272,1024]{2,1,0:T(8,128)(2,1)S(1)}, u32[]{:S(2)}, u32[]{:S(2)}) collective-permute-start(bf16[1,272,1024]{2,1,0:T(8,128)(2,1)} %bitcast.6.refs_0_), channel_id=1, source_target_pairs={{0,8},{1,9},{2,10},{3,11},{4,12},{5,13},{6,14},{7,15},{8,0},{9,1},... | collective-permute-start | bytes 1671176 | tf_op jit(solution)/shard_map/ppermute | solution.py:47
  13.5 2.6 %collective-permute-start.5 = (bf16[1,272,1024]{2,1,0:T(8,128)(2,1)}, bf16[1,272,1024]{2,1,0:T(8,128)(2,1)}, u32[]{:S(2)}, u32[]{:S(2)}) collective-permute-start(bf16[1,272,1024]{2,1,0:T(8,128)(2,1)} %bitcast.6.refs_0_), channel_id=1, source_target_pairs={{0,16},{1,17},{2,18},{3,19},{4,20},{5,21},{6,22},{7,23},{8,24},{9,... | collective-permute-start | bytes 1671176 | tf_op jit(solution)/shard_map/ppermute | solution.py:47
  16.1 9.4 %collective-permute-done.1.refs_1_ = bf16[1,272,1024]{2,1,0:T(8,128)(2,1)} collective-permute-done((bf16[1,272,1024]{2,1,0:T(8,128)(2,1)}, bf16[1,272,1024]{2,1,0:T(8,128)(2,1)}, u32[]{:S(2)}, u32[]{:S(2)}) %collective-permute-start.1) | collective-permute-done | bytes 557088 | tf_op jit(solution)/shard_map/ppermute | solution.py:47
  25.4 0.9 stage.2
  26.3 0.7 copy-done.1
  27.0 1.8 %collective-permute-start.3 = (bf16[144,640]{1,0:T(8,128)(2,1)}, bf16[144,640]{1,0:T(8,128)(2,1)S(1)}, u32[]{:S(2)}, u32[]{:S(2)}) collective-permute-start(bf16[144,640]{1,0:T(8,128)(2,1)} %get-tuple-element.58), channel_id=1, source_target_pairs={{0,4},{1,5},{2,6},{3,7},{4,0},{5,1},{6,2},{7,3},{8,12},{9,13},{10,... | collective-permute-start | bytes 552968 | tf_op jit(solution)/shard_map/ppermute | solution.py:47
  28.8 1.5 %collective-permute-start.4 = (bf16[144,640]{1,0:T(8,128)(2,1)}, bf16[144,640]{1,0:T(8,128)(2,1)S(1)}, u32[]{:S(2)}, u32[]{:S(2)}) collective-permute-start(bf16[144,640]{1,0:T(8,128)(2,1)} %get-tuple-element.59), channel_id=1, source_target_pairs={{0,6},{1,7},{2,4},{3,5},{4,2},{5,3},{6,0},{7,1},{8,14},{9,15},{10,... | collective-permute-start | bytes 552968 | tf_op jit(solution)/shard_map/ppermute | solution.py:47
  30.3 0.2 collective-permute-start.2
  30.5 4.2 %collective-permute-done.3.refs_1_ = bf16[144,640]{1,0:T(8,128)(2,1)S(1)} collective-permute-done((bf16[144,640]{1,0:T(8,128)(2,1)}, bf16[144,640]{1,0:T(8,128)(2,1)S(1)}, u32[]{:S(2)}, u32[]{:S(2)}) %collective-permute-start.3) | collective-permute-done | bytes 184352 | tf_op jit(solution)/shard_map/ppermute | solution.py:47
  34.7 4.0 %collective-permute-done.4.refs_2_ = bf16[144,640]{1,0:T(8,128)(2,1)S(1)} collective-permute-done((bf16[144,640]{1,0:T(8,128)(2,1)}, bf16[144,640]{1,0:T(8,128)(2,1)S(1)}, u32[]{:S(2)}, u32[]{:S(2)}) %collective-permute-start.4) | collective-permute-done | bytes 184352 | tf_op jit(solution)/shard_map/ppermute | solution.py:47
  38.7 1.2 collective-permute-done.2.refs_0_
  39.9 1.0 copy-done.2
  40.8 0.1 stage.3
  41.0 0.1 collective-permute-done.5.refs_3_
  41.1 1.3 pad_maximum_fusion
  42.4 1.4 %collective-permute-start.13 = (bf16[2,272,1024]{2,1,0:T(8,128)(2,1)S(1)}, bf16[2,272,1024]{2,1,0:T(8,128)(2,1)S(1)}, u32[]{:S(2)}, u32[]{:S(2)}) collective-permute-start(bf16[2,272,1024]{2,1,0:T(8,128)(2,1)S(1)} %pad_maximum_fusion), channel_id=1, source_target_pairs={{0,4},{1,5},{2,6},{3,7},{4,0},{5,1},{6,2},{7,3},{8,12},{9,13},{10,... | collective-permute-start | bytes 3342344 | tf_op jit(solution)/shard_map/ppermute | solution.py:47
  43.9 2.6 %collective-permute-start.8 = (bf16[64,640]{1,0:T(8,128)(2,1)S(1)}, bf16[64,640]{1,0:T(8,128)(2,1)S(1)}, u32[]{:S(2)}, u32[]{:S(2)}) collective-permute-start(bf16[64,640]{1,0:T(8,128)(2,1)S(1)} %get-tuple-element.65), channel_id=1, source_target_pairs={{0,16},{1,17},{2,18},{3,19},{4,20},{5,21},{6,22},{7,23},{8,24},{9,... | collective-permute-start | bytes 245768 | tf_op jit(solution)/shard_map/ppermute | solution.py:47
  46.4 1.3 collective-permute-start.9
  47.8 0.2 collective-permute-start.7
  48.0 2.1 %collective-permute-done.8.refs_2_ = bf16[64,640]{1,0:T(8,128)(2,1)S(1)} collective-permute-done((bf16[64,640]{1,0:T(8,128)(2,1)S(1)}, bf16[64,640]{1,0:T(8,128)(2,1)S(1)}, u32[]{:S(2)}, u32[]{:S(2)}) %collective-permute-start.8) | collective-permute-done | bytes 81952 | tf_op jit(solution)/shard_map/ppermute | solution.py:47
  50.1 2.7 %collective-permute-done.9.refs_3_ = bf16[64,640]{1,0:T(8,128)(2,1)S(1)} collective-permute-done((bf16[64,640]{1,0:T(8,128)(2,1)S(1)}, bf16[64,640]{1,0:T(8,128)(2,1)S(1)}, u32[]{:S(2)}, u32[]{:S(2)}) %collective-permute-start.9) | collective-permute-done | bytes 81952 | tf_op jit(solution)/shard_map/ppermute | solution.py:47
  52.8 0.3 collective-permute-done.7.refs_1_
  53.1 2.3 %collective-permute-start.12 = (bf16[32,640]{1,0:T(8,128)(2,1)S(1)}, bf16[32,640]{1,0:T(8,128)(2,1)S(1)}, u32[]{:S(2)}, u32[]{:S(2)}) collective-permute-start(bf16[32,640]{1,0:T(8,128)(2,1)S(1)} %add_convert_fusion), channel_id=1, source_target_pairs={{0,24},{1,25},{2,26},{3,27},{4,28},{5,29},{6,30},{7,31},{8,16},{9,... | collective-permute-start | bytes 122888 | tf_op jit(solution)/shard_map/ppermute | solution.py:47
  55.4 2.2 %collective-permute-start.10 = (bf16[32,640]{1,0:T(8,128)(2,1)S(1)}, bf16[32,640]{1,0:T(8,128)(2,1)S(1)}, u32[]{:S(2)}, u32[]{:S(2)}) collective-permute-start(bf16[32,640]{1,0:T(8,128)(2,1)S(1)} %add_convert_fusion), channel_id=1, source_target_pairs={{0,8},{1,9},{2,10},{3,11},{4,12},{5,13},{6,14},{7,15},{8,0},{9,1},... | collective-permute-start | bytes 122888 | tf_op jit(solution)/shard_map/ppermute | solution.py:47
  57.6 1.5 %collective-permute-done.12 = bf16[32,640]{1,0:T(8,128)(2,1)S(1)} collective-permute-done((bf16[32,640]{1,0:T(8,128)(2,1)S(1)}, bf16[32,640]{1,0:T(8,128)(2,1)S(1)}, u32[]{:S(2)}, u32[]{:S(2)}) %collective-permute-start.12) | collective-permute-done | bytes 40992 | tf_op jit(solution)/shard_map/ppermute | solution.py:47
  59.1 1.3 collective-permute-done.11
  60.5 1.7 %collective-permute-start.17 = (bf16[1,272,1024]{2,1,0:T(8,128)(2,1)}, bf16[1,272,1024]{2,1,0:T(8,128)(2,1)S(1)}, u32[]{:S(2)}, u32[]{:S(2)}) collective-permute-start(bf16[1,272,1024]{2,1,0:T(8,128)(2,1)} %collective-permute-done.5.refs_3_), channel_id=1, source_target_pairs={{0,8},{1,9},{2,10},{3,11},{4,12},{5,13},{6,14},{7,15},{8,0},{9,1},... | collective-permute-start | bytes 1671176 | tf_op jit(solution)/shard_map/ppermute | solution.py:47
  62.2 4.3 %collective-permute-done.13.refs_4_ = bf16[2,272,1024]{2,1,0:T(8,128)(2,1)S(1)} collective-permute-done((bf16[2,272,1024]{2,1,0:T(8,128)(2,1)S(1)}, bf16[2,272,1024]{2,1,0:T(8,128)(2,1)S(1)}, u32[]{:S(2)}, u32[]{:S(2)}) %collective-permute-start.13) | collective-permute-done | bytes 1114144 | tf_op jit(solution)/shard_map/ppermute | solution.py:47
  66.5 1.0 copy-done.5
  67.5 1.4 %collective-permute-start.16 = (bf16[128,640]{1,0:T(8,128)(2,1)S(1)}, bf16[128,640]{1,0:T(8,128)(2,1)S(1)}, u32[]{:S(2)}, u32[]{:S(2)}) collective-permute-start(bf16[128,640]{1,0:T(8,128)(2,1)S(1)} %pad_maximum_fusion.2), channel_id=1, source_target_pairs={{0,6},{1,7},{2,4},{3,5},{4,2},{5,3},{6,0},{7,1},{8,14},{9,15},{10,... | collective-permute-start | bytes 491528 | tf_op jit(solution)/shard_map/ppermute | solution.py:47
  68.9 1.0 collective-permute-start.15
  69.9 1.1 collective-permute-start.14
  71.0 2.8 %collective-permute-done.16 = bf16[128,640]{1,0:T(8,128)(2,1)S(1)} collective-permute-done((bf16[128,640]{1,0:T(8,128)(2,1)S(1)}, bf16[128,640]{1,0:T(8,128)(2,1)S(1)}, u32[]{:S(2)}, u32[]{:S(2)}) %collective-permute-start.16) | collective-permute-done | bytes 163872 | tf_op jit(solution)/shard_map/ppermute | solution.py:47
  73.8 1.2 collective-permute-done.15
  75.0 0.5 collective-permute-done.14
  75.5 0.1 pad_maximum_fusion.1
  75.6 0.8 copy-done.7
  76.4 0.3 cut.1
  76.7 0.8 copy-done.8
  77.4 1.5 %collective-permute-start.19 = (bf16[1,272,1024]{2,1,0:T(8,128)(2,1)S(1)}, bf16[1,272,1024]{2,1,0:T(8,128)(2,1)S(1)}, u32[]{:S(2)}, u32[]{:S(2)}) collective-permute-start(bf16[1,272,1024]{2,1,0:T(8,128)(2,1)S(1)} %copy-done.8), channel_id=1, source_target_pairs={{0,4},{1,5},{2,6},{3,7},{4,0},{5,1},{6,2},{7,3},{8,12},{9,13},{10,... | collective-permute-start | bytes 1671176 | tf_op jit(solution)/shard_map/ppermute | solution.py:47
  78.9 2.8 %collective-permute-start.20 = (bf16[256,512]{1,0:T(8,128)(2,1)S(1)}, bf16[256,512]{1,0:T(8,128)(2,1)S(1)}, u32[]{:S(2)}, u32[]{:S(2)}) collective-permute-start(bf16[256,512]{1,0:T(8,128)(2,1)S(1)} %get-tuple-element.91), channel_id=1, source_target_pairs={{0,8},{1,9},{2,10},{3,11},{4,12},{5,13},{6,14},{7,15},{8,0},{9,1},... | collective-permute-start | bytes 786440 | tf_op jit(solution)/shard_map/ppermute | solution.py:47
  81.7 2.2 %collective-permute-start.21 = (bf16[256,512]{1,0:T(8,128)(2,1)S(1)}, bf16[256,512]{1,0:T(8,128)(2,1)S(1)}, u32[]{:S(2)}, u32[]{:S(2)}) collective-permute-start(bf16[256,512]{1,0:T(8,128)(2,1)S(1)} %get-tuple-element.92), channel_id=1, source_target_pairs={{0,16},{1,17},{2,18},{3,19},{4,20},{5,21},{6,22},{7,23},{8,24},{9,... | collective-permute-start | bytes 786440 | tf_op jit(solution)/shard_map/ppermute | solution.py:47
  83.9 0.2 collective-permute-start.22
  84.1 0.9 collective-permute-start.23
  85.0 10.8 %whiten.1 = (bf16[1024,1024]{1,0:T(8,128)(2,1)S(1)}, f32[1,1024]{1,0:T(1,128)S(1)}) custom-call(s32[1]{0:T(128)} %bitcast.1.place_ref, bf16[16,32,640]{2,1,0:T(8,128)(2,1)S(1)} %bitcast.11, bf16[16,32,640]{2,1,0:T(8,128)(2,1)} %collective-permute-done.18.far_ref, bf16[64,640]{1,0:T(8,128)(2,1)S(1)} %copy-done.10, ...), custom_call_target="tpu_custom_call" | custom-call | flops 10737418240 | bytes 2097152 | tf_op jit(solution)/shard_map/whiten/pallas_call | solution.py:393
  95.8 1.8 %collective-permute-start.24 = (bf16[256,512]{1,0:T(8,128)(2,1)S(1)}, bf16[256,512]{1,0:T(8,128)(2,1)S(1)}, u32[]{:S(2)}, u32[]{:S(2)}) collective-permute-start(bf16[256,512]{1,0:T(8,128)(2,1)S(1)} %get-tuple-element.95), channel_id=1, source_target_pairs={{0,12},{1,13},{2,14},{3,15},{4,8},{5,9},{6,10},{7,11},{8,4},{9,5},... | collective-permute-start | bytes 786440 | tf_op jit(solution)/shard_map/ppermute | solution.py:47
  97.6 3.4 %collective-permute-start.25 = (bf16[256,512]{1,0:T(8,128)(2,1)S(1)}, bf16[256,512]{1,0:T(8,128)(2,1)S(1)}, u32[]{:S(2)}, u32[]{:S(2)}) collective-permute-start(bf16[256,512]{1,0:T(8,128)(2,1)S(1)} %get-tuple-element.96), channel_id=1, source_target_pairs={{0,20},{1,21},{2,22},{3,23},{4,16},{5,17},{6,18},{7,19},{8,28},{9,... | collective-permute-start | bytes 786440 | tf_op jit(solution)/shard_map/ppermute | solution.py:47
  101.0 2.1 %collective-permute-done.21.refs_2_ = bf16[256,512]{1,0:T(8,128)(2,1)S(1)} collective-permute-done((bf16[256,512]{1,0:T(8,128)(2,1)S(1)}, bf16[256,512]{1,0:T(8,128)(2,1)S(1)}, u32[]{:S(2)}, u32[]{:S(2)}) %collective-permute-start.21) | collective-permute-done | bytes 262176 | tf_op jit(solution)/shard_map/ppermute | solution.py:47
  103.1 1.9 %collective-permute-start.26 = (bf16[256,512]{1,0:T(8,128)(2,1)S(1)}, bf16[256,512]{1,0:T(8,128)(2,1)S(1)}, u32[]{:S(2)}, u32[]{:S(2)}) collective-permute-start(bf16[256,512]{1,0:T(8,128)(2,1)S(1)} %get-tuple-element.97), channel_id=1, source_target_pairs={{0,28},{1,29},{2,30},{3,31},{4,24},{5,25},{6,26},{7,27},{8,20},{9,... | collective-permute-start | bytes 786440 | tf_op jit(solution)/shard_map/ppermute | solution.py:47
  105.0 20.5 %contrast.1 = (f32[1,256]{1,0:T(1,128)}, bf16[8,256,1024]{2,1,0:T(8,128)(2,1)S(1)}) custom-call(s32[1]{0:T(128)} %bitcast.group_ref, f32[1,1024]{1,0:T(1,128)S(1)} %get-tuple-element.83.mean_ref, bf16[1024,1024]{1,0:T(8,128)(2,1)S(1)} %get-tuple-element.84.whitener_ref.refs_3_, bf16[1,272,1024]{2,1,0:T(8,128)(2,1)} %bitcast.6.refs_0_, ...), custom_call_target="tpu_custom_call" | custom-call | flops 12884901888 | bytes 8388608 | tf_op jit(solution)/shard_map/contrast/pallas_call | solution.py:485
  125.5 0.4 collective-permute-done.25.refs_6_
  125.9 1.3 weight_pieces.3
  127.2 0.1 collective-permute-start.28
  127.3 1.3 weight_pieces.2
  128.6 0.6 collective-permute-start.27
  129.1 0.1 join.1
  129.2 1.5 %collective-permute-start.29 = (bf16[128,1024]{1,0:T(8,128)(2,1)S(1)}, bf16[128,1024]{1,0:T(8,128)(2,1)S(1)}, u32[]{:S(2)}, u32[]{:S(2)}) collective-permute-start(bf16[128,1024]{1,0:T(8,128)(2,1)S(1)} %join.1), channel_id=1, source_target_pairs={{0,2},{1,3},{2,0},{3,1},{4,6},{5,7},{6,4},{7,5},{8,10},{9,11},{10,... | collective-permute-start | bytes 786440 | tf_op jit(solution)/shard_map/ppermute | solution.py:47
  130.7 6.8 %collective-permute-done.29.refs_2_ = bf16[128,1024]{1,0:T(8,128)(2,1)S(1)} collective-permute-done((bf16[128,1024]{1,0:T(8,128)(2,1)S(1)}, bf16[128,1024]{1,0:T(8,128)(2,1)S(1)}, u32[]{:S(2)}, u32[]{:S(2)}) %collective-permute-start.29) | collective-permute-done | bytes 262176 | tf_op jit(solution)/shard_map/ppermute | solution.py:47
  137.5 1.5 %finish.1 = f32[128,1024]{1,0:T(8,128)} custom-call(f32[128,1024]{1,0:T(8,128)S(1)} %get-tuple-element.98.refs_0_, bf16[128,1024]{1,0:T(8,128)(2,1)S(1)} %collective-permute-done.27.refs_1_, bf16[128,1024]{1,0:T(8,128)(2,1)S(1)} %collective-permute-done.29.refs_2_, bf16[1024,1024]{1,0:T(8,128)(2,1)S(1)} %get-tuple-element.84.whitener_ref.refs_3_), custom_call_target="tpu_custom_call" | custom-call | tf_op jit(solution)/shard_map/finish/pallas_call | solution.py:581
  (32 shorter events, 0.1 us)
Async XLA Ops:
  0.6 0.7 copy-start.3
  1.3 0.7 copy-start.4
  8.8 16.6 %collective-permute-start = (bf16[528,640]{1,0:T(8,128)(2,1)S(1)}, bf16[528,640]{1,0:T(8,128)(2,1)S(1)}, u32[]{:S(2)}, u32[]{:S(2)}) collective-permute-start(bf16[528,640]{1,0:T(8,128)(2,1)S(1)} %get-tuple-element.53.sent_ref), channel_id=1, source_target_pairs={{0,1},{1,0},{2,3},{3,2},{4,5},{5,4},{6,7},{7,6},{8,9},{9,8},{10,11... | collective-permute-start | bytes 2027528 | tf_op jit(solution)/shard_map/ppermute | solution.py:47
  9.3 16.1 %collective-permute-start.1 = (bf16[1,272,1024]{2,1,0:T(8,128)(2,1)}, bf16[1,272,1024]{2,1,0:T(8,128)(2,1)}, u32[]{:S(2)}, u32[]{:S(2)}) collective-permute-start(bf16[1,272,1024]{2,1,0:T(8,128)(2,1)} %bitcast.6.refs_0_), channel_id=1, source_target_pairs={{0,4},{1,5},{2,6},{3,7},{4,0},{5,1},{6,2},{7,3},{8,12},{9,13},{10,... | collective-permute-start | bytes 1671176 | tf_op jit(solution)/shard_map/ppermute | solution.py:47
  11.9 29.1 %collective-permute-start.6 = (bf16[1,272,1024]{2,1,0:T(8,128)(2,1)}, bf16[1,272,1024]{2,1,0:T(8,128)(2,1)S(1)}, u32[]{:S(2)}, u32[]{:S(2)}) collective-permute-start(bf16[1,272,1024]{2,1,0:T(8,128)(2,1)} %bitcast.6.refs_0_), channel_id=1, source_target_pairs={{0,8},{1,9},{2,10},{3,11},{4,12},{5,13},{6,14},{7,15},{8,0},{9,1},... | collective-permute-start | bytes 1671176 | tf_op jit(solution)/shard_map/ppermute | solution.py:47
  13.5 27.6 %collective-permute-start.5 = (bf16[1,272,1024]{2,1,0:T(8,128)(2,1)}, bf16[1,272,1024]{2,1,0:T(8,128)(2,1)}, u32[]{:S(2)}, u32[]{:S(2)}) collective-permute-start(bf16[1,272,1024]{2,1,0:T(8,128)(2,1)} %bitcast.6.refs_0_), channel_id=1, source_target_pairs={{0,16},{1,17},{2,18},{3,19},{4,20},{5,21},{6,22},{7,23},{8,24},{9,... | collective-permute-start | bytes 1671176 | tf_op jit(solution)/shard_map/ppermute | solution.py:47
  26.3 0.7 copy-start.1
  27.0 7.7 %collective-permute-start.3 = (bf16[144,640]{1,0:T(8,128)(2,1)}, bf16[144,640]{1,0:T(8,128)(2,1)S(1)}, u32[]{:S(2)}, u32[]{:S(2)}) collective-permute-start(bf16[144,640]{1,0:T(8,128)(2,1)} %get-tuple-element.58), channel_id=1, source_target_pairs={{0,4},{1,5},{2,6},{3,7},{4,0},{5,1},{6,2},{7,3},{8,12},{9,13},{10,... | collective-permute-start | bytes 552968 | tf_op jit(solution)/shard_map/ppermute | solution.py:47
  28.8 9.9 %collective-permute-start.4 = (bf16[144,640]{1,0:T(8,128)(2,1)}, bf16[144,640]{1,0:T(8,128)(2,1)S(1)}, u32[]{:S(2)}, u32[]{:S(2)}) collective-permute-start(bf16[144,640]{1,0:T(8,128)(2,1)} %get-tuple-element.59), channel_id=1, source_target_pairs={{0,6},{1,7},{2,4},{3,5},{4,2},{5,3},{6,0},{7,1},{8,14},{9,15},{10,... | collective-permute-start | bytes 552968 | tf_op jit(solution)/shard_map/ppermute | solution.py:47
  30.3 9.6 %collective-permute-start.2 = (bf16[144,640]{1,0:T(8,128)(2,1)S(1)}, bf16[144,640]{1,0:T(8,128)(2,1)S(1)}, u32[]{:S(2)}, u32[]{:S(2)}) collective-permute-start(bf16[144,640]{1,0:T(8,128)(2,1)S(1)} %get-tuple-element.57.sent_ref), channel_id=1, source_target_pairs={{0,2},{1,3},{2,0},{3,1},{4,6},{5,7},{6,4},{7,5},{8,10},{9,11},{10,... | collective-permute-start | bytes 552968 | tf_op jit(solution)/shard_map/ppermute | solution.py:47
  39.9 1.0 copy-start.2
  40.9 19.5 %copy-start.9 = (bf16[64,640]{1,0:T(8,128)(2,1)}, bf16[64,640]{1,0:T(8,128)(2,1)S(1)}, u32[]{:S(2)}) copy-start(bf16[64,640]{1,0:T(8,128)(2,1)S(1)} %get-tuple-element.64.refs_0_) | copy-start | bytes 245764
  41.1 35.3 %copy-start = (bf16[256,4096]{1,0:T(8,128)(2,1)S(1)}, bf16[256,4096]{1,0:T(8,128)(2,1)}, u32[]{:S(2)}) copy-start(bf16[256,4096]{1,0:T(8,128)(2,1)} %features_hbm.3) | copy-start | bytes 6291460
  42.4 24.1 %collective-permute-start.13 = (bf16[2,272,1024]{2,1,0:T(8,128)(2,1)S(1)}, bf16[2,272,1024]{2,1,0:T(8,128)(2,1)S(1)}, u32[]{:S(2)}, u32[]{:S(2)}) collective-permute-start(bf16[2,272,1024]{2,1,0:T(8,128)(2,1)S(1)} %pad_maximum_fusion), channel_id=1, source_target_pairs={{0,4},{1,5},{2,6},{3,7},{4,0},{5,1},{6,2},{7,3},{8,12},{9,13},{10,... | collective-permute-start | bytes 3342344 | tf_op jit(solution)/shard_map/ppermute | solution.py:47
  43.9 6.2 %collective-permute-start.8 = (bf16[64,640]{1,0:T(8,128)(2,1)S(1)}, bf16[64,640]{1,0:T(8,128)(2,1)S(1)}, u32[]{:S(2)}, u32[]{:S(2)}) collective-permute-start(bf16[64,640]{1,0:T(8,128)(2,1)S(1)} %get-tuple-element.65), channel_id=1, source_target_pairs={{0,16},{1,17},{2,18},{3,19},{4,20},{5,21},{6,22},{7,23},{8,24},{9,... | collective-permute-start | bytes 245768 | tf_op jit(solution)/shard_map/ppermute | solution.py:47
  46.4 6.4 %collective-permute-start.9 = (bf16[64,640]{1,0:T(8,128)(2,1)S(1)}, bf16[64,640]{1,0:T(8,128)(2,1)S(1)}, u32[]{:S(2)}, u32[]{:S(2)}) collective-permute-start(bf16[64,640]{1,0:T(8,128)(2,1)S(1)} %get-tuple-element.66), channel_id=1, source_target_pairs={{0,24},{1,25},{2,26},{3,27},{4,28},{5,29},{6,30},{7,31},{8,16},{9,... | collective-permute-start | bytes 245768 | tf_op jit(solution)/shard_map/ppermute | solution.py:47
  47.8 5.3 %collective-permute-start.7 = (bf16[64,640]{1,0:T(8,128)(2,1)S(1)}, bf16[64,640]{1,0:T(8,128)(2,1)S(1)}, u32[]{:S(2)}, u32[]{:S(2)}) collective-permute-start(bf16[64,640]{1,0:T(8,128)(2,1)S(1)} %get-tuple-element.64.refs_0_), channel_id=1, source_target_pairs={{0,8},{1,9},{2,10},{3,11},{4,12},{5,13},{6,14},{7,15},{8,0},{9,1},... | collective-permute-start | bytes 245768 | tf_op jit(solution)/shard_map/ppermute | solution.py:47
  53.1 6.0 %collective-permute-start.12 = (bf16[32,640]{1,0:T(8,128)(2,1)S(1)}, bf16[32,640]{1,0:T(8,128)(2,1)S(1)}, u32[]{:S(2)}, u32[]{:S(2)}) collective-permute-start(bf16[32,640]{1,0:T(8,128)(2,1)S(1)} %add_convert_fusion), channel_id=1, source_target_pairs={{0,24},{1,25},{2,26},{3,27},{4,28},{5,29},{6,30},{7,31},{8,16},{9,... | collective-permute-start | bytes 122888 | tf_op jit(solution)/shard_map/ppermute | solution.py:47
  55.4 5.0 %collective-permute-start.11 = (bf16[32,640]{1,0:T(8,128)(2,1)S(1)}, bf16[32,640]{1,0:T(8,128)(2,1)S(1)}, u32[]{:S(2)}, u32[]{:S(2)}) collective-permute-start(bf16[32,640]{1,0:T(8,128)(2,1)S(1)} %add_convert_fusion), channel_id=1, source_target_pairs={{0,16},{1,17},{2,18},{3,19},{4,20},{5,21},{6,22},{7,23},{8,24},{9,... | collective-permute-start | bytes 122888 | tf_op jit(solution)/shard_map/ppermute | solution.py:47
  55.4 5.0 %collective-permute-start.10 = (bf16[32,640]{1,0:T(8,128)(2,1)S(1)}, bf16[32,640]{1,0:T(8,128)(2,1)S(1)}, u32[]{:S(2)}, u32[]{:S(2)}) collective-permute-start(bf16[32,640]{1,0:T(8,128)(2,1)S(1)} %add_convert_fusion), channel_id=1, source_target_pairs={{0,8},{1,9},{2,10},{3,11},{4,12},{5,13},{6,14},{7,15},{8,0},{9,1},... | collective-permute-start | bytes 122888 | tf_op jit(solution)/shard_map/ppermute | solution.py:47
  60.5 15.1 %collective-permute-start.17 = (bf16[1,272,1024]{2,1,0:T(8,128)(2,1)}, bf16[1,272,1024]{2,1,0:T(8,128)(2,1)S(1)}, u32[]{:S(2)}, u32[]{:S(2)}) collective-permute-start(bf16[1,272,1024]{2,1,0:T(8,128)(2,1)} %collective-permute-done.5.refs_3_), channel_id=1, source_target_pairs={{0,8},{1,9},{2,10},{3,11},{4,12},{5,13},{6,14},{7,15},{8,0},{9,1},... | collective-permute-start | bytes 1671176 | tf_op jit(solution)/shard_map/ppermute | solution.py:47
  66.5 1.0 copy-start.5
  67.5 6.2 %collective-permute-start.16 = (bf16[128,640]{1,0:T(8,128)(2,1)S(1)}, bf16[128,640]{1,0:T(8,128)(2,1)S(1)}, u32[]{:S(2)}, u32[]{:S(2)}) collective-permute-start(bf16[128,640]{1,0:T(8,128)(2,1)S(1)} %pad_maximum_fusion.2), channel_id=1, source_target_pairs={{0,6},{1,7},{2,4},{3,5},{4,2},{5,3},{6,0},{7,1},{8,14},{9,15},{10,... | collective-permute-start | bytes 491528 | tf_op jit(solution)/shard_map/ppermute | solution.py:47
  68.9 6.0 %collective-permute-start.15 = (bf16[128,640]{1,0:T(8,128)(2,1)S(1)}, bf16[128,640]{1,0:T(8,128)(2,1)S(1)}, u32[]{:S(2)}, u32[]{:S(2)}) collective-permute-start(bf16[128,640]{1,0:T(8,128)(2,1)S(1)} %pad_maximum_fusion.2), channel_id=1, source_target_pairs={{0,4},{1,5},{2,6},{3,7},{4,0},{5,1},{6,2},{7,3},{8,12},{9,13},{10,... | collective-permute-start | bytes 491528 | tf_op jit(solution)/shard_map/ppermute | solution.py:47
  69.9 5.6 %collective-permute-start.14 = (bf16[128,640]{1,0:T(8,128)(2,1)S(1)}, bf16[128,640]{1,0:T(8,128)(2,1)S(1)}, u32[]{:S(2)}, u32[]{:S(2)}) collective-permute-start(bf16[128,640]{1,0:T(8,128)(2,1)S(1)} %pad_maximum_fusion.2), channel_id=1, source_target_pairs={{0,2},{1,3},{2,0},{3,1},{4,6},{5,7},{6,4},{7,5},{8,10},{9,11},{10,... | collective-permute-start | bytes 491528 | tf_op jit(solution)/shard_map/ppermute | solution.py:47
  75.6 0.8 copy-start.7
  76.4 2.6 %collective-permute-start.18 = (bf16[16,32,640]{2,1,0:T(8,128)(2,1)S(1)}, bf16[16,32,640]{2,1,0:T(8,128)(2,1)}, u32[]{:S(2)}, u32[]{:S(2)}) collective-permute-start(bf16[16,32,640]{2,1,0:T(8,128)(2,1)S(1)} %bitcast.10), channel_id=1, source_target_pairs={{0,1},{1,0},{2,3},{3,2},{4,5},{5,4},{6,7},{7,6},{8,9},{9,8},{10,11... | collective-permute-start | bytes 1966088 | tf_op jit(solution)/shard_map/ppermute | solution.py:47
  76.4 1.1 copy-start.8
  76.4 8.6 %copy-start.10 = (bf16[64,640]{1,0:T(8,128)(2,1)S(1)}, bf16[64,640]{1,0:T(8,128)(2,1)}, u32[]{:S(2)}) copy-start(bf16[64,640]{1,0:T(8,128)(2,1)} %copy-done.9) | copy-start | bytes 245764
  77.4 18.4 %collective-permute-start.19 = (bf16[1,272,1024]{2,1,0:T(8,128)(2,1)S(1)}, bf16[1,272,1024]{2,1,0:T(8,128)(2,1)S(1)}, u32[]{:S(2)}, u32[]{:S(2)}) collective-permute-start(bf16[1,272,1024]{2,1,0:T(8,128)(2,1)S(1)} %copy-done.8), channel_id=1, source_target_pairs={{0,4},{1,5},{2,6},{3,7},{4,0},{5,1},{6,2},{7,3},{8,12},{9,13},{10,... | collective-permute-start | bytes 1671176 | tf_op jit(solution)/shard_map/ppermute | solution.py:47
  78.9 18.7 %collective-permute-start.20 = (bf16[256,512]{1,0:T(8,128)(2,1)S(1)}, bf16[256,512]{1,0:T(8,128)(2,1)S(1)}, u32[]{:S(2)}, u32[]{:S(2)}) collective-permute-start(bf16[256,512]{1,0:T(8,128)(2,1)S(1)} %get-tuple-element.91), channel_id=1, source_target_pairs={{0,8},{1,9},{2,10},{3,11},{4,12},{5,13},{6,14},{7,15},{8,0},{9,1},... | collective-permute-start | bytes 786440 | tf_op jit(solution)/shard_map/ppermute | solution.py:47
  81.7 21.4 %collective-permute-start.21 = (bf16[256,512]{1,0:T(8,128)(2,1)S(1)}, bf16[256,512]{1,0:T(8,128)(2,1)S(1)}, u32[]{:S(2)}, u32[]{:S(2)}) collective-permute-start(bf16[256,512]{1,0:T(8,128)(2,1)S(1)} %get-tuple-element.92), channel_id=1, source_target_pairs={{0,16},{1,17},{2,18},{3,19},{4,20},{5,21},{6,22},{7,23},{8,24},{9,... | collective-permute-start | bytes 786440 | tf_op jit(solution)/shard_map/ppermute | solution.py:47
  83.9 41.5 %collective-permute-start.22 = (bf16[256,512]{1,0:T(8,128)(2,1)S(1)}, bf16[256,512]{1,0:T(8,128)(2,1)S(1)}, u32[]{:S(2)}, u32[]{:S(2)}) collective-permute-start(bf16[256,512]{1,0:T(8,128)(2,1)S(1)} %get-tuple-element.93), channel_id=1, source_target_pairs={{0,24},{1,25},{2,26},{3,27},{4,28},{5,29},{6,30},{7,31},{8,16},{9,... | collective-permute-start | bytes 786440 | tf_op jit(solution)/shard_map/ppermute | solution.py:47
  84.1 41.4 %collective-permute-start.23 = (bf16[256,512]{1,0:T(8,128)(2,1)S(1)}, bf16[256,512]{1,0:T(8,128)(2,1)S(1)}, u32[]{:S(2)}, u32[]{:S(2)}) collective-permute-start(bf16[256,512]{1,0:T(8,128)(2,1)S(1)} %get-tuple-element.94), channel_id=1, source_target_pairs={{0,4},{1,5},{2,6},{3,7},{4,0},{5,1},{6,2},{7,3},{8,12},{9,13},{10,... | collective-permute-start | bytes 786440 | tf_op jit(solution)/shard_map/ppermute | solution.py:47
  85.0 20.0 %copy-start.6 = (bf16[2,272,1024]{2,1,0:T(8,128)(2,1)S(1)}, bf16[2,272,1024]{2,1,0:T(8,128)(2,1)}, u32[]{:S(2)}) copy-start(bf16[2,272,1024]{2,1,0:T(8,128)(2,1)} %copy-done.5) | copy-start | bytes 3342340
  95.8 29.7 %collective-permute-start.24 = (bf16[256,512]{1,0:T(8,128)(2,1)S(1)}, bf16[256,512]{1,0:T(8,128)(2,1)S(1)}, u32[]{:S(2)}, u32[]{:S(2)}) collective-permute-start(bf16[256,512]{1,0:T(8,128)(2,1)S(1)} %get-tuple-element.95), channel_id=1, source_target_pairs={{0,12},{1,13},{2,14},{3,15},{4,8},{5,9},{6,10},{7,11},{8,4},{9,5},... | collective-permute-start | bytes 786440 | tf_op jit(solution)/shard_map/ppermute | solution.py:47
  97.6 28.2 %collective-permute-start.25 = (bf16[256,512]{1,0:T(8,128)(2,1)S(1)}, bf16[256,512]{1,0:T(8,128)(2,1)S(1)}, u32[]{:S(2)}, u32[]{:S(2)}) collective-permute-start(bf16[256,512]{1,0:T(8,128)(2,1)S(1)} %get-tuple-element.96), channel_id=1, source_target_pairs={{0,20},{1,21},{2,22},{3,23},{4,16},{5,17},{6,18},{7,19},{8,28},{9,... | collective-permute-start | bytes 786440 | tf_op jit(solution)/shard_map/ppermute | solution.py:47
  103.1 22.8 %collective-permute-start.26 = (bf16[256,512]{1,0:T(8,128)(2,1)S(1)}, bf16[256,512]{1,0:T(8,128)(2,1)S(1)}, u32[]{:S(2)}, u32[]{:S(2)}) collective-permute-start(bf16[256,512]{1,0:T(8,128)(2,1)S(1)} %get-tuple-element.97), channel_id=1, source_target_pairs={{0,28},{1,29},{2,30},{3,31},{4,24},{5,25},{6,26},{7,27},{8,20},{9,... | collective-permute-start | bytes 786440 | tf_op jit(solution)/shard_map/ppermute | solution.py:47
  127.2 1.9 %collective-permute-start.28 = (bf16[128,1024]{1,0:T(8,128)(2,1)S(1)}, bf16[128,1024]{1,0:T(8,128)(2,1)S(1)}, u32[]{:S(2)}, u32[]{:S(2)}) collective-permute-start(bf16[128,1024]{1,0:T(8,128)(2,1)S(1)} %get-tuple-element.101), channel_id=1, source_target_pairs={{0,1},{1,0},{2,3},{3,2},{4,5},{5,4},{6,7},{7,6},{8,9},{9,8},{10,11... | collective-permute-start | bytes 786440 | tf_op jit(solution)/shard_map/ppermute | solution.py:47
  128.6 2.2 %collective-permute-start.27 = (bf16[128,1024]{1,0:T(8,128)(2,1)S(1)}, bf16[128,1024]{1,0:T(8,128)(2,1)S(1)}, u32[]{:S(2)}, u32[]{:S(2)}) collective-permute-start(bf16[128,1024]{1,0:T(8,128)(2,1)S(1)} %get-tuple-element.99), channel_id=1, source_target_pairs={{0,1},{1,0},{2,3},{3,2},{4,5},{5,4},{6,7},{7,6},{8,9},{9,8},{10,11... | collective-permute-start | bytes 786440 | tf_op jit(solution)/shard_map/ppermute | solution.py:47
  129.2 8.3 %collective-permute-start.29 = (bf16[128,1024]{1,0:T(8,128)(2,1)S(1)}, bf16[128,1024]{1,0:T(8,128)(2,1)S(1)}, u32[]{:S(2)}, u32[]{:S(2)}) collective-permute-start(bf16[128,1024]{1,0:T(8,128)(2,1)S(1)} %join.1), channel_id=1, source_target_pairs={{0,2},{1,3},{2,0},{3,1},{4,6},{5,7},{6,4},{7,5},{8,10},{9,11},{10,... | collective-permute-start | bytes 786440 | tf_op jit(solution)/shard_map/ppermute | solution.py:47

commit v10 on v9

--- a/solution.py
+++ b/solution.py
@@ -619,8 +619,6 @@
         gathered = lax.all_gather(block, "sp", tiled=True)
 
     arrived = [xor_permute(send, 1)]
-    if direct:
-        arrived[0], block_x = lax.optimization_barrier((arrived[0], block_x))
     sent = send
     seen = 1
     stages = []
@@ -632,10 +630,10 @@
         keep, sends, seen = stage(own, keep, sent, arrived, seen, count, embed)
         if direct and stages:
             group_scalar = group.reshape(1)
-            *sends, block_far, block_near, group_scalar = lax.optimization_barrier(
-                (*sends, block_far, block_near, group_scalar)
+            *sends, block_x, block_near, block_far, group_scalar = lax.optimization_barrier(
+                (*sends, block_x, block_near, block_far, group_scalar)
             )
-            slices = cut(group_scalar, features, groups)
+            slices = list(cut(group_scalar, features, groups))
             pair_x = xor_permute(jnp.concatenate([block_far, block_near]), by_x)
         arrived = [xor_permute(piece, (r + 1) << low) for r, piece in enumerate(sends)]
         sent = sends[0]
@@ -657,8 +655,9 @@
     part = part.astype(BF16)
     for number, (low, count) in enumerate(reversed(stages)):
         if direct and number == 1:
-            part, block_far = lax.optimization_barrier((part, block_far))
+            part, block_far, slices[4] = lax.optimization_barrier((part, block_far, slices[4]))
             block_far_near = xor_permute(block_far, by_near)
+            slices[4] = xor_permute(slices[4], by_far)
             part, pair_x = lax.optimization_barrier((part, pair_x))
         part = jnp.concatenate(
             [part] + [xor_permute(part, r << low) for r in range(1, count)], axis=0
@@ -676,9 +675,12 @@
         ]
     other = xor_permute(part, 1)
     if direct:
-        other, *slices = lax.optimization_barrier((other, *slices))
-        slice_order = [0, 2, 4, 6, 1, 3, 5, 7]
-        slices = [xor_permute(slices[k], k * shares) if k else slices[k] for k in slice_order]
+        slice_order = [0, 4, 6, 2, 1, 3, 5, 7]
+        later = slice_order[2:]
+        other, *held = lax.optimization_barrier((other, *(slices[k] for k in later)))
+        for k, piece in zip(later, held):
+            slices[k] = xor_permute(piece, k * shares)
+        slices = [slices[k] for k in slice_order]
 
     whitener, mean = whiten(place.reshape(1), part, other, sums, seen, rows, embed)
     loss, grad = contrast(group.reshape(1), blocks, order, mean, whitener)

time: 141 us -> 142 us (level); the launches traced: 139 us -> 142 us
  waiting for transfers between devices: 44.8 us -> 50.6 us
  starting transfers between devices: 42.7 us -> 38.1 us
    ppermute x30, waiting for transfers between devices: 44.8 us -> 50.6 us  [xor_permute(): return lax.ppermute(piece, AXES, [(i, i ^ mask) for i in range(devices)])]
    ppermute x30, starting transfers between devices: 42.7 us -> 38.1 us  [xor_permute(): return lax.ppermute(piece, AXES, [(i, i ^ mask) for i in range(devices)])]
    unnamed x22 -> x26, local copies, waits for them, and re-layouts: 5.65 us -> 6.25 us
  transfers between devices with their start and end apart: 30 -> 30, of which waited for: 17 -> 13; matrix products, arithmetic and copies ran while one was open for 0% -> 0% of each run, Pallas kernels for 24% -> 24%
where the time goes in v10:
time: 142 us
  waiting for transfers between devices  50.6 us (36%)
  Pallas kernels  44.3 us (31%)
  starting transfers between devices  38.1 us (27%)
  local copies, waits for them, and re-layouts  6.25 us (4%)
    ppermute x30, waiting for transfers between devices, xor_permute(): return lax.ppermute(piece, AXES, [(i, i ^ mask) for i in range(devices)])  50.6 us
    ppermute x30, starting transfers between devices, xor_permute(): return lax.ppermute(piece, AXES, [(i, i ^ mask) for i in range(devices)])  38.1 us
    pallas_call x1, Pallas kernels, contrast(): pl.pallas_call(functools.partial(contrast_kernel, order), in_specs=[smem(...  20.4 us
    pallas_call x1, Pallas kernels, whiten(): pl.pallas_call(make_whiten_kernel(rows, count), in_specs=[smem()] + [vmem...  10.7 us
    pallas_call x1, Pallas kernels, project(): pl.pallas_call(project_kernel, in_specs=[smem(), smem(), hbm, hbm, hbm],...  6.81 us
    unnamed x26, local copies, waits for them, and re-layouts  6.25 us
  transfers between devices with their start and end apart: 30, of which 13 were waited for; matrix products, arithmetic and copies ran while one was open for 0% of the time, Pallas kernels for 24%

profile of v10, /device:TPU:0, one launch (start us, length us, event | category | flops | bytes accessed | tf_op | source)
XLA Modules:
  0.0 141.5 jit_solution(7272769875094528719)
XLA Ops:
  0.6 0.7 copy-done.1
  1.3 0.7 copy-done.2
  2.0 6.8 %project.1 = (bf16[272,1024]{1,0:T(8,128)(2,1)}, bf16[528,640]{1,0:T(8,128)(2,1)S(1)}, f32[512,640]{1,0:T(8,128)S(1)}) custom-call(s32[1]{0:T(128)} %bitcast.4.me_ref, s32[1,4]{1,0:T(1,128)S(1)} %copy-done.2, bf16[256,4096]{1,0:T(8,128)(2,1)} %features_hbm.3, bf16[4096,1024]{1,0:T(8,128)(2,1)} %weight_hbm.1, s32[4,256]{1,0:T(4,128)S(1)} %bitcast.12), custom_call_target="tpu_custom_call" | custom-call | flops 2147483648 | bytes 8388608 | tf_op jit(solution)/shard_map/project/pallas_call | solution.py:186
  8.8 0.5 collective-permute-start
  9.3 3.7 %collective-permute-start.6 = (bf16[1,272,1024]{2,1,0:T(8,128)(2,1)}, bf16[1,272,1024]{2,1,0:T(8,128)(2,1)S(1)}, u32[]{:S(2)}, u32[]{:S(2)}) collective-permute-start(bf16[1,272,1024]{2,1,0:T(8,128)(2,1)} %bitcast.6.refs_0_), channel_id=1, source_target_pairs={{0,16},{1,17},{2,18},{3,19},{4,20},{5,21},{6,22},{7,23},{8,24},{9,... | collective-permute-start | bytes 1671176 | tf_op jit(solution)/shard_map/ppermute | solution.py:47
  13.0 1.6 %collective-permute-start.5 = (bf16[1,272,1024]{2,1,0:T(8,128)(2,1)}, bf16[1,272,1024]{2,1,0:T(8,128)(2,1)}, u32[]{:S(2)}, u32[]{:S(2)}) collective-permute-start(bf16[1,272,1024]{2,1,0:T(8,128)(2,1)} %bitcast.6.refs_0_), channel_id=1, source_target_pairs={{0,8},{1,9},{2,10},{3,11},{4,12},{5,13},{6,14},{7,15},{8,0},{9,1},... | collective-permute-start | bytes 1671176 | tf_op jit(solution)/shard_map/ppermute | solution.py:47
  14.6 1.5 %collective-permute-start.4 = (bf16[1,272,1024]{2,1,0:T(8,128)(2,1)}, bf16[1,272,1024]{2,1,0:T(8,128)(2,1)}, u32[]{:S(2)}, u32[]{:S(2)}) collective-permute-start(bf16[1,272,1024]{2,1,0:T(8,128)(2,1)} %bitcast.6.refs_0_), channel_id=1, source_target_pairs={{0,4},{1,5},{2,6},{3,7},{4,0},{5,1},{6,2},{7,3},{8,12},{9,13},{10,... | collective-permute-start | bytes 1671176 | tf_op jit(solution)/shard_map/ppermute | solution.py:47
  16.0 0.0 collective-permute-done.refs_0_
  16.0 0.9 stage.2
  16.9 0.5 collective-permute-start.2
  17.4 2.4 %collective-permute-start.3 = (bf16[144,640]{1,0:T(8,128)(2,1)}, bf16[144,640]{1,0:T(8,128)(2,1)S(1)}, u32[]{:S(2)}, u32[]{:S(2)}) collective-permute-start(bf16[144,640]{1,0:T(8,128)(2,1)} %get-tuple-element.55), channel_id=1, source_target_pairs={{0,6},{1,7},{2,4},{3,5},{4,2},{5,3},{6,0},{7,1},{8,14},{9,15},{10,... | collective-permute-start | bytes 552968 | tf_op jit(solution)/shard_map/ppermute | solution.py:47
  19.9 14.3 %collective-permute-done.2.refs_1_ = bf16[144,640]{1,0:T(8,128)(2,1)S(1)} collective-permute-done((bf16[144,640]{1,0:T(8,128)(2,1)S(1)}, bf16[144,640]{1,0:T(8,128)(2,1)S(1)}, u32[]{:S(2)}, u32[]{:S(2)}) %collective-permute-start.2) | collective-permute-done | bytes 184352 | tf_op jit(solution)/shard_map/ppermute | solution.py:47
  34.2 1.5 %collective-permute-start.1 = (bf16[144,640]{1,0:T(8,128)(2,1)}, bf16[144,640]{1,0:T(8,128)(2,1)S(1)}, u32[]{:S(2)}, u32[]{:S(2)}) collective-permute-start(bf16[144,640]{1,0:T(8,128)(2,1)} %get-tuple-element.53.sent_ref), channel_id=1, source_target_pairs={{0,2},{1,3},{2,0},{3,1},{4,6},{5,7},{6,4},{7,5},{8,10},{9,11},{10,... | collective-permute-start | bytes 552968 | tf_op jit(solution)/shard_map/ppermute | solution.py:47
  35.7 2.4 %collective-permute-done.3.refs_2_ = bf16[144,640]{1,0:T(8,128)(2,1)S(1)} collective-permute-done((bf16[144,640]{1,0:T(8,128)(2,1)}, bf16[144,640]{1,0:T(8,128)(2,1)S(1)}, u32[]{:S(2)}, u32[]{:S(2)}) %collective-permute-start.3) | collective-permute-done | bytes 184352 | tf_op jit(solution)/shard_map/ppermute | solution.py:47
  38.1 3.8 %collective-permute-done.1.refs_0_ = bf16[144,640]{1,0:T(8,128)(2,1)S(1)} collective-permute-done((bf16[144,640]{1,0:T(8,128)(2,1)}, bf16[144,640]{1,0:T(8,128)(2,1)S(1)}, u32[]{:S(2)}, u32[]{:S(2)}) %collective-permute-start.1) | collective-permute-done | bytes 184352 | tf_op jit(solution)/shard_map/ppermute | solution.py:47
  41.9 1.0 stage.3
  43.0 0.0 copy-start
  43.0 1.3 pad_maximum_fusion
  44.3 1.6 %collective-permute-start.13 = (bf16[2,272,1024]{2,1,0:T(8,128)(2,1)S(1)}, bf16[2,272,1024]{2,1,0:T(8,128)(2,1)S(1)}, u32[]{:S(2)}, u32[]{:S(2)}) collective-permute-start(bf16[2,272,1024]{2,1,0:T(8,128)(2,1)S(1)} %pad_maximum_fusion), channel_id=1, source_target_pairs={{0,4},{1,5},{2,6},{3,7},{4,0},{5,1},{6,2},{7,3},{8,12},{9,13},{10,... | collective-permute-start | bytes 3342344 | tf_op jit(solution)/shard_map/ppermute | solution.py:47
  45.9 0.3 collective-permute-start.8
  46.2 2.5 %collective-permute-start.9 = (bf16[64,640]{1,0:T(8,128)(2,1)S(1)}, bf16[64,640]{1,0:T(8,128)(2,1)S(1)}, u32[]{:S(2)}, u32[]{:S(2)}) collective-permute-start(bf16[64,640]{1,0:T(8,128)(2,1)S(1)} %get-tuple-element.63), channel_id=1, source_target_pairs={{0,24},{1,25},{2,26},{3,27},{4,28},{5,29},{6,30},{7,31},{8,16},{9,... | collective-permute-start | bytes 245768 | tf_op jit(solution)/shard_map/ppermute | solution.py:47
  48.7 0.7 collective-permute-start.7
  49.4 5.1 %collective-permute-done.8.refs_2_ = bf16[64,640]{1,0:T(8,128)(2,1)S(1)} collective-permute-done((bf16[64,640]{1,0:T(8,128)(2,1)S(1)}, bf16[64,640]{1,0:T(8,128)(2,1)S(1)}, u32[]{:S(2)}, u32[]{:S(2)}) %collective-permute-start.8) | collective-permute-done | bytes 81952 | tf_op jit(solution)/shard_map/ppermute | solution.py:47
  54.4 0.7 collective-permute-done.7.refs_1_
  55.2 0.6 collective-permute-start.12
  55.8 2.3 %collective-permute-start.11 = (bf16[32,640]{1,0:T(8,128)(2,1)S(1)}, bf16[32,640]{1,0:T(8,128)(2,1)S(1)}, u32[]{:S(2)}, u32[]{:S(2)}) collective-permute-start(bf16[32,640]{1,0:T(8,128)(2,1)S(1)} %add_convert_fusion), channel_id=1, source_target_pairs={{0,16},{1,17},{2,18},{3,19},{4,20},{5,21},{6,22},{7,23},{8,24},{9,... | collective-permute-start | bytes 122888 | tf_op jit(solution)/shard_map/ppermute | solution.py:47
  58.1 1.5 %collective-permute-start.10 = (bf16[32,640]{1,0:T(8,128)(2,1)S(1)}, bf16[32,640]{1,0:T(8,128)(2,1)S(1)}, u32[]{:S(2)}, u32[]{:S(2)}) collective-permute-start(bf16[32,640]{1,0:T(8,128)(2,1)S(1)} %add_convert_fusion), channel_id=1, source_target_pairs={{0,8},{1,9},{2,10},{3,11},{4,12},{5,13},{6,14},{7,15},{8,0},{9,1},... | collective-permute-start | bytes 122888 | tf_op jit(solution)/shard_map/ppermute | solution.py:47
  59.6 0.3 cut.1
  59.9 0.7 copy-done.3
  60.6 0.7 copy-done.5
  61.3 0.7 copy-done.7
  62.0 0.7 copy-done.9
  62.7 0.7 copy-done.10
  63.4 0.7 copy-done.11
  64.1 0.7 copy-done.12
  64.9 0.6 collective-permute-start.17
  65.4 5.4 %collective-permute-done.13.refs_4_ = bf16[2,272,1024]{2,1,0:T(8,128)(2,1)S(1)} collective-permute-done((bf16[2,272,1024]{2,1,0:T(8,128)(2,1)S(1)}, bf16[2,272,1024]{2,1,0:T(8,128)(2,1)S(1)}, u32[]{:S(2)}, u32[]{:S(2)}) %collective-permute-start.13) | collective-permute-done | bytes 1114144 | tf_op jit(solution)/shard_map/ppermute | solution.py:47
  70.8 0.6 collective-permute-start.16
  71.4 0.9 collective-permute-start.15
  72.3 2.0 %collective-permute-start.14 = (bf16[128,640]{1,0:T(8,128)(2,1)S(1)}, bf16[128,640]{1,0:T(8,128)(2,1)S(1)}, u32[]{:S(2)}, u32[]{:S(2)}) collective-permute-start(bf16[128,640]{1,0:T(8,128)(2,1)S(1)} %pad_maximum_fusion.2), channel_id=1, source_target_pairs={{0,2},{1,3},{2,0},{3,1},{4,6},{5,7},{6,4},{7,5},{8,10},{9,11},{10,... | collective-permute-start | bytes 491528 | tf_op jit(solution)/shard_map/ppermute | solution.py:47
  74.3 4.4 %collective-permute-done.16 = bf16[128,640]{1,0:T(8,128)(2,1)S(1)} collective-permute-done((bf16[128,640]{1,0:T(8,128)(2,1)S(1)}, bf16[128,640]{1,0:T(8,128)(2,1)S(1)}, u32[]{:S(2)}, u32[]{:S(2)}) %collective-permute-start.16) | collective-permute-done | bytes 163872 | tf_op jit(solution)/shard_map/ppermute | solution.py:47
  78.7 0.6 collective-permute-done.15
  79.3 1.2 collective-permute-done.14
  80.4 0.1 pad_maximum_fusion.1
  80.5 0.1 collective-permute-start.18
  80.6 0.4 collective-permute-start.20
  81.0 1.5 %collective-permute-start.19 = (bf16[1,272,1024]{2,1,0:T(8,128)(2,1)S(1)}, bf16[1,272,1024]{2,1,0:T(8,128)(2,1)S(1)}, u32[]{:S(2)}, u32[]{:S(2)}) collective-permute-start(bf16[1,272,1024]{2,1,0:T(8,128)(2,1)S(1)} %collective-permute-done.17.refs_5_), channel_id=1, source_target_pairs={{0,4},{1,5},{2,6},{3,7},{4,0},{5,1},{6,2},{7,3},{8,12},{9,13},{10,... | collective-permute-start | bytes 1671176 | tf_op jit(solution)/shard_map/ppermute | solution.py:47
  82.5 0.3 collective-permute-done.18.far_ref
  82.8 2.2 %collective-permute-start.21 = (bf16[256,512]{1,0:T(8,128)(2,1)}, bf16[256,512]{1,0:T(8,128)(2,1)S(1)}, u32[]{:S(2)}, u32[]{:S(2)}) collective-permute-start(bf16[256,512]{1,0:T(8,128)(2,1)} %copy-done.11), channel_id=1, source_target_pairs={{0,24},{1,25},{2,26},{3,27},{4,28},{5,29},{6,30},{7,31},{8,16},{9,... | collective-permute-start | bytes 786440 | tf_op jit(solution)/shard_map/ppermute | solution.py:47
  85.0 0.7 collective-permute-start.22
  85.6 0.5 collective-permute-start.23
  86.2 10.7 %whiten.1 = (bf16[1024,1024]{1,0:T(8,128)(2,1)S(1)}, f32[1,1024]{1,0:T(1,128)S(1)}) custom-call(s32[1]{0:T(128)} %bitcast.1.place_ref, bf16[16,32,640]{2,1,0:T(8,128)(2,1)S(1)} %bitcast.11, bf16[16,32,640]{2,1,0:T(8,128)(2,1)} %collective-permute-done.18.far_ref, bf16[64,640]{1,0:T(8,128)(2,1)S(1)} %get-tuple-element.61.refs_0_, ...), custom_call_target="tpu_custom_call" | custom-call | flops 10737418240 | bytes 2097152 | tf_op jit(solution)/shard_map/whiten/pallas_call | solution.py:393
  96.9 4.7 %collective-permute-done.20.refs_1_ = bf16[256,512]{1,0:T(8,128)(2,1)S(1)} collective-permute-done((bf16[256,512]{1,0:T(8,128)(2,1)}, bf16[256,512]{1,0:T(8,128)(2,1)S(1)}, u32[]{:S(2)}, u32[]{:S(2)}) %collective-permute-start.20) | collective-permute-done | bytes 262176 | tf_op jit(solution)/shard_map/ppermute | solution.py:47
  101.6 2.2 %collective-permute-start.25 = (bf16[256,512]{1,0:T(8,128)(2,1)S(1)}, bf16[256,512]{1,0:T(8,128)(2,1)S(1)}, u32[]{:S(2)}, u32[]{:S(2)}) collective-permute-start(bf16[256,512]{1,0:T(8,128)(2,1)S(1)} %copy-done.6), channel_id=1, source_target_pairs={{0,20},{1,21},{2,22},{3,23},{4,16},{5,17},{6,18},{7,19},{8,28},{9,... | collective-permute-start | bytes 786440 | tf_op jit(solution)/shard_map/ppermute | solution.py:47
  103.9 4.0 %collective-permute-start.26 = (bf16[256,512]{1,0:T(8,128)(2,1)S(1)}, bf16[256,512]{1,0:T(8,128)(2,1)S(1)}, u32[]{:S(2)}, u32[]{:S(2)}) collective-permute-start(bf16[256,512]{1,0:T(8,128)(2,1)S(1)} %copy-done.4), channel_id=1, source_target_pairs={{0,28},{1,29},{2,30},{3,31},{4,24},{5,25},{6,26},{7,27},{8,20},{9,... | collective-permute-start | bytes 786440 | tf_op jit(solution)/shard_map/ppermute | solution.py:47
  107.9 20.4 %contrast.1 = (f32[1,256]{1,0:T(1,128)}, bf16[8,256,1024]{2,1,0:T(8,128)(2,1)S(1)}) custom-call(s32[1]{0:T(128)} %bitcast.group_ref, f32[1,1024]{1,0:T(1,128)S(1)} %get-tuple-element.79.mean_ref, bf16[1024,1024]{1,0:T(8,128)(2,1)S(1)} %get-tuple-element.80.whitener_ref.refs_3_, bf16[1,272,1024]{2,1,0:T(8,128)(2,1)} %bitcast.6.refs_0_, ...), custom_call_target="tpu_custom_call" | custom-call | flops 12884901888 | bytes 8388608 | tf_op jit(solution)/shard_map/contrast/pallas_call | solution.py:485
  128.4 1.3 weight_pieces.3
  129.7 0.1 collective-permute-start.28
  129.8 1.3 weight_pieces.2
  131.0 0.6 collective-permute-start.27
  131.7 0.6 collective-permute-start.29
  132.3 0.5 collective-permute-done.27.refs_1_
  132.8 7.2 %collective-permute-done.29.refs_2_ = bf16[128,1024]{1,0:T(8,128)(2,1)S(1)} collective-permute-done((bf16[128,1024]{1,0:T(8,128)(2,1)S(1)}, bf16[128,1024]{1,0:T(8,128)(2,1)S(1)}, u32[]{:S(2)}, u32[]{:S(2)}) %collective-permute-start.29) | collective-permute-done | bytes 262176 | tf_op jit(solution)/shard_map/ppermute | solution.py:47
  140.0 1.5 %finish.1 = f32[128,1024]{1,0:T(8,128)} custom-call(f32[128,1024]{1,0:T(8,128)S(1)} %get-tuple-element.94.refs_0_, bf16[128,1024]{1,0:T(8,128)(2,1)S(1)} %collective-permute-done.27.refs_1_, bf16[128,1024]{1,0:T(8,128)(2,1)S(1)} %collective-permute-done.29.refs_2_, bf16[1024,1024]{1,0:T(8,128)(2,1)S(1)} %get-tuple-element.80.whitener_ref.refs_3_), custom_call_target="tpu_custom_call" | custom-call | tf_op jit(solution)/shard_map/finish/pallas_call | solution.py:581
  (36 shorter events, 0.2 us)
Async XLA Ops:
  0.6 0.7 copy-start.1
  1.3 0.7 copy-start.2
  8.8 7.2 %collective-permute-start = (bf16[528,640]{1,0:T(8,128)(2,1)S(1)}, bf16[528,640]{1,0:T(8,128)(2,1)S(1)}, u32[]{:S(2)}, u32[]{:S(2)}) collective-permute-start(bf16[528,640]{1,0:T(8,128)(2,1)S(1)} %get-tuple-element.51.sent_ref), channel_id=1, source_target_pairs={{0,1},{1,0},{2,3},{3,2},{4,5},{5,4},{6,7},{7,6},{8,9},{9,8},{10,11... | collective-permute-start | bytes 2027528 | tf_op jit(solution)/shard_map/ppermute | solution.py:47
  9.3 33.7 %collective-permute-start.6 = (bf16[1,272,1024]{2,1,0:T(8,128)(2,1)}, bf16[1,272,1024]{2,1,0:T(8,128)(2,1)S(1)}, u32[]{:S(2)}, u32[]{:S(2)}) collective-permute-start(bf16[1,272,1024]{2,1,0:T(8,128)(2,1)} %bitcast.6.refs_0_), channel_id=1, source_target_pairs={{0,16},{1,17},{2,18},{3,19},{4,20},{5,21},{6,22},{7,23},{8,24},{9,... | collective-permute-start | bytes 1671176 | tf_op jit(solution)/shard_map/ppermute | solution.py:47
  13.0 30.0 %collective-permute-start.5 = (bf16[1,272,1024]{2,1,0:T(8,128)(2,1)}, bf16[1,272,1024]{2,1,0:T(8,128)(2,1)}, u32[]{:S(2)}, u32[]{:S(2)}) collective-permute-start(bf16[1,272,1024]{2,1,0:T(8,128)(2,1)} %bitcast.6.refs_0_), channel_id=1, source_target_pairs={{0,8},{1,9},{2,10},{3,11},{4,12},{5,13},{6,14},{7,15},{8,0},{9,1},... | collective-permute-start | bytes 1671176 | tf_op jit(solution)/shard_map/ppermute | solution.py:47
  14.6 28.4 %collective-permute-start.4 = (bf16[1,272,1024]{2,1,0:T(8,128)(2,1)}, bf16[1,272,1024]{2,1,0:T(8,128)(2,1)}, u32[]{:S(2)}, u32[]{:S(2)}) collective-permute-start(bf16[1,272,1024]{2,1,0:T(8,128)(2,1)} %bitcast.6.refs_0_), channel_id=1, source_target_pairs={{0,4},{1,5},{2,6},{3,7},{4,0},{5,1},{6,2},{7,3},{8,12},{9,13},{10,... | collective-permute-start | bytes 1671176 | tf_op jit(solution)/shard_map/ppermute | solution.py:47
  16.9 17.3 %collective-permute-start.2 = (bf16[144,640]{1,0:T(8,128)(2,1)S(1)}, bf16[144,640]{1,0:T(8,128)(2,1)S(1)}, u32[]{:S(2)}, u32[]{:S(2)}) collective-permute-start(bf16[144,640]{1,0:T(8,128)(2,1)S(1)} %get-tuple-element.54), channel_id=1, source_target_pairs={{0,4},{1,5},{2,6},{3,7},{4,0},{5,1},{6,2},{7,3},{8,12},{9,13},{10,... | collective-permute-start | bytes 552968 | tf_op jit(solution)/shard_map/ppermute | solution.py:47
  17.4 20.7 %collective-permute-start.3 = (bf16[144,640]{1,0:T(8,128)(2,1)}, bf16[144,640]{1,0:T(8,128)(2,1)S(1)}, u32[]{:S(2)}, u32[]{:S(2)}) collective-permute-start(bf16[144,640]{1,0:T(8,128)(2,1)} %get-tuple-element.55), channel_id=1, source_target_pairs={{0,6},{1,7},{2,4},{3,5},{4,2},{5,3},{6,0},{7,1},{8,14},{9,15},{10,... | collective-permute-start | bytes 552968 | tf_op jit(solution)/shard_map/ppermute | solution.py:47
  34.2 7.7 %collective-permute-start.1 = (bf16[144,640]{1,0:T(8,128)(2,1)}, bf16[144,640]{1,0:T(8,128)(2,1)S(1)}, u32[]{:S(2)}, u32[]{:S(2)}) collective-permute-start(bf16[144,640]{1,0:T(8,128)(2,1)} %get-tuple-element.53.sent_ref), channel_id=1, source_target_pairs={{0,2},{1,3},{2,0},{3,1},{4,6},{5,7},{6,4},{7,5},{8,10},{9,11},{10,... | collective-permute-start | bytes 552968 | tf_op jit(solution)/shard_map/ppermute | solution.py:47
  43.0 16.7 %copy-start = (bf16[256,4096]{1,0:T(8,128)(2,1)S(1)}, bf16[256,4096]{1,0:T(8,128)(2,1)}, u32[]{:S(2)}) copy-start(bf16[256,4096]{1,0:T(8,128)(2,1)} %features_hbm.3) | copy-start | bytes 6291460
  44.3 26.5 %collective-permute-start.13 = (bf16[2,272,1024]{2,1,0:T(8,128)(2,1)S(1)}, bf16[2,272,1024]{2,1,0:T(8,128)(2,1)S(1)}, u32[]{:S(2)}, u32[]{:S(2)}) collective-permute-start(bf16[2,272,1024]{2,1,0:T(8,128)(2,1)S(1)} %pad_maximum_fusion), channel_id=1, source_target_pairs={{0,4},{1,5},{2,6},{3,7},{4,0},{5,1},{6,2},{7,3},{8,12},{9,13},{10,... | collective-permute-start | bytes 3342344 | tf_op jit(solution)/shard_map/ppermute | solution.py:47
  45.9 8.6 %collective-permute-start.8 = (bf16[64,640]{1,0:T(8,128)(2,1)S(1)}, bf16[64,640]{1,0:T(8,128)(2,1)S(1)}, u32[]{:S(2)}, u32[]{:S(2)}) collective-permute-start(bf16[64,640]{1,0:T(8,128)(2,1)S(1)} %get-tuple-element.62), channel_id=1, source_target_pairs={{0,16},{1,17},{2,18},{3,19},{4,20},{5,21},{6,22},{7,23},{8,24},{9,... | collective-permute-start | bytes 245768 | tf_op jit(solution)/shard_map/ppermute | solution.py:47
  46.2 8.2 %collective-permute-start.9 = (bf16[64,640]{1,0:T(8,128)(2,1)S(1)}, bf16[64,640]{1,0:T(8,128)(2,1)S(1)}, u32[]{:S(2)}, u32[]{:S(2)}) collective-permute-start(bf16[64,640]{1,0:T(8,128)(2,1)S(1)} %get-tuple-element.63), channel_id=1, source_target_pairs={{0,24},{1,25},{2,26},{3,27},{4,28},{5,29},{6,30},{7,31},{8,16},{9,... | collective-permute-start | bytes 245768 | tf_op jit(solution)/shard_map/ppermute | solution.py:47
  48.7 6.5 %collective-permute-start.7 = (bf16[64,640]{1,0:T(8,128)(2,1)S(1)}, bf16[64,640]{1,0:T(8,128)(2,1)S(1)}, u32[]{:S(2)}, u32[]{:S(2)}) collective-permute-start(bf16[64,640]{1,0:T(8,128)(2,1)S(1)} %get-tuple-element.61.refs_0_), channel_id=1, source_target_pairs={{0,8},{1,9},{2,10},{3,11},{4,12},{5,13},{6,14},{7,15},{8,0},{9,1},... | collective-permute-start | bytes 245768 | tf_op jit(solution)/shard_map/ppermute | solution.py:47
  55.2 9.6 %collective-permute-start.12 = (bf16[32,640]{1,0:T(8,128)(2,1)S(1)}, bf16[32,640]{1,0:T(8,128)(2,1)S(1)}, u32[]{:S(2)}, u32[]{:S(2)}) collective-permute-start(bf16[32,640]{1,0:T(8,128)(2,1)S(1)} %add_convert_fusion), channel_id=1, source_target_pairs={{0,24},{1,25},{2,26},{3,27},{4,28},{5,29},{6,30},{7,31},{8,16},{9,... | collective-permute-start | bytes 122888 | tf_op jit(solution)/shard_map/ppermute | solution.py:47
  55.8 9.0 %collective-permute-start.11 = (bf16[32,640]{1,0:T(8,128)(2,1)S(1)}, bf16[32,640]{1,0:T(8,128)(2,1)S(1)}, u32[]{:S(2)}, u32[]{:S(2)}) collective-permute-start(bf16[32,640]{1,0:T(8,128)(2,1)S(1)} %add_convert_fusion), channel_id=1, source_target_pairs={{0,16},{1,17},{2,18},{3,19},{4,20},{5,21},{6,22},{7,23},{8,24},{9,... | collective-permute-start | bytes 122888 | tf_op jit(solution)/shard_map/ppermute | solution.py:47
  58.1 6.7 %collective-permute-start.10 = (bf16[32,640]{1,0:T(8,128)(2,1)S(1)}, bf16[32,640]{1,0:T(8,128)(2,1)S(1)}, u32[]{:S(2)}, u32[]{:S(2)}) collective-permute-start(bf16[32,640]{1,0:T(8,128)(2,1)S(1)} %add_convert_fusion), channel_id=1, source_target_pairs={{0,8},{1,9},{2,10},{3,11},{4,12},{5,13},{6,14},{7,15},{8,0},{9,1},... | collective-permute-start | bytes 122888 | tf_op jit(solution)/shard_map/ppermute | solution.py:47
  59.9 0.7 copy-start.3
  60.6 0.7 copy-start.5
  61.3 0.7 copy-start.7
  62.0 0.7 copy-start.9
  62.7 0.7 copy-start.10
  63.4 0.7 copy-start.11
  64.1 0.7 copy-start.12
  64.9 15.6 %collective-permute-start.17 = (bf16[1,272,1024]{2,1,0:T(8,128)(2,1)S(1)}, bf16[1,272,1024]{2,1,0:T(8,128)(2,1)S(1)}, u32[]{:S(2)}, u32[]{:S(2)}) collective-permute-start(bf16[1,272,1024]{2,1,0:T(8,128)(2,1)S(1)} %collective-permute-done.6.refs_3_), channel_id=1, source_target_pairs={{0,8},{1,9},{2,10},{3,11},{4,12},{5,13},{6,14},{7,15},{8,0},{9,1},... | collective-permute-start | bytes 1671176 | tf_op jit(solution)/shard_map/ppermute | solution.py:47
  70.8 7.9 %collective-permute-start.16 = (bf16[128,640]{1,0:T(8,128)(2,1)S(1)}, bf16[128,640]{1,0:T(8,128)(2,1)S(1)}, u32[]{:S(2)}, u32[]{:S(2)}) collective-permute-start(bf16[128,640]{1,0:T(8,128)(2,1)S(1)} %pad_maximum_fusion.2), channel_id=1, source_target_pairs={{0,6},{1,7},{2,4},{3,5},{4,2},{5,3},{6,0},{7,1},{8,14},{9,15},{10,... | collective-permute-start | bytes 491528 | tf_op jit(solution)/shard_map/ppermute | solution.py:47
  71.4 7.8 %collective-permute-start.15 = (bf16[128,640]{1,0:T(8,128)(2,1)S(1)}, bf16[128,640]{1,0:T(8,128)(2,1)S(1)}, u32[]{:S(2)}, u32[]{:S(2)}) collective-permute-start(bf16[128,640]{1,0:T(8,128)(2,1)S(1)} %pad_maximum_fusion.2), channel_id=1, source_target_pairs={{0,4},{1,5},{2,6},{3,7},{4,0},{5,1},{6,2},{7,3},{8,12},{9,13},{10,... | collective-permute-start | bytes 491528 | tf_op jit(solution)/shard_map/ppermute | solution.py:47
  72.3 8.1 %collective-permute-start.14 = (bf16[128,640]{1,0:T(8,128)(2,1)S(1)}, bf16[128,640]{1,0:T(8,128)(2,1)S(1)}, u32[]{:S(2)}, u32[]{:S(2)}) collective-permute-start(bf16[128,640]{1,0:T(8,128)(2,1)S(1)} %pad_maximum_fusion.2), channel_id=1, source_target_pairs={{0,2},{1,3},{2,0},{3,1},{4,6},{5,7},{6,4},{7,5},{8,10},{9,11},{10,... | collective-permute-start | bytes 491528 | tf_op jit(solution)/shard_map/ppermute | solution.py:47
  80.5 2.3 %collective-permute-start.18 = (bf16[16,32,640]{2,1,0:T(8,128)(2,1)S(1)}, bf16[16,32,640]{2,1,0:T(8,128)(2,1)}, u32[]{:S(2)}, u32[]{:S(2)}) collective-permute-start(bf16[16,32,640]{2,1,0:T(8,128)(2,1)S(1)} %bitcast.10), channel_id=1, source_target_pairs={{0,1},{1,0},{2,3},{3,2},{4,5},{5,4},{6,7},{7,6},{8,9},{9,8},{10,11... | collective-permute-start | bytes 1966088 | tf_op jit(solution)/shard_map/ppermute | solution.py:47
  80.6 21.0 %collective-permute-start.20 = (bf16[256,512]{1,0:T(8,128)(2,1)}, bf16[256,512]{1,0:T(8,128)(2,1)S(1)}, u32[]{:S(2)}, u32[]{:S(2)}) collective-permute-start(bf16[256,512]{1,0:T(8,128)(2,1)} %copy-done.12), channel_id=1, source_target_pairs={{0,16},{1,17},{2,18},{3,19},{4,20},{5,21},{6,22},{7,23},{8,24},{9,... | collective-permute-start | bytes 786440 | tf_op jit(solution)/shard_map/ppermute | solution.py:47
  81.0 20.7 %collective-permute-start.19 = (bf16[1,272,1024]{2,1,0:T(8,128)(2,1)S(1)}, bf16[1,272,1024]{2,1,0:T(8,128)(2,1)S(1)}, u32[]{:S(2)}, u32[]{:S(2)}) collective-permute-start(bf16[1,272,1024]{2,1,0:T(8,128)(2,1)S(1)} %collective-permute-done.17.refs_5_), channel_id=1, source_target_pairs={{0,4},{1,5},{2,6},{3,7},{4,0},{5,1},{6,2},{7,3},{8,12},{9,13},{10,... | collective-permute-start | bytes 1671176 | tf_op jit(solution)/shard_map/ppermute | solution.py:47
  82.8 21.1 %collective-permute-start.21 = (bf16[256,512]{1,0:T(8,128)(2,1)}, bf16[256,512]{1,0:T(8,128)(2,1)S(1)}, u32[]{:S(2)}, u32[]{:S(2)}) collective-permute-start(bf16[256,512]{1,0:T(8,128)(2,1)} %copy-done.11), channel_id=1, source_target_pairs={{0,24},{1,25},{2,26},{3,27},{4,28},{5,29},{6,30},{7,31},{8,16},{9,... | collective-permute-start | bytes 786440 | tf_op jit(solution)/shard_map/ppermute | solution.py:47
  85.0 43.4 %collective-permute-start.22 = (bf16[256,512]{1,0:T(8,128)(2,1)}, bf16[256,512]{1,0:T(8,128)(2,1)S(1)}, u32[]{:S(2)}, u32[]{:S(2)}) collective-permute-start(bf16[256,512]{1,0:T(8,128)(2,1)} %copy-done.10), channel_id=1, source_target_pairs={{0,8},{1,9},{2,10},{3,11},{4,12},{5,13},{6,14},{7,15},{8,0},{9,1},... | collective-permute-start | bytes 786440 | tf_op jit(solution)/shard_map/ppermute | solution.py:47
  85.6 42.7 %collective-permute-start.23 = (bf16[256,512]{1,0:T(8,128)(2,1)}, bf16[256,512]{1,0:T(8,128)(2,1)S(1)}, u32[]{:S(2)}, u32[]{:S(2)}) collective-permute-start(bf16[256,512]{1,0:T(8,128)(2,1)} %copy-done.9), channel_id=1, source_target_pairs={{0,4},{1,5},{2,6},{3,7},{4,0},{5,1},{6,2},{7,3},{8,12},{9,13},{10,... | collective-permute-start | bytes 786440 | tf_op jit(solution)/shard_map/ppermute | solution.py:47
  86.2 15.5 %copy-start.8 = (bf16[256,512]{1,0:T(8,128)(2,1)S(1)}, bf16[256,512]{1,0:T(8,128)(2,1)}, u32[]{:S(2)}) copy-start(bf16[256,512]{1,0:T(8,128)(2,1)} %copy-done.7) | copy-start | bytes 786436
  86.2 15.5 %copy-start.6 = (bf16[256,512]{1,0:T(8,128)(2,1)S(1)}, bf16[256,512]{1,0:T(8,128)(2,1)}, u32[]{:S(2)}) copy-start(bf16[256,512]{1,0:T(8,128)(2,1)} %copy-done.5) | copy-start | bytes 786436
  86.2 17.7 %copy-start.4 = (bf16[256,512]{1,0:T(8,128)(2,1)S(1)}, bf16[256,512]{1,0:T(8,128)(2,1)}, u32[]{:S(2)}) copy-start(bf16[256,512]{1,0:T(8,128)(2,1)} %copy-done.3) | copy-start | bytes 786436
  101.6 26.7 %collective-permute-start.24 = (bf16[256,512]{1,0:T(8,128)(2,1)S(1)}, bf16[256,512]{1,0:T(8,128)(2,1)S(1)}, u32[]{:S(2)}, u32[]{:S(2)}) collective-permute-start(bf16[256,512]{1,0:T(8,128)(2,1)S(1)} %copy-done.8), channel_id=1, source_target_pairs={{0,12},{1,13},{2,14},{3,15},{4,8},{5,9},{6,10},{7,11},{8,4},{9,5},... | collective-permute-start | bytes 786440 | tf_op jit(solution)/shard_map/ppermute | solution.py:47
  101.6 26.7 %collective-permute-start.25 = (bf16[256,512]{1,0:T(8,128)(2,1)S(1)}, bf16[256,512]{1,0:T(8,128)(2,1)S(1)}, u32[]{:S(2)}, u32[]{:S(2)}) collective-permute-start(bf16[256,512]{1,0:T(8,128)(2,1)S(1)} %copy-done.6), channel_id=1, source_target_pairs={{0,20},{1,21},{2,22},{3,23},{4,16},{5,17},{6,18},{7,19},{8,28},{9,... | collective-permute-start | bytes 786440 | tf_op jit(solution)/shard_map/ppermute | solution.py:47
  103.9 24.5 %collective-permute-start.26 = (bf16[256,512]{1,0:T(8,128)(2,1)S(1)}, bf16[256,512]{1,0:T(8,128)(2,1)S(1)}, u32[]{:S(2)}, u32[]{:S(2)}) collective-permute-start(bf16[256,512]{1,0:T(8,128)(2,1)S(1)} %copy-done.4), channel_id=1, source_target_pairs={{0,28},{1,29},{2,30},{3,31},{4,24},{5,25},{6,26},{7,27},{8,20},{9,... | collective-permute-start | bytes 786440 | tf_op jit(solution)/shard_map/ppermute | solution.py:47
  129.7 1.9 %collective-permute-start.28 = (bf16[128,1024]{1,0:T(8,128)(2,1)S(1)}, bf16[128,1024]{1,0:T(8,128)(2,1)S(1)}, u32[]{:S(2)}, u32[]{:S(2)}) collective-permute-start(bf16[128,1024]{1,0:T(8,128)(2,1)S(1)} %get-tuple-element.97), channel_id=1, source_target_pairs={{0,1},{1,0},{2,3},{3,2},{4,5},{5,4},{6,7},{7,6},{8,9},{9,8},{10,11... | collective-permute-start | bytes 786440 | tf_op jit(solution)/shard_map/ppermute | solution.py:47
  131.0 1.7 %collective-permute-start.27 = (bf16[128,1024]{1,0:T(8,128)(2,1)S(1)}, bf16[128,1024]{1,0:T(8,128)(2,1)S(1)}, u32[]{:S(2)}, u32[]{:S(2)}) collective-permute-start(bf16[128,1024]{1,0:T(8,128)(2,1)S(1)} %get-tuple-element.95), channel_id=1, source_target_pairs={{0,1},{1,0},{2,3},{3,2},{4,5},{5,4},{6,7},{7,6},{8,9},{9,8},{10,11... | collective-permute-start | bytes 786440 | tf_op jit(solution)/shard_map/ppermute | solution.py:47
  131.7 8.3 %collective-permute-start.29 = (bf16[128,1024]{1,0:T(8,128)(2,1)S(1)}, bf16[128,1024]{1,0:T(8,128)(2,1)S(1)}, u32[]{:S(2)}, u32[]{:S(2)}) collective-permute-start(bf16[128,1024]{1,0:T(8,128)(2,1)S(1)} %join.1), channel_id=1, source_target_pairs={{0,2},{1,3},{2,0},{3,1},{4,6},{5,7},{6,4},{7,5},{8,10},{9,11},{10,... | collective-permute-start | bytes 786440 | tf_op jit(solution)/shard_map/ppermute | solution.py:47

commit v11 on v10

--- a/solution.py
+++ b/solution.py
@@ -614,7 +614,6 @@
     if direct:
         block_x = xor_permute(block, by_x)
         block_far = xor_permute(block, by_far)
-        block_near = xor_permute(block, by_near)
     else:
         gathered = lax.all_gather(block, "sp", tiled=True)
 
@@ -629,12 +628,8 @@
         own = (me >> low) & (count - 1)
         keep, sends, seen = stage(own, keep, sent, arrived, seen, count, embed)
         if direct and stages:
-            group_scalar = group.reshape(1)
-            *sends, block_x, block_near, block_far, group_scalar = lax.optimization_barrier(
-                (*sends, block_x, block_near, block_far, group_scalar)
-            )
-            slices = list(cut(group_scalar, features, groups))
-            pair_x = xor_permute(jnp.concatenate([block_far, block_near]), by_x)
+            *sends, block_far, block_x = lax.optimization_barrier((*sends, block_far, block_x))
+            far_x = xor_permute(block_far, by_x)
         arrived = [xor_permute(piece, (r + 1) << low) for r, piece in enumerate(sends)]
         sent = sends[0]
         stages.append((low, count))
@@ -655,34 +650,39 @@
     part = part.astype(BF16)
     for number, (low, count) in enumerate(reversed(stages)):
         if direct and number == 1:
-            part, block_far, slices[4] = lax.optimization_barrier((part, block_far, slices[4]))
-            block_far_near = xor_permute(block_far, by_near)
-            slices[4] = xor_permute(slices[4], by_far)
-            part, pair_x = lax.optimization_barrier((part, pair_x))
+            part, block_far, block = lax.optimization_barrier((part, block_far, block))
+            far_near = xor_permute(block_far, by_near)
+            block_near = xor_permute(block, by_near)
+            part, far_x = lax.optimization_barrier((part, far_x))
         part = jnp.concatenate(
             [part] + [xor_permute(part, r << low) for r in range(1, count)], axis=0
         )
     part = part.reshape(-1, size, part.shape[1])
     if direct:
-        part, block_far_near = lax.optimization_barrier((part, block_far_near))
-        far_near_x = xor_permute(block_far_near, by_x)
-        blocks = [block, block_x, block_near, block_far, pair_x, block_far_near, far_near_x]
-        order = [0, 1, 2, 4, 5, 3, 6, 7]
+        group_scalar = group.reshape(1)
+        part, far_near, group_scalar = lax.optimization_barrier((part, far_near, group_scalar))
+        far_near_x = xor_permute(far_near, by_x)
+        slices = list(cut(group_scalar, features, groups))
+        slices[4] = xor_permute(slices[4], by_far)
     else:
         order = slice_order = list(range(groups))
         blocks = [
             lax.dynamic_index_in_dim(gathered, group ^ k, 0, keepdims=True) for k in order
         ]
     other = xor_permute(part, 1)
+    whitener, mean = whiten(place.reshape(1), part, other, sums, seen, rows, embed)
     if direct:
-        slice_order = [0, 4, 6, 2, 1, 3, 5, 7]
-        later = slice_order[2:]
-        other, *held = lax.optimization_barrier((other, *(slices[k] for k in later)))
+        later = (2, 6, 5, 7, 1, 3)
+        mean, block_near, far_near_x, slices[4], *held = lax.optimization_barrier(
+            (mean, block_near, far_near_x, slices[4], *(slices[k] for k in later))
+        )
+        near_x = xor_permute(block_near, by_x)
         for k, piece in zip(later, held):
             slices[k] = xor_permute(piece, k * shares)
+        slice_order = [0, 4, *later]
         slices = [slices[k] for k in slice_order]
-
-    whitener, mean = whiten(place.reshape(1), part, other, sums, seen, rows, embed)
+        blocks = [block, block_x, block_near, near_x, block_far, far_x, far_near, far_near_x]
+        order = list(range(groups))
     loss, grad = contrast(group.reshape(1), blocks, order, mean, whitener)
     group, window = group.reshape(1), window.reshape(1)
     pieces = []

time: 142 us -> 148 us (1.042)
  waiting for transfers between devices: 50.6 us -> 61.1 us
  local copies, waits for them, and re-layouts: 6.25 us -> 2.16 us
  starting transfers between devices: 38.1 us -> 40.5 us
    ppermute x30 -> x31, waiting for transfers between devices: 50.6 us -> 61.1 us  [xor_permute(): return lax.ppermute(piece, AXES, [(i, i ^ mask) for i in range(devices)])]
    unnamed x26 -> x14, local copies, waits for them, and re-layouts: 6.25 us -> 2.16 us
    ppermute x30 -> x31, starting transfers between devices: 38.1 us -> 40.5 us  [xor_permute(): return lax.ppermute(piece, AXES, [(i, i ^ mask) for i in range(devices)])]
  transfers between devices with their start and end apart: 30 -> 31, of which waited for: 13 -> 15; matrix products, arithmetic and copies ran while one was open for 0% -> 0% of each run, Pallas kernels for 24% -> 23%
where the time goes in v11:
time: 148 us
  waiting for transfers between devices  61.1 us (41%)
  Pallas kernels  43.3 us (29%)
  starting transfers between devices  40.5 us (27%)
  local copies, waits for them, and re-layouts  2.16 us (1%)
    ppermute x31, waiting for transfers between devices, xor_permute(): return lax.ppermute(piece, AXES, [(i, i ^ mask) for i in range(devices)])  61.1 us
    ppermute x31, starting transfers between devices, xor_permute(): return lax.ppermute(piece, AXES, [(i, i ^ mask) for i in range(devices)])  40.5 us
    pallas_call x1, Pallas kernels, contrast(): pl.pallas_call(functools.partial(contrast_kernel, order), in_specs=[smem(...  20.4 us
    pallas_call x1, Pallas kernels, whiten(): pl.pallas_call(make_whiten_kernel(rows, count), in_specs=[smem()] + [vmem...  10.7 us
    pallas_call x1, Pallas kernels, project(): pl.pallas_call(project_kernel, in_specs=[smem(), smem(), hbm, hbm, hbm],...  6.81 us
  transfers between devices with their start and end apart: 31, of which 15 were waited for; matrix products, arithmetic and copies ran while one was open for 0% of the time, Pallas kernels for 23%

profile of v11, /device:TPU:0, one launch (start us, length us, event | category | flops | bytes accessed | tf_op | source)
XLA Modules:
  0.0 147.9 jit_solution(6057864831019351538)
XLA Ops:
  0.6 0.7 copy-done.1
  1.3 0.7 copy-done.2
  2.0 6.8 %project.1 = (bf16[272,1024]{1,0:T(8,128)(2,1)}, bf16[528,640]{1,0:T(8,128)(2,1)S(1)}, f32[512,640]{1,0:T(8,128)S(1)}) custom-call(s32[1]{0:T(128)} %bitcast.4.me_ref, s32[1,4]{1,0:T(1,128)S(1)} %copy-done.2, bf16[256,4096]{1,0:T(8,128)(2,1)} %features_hbm.3, bf16[4096,1024]{1,0:T(8,128)(2,1)} %weight_hbm.1, s32[4,256]{1,0:T(4,128)S(1)} %bitcast.12), custom_call_target="tpu_custom_call" | custom-call | flops 2147483648 | bytes 8388608 | tf_op jit(solution)/shard_map/project/pallas_call | solution.py:186
  8.8 0.5 collective-permute-start
  9.3 2.6 %collective-permute-start.5 = (bf16[1,272,1024]{2,1,0:T(8,128)(2,1)}, bf16[1,272,1024]{2,1,0:T(8,128)(2,1)}, u32[]{:S(2)}, u32[]{:S(2)}) collective-permute-start(bf16[1,272,1024]{2,1,0:T(8,128)(2,1)} %bitcast.6.refs_0_), channel_id=1, source_target_pairs={{0,4},{1,5},{2,6},{3,7},{4,0},{5,1},{6,2},{7,3},{8,12},{9,13},{10,... | collective-permute-start | bytes 1671176 | tf_op jit(solution)/shard_map/ppermute | solution.py:47
  11.9 2.6 %collective-permute-start.4 = (bf16[1,272,1024]{2,1,0:T(8,128)(2,1)}, bf16[1,272,1024]{2,1,0:T(8,128)(2,1)}, u32[]{:S(2)}, u32[]{:S(2)}) collective-permute-start(bf16[1,272,1024]{2,1,0:T(8,128)(2,1)} %bitcast.6.refs_0_), channel_id=1, source_target_pairs={{0,16},{1,17},{2,18},{3,19},{4,20},{5,21},{6,22},{7,23},{8,24},{9,... | collective-permute-start | bytes 1671176 | tf_op jit(solution)/shard_map/ppermute | solution.py:47
  14.5 0.0 collective-permute-done.refs_0_
  14.5 0.8 stage.2
  15.3 0.5 collective-permute-start.2
  15.8 2.4 %collective-permute-start.3 = (bf16[144,640]{1,0:T(8,128)(2,1)S(1)}, bf16[144,640]{1,0:T(8,128)(2,1)S(1)}, u32[]{:S(2)}, u32[]{:S(2)}) collective-permute-start(bf16[144,640]{1,0:T(8,128)(2,1)S(1)} %get-tuple-element.57), channel_id=1, source_target_pairs={{0,6},{1,7},{2,4},{3,5},{4,2},{5,3},{6,0},{7,1},{8,14},{9,15},{10,... | collective-permute-start | bytes 552968 | tf_op jit(solution)/shard_map/ppermute | solution.py:47
  18.2 0.5 collective-permute-start.1
  18.7 10.8 %collective-permute-done.2.refs_1_ = bf16[144,640]{1,0:T(8,128)(2,1)S(1)} collective-permute-done((bf16[144,640]{1,0:T(8,128)(2,1)}, bf16[144,640]{1,0:T(8,128)(2,1)S(1)}, u32[]{:S(2)}, u32[]{:S(2)}) %collective-permute-start.2) | collective-permute-done | bytes 184352 | tf_op jit(solution)/shard_map/ppermute | solution.py:47
  29.5 4.9 %collective-permute-done.3.refs_2_ = bf16[144,640]{1,0:T(8,128)(2,1)S(1)} collective-permute-done((bf16[144,640]{1,0:T(8,128)(2,1)S(1)}, bf16[144,640]{1,0:T(8,128)(2,1)S(1)}, u32[]{:S(2)}, u32[]{:S(2)}) %collective-permute-start.3) | collective-permute-done | bytes 184352 | tf_op jit(solution)/shard_map/ppermute | solution.py:47
  34.4 0.1 stage.3
  34.6 0.0 copy-start.5
  34.6 5.2 %collective-permute-done.4.refs_4_ = bf16[1,272,1024]{2,1,0:T(8,128)(2,1)} collective-permute-done((bf16[1,272,1024]{2,1,0:T(8,128)(2,1)}, bf16[1,272,1024]{2,1,0:T(8,128)(2,1)}, u32[]{:S(2)}, u32[]{:S(2)}) %collective-permute-start.4) | collective-permute-done | bytes 557088 | tf_op jit(solution)/shard_map/ppermute | solution.py:47
  39.7 0.0 collective-permute-start.7
  39.8 3.5 %collective-permute-start.8 = (bf16[64,640]{1,0:T(8,128)(2,1)S(1)}, bf16[64,640]{1,0:T(8,128)(2,1)S(1)}, u32[]{:S(2)}, u32[]{:S(2)}) collective-permute-start(bf16[64,640]{1,0:T(8,128)(2,1)S(1)} %get-tuple-element.65), channel_id=1, source_target_pairs={{0,24},{1,25},{2,26},{3,27},{4,28},{5,29},{6,30},{7,31},{8,16},{9,... | collective-permute-start | bytes 245768 | tf_op jit(solution)/shard_map/ppermute | solution.py:47
  43.2 0.6 collective-permute-start.6
  43.8 0.5 collective-permute-start.12
  44.3 5.0 %collective-permute-done.7.refs_2_ = bf16[64,640]{1,0:T(8,128)(2,1)S(1)} collective-permute-done((bf16[64,640]{1,0:T(8,128)(2,1)S(1)}, bf16[64,640]{1,0:T(8,128)(2,1)S(1)}, u32[]{:S(2)}, u32[]{:S(2)}) %collective-permute-start.7) | collective-permute-done | bytes 81952 | tf_op jit(solution)/shard_map/ppermute | solution.py:47
  49.3 0.0 collective-permute-done.8.refs_3_
  49.3 0.5 collective-permute-done.6.refs_1_
  49.8 2.3 %collective-permute-start.11 = (bf16[32,640]{1,0:T(8,128)(2,1)S(1)}, bf16[32,640]{1,0:T(8,128)(2,1)S(1)}, u32[]{:S(2)}, u32[]{:S(2)}) collective-permute-start(bf16[32,640]{1,0:T(8,128)(2,1)S(1)} %add_convert_fusion), channel_id=1, source_target_pairs={{0,24},{1,25},{2,26},{3,27},{4,28},{5,29},{6,30},{7,31},{8,16},{9,... | collective-permute-start | bytes 122888 | tf_op jit(solution)/shard_map/ppermute | solution.py:47
  52.1 0.3 collective-permute-start.10
  52.4 1.9 %collective-permute-start.9 = (bf16[32,640]{1,0:T(8,128)(2,1)S(1)}, bf16[32,640]{1,0:T(8,128)(2,1)S(1)}, u32[]{:S(2)}, u32[]{:S(2)}) collective-permute-start(bf16[32,640]{1,0:T(8,128)(2,1)S(1)} %add_convert_fusion), channel_id=1, source_target_pairs={{0,8},{1,9},{2,10},{3,11},{4,12},{5,13},{6,14},{7,15},{8,0},{9,1},... | collective-permute-start | bytes 122888 | tf_op jit(solution)/shard_map/ppermute | solution.py:47
  54.2 1.4 collective-permute-done.11
  55.7 1.4 collective-permute-done.10
  57.1 0.1 collective-permute-done.9
  57.2 1.1 collective-permute-start.16
  58.3 1.5 %collective-permute-start.15 = (bf16[128,640]{1,0:T(8,128)(2,1)S(1)}, bf16[128,640]{1,0:T(8,128)(2,1)S(1)}, u32[]{:S(2)}, u32[]{:S(2)}) collective-permute-start(bf16[128,640]{1,0:T(8,128)(2,1)S(1)} %pad_maximum_fusion.1), channel_id=1, source_target_pairs={{0,6},{1,7},{2,4},{3,5},{4,2},{5,3},{6,0},{7,1},{8,14},{9,15},{10,... | collective-permute-start | bytes 491528 | tf_op jit(solution)/shard_map/ppermute | solution.py:47
  59.8 1.5 %collective-permute-start.14 = (bf16[128,640]{1,0:T(8,128)(2,1)S(1)}, bf16[128,640]{1,0:T(8,128)(2,1)S(1)}, u32[]{:S(2)}, u32[]{:S(2)}) collective-permute-start(bf16[128,640]{1,0:T(8,128)(2,1)S(1)} %pad_maximum_fusion.1), channel_id=1, source_target_pairs={{0,4},{1,5},{2,6},{3,7},{4,0},{5,1},{6,2},{7,3},{8,12},{9,13},{10,... | collective-permute-start | bytes 491528 | tf_op jit(solution)/shard_map/ppermute | solution.py:47
  61.3 0.5 collective-permute-start.13
  61.8 3.6 %collective-permute-done.15 = bf16[128,640]{1,0:T(8,128)(2,1)S(1)} collective-permute-done((bf16[128,640]{1,0:T(8,128)(2,1)S(1)}, bf16[128,640]{1,0:T(8,128)(2,1)S(1)}, u32[]{:S(2)}, u32[]{:S(2)}) %collective-permute-start.15) | collective-permute-done | bytes 163872 | tf_op jit(solution)/shard_map/ppermute | solution.py:47
  65.4 1.8 %collective-permute-done.14 = bf16[128,640]{1,0:T(8,128)(2,1)S(1)} collective-permute-done((bf16[128,640]{1,0:T(8,128)(2,1)S(1)}, bf16[128,640]{1,0:T(8,128)(2,1)S(1)}, u32[]{:S(2)}, u32[]{:S(2)}) %collective-permute-start.14) | collective-permute-done | bytes 163872 | tf_op jit(solution)/shard_map/ppermute | solution.py:47
  67.2 0.0 collective-permute-done.13
  67.2 0.1 pad_maximum_fusion
  67.3 4.0 %collective-permute-done.16.refs_6_ = bf16[1,272,1024]{2,1,0:T(8,128)(2,1)S(1)} collective-permute-done((bf16[1,272,1024]{2,1,0:T(8,128)(2,1)}, bf16[1,272,1024]{2,1,0:T(8,128)(2,1)S(1)}, u32[]{:S(2)}, u32[]{:S(2)}) %collective-permute-start.16) | collective-permute-done | bytes 557088 | tf_op jit(solution)/shard_map/ppermute | solution.py:47
  71.3 0.8 copy-done.3
  72.1 0.0 collective-permute-start.17
  72.1 0.3 collective-permute-start.18
  72.4 0.5 collective-permute-start.19
  73.0 0.3 cut.1
  73.3 1.6 %collective-permute-start.20 = (bf16[256,512]{1,0:T(8,128)(2,1)S(1)}, bf16[256,512]{1,0:T(8,128)(2,1)S(1)}, u32[]{:S(2)}, u32[]{:S(2)}) collective-permute-start(bf16[256,512]{1,0:T(8,128)(2,1)S(1)} %get-tuple-element.75), channel_id=1, source_target_pairs={{0,16},{1,17},{2,18},{3,19},{4,20},{5,21},{6,22},{7,23},{8,24},{9,... | collective-permute-start | bytes 786440 | tf_op jit(solution)/shard_map/ppermute | solution.py:47
  74.9 0.0 collective-permute-done.17.far_ref
  74.9 10.7 %whiten.1 = (bf16[1024,1024]{1,0:T(8,128)(2,1)S(1)}, f32[1,1024]{1,0:T(1,128)S(1)}) custom-call(s32[1]{0:T(128)} %bitcast.1.place_ref, bf16[16,32,640]{2,1,0:T(8,128)(2,1)S(1)} %bitcast.11, bf16[16,32,640]{2,1,0:T(8,128)(2,1)} %collective-permute-done.17.far_ref, bf16[64,640]{1,0:T(8,128)(2,1)S(1)} %copy-done.6, ...), custom_call_target="tpu_custom_call" | custom-call | flops 10737418240 | bytes 2097152 | tf_op jit(solution)/shard_map/whiten/pallas_call | solution.py:393
  85.6 7.3 %collective-permute-done.18.refs_2_ = bf16[1,272,1024]{2,1,0:T(8,128)(2,1)S(1)} collective-permute-done((bf16[1,272,1024]{2,1,0:T(8,128)(2,1)}, bf16[1,272,1024]{2,1,0:T(8,128)(2,1)S(1)}, u32[]{:S(2)}, u32[]{:S(2)}) %collective-permute-start.18) | collective-permute-done | bytes 557088 | tf_op jit(solution)/shard_map/ppermute | solution.py:47
  93.0 0.5 collective-permute-start.21
  93.5 1.2 collective-permute-start.22
  94.7 1.5 %collective-permute-start.23 = (bf16[256,512]{1,0:T(8,128)(2,1)S(1)}, bf16[256,512]{1,0:T(8,128)(2,1)S(1)}, u32[]{:S(2)}, u32[]{:S(2)}) collective-permute-start(bf16[256,512]{1,0:T(8,128)(2,1)S(1)} %get-tuple-element.93), channel_id=1, source_target_pairs={{0,24},{1,25},{2,26},{3,27},{4,28},{5,29},{6,30},{7,31},{8,16},{9,... | collective-permute-start | bytes 786440 | tf_op jit(solution)/shard_map/ppermute | solution.py:47
  96.2 1.8 %collective-permute-start.24 = (bf16[256,512]{1,0:T(8,128)(2,1)S(1)}, bf16[256,512]{1,0:T(8,128)(2,1)S(1)}, u32[]{:S(2)}, u32[]{:S(2)}) collective-permute-start(bf16[256,512]{1,0:T(8,128)(2,1)S(1)} %get-tuple-element.94), channel_id=1, source_target_pairs={{0,20},{1,21},{2,22},{3,23},{4,16},{5,17},{6,18},{7,19},{8,28},{9,... | collective-permute-start | bytes 786440 | tf_op jit(solution)/shard_map/ppermute | solution.py:47
  97.9 1.5 %collective-permute-start.25 = (bf16[256,512]{1,0:T(8,128)(2,1)S(1)}, bf16[256,512]{1,0:T(8,128)(2,1)S(1)}, u32[]{:S(2)}, u32[]{:S(2)}) collective-permute-start(bf16[256,512]{1,0:T(8,128)(2,1)S(1)} %get-tuple-element.95), channel_id=1, source_target_pairs={{0,28},{1,29},{2,30},{3,31},{4,24},{5,25},{6,26},{7,27},{8,20},{9,... | collective-permute-start | bytes 786440 | tf_op jit(solution)/shard_map/ppermute | solution.py:47
  99.4 4.2 %collective-permute-done.22.refs_2_ = bf16[256,512]{1,0:T(8,128)(2,1)S(1)} collective-permute-done((bf16[256,512]{1,0:T(8,128)(2,1)S(1)}, bf16[256,512]{1,0:T(8,128)(2,1)S(1)}, u32[]{:S(2)}, u32[]{:S(2)}) %collective-permute-start.22) | collective-permute-done | bytes 262176 | tf_op jit(solution)/shard_map/ppermute | solution.py:47
  103.6 1.5 %collective-permute-start.26 = (bf16[256,512]{1,0:T(8,128)(2,1)S(1)}, bf16[256,512]{1,0:T(8,128)(2,1)S(1)}, u32[]{:S(2)}, u32[]{:S(2)}) collective-permute-start(bf16[256,512]{1,0:T(8,128)(2,1)S(1)} %get-tuple-element.96), channel_id=1, source_target_pairs={{0,4},{1,5},{2,6},{3,7},{4,0},{5,1},{6,2},{7,3},{8,12},{9,13},{10,... | collective-permute-start | bytes 786440 | tf_op jit(solution)/shard_map/ppermute | solution.py:47
  105.1 4.1 %collective-permute-done.21.refs_3_ = bf16[1,272,1024]{2,1,0:T(8,128)(2,1)S(1)} collective-permute-done((bf16[1,272,1024]{2,1,0:T(8,128)(2,1)S(1)}, bf16[1,272,1024]{2,1,0:T(8,128)(2,1)S(1)}, u32[]{:S(2)}, u32[]{:S(2)}) %collective-permute-start.21) | collective-permute-done | bytes 557088 | tf_op jit(solution)/shard_map/ppermute | solution.py:47
  109.3 5.0 %collective-permute-start.27 = (bf16[256,512]{1,0:T(8,128)(2,1)S(1)}, bf16[256,512]{1,0:T(8,128)(2,1)S(1)}, u32[]{:S(2)}, u32[]{:S(2)}) collective-permute-start(bf16[256,512]{1,0:T(8,128)(2,1)S(1)} %get-tuple-element.97), channel_id=1, source_target_pairs={{0,12},{1,13},{2,14},{3,15},{4,8},{5,9},{6,10},{7,11},{8,4},{9,5},... | collective-permute-start | bytes 786440 | tf_op jit(solution)/shard_map/ppermute | solution.py:47
  114.3 20.4 %contrast.1 = (f32[1,256]{1,0:T(1,128)}, bf16[8,256,1024]{2,1,0:T(8,128)(2,1)S(1)}) custom-call(s32[1]{0:T(128)} %bitcast.group_ref, f32[1,1024]{1,0:T(1,128)S(1)} %get-tuple-element.82.mean_ref, bf16[1024,1024]{1,0:T(8,128)(2,1)S(1)} %get-tuple-element.83.whitener_ref.refs_3_, bf16[1,272,1024]{2,1,0:T(8,128)(2,1)} %bitcast.6.refs_0_, ...), custom_call_target="tpu_custom_call" | custom-call | flops 12884901888 | bytes 8388608 | tf_op jit(solution)/shard_map/contrast/pallas_call | solution.py:485
  134.8 1.3 weight_pieces.3
  136.1 0.1 collective-permute-start.29
  136.2 1.3 weight_pieces.2
  137.5 0.6 collective-permute-start.28
  138.1 1.6 %collective-permute-start.30 = (bf16[128,1024]{1,0:T(8,128)(2,1)S(1)}, bf16[128,1024]{1,0:T(8,128)(2,1)S(1)}, u32[]{:S(2)}, u32[]{:S(2)}) collective-permute-start(bf16[128,1024]{1,0:T(8,128)(2,1)S(1)} %join.1), channel_id=1, source_target_pairs={{0,2},{1,3},{2,0},{3,1},{4,6},{5,7},{6,4},{7,5},{8,10},{9,11},{10,... | collective-permute-start | bytes 786440 | tf_op jit(solution)/shard_map/ppermute | solution.py:47
  139.7 6.7 %collective-permute-done.30.refs_2_ = bf16[128,1024]{1,0:T(8,128)(2,1)S(1)} collective-permute-done((bf16[128,1024]{1,0:T(8,128)(2,1)S(1)}, bf16[128,1024]{1,0:T(8,128)(2,1)S(1)}, u32[]{:S(2)}, u32[]{:S(2)}) %collective-permute-start.30) | collective-permute-done | bytes 262176 | tf_op jit(solution)/shard_map/ppermute | solution.py:47
  146.4 1.5 %finish.1 = f32[128,1024]{1,0:T(8,128)} custom-call(f32[128,1024]{1,0:T(8,128)S(1)} %get-tuple-element.98.refs_0_, bf16[128,1024]{1,0:T(8,128)(2,1)S(1)} %collective-permute-done.28.refs_1_, bf16[128,1024]{1,0:T(8,128)(2,1)S(1)} %collective-permute-done.30.refs_2_, bf16[1024,1024]{1,0:T(8,128)(2,1)S(1)} %get-tuple-element.83.whitener_ref.refs_3_), custom_call_target="tpu_custom_call" | custom-call | tf_op jit(solution)/shard_map/finish/pallas_call | solution.py:581
  (25 shorter events, 0.1 us)
Async XLA Ops:
  0.6 0.7 copy-start.1
  1.3 0.7 copy-start.2
  8.8 5.7 %collective-permute-start = (bf16[528,640]{1,0:T(8,128)(2,1)S(1)}, bf16[528,640]{1,0:T(8,128)(2,1)S(1)}, u32[]{:S(2)}, u32[]{:S(2)}) collective-permute-start(bf16[528,640]{1,0:T(8,128)(2,1)S(1)} %get-tuple-element.53.sent_ref), channel_id=1, source_target_pairs={{0,1},{1,0},{2,3},{3,2},{4,5},{5,4},{6,7},{7,6},{8,9},{9,8},{10,11... | collective-permute-start | bytes 2027528 | tf_op jit(solution)/shard_map/ppermute | solution.py:47
  9.3 25.3 %collective-permute-start.5 = (bf16[1,272,1024]{2,1,0:T(8,128)(2,1)}, bf16[1,272,1024]{2,1,0:T(8,128)(2,1)}, u32[]{:S(2)}, u32[]{:S(2)}) collective-permute-start(bf16[1,272,1024]{2,1,0:T(8,128)(2,1)} %bitcast.6.refs_0_), channel_id=1, source_target_pairs={{0,4},{1,5},{2,6},{3,7},{4,0},{5,1},{6,2},{7,3},{8,12},{9,13},{10,... | collective-permute-start | bytes 1671176 | tf_op jit(solution)/shard_map/ppermute | solution.py:47
  11.9 27.9 %collective-permute-start.4 = (bf16[1,272,1024]{2,1,0:T(8,128)(2,1)}, bf16[1,272,1024]{2,1,0:T(8,128)(2,1)}, u32[]{:S(2)}, u32[]{:S(2)}) collective-permute-start(bf16[1,272,1024]{2,1,0:T(8,128)(2,1)} %bitcast.6.refs_0_), channel_id=1, source_target_pairs={{0,16},{1,17},{2,18},{3,19},{4,20},{5,21},{6,22},{7,23},{8,24},{9,... | collective-permute-start | bytes 1671176 | tf_op jit(solution)/shard_map/ppermute | solution.py:47
  15.3 14.3 %collective-permute-start.2 = (bf16[144,640]{1,0:T(8,128)(2,1)}, bf16[144,640]{1,0:T(8,128)(2,1)S(1)}, u32[]{:S(2)}, u32[]{:S(2)}) collective-permute-start(bf16[144,640]{1,0:T(8,128)(2,1)} %get-tuple-element.56), channel_id=1, source_target_pairs={{0,4},{1,5},{2,6},{3,7},{4,0},{5,1},{6,2},{7,3},{8,12},{9,13},{10,... | collective-permute-start | bytes 552968 | tf_op jit(solution)/shard_map/ppermute | solution.py:47
  15.8 18.6 %collective-permute-start.3 = (bf16[144,640]{1,0:T(8,128)(2,1)S(1)}, bf16[144,640]{1,0:T(8,128)(2,1)S(1)}, u32[]{:S(2)}, u32[]{:S(2)}) collective-permute-start(bf16[144,640]{1,0:T(8,128)(2,1)S(1)} %get-tuple-element.57), channel_id=1, source_target_pairs={{0,6},{1,7},{2,4},{3,5},{4,2},{5,3},{6,0},{7,1},{8,14},{9,15},{10,... | collective-permute-start | bytes 552968 | tf_op jit(solution)/shard_map/ppermute | solution.py:47
  18.2 16.2 %collective-permute-start.1 = (bf16[144,640]{1,0:T(8,128)(2,1)S(1)}, bf16[144,640]{1,0:T(8,128)(2,1)S(1)}, u32[]{:S(2)}, u32[]{:S(2)}) collective-permute-start(bf16[144,640]{1,0:T(8,128)(2,1)S(1)} %get-tuple-element.55.sent_ref), channel_id=1, source_target_pairs={{0,2},{1,3},{2,0},{3,1},{4,6},{5,7},{6,4},{7,5},{8,10},{9,11},{10,... | collective-permute-start | bytes 552968 | tf_op jit(solution)/shard_map/ppermute | solution.py:47
  34.4 38.5 %copy-start = (bf16[256,4096]{1,0:T(8,128)(2,1)S(1)}, bf16[256,4096]{1,0:T(8,128)(2,1)}, u32[]{:S(2)}) copy-start(bf16[256,4096]{1,0:T(8,128)(2,1)} %features_hbm.3) | copy-start | bytes 6291460
  34.6 37.5 %copy-start.5 = (bf16[64,640]{1,0:T(8,128)(2,1)}, bf16[64,640]{1,0:T(8,128)(2,1)S(1)}, u32[]{:S(2)}) copy-start(bf16[64,640]{1,0:T(8,128)(2,1)S(1)} %get-tuple-element.63.refs_0_) | copy-start | bytes 245764
  39.7 9.5 %collective-permute-start.7 = (bf16[64,640]{1,0:T(8,128)(2,1)S(1)}, bf16[64,640]{1,0:T(8,128)(2,1)S(1)}, u32[]{:S(2)}, u32[]{:S(2)}) collective-permute-start(bf16[64,640]{1,0:T(8,128)(2,1)S(1)} %get-tuple-element.64), channel_id=1, source_target_pairs={{0,16},{1,17},{2,18},{3,19},{4,20},{5,21},{6,22},{7,23},{8,24},{9,... | collective-permute-start | bytes 245768 | tf_op jit(solution)/shard_map/ppermute | solution.py:47
  39.8 9.5 %collective-permute-start.8 = (bf16[64,640]{1,0:T(8,128)(2,1)S(1)}, bf16[64,640]{1,0:T(8,128)(2,1)S(1)}, u32[]{:S(2)}, u32[]{:S(2)}) collective-permute-start(bf16[64,640]{1,0:T(8,128)(2,1)S(1)} %get-tuple-element.65), channel_id=1, source_target_pairs={{0,24},{1,25},{2,26},{3,27},{4,28},{5,29},{6,30},{7,31},{8,16},{9,... | collective-permute-start | bytes 245768 | tf_op jit(solution)/shard_map/ppermute | solution.py:47
  43.2 6.5 %collective-permute-start.6 = (bf16[64,640]{1,0:T(8,128)(2,1)S(1)}, bf16[64,640]{1,0:T(8,128)(2,1)S(1)}, u32[]{:S(2)}, u32[]{:S(2)}) collective-permute-start(bf16[64,640]{1,0:T(8,128)(2,1)S(1)} %get-tuple-element.63.refs_0_), channel_id=1, source_target_pairs={{0,8},{1,9},{2,10},{3,11},{4,12},{5,13},{6,14},{7,15},{8,0},{9,1},... | collective-permute-start | bytes 245768 | tf_op jit(solution)/shard_map/ppermute | solution.py:47
  43.8 14.5 %collective-permute-start.12 = (bf16[1,272,1024]{2,1,0:T(8,128)(2,1)}, bf16[1,272,1024]{2,1,0:T(8,128)(2,1)S(1)}, u32[]{:S(2)}, u32[]{:S(2)}) collective-permute-start(bf16[1,272,1024]{2,1,0:T(8,128)(2,1)} %collective-permute-done.4.refs_4_), channel_id=1, source_target_pairs={{0,4},{1,5},{2,6},{3,7},{4,0},{5,1},{6,2},{7,3},{8,12},{9,13},{10,... | collective-permute-start | bytes 1671176 | tf_op jit(solution)/shard_map/ppermute | solution.py:47
  49.8 5.9 %collective-permute-start.11 = (bf16[32,640]{1,0:T(8,128)(2,1)S(1)}, bf16[32,640]{1,0:T(8,128)(2,1)S(1)}, u32[]{:S(2)}, u32[]{:S(2)}) collective-permute-start(bf16[32,640]{1,0:T(8,128)(2,1)S(1)} %add_convert_fusion), channel_id=1, source_target_pairs={{0,24},{1,25},{2,26},{3,27},{4,28},{5,29},{6,30},{7,31},{8,16},{9,... | collective-permute-start | bytes 122888 | tf_op jit(solution)/shard_map/ppermute | solution.py:47
  52.1 5.0 %collective-permute-start.10 = (bf16[32,640]{1,0:T(8,128)(2,1)S(1)}, bf16[32,640]{1,0:T(8,128)(2,1)S(1)}, u32[]{:S(2)}, u32[]{:S(2)}) collective-permute-start(bf16[32,640]{1,0:T(8,128)(2,1)S(1)} %add_convert_fusion), channel_id=1, source_target_pairs={{0,16},{1,17},{2,18},{3,19},{4,20},{5,21},{6,22},{7,23},{8,24},{9,... | collective-permute-start | bytes 122888 | tf_op jit(solution)/shard_map/ppermute | solution.py:47
  52.4 4.8 %collective-permute-start.9 = (bf16[32,640]{1,0:T(8,128)(2,1)S(1)}, bf16[32,640]{1,0:T(8,128)(2,1)S(1)}, u32[]{:S(2)}, u32[]{:S(2)}) collective-permute-start(bf16[32,640]{1,0:T(8,128)(2,1)S(1)} %add_convert_fusion), channel_id=1, source_target_pairs={{0,8},{1,9},{2,10},{3,11},{4,12},{5,13},{6,14},{7,15},{8,0},{9,1},... | collective-permute-start | bytes 122888 | tf_op jit(solution)/shard_map/ppermute | solution.py:47
  57.2 14.1 %collective-permute-start.16 = (bf16[1,272,1024]{2,1,0:T(8,128)(2,1)}, bf16[1,272,1024]{2,1,0:T(8,128)(2,1)S(1)}, u32[]{:S(2)}, u32[]{:S(2)}) collective-permute-start(bf16[1,272,1024]{2,1,0:T(8,128)(2,1)} %collective-permute-done.4.refs_4_), channel_id=1, source_target_pairs={{0,8},{1,9},{2,10},{3,11},{4,12},{5,13},{6,14},{7,15},{8,0},{9,1},... | collective-permute-start | bytes 1671176 | tf_op jit(solution)/shard_map/ppermute | solution.py:47
  58.3 7.1 %collective-permute-start.15 = (bf16[128,640]{1,0:T(8,128)(2,1)S(1)}, bf16[128,640]{1,0:T(8,128)(2,1)S(1)}, u32[]{:S(2)}, u32[]{:S(2)}) collective-permute-start(bf16[128,640]{1,0:T(8,128)(2,1)S(1)} %pad_maximum_fusion.1), channel_id=1, source_target_pairs={{0,6},{1,7},{2,4},{3,5},{4,2},{5,3},{6,0},{7,1},{8,14},{9,15},{10,... | collective-permute-start | bytes 491528 | tf_op jit(solution)/shard_map/ppermute | solution.py:47
  59.8 7.4 %collective-permute-start.14 = (bf16[128,640]{1,0:T(8,128)(2,1)S(1)}, bf16[128,640]{1,0:T(8,128)(2,1)S(1)}, u32[]{:S(2)}, u32[]{:S(2)}) collective-permute-start(bf16[128,640]{1,0:T(8,128)(2,1)S(1)} %pad_maximum_fusion.1), channel_id=1, source_target_pairs={{0,4},{1,5},{2,6},{3,7},{4,0},{5,1},{6,2},{7,3},{8,12},{9,13},{10,... | collective-permute-start | bytes 491528 | tf_op jit(solution)/shard_map/ppermute | solution.py:47
  61.3 5.9 %collective-permute-start.13 = (bf16[128,640]{1,0:T(8,128)(2,1)S(1)}, bf16[128,640]{1,0:T(8,128)(2,1)S(1)}, u32[]{:S(2)}, u32[]{:S(2)}) collective-permute-start(bf16[128,640]{1,0:T(8,128)(2,1)S(1)} %pad_maximum_fusion.1), channel_id=1, source_target_pairs={{0,2},{1,3},{2,0},{3,1},{4,6},{5,7},{6,4},{7,5},{8,10},{9,11},{10,... | collective-permute-start | bytes 491528 | tf_op jit(solution)/shard_map/ppermute | solution.py:47
  71.3 0.8 copy-start.3
  72.1 2.8 %collective-permute-start.17 = (bf16[16,32,640]{2,1,0:T(8,128)(2,1)S(1)}, bf16[16,32,640]{2,1,0:T(8,128)(2,1)}, u32[]{:S(2)}, u32[]{:S(2)}) collective-permute-start(bf16[16,32,640]{2,1,0:T(8,128)(2,1)S(1)} %bitcast.10), channel_id=1, source_target_pairs={{0,1},{1,0},{2,3},{3,2},{4,5},{5,4},{6,7},{7,6},{8,9},{9,8},{10,11... | collective-permute-start | bytes 1966088 | tf_op jit(solution)/shard_map/ppermute | solution.py:47
  72.1 2.8 %copy-start.6 = (bf16[64,640]{1,0:T(8,128)(2,1)S(1)}, bf16[64,640]{1,0:T(8,128)(2,1)}, u32[]{:S(2)}) copy-start(bf16[64,640]{1,0:T(8,128)(2,1)} %copy-done.5) | copy-start | bytes 245764
  72.1 20.9 %collective-permute-start.18 = (bf16[1,272,1024]{2,1,0:T(8,128)(2,1)}, bf16[1,272,1024]{2,1,0:T(8,128)(2,1)S(1)}, u32[]{:S(2)}, u32[]{:S(2)}) collective-permute-start(bf16[1,272,1024]{2,1,0:T(8,128)(2,1)} %bitcast.6.refs_0_), channel_id=1, source_target_pairs={{0,8},{1,9},{2,10},{3,11},{4,12},{5,13},{6,14},{7,15},{8,0},{9,1},... | collective-permute-start | bytes 1671176 | tf_op jit(solution)/shard_map/ppermute | solution.py:47
  72.4 20.5 %collective-permute-start.19 = (bf16[1,272,1024]{2,1,0:T(8,128)(2,1)}, bf16[1,272,1024]{2,1,0:T(8,128)(2,1)S(1)}, u32[]{:S(2)}, u32[]{:S(2)}) collective-permute-start(bf16[1,272,1024]{2,1,0:T(8,128)(2,1)} %copy-done.3), channel_id=1, source_target_pairs={{0,4},{1,5},{2,6},{3,7},{4,0},{5,1},{6,2},{7,3},{8,12},{9,13},{10,... | collective-permute-start | bytes 1671176 | tf_op jit(solution)/shard_map/ppermute | solution.py:47
  73.3 19.7 %collective-permute-start.20 = (bf16[256,512]{1,0:T(8,128)(2,1)S(1)}, bf16[256,512]{1,0:T(8,128)(2,1)S(1)}, u32[]{:S(2)}, u32[]{:S(2)}) collective-permute-start(bf16[256,512]{1,0:T(8,128)(2,1)S(1)} %get-tuple-element.75), channel_id=1, source_target_pairs={{0,16},{1,17},{2,18},{3,19},{4,20},{5,21},{6,22},{7,23},{8,24},{9,... | collective-permute-start | bytes 786440 | tf_op jit(solution)/shard_map/ppermute | solution.py:47
  74.9 39.4 %copy-start.4 = (bf16[1,272,1024]{2,1,0:T(8,128)(2,1)S(1)}, bf16[1,272,1024]{2,1,0:T(8,128)(2,1)}, u32[]{:S(2)}) copy-start(bf16[1,272,1024]{2,1,0:T(8,128)(2,1)} %copy-done.3) | copy-start | bytes 1671172
  93.0 16.3 %collective-permute-start.21 = (bf16[1,272,1024]{2,1,0:T(8,128)(2,1)S(1)}, bf16[1,272,1024]{2,1,0:T(8,128)(2,1)S(1)}, u32[]{:S(2)}, u32[]{:S(2)}) collective-permute-start(bf16[1,272,1024]{2,1,0:T(8,128)(2,1)S(1)} %collective-permute-done.18.refs_2_), channel_id=1, source_target_pairs={{0,4},{1,5},{2,6},{3,7},{4,0},{5,1},{6,2},{7,3},{8,12},{9,13},{10,... | collective-permute-start | bytes 1671176 | tf_op jit(solution)/shard_map/ppermute | solution.py:47
  93.5 10.1 %collective-permute-start.22 = (bf16[256,512]{1,0:T(8,128)(2,1)S(1)}, bf16[256,512]{1,0:T(8,128)(2,1)S(1)}, u32[]{:S(2)}, u32[]{:S(2)}) collective-permute-start(bf16[256,512]{1,0:T(8,128)(2,1)S(1)} %get-tuple-element.92), channel_id=1, source_target_pairs={{0,8},{1,9},{2,10},{3,11},{4,12},{5,13},{6,14},{7,15},{8,0},{9,1},... | collective-permute-start | bytes 786440 | tf_op jit(solution)/shard_map/ppermute | solution.py:47
  94.7 40.1 %collective-permute-start.23 = (bf16[256,512]{1,0:T(8,128)(2,1)S(1)}, bf16[256,512]{1,0:T(8,128)(2,1)S(1)}, u32[]{:S(2)}, u32[]{:S(2)}) collective-permute-start(bf16[256,512]{1,0:T(8,128)(2,1)S(1)} %get-tuple-element.93), channel_id=1, source_target_pairs={{0,24},{1,25},{2,26},{3,27},{4,28},{5,29},{6,30},{7,31},{8,16},{9,... | collective-permute-start | bytes 786440 | tf_op jit(solution)/shard_map/ppermute | solution.py:47
  96.2 38.6 %collective-permute-start.24 = (bf16[256,512]{1,0:T(8,128)(2,1)S(1)}, bf16[256,512]{1,0:T(8,128)(2,1)S(1)}, u32[]{:S(2)}, u32[]{:S(2)}) collective-permute-start(bf16[256,512]{1,0:T(8,128)(2,1)S(1)} %get-tuple-element.94), channel_id=1, source_target_pairs={{0,20},{1,21},{2,22},{3,23},{4,16},{5,17},{6,18},{7,19},{8,28},{9,... | collective-permute-start | bytes 786440 | tf_op jit(solution)/shard_map/ppermute | solution.py:47
  97.9 36.8 %collective-permute-start.25 = (bf16[256,512]{1,0:T(8,128)(2,1)S(1)}, bf16[256,512]{1,0:T(8,128)(2,1)S(1)}, u32[]{:S(2)}, u32[]{:S(2)}) collective-permute-start(bf16[256,512]{1,0:T(8,128)(2,1)S(1)} %get-tuple-element.95), channel_id=1, source_target_pairs={{0,28},{1,29},{2,30},{3,31},{4,24},{5,25},{6,26},{7,27},{8,20},{9,... | collective-permute-start | bytes 786440 | tf_op jit(solution)/shard_map/ppermute | solution.py:47
  103.6 31.1 %collective-permute-start.26 = (bf16[256,512]{1,0:T(8,128)(2,1)S(1)}, bf16[256,512]{1,0:T(8,128)(2,1)S(1)}, u32[]{:S(2)}, u32[]{:S(2)}) collective-permute-start(bf16[256,512]{1,0:T(8,128)(2,1)S(1)} %get-tuple-element.96), channel_id=1, source_target_pairs={{0,4},{1,5},{2,6},{3,7},{4,0},{5,1},{6,2},{7,3},{8,12},{9,13},{10,... | collective-permute-start | bytes 786440 | tf_op jit(solution)/shard_map/ppermute | solution.py:47
  109.3 25.5 %collective-permute-start.27 = (bf16[256,512]{1,0:T(8,128)(2,1)S(1)}, bf16[256,512]{1,0:T(8,128)(2,1)S(1)}, u32[]{:S(2)}, u32[]{:S(2)}) collective-permute-start(bf16[256,512]{1,0:T(8,128)(2,1)S(1)} %get-tuple-element.97), channel_id=1, source_target_pairs={{0,12},{1,13},{2,14},{3,15},{4,8},{5,9},{6,10},{7,11},{8,4},{9,5},... | collective-permute-start | bytes 786440 | tf_op jit(solution)/shard_map/ppermute | solution.py:47
  136.1 1.9 %collective-permute-start.29 = (bf16[128,1024]{1,0:T(8,128)(2,1)S(1)}, bf16[128,1024]{1,0:T(8,128)(2,1)S(1)}, u32[]{:S(2)}, u32[]{:S(2)}) collective-permute-start(bf16[128,1024]{1,0:T(8,128)(2,1)S(1)} %get-tuple-element.101), channel_id=1, source_target_pairs={{0,1},{1,0},{2,3},{3,2},{4,5},{5,4},{6,7},{7,6},{8,9},{9,8},{10,11... | collective-permute-start | bytes 786440 | tf_op jit(solution)/shard_map/ppermute | solution.py:47
  137.5 2.2 %collective-permute-start.28 = (bf16[128,1024]{1,0:T(8,128)(2,1)S(1)}, bf16[128,1024]{1,0:T(8,128)(2,1)S(1)}, u32[]{:S(2)}, u32[]{:S(2)}) collective-permute-start(bf16[128,1024]{1,0:T(8,128)(2,1)S(1)} %get-tuple-element.99), channel_id=1, source_target_pairs={{0,1},{1,0},{2,3},{3,2},{4,5},{5,4},{6,7},{7,6},{8,9},{9,8},{10,11... | collective-permute-start | bytes 786440 | tf_op jit(solution)/shard_map/ppermute | solution.py:47
  138.1 8.3 %collective-permute-start.30 = (bf16[128,1024]{1,0:T(8,128)(2,1)S(1)}, bf16[128,1024]{1,0:T(8,128)(2,1)S(1)}, u32[]{:S(2)}, u32[]{:S(2)}) collective-permute-start(bf16[128,1024]{1,0:T(8,128)(2,1)S(1)} %join.1), channel_id=1, source_target_pairs={{0,2},{1,3},{2,0},{3,1},{4,6},{5,7},{6,4},{7,5},{8,10},{9,11},{10,... | collective-permute-start | bytes 786440 | tf_op jit(solution)/shard_map/ppermute | solution.py:47

commit v12 on v9

--- a/solution.py
+++ b/solution.py
@@ -632,11 +632,11 @@
         keep, sends, seen = stage(own, keep, sent, arrived, seen, count, embed)
         if direct and stages:
             group_scalar = group.reshape(1)
-            *sends, block_far, block_near, group_scalar = lax.optimization_barrier(
-                (*sends, block_far, block_near, group_scalar)
+            *sends, block_near, block_far, group_scalar = lax.optimization_barrier(
+                (*sends, block_near, block_far, group_scalar)
             )
             slices = cut(group_scalar, features, groups)
-            pair_x = xor_permute(jnp.concatenate([block_far, block_near]), by_x)
+            far_x = xor_permute(block_far, by_x)
         arrived = [xor_permute(piece, (r + 1) << low) for r, piece in enumerate(sends)]
         sent = sends[0]
         stages.append((low, count))
@@ -659,16 +659,16 @@
         if direct and number == 1:
             part, block_far = lax.optimization_barrier((part, block_far))
             block_far_near = xor_permute(block_far, by_near)
-            part, pair_x = lax.optimization_barrier((part, pair_x))
+            part, far_x = lax.optimization_barrier((part, far_x))
         part = jnp.concatenate(
             [part] + [xor_permute(part, r << low) for r in range(1, count)], axis=0
         )
     part = part.reshape(-1, size, part.shape[1])
     if direct:
         part, block_far_near = lax.optimization_barrier((part, block_far_near))
-        far_near_x = xor_permute(block_far_near, by_x)
-        blocks = [block, block_x, block_near, block_far, pair_x, block_far_near, far_near_x]
-        order = [0, 1, 2, 4, 5, 3, 6, 7]
+        pair_x = xor_permute(jnp.concatenate([block_near, block_far_near]), by_x)
+        blocks = [block, block_x, block_near, block_far, far_x, block_far_near, pair_x]
+        order = [0, 1, 2, 4, 5, 6, 3, 7]
     else:
         order = slice_order = list(range(groups))
         blocks = [

time: 141 us -> 144 us (1.021)
  the two profiles are of different devices: /device:TPU:0 before, /device:TPU:14 now
where the time goes in v12:
time: 144 us
  waiting for transfers between devices  57.9 us (40%)
  Pallas kernels  43.9 us (30%)
  starting transfers between devices  35.2 us (24%)
  local copies, waits for them, and re-layouts  4.69 us (3%)
    ppermute x30, waiting for transfers between devices, xor_permute(): return lax.ppermute(piece, AXES, [(i, i ^ mask) for i in range(devices)])  57.9 us
    ppermute x30, starting transfers between devices, xor_permute(): return lax.ppermute(piece, AXES, [(i, i ^ mask) for i in range(devices)])  35.2 us
    pallas_call x1, Pallas kernels, contrast(): pl.pallas_call(functools.partial(contrast_kernel, order), in_specs=[smem(...  20.8 us
    pallas_call x1, Pallas kernels, whiten(): pl.pallas_call(make_whiten_kernel(rows, count), in_specs=[smem()] + [vmem...  10.8 us
    pallas_call x1, Pallas kernels, project(): pl.pallas_call(project_kernel, in_specs=[smem(), smem(), hbm, hbm, hbm],...  6.8 us
    unnamed x22, local copies, waits for them, and re-layouts  4.69 us
  transfers between devices with their start and end apart: 30, of which 17 were waited for; matrix products, arithmetic and copies ran while one was open for 1% of the time, Pallas kernels for 24%

profile of v12, /device:TPU:14, one launch (start us, length us, event | category | flops | bytes accessed | tf_op | source)
XLA Modules:
  0.0 143.7 jit_solution(16532099434637888533)
XLA Ops:
  0.6 0.7 copy-done.5
  1.3 0.7 copy-done.6
  2.0 6.8 %project.1 = (bf16[272,1024]{1,0:T(8,128)(2,1)}, bf16[528,640]{1,0:T(8,128)(2,1)S(1)}, f32[512,640]{1,0:T(8,128)S(1)}) custom-call(s32[1]{0:T(128)} %bitcast.4.me_ref, s32[1,4]{1,0:T(1,128)S(1)} %copy-done.6, bf16[256,4096]{1,0:T(8,128)(2,1)} %features_hbm.3, bf16[4096,1024]{1,0:T(8,128)(2,1)} %weight_hbm.1, s32[4,256]{1,0:T(4,128)S(1)} %bitcast.12), custom_call_target="tpu_custom_call" | custom-call | flops 2147483648 | bytes 8388608 | tf_op jit(solution)/shard_map/project/pallas_call | solution.py:186
  8.8 0.1 collective-permute-start
  8.9 0.6 collective-permute-start.1
  9.5 2.6 %collective-permute-start.6 = (bf16[1,272,1024]{2,1,0:T(8,128)(2,1)}, bf16[1,272,1024]{2,1,0:T(8,128)(2,1)}, u32[]{:S(2)}, u32[]{:S(2)}) collective-permute-start(bf16[1,272,1024]{2,1,0:T(8,128)(2,1)} %bitcast.6.refs_0_), channel_id=1, source_target_pairs={{0,16},{1,17},{2,18},{3,19},{4,20},{5,21},{6,22},{7,23},{8,24},{9,... | collective-permute-start | bytes 1671176 | tf_op jit(solution)/shard_map/ppermute | solution.py:47
  12.1 0.4 collective-permute-start.5
  12.5 11.7 %collective-permute-done.1.refs_1_ = bf16[1,272,1024]{2,1,0:T(8,128)(2,1)} collective-permute-done((bf16[1,272,1024]{2,1,0:T(8,128)(2,1)}, bf16[1,272,1024]{2,1,0:T(8,128)(2,1)}, u32[]{:S(2)}, u32[]{:S(2)}) %collective-permute-start.1) | collective-permute-done | bytes 557088 | tf_op jit(solution)/shard_map/ppermute | solution.py:47
  24.2 0.9 stage.2
  25.1 0.7 copy-done.3
  25.8 0.5 collective-permute-start.3
  26.3 1.4 collective-permute-start.4
  27.8 1.5 %collective-permute-start.2 = (bf16[144,640]{1,0:T(8,128)(2,1)S(1)}, bf16[144,640]{1,0:T(8,128)(2,1)S(1)}, u32[]{:S(2)}, u32[]{:S(2)}) collective-permute-start(bf16[144,640]{1,0:T(8,128)(2,1)S(1)} %get-tuple-element.57.sent_ref), channel_id=1, source_target_pairs={{0,2},{1,3},{2,0},{3,1},{4,6},{5,7},{6,4},{7,5},{8,10},{9,11},{10,... | collective-permute-start | bytes 552968 | tf_op jit(solution)/shard_map/ppermute | solution.py:47
  29.3 4.3 %collective-permute-done.3.refs_1_ = bf16[144,640]{1,0:T(8,128)(2,1)S(1)} collective-permute-done((bf16[144,640]{1,0:T(8,128)(2,1)}, bf16[144,640]{1,0:T(8,128)(2,1)S(1)}, u32[]{:S(2)}, u32[]{:S(2)}) %collective-permute-start.3) | collective-permute-done | bytes 184352 | tf_op jit(solution)/shard_map/ppermute | solution.py:47
  33.6 2.7 %collective-permute-done.4.refs_2_ = bf16[144,640]{1,0:T(8,128)(2,1)S(1)} collective-permute-done((bf16[144,640]{1,0:T(8,128)(2,1)}, bf16[144,640]{1,0:T(8,128)(2,1)S(1)}, u32[]{:S(2)}, u32[]{:S(2)}) %collective-permute-start.4) | collective-permute-done | bytes 184352 | tf_op jit(solution)/shard_map/ppermute | solution.py:47
  36.2 1.2 collective-permute-done.2.refs_0_
  37.4 1.0 copy-done.4
  38.3 0.1 stage.3
  38.5 0.0 copy-start.9
  38.5 2.7 %collective-permute-start.8 = (bf16[64,640]{1,0:T(8,128)(2,1)S(1)}, bf16[64,640]{1,0:T(8,128)(2,1)S(1)}, u32[]{:S(2)}, u32[]{:S(2)}) collective-permute-start(bf16[64,640]{1,0:T(8,128)(2,1)S(1)} %get-tuple-element.65), channel_id=1, source_target_pairs={{0,16},{1,17},{2,18},{3,19},{4,20},{5,21},{6,22},{7,23},{8,24},{9,... | collective-permute-start | bytes 245768 | tf_op jit(solution)/shard_map/ppermute | solution.py:47
  41.1 1.8 %collective-permute-start.7 = (bf16[64,640]{1,0:T(8,128)(2,1)S(1)}, bf16[64,640]{1,0:T(8,128)(2,1)S(1)}, u32[]{:S(2)}, u32[]{:S(2)}) collective-permute-start(bf16[64,640]{1,0:T(8,128)(2,1)S(1)} %get-tuple-element.64.refs_0_), channel_id=1, source_target_pairs={{0,8},{1,9},{2,10},{3,11},{4,12},{5,13},{6,14},{7,15},{8,0},{9,1},... | collective-permute-start | bytes 245768 | tf_op jit(solution)/shard_map/ppermute | solution.py:47
  42.9 0.5 collective-permute-start.13
  43.5 1.7 %collective-permute-done.8.refs_2_ = bf16[64,640]{1,0:T(8,128)(2,1)S(1)} collective-permute-done((bf16[64,640]{1,0:T(8,128)(2,1)S(1)}, bf16[64,640]{1,0:T(8,128)(2,1)S(1)}, u32[]{:S(2)}, u32[]{:S(2)}) %collective-permute-start.8) | collective-permute-done | bytes 81952 | tf_op jit(solution)/shard_map/ppermute | solution.py:47
  45.2 1.9 %collective-permute-done.9.refs_3_ = bf16[64,640]{1,0:T(8,128)(2,1)S(1)} collective-permute-done((bf16[64,640]{1,0:T(8,128)(2,1)S(1)}, bf16[64,640]{1,0:T(8,128)(2,1)S(1)}, u32[]{:S(2)}, u32[]{:S(2)}) %collective-permute-start.9) | collective-permute-done | bytes 81952 | tf_op jit(solution)/shard_map/ppermute | solution.py:47
  47.1 1.6 %collective-permute-start.12 = (bf16[32,640]{1,0:T(8,128)(2,1)S(1)}, bf16[32,640]{1,0:T(8,128)(2,1)S(1)}, u32[]{:S(2)}, u32[]{:S(2)}) collective-permute-start(bf16[32,640]{1,0:T(8,128)(2,1)S(1)} %add_convert_fusion), channel_id=1, source_target_pairs={{0,24},{1,25},{2,26},{3,27},{4,28},{5,29},{6,30},{7,31},{8,16},{9,... | collective-permute-start | bytes 122888 | tf_op jit(solution)/shard_map/ppermute | solution.py:47
  48.7 2.2 %collective-permute-start.11 = (bf16[32,640]{1,0:T(8,128)(2,1)S(1)}, bf16[32,640]{1,0:T(8,128)(2,1)S(1)}, u32[]{:S(2)}, u32[]{:S(2)}) collective-permute-start(bf16[32,640]{1,0:T(8,128)(2,1)S(1)} %add_convert_fusion), channel_id=1, source_target_pairs={{0,16},{1,17},{2,18},{3,19},{4,20},{5,21},{6,22},{7,23},{8,24},{9,... | collective-permute-start | bytes 122888 | tf_op jit(solution)/shard_map/ppermute | solution.py:47
  50.8 0.0 collective-permute-start.10
  50.9 0.6 collective-permute-done.12
  51.4 2.1 %collective-permute-done.11 = bf16[32,640]{1,0:T(8,128)(2,1)S(1)} collective-permute-done((bf16[32,640]{1,0:T(8,128)(2,1)S(1)}, bf16[32,640]{1,0:T(8,128)(2,1)S(1)}, u32[]{:S(2)}, u32[]{:S(2)}) %collective-permute-start.11) | collective-permute-done | bytes 40992 | tf_op jit(solution)/shard_map/ppermute | solution.py:47
  53.6 1.7 %collective-permute-done.10 = bf16[32,640]{1,0:T(8,128)(2,1)S(1)} collective-permute-done((bf16[32,640]{1,0:T(8,128)(2,1)S(1)}, bf16[32,640]{1,0:T(8,128)(2,1)S(1)}, u32[]{:S(2)}, u32[]{:S(2)}) %collective-permute-start.10) | collective-permute-done | bytes 40992 | tf_op jit(solution)/shard_map/ppermute | solution.py:47
  55.3 0.7 collective-permute-start.17
  56.0 0.8 copy-done.7
  56.8 1.5 %collective-permute-start.16 = (bf16[128,640]{1,0:T(8,128)(2,1)S(1)}, bf16[128,640]{1,0:T(8,128)(2,1)S(1)}, u32[]{:S(2)}, u32[]{:S(2)}) collective-permute-start(bf16[128,640]{1,0:T(8,128)(2,1)S(1)} %pad_maximum_fusion.2), channel_id=1, source_target_pairs={{0,6},{1,7},{2,4},{3,5},{4,2},{5,3},{6,0},{7,1},{8,14},{9,15},{10,... | collective-permute-start | bytes 491528 | tf_op jit(solution)/shard_map/ppermute | solution.py:47
  58.3 1.4 collective-permute-start.15
  59.7 0.6 collective-permute-start.14
  60.3 2.7 %collective-permute-done.16 = bf16[128,640]{1,0:T(8,128)(2,1)S(1)} collective-permute-done((bf16[128,640]{1,0:T(8,128)(2,1)S(1)}, bf16[128,640]{1,0:T(8,128)(2,1)S(1)}, u32[]{:S(2)}, u32[]{:S(2)}) %collective-permute-start.16) | collective-permute-done | bytes 163872 | tf_op jit(solution)/shard_map/ppermute | solution.py:47
  63.0 1.7 %collective-permute-done.15 = bf16[128,640]{1,0:T(8,128)(2,1)S(1)} collective-permute-done((bf16[128,640]{1,0:T(8,128)(2,1)S(1)}, bf16[128,640]{1,0:T(8,128)(2,1)S(1)}, u32[]{:S(2)}, u32[]{:S(2)}) %collective-permute-start.15) | collective-permute-done | bytes 163872 | tf_op jit(solution)/shard_map/ppermute | solution.py:47
  64.8 0.3 collective-permute-done.14
  65.0 0.1 pad_maximum_fusion.1
  65.1 1.0 collective-permute-done.17.refs_5_
  66.1 1.1 pad_maximum_fusion
  67.2 0.8 copy-done.1
  68.0 1.5 %collective-permute-start.19 = (bf16[2,272,1024]{2,1,0:T(8,128)(2,1)}, bf16[2,272,1024]{2,1,0:T(8,128)(2,1)}, u32[]{:S(2)}, u32[]{:S(2)}) collective-permute-start(bf16[2,272,1024]{2,1,0:T(8,128)(2,1)} %pad_maximum_fusion), channel_id=1, source_target_pairs={{0,4},{1,5},{2,6},{3,7},{4,0},{5,1},{6,2},{7,3},{8,12},{9,13},{10,... | collective-permute-start | bytes 3342344 | tf_op jit(solution)/shard_map/ppermute | solution.py:47
  69.5 0.3 cut.1
  69.8 1.3 collective-permute-start.20
  71.2 1.9 %collective-permute-start.21 = (bf16[256,512]{1,0:T(8,128)(2,1)S(1)}, bf16[256,512]{1,0:T(8,128)(2,1)S(1)}, u32[]{:S(2)}, u32[]{:S(2)}) collective-permute-start(bf16[256,512]{1,0:T(8,128)(2,1)S(1)} %get-tuple-element.92), channel_id=1, source_target_pairs={{0,16},{1,17},{2,18},{3,19},{4,20},{5,21},{6,22},{7,23},{8,24},{9,... | collective-permute-start | bytes 786440 | tf_op jit(solution)/shard_map/ppermute | solution.py:47
  73.1 0.3 collective-permute-start.22
  73.4 0.5 collective-permute-start.23
  73.9 10.8 %whiten.1 = (bf16[1024,1024]{1,0:T(8,128)(2,1)S(1)}, f32[1,1024]{1,0:T(1,128)S(1)}) custom-call(s32[1]{0:T(128)} %bitcast.1.place_ref, bf16[16,32,640]{2,1,0:T(8,128)(2,1)S(1)} %bitcast.11, bf16[16,32,640]{2,1,0:T(8,128)(2,1)} %collective-permute-done.18.far_ref, bf16[64,640]{1,0:T(8,128)(2,1)S(1)} %copy-done.10, ...), custom_call_target="tpu_custom_call" | custom-call | flops 10737418240 | bytes 2097152 | tf_op jit(solution)/shard_map/whiten/pallas_call | solution.py:393
  84.8 3.2 %collective-permute-start.24 = (bf16[256,512]{1,0:T(8,128)(2,1)S(1)}, bf16[256,512]{1,0:T(8,128)(2,1)S(1)}, u32[]{:S(2)}, u32[]{:S(2)}) collective-permute-start(bf16[256,512]{1,0:T(8,128)(2,1)S(1)} %get-tuple-element.95), channel_id=1, source_target_pairs={{0,12},{1,13},{2,14},{3,15},{4,8},{5,9},{6,10},{7,11},{8,4},{9,5},... | collective-permute-start | bytes 786440 | tf_op jit(solution)/shard_map/ppermute | solution.py:47
  87.9 3.1 %collective-permute-done.21.refs_2_ = bf16[256,512]{1,0:T(8,128)(2,1)S(1)} collective-permute-done((bf16[256,512]{1,0:T(8,128)(2,1)S(1)}, bf16[256,512]{1,0:T(8,128)(2,1)S(1)}, u32[]{:S(2)}, u32[]{:S(2)}) %collective-permute-start.21) | collective-permute-done | bytes 262176 | tf_op jit(solution)/shard_map/ppermute | solution.py:47
  91.1 2.9 %collective-permute-start.25 = (bf16[256,512]{1,0:T(8,128)(2,1)S(1)}, bf16[256,512]{1,0:T(8,128)(2,1)S(1)}, u32[]{:S(2)}, u32[]{:S(2)}) collective-permute-start(bf16[256,512]{1,0:T(8,128)(2,1)S(1)} %get-tuple-element.96), channel_id=1, source_target_pairs={{0,20},{1,21},{2,22},{3,23},{4,16},{5,17},{6,18},{7,19},{8,28},{9,... | collective-permute-start | bytes 786440 | tf_op jit(solution)/shard_map/ppermute | solution.py:47
  93.9 13.0 %collective-permute-done.19.refs_6_ = bf16[2,272,1024]{2,1,0:T(8,128)(2,1)} collective-permute-done((bf16[2,272,1024]{2,1,0:T(8,128)(2,1)}, bf16[2,272,1024]{2,1,0:T(8,128)(2,1)}, u32[]{:S(2)}, u32[]{:S(2)}) %collective-permute-start.19) | collective-permute-done | bytes 1114144 | tf_op jit(solution)/shard_map/ppermute | solution.py:47
  106.9 2.7 %collective-permute-start.26 = (bf16[256,512]{1,0:T(8,128)(2,1)S(1)}, bf16[256,512]{1,0:T(8,128)(2,1)S(1)}, u32[]{:S(2)}, u32[]{:S(2)}) collective-permute-start(bf16[256,512]{1,0:T(8,128)(2,1)S(1)} %get-tuple-element.97), channel_id=1, source_target_pairs={{0,28},{1,29},{2,30},{3,31},{4,24},{5,25},{6,26},{7,27},{8,20},{9,... | collective-permute-start | bytes 786440 | tf_op jit(solution)/shard_map/ppermute | solution.py:47
  109.6 20.8 %contrast.1 = (f32[1,256]{1,0:T(1,128)}, bf16[8,256,1024]{2,1,0:T(8,128)(2,1)S(1)}) custom-call(s32[1]{0:T(128)} %bitcast.group_ref, f32[1,1024]{1,0:T(1,128)S(1)} %get-tuple-element.82.mean_ref, bf16[1024,1024]{1,0:T(8,128)(2,1)S(1)} %get-tuple-element.83.whitener_ref.refs_3_, bf16[1,272,1024]{2,1,0:T(8,128)(2,1)} %bitcast.6.refs_0_, ...), custom_call_target="tpu_custom_call" | custom-call | flops 12884901888 | bytes 8388608 | tf_op jit(solution)/shard_map/contrast/pallas_call | solution.py:485
  130.5 1.3 weight_pieces.3
  131.8 0.1 collective-permute-start.28
  131.9 1.3 weight_pieces.2
  133.2 0.5 collective-permute-start.27
  133.8 0.1 join.1
  133.8 0.1 collective-permute-start.29
  133.9 1.0 collective-permute-done.27.refs_1_
  134.9 7.2 %collective-permute-done.29.refs_2_ = bf16[128,1024]{1,0:T(8,128)(2,1)S(1)} collective-permute-done((bf16[128,1024]{1,0:T(8,128)(2,1)S(1)}, bf16[128,1024]{1,0:T(8,128)(2,1)S(1)}, u32[]{:S(2)}, u32[]{:S(2)}) %collective-permute-start.29) | collective-permute-done | bytes 262176 | tf_op jit(solution)/shard_map/ppermute | solution.py:47
  142.1 1.5 %finish.1 = f32[128,1024]{1,0:T(8,128)} custom-call(f32[128,1024]{1,0:T(8,128)S(1)} %get-tuple-element.98.refs_0_, bf16[128,1024]{1,0:T(8,128)(2,1)S(1)} %collective-permute-done.27.refs_1_, bf16[128,1024]{1,0:T(8,128)(2,1)S(1)} %collective-permute-done.29.refs_2_, bf16[1024,1024]{1,0:T(8,128)(2,1)S(1)} %get-tuple-element.83.whitener_ref.refs_3_), custom_call_target="tpu_custom_call" | custom-call | tf_op jit(solution)/shard_map/finish/pallas_call | solution.py:581
  (32 shorter events, 0.1 us)
Async XLA Ops:
  0.6 0.7 copy-start.5
  1.3 0.7 copy-start.6
  8.8 15.4 %collective-permute-start = (bf16[528,640]{1,0:T(8,128)(2,1)S(1)}, bf16[528,640]{1,0:T(8,128)(2,1)S(1)}, u32[]{:S(2)}, u32[]{:S(2)}) collective-permute-start(bf16[528,640]{1,0:T(8,128)(2,1)S(1)} %get-tuple-element.53.sent_ref), channel_id=1, source_target_pairs={{0,1},{1,0},{2,3},{3,2},{4,5},{5,4},{6,7},{7,6},{8,9},{9,8},{10,11... | collective-permute-start | bytes 2027528 | tf_op jit(solution)/shard_map/ppermute | solution.py:47
  8.9 15.4 %collective-permute-start.1 = (bf16[1,272,1024]{2,1,0:T(8,128)(2,1)}, bf16[1,272,1024]{2,1,0:T(8,128)(2,1)}, u32[]{:S(2)}, u32[]{:S(2)}) collective-permute-start(bf16[1,272,1024]{2,1,0:T(8,128)(2,1)} %bitcast.6.refs_0_), channel_id=1, source_target_pairs={{0,4},{1,5},{2,6},{3,7},{4,0},{5,1},{6,2},{7,3},{8,12},{9,13},{10,... | collective-permute-start | bytes 1671176 | tf_op jit(solution)/shard_map/ppermute | solution.py:47
  9.5 29.0 %collective-permute-start.6 = (bf16[1,272,1024]{2,1,0:T(8,128)(2,1)}, bf16[1,272,1024]{2,1,0:T(8,128)(2,1)}, u32[]{:S(2)}, u32[]{:S(2)}) collective-permute-start(bf16[1,272,1024]{2,1,0:T(8,128)(2,1)} %bitcast.6.refs_0_), channel_id=1, source_target_pairs={{0,16},{1,17},{2,18},{3,19},{4,20},{5,21},{6,22},{7,23},{8,24},{9,... | collective-permute-start | bytes 1671176 | tf_op jit(solution)/shard_map/ppermute | solution.py:47
  12.1 26.4 %collective-permute-start.5 = (bf16[1,272,1024]{2,1,0:T(8,128)(2,1)}, bf16[1,272,1024]{2,1,0:T(8,128)(2,1)S(1)}, u32[]{:S(2)}, u32[]{:S(2)}) collective-permute-start(bf16[1,272,1024]{2,1,0:T(8,128)(2,1)} %bitcast.6.refs_0_), channel_id=1, source_target_pairs={{0,8},{1,9},{2,10},{3,11},{4,12},{5,13},{6,14},{7,15},{8,0},{9,1},... | collective-permute-start | bytes 1671176 | tf_op jit(solution)/shard_map/ppermute | solution.py:47
  25.1 0.7 copy-start.3
  25.8 7.8 %collective-permute-start.3 = (bf16[144,640]{1,0:T(8,128)(2,1)}, bf16[144,640]{1,0:T(8,128)(2,1)S(1)}, u32[]{:S(2)}, u32[]{:S(2)}) collective-permute-start(bf16[144,640]{1,0:T(8,128)(2,1)} %get-tuple-element.58), channel_id=1, source_target_pairs={{0,4},{1,5},{2,6},{3,7},{4,0},{5,1},{6,2},{7,3},{8,12},{9,13},{10,... | collective-permute-start | bytes 552968 | tf_op jit(solution)/shard_map/ppermute | solution.py:47
  26.3 9.9 %collective-permute-start.4 = (bf16[144,640]{1,0:T(8,128)(2,1)}, bf16[144,640]{1,0:T(8,128)(2,1)S(1)}, u32[]{:S(2)}, u32[]{:S(2)}) collective-permute-start(bf16[144,640]{1,0:T(8,128)(2,1)} %get-tuple-element.59), channel_id=1, source_target_pairs={{0,6},{1,7},{2,4},{3,5},{4,2},{5,3},{6,0},{7,1},{8,14},{9,15},{10,... | collective-permute-start | bytes 552968 | tf_op jit(solution)/shard_map/ppermute | solution.py:47
  27.8 9.6 %collective-permute-start.2 = (bf16[144,640]{1,0:T(8,128)(2,1)S(1)}, bf16[144,640]{1,0:T(8,128)(2,1)S(1)}, u32[]{:S(2)}, u32[]{:S(2)}) collective-permute-start(bf16[144,640]{1,0:T(8,128)(2,1)S(1)} %get-tuple-element.57.sent_ref), channel_id=1, source_target_pairs={{0,2},{1,3},{2,0},{3,1},{4,6},{5,7},{6,4},{7,5},{8,10},{9,11},{10,... | collective-permute-start | bytes 552968 | tf_op jit(solution)/shard_map/ppermute | solution.py:47
  37.4 1.0 copy-start.4
  38.5 27.7 %copy-start.9 = (bf16[64,640]{1,0:T(8,128)(2,1)}, bf16[64,640]{1,0:T(8,128)(2,1)S(1)}, u32[]{:S(2)}) copy-start(bf16[64,640]{1,0:T(8,128)(2,1)S(1)} %get-tuple-element.64.refs_0_) | copy-start | bytes 245764
  38.5 6.7 %collective-permute-start.8 = (bf16[64,640]{1,0:T(8,128)(2,1)S(1)}, bf16[64,640]{1,0:T(8,128)(2,1)S(1)}, u32[]{:S(2)}, u32[]{:S(2)}) collective-permute-start(bf16[64,640]{1,0:T(8,128)(2,1)S(1)} %get-tuple-element.65), channel_id=1, source_target_pairs={{0,16},{1,17},{2,18},{3,19},{4,20},{5,21},{6,22},{7,23},{8,24},{9,... | collective-permute-start | bytes 245768 | tf_op jit(solution)/shard_map/ppermute | solution.py:47
  41.1 5.9 %collective-permute-start.9 = (bf16[64,640]{1,0:T(8,128)(2,1)S(1)}, bf16[64,640]{1,0:T(8,128)(2,1)S(1)}, u32[]{:S(2)}, u32[]{:S(2)}) collective-permute-start(bf16[64,640]{1,0:T(8,128)(2,1)S(1)} %get-tuple-element.66), channel_id=1, source_target_pairs={{0,24},{1,25},{2,26},{3,27},{4,28},{5,29},{6,30},{7,31},{8,16},{9,... | collective-permute-start | bytes 245768 | tf_op jit(solution)/shard_map/ppermute | solution.py:47
  41.1 5.9 %collective-permute-start.7 = (bf16[64,640]{1,0:T(8,128)(2,1)S(1)}, bf16[64,640]{1,0:T(8,128)(2,1)S(1)}, u32[]{:S(2)}, u32[]{:S(2)}) collective-permute-start(bf16[64,640]{1,0:T(8,128)(2,1)S(1)} %get-tuple-element.64.refs_0_), channel_id=1, source_target_pairs={{0,8},{1,9},{2,10},{3,11},{4,12},{5,13},{6,14},{7,15},{8,0},{9,1},... | collective-permute-start | bytes 245768 | tf_op jit(solution)/shard_map/ppermute | solution.py:47
  42.9 13.0 %collective-permute-start.13 = (bf16[1,272,1024]{2,1,0:T(8,128)(2,1)}, bf16[1,272,1024]{2,1,0:T(8,128)(2,1)S(1)}, u32[]{:S(2)}, u32[]{:S(2)}) collective-permute-start(bf16[1,272,1024]{2,1,0:T(8,128)(2,1)} %collective-permute-done.6.refs_3_), channel_id=1, source_target_pairs={{0,4},{1,5},{2,6},{3,7},{4,0},{5,1},{6,2},{7,3},{8,12},{9,13},{10,... | collective-permute-start | bytes 1671176 | tf_op jit(solution)/shard_map/ppermute | solution.py:47
  47.1 4.3 %collective-permute-start.12 = (bf16[32,640]{1,0:T(8,128)(2,1)S(1)}, bf16[32,640]{1,0:T(8,128)(2,1)S(1)}, u32[]{:S(2)}, u32[]{:S(2)}) collective-permute-start(bf16[32,640]{1,0:T(8,128)(2,1)S(1)} %add_convert_fusion), channel_id=1, source_target_pairs={{0,24},{1,25},{2,26},{3,27},{4,28},{5,29},{6,30},{7,31},{8,16},{9,... | collective-permute-start | bytes 122888 | tf_op jit(solution)/shard_map/ppermute | solution.py:47
  48.7 4.9 %collective-permute-start.11 = (bf16[32,640]{1,0:T(8,128)(2,1)S(1)}, bf16[32,640]{1,0:T(8,128)(2,1)S(1)}, u32[]{:S(2)}, u32[]{:S(2)}) collective-permute-start(bf16[32,640]{1,0:T(8,128)(2,1)S(1)} %add_convert_fusion), channel_id=1, source_target_pairs={{0,16},{1,17},{2,18},{3,19},{4,20},{5,21},{6,22},{7,23},{8,24},{9,... | collective-permute-start | bytes 122888 | tf_op jit(solution)/shard_map/ppermute | solution.py:47
  50.8 4.4 %collective-permute-start.10 = (bf16[32,640]{1,0:T(8,128)(2,1)S(1)}, bf16[32,640]{1,0:T(8,128)(2,1)S(1)}, u32[]{:S(2)}, u32[]{:S(2)}) collective-permute-start(bf16[32,640]{1,0:T(8,128)(2,1)S(1)} %add_convert_fusion), channel_id=1, source_target_pairs={{0,8},{1,9},{2,10},{3,11},{4,12},{5,13},{6,14},{7,15},{8,0},{9,1},... | collective-permute-start | bytes 122888 | tf_op jit(solution)/shard_map/ppermute | solution.py:47
  55.3 10.9 %collective-permute-start.17 = (bf16[1,272,1024]{2,1,0:T(8,128)(2,1)}, bf16[1,272,1024]{2,1,0:T(8,128)(2,1)S(1)}, u32[]{:S(2)}, u32[]{:S(2)}) collective-permute-start(bf16[1,272,1024]{2,1,0:T(8,128)(2,1)} %collective-permute-done.6.refs_3_), channel_id=1, source_target_pairs={{0,8},{1,9},{2,10},{3,11},{4,12},{5,13},{6,14},{7,15},{8,0},{9,1},... | collective-permute-start | bytes 1671176 | tf_op jit(solution)/shard_map/ppermute | solution.py:47
  56.0 0.8 copy-start.7
  56.8 6.2 %collective-permute-start.16 = (bf16[128,640]{1,0:T(8,128)(2,1)S(1)}, bf16[128,640]{1,0:T(8,128)(2,1)S(1)}, u32[]{:S(2)}, u32[]{:S(2)}) collective-permute-start(bf16[128,640]{1,0:T(8,128)(2,1)S(1)} %pad_maximum_fusion.2), channel_id=1, source_target_pairs={{0,6},{1,7},{2,4},{3,5},{4,2},{5,3},{6,0},{7,1},{8,14},{9,15},{10,... | collective-permute-start | bytes 491528 | tf_op jit(solution)/shard_map/ppermute | solution.py:47
  58.3 6.5 %collective-permute-start.15 = (bf16[128,640]{1,0:T(8,128)(2,1)S(1)}, bf16[128,640]{1,0:T(8,128)(2,1)S(1)}, u32[]{:S(2)}, u32[]{:S(2)}) collective-permute-start(bf16[128,640]{1,0:T(8,128)(2,1)S(1)} %pad_maximum_fusion.2), channel_id=1, source_target_pairs={{0,4},{1,5},{2,6},{3,7},{4,0},{5,1},{6,2},{7,3},{8,12},{9,13},{10,... | collective-permute-start | bytes 491528 | tf_op jit(solution)/shard_map/ppermute | solution.py:47
  59.7 5.3 %collective-permute-start.14 = (bf16[128,640]{1,0:T(8,128)(2,1)S(1)}, bf16[128,640]{1,0:T(8,128)(2,1)S(1)}, u32[]{:S(2)}, u32[]{:S(2)}) collective-permute-start(bf16[128,640]{1,0:T(8,128)(2,1)S(1)} %pad_maximum_fusion.2), channel_id=1, source_target_pairs={{0,2},{1,3},{2,0},{3,1},{4,6},{5,7},{6,4},{7,5},{8,10},{9,11},{10,... | collective-permute-start | bytes 491528 | tf_op jit(solution)/shard_map/ppermute | solution.py:47
  65.1 4.5 %copy-start = (bf16[256,4096]{1,0:T(8,128)(2,1)S(1)}, bf16[256,4096]{1,0:T(8,128)(2,1)}, u32[]{:S(2)}) copy-start(bf16[256,4096]{1,0:T(8,128)(2,1)} %features_hbm.3) | copy-start | bytes 6291460
  66.1 3.7 %collective-permute-start.18 = (bf16[16,32,640]{2,1,0:T(8,128)(2,1)S(1)}, bf16[16,32,640]{2,1,0:T(8,128)(2,1)}, u32[]{:S(2)}, u32[]{:S(2)}) collective-permute-start(bf16[16,32,640]{2,1,0:T(8,128)(2,1)S(1)} %bitcast.10), channel_id=1, source_target_pairs={{0,1},{1,0},{2,3},{3,2},{4,5},{5,4},{6,7},{7,6},{8,9},{9,8},{10,11... | collective-permute-start | bytes 1966088 | tf_op jit(solution)/shard_map/ppermute | solution.py:47
  67.2 0.8 copy-start.1
  68.0 38.9 %collective-permute-start.19 = (bf16[2,272,1024]{2,1,0:T(8,128)(2,1)}, bf16[2,272,1024]{2,1,0:T(8,128)(2,1)}, u32[]{:S(2)}, u32[]{:S(2)}) collective-permute-start(bf16[2,272,1024]{2,1,0:T(8,128)(2,1)} %pad_maximum_fusion), channel_id=1, source_target_pairs={{0,4},{1,5},{2,6},{3,7},{4,0},{5,1},{6,2},{7,3},{8,12},{9,13},{10,... | collective-permute-start | bytes 3342344 | tf_op jit(solution)/shard_map/ppermute | solution.py:47
  69.5 4.4 %copy-start.10 = (bf16[64,640]{1,0:T(8,128)(2,1)S(1)}, bf16[64,640]{1,0:T(8,128)(2,1)}, u32[]{:S(2)}) copy-start(bf16[64,640]{1,0:T(8,128)(2,1)} %copy-done.9) | copy-start | bytes 245764
  69.8 14.9 %collective-permute-start.20 = (bf16[256,512]{1,0:T(8,128)(2,1)S(1)}, bf16[256,512]{1,0:T(8,128)(2,1)S(1)}, u32[]{:S(2)}, u32[]{:S(2)}) collective-permute-start(bf16[256,512]{1,0:T(8,128)(2,1)S(1)} %get-tuple-element.91), channel_id=1, source_target_pairs={{0,8},{1,9},{2,10},{3,11},{4,12},{5,13},{6,14},{7,15},{8,0},{9,1},... | collective-permute-start | bytes 786440 | tf_op jit(solution)/shard_map/ppermute | solution.py:47
  71.2 19.9 %collective-permute-start.21 = (bf16[256,512]{1,0:T(8,128)(2,1)S(1)}, bf16[256,512]{1,0:T(8,128)(2,1)S(1)}, u32[]{:S(2)}, u32[]{:S(2)}) collective-permute-start(bf16[256,512]{1,0:T(8,128)(2,1)S(1)} %get-tuple-element.92), channel_id=1, source_target_pairs={{0,16},{1,17},{2,18},{3,19},{4,20},{5,21},{6,22},{7,23},{8,24},{9,... | collective-permute-start | bytes 786440 | tf_op jit(solution)/shard_map/ppermute | solution.py:47
  73.1 57.4 %collective-permute-start.22 = (bf16[256,512]{1,0:T(8,128)(2,1)S(1)}, bf16[256,512]{1,0:T(8,128)(2,1)S(1)}, u32[]{:S(2)}, u32[]{:S(2)}) collective-permute-start(bf16[256,512]{1,0:T(8,128)(2,1)S(1)} %get-tuple-element.93), channel_id=1, source_target_pairs={{0,24},{1,25},{2,26},{3,27},{4,28},{5,29},{6,30},{7,31},{8,16},{9,... | collective-permute-start | bytes 786440 | tf_op jit(solution)/shard_map/ppermute | solution.py:47
  73.4 57.1 %collective-permute-start.23 = (bf16[256,512]{1,0:T(8,128)(2,1)S(1)}, bf16[256,512]{1,0:T(8,128)(2,1)S(1)}, u32[]{:S(2)}, u32[]{:S(2)}) collective-permute-start(bf16[256,512]{1,0:T(8,128)(2,1)S(1)} %get-tuple-element.94), channel_id=1, source_target_pairs={{0,4},{1,5},{2,6},{3,7},{4,0},{5,1},{6,2},{7,3},{8,12},{9,13},{10,... | collective-permute-start | bytes 786440 | tf_op jit(solution)/shard_map/ppermute | solution.py:47
  73.9 35.7 %copy-start.2 = (bf16[1,272,1024]{2,1,0:T(8,128)(2,1)S(1)}, bf16[1,272,1024]{2,1,0:T(8,128)(2,1)}, u32[]{:S(2)}) copy-start(bf16[1,272,1024]{2,1,0:T(8,128)(2,1)} %copy-done.1) | copy-start | bytes 1671172
  73.9 35.7 %copy-start.8 = (bf16[1,272,1024]{2,1,0:T(8,128)(2,1)S(1)}, bf16[1,272,1024]{2,1,0:T(8,128)(2,1)}, u32[]{:S(2)}) copy-start(bf16[1,272,1024]{2,1,0:T(8,128)(2,1)} %copy-done.7) | copy-start | bytes 1671172
  84.8 45.7 %collective-permute-start.24 = (bf16[256,512]{1,0:T(8,128)(2,1)S(1)}, bf16[256,512]{1,0:T(8,128)(2,1)S(1)}, u32[]{:S(2)}, u32[]{:S(2)}) collective-permute-start(bf16[256,512]{1,0:T(8,128)(2,1)S(1)} %get-tuple-element.95), channel_id=1, source_target_pairs={{0,12},{1,13},{2,14},{3,15},{4,8},{5,9},{6,10},{7,11},{8,4},{9,5},... | collective-permute-start | bytes 786440 | tf_op jit(solution)/shard_map/ppermute | solution.py:47
  91.1 39.4 %collective-permute-start.25 = (bf16[256,512]{1,0:T(8,128)(2,1)S(1)}, bf16[256,512]{1,0:T(8,128)(2,1)S(1)}, u32[]{:S(2)}, u32[]{:S(2)}) collective-permute-start(bf16[256,512]{1,0:T(8,128)(2,1)S(1)} %get-tuple-element.96), channel_id=1, source_target_pairs={{0,20},{1,21},{2,22},{3,23},{4,16},{5,17},{6,18},{7,19},{8,28},{9,... | collective-permute-start | bytes 786440 | tf_op jit(solution)/shard_map/ppermute | solution.py:47
  106.9 23.6 %collective-permute-start.26 = (bf16[256,512]{1,0:T(8,128)(2,1)S(1)}, bf16[256,512]{1,0:T(8,128)(2,1)S(1)}, u32[]{:S(2)}, u32[]{:S(2)}) collective-permute-start(bf16[256,512]{1,0:T(8,128)(2,1)S(1)} %get-tuple-element.97), channel_id=1, source_target_pairs={{0,28},{1,29},{2,30},{3,31},{4,24},{5,25},{6,26},{7,27},{8,20},{9,... | collective-permute-start | bytes 786440 | tf_op jit(solution)/shard_map/ppermute | solution.py:47
  131.8 1.9 %collective-permute-start.28 = (bf16[128,1024]{1,0:T(8,128)(2,1)S(1)}, bf16[128,1024]{1,0:T(8,128)(2,1)S(1)}, u32[]{:S(2)}, u32[]{:S(2)}) collective-permute-start(bf16[128,1024]{1,0:T(8,128)(2,1)S(1)} %get-tuple-element.101), channel_id=1, source_target_pairs={{0,1},{1,0},{2,3},{3,2},{4,5},{5,4},{6,7},{7,6},{8,9},{9,8},{10,11... | collective-permute-start | bytes 786440 | tf_op jit(solution)/shard_map/ppermute | solution.py:47
  133.2 1.7 %collective-permute-start.27 = (bf16[128,1024]{1,0:T(8,128)(2,1)S(1)}, bf16[128,1024]{1,0:T(8,128)(2,1)S(1)}, u32[]{:S(2)}, u32[]{:S(2)}) collective-permute-start(bf16[128,1024]{1,0:T(8,128)(2,1)S(1)} %get-tuple-element.99), channel_id=1, source_target_pairs={{0,1},{1,0},{2,3},{3,2},{4,5},{5,4},{6,7},{7,6},{8,9},{9,8},{10,11... | collective-permute-start | bytes 786440 | tf_op jit(solution)/shard_map/ppermute | solution.py:47
  133.8 8.3 %collective-permute-start.29 = (bf16[128,1024]{1,0:T(8,128)(2,1)S(1)}, bf16[128,1024]{1,0:T(8,128)(2,1)S(1)}, u32[]{:S(2)}, u32[]{:S(2)}) collective-permute-start(bf16[128,1024]{1,0:T(8,128)(2,1)S(1)} %join.1), channel_id=1, source_target_pairs={{0,2},{1,3},{2,0},{3,1},{4,6},{5,7},{6,4},{7,5},{8,10},{9,11},{10,... | collective-permute-start | bytes 786440 | tf_op jit(solution)/shard_map/ppermute | solution.py:47

commit v13 on v9

--- a/solution.py
+++ b/solution.py
@@ -52,12 +52,12 @@
     return high, (value - high.astype(F32)).astype(BF16)
 
 
-def cut_kernel(group_ref, features_hbm, *refs):
+def cut_kernel(ids_ref, features_hbm, *refs):
     outs, sems = refs[:-1], refs[-1]
     columns = outs[0].shape[1]
     copies = []
     for k, out in enumerate(outs):
-        start = pl.multiple_of((group_ref[0] ^ k) * columns, columns)
+        start = pl.multiple_of((ids_ref[0] ^ k) * columns, columns)
         copies.append(
             pltpu.make_async_copy(features_hbm.at[:, pl.ds(start, columns)], out, sems.at[k])
         )
@@ -66,7 +66,7 @@
         copy.wait()
 
 
-def cut(group, features, groups):
+def cut(ids, features, groups):
     rows, depth = features.shape
     return pl.pallas_call(
         cut_kernel,
@@ -76,7 +76,7 @@
         scratch_shapes=[pltpu.SemaphoreType.DMA((groups,))],
         compiler_params=params(8),
         name="cut",
-    )(group, features)
+    )(ids, features)
 
 
 def pack_sums(sums, packed, rows):
@@ -100,7 +100,7 @@
 
 
 def project_kernel(
-    me_ref,
+    ids_ref,
     offsets_ref,
     features_hbm,
     weight_hbm,
@@ -163,7 +163,7 @@
     wide[:, embed:] = projected[:, : packed - LANES]
     ones = jnp.ones((rows, LANES), BF16)
     means[...] = jnp.broadcast_to(sums * (1.0 / rows), means.shape)
-    core = me_ref[0] & 1
+    core = ids_ref[2] & 1
     for side, out in ((1, send_ref), (0, keep_ref)):
         for r in range(blocks // 2):
             block = (core ^ side) * (blocks // 2) + r
@@ -178,7 +178,7 @@
                 out[r * LANES : (r + 1) * LANES, at] = value.astype(out.dtype)
 
 
-def project(me, offsets, features, weight, ortholog):
+def project(ids, offsets, features, weight, ortholog):
     rows, depth = features.shape
     embed = weight.shape[1]
     packed = embed // 2 + LANES
@@ -205,15 +205,15 @@
             flops=2 * rows * depth * embed, bytes_accessed=2 * depth * embed, transcendentals=0
         ),
         name="project",
-    )(me, offsets, features, weight, ortholog)
-
-
-def make_stage_kernel(seen, arrivals, count, embed):
-    def kernel(own_ref, keep_ref, sent_ref, *refs):
+    )(ids, offsets, features, weight, ortholog)
+
+
+def make_stage_kernel(seen, arrivals, low, count, embed):
+    def kernel(ids_ref, keep_ref, sent_ref, *refs):
         arrived, next_keep, outs = refs[:arrivals], refs[arrivals], refs[arrivals + 1 :]
         full, packed = keep_ref.shape
         share = full // count
-        own = own_ref[0]
+        own = (ids_ref[2] >> low) & (count - 1)
         sums = [unpack_sums(ref[full:, :], seen, embed) for ref in (sent_ref, *arrived)]
         block = pack_sums(jnp.concatenate(sums, axis=0), packed, outs[0].shape[0] - share)
         for r in range(count):
@@ -230,13 +230,13 @@
     return kernel
 
 
-def stage(own, keep, sent, arrived, seen, count, embed):
+def stage(ids, keep, sent, arrived, seen, low, count, embed):
     full, packed = keep.shape
     share = full // count
     held = seen * (1 + len(arrived))
     tail = -(-4 * held // TAIL) * TAIL
     out = pl.pallas_call(
-        make_stage_kernel(seen, len(arrived), count, embed),
+        make_stage_kernel(seen, len(arrived), low, count, embed),
         in_specs=[smem()] + [vmem()] * (2 + len(arrived)),
         out_specs=[vmem()] * count,
         out_shape=[jax.ShapeDtypeStruct((share, packed), F32)]
@@ -246,20 +246,23 @@
             flops=full * packed, bytes_accessed=4 * full * packed, transcendentals=0
         ),
         name="stage",
-    )(own.reshape(1), keep, sent, *arrived)
+    )(ids, keep, sent, *arrived)
     return out[0], out[1:], held
 
 
-def make_whiten_kernel(rows, count):
+def make_whiten_kernel(rows, count, stages):
     def kernel(
-        place_ref,
+        ids_ref,
         near_ref,
         far_ref,
         *refs,
     ):
         sums_refs = refs[:-7]
         whitener_ref, mean_ref, scaled, rest, first, left, right = refs[-7:]
-        place = place_ref[0]
+        me = ids_ref[2]
+        place = me & 1
+        for low, size in stages:
+            place = place * size + ((me >> low) & (size - 1))
         embed = scaled.shape[0]
         blocks = embed // LANES
         half = blocks // 2
@@ -388,10 +391,10 @@
     return kernel
 
 
-def whiten(place, near, far, sums, count, rows, embed):
+def whiten(ids, near, far, sums, count, stages, rows, embed):
     square = (embed, embed)
     return pl.pallas_call(
-        make_whiten_kernel(rows, count),
+        make_whiten_kernel(rows, count, stages),
         in_specs=[smem()] + [vmem()] * (2 + len(sums)),
         out_specs=[vmem(), vmem()],
         out_shape=[
@@ -404,16 +407,16 @@
             flops=5 * 2 * embed**3, bytes_accessed=2 * embed**2, transcendentals=0
         ),
         name="whiten",
-    )(place, near, far, *sums)
-
-
-def contrast_kernel(order, group_ref, mean_ref, whitener_ref, *refs):
+    )(ids, near, far, *sums)
+
+
+def contrast_kernel(order, ids_ref, mean_ref, whitener_ref, *refs):
     loss_ref, grad_ref, white, tables, numbers, offsets_ref, sem = refs[-11:-4]
     even, odd = (refs[-4], refs[-3]), (refs[-2], refs[-1])
     block_refs = [ref.at[i] for ref in refs[:-11] for i in range(ref.shape[0])]
     block_refs = [block_refs[order.index(k)] for k in range(len(order))]
     groups, rows, embed = white.shape
-    group = group_ref[0]
+    group = ids_ref[0]
 
     for k in range(0, groups, 2):
         pair = block_refs[k : k + 2]
@@ -478,7 +481,7 @@
             loss_ref[...] = jnp.where(group % 2 == 0, first, second)
 
 
-def contrast(group, blocks, order, mean, whitener):
+def contrast(ids, blocks, order, mean, whitener):
     groups = len(order)
     rows, embed = blocks[0].shape[1:]
     rows -= TAIL
@@ -505,37 +508,37 @@
             transcendentals=groups * PARTNERS * rows * rows,
         ),
         name="contrast",
-    )(group, mean, whitener, *blocks)
-
-
-def pieces_kernel(share, masks, order, group_ref, window_ref, grad_ref, *refs):
+    )(ids, mean, whitener, *blocks)
+
+
+def pieces_kernel(share, masks, order, ids_ref, grad_ref, *refs):
     groups = grad_ref.shape[0]
     features, (keep_ref, send_ref, total) = refs[:groups], refs[groups:]
 
     def columns(at):
         value = None
         for k, feature_ref in zip(order, features):
-            term = dot(feature_ref[:, at], grad_ref[group_ref[0] ^ k], (0, 0))
+            term = dot(feature_ref[:, at], grad_ref[ids_ref[0] ^ k], (0, 0))
             value = term if value is None else value + term
         return value
 
     if share % LANES:
         total[...] = columns(slice(None))
     for n, mask in enumerate(masks):
-        at = pl.ds(pl.multiple_of((window_ref[0] ^ mask) * share, share), share)
+        at = pl.ds(pl.multiple_of((ids_ref[1] ^ mask) * share, share), share)
         value = total[at, :] if share % LANES else columns(at)
         out, n = (send_ref, n - len(masks) // 2) if n >= len(masks) // 2 else (keep_ref, n)
         out[n * share : (n + 1) * share, :] = value.astype(out.dtype)
 
 
-def weight_pieces(group, window, grad, slices, order, shares, masks):
+def weight_pieces(ids, grad, slices, order, shares, masks):
     groups, rows, embed = grad.shape
     columns = slices[0].shape[1]
     share = columns // shares
     half = len(masks) // 2 * share
     return pl.pallas_call(
         functools.partial(pieces_kernel, share, masks, order),
-        in_specs=[smem(), smem()] + [vmem()] * (1 + len(slices)),
+        in_specs=[smem()] + [vmem()] * (1 + len(slices)),
         out_specs=[vmem()] * 2,
         out_shape=[
             jax.ShapeDtypeStruct((half, embed), F32),
@@ -549,7 +552,7 @@
             transcendentals=0,
         ),
         name="weight_pieces",
-    )(group, window, grad, *slices)
+    )(ids, grad, *slices)
 
 
 def join_kernel(keep_ref, arrived_ref, out_ref):
@@ -597,6 +600,7 @@
     group = lax.axis_index("sp").astype(jnp.int32)
     window = lax.axis_index("win").astype(jnp.int32)
     me = group * shares + window
+    ids = jnp.stack([group, window, me])
 
     direct = groups == 8
     by_x, by_near, by_far = shares, 2 * shares, 4 * shares
@@ -608,7 +612,7 @@
         ]
 
     block, send, keep = project(
-        me.reshape(1), partner_offsets, features, proj_weight, ortholog_index.T
+        ids, partner_offsets, features, proj_weight, ortholog_index.T
     )
     block = block[None]
     if direct:
@@ -625,22 +629,17 @@
     seen = 1
     stages = []
     low = 1
-    place = me & 1
     while keep.shape[0] > 32:
         count = 4
-        own = (me >> low) & (count - 1)
-        keep, sends, seen = stage(own, keep, sent, arrived, seen, count, embed)
+        keep, sends, seen = stage(ids, keep, sent, arrived, seen, low, count, embed)
         if direct and stages:
-            group_scalar = group.reshape(1)
-            *sends, block_far, block_near, group_scalar = lax.optimization_barrier(
-                (*sends, block_far, block_near, group_scalar)
+            *sends, block_near, block_far = lax.optimization_barrier(
+                (*sends, block_near, block_far)
             )
-            slices = cut(group_scalar, features, groups)
             pair_x = xor_permute(jnp.concatenate([block_far, block_near]), by_x)
         arrived = [xor_permute(piece, (r + 1) << low) for r, piece in enumerate(sends)]
         sent = sends[0]
         stages.append((low, count))
-        place = place * count + own
         low += 2
     size = keep.shape[0]
     part = keep
@@ -665,7 +664,8 @@
         )
     part = part.reshape(-1, size, part.shape[1])
     if direct:
-        part, block_far_near = lax.optimization_barrier((part, block_far_near))
+        part, block_far_near, ids = lax.optimization_barrier((part, block_far_near, ids))
+        slices = cut(ids, features, groups)
         far_near_x = xor_permute(block_far_near, by_x)
         blocks = [block, block_x, block_near, block_far, pair_x, block_far_near, far_near_x]
         order = [0, 1, 2, 4, 5, 3, 6, 7]
@@ -677,16 +677,15 @@
     other = xor_permute(part, 1)
     if direct:
         other, *slices = lax.optimization_barrier((other, *slices))
-        slice_order = [0, 2, 4, 6, 1, 3, 5, 7]
+        slice_order = [0, 4, 2, 6, 1, 3, 5, 7]
         slices = [xor_permute(slices[k], k * shares) if k else slices[k] for k in slice_order]
 
-    whitener, mean = whiten(place.reshape(1), part, other, sums, seen, rows, embed)
-    loss, grad = contrast(group.reshape(1), blocks, order, mean, whitener)
-    group, window = group.reshape(1), window.reshape(1)
+    whitener, mean = whiten(ids, part, other, sums, seen, tuple(stages), rows, embed)
+    loss, grad = contrast(ids, blocks, order, mean, whitener)
     pieces = []
     for mask in reversed(range(0, shares, 2)):
         keep, send = weight_pieces(
-            group, window, grad, slices, slice_order, shares, (mask, mask + 1)
+            ids, grad, slices, slice_order, shares, (mask, mask + 1)
         )
         arrived = xor_permute(send, 1)
         if mask:

time: 141 us -> 137 us (0.972)
  local copies, waits for them, and re-layouts: 5.65 us -> 1.35 us
    unnamed x22 -> x6, local copies, waits for them, and re-layouts: 5.65 us -> 1.35 us
  transfers between devices with their start and end apart: 30 -> 30, of which waited for: 17 -> 16; matrix products, arithmetic and copies ran while one was open for 0% -> 0% of each run, Pallas kernels for 24% -> 25%
where the time goes in v13:
time: 137 us; the launch traced here: 136 us
  waiting for transfers between devices  46 us (34%)
  starting transfers between devices  43.9 us (32%)
  Pallas kernels  43.3 us (32%)
    ppermute x30, waiting for transfers between devices, xor_permute(): return lax.ppermute(piece, AXES, [(i, i ^ mask) for i in range(devices)])  46 us
    ppermute x30, starting transfers between devices, xor_permute(): return lax.ppermute(piece, AXES, [(i, i ^ mask) for i in range(devices)])  43.9 us
    pallas_call x1, Pallas kernels, contrast(): pl.pallas_call(functools.partial(contrast_kernel, order), in_specs=[smem(...  19.6 us
    pallas_call x1, Pallas kernels, whiten(): pl.pallas_call(make_whiten_kernel(rows, count, stages), in_specs=[smem()]...  10.2 us
    pallas_call x1, Pallas kernels, project(): pl.pallas_call(project_kernel, in_specs=[smem(), smem(), hbm, hbm, hbm],...  6.05 us
    pallas_call x2, Pallas kernels, weight_pieces(): pl.pallas_call(functools.partial(pieces_kernel, share, masks, order), in_...  3.68 us
  transfers between devices with their start and end apart: 30, of which 16 were waited for; matrix products, arithmetic and copies ran while one was open for 0% of the time, Pallas kernels for 25%

profile of v13, /device:TPU:0, one launch (start us, length us, event | category | flops | bytes accessed | tf_op | source)
XLA Modules:
  0.0 135.6 jit_solution(16885367921427526794)
XLA Ops:
  0.6 0.1 pad_add_fusion.ids_ref
  0.7 0.7 copy-done.1
  1.4 0.7 copy-done.2
  2.1 6.1 %project.1 = (bf16[272,1024]{1,0:T(8,128)(2,1)S(1)}, bf16[528,640]{1,0:T(8,128)(2,1)S(1)}, f32[512,640]{1,0:T(8,128)S(1)}) custom-call(s32[3]{0:T(128)S(1)} %pad_add_fusion.ids_ref, s32[1,4]{1,0:T(1,128)S(1)} %copy-done.2, bf16[256,4096]{1,0:T(8,128)(2,1)} %features_hbm.3, bf16[4096,1024]{1,0:T(8,128)(2,1)} %weight_hbm.1, s32[4,256]{1,0:T(4,128)S(1)} %bitcast.9), custom_call_target="tpu_custom_call" | custom-call | flops 2147483648 | bytes 8388608 | tf_op jit(solution)/shard_map/project/pallas_call | solution.py:186
  8.1 0.5 collective-permute-start
  8.6 2.6 %collective-permute-start.1 = (bf16[1,272,1024]{2,1,0:T(8,128)(2,1)S(1)}, bf16[1,272,1024]{2,1,0:T(8,128)(2,1)S(1)}, u32[]{:S(2)}, u32[]{:S(2)}) collective-permute-start(bf16[1,272,1024]{2,1,0:T(8,128)(2,1)S(1)} %bitcast.10), channel_id=1, source_target_pairs={{0,4},{1,5},{2,6},{3,7},{4,0},{5,1},{6,2},{7,3},{8,12},{9,13},{10,... | collective-permute-start | bytes 1671176 | tf_op jit(solution)/shard_map/ppermute | solution.py:47
  11.2 2.6 %collective-permute-start.6 = (bf16[1,272,1024]{2,1,0:T(8,128)(2,1)S(1)}, bf16[1,272,1024]{2,1,0:T(8,128)(2,1)S(1)}, u32[]{:S(2)}, u32[]{:S(2)}) collective-permute-start(bf16[1,272,1024]{2,1,0:T(8,128)(2,1)S(1)} %bitcast.11), channel_id=1, source_target_pairs={{0,16},{1,17},{2,18},{3,19},{4,20},{5,21},{6,22},{7,23},{8,24},{9,... | collective-permute-start | bytes 1671176 | tf_op jit(solution)/shard_map/ppermute | solution.py:47
  13.8 1.6 %collective-permute-start.5 = (bf16[1,272,1024]{2,1,0:T(8,128)(2,1)S(1)}, bf16[1,272,1024]{2,1,0:T(8,128)(2,1)S(1)}, u32[]{:S(2)}, u32[]{:S(2)}) collective-permute-start(bf16[1,272,1024]{2,1,0:T(8,128)(2,1)S(1)} %bitcast.12), channel_id=1, source_target_pairs={{0,8},{1,9},{2,10},{3,11},{4,12},{5,13},{6,14},{7,15},{8,0},{9,1},... | collective-permute-start | bytes 1671176 | tf_op jit(solution)/shard_map/ppermute | solution.py:47
  15.4 9.1 %collective-permute-done.1.refs_1_ = bf16[1,272,1024]{2,1,0:T(8,128)(2,1)S(1)} collective-permute-done((bf16[1,272,1024]{2,1,0:T(8,128)(2,1)S(1)}, bf16[1,272,1024]{2,1,0:T(8,128)(2,1)S(1)}, u32[]{:S(2)}, u32[]{:S(2)}) %collective-permute-start.1) | collective-permute-done | bytes 557088 | tf_op jit(solution)/shard_map/ppermute | solution.py:47
  24.4 0.0 collective-permute-done.refs_0_
  24.4 0.7 stage.2
  25.1 1.8 %collective-permute-start.3 = (bf16[144,640]{1,0:T(8,128)(2,1)S(1)}, bf16[144,640]{1,0:T(8,128)(2,1)S(1)}, u32[]{:S(2)}, u32[]{:S(2)}) collective-permute-start(bf16[144,640]{1,0:T(8,128)(2,1)S(1)} %get-tuple-element.58), channel_id=1, source_target_pairs={{0,4},{1,5},{2,6},{3,7},{4,0},{5,1},{6,2},{7,3},{8,12},{9,13},{10,... | collective-permute-start | bytes 552968 | tf_op jit(solution)/shard_map/ppermute | solution.py:47
  26.9 1.5 %collective-permute-start.4 = (bf16[144,640]{1,0:T(8,128)(2,1)S(1)}, bf16[144,640]{1,0:T(8,128)(2,1)S(1)}, u32[]{:S(2)}, u32[]{:S(2)}) collective-permute-start(bf16[144,640]{1,0:T(8,128)(2,1)S(1)} %get-tuple-element.59), channel_id=1, source_target_pairs={{0,6},{1,7},{2,4},{3,5},{4,2},{5,3},{6,0},{7,1},{8,14},{9,15},{10,... | collective-permute-start | bytes 552968 | tf_op jit(solution)/shard_map/ppermute | solution.py:47
  28.4 0.2 collective-permute-start.2
  28.7 4.0 %collective-permute-done.3.refs_1_ = bf16[144,640]{1,0:T(8,128)(2,1)S(1)} collective-permute-done((bf16[144,640]{1,0:T(8,128)(2,1)S(1)}, bf16[144,640]{1,0:T(8,128)(2,1)S(1)}, u32[]{:S(2)}, u32[]{:S(2)}) %collective-permute-start.3) | collective-permute-done | bytes 184352 | tf_op jit(solution)/shard_map/ppermute | solution.py:47
  32.7 4.0 %collective-permute-done.4.refs_2_ = bf16[144,640]{1,0:T(8,128)(2,1)S(1)} collective-permute-done((bf16[144,640]{1,0:T(8,128)(2,1)S(1)}, bf16[144,640]{1,0:T(8,128)(2,1)S(1)}, u32[]{:S(2)}, u32[]{:S(2)}) %collective-permute-start.4) | collective-permute-done | bytes 184352 | tf_op jit(solution)/shard_map/ppermute | solution.py:47
  36.7 1.4 %collective-permute-done.2.refs_0_ = bf16[144,640]{1,0:T(8,128)(2,1)S(1)} collective-permute-done((bf16[144,640]{1,0:T(8,128)(2,1)S(1)}, bf16[144,640]{1,0:T(8,128)(2,1)S(1)}, u32[]{:S(2)}, u32[]{:S(2)}) %collective-permute-start.2) | collective-permute-done | bytes 184352 | tf_op jit(solution)/shard_map/ppermute | solution.py:47
  38.0 0.6 stage.3
  38.7 0.2 collective-permute-done.6.refs_3_
  38.8 0.2 collective-permute-done.5.refs_2_
  39.0 0.1 pad_maximum_fusion
  39.1 1.2 collective-permute-start.13
  40.4 2.6 %collective-permute-start.8 = (bf16[64,640]{1,0:T(8,128)(2,1)S(1)}, bf16[64,640]{1,0:T(8,128)(2,1)S(1)}, u32[]{:S(2)}, u32[]{:S(2)}) collective-permute-start(bf16[64,640]{1,0:T(8,128)(2,1)S(1)} %get-tuple-element.65), channel_id=1, source_target_pairs={{0,16},{1,17},{2,18},{3,19},{4,20},{5,21},{6,22},{7,23},{8,24},{9,... | collective-permute-start | bytes 245768 | tf_op jit(solution)/shard_map/ppermute | solution.py:47
  43.0 1.3 collective-permute-start.9
  44.3 0.2 collective-permute-start.7
  44.5 3.4 %collective-permute-done.8.refs_2_ = bf16[64,640]{1,0:T(8,128)(2,1)S(1)} collective-permute-done((bf16[64,640]{1,0:T(8,128)(2,1)S(1)}, bf16[64,640]{1,0:T(8,128)(2,1)S(1)}, u32[]{:S(2)}, u32[]{:S(2)}) %collective-permute-start.8) | collective-permute-done | bytes 81952 | tf_op jit(solution)/shard_map/ppermute | solution.py:47
  47.9 1.4 %collective-permute-done.9.refs_3_ = bf16[64,640]{1,0:T(8,128)(2,1)S(1)} collective-permute-done((bf16[64,640]{1,0:T(8,128)(2,1)S(1)}, bf16[64,640]{1,0:T(8,128)(2,1)S(1)}, u32[]{:S(2)}, u32[]{:S(2)}) %collective-permute-start.9) | collective-permute-done | bytes 81952 | tf_op jit(solution)/shard_map/ppermute | solution.py:47
  49.4 0.3 collective-permute-done.7.refs_1_
  49.7 2.6 %collective-permute-start.12 = (bf16[32,640]{1,0:T(8,128)(2,1)S(1)}, bf16[32,640]{1,0:T(8,128)(2,1)S(1)}, u32[]{:S(2)}, u32[]{:S(2)}) collective-permute-start(bf16[32,640]{1,0:T(8,128)(2,1)S(1)} %add_convert_fusion), channel_id=1, source_target_pairs={{0,24},{1,25},{2,26},{3,27},{4,28},{5,29},{6,30},{7,31},{8,16},{9,... | collective-permute-start | bytes 122888 | tf_op jit(solution)/shard_map/ppermute | solution.py:47
  52.3 1.9 %collective-permute-start.10 = (bf16[32,640]{1,0:T(8,128)(2,1)S(1)}, bf16[32,640]{1,0:T(8,128)(2,1)S(1)}, u32[]{:S(2)}, u32[]{:S(2)}) collective-permute-start(bf16[32,640]{1,0:T(8,128)(2,1)S(1)} %add_convert_fusion), channel_id=1, source_target_pairs={{0,8},{1,9},{2,10},{3,11},{4,12},{5,13},{6,14},{7,15},{8,0},{9,1},... | collective-permute-start | bytes 122888 | tf_op jit(solution)/shard_map/ppermute | solution.py:47
  54.1 1.4 %collective-permute-done.12 = bf16[32,640]{1,0:T(8,128)(2,1)S(1)} collective-permute-done((bf16[32,640]{1,0:T(8,128)(2,1)S(1)}, bf16[32,640]{1,0:T(8,128)(2,1)S(1)}, u32[]{:S(2)}, u32[]{:S(2)}) %collective-permute-start.12) | collective-permute-done | bytes 40992 | tf_op jit(solution)/shard_map/ppermute | solution.py:47
  55.6 1.7 %collective-permute-done.11 = bf16[32,640]{1,0:T(8,128)(2,1)S(1)} collective-permute-done((bf16[32,640]{1,0:T(8,128)(2,1)S(1)}, bf16[32,640]{1,0:T(8,128)(2,1)S(1)}, u32[]{:S(2)}, u32[]{:S(2)}) %collective-permute-start.11) | collective-permute-done | bytes 40992 | tf_op jit(solution)/shard_map/ppermute | solution.py:47
  57.3 1.3 collective-permute-start.17
  58.6 6.2 %collective-permute-done.13.refs_4_ = bf16[2,272,1024]{2,1,0:T(8,128)(2,1)S(1)} collective-permute-done((bf16[2,272,1024]{2,1,0:T(8,128)(2,1)S(1)}, bf16[2,272,1024]{2,1,0:T(8,128)(2,1)S(1)}, u32[]{:S(2)}, u32[]{:S(2)}) %collective-permute-start.13) | collective-permute-done | bytes 1114144 | tf_op jit(solution)/shard_map/ppermute | solution.py:47
  64.8 1.5 %collective-permute-start.16 = (bf16[128,640]{1,0:T(8,128)(2,1)S(1)}, bf16[128,640]{1,0:T(8,128)(2,1)S(1)}, u32[]{:S(2)}, u32[]{:S(2)}) collective-permute-start(bf16[128,640]{1,0:T(8,128)(2,1)S(1)} %pad_maximum_fusion.2), channel_id=1, source_target_pairs={{0,6},{1,7},{2,4},{3,5},{4,2},{5,3},{6,0},{7,1},{8,14},{9,15},{10,... | collective-permute-start | bytes 491528 | tf_op jit(solution)/shard_map/ppermute | solution.py:47
  66.3 1.5 %collective-permute-start.15 = (bf16[128,640]{1,0:T(8,128)(2,1)S(1)}, bf16[128,640]{1,0:T(8,128)(2,1)S(1)}, u32[]{:S(2)}, u32[]{:S(2)}) collective-permute-start(bf16[128,640]{1,0:T(8,128)(2,1)S(1)} %pad_maximum_fusion.2), channel_id=1, source_target_pairs={{0,4},{1,5},{2,6},{3,7},{4,0},{5,1},{6,2},{7,3},{8,12},{9,13},{10,... | collective-permute-start | bytes 491528 | tf_op jit(solution)/shard_map/ppermute | solution.py:47
  67.8 0.5 collective-permute-start.14
  68.3 3.5 %collective-permute-done.16 = bf16[128,640]{1,0:T(8,128)(2,1)S(1)} collective-permute-done((bf16[128,640]{1,0:T(8,128)(2,1)S(1)}, bf16[128,640]{1,0:T(8,128)(2,1)S(1)}, u32[]{:S(2)}, u32[]{:S(2)}) %collective-permute-start.16) | collective-permute-done | bytes 163872 | tf_op jit(solution)/shard_map/ppermute | solution.py:47
  71.7 1.8 %collective-permute-done.15 = bf16[128,640]{1,0:T(8,128)(2,1)S(1)} collective-permute-done((bf16[128,640]{1,0:T(8,128)(2,1)S(1)}, bf16[128,640]{1,0:T(8,128)(2,1)S(1)}, u32[]{:S(2)}, u32[]{:S(2)}) %collective-permute-start.15) | collective-permute-done | bytes 163872 | tf_op jit(solution)/shard_map/ppermute | solution.py:47
  73.5 0.1 pad_maximum_fusion.1
  73.6 0.1 collective-permute-start.18
  73.7 0.6 collective-permute-start.19
  74.3 0.8 cut.1
  75.1 0.7 collective-permute-done.18.far_ref
  75.8 1.8 %collective-permute-start.20 = (bf16[256,512]{1,0:T(8,128)(2,1)S(1)}, bf16[256,512]{1,0:T(8,128)(2,1)S(1)}, u32[]{:S(2)}, u32[]{:S(2)}) collective-permute-start(bf16[256,512]{1,0:T(8,128)(2,1)S(1)} %get-tuple-element.91), channel_id=1, source_target_pairs={{0,16},{1,17},{2,18},{3,19},{4,20},{5,21},{6,22},{7,23},{8,24},{9,... | collective-permute-start | bytes 786440 | tf_op jit(solution)/shard_map/ppermute | solution.py:47
  77.6 3.9 %collective-permute-start.21 = (bf16[256,512]{1,0:T(8,128)(2,1)S(1)}, bf16[256,512]{1,0:T(8,128)(2,1)S(1)}, u32[]{:S(2)}, u32[]{:S(2)}) collective-permute-start(bf16[256,512]{1,0:T(8,128)(2,1)S(1)} %get-tuple-element.92), channel_id=1, source_target_pairs={{0,8},{1,9},{2,10},{3,11},{4,12},{5,13},{6,14},{7,15},{8,0},{9,1},... | collective-permute-start | bytes 786440 | tf_op jit(solution)/shard_map/ppermute | solution.py:47
  81.5 0.0 collective-permute-start.22
  81.5 0.9 collective-permute-start.23
  82.4 10.2 %whiten.1 = (bf16[1024,1024]{1,0:T(8,128)(2,1)S(1)}, f32[1,1024]{1,0:T(1,128)S(1)}) custom-call(s32[3]{0:T(128)S(1)} %pad_add_fusion.ids_ref, bf16[16,32,640]{2,1,0:T(8,128)(2,1)S(1)} %bitcast.8, bf16[16,32,640]{2,1,0:T(8,128)(2,1)S(1)} %collective-permute-done.18.far_ref, bf16[64,640]{1,0:T(8,128)(2,1)S(1)} %get-tuple-element.64.refs_0_, ...), custom_call_target="tpu_custom_call" | custom-call | flops 10737418240 | bytes 2097152 | tf_op jit(solution)/shard_map/whiten/pallas_call | solution.py:396
  92.6 0.0 collective-permute-done.19.refs_6_
  92.6 1.2 collective-permute-start.24
  93.8 0.0 collective-permute-done.20.refs_1_
  93.8 4.2 %collective-permute-start.25 = (bf16[256,512]{1,0:T(8,128)(2,1)S(1)}, bf16[256,512]{1,0:T(8,128)(2,1)S(1)}, u32[]{:S(2)}, u32[]{:S(2)}) collective-permute-start(bf16[256,512]{1,0:T(8,128)(2,1)S(1)} %get-tuple-element.96), channel_id=1, source_target_pairs={{0,20},{1,21},{2,22},{3,23},{4,16},{5,17},{6,18},{7,19},{8,28},{9,... | collective-permute-start | bytes 786440 | tf_op jit(solution)/shard_map/ppermute | solution.py:47
  98.0 0.0 collective-permute-done.21.refs_2_
  98.0 3.8 %collective-permute-start.26 = (bf16[256,512]{1,0:T(8,128)(2,1)S(1)}, bf16[256,512]{1,0:T(8,128)(2,1)S(1)}, u32[]{:S(2)}, u32[]{:S(2)}) collective-permute-start(bf16[256,512]{1,0:T(8,128)(2,1)S(1)} %get-tuple-element.97), channel_id=1, source_target_pairs={{0,28},{1,29},{2,30},{3,31},{4,24},{5,25},{6,26},{7,27},{8,20},{9,... | collective-permute-start | bytes 786440 | tf_op jit(solution)/shard_map/ppermute | solution.py:47
  101.7 19.6 %contrast.1 = (f32[1,256]{1,0:T(1,128)}, bf16[8,256,1024]{2,1,0:T(8,128)(2,1)S(1)}) custom-call(s32[3]{0:T(128)S(1)} %pad_add_fusion.ids_ref, f32[1,1024]{1,0:T(1,128)S(1)} %get-tuple-element.83.mean_ref, bf16[1024,1024]{1,0:T(8,128)(2,1)S(1)} %get-tuple-element.84.whitener_ref.refs_3_, bf16[1,272,1024]{2,1,0:T(8,128)(2,1)S(1)} %bitcast.13, ...), custom_call_target="tpu_custom_call" | custom-call | flops 12884901888 | bytes 8388608 | tf_op jit(solution)/shard_map/contrast/pallas_call | solution.py:488
  121.3 0.0 collective-permute-done.24.refs_5_
  121.4 1.9 %weight_pieces.3 = (f32[128,1024]{1,0:T(8,128)S(1)}, bf16[128,1024]{1,0:T(8,128)(2,1)S(1)}) custom-call(s32[3]{0:T(128)S(1)} %pad_add_fusion.ids_ref, bf16[8,256,1024]{2,1,0:T(8,128)(2,1)S(1)} %get-tuple-element.89.grad_ref, bf16[256,512]{1,0:T(8,128)(2,1)S(1)} %get-tuple-element.90.refs_0_, bf16[256,512]{1,0:T(8,128)(2,1)S(1)} %collective-permute-done.20.refs_1_, ...), custom_call_target="tpu_custom_call" | custom-call | flops 1073741824 | bytes 6291456 | tf_op jit(solution)/shard_map/weight_pieces/pallas_call | solution.py:539
  123.2 0.1 collective-permute-start.28
  123.3 1.8 %weight_pieces.2 = (f32[128,1024]{1,0:T(8,128)S(1)}, bf16[128,1024]{1,0:T(8,128)(2,1)S(1)}) custom-call(s32[3]{0:T(128)S(1)} %pad_add_fusion.ids_ref, bf16[8,256,1024]{2,1,0:T(8,128)(2,1)S(1)} %get-tuple-element.89.grad_ref, bf16[256,512]{1,0:T(8,128)(2,1)S(1)} %get-tuple-element.90.refs_0_, bf16[256,512]{1,0:T(8,128)(2,1)S(1)} %collective-permute-done.20.refs_1_, ...), custom_call_target="tpu_custom_call" | custom-call | flops 1073741824 | bytes 6291456 | tf_op jit(solution)/shard_map/weight_pieces/pallas_call | solution.py:539
  125.1 0.6 collective-permute-start.27
  125.7 1.5 %collective-permute-start.29 = (bf16[128,1024]{1,0:T(8,128)(2,1)S(1)}, bf16[128,1024]{1,0:T(8,128)(2,1)S(1)}, u32[]{:S(2)}, u32[]{:S(2)}) collective-permute-start(bf16[128,1024]{1,0:T(8,128)(2,1)S(1)} %join.1), channel_id=1, source_target_pairs={{0,2},{1,3},{2,0},{3,1},{4,6},{5,7},{6,4},{7,5},{8,10},{9,11},{10,... | collective-permute-start | bytes 786440 | tf_op jit(solution)/shard_map/ppermute | solution.py:47
  127.3 6.8 %collective-permute-done.29.refs_2_ = bf16[128,1024]{1,0:T(8,128)(2,1)S(1)} collective-permute-done((bf16[128,1024]{1,0:T(8,128)(2,1)S(1)}, bf16[128,1024]{1,0:T(8,128)(2,1)S(1)}, u32[]{:S(2)}, u32[]{:S(2)}) %collective-permute-start.29) | collective-permute-done | bytes 262176 | tf_op jit(solution)/shard_map/ppermute | solution.py:47
  134.1 1.6 %finish.1 = f32[128,1024]{1,0:T(8,128)} custom-call(f32[128,1024]{1,0:T(8,128)S(1)} %get-tuple-element.98.refs_0_, bf16[128,1024]{1,0:T(8,128)(2,1)S(1)} %collective-permute-done.27.refs_1_, bf16[128,1024]{1,0:T(8,128)(2,1)S(1)} %collective-permute-done.29.refs_2_, bf16[1024,1024]{1,0:T(8,128)(2,1)S(1)} %get-tuple-element.84.whitener_ref.refs_3_), custom_call_target="tpu_custom_call" | custom-call | tf_op jit(solution)/shard_map/finish/pallas_call | solution.py:584
  (17 shorter events, 0.1 us)
Async XLA Ops:
  0.7 0.7 copy-start.1
  1.4 0.7 copy-start.2
  8.1 16.3 %collective-permute-start = (bf16[528,640]{1,0:T(8,128)(2,1)S(1)}, bf16[528,640]{1,0:T(8,128)(2,1)S(1)}, u32[]{:S(2)}, u32[]{:S(2)}) collective-permute-start(bf16[528,640]{1,0:T(8,128)(2,1)S(1)} %get-tuple-element.53.sent_ref), channel_id=1, source_target_pairs={{0,1},{1,0},{2,3},{3,2},{4,5},{5,4},{6,7},{7,6},{8,9},{9,8},{10,11... | collective-permute-start | bytes 2027528 | tf_op jit(solution)/shard_map/ppermute | solution.py:47
  8.6 15.8 %collective-permute-start.1 = (bf16[1,272,1024]{2,1,0:T(8,128)(2,1)S(1)}, bf16[1,272,1024]{2,1,0:T(8,128)(2,1)S(1)}, u32[]{:S(2)}, u32[]{:S(2)}) collective-permute-start(bf16[1,272,1024]{2,1,0:T(8,128)(2,1)S(1)} %bitcast.10), channel_id=1, source_target_pairs={{0,4},{1,5},{2,6},{3,7},{4,0},{5,1},{6,2},{7,3},{8,12},{9,13},{10,... | collective-permute-start | bytes 1671176 | tf_op jit(solution)/shard_map/ppermute | solution.py:47
  11.2 27.6 %collective-permute-start.6 = (bf16[1,272,1024]{2,1,0:T(8,128)(2,1)S(1)}, bf16[1,272,1024]{2,1,0:T(8,128)(2,1)S(1)}, u32[]{:S(2)}, u32[]{:S(2)}) collective-permute-start(bf16[1,272,1024]{2,1,0:T(8,128)(2,1)S(1)} %bitcast.11), channel_id=1, source_target_pairs={{0,16},{1,17},{2,18},{3,19},{4,20},{5,21},{6,22},{7,23},{8,24},{9,... | collective-permute-start | bytes 1671176 | tf_op jit(solution)/shard_map/ppermute | solution.py:47
  13.8 25.2 %collective-permute-start.5 = (bf16[1,272,1024]{2,1,0:T(8,128)(2,1)S(1)}, bf16[1,272,1024]{2,1,0:T(8,128)(2,1)S(1)}, u32[]{:S(2)}, u32[]{:S(2)}) collective-permute-start(bf16[1,272,1024]{2,1,0:T(8,128)(2,1)S(1)} %bitcast.12), channel_id=1, source_target_pairs={{0,8},{1,9},{2,10},{3,11},{4,12},{5,13},{6,14},{7,15},{8,0},{9,1},... | collective-permute-start | bytes 1671176 | tf_op jit(solution)/shard_map/ppermute | solution.py:47
  25.1 7.6 %collective-permute-start.3 = (bf16[144,640]{1,0:T(8,128)(2,1)S(1)}, bf16[144,640]{1,0:T(8,128)(2,1)S(1)}, u32[]{:S(2)}, u32[]{:S(2)}) collective-permute-start(bf16[144,640]{1,0:T(8,128)(2,1)S(1)} %get-tuple-element.58), channel_id=1, source_target_pairs={{0,4},{1,5},{2,6},{3,7},{4,0},{5,1},{6,2},{7,3},{8,12},{9,13},{10,... | collective-permute-start | bytes 552968 | tf_op jit(solution)/shard_map/ppermute | solution.py:47
  26.9 9.7 %collective-permute-start.4 = (bf16[144,640]{1,0:T(8,128)(2,1)S(1)}, bf16[144,640]{1,0:T(8,128)(2,1)S(1)}, u32[]{:S(2)}, u32[]{:S(2)}) collective-permute-start(bf16[144,640]{1,0:T(8,128)(2,1)S(1)} %get-tuple-element.59), channel_id=1, source_target_pairs={{0,6},{1,7},{2,4},{3,5},{4,2},{5,3},{6,0},{7,1},{8,14},{9,15},{10,... | collective-permute-start | bytes 552968 | tf_op jit(solution)/shard_map/ppermute | solution.py:47
  28.4 9.6 %collective-permute-start.2 = (bf16[144,640]{1,0:T(8,128)(2,1)S(1)}, bf16[144,640]{1,0:T(8,128)(2,1)S(1)}, u32[]{:S(2)}, u32[]{:S(2)}) collective-permute-start(bf16[144,640]{1,0:T(8,128)(2,1)S(1)} %get-tuple-element.57.sent_ref), channel_id=1, source_target_pairs={{0,2},{1,3},{2,0},{3,1},{4,6},{5,7},{6,4},{7,5},{8,10},{9,11},{10,... | collective-permute-start | bytes 552968 | tf_op jit(solution)/shard_map/ppermute | solution.py:47
  39.0 35.2 %copy-start = (bf16[256,4096]{1,0:T(8,128)(2,1)S(1)}, bf16[256,4096]{1,0:T(8,128)(2,1)}, u32[]{:S(2)}) copy-start(bf16[256,4096]{1,0:T(8,128)(2,1)} %features_hbm.3) | copy-start | bytes 6291460
  39.1 25.6 %collective-permute-start.13 = (bf16[2,272,1024]{2,1,0:T(8,128)(2,1)S(1)}, bf16[2,272,1024]{2,1,0:T(8,128)(2,1)S(1)}, u32[]{:S(2)}, u32[]{:S(2)}) collective-permute-start(bf16[2,272,1024]{2,1,0:T(8,128)(2,1)S(1)} %pad_maximum_fusion), channel_id=1, source_target_pairs={{0,4},{1,5},{2,6},{3,7},{4,0},{5,1},{6,2},{7,3},{8,12},{9,13},{10,... | collective-permute-start | bytes 3342344 | tf_op jit(solution)/shard_map/ppermute | solution.py:47
  40.4 7.5 %collective-permute-start.8 = (bf16[64,640]{1,0:T(8,128)(2,1)S(1)}, bf16[64,640]{1,0:T(8,128)(2,1)S(1)}, u32[]{:S(2)}, u32[]{:S(2)}) collective-permute-start(bf16[64,640]{1,0:T(8,128)(2,1)S(1)} %get-tuple-element.65), channel_id=1, source_target_pairs={{0,16},{1,17},{2,18},{3,19},{4,20},{5,21},{6,22},{7,23},{8,24},{9,... | collective-permute-start | bytes 245768 | tf_op jit(solution)/shard_map/ppermute | solution.py:47
  43.0 6.4 %collective-permute-start.9 = (bf16[64,640]{1,0:T(8,128)(2,1)S(1)}, bf16[64,640]{1,0:T(8,128)(2,1)S(1)}, u32[]{:S(2)}, u32[]{:S(2)}) collective-permute-start(bf16[64,640]{1,0:T(8,128)(2,1)S(1)} %get-tuple-element.66), channel_id=1, source_target_pairs={{0,24},{1,25},{2,26},{3,27},{4,28},{5,29},{6,30},{7,31},{8,16},{9,... | collective-permute-start | bytes 245768 | tf_op jit(solution)/shard_map/ppermute | solution.py:47
  44.3 5.3 %collective-permute-start.7 = (bf16[64,640]{1,0:T(8,128)(2,1)S(1)}, bf16[64,640]{1,0:T(8,128)(2,1)S(1)}, u32[]{:S(2)}, u32[]{:S(2)}) collective-permute-start(bf16[64,640]{1,0:T(8,128)(2,1)S(1)} %get-tuple-element.64.refs_0_), channel_id=1, source_target_pairs={{0,8},{1,9},{2,10},{3,11},{4,12},{5,13},{6,14},{7,15},{8,0},{9,1},... | collective-permute-start | bytes 245768 | tf_op jit(solution)/shard_map/ppermute | solution.py:47
  49.7 5.9 %collective-permute-start.12 = (bf16[32,640]{1,0:T(8,128)(2,1)S(1)}, bf16[32,640]{1,0:T(8,128)(2,1)S(1)}, u32[]{:S(2)}, u32[]{:S(2)}) collective-permute-start(bf16[32,640]{1,0:T(8,128)(2,1)S(1)} %add_convert_fusion), channel_id=1, source_target_pairs={{0,24},{1,25},{2,26},{3,27},{4,28},{5,29},{6,30},{7,31},{8,16},{9,... | collective-permute-start | bytes 122888 | tf_op jit(solution)/shard_map/ppermute | solution.py:47
  52.3 5.0 %collective-permute-start.11 = (bf16[32,640]{1,0:T(8,128)(2,1)S(1)}, bf16[32,640]{1,0:T(8,128)(2,1)S(1)}, u32[]{:S(2)}, u32[]{:S(2)}) collective-permute-start(bf16[32,640]{1,0:T(8,128)(2,1)S(1)} %add_convert_fusion), channel_id=1, source_target_pairs={{0,16},{1,17},{2,18},{3,19},{4,20},{5,21},{6,22},{7,23},{8,24},{9,... | collective-permute-start | bytes 122888 | tf_op jit(solution)/shard_map/ppermute | solution.py:47
  52.3 5.0 %collective-permute-start.10 = (bf16[32,640]{1,0:T(8,128)(2,1)S(1)}, bf16[32,640]{1,0:T(8,128)(2,1)S(1)}, u32[]{:S(2)}, u32[]{:S(2)}) collective-permute-start(bf16[32,640]{1,0:T(8,128)(2,1)S(1)} %add_convert_fusion), channel_id=1, source_target_pairs={{0,8},{1,9},{2,10},{3,11},{4,12},{5,13},{6,14},{7,15},{8,0},{9,1},... | collective-permute-start | bytes 122888 | tf_op jit(solution)/shard_map/ppermute | solution.py:47
  57.3 16.3 %collective-permute-start.17 = (bf16[1,272,1024]{2,1,0:T(8,128)(2,1)S(1)}, bf16[1,272,1024]{2,1,0:T(8,128)(2,1)S(1)}, u32[]{:S(2)}, u32[]{:S(2)}) collective-permute-start(bf16[1,272,1024]{2,1,0:T(8,128)(2,1)S(1)} %collective-permute-done.6.refs_3_), channel_id=1, source_target_pairs={{0,8},{1,9},{2,10},{3,11},{4,12},{5,13},{6,14},{7,15},{8,0},{9,1},... | collective-permute-start | bytes 1671176 | tf_op jit(solution)/shard_map/ppermute | solution.py:47
  64.8 7.0 %collective-permute-start.16 = (bf16[128,640]{1,0:T(8,128)(2,1)S(1)}, bf16[128,640]{1,0:T(8,128)(2,1)S(1)}, u32[]{:S(2)}, u32[]{:S(2)}) collective-permute-start(bf16[128,640]{1,0:T(8,128)(2,1)S(1)} %pad_maximum_fusion.2), channel_id=1, source_target_pairs={{0,6},{1,7},{2,4},{3,5},{4,2},{5,3},{6,0},{7,1},{8,14},{9,15},{10,... | collective-permute-start | bytes 491528 | tf_op jit(solution)/shard_map/ppermute | solution.py:47
  66.3 7.3 %collective-permute-start.15 = (bf16[128,640]{1,0:T(8,128)(2,1)S(1)}, bf16[128,640]{1,0:T(8,128)(2,1)S(1)}, u32[]{:S(2)}, u32[]{:S(2)}) collective-permute-start(bf16[128,640]{1,0:T(8,128)(2,1)S(1)} %pad_maximum_fusion.2), channel_id=1, source_target_pairs={{0,4},{1,5},{2,6},{3,7},{4,0},{5,1},{6,2},{7,3},{8,12},{9,13},{10,... | collective-permute-start | bytes 491528 | tf_op jit(solution)/shard_map/ppermute | solution.py:47
  67.8 5.8 %collective-permute-start.14 = (bf16[128,640]{1,0:T(8,128)(2,1)S(1)}, bf16[128,640]{1,0:T(8,128)(2,1)S(1)}, u32[]{:S(2)}, u32[]{:S(2)}) collective-permute-start(bf16[128,640]{1,0:T(8,128)(2,1)S(1)} %pad_maximum_fusion.2), channel_id=1, source_target_pairs={{0,2},{1,3},{2,0},{3,1},{4,6},{5,7},{6,4},{7,5},{8,10},{9,11},{10,... | collective-permute-start | bytes 491528 | tf_op jit(solution)/shard_map/ppermute | solution.py:47
  73.6 2.2 %collective-permute-start.18 = (bf16[16,32,640]{2,1,0:T(8,128)(2,1)S(1)}, bf16[16,32,640]{2,1,0:T(8,128)(2,1)S(1)}, u32[]{:S(2)}, u32[]{:S(2)}) collective-permute-start(bf16[16,32,640]{2,1,0:T(8,128)(2,1)S(1)} %bitcast.7), channel_id=1, source_target_pairs={{0,1},{1,0},{2,3},{3,2},{4,5},{5,4},{6,7},{7,6},{8,9},{9,8},{10,11... | collective-permute-start | bytes 1966088 | tf_op jit(solution)/shard_map/ppermute | solution.py:47
  73.7 18.9 %collective-permute-start.19 = (bf16[1,272,1024]{2,1,0:T(8,128)(2,1)S(1)}, bf16[1,272,1024]{2,1,0:T(8,128)(2,1)S(1)}, u32[]{:S(2)}, u32[]{:S(2)}) collective-permute-start(bf16[1,272,1024]{2,1,0:T(8,128)(2,1)S(1)} %collective-permute-done.17.refs_5_), channel_id=1, source_target_pairs={{0,4},{1,5},{2,6},{3,7},{4,0},{5,1},{6,2},{7,3},{8,12},{9,13},{10,... | collective-permute-start | bytes 1671176 | tf_op jit(solution)/shard_map/ppermute | solution.py:47
  75.8 18.0 %collective-permute-start.20 = (bf16[256,512]{1,0:T(8,128)(2,1)S(1)}, bf16[256,512]{1,0:T(8,128)(2,1)S(1)}, u32[]{:S(2)}, u32[]{:S(2)}) collective-permute-start(bf16[256,512]{1,0:T(8,128)(2,1)S(1)} %get-tuple-element.91), channel_id=1, source_target_pairs={{0,16},{1,17},{2,18},{3,19},{4,20},{5,21},{6,22},{7,23},{8,24},{9,... | collective-permute-start | bytes 786440 | tf_op jit(solution)/shard_map/ppermute | solution.py:47
  77.6 20.4 %collective-permute-start.21 = (bf16[256,512]{1,0:T(8,128)(2,1)S(1)}, bf16[256,512]{1,0:T(8,128)(2,1)S(1)}, u32[]{:S(2)}, u32[]{:S(2)}) collective-permute-start(bf16[256,512]{1,0:T(8,128)(2,1)S(1)} %get-tuple-element.92), channel_id=1, source_target_pairs={{0,8},{1,9},{2,10},{3,11},{4,12},{5,13},{6,14},{7,15},{8,0},{9,1},... | collective-permute-start | bytes 786440 | tf_op jit(solution)/shard_map/ppermute | solution.py:47
  81.5 39.8 %collective-permute-start.22 = (bf16[256,512]{1,0:T(8,128)(2,1)S(1)}, bf16[256,512]{1,0:T(8,128)(2,1)S(1)}, u32[]{:S(2)}, u32[]{:S(2)}) collective-permute-start(bf16[256,512]{1,0:T(8,128)(2,1)S(1)} %get-tuple-element.93), channel_id=1, source_target_pairs={{0,24},{1,25},{2,26},{3,27},{4,28},{5,29},{6,30},{7,31},{8,16},{9,... | collective-permute-start | bytes 786440 | tf_op jit(solution)/shard_map/ppermute | solution.py:47
  81.5 39.8 %collective-permute-start.23 = (bf16[256,512]{1,0:T(8,128)(2,1)S(1)}, bf16[256,512]{1,0:T(8,128)(2,1)S(1)}, u32[]{:S(2)}, u32[]{:S(2)}) collective-permute-start(bf16[256,512]{1,0:T(8,128)(2,1)S(1)} %get-tuple-element.94), channel_id=1, source_target_pairs={{0,4},{1,5},{2,6},{3,7},{4,0},{5,1},{6,2},{7,3},{8,12},{9,13},{10,... | collective-permute-start | bytes 786440 | tf_op jit(solution)/shard_map/ppermute | solution.py:47
  92.6 28.7 %collective-permute-start.24 = (bf16[256,512]{1,0:T(8,128)(2,1)S(1)}, bf16[256,512]{1,0:T(8,128)(2,1)S(1)}, u32[]{:S(2)}, u32[]{:S(2)}) collective-permute-start(bf16[256,512]{1,0:T(8,128)(2,1)S(1)} %get-tuple-element.95), channel_id=1, source_target_pairs={{0,12},{1,13},{2,14},{3,15},{4,8},{5,9},{6,10},{7,11},{8,4},{9,5},... | collective-permute-start | bytes 786440 | tf_op jit(solution)/shard_map/ppermute | solution.py:47
  93.8 27.5 %collective-permute-start.25 = (bf16[256,512]{1,0:T(8,128)(2,1)S(1)}, bf16[256,512]{1,0:T(8,128)(2,1)S(1)}, u32[]{:S(2)}, u32[]{:S(2)}) collective-permute-start(bf16[256,512]{1,0:T(8,128)(2,1)S(1)} %get-tuple-element.96), channel_id=1, source_target_pairs={{0,20},{1,21},{2,22},{3,23},{4,16},{5,17},{6,18},{7,19},{8,28},{9,... | collective-permute-start | bytes 786440 | tf_op jit(solution)/shard_map/ppermute | solution.py:47
  98.0 23.4 %collective-permute-start.26 = (bf16[256,512]{1,0:T(8,128)(2,1)S(1)}, bf16[256,512]{1,0:T(8,128)(2,1)S(1)}, u32[]{:S(2)}, u32[]{:S(2)}) collective-permute-start(bf16[256,512]{1,0:T(8,128)(2,1)S(1)} %get-tuple-element.97), channel_id=1, source_target_pairs={{0,28},{1,29},{2,30},{3,31},{4,24},{5,25},{6,26},{7,27},{8,20},{9,... | collective-permute-start | bytes 786440 | tf_op jit(solution)/shard_map/ppermute | solution.py:47
  123.2 2.5 %collective-permute-start.28 = (bf16[128,1024]{1,0:T(8,128)(2,1)S(1)}, bf16[128,1024]{1,0:T(8,128)(2,1)S(1)}, u32[]{:S(2)}, u32[]{:S(2)}) collective-permute-start(bf16[128,1024]{1,0:T(8,128)(2,1)S(1)} %get-tuple-element.101), channel_id=1, source_target_pairs={{0,1},{1,0},{2,3},{3,2},{4,5},{5,4},{6,7},{7,6},{8,9},{9,8},{10,11... | collective-permute-start | bytes 786440 | tf_op jit(solution)/shard_map/ppermute | solution.py:47
  125.1 2.1 %collective-permute-start.27 = (bf16[128,1024]{1,0:T(8,128)(2,1)S(1)}, bf16[128,1024]{1,0:T(8,128)(2,1)S(1)}, u32[]{:S(2)}, u32[]{:S(2)}) collective-permute-start(bf16[128,1024]{1,0:T(8,128)(2,1)S(1)} %get-tuple-element.99), channel_id=1, source_target_pairs={{0,1},{1,0},{2,3},{3,2},{4,5},{5,4},{6,7},{7,6},{8,9},{9,8},{10,11... | collective-permute-start | bytes 786440 | tf_op jit(solution)/shard_map/ppermute | solution.py:47
  125.7 8.3 %collective-permute-start.29 = (bf16[128,1024]{1,0:T(8,128)(2,1)S(1)}, bf16[128,1024]{1,0:T(8,128)(2,1)S(1)}, u32[]{:S(2)}, u32[]{:S(2)}) collective-permute-start(bf16[128,1024]{1,0:T(8,128)(2,1)S(1)} %join.1), channel_id=1, source_target_pairs={{0,2},{1,3},{2,0},{3,1},{4,6},{5,7},{6,4},{7,5},{8,10},{9,11},{10,... | collective-permute-start | bytes 786440 | tf_op jit(solution)/shard_map/ppermute | solution.py:47

commit v14 on v13

--- a/solution.py
+++ b/solution.py
@@ -71,7 +71,7 @@
     return pl.pallas_call(
         cut_kernel,
         in_specs=[smem(), pl.BlockSpec(memory_space=pltpu.HBM)],
-        out_specs=[pl.BlockSpec(memory_space=pltpu.HBM)] * groups,
+        out_specs=[vmem()] * groups,
         out_shape=[jax.ShapeDtypeStruct((rows, depth // groups), BF16)] * groups,
         scratch_shapes=[pltpu.SemaphoreType.DMA((groups,))],
         compiler_params=params(8),
@@ -677,7 +677,7 @@
     other = xor_permute(part, 1)
     if direct:
         other, *slices = lax.optimization_barrier((other, *slices))
-        slice_order = [0, 4, 2, 6, 1, 3, 5, 7]
+        slice_order = [0, 4, 2, 6, 5, 7, 1, 3]
         slices = [xor_permute(slices[k], k * shares) if k else slices[k] for k in slice_order]
 
     whitener, mean = whiten(ids, part, other, sums, seen, tuple(stages), rows, embed)

time: 137 us -> 137 us (level)
  starting transfers between devices: 43.9 us -> 40.3 us
  waiting for transfers between devices: 46 us -> 48.4 us
    ppermute x30, starting transfers between devices: 43.9 us -> 40.3 us  [xor_permute(): return lax.ppermute(piece, AXES, [(i, i ^ mask) for i in range(devices)])]
    ppermute x30, waiting for transfers between devices: 46 us -> 48.4 us  [xor_permute(): return lax.ppermute(piece, AXES, [(i, i ^ mask) for i in range(devices)])]
  transfers between devices with their start and end apart: 30 -> 30, of which waited for: 16 -> 18; matrix products, arithmetic and copies ran while one was open for 0% -> 0% of each run, Pallas kernels for 25% -> 25%
where the time goes in v14:
time: 137 us; the launch traced here: 134 us
  waiting for transfers between devices  48.4 us (35%)
  Pallas kernels  43.3 us (32%)
  starting transfers between devices  40.3 us (29%)
    ppermute x30, waiting for transfers between devices, xor_permute(): return lax.ppermute(piece, AXES, [(i, i ^ mask) for i in range(devices)])  48.4 us
    ppermute x30, starting transfers between devices, xor_permute(): return lax.ppermute(piece, AXES, [(i, i ^ mask) for i in range(devices)])  40.3 us
    pallas_call x1, Pallas kernels, contrast(): pl.pallas_call(functools.partial(contrast_kernel, order), in_specs=[smem(...  19.6 us
    pallas_call x1, Pallas kernels, whiten(): pl.pallas_call(make_whiten_kernel(rows, count, stages), in_specs=[smem()]...  10.2 us
    pallas_call x1, Pallas kernels, project(): pl.pallas_call(project_kernel, in_specs=[smem(), smem(), hbm, hbm, hbm],...  6.05 us
    pallas_call x2, Pallas kernels, weight_pieces(): pl.pallas_call(functools.partial(pieces_kernel, share, masks, order), in_...  3.68 us
  transfers between devices with their start and end apart: 30, of which 18 were waited for; matrix products, arithmetic and copies ran while one was open for 0% of the time, Pallas kernels for 25%

profile of v14, /device:TPU:0, one launch (start us, length us, event | category | flops | bytes accessed | tf_op | source)
XLA Modules:
  0.0 134.3 jit_solution(7986577669655433497)
XLA Ops:
  0.6 0.1 pad_add_fusion.ids_ref
  0.7 0.7 copy-done.1
  1.4 0.7 copy-done.2
  2.1 6.1 %project.1 = (bf16[272,1024]{1,0:T(8,128)(2,1)S(1)}, bf16[528,640]{1,0:T(8,128)(2,1)S(1)}, f32[512,640]{1,0:T(8,128)S(1)}) custom-call(s32[3]{0:T(128)S(1)} %pad_add_fusion.ids_ref, s32[1,4]{1,0:T(1,128)S(1)} %copy-done.2, bf16[256,4096]{1,0:T(8,128)(2,1)} %features_hbm.3, bf16[4096,1024]{1,0:T(8,128)(2,1)} %weight_hbm.1, s32[4,256]{1,0:T(4,128)S(1)} %bitcast.9), custom_call_target="tpu_custom_call" | custom-call | flops 2147483648 | bytes 8388608 | tf_op jit(solution)/shard_map/project/pallas_call | solution.py:186
  8.1 0.5 collective-permute-start
  8.6 2.6 %collective-permute-start.1 = (bf16[1,272,1024]{2,1,0:T(8,128)(2,1)S(1)}, bf16[1,272,1024]{2,1,0:T(8,128)(2,1)S(1)}, u32[]{:S(2)}, u32[]{:S(2)}) collective-permute-start(bf16[1,272,1024]{2,1,0:T(8,128)(2,1)S(1)} %bitcast.10), channel_id=1, source_target_pairs={{0,4},{1,5},{2,6},{3,7},{4,0},{5,1},{6,2},{7,3},{8,12},{9,13},{10,... | collective-permute-start | bytes 1671176 | tf_op jit(solution)/shard_map/ppermute | solution.py:47
  11.2 2.6 %collective-permute-start.6 = (bf16[1,272,1024]{2,1,0:T(8,128)(2,1)S(1)}, bf16[1,272,1024]{2,1,0:T(8,128)(2,1)S(1)}, u32[]{:S(2)}, u32[]{:S(2)}) collective-permute-start(bf16[1,272,1024]{2,1,0:T(8,128)(2,1)S(1)} %bitcast.11), channel_id=1, source_target_pairs={{0,16},{1,17},{2,18},{3,19},{4,20},{5,21},{6,22},{7,23},{8,24},{9,... | collective-permute-start | bytes 1671176 | tf_op jit(solution)/shard_map/ppermute | solution.py:47
  13.8 1.6 %collective-permute-start.5 = (bf16[1,272,1024]{2,1,0:T(8,128)(2,1)S(1)}, bf16[1,272,1024]{2,1,0:T(8,128)(2,1)S(1)}, u32[]{:S(2)}, u32[]{:S(2)}) collective-permute-start(bf16[1,272,1024]{2,1,0:T(8,128)(2,1)S(1)} %bitcast.12), channel_id=1, source_target_pairs={{0,8},{1,9},{2,10},{3,11},{4,12},{5,13},{6,14},{7,15},{8,0},{9,1},... | collective-permute-start | bytes 1671176 | tf_op jit(solution)/shard_map/ppermute | solution.py:47
  15.4 9.1 %collective-permute-done.1.refs_1_ = bf16[1,272,1024]{2,1,0:T(8,128)(2,1)S(1)} collective-permute-done((bf16[1,272,1024]{2,1,0:T(8,128)(2,1)S(1)}, bf16[1,272,1024]{2,1,0:T(8,128)(2,1)S(1)}, u32[]{:S(2)}, u32[]{:S(2)}) %collective-permute-start.1) | collective-permute-done | bytes 557088 | tf_op jit(solution)/shard_map/ppermute | solution.py:47
  24.4 0.0 collective-permute-done.refs_0_
  24.4 0.7 stage.2
  25.1 1.8 %collective-permute-start.3 = (bf16[144,640]{1,0:T(8,128)(2,1)S(1)}, bf16[144,640]{1,0:T(8,128)(2,1)S(1)}, u32[]{:S(2)}, u32[]{:S(2)}) collective-permute-start(bf16[144,640]{1,0:T(8,128)(2,1)S(1)} %get-tuple-element.58), channel_id=1, source_target_pairs={{0,4},{1,5},{2,6},{3,7},{4,0},{5,1},{6,2},{7,3},{8,12},{9,13},{10,... | collective-permute-start | bytes 552968 | tf_op jit(solution)/shard_map/ppermute | solution.py:47
  26.9 1.5 %collective-permute-start.4 = (bf16[144,640]{1,0:T(8,128)(2,1)S(1)}, bf16[144,640]{1,0:T(8,128)(2,1)S(1)}, u32[]{:S(2)}, u32[]{:S(2)}) collective-permute-start(bf16[144,640]{1,0:T(8,128)(2,1)S(1)} %get-tuple-element.59), channel_id=1, source_target_pairs={{0,6},{1,7},{2,4},{3,5},{4,2},{5,3},{6,0},{7,1},{8,14},{9,15},{10,... | collective-permute-start | bytes 552968 | tf_op jit(solution)/shard_map/ppermute | solution.py:47
  28.4 0.2 collective-permute-start.2
  28.7 4.0 %collective-permute-done.3.refs_1_ = bf16[144,640]{1,0:T(8,128)(2,1)S(1)} collective-permute-done((bf16[144,640]{1,0:T(8,128)(2,1)S(1)}, bf16[144,640]{1,0:T(8,128)(2,1)S(1)}, u32[]{:S(2)}, u32[]{:S(2)}) %collective-permute-start.3) | collective-permute-done | bytes 184352 | tf_op jit(solution)/shard_map/ppermute | solution.py:47
  32.7 4.0 %collective-permute-done.4.refs_2_ = bf16[144,640]{1,0:T(8,128)(2,1)S(1)} collective-permute-done((bf16[144,640]{1,0:T(8,128)(2,1)S(1)}, bf16[144,640]{1,0:T(8,128)(2,1)S(1)}, u32[]{:S(2)}, u32[]{:S(2)}) %collective-permute-start.4) | collective-permute-done | bytes 184352 | tf_op jit(solution)/shard_map/ppermute | solution.py:47
  36.7 1.4 %collective-permute-done.2.refs_0_ = bf16[144,640]{1,0:T(8,128)(2,1)S(1)} collective-permute-done((bf16[144,640]{1,0:T(8,128)(2,1)S(1)}, bf16[144,640]{1,0:T(8,128)(2,1)S(1)}, u32[]{:S(2)}, u32[]{:S(2)}) %collective-permute-start.2) | collective-permute-done | bytes 184352 | tf_op jit(solution)/shard_map/ppermute | solution.py:47
  38.0 0.6 stage.3
  38.7 0.2 collective-permute-done.6.refs_3_
  38.8 0.2 collective-permute-done.5.refs_2_
  39.0 0.1 pad_maximum_fusion
  39.1 1.2 collective-permute-start.13
  40.4 2.6 %collective-permute-start.8 = (bf16[64,640]{1,0:T(8,128)(2,1)S(1)}, bf16[64,640]{1,0:T(8,128)(2,1)S(1)}, u32[]{:S(2)}, u32[]{:S(2)}) collective-permute-start(bf16[64,640]{1,0:T(8,128)(2,1)S(1)} %get-tuple-element.65), channel_id=1, source_target_pairs={{0,16},{1,17},{2,18},{3,19},{4,20},{5,21},{6,22},{7,23},{8,24},{9,... | collective-permute-start | bytes 245768 | tf_op jit(solution)/shard_map/ppermute | solution.py:47
  43.0 1.3 %collective-permute-start.9 = (bf16[64,640]{1,0:T(8,128)(2,1)S(1)}, bf16[64,640]{1,0:T(8,128)(2,1)S(1)}, u32[]{:S(2)}, u32[]{:S(2)}) collective-permute-start(bf16[64,640]{1,0:T(8,128)(2,1)S(1)} %get-tuple-element.66), channel_id=1, source_target_pairs={{0,24},{1,25},{2,26},{3,27},{4,28},{5,29},{6,30},{7,31},{8,16},{9,... | collective-permute-start | bytes 245768 | tf_op jit(solution)/shard_map/ppermute | solution.py:47
  44.3 0.2 collective-permute-start.7
  44.5 3.4 %collective-permute-done.8.refs_2_ = bf16[64,640]{1,0:T(8,128)(2,1)S(1)} collective-permute-done((bf16[64,640]{1,0:T(8,128)(2,1)S(1)}, bf16[64,640]{1,0:T(8,128)(2,1)S(1)}, u32[]{:S(2)}, u32[]{:S(2)}) %collective-permute-start.8) | collective-permute-done | bytes 81952 | tf_op jit(solution)/shard_map/ppermute | solution.py:47
  47.9 1.4 %collective-permute-done.9.refs_3_ = bf16[64,640]{1,0:T(8,128)(2,1)S(1)} collective-permute-done((bf16[64,640]{1,0:T(8,128)(2,1)S(1)}, bf16[64,640]{1,0:T(8,128)(2,1)S(1)}, u32[]{:S(2)}, u32[]{:S(2)}) %collective-permute-start.9) | collective-permute-done | bytes 81952 | tf_op jit(solution)/shard_map/ppermute | solution.py:47
  49.4 0.3 collective-permute-done.7.refs_1_
  49.7 2.6 %collective-permute-start.12 = (bf16[32,640]{1,0:T(8,128)(2,1)S(1)}, bf16[32,640]{1,0:T(8,128)(2,1)S(1)}, u32[]{:S(2)}, u32[]{:S(2)}) collective-permute-start(bf16[32,640]{1,0:T(8,128)(2,1)S(1)} %add_convert_fusion), channel_id=1, source_target_pairs={{0,24},{1,25},{2,26},{3,27},{4,28},{5,29},{6,30},{7,31},{8,16},{9,... | collective-permute-start | bytes 122888 | tf_op jit(solution)/shard_map/ppermute | solution.py:47
  52.3 1.9 %collective-permute-start.10 = (bf16[32,640]{1,0:T(8,128)(2,1)S(1)}, bf16[32,640]{1,0:T(8,128)(2,1)S(1)}, u32[]{:S(2)}, u32[]{:S(2)}) collective-permute-start(bf16[32,640]{1,0:T(8,128)(2,1)S(1)} %add_convert_fusion), channel_id=1, source_target_pairs={{0,8},{1,9},{2,10},{3,11},{4,12},{5,13},{6,14},{7,15},{8,0},{9,1},... | collective-permute-start | bytes 122888 | tf_op jit(solution)/shard_map/ppermute | solution.py:47
  54.1 1.4 %collective-permute-done.12 = bf16[32,640]{1,0:T(8,128)(2,1)S(1)} collective-permute-done((bf16[32,640]{1,0:T(8,128)(2,1)S(1)}, bf16[32,640]{1,0:T(8,128)(2,1)S(1)}, u32[]{:S(2)}, u32[]{:S(2)}) %collective-permute-start.12) | collective-permute-done | bytes 40992 | tf_op jit(solution)/shard_map/ppermute | solution.py:47
  55.6 1.7 %collective-permute-done.11 = bf16[32,640]{1,0:T(8,128)(2,1)S(1)} collective-permute-done((bf16[32,640]{1,0:T(8,128)(2,1)S(1)}, bf16[32,640]{1,0:T(8,128)(2,1)S(1)}, u32[]{:S(2)}, u32[]{:S(2)}) %collective-permute-start.11) | collective-permute-done | bytes 40992 | tf_op jit(solution)/shard_map/ppermute | solution.py:47
  57.3 1.3 collective-permute-start.17
  58.6 6.2 %collective-permute-done.13.refs_4_ = bf16[2,272,1024]{2,1,0:T(8,128)(2,1)S(1)} collective-permute-done((bf16[2,272,1024]{2,1,0:T(8,128)(2,1)S(1)}, bf16[2,272,1024]{2,1,0:T(8,128)(2,1)S(1)}, u32[]{:S(2)}, u32[]{:S(2)}) %collective-permute-start.13) | collective-permute-done | bytes 1114144 | tf_op jit(solution)/shard_map/ppermute | solution.py:47
  64.8 1.5 %collective-permute-start.16 = (bf16[128,640]{1,0:T(8,128)(2,1)S(1)}, bf16[128,640]{1,0:T(8,128)(2,1)S(1)}, u32[]{:S(2)}, u32[]{:S(2)}) collective-permute-start(bf16[128,640]{1,0:T(8,128)(2,1)S(1)} %pad_maximum_fusion.2), channel_id=1, source_target_pairs={{0,6},{1,7},{2,4},{3,5},{4,2},{5,3},{6,0},{7,1},{8,14},{9,15},{10,... | collective-permute-start | bytes 491528 | tf_op jit(solution)/shard_map/ppermute | solution.py:47
  66.3 1.5 %collective-permute-start.15 = (bf16[128,640]{1,0:T(8,128)(2,1)S(1)}, bf16[128,640]{1,0:T(8,128)(2,1)S(1)}, u32[]{:S(2)}, u32[]{:S(2)}) collective-permute-start(bf16[128,640]{1,0:T(8,128)(2,1)S(1)} %pad_maximum_fusion.2), channel_id=1, source_target_pairs={{0,4},{1,5},{2,6},{3,7},{4,0},{5,1},{6,2},{7,3},{8,12},{9,13},{10,... | collective-permute-start | bytes 491528 | tf_op jit(solution)/shard_map/ppermute | solution.py:47
  67.8 0.5 collective-permute-start.14
  68.3 3.5 %collective-permute-done.16 = bf16[128,640]{1,0:T(8,128)(2,1)S(1)} collective-permute-done((bf16[128,640]{1,0:T(8,128)(2,1)S(1)}, bf16[128,640]{1,0:T(8,128)(2,1)S(1)}, u32[]{:S(2)}, u32[]{:S(2)}) %collective-permute-start.16) | collective-permute-done | bytes 163872 | tf_op jit(solution)/shard_map/ppermute | solution.py:47
  71.7 1.8 %collective-permute-done.15 = bf16[128,640]{1,0:T(8,128)(2,1)S(1)} collective-permute-done((bf16[128,640]{1,0:T(8,128)(2,1)S(1)}, bf16[128,640]{1,0:T(8,128)(2,1)S(1)}, u32[]{:S(2)}, u32[]{:S(2)}) %collective-permute-start.15) | collective-permute-done | bytes 163872 | tf_op jit(solution)/shard_map/ppermute | solution.py:47
  73.5 0.1 pad_maximum_fusion.1
  73.6 0.0 collective-permute-done.17.refs_5_
  73.6 0.1 collective-permute-start.18
  73.7 0.6 collective-permute-start.19
  74.3 0.8 cut.1
  75.1 0.7 collective-permute-done.18.far_ref
  75.8 1.8 %collective-permute-start.20 = (bf16[256,512]{1,0:T(8,128)(2,1)S(1)}, bf16[256,512]{1,0:T(8,128)(2,1)S(1)}, u32[]{:S(2)}, u32[]{:S(2)}) collective-permute-start(bf16[256,512]{1,0:T(8,128)(2,1)S(1)} %get-tuple-element.91), channel_id=1, source_target_pairs={{0,16},{1,17},{2,18},{3,19},{4,20},{5,21},{6,22},{7,23},{8,24},{9,... | collective-permute-start | bytes 786440 | tf_op jit(solution)/shard_map/ppermute | solution.py:47
  77.6 3.9 %collective-permute-start.21 = (bf16[256,512]{1,0:T(8,128)(2,1)S(1)}, bf16[256,512]{1,0:T(8,128)(2,1)S(1)}, u32[]{:S(2)}, u32[]{:S(2)}) collective-permute-start(bf16[256,512]{1,0:T(8,128)(2,1)S(1)} %get-tuple-element.92), channel_id=1, source_target_pairs={{0,8},{1,9},{2,10},{3,11},{4,12},{5,13},{6,14},{7,15},{8,0},{9,1},... | collective-permute-start | bytes 786440 | tf_op jit(solution)/shard_map/ppermute | solution.py:47
  81.5 0.0 collective-permute-start.22
  81.5 1.8 %collective-permute-start.23 = (bf16[256,512]{1,0:T(8,128)(2,1)S(1)}, bf16[256,512]{1,0:T(8,128)(2,1)S(1)}, u32[]{:S(2)}, u32[]{:S(2)}) collective-permute-start(bf16[256,512]{1,0:T(8,128)(2,1)S(1)} %get-tuple-element.94), channel_id=1, source_target_pairs={{0,20},{1,21},{2,22},{3,23},{4,16},{5,17},{6,18},{7,19},{8,28},{9,... | collective-permute-start | bytes 786440 | tf_op jit(solution)/shard_map/ppermute | solution.py:47
  83.3 10.2 %whiten.1 = (bf16[1024,1024]{1,0:T(8,128)(2,1)S(1)}, f32[1,1024]{1,0:T(1,128)S(1)}) custom-call(s32[3]{0:T(128)S(1)} %pad_add_fusion.ids_ref, bf16[16,32,640]{2,1,0:T(8,128)(2,1)S(1)} %bitcast.8, bf16[16,32,640]{2,1,0:T(8,128)(2,1)S(1)} %collective-permute-done.18.far_ref, bf16[64,640]{1,0:T(8,128)(2,1)S(1)} %get-tuple-element.64.refs_0_, ...), custom_call_target="tpu_custom_call" | custom-call | flops 10737418240 | bytes 2097152 | tf_op jit(solution)/shard_map/whiten/pallas_call | solution.py:396
  93.5 0.0 collective-permute-done.19.refs_6_
  93.5 2.4 %collective-permute-start.24 = (bf16[256,512]{1,0:T(8,128)(2,1)S(1)}, bf16[256,512]{1,0:T(8,128)(2,1)S(1)}, u32[]{:S(2)}, u32[]{:S(2)}) collective-permute-start(bf16[256,512]{1,0:T(8,128)(2,1)S(1)} %get-tuple-element.95), channel_id=1, source_target_pairs={{0,28},{1,29},{2,30},{3,31},{4,24},{5,25},{6,26},{7,27},{8,20},{9,... | collective-permute-start | bytes 786440 | tf_op jit(solution)/shard_map/ppermute | solution.py:47
  95.9 1.1 collective-permute-start.25
  97.1 1.0 collective-permute-start.26
  98.1 19.6 %contrast.1 = (f32[1,256]{1,0:T(1,128)}, bf16[8,256,1024]{2,1,0:T(8,128)(2,1)S(1)}) custom-call(s32[3]{0:T(128)S(1)} %pad_add_fusion.ids_ref, f32[1,1024]{1,0:T(1,128)S(1)} %get-tuple-element.83.mean_ref, bf16[1024,1024]{1,0:T(8,128)(2,1)S(1)} %get-tuple-element.84.whitener_ref.refs_3_, bf16[1,272,1024]{2,1,0:T(8,128)(2,1)S(1)} %bitcast.13, ...), custom_call_target="tpu_custom_call" | custom-call | flops 12884901888 | bytes 8388608 | tf_op jit(solution)/shard_map/contrast/pallas_call | solution.py:488
  117.7 2.3 %collective-permute-done.23.refs_4_ = bf16[256,512]{1,0:T(8,128)(2,1)S(1)} collective-permute-done((bf16[256,512]{1,0:T(8,128)(2,1)S(1)}, bf16[256,512]{1,0:T(8,128)(2,1)S(1)}, u32[]{:S(2)}, u32[]{:S(2)}) %collective-permute-start.23) | collective-permute-done | bytes 262176 | tf_op jit(solution)/shard_map/ppermute | solution.py:47
  119.9 0.1 collective-permute-done.25.refs_6_
  120.1 1.9 %weight_pieces.3 = (f32[128,1024]{1,0:T(8,128)S(1)}, bf16[128,1024]{1,0:T(8,128)(2,1)S(1)}) custom-call(s32[3]{0:T(128)S(1)} %pad_add_fusion.ids_ref, bf16[8,256,1024]{2,1,0:T(8,128)(2,1)S(1)} %get-tuple-element.89.grad_ref, bf16[256,512]{1,0:T(8,128)(2,1)S(1)} %get-tuple-element.90.refs_0_, bf16[256,512]{1,0:T(8,128)(2,1)S(1)} %collective-permute-done.20.refs_1_, ...), custom_call_target="tpu_custom_call" | custom-call | flops 1073741824 | bytes 6291456 | tf_op jit(solution)/shard_map/weight_pieces/pallas_call | solution.py:539
  121.9 0.1 collective-permute-start.28
  122.0 1.8 %weight_pieces.2 = (f32[128,1024]{1,0:T(8,128)S(1)}, bf16[128,1024]{1,0:T(8,128)(2,1)S(1)}) custom-call(s32[3]{0:T(128)S(1)} %pad_add_fusion.ids_ref, bf16[8,256,1024]{2,1,0:T(8,128)(2,1)S(1)} %get-tuple-element.89.grad_ref, bf16[256,512]{1,0:T(8,128)(2,1)S(1)} %get-tuple-element.90.refs_0_, bf16[256,512]{1,0:T(8,128)(2,1)S(1)} %collective-permute-done.20.refs_1_, ...), custom_call_target="tpu_custom_call" | custom-call | flops 1073741824 | bytes 6291456 | tf_op jit(solution)/shard_map/weight_pieces/pallas_call | solution.py:539
  123.8 0.6 collective-permute-start.27
  124.4 1.5 %collective-permute-start.29 = (bf16[128,1024]{1,0:T(8,128)(2,1)S(1)}, bf16[128,1024]{1,0:T(8,128)(2,1)S(1)}, u32[]{:S(2)}, u32[]{:S(2)}) collective-permute-start(bf16[128,1024]{1,0:T(8,128)(2,1)S(1)} %join.1), channel_id=1, source_target_pairs={{0,2},{1,3},{2,0},{3,1},{4,6},{5,7},{6,4},{7,5},{8,10},{9,11},{10,... | collective-permute-start | bytes 786440 | tf_op jit(solution)/shard_map/ppermute | solution.py:47
  126.0 6.8 %collective-permute-done.29.refs_2_ = bf16[128,1024]{1,0:T(8,128)(2,1)S(1)} collective-permute-done((bf16[128,1024]{1,0:T(8,128)(2,1)S(1)}, bf16[128,1024]{1,0:T(8,128)(2,1)S(1)}, u32[]{:S(2)}, u32[]{:S(2)}) %collective-permute-start.29) | collective-permute-done | bytes 262176 | tf_op jit(solution)/shard_map/ppermute | solution.py:47
  132.8 1.5 %finish.1 = f32[128,1024]{1,0:T(8,128)} custom-call(f32[128,1024]{1,0:T(8,128)S(1)} %get-tuple-element.98.refs_0_, bf16[128,1024]{1,0:T(8,128)(2,1)S(1)} %collective-permute-done.27.refs_1_, bf16[128,1024]{1,0:T(8,128)(2,1)S(1)} %collective-permute-done.29.refs_2_, bf16[1024,1024]{1,0:T(8,128)(2,1)S(1)} %get-tuple-element.84.whitener_ref.refs_3_), custom_call_target="tpu_custom_call" | custom-call | tf_op jit(solution)/shard_map/finish/pallas_call | solution.py:584
  (17 shorter events, 0.1 us)
Async XLA Ops:
  0.7 0.7 copy-start.1
  1.4 0.7 copy-start.2
  8.1 16.3 %collective-permute-start = (bf16[528,640]{1,0:T(8,128)(2,1)S(1)}, bf16[528,640]{1,0:T(8,128)(2,1)S(1)}, u32[]{:S(2)}, u32[]{:S(2)}) collective-permute-start(bf16[528,640]{1,0:T(8,128)(2,1)S(1)} %get-tuple-element.53.sent_ref), channel_id=1, source_target_pairs={{0,1},{1,0},{2,3},{3,2},{4,5},{5,4},{6,7},{7,6},{8,9},{9,8},{10,11... | collective-permute-start | bytes 2027528 | tf_op jit(solution)/shard_map/ppermute | solution.py:47
  8.6 15.8 %collective-permute-start.1 = (bf16[1,272,1024]{2,1,0:T(8,128)(2,1)S(1)}, bf16[1,272,1024]{2,1,0:T(8,128)(2,1)S(1)}, u32[]{:S(2)}, u32[]{:S(2)}) collective-permute-start(bf16[1,272,1024]{2,1,0:T(8,128)(2,1)S(1)} %bitcast.10), channel_id=1, source_target_pairs={{0,4},{1,5},{2,6},{3,7},{4,0},{5,1},{6,2},{7,3},{8,12},{9,13},{10,... | collective-permute-start | bytes 1671176 | tf_op jit(solution)/shard_map/ppermute | solution.py:47
  11.2 27.6 %collective-permute-start.6 = (bf16[1,272,1024]{2,1,0:T(8,128)(2,1)S(1)}, bf16[1,272,1024]{2,1,0:T(8,128)(2,1)S(1)}, u32[]{:S(2)}, u32[]{:S(2)}) collective-permute-start(bf16[1,272,1024]{2,1,0:T(8,128)(2,1)S(1)} %bitcast.11), channel_id=1, source_target_pairs={{0,16},{1,17},{2,18},{3,19},{4,20},{5,21},{6,22},{7,23},{8,24},{9,... | collective-permute-start | bytes 1671176 | tf_op jit(solution)/shard_map/ppermute | solution.py:47
  13.8 25.2 %collective-permute-start.5 = (bf16[1,272,1024]{2,1,0:T(8,128)(2,1)S(1)}, bf16[1,272,1024]{2,1,0:T(8,128)(2,1)S(1)}, u32[]{:S(2)}, u32[]{:S(2)}) collective-permute-start(bf16[1,272,1024]{2,1,0:T(8,128)(2,1)S(1)} %bitcast.12), channel_id=1, source_target_pairs={{0,8},{1,9},{2,10},{3,11},{4,12},{5,13},{6,14},{7,15},{8,0},{9,1},... | collective-permute-start | bytes 1671176 | tf_op jit(solution)/shard_map/ppermute | solution.py:47
  25.1 7.6 %collective-permute-start.3 = (bf16[144,640]{1,0:T(8,128)(2,1)S(1)}, bf16[144,640]{1,0:T(8,128)(2,1)S(1)}, u32[]{:S(2)}, u32[]{:S(2)}) collective-permute-start(bf16[144,640]{1,0:T(8,128)(2,1)S(1)} %get-tuple-element.58), channel_id=1, source_target_pairs={{0,4},{1,5},{2,6},{3,7},{4,0},{5,1},{6,2},{7,3},{8,12},{9,13},{10,... | collective-permute-start | bytes 552968 | tf_op jit(solution)/shard_map/ppermute | solution.py:47
  26.9 9.7 %collective-permute-start.4 = (bf16[144,640]{1,0:T(8,128)(2,1)S(1)}, bf16[144,640]{1,0:T(8,128)(2,1)S(1)}, u32[]{:S(2)}, u32[]{:S(2)}) collective-permute-start(bf16[144,640]{1,0:T(8,128)(2,1)S(1)} %get-tuple-element.59), channel_id=1, source_target_pairs={{0,6},{1,7},{2,4},{3,5},{4,2},{5,3},{6,0},{7,1},{8,14},{9,15},{10,... | collective-permute-start | bytes 552968 | tf_op jit(solution)/shard_map/ppermute | solution.py:47
  28.4 9.6 %collective-permute-start.2 = (bf16[144,640]{1,0:T(8,128)(2,1)S(1)}, bf16[144,640]{1,0:T(8,128)(2,1)S(1)}, u32[]{:S(2)}, u32[]{:S(2)}) collective-permute-start(bf16[144,640]{1,0:T(8,128)(2,1)S(1)} %get-tuple-element.57.sent_ref), channel_id=1, source_target_pairs={{0,2},{1,3},{2,0},{3,1},{4,6},{5,7},{6,4},{7,5},{8,10},{9,11},{10,... | collective-permute-start | bytes 552968 | tf_op jit(solution)/shard_map/ppermute | solution.py:47
  39.0 35.2 %copy-start = (bf16[256,4096]{1,0:T(8,128)(2,1)S(1)}, bf16[256,4096]{1,0:T(8,128)(2,1)}, u32[]{:S(2)}) copy-start(bf16[256,4096]{1,0:T(8,128)(2,1)} %features_hbm.3) | copy-start | bytes 6291460
  39.1 25.6 %collective-permute-start.13 = (bf16[2,272,1024]{2,1,0:T(8,128)(2,1)S(1)}, bf16[2,272,1024]{2,1,0:T(8,128)(2,1)S(1)}, u32[]{:S(2)}, u32[]{:S(2)}) collective-permute-start(bf16[2,272,1024]{2,1,0:T(8,128)(2,1)S(1)} %pad_maximum_fusion), channel_id=1, source_target_pairs={{0,4},{1,5},{2,6},{3,7},{4,0},{5,1},{6,2},{7,3},{8,12},{9,13},{10,... | collective-permute-start | bytes 3342344 | tf_op jit(solution)/shard_map/ppermute | solution.py:47
  40.4 7.5 %collective-permute-start.8 = (bf16[64,640]{1,0:T(8,128)(2,1)S(1)}, bf16[64,640]{1,0:T(8,128)(2,1)S(1)}, u32[]{:S(2)}, u32[]{:S(2)}) collective-permute-start(bf16[64,640]{1,0:T(8,128)(2,1)S(1)} %get-tuple-element.65), channel_id=1, source_target_pairs={{0,16},{1,17},{2,18},{3,19},{4,20},{5,21},{6,22},{7,23},{8,24},{9,... | collective-permute-start | bytes 245768 | tf_op jit(solution)/shard_map/ppermute | solution.py:47
  43.0 6.4 %collective-permute-start.9 = (bf16[64,640]{1,0:T(8,128)(2,1)S(1)}, bf16[64,640]{1,0:T(8,128)(2,1)S(1)}, u32[]{:S(2)}, u32[]{:S(2)}) collective-permute-start(bf16[64,640]{1,0:T(8,128)(2,1)S(1)} %get-tuple-element.66), channel_id=1, source_target_pairs={{0,24},{1,25},{2,26},{3,27},{4,28},{5,29},{6,30},{7,31},{8,16},{9,... | collective-permute-start | bytes 245768 | tf_op jit(solution)/shard_map/ppermute | solution.py:47
  44.3 5.3 %collective-permute-start.7 = (bf16[64,640]{1,0:T(8,128)(2,1)S(1)}, bf16[64,640]{1,0:T(8,128)(2,1)S(1)}, u32[]{:S(2)}, u32[]{:S(2)}) collective-permute-start(bf16[64,640]{1,0:T(8,128)(2,1)S(1)} %get-tuple-element.64.refs_0_), channel_id=1, source_target_pairs={{0,8},{1,9},{2,10},{3,11},{4,12},{5,13},{6,14},{7,15},{8,0},{9,1},... | collective-permute-start | bytes 245768 | tf_op jit(solution)/shard_map/ppermute | solution.py:47
  49.7 5.9 %collective-permute-start.12 = (bf16[32,640]{1,0:T(8,128)(2,1)S(1)}, bf16[32,640]{1,0:T(8,128)(2,1)S(1)}, u32[]{:S(2)}, u32[]{:S(2)}) collective-permute-start(bf16[32,640]{1,0:T(8,128)(2,1)S(1)} %add_convert_fusion), channel_id=1, source_target_pairs={{0,24},{1,25},{2,26},{3,27},{4,28},{5,29},{6,30},{7,31},{8,16},{9,... | collective-permute-start | bytes 122888 | tf_op jit(solution)/shard_map/ppermute | solution.py:47
  52.3 5.0 %collective-permute-start.11 = (bf16[32,640]{1,0:T(8,128)(2,1)S(1)}, bf16[32,640]{1,0:T(8,128)(2,1)S(1)}, u32[]{:S(2)}, u32[]{:S(2)}) collective-permute-start(bf16[32,640]{1,0:T(8,128)(2,1)S(1)} %add_convert_fusion), channel_id=1, source_target_pairs={{0,16},{1,17},{2,18},{3,19},{4,20},{5,21},{6,22},{7,23},{8,24},{9,... | collective-permute-start | bytes 122888 | tf_op jit(solution)/shard_map/ppermute | solution.py:47
  52.3 5.0 %collective-permute-start.10 = (bf16[32,640]{1,0:T(8,128)(2,1)S(1)}, bf16[32,640]{1,0:T(8,128)(2,1)S(1)}, u32[]{:S(2)}, u32[]{:S(2)}) collective-permute-start(bf16[32,640]{1,0:T(8,128)(2,1)S(1)} %add_convert_fusion), channel_id=1, source_target_pairs={{0,8},{1,9},{2,10},{3,11},{4,12},{5,13},{6,14},{7,15},{8,0},{9,1},... | collective-permute-start | bytes 122888 | tf_op jit(solution)/shard_map/ppermute | solution.py:47
  57.3 16.3 %collective-permute-start.17 = (bf16[1,272,1024]{2,1,0:T(8,128)(2,1)S(1)}, bf16[1,272,1024]{2,1,0:T(8,128)(2,1)S(1)}, u32[]{:S(2)}, u32[]{:S(2)}) collective-permute-start(bf16[1,272,1024]{2,1,0:T(8,128)(2,1)S(1)} %collective-permute-done.6.refs_3_), channel_id=1, source_target_pairs={{0,8},{1,9},{2,10},{3,11},{4,12},{5,13},{6,14},{7,15},{8,0},{9,1},... | collective-permute-start | bytes 1671176 | tf_op jit(solution)/shard_map/ppermute | solution.py:47
  64.8 7.0 %collective-permute-start.16 = (bf16[128,640]{1,0:T(8,128)(2,1)S(1)}, bf16[128,640]{1,0:T(8,128)(2,1)S(1)}, u32[]{:S(2)}, u32[]{:S(2)}) collective-permute-start(bf16[128,640]{1,0:T(8,128)(2,1)S(1)} %pad_maximum_fusion.2), channel_id=1, source_target_pairs={{0,6},{1,7},{2,4},{3,5},{4,2},{5,3},{6,0},{7,1},{8,14},{9,15},{10,... | collective-permute-start | bytes 491528 | tf_op jit(solution)/shard_map/ppermute | solution.py:47
  66.3 7.3 %collective-permute-start.15 = (bf16[128,640]{1,0:T(8,128)(2,1)S(1)}, bf16[128,640]{1,0:T(8,128)(2,1)S(1)}, u32[]{:S(2)}, u32[]{:S(2)}) collective-permute-start(bf16[128,640]{1,0:T(8,128)(2,1)S(1)} %pad_maximum_fusion.2), channel_id=1, source_target_pairs={{0,4},{1,5},{2,6},{3,7},{4,0},{5,1},{6,2},{7,3},{8,12},{9,13},{10,... | collective-permute-start | bytes 491528 | tf_op jit(solution)/shard_map/ppermute | solution.py:47
  67.8 5.8 %collective-permute-start.14 = (bf16[128,640]{1,0:T(8,128)(2,1)S(1)}, bf16[128,640]{1,0:T(8,128)(2,1)S(1)}, u32[]{:S(2)}, u32[]{:S(2)}) collective-permute-start(bf16[128,640]{1,0:T(8,128)(2,1)S(1)} %pad_maximum_fusion.2), channel_id=1, source_target_pairs={{0,2},{1,3},{2,0},{3,1},{4,6},{5,7},{6,4},{7,5},{8,10},{9,11},{10,... | collective-permute-start | bytes 491528 | tf_op jit(solution)/shard_map/ppermute | solution.py:47
  73.6 2.2 %collective-permute-start.18 = (bf16[16,32,640]{2,1,0:T(8,128)(2,1)S(1)}, bf16[16,32,640]{2,1,0:T(8,128)(2,1)S(1)}, u32[]{:S(2)}, u32[]{:S(2)}) collective-permute-start(bf16[16,32,640]{2,1,0:T(8,128)(2,1)S(1)} %bitcast.7), channel_id=1, source_target_pairs={{0,1},{1,0},{2,3},{3,2},{4,5},{5,4},{6,7},{7,6},{8,9},{9,8},{10,11... | collective-permute-start | bytes 1966088 | tf_op jit(solution)/shard_map/ppermute | solution.py:47
  73.7 19.8 %collective-permute-start.19 = (bf16[1,272,1024]{2,1,0:T(8,128)(2,1)S(1)}, bf16[1,272,1024]{2,1,0:T(8,128)(2,1)S(1)}, u32[]{:S(2)}, u32[]{:S(2)}) collective-permute-start(bf16[1,272,1024]{2,1,0:T(8,128)(2,1)S(1)} %collective-permute-done.17.refs_5_), channel_id=1, source_target_pairs={{0,4},{1,5},{2,6},{3,7},{4,0},{5,1},{6,2},{7,3},{8,12},{9,13},{10,... | collective-permute-start | bytes 1671176 | tf_op jit(solution)/shard_map/ppermute | solution.py:47
  75.8 20.2 %collective-permute-start.20 = (bf16[256,512]{1,0:T(8,128)(2,1)S(1)}, bf16[256,512]{1,0:T(8,128)(2,1)S(1)}, u32[]{:S(2)}, u32[]{:S(2)}) collective-permute-start(bf16[256,512]{1,0:T(8,128)(2,1)S(1)} %get-tuple-element.91), channel_id=1, source_target_pairs={{0,16},{1,17},{2,18},{3,19},{4,20},{5,21},{6,22},{7,23},{8,24},{9,... | collective-permute-start | bytes 786440 | tf_op jit(solution)/shard_map/ppermute | solution.py:47
  77.6 19.5 %collective-permute-start.21 = (bf16[256,512]{1,0:T(8,128)(2,1)S(1)}, bf16[256,512]{1,0:T(8,128)(2,1)S(1)}, u32[]{:S(2)}, u32[]{:S(2)}) collective-permute-start(bf16[256,512]{1,0:T(8,128)(2,1)S(1)} %get-tuple-element.92), channel_id=1, source_target_pairs={{0,8},{1,9},{2,10},{3,11},{4,12},{5,13},{6,14},{7,15},{8,0},{9,1},... | collective-permute-start | bytes 786440 | tf_op jit(solution)/shard_map/ppermute | solution.py:47
  81.5 36.2 %collective-permute-start.22 = (bf16[256,512]{1,0:T(8,128)(2,1)S(1)}, bf16[256,512]{1,0:T(8,128)(2,1)S(1)}, u32[]{:S(2)}, u32[]{:S(2)}) collective-permute-start(bf16[256,512]{1,0:T(8,128)(2,1)S(1)} %get-tuple-element.93), channel_id=1, source_target_pairs={{0,24},{1,25},{2,26},{3,27},{4,28},{5,29},{6,30},{7,31},{8,16},{9,... | collective-permute-start | bytes 786440 | tf_op jit(solution)/shard_map/ppermute | solution.py:47
  81.5 38.5 %collective-permute-start.23 = (bf16[256,512]{1,0:T(8,128)(2,1)S(1)}, bf16[256,512]{1,0:T(8,128)(2,1)S(1)}, u32[]{:S(2)}, u32[]{:S(2)}) collective-permute-start(bf16[256,512]{1,0:T(8,128)(2,1)S(1)} %get-tuple-element.94), channel_id=1, source_target_pairs={{0,20},{1,21},{2,22},{3,23},{4,16},{5,17},{6,18},{7,19},{8,28},{9,... | collective-permute-start | bytes 786440 | tf_op jit(solution)/shard_map/ppermute | solution.py:47
  93.5 26.4 %collective-permute-start.24 = (bf16[256,512]{1,0:T(8,128)(2,1)S(1)}, bf16[256,512]{1,0:T(8,128)(2,1)S(1)}, u32[]{:S(2)}, u32[]{:S(2)}) collective-permute-start(bf16[256,512]{1,0:T(8,128)(2,1)S(1)} %get-tuple-element.95), channel_id=1, source_target_pairs={{0,28},{1,29},{2,30},{3,31},{4,24},{5,25},{6,26},{7,27},{8,20},{9,... | collective-permute-start | bytes 786440 | tf_op jit(solution)/shard_map/ppermute | solution.py:47
  95.9 24.1 %collective-permute-start.25 = (bf16[256,512]{1,0:T(8,128)(2,1)S(1)}, bf16[256,512]{1,0:T(8,128)(2,1)S(1)}, u32[]{:S(2)}, u32[]{:S(2)}) collective-permute-start(bf16[256,512]{1,0:T(8,128)(2,1)S(1)} %get-tuple-element.96), channel_id=1, source_target_pairs={{0,4},{1,5},{2,6},{3,7},{4,0},{5,1},{6,2},{7,3},{8,12},{9,13},{10,... | collective-permute-start | bytes 786440 | tf_op jit(solution)/shard_map/ppermute | solution.py:47
  97.1 23.0 %collective-permute-start.26 = (bf16[256,512]{1,0:T(8,128)(2,1)S(1)}, bf16[256,512]{1,0:T(8,128)(2,1)S(1)}, u32[]{:S(2)}, u32[]{:S(2)}) collective-permute-start(bf16[256,512]{1,0:T(8,128)(2,1)S(1)} %get-tuple-element.97), channel_id=1, source_target_pairs={{0,12},{1,13},{2,14},{3,15},{4,8},{5,9},{6,10},{7,11},{8,4},{9,5},... | collective-permute-start | bytes 786440 | tf_op jit(solution)/shard_map/ppermute | solution.py:47
  121.9 2.5 %collective-permute-start.28 = (bf16[128,1024]{1,0:T(8,128)(2,1)S(1)}, bf16[128,1024]{1,0:T(8,128)(2,1)S(1)}, u32[]{:S(2)}, u32[]{:S(2)}) collective-permute-start(bf16[128,1024]{1,0:T(8,128)(2,1)S(1)} %get-tuple-element.101), channel_id=1, source_target_pairs={{0,1},{1,0},{2,3},{3,2},{4,5},{5,4},{6,7},{7,6},{8,9},{9,8},{10,11... | collective-permute-start | bytes 786440 | tf_op jit(solution)/shard_map/ppermute | solution.py:47
  123.8 2.1 %collective-permute-start.27 = (bf16[128,1024]{1,0:T(8,128)(2,1)S(1)}, bf16[128,1024]{1,0:T(8,128)(2,1)S(1)}, u32[]{:S(2)}, u32[]{:S(2)}) collective-permute-start(bf16[128,1024]{1,0:T(8,128)(2,1)S(1)} %get-tuple-element.99), channel_id=1, source_target_pairs={{0,1},{1,0},{2,3},{3,2},{4,5},{5,4},{6,7},{7,6},{8,9},{9,8},{10,11... | collective-permute-start | bytes 786440 | tf_op jit(solution)/shard_map/ppermute | solution.py:47
  124.4 8.3 %collective-permute-start.29 = (bf16[128,1024]{1,0:T(8,128)(2,1)S(1)}, bf16[128,1024]{1,0:T(8,128)(2,1)S(1)}, u32[]{:S(2)}, u32[]{:S(2)}) collective-permute-start(bf16[128,1024]{1,0:T(8,128)(2,1)S(1)} %join.1), channel_id=1, source_target_pairs={{0,2},{1,3},{2,0},{3,1},{4,6},{5,7},{6,4},{7,5},{8,10},{9,11},{10,... | collective-permute-start | bytes 786440 | tf_op jit(solution)/shard_map/ppermute | solution.py:47

commit v15 on v14

--- a/solution.py
+++ b/solution.py
@@ -636,7 +636,7 @@
             *sends, block_near, block_far = lax.optimization_barrier(
                 (*sends, block_near, block_far)
             )
-            pair_x = xor_permute(jnp.concatenate([block_far, block_near]), by_x)
+            far_x = xor_permute(block_far, by_x)
         arrived = [xor_permute(piece, (r + 1) << low) for r, piece in enumerate(sends)]
         sent = sends[0]
         stages.append((low, count))
@@ -657,18 +657,19 @@
     for number, (low, count) in enumerate(reversed(stages)):
         if direct and number == 1:
             part, block_far = lax.optimization_barrier((part, block_far))
-            block_far_near = xor_permute(block_far, by_near)
-            part, pair_x = lax.optimization_barrier((part, pair_x))
+            far_near = xor_permute(block_far, by_near)
+            part, far_x = lax.optimization_barrier((part, far_x))
         part = jnp.concatenate(
             [part] + [xor_permute(part, r << low) for r in range(1, count)], axis=0
         )
     part = part.reshape(-1, size, part.shape[1])
     if direct:
-        part, block_far_near, ids = lax.optimization_barrier((part, block_far_near, ids))
+        part, far_near, block_near, ids = lax.optimization_barrier(
+            (part, far_near, block_near, ids)
+        )
+        near_x = xor_permute(block_near, by_x)
+        far_near_x = xor_permute(far_near, by_x)
         slices = cut(ids, features, groups)
-        far_near_x = xor_permute(block_far_near, by_x)
-        blocks = [block, block_x, block_near, block_far, pair_x, block_far_near, far_near_x]
-        order = [0, 1, 2, 4, 5, 3, 6, 7]
     else:
         order = slice_order = list(range(groups))
         blocks = [
@@ -677,10 +678,14 @@
     other = xor_permute(part, 1)
     if direct:
         other, *slices = lax.optimization_barrier((other, *slices))
-        slice_order = [0, 4, 2, 6, 5, 7, 1, 3]
+        slice_order = [0, 2, 4, 6, 5, 7, 1, 3]
         slices = [xor_permute(slices[k], k * shares) if k else slices[k] for k in slice_order]
 
     whitener, mean = whiten(ids, part, other, sums, seen, tuple(stages), rows, embed)
+    if direct:
+        mean, near_x = lax.optimization_barrier((mean, near_x))
+        blocks = [block, block_x, block_near, near_x, block_far, far_x, far_near, far_near_x]
+        order = list(range(groups))
     loss, grad = contrast(ids, blocks, order, mean, whitener)
     pieces = []
     for mask in reversed(range(0, shares, 2)):

time: 137 us -> 139 us (1.015); the launches traced: 134 us -> 139 us
  starting transfers between devices: 40.3 us -> 44.2 us
    ppermute x30 -> x31, starting transfers between devices: 40.3 us -> 44.2 us  [xor_permute(): return lax.ppermute(piece, AXES, [(i, i ^ mask) for i in range(devices)])]
    ppermute x30 -> x31, waiting for transfers between devices: 48.4 us -> 49.2 us  [xor_permute(): return lax.ppermute(piece, AXES, [(i, i ^ mask) for i in range(devices)])]
  transfers between devices with their start and end apart: 30 -> 31, of which waited for: 18 -> 16; matrix products, arithmetic and copies ran while one was open for 0% -> 0% of each run, Pallas kernels for 25% -> 24%
where the time goes in v15:
time: 139 us
  waiting for transfers between devices  49.2 us (35%)
  starting transfers between devices  44.2 us (32%)
  Pallas kernels  43.3 us (31%)
    ppermute x31, waiting for transfers between devices, xor_permute(): return lax.ppermute(piece, AXES, [(i, i ^ mask) for i in range(devices)])  49.2 us
    ppermute x31, starting transfers between devices, xor_permute(): return lax.ppermute(piece, AXES, [(i, i ^ mask) for i in range(devices)])  44.2 us
    pallas_call x1, Pallas kernels, contrast(): pl.pallas_call(functools.partial(contrast_kernel, order), in_specs=[smem(...  19.6 us
    pallas_call x1, Pallas kernels, whiten(): pl.pallas_call(make_whiten_kernel(rows, count, stages), in_specs=[smem()]...  10.2 us
    pallas_call x1, Pallas kernels, project(): pl.pallas_call(project_kernel, in_specs=[smem(), smem(), hbm, hbm, hbm],...  6.05 us
    pallas_call x2, Pallas kernels, weight_pieces(): pl.pallas_call(functools.partial(pieces_kernel, share, masks, order), in_...  3.68 us
  transfers between devices with their start and end apart: 31, of which 16 were waited for; matrix products, arithmetic and copies ran while one was open for 0% of the time, Pallas kernels for 24%

profile of v15, /device:TPU:0, one launch (start us, length us, event | category | flops | bytes accessed | tf_op | source)
XLA Modules:
  0.0 139.0 jit_solution(4558234675884389895)
XLA Ops:
  0.6 0.1 pad_add_fusion.ids_ref
  0.7 0.7 copy-done.1
  1.4 0.7 copy-done.2
  2.1 6.1 %project.1 = (bf16[272,1024]{1,0:T(8,128)(2,1)S(1)}, bf16[528,640]{1,0:T(8,128)(2,1)S(1)}, f32[512,640]{1,0:T(8,128)S(1)}) custom-call(s32[3]{0:T(128)S(1)} %pad_add_fusion.ids_ref, s32[1,4]{1,0:T(1,128)S(1)} %copy-done.2, bf16[256,4096]{1,0:T(8,128)(2,1)} %features_hbm.3, bf16[4096,1024]{1,0:T(8,128)(2,1)} %weight_hbm.1, s32[4,256]{1,0:T(4,128)S(1)} %bitcast.9), custom_call_target="tpu_custom_call" | custom-call | flops 2147483648 | bytes 8388608 | tf_op jit(solution)/shard_map/project/pallas_call | solution.py:186
  8.1 0.5 collective-permute-start
  8.6 2.6 %collective-permute-start.1 = (bf16[1,272,1024]{2,1,0:T(8,128)(2,1)S(1)}, bf16[1,272,1024]{2,1,0:T(8,128)(2,1)S(1)}, u32[]{:S(2)}, u32[]{:S(2)}) collective-permute-start(bf16[1,272,1024]{2,1,0:T(8,128)(2,1)S(1)} %bitcast.10), channel_id=1, source_target_pairs={{0,4},{1,5},{2,6},{3,7},{4,0},{5,1},{6,2},{7,3},{8,12},{9,13},{10,... | collective-permute-start | bytes 1671176 | tf_op jit(solution)/shard_map/ppermute | solution.py:47
  11.2 2.6 %collective-permute-start.6 = (bf16[1,272,1024]{2,1,0:T(8,128)(2,1)S(1)}, bf16[1,272,1024]{2,1,0:T(8,128)(2,1)S(1)}, u32[]{:S(2)}, u32[]{:S(2)}) collective-permute-start(bf16[1,272,1024]{2,1,0:T(8,128)(2,1)S(1)} %bitcast.11), channel_id=1, source_target_pairs={{0,16},{1,17},{2,18},{3,19},{4,20},{5,21},{6,22},{7,23},{8,24},{9,... | collective-permute-start | bytes 1671176 | tf_op jit(solution)/shard_map/ppermute | solution.py:47
  13.8 1.6 %collective-permute-start.5 = (bf16[1,272,1024]{2,1,0:T(8,128)(2,1)S(1)}, bf16[1,272,1024]{2,1,0:T(8,128)(2,1)S(1)}, u32[]{:S(2)}, u32[]{:S(2)}) collective-permute-start(bf16[1,272,1024]{2,1,0:T(8,128)(2,1)S(1)} %bitcast.12), channel_id=1, source_target_pairs={{0,8},{1,9},{2,10},{3,11},{4,12},{5,13},{6,14},{7,15},{8,0},{9,1},... | collective-permute-start | bytes 1671176 | tf_op jit(solution)/shard_map/ppermute | solution.py:47
  15.4 9.1 %collective-permute-done.1.refs_1_ = bf16[1,272,1024]{2,1,0:T(8,128)(2,1)S(1)} collective-permute-done((bf16[1,272,1024]{2,1,0:T(8,128)(2,1)S(1)}, bf16[1,272,1024]{2,1,0:T(8,128)(2,1)S(1)}, u32[]{:S(2)}, u32[]{:S(2)}) %collective-permute-start.1) | collective-permute-done | bytes 557088 | tf_op jit(solution)/shard_map/ppermute | solution.py:47
  24.4 0.7 stage.2
  25.1 1.8 %collective-permute-start.3 = (bf16[144,640]{1,0:T(8,128)(2,1)S(1)}, bf16[144,640]{1,0:T(8,128)(2,1)S(1)}, u32[]{:S(2)}, u32[]{:S(2)}) collective-permute-start(bf16[144,640]{1,0:T(8,128)(2,1)S(1)} %get-tuple-element.61), channel_id=1, source_target_pairs={{0,4},{1,5},{2,6},{3,7},{4,0},{5,1},{6,2},{7,3},{8,12},{9,13},{10,... | collective-permute-start | bytes 552968 | tf_op jit(solution)/shard_map/ppermute | solution.py:47
  26.9 1.5 %collective-permute-start.4 = (bf16[144,640]{1,0:T(8,128)(2,1)S(1)}, bf16[144,640]{1,0:T(8,128)(2,1)S(1)}, u32[]{:S(2)}, u32[]{:S(2)}) collective-permute-start(bf16[144,640]{1,0:T(8,128)(2,1)S(1)} %get-tuple-element.62), channel_id=1, source_target_pairs={{0,6},{1,7},{2,4},{3,5},{4,2},{5,3},{6,0},{7,1},{8,14},{9,15},{10,... | collective-permute-start | bytes 552968 | tf_op jit(solution)/shard_map/ppermute | solution.py:47
  28.4 0.2 collective-permute-start.2
  28.7 4.0 %collective-permute-done.3.refs_1_ = bf16[144,640]{1,0:T(8,128)(2,1)S(1)} collective-permute-done((bf16[144,640]{1,0:T(8,128)(2,1)S(1)}, bf16[144,640]{1,0:T(8,128)(2,1)S(1)}, u32[]{:S(2)}, u32[]{:S(2)}) %collective-permute-start.3) | collective-permute-done | bytes 184352 | tf_op jit(solution)/shard_map/ppermute | solution.py:47
  32.7 4.0 %collective-permute-done.4.refs_2_ = bf16[144,640]{1,0:T(8,128)(2,1)S(1)} collective-permute-done((bf16[144,640]{1,0:T(8,128)(2,1)S(1)}, bf16[144,640]{1,0:T(8,128)(2,1)S(1)}, u32[]{:S(2)}, u32[]{:S(2)}) %collective-permute-start.4) | collective-permute-done | bytes 184352 | tf_op jit(solution)/shard_map/ppermute | solution.py:47
  36.7 1.4 collective-permute-done.2.refs_0_
  38.0 0.6 stage.3
  38.7 0.2 collective-permute-done.6.refs_4_
  38.8 0.2 collective-permute-done.5.refs_2_
  39.0 2.3 %collective-permute-start.8 = (bf16[64,640]{1,0:T(8,128)(2,1)S(1)}, bf16[64,640]{1,0:T(8,128)(2,1)S(1)}, u32[]{:S(2)}, u32[]{:S(2)}) collective-permute-start(bf16[64,640]{1,0:T(8,128)(2,1)S(1)} %get-tuple-element.68), channel_id=1, source_target_pairs={{0,16},{1,17},{2,18},{3,19},{4,20},{5,21},{6,22},{7,23},{8,24},{9,... | collective-permute-start | bytes 245768 | tf_op jit(solution)/shard_map/ppermute | solution.py:47
  41.4 1.5 %collective-permute-start.9 = (bf16[64,640]{1,0:T(8,128)(2,1)S(1)}, bf16[64,640]{1,0:T(8,128)(2,1)S(1)}, u32[]{:S(2)}, u32[]{:S(2)}) collective-permute-start(bf16[64,640]{1,0:T(8,128)(2,1)S(1)} %get-tuple-element.69), channel_id=1, source_target_pairs={{0,24},{1,25},{2,26},{3,27},{4,28},{5,29},{6,30},{7,31},{8,16},{9,... | collective-permute-start | bytes 245768 | tf_op jit(solution)/shard_map/ppermute | solution.py:47
  42.8 0.1 collective-permute-start.7
  42.9 1.5 %collective-permute-start.13 = (bf16[1,272,1024]{2,1,0:T(8,128)(2,1)S(1)}, bf16[1,272,1024]{2,1,0:T(8,128)(2,1)S(1)}, u32[]{:S(2)}, u32[]{:S(2)}) collective-permute-start(bf16[1,272,1024]{2,1,0:T(8,128)(2,1)S(1)} %collective-permute-done.6.refs_4_), channel_id=1, source_target_pairs={{0,4},{1,5},{2,6},{3,7},{4,0},{5,1},{6,2},{7,3},{8,12},{9,13},{10,... | collective-permute-start | bytes 1671176 | tf_op jit(solution)/shard_map/ppermute | solution.py:47
  44.4 3.9 %collective-permute-done.8.refs_2_ = bf16[64,640]{1,0:T(8,128)(2,1)S(1)} collective-permute-done((bf16[64,640]{1,0:T(8,128)(2,1)S(1)}, bf16[64,640]{1,0:T(8,128)(2,1)S(1)}, u32[]{:S(2)}, u32[]{:S(2)}) %collective-permute-start.8) | collective-permute-done | bytes 81952 | tf_op jit(solution)/shard_map/ppermute | solution.py:47
  48.3 0.0 collective-permute-done.9.refs_3_
  48.3 0.4 collective-permute-done.7.refs_1_
  48.7 2.6 %collective-permute-start.12 = (bf16[32,640]{1,0:T(8,128)(2,1)S(1)}, bf16[32,640]{1,0:T(8,128)(2,1)S(1)}, u32[]{:S(2)}, u32[]{:S(2)}) collective-permute-start(bf16[32,640]{1,0:T(8,128)(2,1)S(1)} %add_convert_fusion), channel_id=1, source_target_pairs={{0,24},{1,25},{2,26},{3,27},{4,28},{5,29},{6,30},{7,31},{8,16},{9,... | collective-permute-start | bytes 122888 | tf_op jit(solution)/shard_map/ppermute | solution.py:47
  51.3 0.1 collective-permute-start.11
  51.4 1.8 %collective-permute-start.10 = (bf16[32,640]{1,0:T(8,128)(2,1)S(1)}, bf16[32,640]{1,0:T(8,128)(2,1)S(1)}, u32[]{:S(2)}, u32[]{:S(2)}) collective-permute-start(bf16[32,640]{1,0:T(8,128)(2,1)S(1)} %add_convert_fusion), channel_id=1, source_target_pairs={{0,8},{1,9},{2,10},{3,11},{4,12},{5,13},{6,14},{7,15},{8,0},{9,1},... | collective-permute-start | bytes 122888 | tf_op jit(solution)/shard_map/ppermute | solution.py:47
  53.1 1.6 %collective-permute-done.12 = bf16[32,640]{1,0:T(8,128)(2,1)S(1)} collective-permute-done((bf16[32,640]{1,0:T(8,128)(2,1)S(1)}, bf16[32,640]{1,0:T(8,128)(2,1)S(1)}, u32[]{:S(2)}, u32[]{:S(2)}) %collective-permute-start.12) | collective-permute-done | bytes 40992 | tf_op jit(solution)/shard_map/ppermute | solution.py:47
  54.7 1.8 %collective-permute-done.11 = bf16[32,640]{1,0:T(8,128)(2,1)S(1)} collective-permute-done((bf16[32,640]{1,0:T(8,128)(2,1)S(1)}, bf16[32,640]{1,0:T(8,128)(2,1)S(1)}, u32[]{:S(2)}, u32[]{:S(2)}) %collective-permute-start.11) | collective-permute-done | bytes 40992 | tf_op jit(solution)/shard_map/ppermute | solution.py:47
  56.6 0.9 collective-permute-start.17
  57.4 1.5 %collective-permute-start.16 = (bf16[128,640]{1,0:T(8,128)(2,1)S(1)}, bf16[128,640]{1,0:T(8,128)(2,1)S(1)}, u32[]{:S(2)}, u32[]{:S(2)}) collective-permute-start(bf16[128,640]{1,0:T(8,128)(2,1)S(1)} %pad_maximum_fusion.1), channel_id=1, source_target_pairs={{0,6},{1,7},{2,4},{3,5},{4,2},{5,3},{6,0},{7,1},{8,14},{9,15},{10,... | collective-permute-start | bytes 491528 | tf_op jit(solution)/shard_map/ppermute | solution.py:47
  58.9 1.1 collective-permute-start.15
  60.1 0.9 collective-permute-start.14
  60.9 3.1 %collective-permute-done.16 = bf16[128,640]{1,0:T(8,128)(2,1)S(1)} collective-permute-done((bf16[128,640]{1,0:T(8,128)(2,1)S(1)}, bf16[128,640]{1,0:T(8,128)(2,1)S(1)}, u32[]{:S(2)}, u32[]{:S(2)}) %collective-permute-start.16) | collective-permute-done | bytes 163872 | tf_op jit(solution)/shard_map/ppermute | solution.py:47
  64.0 1.9 %collective-permute-done.15 = bf16[128,640]{1,0:T(8,128)(2,1)S(1)} collective-permute-done((bf16[128,640]{1,0:T(8,128)(2,1)S(1)}, bf16[128,640]{1,0:T(8,128)(2,1)S(1)}, u32[]{:S(2)}, u32[]{:S(2)}) %collective-permute-start.15) | collective-permute-done | bytes 163872 | tf_op jit(solution)/shard_map/ppermute | solution.py:47
  65.9 0.1 pad_maximum_fusion
  66.0 2.4 %collective-permute-done.17.refs_6_ = bf16[1,272,1024]{2,1,0:T(8,128)(2,1)S(1)} collective-permute-done((bf16[1,272,1024]{2,1,0:T(8,128)(2,1)S(1)}, bf16[1,272,1024]{2,1,0:T(8,128)(2,1)S(1)}, u32[]{:S(2)}, u32[]{:S(2)}) %collective-permute-start.17) | collective-permute-done | bytes 557088 | tf_op jit(solution)/shard_map/ppermute | solution.py:47
  68.3 0.0 collective-permute-start.18
  68.3 0.3 collective-permute-start.19
  68.6 1.7 %collective-permute-start.20 = (bf16[1,272,1024]{2,1,0:T(8,128)(2,1)S(1)}, bf16[1,272,1024]{2,1,0:T(8,128)(2,1)S(1)}, u32[]{:S(2)}, u32[]{:S(2)}) collective-permute-start(bf16[1,272,1024]{2,1,0:T(8,128)(2,1)S(1)} %collective-permute-done.17.refs_6_), channel_id=1, source_target_pairs={{0,4},{1,5},{2,6},{3,7},{4,0},{5,1},{6,2},{7,3},{8,12},{9,13},{10,... | collective-permute-start | bytes 1671176 | tf_op jit(solution)/shard_map/ppermute | solution.py:47
  70.4 0.8 cut.1
  71.2 0.0 collective-permute-done.18.far_ref
  71.2 0.8 collective-permute-start.21
  72.0 1.8 %collective-permute-start.22 = (bf16[256,512]{1,0:T(8,128)(2,1)S(1)}, bf16[256,512]{1,0:T(8,128)(2,1)S(1)}, u32[]{:S(2)}, u32[]{:S(2)}) collective-permute-start(bf16[256,512]{1,0:T(8,128)(2,1)S(1)} %get-tuple-element.98), channel_id=1, source_target_pairs={{0,16},{1,17},{2,18},{3,19},{4,20},{5,21},{6,22},{7,23},{8,24},{9,... | collective-permute-start | bytes 786440 | tf_op jit(solution)/shard_map/ppermute | solution.py:47
  73.8 1.8 %collective-permute-start.23 = (bf16[256,512]{1,0:T(8,128)(2,1)S(1)}, bf16[256,512]{1,0:T(8,128)(2,1)S(1)}, u32[]{:S(2)}, u32[]{:S(2)}) collective-permute-start(bf16[256,512]{1,0:T(8,128)(2,1)S(1)} %get-tuple-element.99), channel_id=1, source_target_pairs={{0,24},{1,25},{2,26},{3,27},{4,28},{5,29},{6,30},{7,31},{8,16},{9,... | collective-permute-start | bytes 786440 | tf_op jit(solution)/shard_map/ppermute | solution.py:47
  75.7 10.2 %whiten.1 = (bf16[1024,1024]{1,0:T(8,128)(2,1)S(1)}, f32[1,1024]{1,0:T(1,128)S(1)}) custom-call(s32[3]{0:T(128)S(1)} %pad_add_fusion.ids_ref, bf16[16,32,640]{2,1,0:T(8,128)(2,1)S(1)} %bitcast.8, bf16[16,32,640]{2,1,0:T(8,128)(2,1)S(1)} %collective-permute-done.18.far_ref, bf16[64,640]{1,0:T(8,128)(2,1)S(1)} %get-tuple-element.67.refs_0_, ...), custom_call_target="tpu_custom_call" | custom-call | flops 10737418240 | bytes 2097152 | tf_op jit(solution)/shard_map/whiten/pallas_call | solution.py:396
  85.9 0.7 collective-permute-start.24
  86.6 8.8 %collective-permute-done.20.refs_7_ = bf16[1,272,1024]{2,1,0:T(8,128)(2,1)S(1)} collective-permute-done((bf16[1,272,1024]{2,1,0:T(8,128)(2,1)S(1)}, bf16[1,272,1024]{2,1,0:T(8,128)(2,1)S(1)}, u32[]{:S(2)}, u32[]{:S(2)}) %collective-permute-start.20) | collective-permute-done | bytes 557088 | tf_op jit(solution)/shard_map/ppermute | solution.py:47
  95.3 2.1 %collective-permute-start.25 = (bf16[256,512]{1,0:T(8,128)(2,1)S(1)}, bf16[256,512]{1,0:T(8,128)(2,1)S(1)}, u32[]{:S(2)}, u32[]{:S(2)}) collective-permute-start(bf16[256,512]{1,0:T(8,128)(2,1)S(1)} %get-tuple-element.101), channel_id=1, source_target_pairs={{0,28},{1,29},{2,30},{3,31},{4,24},{5,25},{6,26},{7,27},{8,20},{9,... | collective-permute-start | bytes 786440 | tf_op jit(solution)/shard_map/ppermute | solution.py:47
  97.4 0.0 collective-permute-done.21.refs_1_
  97.4 1.4 %collective-permute-start.26 = (bf16[256,512]{1,0:T(8,128)(2,1)S(1)}, bf16[256,512]{1,0:T(8,128)(2,1)S(1)}, u32[]{:S(2)}, u32[]{:S(2)}) collective-permute-start(bf16[256,512]{1,0:T(8,128)(2,1)S(1)} %get-tuple-element.102), channel_id=1, source_target_pairs={{0,4},{1,5},{2,6},{3,7},{4,0},{5,1},{6,2},{7,3},{8,12},{9,13},{10,... | collective-permute-start | bytes 786440 | tf_op jit(solution)/shard_map/ppermute | solution.py:47
  98.8 0.2 collective-permute-done.22.refs_2_
  99.0 5.5 %collective-permute-start.27 = (bf16[256,512]{1,0:T(8,128)(2,1)S(1)}, bf16[256,512]{1,0:T(8,128)(2,1)S(1)}, u32[]{:S(2)}, u32[]{:S(2)}) collective-permute-start(bf16[256,512]{1,0:T(8,128)(2,1)S(1)} %get-tuple-element.103), channel_id=1, source_target_pairs={{0,12},{1,13},{2,14},{3,15},{4,8},{5,9},{6,10},{7,11},{8,4},{9,5},... | collective-permute-start | bytes 786440 | tf_op jit(solution)/shard_map/ppermute | solution.py:47
  104.5 19.6 %contrast.1 = (f32[1,256]{1,0:T(1,128)}, bf16[8,256,1024]{2,1,0:T(8,128)(2,1)S(1)}) custom-call(s32[3]{0:T(128)S(1)} %pad_add_fusion.ids_ref, f32[1,1024]{1,0:T(1,128)S(1)} %get-tuple-element.88.mean_ref, bf16[1024,1024]{1,0:T(8,128)(2,1)S(1)} %get-tuple-element.89.whitener_ref.refs_3_, bf16[1,272,1024]{2,1,0:T(8,128)(2,1)S(1)} %bitcast.13, ...), custom_call_target="tpu_custom_call" | custom-call | flops 12884901888 | bytes 8388608 | tf_op jit(solution)/shard_map/contrast/pallas_call | solution.py:488
  124.1 0.0 collective-permute-done.25.refs_5_
  124.2 1.9 %weight_pieces.3 = (f32[128,1024]{1,0:T(8,128)S(1)}, bf16[128,1024]{1,0:T(8,128)(2,1)S(1)}) custom-call(s32[3]{0:T(128)S(1)} %pad_add_fusion.ids_ref, bf16[8,256,1024]{2,1,0:T(8,128)(2,1)S(1)} %get-tuple-element.95.grad_ref, bf16[256,512]{1,0:T(8,128)(2,1)S(1)} %get-tuple-element.96.refs_0_, bf16[256,512]{1,0:T(8,128)(2,1)S(1)} %collective-permute-done.21.refs_1_, ...), custom_call_target="tpu_custom_call" | custom-call | flops 1073741824 | bytes 6291456 | tf_op jit(solution)/shard_map/weight_pieces/pallas_call | solution.py:539
  126.0 0.1 collective-permute-start.29
  126.1 1.8 %weight_pieces.2 = (f32[128,1024]{1,0:T(8,128)S(1)}, bf16[128,1024]{1,0:T(8,128)(2,1)S(1)}) custom-call(s32[3]{0:T(128)S(1)} %pad_add_fusion.ids_ref, bf16[8,256,1024]{2,1,0:T(8,128)(2,1)S(1)} %get-tuple-element.95.grad_ref, bf16[256,512]{1,0:T(8,128)(2,1)S(1)} %get-tuple-element.96.refs_0_, bf16[256,512]{1,0:T(8,128)(2,1)S(1)} %collective-permute-done.21.refs_1_, ...), custom_call_target="tpu_custom_call" | custom-call | flops 1073741824 | bytes 6291456 | tf_op jit(solution)/shard_map/weight_pieces/pallas_call | solution.py:539
  127.9 0.6 collective-permute-start.28
  128.6 2.4 %collective-permute-start.30 = (bf16[128,1024]{1,0:T(8,128)(2,1)S(1)}, bf16[128,1024]{1,0:T(8,128)(2,1)S(1)}, u32[]{:S(2)}, u32[]{:S(2)}) collective-permute-start(bf16[128,1024]{1,0:T(8,128)(2,1)S(1)} %join.1), channel_id=1, source_target_pairs={{0,2},{1,3},{2,0},{3,1},{4,6},{5,7},{6,4},{7,5},{8,10},{9,11},{10,... | collective-permute-start | bytes 786440 | tf_op jit(solution)/shard_map/ppermute | solution.py:47
  130.9 6.5 %collective-permute-done.30.refs_2_ = bf16[128,1024]{1,0:T(8,128)(2,1)S(1)} collective-permute-done((bf16[128,1024]{1,0:T(8,128)(2,1)S(1)}, bf16[128,1024]{1,0:T(8,128)(2,1)S(1)}, u32[]{:S(2)}, u32[]{:S(2)}) %collective-permute-start.30) | collective-permute-done | bytes 262176 | tf_op jit(solution)/shard_map/ppermute | solution.py:47
  137.4 1.5 %finish.1 = f32[128,1024]{1,0:T(8,128)} custom-call(f32[128,1024]{1,0:T(8,128)S(1)} %get-tuple-element.104.refs_0_, bf16[128,1024]{1,0:T(8,128)(2,1)S(1)} %collective-permute-done.28.refs_1_, bf16[128,1024]{1,0:T(8,128)(2,1)S(1)} %collective-permute-done.30.refs_2_, bf16[1024,1024]{1,0:T(8,128)(2,1)S(1)} %get-tuple-element.89.whitener_ref.refs_3_), custom_call_target="tpu_custom_call" | custom-call | tf_op jit(solution)/shard_map/finish/pallas_call | solution.py:584
  (18 shorter events, 0.1 us)
Async XLA Ops:
  0.7 0.7 copy-start.1
  1.4 0.7 copy-start.2
  8.1 16.3 %collective-permute-start = (bf16[528,640]{1,0:T(8,128)(2,1)S(1)}, bf16[528,640]{1,0:T(8,128)(2,1)S(1)}, u32[]{:S(2)}, u32[]{:S(2)}) collective-permute-start(bf16[528,640]{1,0:T(8,128)(2,1)S(1)} %get-tuple-element.56.sent_ref), channel_id=1, source_target_pairs={{0,1},{1,0},{2,3},{3,2},{4,5},{5,4},{6,7},{7,6},{8,9},{9,8},{10,11... | collective-permute-start | bytes 2027528 | tf_op jit(solution)/shard_map/ppermute | solution.py:47
  8.6 15.8 %collective-permute-start.1 = (bf16[1,272,1024]{2,1,0:T(8,128)(2,1)S(1)}, bf16[1,272,1024]{2,1,0:T(8,128)(2,1)S(1)}, u32[]{:S(2)}, u32[]{:S(2)}) collective-permute-start(bf16[1,272,1024]{2,1,0:T(8,128)(2,1)S(1)} %bitcast.10), channel_id=1, source_target_pairs={{0,4},{1,5},{2,6},{3,7},{4,0},{5,1},{6,2},{7,3},{8,12},{9,13},{10,... | collective-permute-start | bytes 1671176 | tf_op jit(solution)/shard_map/ppermute | solution.py:47
  11.2 27.6 %collective-permute-start.6 = (bf16[1,272,1024]{2,1,0:T(8,128)(2,1)S(1)}, bf16[1,272,1024]{2,1,0:T(8,128)(2,1)S(1)}, u32[]{:S(2)}, u32[]{:S(2)}) collective-permute-start(bf16[1,272,1024]{2,1,0:T(8,128)(2,1)S(1)} %bitcast.11), channel_id=1, source_target_pairs={{0,16},{1,17},{2,18},{3,19},{4,20},{5,21},{6,22},{7,23},{8,24},{9,... | collective-permute-start | bytes 1671176 | tf_op jit(solution)/shard_map/ppermute | solution.py:47
  13.8 25.2 %collective-permute-start.5 = (bf16[1,272,1024]{2,1,0:T(8,128)(2,1)S(1)}, bf16[1,272,1024]{2,1,0:T(8,128)(2,1)S(1)}, u32[]{:S(2)}, u32[]{:S(2)}) collective-permute-start(bf16[1,272,1024]{2,1,0:T(8,128)(2,1)S(1)} %bitcast.12), channel_id=1, source_target_pairs={{0,8},{1,9},{2,10},{3,11},{4,12},{5,13},{6,14},{7,15},{8,0},{9,1},... | collective-permute-start | bytes 1671176 | tf_op jit(solution)/shard_map/ppermute | solution.py:47
  25.1 7.6 %collective-permute-start.3 = (bf16[144,640]{1,0:T(8,128)(2,1)S(1)}, bf16[144,640]{1,0:T(8,128)(2,1)S(1)}, u32[]{:S(2)}, u32[]{:S(2)}) collective-permute-start(bf16[144,640]{1,0:T(8,128)(2,1)S(1)} %get-tuple-element.61), channel_id=1, source_target_pairs={{0,4},{1,5},{2,6},{3,7},{4,0},{5,1},{6,2},{7,3},{8,12},{9,13},{10,... | collective-permute-start | bytes 552968 | tf_op jit(solution)/shard_map/ppermute | solution.py:47
  26.9 9.7 %collective-permute-start.4 = (bf16[144,640]{1,0:T(8,128)(2,1)S(1)}, bf16[144,640]{1,0:T(8,128)(2,1)S(1)}, u32[]{:S(2)}, u32[]{:S(2)}) collective-permute-start(bf16[144,640]{1,0:T(8,128)(2,1)S(1)} %get-tuple-element.62), channel_id=1, source_target_pairs={{0,6},{1,7},{2,4},{3,5},{4,2},{5,3},{6,0},{7,1},{8,14},{9,15},{10,... | collective-permute-start | bytes 552968 | tf_op jit(solution)/shard_map/ppermute | solution.py:47
  28.4 9.6 %collective-permute-start.2 = (bf16[144,640]{1,0:T(8,128)(2,1)S(1)}, bf16[144,640]{1,0:T(8,128)(2,1)S(1)}, u32[]{:S(2)}, u32[]{:S(2)}) collective-permute-start(bf16[144,640]{1,0:T(8,128)(2,1)S(1)} %get-tuple-element.60.sent_ref), channel_id=1, source_target_pairs={{0,2},{1,3},{2,0},{3,1},{4,6},{5,7},{6,4},{7,5},{8,10},{9,11},{10,... | collective-permute-start | bytes 552968 | tf_op jit(solution)/shard_map/ppermute | solution.py:47
  38.0 32.3 %copy-start = (bf16[256,4096]{1,0:T(8,128)(2,1)S(1)}, bf16[256,4096]{1,0:T(8,128)(2,1)}, u32[]{:S(2)}) copy-start(bf16[256,4096]{1,0:T(8,128)(2,1)} %features_hbm.3) | copy-start | bytes 6291460
  39.0 9.3 %collective-permute-start.8 = (bf16[64,640]{1,0:T(8,128)(2,1)S(1)}, bf16[64,640]{1,0:T(8,128)(2,1)S(1)}, u32[]{:S(2)}, u32[]{:S(2)}) collective-permute-start(bf16[64,640]{1,0:T(8,128)(2,1)S(1)} %get-tuple-element.68), channel_id=1, source_target_pairs={{0,16},{1,17},{2,18},{3,19},{4,20},{5,21},{6,22},{7,23},{8,24},{9,... | collective-permute-start | bytes 245768 | tf_op jit(solution)/shard_map/ppermute | solution.py:47
  41.4 6.9 %collective-permute-start.9 = (bf16[64,640]{1,0:T(8,128)(2,1)S(1)}, bf16[64,640]{1,0:T(8,128)(2,1)S(1)}, u32[]{:S(2)}, u32[]{:S(2)}) collective-permute-start(bf16[64,640]{1,0:T(8,128)(2,1)S(1)} %get-tuple-element.69), channel_id=1, source_target_pairs={{0,24},{1,25},{2,26},{3,27},{4,28},{5,29},{6,30},{7,31},{8,16},{9,... | collective-permute-start | bytes 245768 | tf_op jit(solution)/shard_map/ppermute | solution.py:47
  42.8 5.8 %collective-permute-start.7 = (bf16[64,640]{1,0:T(8,128)(2,1)S(1)}, bf16[64,640]{1,0:T(8,128)(2,1)S(1)}, u32[]{:S(2)}, u32[]{:S(2)}) collective-permute-start(bf16[64,640]{1,0:T(8,128)(2,1)S(1)} %get-tuple-element.67.refs_0_), channel_id=1, source_target_pairs={{0,8},{1,9},{2,10},{3,11},{4,12},{5,13},{6,14},{7,15},{8,0},{9,1},... | collective-permute-start | bytes 245768 | tf_op jit(solution)/shard_map/ppermute | solution.py:47
  42.9 14.5 %collective-permute-start.13 = (bf16[1,272,1024]{2,1,0:T(8,128)(2,1)S(1)}, bf16[1,272,1024]{2,1,0:T(8,128)(2,1)S(1)}, u32[]{:S(2)}, u32[]{:S(2)}) collective-permute-start(bf16[1,272,1024]{2,1,0:T(8,128)(2,1)S(1)} %collective-permute-done.6.refs_4_), channel_id=1, source_target_pairs={{0,4},{1,5},{2,6},{3,7},{4,0},{5,1},{6,2},{7,3},{8,12},{9,13},{10,... | collective-permute-start | bytes 1671176 | tf_op jit(solution)/shard_map/ppermute | solution.py:47
  48.7 6.1 %collective-permute-start.12 = (bf16[32,640]{1,0:T(8,128)(2,1)S(1)}, bf16[32,640]{1,0:T(8,128)(2,1)S(1)}, u32[]{:S(2)}, u32[]{:S(2)}) collective-permute-start(bf16[32,640]{1,0:T(8,128)(2,1)S(1)} %add_convert_fusion), channel_id=1, source_target_pairs={{0,24},{1,25},{2,26},{3,27},{4,28},{5,29},{6,30},{7,31},{8,16},{9,... | collective-permute-start | bytes 122888 | tf_op jit(solution)/shard_map/ppermute | solution.py:47
  51.3 5.3 %collective-permute-start.11 = (bf16[32,640]{1,0:T(8,128)(2,1)S(1)}, bf16[32,640]{1,0:T(8,128)(2,1)S(1)}, u32[]{:S(2)}, u32[]{:S(2)}) collective-permute-start(bf16[32,640]{1,0:T(8,128)(2,1)S(1)} %add_convert_fusion), channel_id=1, source_target_pairs={{0,16},{1,17},{2,18},{3,19},{4,20},{5,21},{6,22},{7,23},{8,24},{9,... | collective-permute-start | bytes 122888 | tf_op jit(solution)/shard_map/ppermute | solution.py:47
  51.4 5.2 %collective-permute-start.10 = (bf16[32,640]{1,0:T(8,128)(2,1)S(1)}, bf16[32,640]{1,0:T(8,128)(2,1)S(1)}, u32[]{:S(2)}, u32[]{:S(2)}) collective-permute-start(bf16[32,640]{1,0:T(8,128)(2,1)S(1)} %add_convert_fusion), channel_id=1, source_target_pairs={{0,8},{1,9},{2,10},{3,11},{4,12},{5,13},{6,14},{7,15},{8,0},{9,1},... | collective-permute-start | bytes 122888 | tf_op jit(solution)/shard_map/ppermute | solution.py:47
  56.6 11.8 %collective-permute-start.17 = (bf16[1,272,1024]{2,1,0:T(8,128)(2,1)S(1)}, bf16[1,272,1024]{2,1,0:T(8,128)(2,1)S(1)}, u32[]{:S(2)}, u32[]{:S(2)}) collective-permute-start(bf16[1,272,1024]{2,1,0:T(8,128)(2,1)S(1)} %collective-permute-done.6.refs_4_), channel_id=1, source_target_pairs={{0,8},{1,9},{2,10},{3,11},{4,12},{5,13},{6,14},{7,15},{8,0},{9,1},... | collective-permute-start | bytes 1671176 | tf_op jit(solution)/shard_map/ppermute | solution.py:47
  57.4 6.6 %collective-permute-start.16 = (bf16[128,640]{1,0:T(8,128)(2,1)S(1)}, bf16[128,640]{1,0:T(8,128)(2,1)S(1)}, u32[]{:S(2)}, u32[]{:S(2)}) collective-permute-start(bf16[128,640]{1,0:T(8,128)(2,1)S(1)} %pad_maximum_fusion.1), channel_id=1, source_target_pairs={{0,6},{1,7},{2,4},{3,5},{4,2},{5,3},{6,0},{7,1},{8,14},{9,15},{10,... | collective-permute-start | bytes 491528 | tf_op jit(solution)/shard_map/ppermute | solution.py:47
  58.9 7.0 %collective-permute-start.15 = (bf16[128,640]{1,0:T(8,128)(2,1)S(1)}, bf16[128,640]{1,0:T(8,128)(2,1)S(1)}, u32[]{:S(2)}, u32[]{:S(2)}) collective-permute-start(bf16[128,640]{1,0:T(8,128)(2,1)S(1)} %pad_maximum_fusion.1), channel_id=1, source_target_pairs={{0,4},{1,5},{2,6},{3,7},{4,0},{5,1},{6,2},{7,3},{8,12},{9,13},{10,... | collective-permute-start | bytes 491528 | tf_op jit(solution)/shard_map/ppermute | solution.py:47
  60.1 5.8 %collective-permute-start.14 = (bf16[128,640]{1,0:T(8,128)(2,1)S(1)}, bf16[128,640]{1,0:T(8,128)(2,1)S(1)}, u32[]{:S(2)}, u32[]{:S(2)}) collective-permute-start(bf16[128,640]{1,0:T(8,128)(2,1)S(1)} %pad_maximum_fusion.1), channel_id=1, source_target_pairs={{0,2},{1,3},{2,0},{3,1},{4,6},{5,7},{6,4},{7,5},{8,10},{9,11},{10,... | collective-permute-start | bytes 491528 | tf_op jit(solution)/shard_map/ppermute | solution.py:47
  68.3 2.9 %collective-permute-start.18 = (bf16[16,32,640]{2,1,0:T(8,128)(2,1)S(1)}, bf16[16,32,640]{2,1,0:T(8,128)(2,1)S(1)}, u32[]{:S(2)}, u32[]{:S(2)}) collective-permute-start(bf16[16,32,640]{2,1,0:T(8,128)(2,1)S(1)} %bitcast.7), channel_id=1, source_target_pairs={{0,1},{1,0},{2,3},{3,2},{4,5},{5,4},{6,7},{7,6},{8,9},{9,8},{10,11... | collective-permute-start | bytes 1966088 | tf_op jit(solution)/shard_map/ppermute | solution.py:47
  68.3 17.5 %collective-permute-start.19 = (bf16[1,272,1024]{2,1,0:T(8,128)(2,1)S(1)}, bf16[1,272,1024]{2,1,0:T(8,128)(2,1)S(1)}, u32[]{:S(2)}, u32[]{:S(2)}) collective-permute-start(bf16[1,272,1024]{2,1,0:T(8,128)(2,1)S(1)} %collective-permute-done.5.refs_2_), channel_id=1, source_target_pairs={{0,4},{1,5},{2,6},{3,7},{4,0},{5,1},{6,2},{7,3},{8,12},{9,13},{10,... | collective-permute-start | bytes 1671176 | tf_op jit(solution)/shard_map/ppermute | solution.py:47
  68.6 26.7 %collective-permute-start.20 = (bf16[1,272,1024]{2,1,0:T(8,128)(2,1)S(1)}, bf16[1,272,1024]{2,1,0:T(8,128)(2,1)S(1)}, u32[]{:S(2)}, u32[]{:S(2)}) collective-permute-start(bf16[1,272,1024]{2,1,0:T(8,128)(2,1)S(1)} %collective-permute-done.17.refs_6_), channel_id=1, source_target_pairs={{0,4},{1,5},{2,6},{3,7},{4,0},{5,1},{6,2},{7,3},{8,12},{9,13},{10,... | collective-permute-start | bytes 1671176 | tf_op jit(solution)/shard_map/ppermute | solution.py:47
  71.2 26.2 %collective-permute-start.21 = (bf16[256,512]{1,0:T(8,128)(2,1)S(1)}, bf16[256,512]{1,0:T(8,128)(2,1)S(1)}, u32[]{:S(2)}, u32[]{:S(2)}) collective-permute-start(bf16[256,512]{1,0:T(8,128)(2,1)S(1)} %get-tuple-element.97), channel_id=1, source_target_pairs={{0,8},{1,9},{2,10},{3,11},{4,12},{5,13},{6,14},{7,15},{8,0},{9,1},... | collective-permute-start | bytes 786440 | tf_op jit(solution)/shard_map/ppermute | solution.py:47
  72.0 27.0 %collective-permute-start.22 = (bf16[256,512]{1,0:T(8,128)(2,1)S(1)}, bf16[256,512]{1,0:T(8,128)(2,1)S(1)}, u32[]{:S(2)}, u32[]{:S(2)}) collective-permute-start(bf16[256,512]{1,0:T(8,128)(2,1)S(1)} %get-tuple-element.98), channel_id=1, source_target_pairs={{0,16},{1,17},{2,18},{3,19},{4,20},{5,21},{6,22},{7,23},{8,24},{9,... | collective-permute-start | bytes 786440 | tf_op jit(solution)/shard_map/ppermute | solution.py:47
  73.8 50.3 %collective-permute-start.23 = (bf16[256,512]{1,0:T(8,128)(2,1)S(1)}, bf16[256,512]{1,0:T(8,128)(2,1)S(1)}, u32[]{:S(2)}, u32[]{:S(2)}) collective-permute-start(bf16[256,512]{1,0:T(8,128)(2,1)S(1)} %get-tuple-element.99), channel_id=1, source_target_pairs={{0,24},{1,25},{2,26},{3,27},{4,28},{5,29},{6,30},{7,31},{8,16},{9,... | collective-permute-start | bytes 786440 | tf_op jit(solution)/shard_map/ppermute | solution.py:47
  85.9 38.2 %collective-permute-start.24 = (bf16[256,512]{1,0:T(8,128)(2,1)S(1)}, bf16[256,512]{1,0:T(8,128)(2,1)S(1)}, u32[]{:S(2)}, u32[]{:S(2)}) collective-permute-start(bf16[256,512]{1,0:T(8,128)(2,1)S(1)} %get-tuple-element.100), channel_id=1, source_target_pairs={{0,20},{1,21},{2,22},{3,23},{4,16},{5,17},{6,18},{7,19},{8,28},{9,... | collective-permute-start | bytes 786440 | tf_op jit(solution)/shard_map/ppermute | solution.py:47
  95.3 28.8 %collective-permute-start.25 = (bf16[256,512]{1,0:T(8,128)(2,1)S(1)}, bf16[256,512]{1,0:T(8,128)(2,1)S(1)}, u32[]{:S(2)}, u32[]{:S(2)}) collective-permute-start(bf16[256,512]{1,0:T(8,128)(2,1)S(1)} %get-tuple-element.101), channel_id=1, source_target_pairs={{0,28},{1,29},{2,30},{3,31},{4,24},{5,25},{6,26},{7,27},{8,20},{9,... | collective-permute-start | bytes 786440 | tf_op jit(solution)/shard_map/ppermute | solution.py:47
  97.4 26.8 %collective-permute-start.26 = (bf16[256,512]{1,0:T(8,128)(2,1)S(1)}, bf16[256,512]{1,0:T(8,128)(2,1)S(1)}, u32[]{:S(2)}, u32[]{:S(2)}) collective-permute-start(bf16[256,512]{1,0:T(8,128)(2,1)S(1)} %get-tuple-element.102), channel_id=1, source_target_pairs={{0,4},{1,5},{2,6},{3,7},{4,0},{5,1},{6,2},{7,3},{8,12},{9,13},{10,... | collective-permute-start | bytes 786440 | tf_op jit(solution)/shard_map/ppermute | solution.py:47
  99.0 25.2 %collective-permute-start.27 = (bf16[256,512]{1,0:T(8,128)(2,1)S(1)}, bf16[256,512]{1,0:T(8,128)(2,1)S(1)}, u32[]{:S(2)}, u32[]{:S(2)}) collective-permute-start(bf16[256,512]{1,0:T(8,128)(2,1)S(1)} %get-tuple-element.103), channel_id=1, source_target_pairs={{0,12},{1,13},{2,14},{3,15},{4,8},{5,9},{6,10},{7,11},{8,4},{9,5},... | collective-permute-start | bytes 786440 | tf_op jit(solution)/shard_map/ppermute | solution.py:47
  126.0 2.5 %collective-permute-start.29 = (bf16[128,1024]{1,0:T(8,128)(2,1)S(1)}, bf16[128,1024]{1,0:T(8,128)(2,1)S(1)}, u32[]{:S(2)}, u32[]{:S(2)}) collective-permute-start(bf16[128,1024]{1,0:T(8,128)(2,1)S(1)} %get-tuple-element.107), channel_id=1, source_target_pairs={{0,1},{1,0},{2,3},{3,2},{4,5},{5,4},{6,7},{7,6},{8,9},{9,8},{10,11... | collective-permute-start | bytes 786440 | tf_op jit(solution)/shard_map/ppermute | solution.py:47
  127.9 3.0 %collective-permute-start.28 = (bf16[128,1024]{1,0:T(8,128)(2,1)S(1)}, bf16[128,1024]{1,0:T(8,128)(2,1)S(1)}, u32[]{:S(2)}, u32[]{:S(2)}) collective-permute-start(bf16[128,1024]{1,0:T(8,128)(2,1)S(1)} %get-tuple-element.105), channel_id=1, source_target_pairs={{0,1},{1,0},{2,3},{3,2},{4,5},{5,4},{6,7},{7,6},{8,9},{9,8},{10,11... | collective-permute-start | bytes 786440 | tf_op jit(solution)/shard_map/ppermute | solution.py:47
  128.6 8.9 %collective-permute-start.30 = (bf16[128,1024]{1,0:T(8,128)(2,1)S(1)}, bf16[128,1024]{1,0:T(8,128)(2,1)S(1)}, u32[]{:S(2)}, u32[]{:S(2)}) collective-permute-start(bf16[128,1024]{1,0:T(8,128)(2,1)S(1)} %join.1), channel_id=1, source_target_pairs={{0,2},{1,3},{2,0},{3,1},{4,6},{5,7},{6,4},{7,5},{8,10},{9,11},{10,... | collective-permute-start | bytes 786440 | tf_op jit(solution)/shard_map/ppermute | solution.py:47

commit v16 on v15

--- a/solution.py
+++ b/solution.py
@@ -668,7 +668,6 @@
             (part, far_near, block_near, ids)
         )
         near_x = xor_permute(block_near, by_x)
-        far_near_x = xor_permute(far_near, by_x)
         slices = cut(ids, features, groups)
     else:
         order = slice_order = list(range(groups))
@@ -679,7 +678,14 @@
     if direct:
         other, *slices = lax.optimization_barrier((other, *slices))
         slice_order = [0, 2, 4, 6, 5, 7, 1, 3]
-        slices = [xor_permute(slices[k], k * shares) if k else slices[k] for k in slice_order]
+        for k in (2, 4, 6, 5):
+            slices[k] = xor_permute(slices[k], k * shares)
+        for k, before in ((7, 2), (1, 4)):
+            slices[k], slices[before] = lax.optimization_barrier((slices[k], slices[before]))
+            slices[k] = xor_permute(slices[k], k * shares)
+        slices[3] = xor_permute(slices[3], 3 * shares)
+        slices = [slices[k] for k in slice_order]
+        far_near_x = xor_permute(far_near, by_x)
 
     whitener, mean = whiten(ids, part, other, sums, seen, tuple(stages), rows, embed)
     if direct:

time: 139 us -> 140 us (level); the launches traced: 139 us -> 137 us
  starting transfers between devices: 44.2 us -> 42 us
    ppermute x31, starting transfers between devices: 44.2 us -> 42 us  [xor_permute(): return lax.ppermute(piece, AXES, [(i, i ^ mask) for i in range(devices)])]
  transfers between devices with their start and end apart: 31 -> 31, of which waited for: 16 -> 15; matrix products, arithmetic and copies ran while one was open for 0% -> 0% of each run, Pallas kernels for 24% -> 25%
where the time goes in v16:
time: 140 us; the launch traced here: 137 us
  waiting for transfers between devices  49.9 us (36%)
  Pallas kernels  43.3 us (31%)
  starting transfers between devices  42 us (30%)
    ppermute x31, waiting for transfers between devices, xor_permute(): return lax.ppermute(piece, AXES, [(i, i ^ mask) for i in range(devices)])  49.9 us
    ppermute x31, starting transfers between devices, xor_permute(): return lax.ppermute(piece, AXES, [(i, i ^ mask) for i in range(devices)])  42 us
    pallas_call x1, Pallas kernels, contrast(): pl.pallas_call(functools.partial(contrast_kernel, order), in_specs=[smem(...  19.6 us
    pallas_call x1, Pallas kernels, whiten(): pl.pallas_call(make_whiten_kernel(rows, count, stages), in_specs=[smem()]...  10.2 us
    pallas_call x1, Pallas kernels, project(): pl.pallas_call(project_kernel, in_specs=[smem(), smem(), hbm, hbm, hbm],...  6.05 us
    pallas_call x2, Pallas kernels, weight_pieces(): pl.pallas_call(functools.partial(pieces_kernel, share, masks, order), in_...  3.68 us
  transfers between devices with their start and end apart: 31, of which 15 were waited for; matrix products, arithmetic and copies ran while one was open for 0% of the time, Pallas kernels for 25%

profile of v16, /device:TPU:0, one launch (start us, length us, event | category | flops | bytes accessed | tf_op | source)
XLA Modules:
  0.0 137.5 jit_solution(3365122698677258734)
XLA Ops:
  0.6 0.1 pad_add_fusion.ids_ref
  0.7 0.7 copy-done.1
  1.4 0.7 copy-done.2
  2.1 6.1 %project.1 = (bf16[272,1024]{1,0:T(8,128)(2,1)S(1)}, bf16[528,640]{1,0:T(8,128)(2,1)S(1)}, f32[512,640]{1,0:T(8,128)S(1)}) custom-call(s32[3]{0:T(128)S(1)} %pad_add_fusion.ids_ref, s32[1,4]{1,0:T(1,128)S(1)} %copy-done.2, bf16[256,4096]{1,0:T(8,128)(2,1)} %features_hbm.3, bf16[4096,1024]{1,0:T(8,128)(2,1)} %weight_hbm.1, s32[4,256]{1,0:T(4,128)S(1)} %bitcast.9), custom_call_target="tpu_custom_call" | custom-call | flops 2147483648 | bytes 8388608 | tf_op jit(solution)/shard_map/project/pallas_call | solution.py:186
  8.1 0.5 collective-permute-start
  8.6 2.6 %collective-permute-start.1 = (bf16[1,272,1024]{2,1,0:T(8,128)(2,1)S(1)}, bf16[1,272,1024]{2,1,0:T(8,128)(2,1)S(1)}, u32[]{:S(2)}, u32[]{:S(2)}) collective-permute-start(bf16[1,272,1024]{2,1,0:T(8,128)(2,1)S(1)} %bitcast.10), channel_id=1, source_target_pairs={{0,4},{1,5},{2,6},{3,7},{4,0},{5,1},{6,2},{7,3},{8,12},{9,13},{10,... | collective-permute-start | bytes 1671176 | tf_op jit(solution)/shard_map/ppermute | solution.py:47
  11.2 2.6 %collective-permute-start.6 = (bf16[1,272,1024]{2,1,0:T(8,128)(2,1)S(1)}, bf16[1,272,1024]{2,1,0:T(8,128)(2,1)S(1)}, u32[]{:S(2)}, u32[]{:S(2)}) collective-permute-start(bf16[1,272,1024]{2,1,0:T(8,128)(2,1)S(1)} %bitcast.11), channel_id=1, source_target_pairs={{0,16},{1,17},{2,18},{3,19},{4,20},{5,21},{6,22},{7,23},{8,24},{9,... | collective-permute-start | bytes 1671176 | tf_op jit(solution)/shard_map/ppermute | solution.py:47
  13.8 1.6 %collective-permute-start.5 = (bf16[1,272,1024]{2,1,0:T(8,128)(2,1)S(1)}, bf16[1,272,1024]{2,1,0:T(8,128)(2,1)S(1)}, u32[]{:S(2)}, u32[]{:S(2)}) collective-permute-start(bf16[1,272,1024]{2,1,0:T(8,128)(2,1)S(1)} %bitcast.12), channel_id=1, source_target_pairs={{0,8},{1,9},{2,10},{3,11},{4,12},{5,13},{6,14},{7,15},{8,0},{9,1},... | collective-permute-start | bytes 1671176 | tf_op jit(solution)/shard_map/ppermute | solution.py:47
  15.4 9.1 %collective-permute-done.1.refs_1_ = bf16[1,272,1024]{2,1,0:T(8,128)(2,1)S(1)} collective-permute-done((bf16[1,272,1024]{2,1,0:T(8,128)(2,1)S(1)}, bf16[1,272,1024]{2,1,0:T(8,128)(2,1)S(1)}, u32[]{:S(2)}, u32[]{:S(2)}) %collective-permute-start.1) | collective-permute-done | bytes 557088 | tf_op jit(solution)/shard_map/ppermute | solution.py:47
  24.4 0.7 stage.2
  25.1 1.8 %collective-permute-start.3 = (bf16[144,640]{1,0:T(8,128)(2,1)S(1)}, bf16[144,640]{1,0:T(8,128)(2,1)S(1)}, u32[]{:S(2)}, u32[]{:S(2)}) collective-permute-start(bf16[144,640]{1,0:T(8,128)(2,1)S(1)} %get-tuple-element.65), channel_id=1, source_target_pairs={{0,4},{1,5},{2,6},{3,7},{4,0},{5,1},{6,2},{7,3},{8,12},{9,13},{10,... | collective-permute-start | bytes 552968 | tf_op jit(solution)/shard_map/ppermute | solution.py:47
  26.9 1.5 %collective-permute-start.4 = (bf16[144,640]{1,0:T(8,128)(2,1)S(1)}, bf16[144,640]{1,0:T(8,128)(2,1)S(1)}, u32[]{:S(2)}, u32[]{:S(2)}) collective-permute-start(bf16[144,640]{1,0:T(8,128)(2,1)S(1)} %get-tuple-element.66), channel_id=1, source_target_pairs={{0,6},{1,7},{2,4},{3,5},{4,2},{5,3},{6,0},{7,1},{8,14},{9,15},{10,... | collective-permute-start | bytes 552968 | tf_op jit(solution)/shard_map/ppermute | solution.py:47
  28.4 0.2 collective-permute-start.2
  28.7 4.0 %collective-permute-done.3.refs_1_ = bf16[144,640]{1,0:T(8,128)(2,1)S(1)} collective-permute-done((bf16[144,640]{1,0:T(8,128)(2,1)S(1)}, bf16[144,640]{1,0:T(8,128)(2,1)S(1)}, u32[]{:S(2)}, u32[]{:S(2)}) %collective-permute-start.3) | collective-permute-done | bytes 184352 | tf_op jit(solution)/shard_map/ppermute | solution.py:47
  32.7 4.0 %collective-permute-done.4.refs_2_ = bf16[144,640]{1,0:T(8,128)(2,1)S(1)} collective-permute-done((bf16[144,640]{1,0:T(8,128)(2,1)S(1)}, bf16[144,640]{1,0:T(8,128)(2,1)S(1)}, u32[]{:S(2)}, u32[]{:S(2)}) %collective-permute-start.4) | collective-permute-done | bytes 184352 | tf_op jit(solution)/shard_map/ppermute | solution.py:47
  36.7 1.4 collective-permute-done.2.refs_0_
  38.0 0.6 stage.3
  38.7 0.2 collective-permute-done.6.refs_4_
  38.8 0.2 collective-permute-done.5.refs_2_
  39.0 2.3 %collective-permute-start.8 = (bf16[64,640]{1,0:T(8,128)(2,1)S(1)}, bf16[64,640]{1,0:T(8,128)(2,1)S(1)}, u32[]{:S(2)}, u32[]{:S(2)}) collective-permute-start(bf16[64,640]{1,0:T(8,128)(2,1)S(1)} %get-tuple-element.72), channel_id=1, source_target_pairs={{0,16},{1,17},{2,18},{3,19},{4,20},{5,21},{6,22},{7,23},{8,24},{9,... | collective-permute-start | bytes 245768 | tf_op jit(solution)/shard_map/ppermute | solution.py:47
  41.4 1.5 %collective-permute-start.9 = (bf16[64,640]{1,0:T(8,128)(2,1)S(1)}, bf16[64,640]{1,0:T(8,128)(2,1)S(1)}, u32[]{:S(2)}, u32[]{:S(2)}) collective-permute-start(bf16[64,640]{1,0:T(8,128)(2,1)S(1)} %get-tuple-element.73), channel_id=1, source_target_pairs={{0,24},{1,25},{2,26},{3,27},{4,28},{5,29},{6,30},{7,31},{8,16},{9,... | collective-permute-start | bytes 245768 | tf_op jit(solution)/shard_map/ppermute | solution.py:47
  42.8 0.1 collective-permute-start.7
  42.9 1.5 %collective-permute-start.13 = (bf16[1,272,1024]{2,1,0:T(8,128)(2,1)S(1)}, bf16[1,272,1024]{2,1,0:T(8,128)(2,1)S(1)}, u32[]{:S(2)}, u32[]{:S(2)}) collective-permute-start(bf16[1,272,1024]{2,1,0:T(8,128)(2,1)S(1)} %collective-permute-done.6.refs_4_), channel_id=1, source_target_pairs={{0,4},{1,5},{2,6},{3,7},{4,0},{5,1},{6,2},{7,3},{8,12},{9,13},{10,... | collective-permute-start | bytes 1671176 | tf_op jit(solution)/shard_map/ppermute | solution.py:47
  44.4 3.9 %collective-permute-done.8.refs_2_ = bf16[64,640]{1,0:T(8,128)(2,1)S(1)} collective-permute-done((bf16[64,640]{1,0:T(8,128)(2,1)S(1)}, bf16[64,640]{1,0:T(8,128)(2,1)S(1)}, u32[]{:S(2)}, u32[]{:S(2)}) %collective-permute-start.8) | collective-permute-done | bytes 81952 | tf_op jit(solution)/shard_map/ppermute | solution.py:47
  48.3 0.4 collective-permute-done.7.refs_1_
  48.7 2.6 %collective-permute-start.12 = (bf16[32,640]{1,0:T(8,128)(2,1)S(1)}, bf16[32,640]{1,0:T(8,128)(2,1)S(1)}, u32[]{:S(2)}, u32[]{:S(2)}) collective-permute-start(bf16[32,640]{1,0:T(8,128)(2,1)S(1)} %add_convert_fusion), channel_id=1, source_target_pairs={{0,24},{1,25},{2,26},{3,27},{4,28},{5,29},{6,30},{7,31},{8,16},{9,... | collective-permute-start | bytes 122888 | tf_op jit(solution)/shard_map/ppermute | solution.py:47
  51.3 0.1 collective-permute-start.11
  51.4 1.8 %collective-permute-start.10 = (bf16[32,640]{1,0:T(8,128)(2,1)S(1)}, bf16[32,640]{1,0:T(8,128)(2,1)S(1)}, u32[]{:S(2)}, u32[]{:S(2)}) collective-permute-start(bf16[32,640]{1,0:T(8,128)(2,1)S(1)} %add_convert_fusion), channel_id=1, source_target_pairs={{0,8},{1,9},{2,10},{3,11},{4,12},{5,13},{6,14},{7,15},{8,0},{9,1},... | collective-permute-start | bytes 122888 | tf_op jit(solution)/shard_map/ppermute | solution.py:47
  53.1 1.6 %collective-permute-done.12 = bf16[32,640]{1,0:T(8,128)(2,1)S(1)} collective-permute-done((bf16[32,640]{1,0:T(8,128)(2,1)S(1)}, bf16[32,640]{1,0:T(8,128)(2,1)S(1)}, u32[]{:S(2)}, u32[]{:S(2)}) %collective-permute-start.12) | collective-permute-done | bytes 40992 | tf_op jit(solution)/shard_map/ppermute | solution.py:47
  54.7 1.8 %collective-permute-done.11 = bf16[32,640]{1,0:T(8,128)(2,1)S(1)} collective-permute-done((bf16[32,640]{1,0:T(8,128)(2,1)S(1)}, bf16[32,640]{1,0:T(8,128)(2,1)S(1)}, u32[]{:S(2)}, u32[]{:S(2)}) %collective-permute-start.11) | collective-permute-done | bytes 40992 | tf_op jit(solution)/shard_map/ppermute | solution.py:47
  56.6 0.9 collective-permute-start.17
  57.4 0.0 collective-permute-done.13.refs_5_
  57.4 1.5 %collective-permute-start.16 = (bf16[128,640]{1,0:T(8,128)(2,1)S(1)}, bf16[128,640]{1,0:T(8,128)(2,1)S(1)}, u32[]{:S(2)}, u32[]{:S(2)}) collective-permute-start(bf16[128,640]{1,0:T(8,128)(2,1)S(1)} %pad_maximum_fusion.1), channel_id=1, source_target_pairs={{0,6},{1,7},{2,4},{3,5},{4,2},{5,3},{6,0},{7,1},{8,14},{9,15},{10,... | collective-permute-start | bytes 491528 | tf_op jit(solution)/shard_map/ppermute | solution.py:47
  58.9 1.1 collective-permute-start.15
  60.1 0.9 collective-permute-start.14
  60.9 3.1 %collective-permute-done.16 = bf16[128,640]{1,0:T(8,128)(2,1)S(1)} collective-permute-done((bf16[128,640]{1,0:T(8,128)(2,1)S(1)}, bf16[128,640]{1,0:T(8,128)(2,1)S(1)}, u32[]{:S(2)}, u32[]{:S(2)}) %collective-permute-start.16) | collective-permute-done | bytes 163872 | tf_op jit(solution)/shard_map/ppermute | solution.py:47
  64.0 1.9 %collective-permute-done.15 = bf16[128,640]{1,0:T(8,128)(2,1)S(1)} collective-permute-done((bf16[128,640]{1,0:T(8,128)(2,1)S(1)}, bf16[128,640]{1,0:T(8,128)(2,1)S(1)}, u32[]{:S(2)}, u32[]{:S(2)}) %collective-permute-start.15) | collective-permute-done | bytes 163872 | tf_op jit(solution)/shard_map/ppermute | solution.py:47
  65.9 0.0 collective-permute-done.14
  65.9 0.1 pad_maximum_fusion
  66.0 2.4 %collective-permute-done.17.refs_6_ = bf16[1,272,1024]{2,1,0:T(8,128)(2,1)S(1)} collective-permute-done((bf16[1,272,1024]{2,1,0:T(8,128)(2,1)S(1)}, bf16[1,272,1024]{2,1,0:T(8,128)(2,1)S(1)}, u32[]{:S(2)}, u32[]{:S(2)}) %collective-permute-start.17) | collective-permute-done | bytes 557088 | tf_op jit(solution)/shard_map/ppermute | solution.py:47
  68.3 0.0 collective-permute-start.18
  68.3 0.3 collective-permute-start.19
  68.6 1.7 %collective-permute-start.20 = (bf16[1,272,1024]{2,1,0:T(8,128)(2,1)S(1)}, bf16[1,272,1024]{2,1,0:T(8,128)(2,1)S(1)}, u32[]{:S(2)}, u32[]{:S(2)}) collective-permute-start(bf16[1,272,1024]{2,1,0:T(8,128)(2,1)S(1)} %collective-permute-done.17.refs_6_), channel_id=1, source_target_pairs={{0,4},{1,5},{2,6},{3,7},{4,0},{5,1},{6,2},{7,3},{8,12},{9,13},{10,... | collective-permute-start | bytes 1671176 | tf_op jit(solution)/shard_map/ppermute | solution.py:47
  70.4 0.8 cut.1
  71.2 0.0 collective-permute-done.18.far_ref
  71.2 0.8 collective-permute-start.21
  72.0 1.8 %collective-permute-start.22 = (bf16[256,512]{1,0:T(8,128)(2,1)S(1)}, bf16[256,512]{1,0:T(8,128)(2,1)S(1)}, u32[]{:S(2)}, u32[]{:S(2)}) collective-permute-start(bf16[256,512]{1,0:T(8,128)(2,1)S(1)} %get-tuple-element.105), channel_id=1, source_target_pairs={{0,16},{1,17},{2,18},{3,19},{4,20},{5,21},{6,22},{7,23},{8,24},{9,... | collective-permute-start | bytes 786440 | tf_op jit(solution)/shard_map/ppermute | solution.py:47
  73.8 1.8 %collective-permute-start.23 = (bf16[256,512]{1,0:T(8,128)(2,1)S(1)}, bf16[256,512]{1,0:T(8,128)(2,1)S(1)}, u32[]{:S(2)}, u32[]{:S(2)}) collective-permute-start(bf16[256,512]{1,0:T(8,128)(2,1)S(1)} %get-tuple-element.107), channel_id=1, source_target_pairs={{0,24},{1,25},{2,26},{3,27},{4,28},{5,29},{6,30},{7,31},{8,16},{9,... | collective-permute-start | bytes 786440 | tf_op jit(solution)/shard_map/ppermute | solution.py:47
  75.7 10.2 %whiten.1 = (bf16[1024,1024]{1,0:T(8,128)(2,1)S(1)}, f32[1,1024]{1,0:T(1,128)S(1)}) custom-call(s32[3]{0:T(128)S(1)} %pad_add_fusion.ids_ref, bf16[16,32,640]{2,1,0:T(8,128)(2,1)S(1)} %bitcast.8, bf16[16,32,640]{2,1,0:T(8,128)(2,1)S(1)} %collective-permute-done.18.far_ref, bf16[64,640]{1,0:T(8,128)(2,1)S(1)} %get-tuple-element.71.refs_0_, ...), custom_call_target="tpu_custom_call" | custom-call | flops 10737418240 | bytes 2097152 | tf_op jit(solution)/shard_map/whiten/pallas_call | solution.py:396
  85.9 0.7 collective-permute-start.24
  86.6 2.9 %collective-permute-start.27 = (bf16[256,512]{1,0:T(8,128)(2,1)S(1)}, bf16[256,512]{1,0:T(8,128)(2,1)S(1)}, u32[]{:S(2)}, u32[]{:S(2)}) collective-permute-start(bf16[256,512]{1,0:T(8,128)(2,1)S(1)} %get-tuple-element.111), channel_id=1, source_target_pairs={{0,12},{1,13},{2,14},{3,15},{4,8},{5,9},{6,10},{7,11},{8,4},{9,5},... | collective-permute-start | bytes 786440 | tf_op jit(solution)/shard_map/ppermute | solution.py:47
  89.4 9.6 %collective-permute-done.22.refs_2_ = bf16[256,512]{1,0:T(8,128)(2,1)S(1)} collective-permute-done((bf16[256,512]{1,0:T(8,128)(2,1)S(1)}, bf16[256,512]{1,0:T(8,128)(2,1)S(1)}, u32[]{:S(2)}, u32[]{:S(2)}) %collective-permute-start.22) | collective-permute-done | bytes 262176 | tf_op jit(solution)/shard_map/ppermute | solution.py:47
  99.0 2.2 %collective-permute-start.25 = (bf16[256,512]{1,0:T(8,128)(2,1)S(1)}, bf16[256,512]{1,0:T(8,128)(2,1)S(1)}, u32[]{:S(2)}, u32[]{:S(2)}) collective-permute-start(bf16[256,512]{1,0:T(8,128)(2,1)S(1)} %get-tuple-element.109), channel_id=1, source_target_pairs={{0,28},{1,29},{2,30},{3,31},{4,24},{5,25},{6,26},{7,27},{8,20},{9,... | collective-permute-start | bytes 786440 | tf_op jit(solution)/shard_map/ppermute | solution.py:47
  101.2 1.8 %collective-permute-start.26 = (bf16[256,512]{1,0:T(8,128)(2,1)S(1)}, bf16[256,512]{1,0:T(8,128)(2,1)S(1)}, u32[]{:S(2)}, u32[]{:S(2)}) collective-permute-start(bf16[256,512]{1,0:T(8,128)(2,1)S(1)} %get-tuple-element.110), channel_id=1, source_target_pairs={{0,4},{1,5},{2,6},{3,7},{4,0},{5,1},{6,2},{7,3},{8,12},{9,13},{10,... | collective-permute-start | bytes 786440 | tf_op jit(solution)/shard_map/ppermute | solution.py:47
  103.0 19.6 %contrast.1 = (f32[1,256]{1,0:T(1,128)}, bf16[8,256,1024]{2,1,0:T(8,128)(2,1)S(1)}) custom-call(s32[3]{0:T(128)S(1)} %pad_add_fusion.ids_ref, f32[1,1024]{1,0:T(1,128)S(1)} %get-tuple-element.92.mean_ref, bf16[1024,1024]{1,0:T(8,128)(2,1)S(1)} %get-tuple-element.93.whitener_ref.refs_3_, bf16[1,272,1024]{2,1,0:T(8,128)(2,1)S(1)} %bitcast.13, ...), custom_call_target="tpu_custom_call" | custom-call | flops 12884901888 | bytes 8388608 | tf_op jit(solution)/shard_map/contrast/pallas_call | solution.py:488
  122.6 0.0 collective-permute-done.24.refs_4_
  122.6 0.0 collective-permute-done.27.refs_7_
  122.7 1.9 %weight_pieces.3 = (f32[128,1024]{1,0:T(8,128)S(1)}, bf16[128,1024]{1,0:T(8,128)(2,1)S(1)}) custom-call(s32[3]{0:T(128)S(1)} %pad_add_fusion.ids_ref, bf16[8,256,1024]{2,1,0:T(8,128)(2,1)S(1)} %get-tuple-element.99.grad_ref, bf16[256,512]{1,0:T(8,128)(2,1)S(1)} %get-tuple-element.100.refs_0_, bf16[256,512]{1,0:T(8,128)(2,1)S(1)} %collective-permute-done.21.refs_1_, ...), custom_call_target="tpu_custom_call" | custom-call | flops 1073741824 | bytes 6291456 | tf_op jit(solution)/shard_map/weight_pieces/pallas_call | solution.py:539
  124.5 0.1 collective-permute-start.29
  124.6 1.8 %weight_pieces.2 = (f32[128,1024]{1,0:T(8,128)S(1)}, bf16[128,1024]{1,0:T(8,128)(2,1)S(1)}) custom-call(s32[3]{0:T(128)S(1)} %pad_add_fusion.ids_ref, bf16[8,256,1024]{2,1,0:T(8,128)(2,1)S(1)} %get-tuple-element.99.grad_ref, bf16[256,512]{1,0:T(8,128)(2,1)S(1)} %get-tuple-element.100.refs_0_, bf16[256,512]{1,0:T(8,128)(2,1)S(1)} %collective-permute-done.21.refs_1_, ...), custom_call_target="tpu_custom_call" | custom-call | flops 1073741824 | bytes 6291456 | tf_op jit(solution)/shard_map/weight_pieces/pallas_call | solution.py:539
  126.4 0.6 collective-permute-start.28
  127.1 2.4 %collective-permute-start.30 = (bf16[128,1024]{1,0:T(8,128)(2,1)S(1)}, bf16[128,1024]{1,0:T(8,128)(2,1)S(1)}, u32[]{:S(2)}, u32[]{:S(2)}) collective-permute-start(bf16[128,1024]{1,0:T(8,128)(2,1)S(1)} %join.1), channel_id=1, source_target_pairs={{0,2},{1,3},{2,0},{3,1},{4,6},{5,7},{6,4},{7,5},{8,10},{9,11},{10,... | collective-permute-start | bytes 786440 | tf_op jit(solution)/shard_map/ppermute | solution.py:47
  129.4 6.5 %collective-permute-done.30.refs_2_ = bf16[128,1024]{1,0:T(8,128)(2,1)S(1)} collective-permute-done((bf16[128,1024]{1,0:T(8,128)(2,1)S(1)}, bf16[128,1024]{1,0:T(8,128)(2,1)S(1)}, u32[]{:S(2)}, u32[]{:S(2)}) %collective-permute-start.30) | collective-permute-done | bytes 262176 | tf_op jit(solution)/shard_map/ppermute | solution.py:47
  135.9 1.5 %finish.1 = f32[128,1024]{1,0:T(8,128)} custom-call(f32[128,1024]{1,0:T(8,128)S(1)} %get-tuple-element.112.refs_0_, bf16[128,1024]{1,0:T(8,128)(2,1)S(1)} %collective-permute-done.28.refs_1_, bf16[128,1024]{1,0:T(8,128)(2,1)S(1)} %collective-permute-done.30.refs_2_, bf16[1024,1024]{1,0:T(8,128)(2,1)S(1)} %get-tuple-element.93.whitener_ref.refs_3_), custom_call_target="tpu_custom_call" | custom-call | tf_op jit(solution)/shard_map/finish/pallas_call | solution.py:584
  (18 shorter events, 0.1 us)
Async XLA Ops:
  0.7 0.7 copy-start.1
  1.4 0.7 copy-start.2
  8.1 16.3 %collective-permute-start = (bf16[528,640]{1,0:T(8,128)(2,1)S(1)}, bf16[528,640]{1,0:T(8,128)(2,1)S(1)}, u32[]{:S(2)}, u32[]{:S(2)}) collective-permute-start(bf16[528,640]{1,0:T(8,128)(2,1)S(1)} %get-tuple-element.60.sent_ref), channel_id=1, source_target_pairs={{0,1},{1,0},{2,3},{3,2},{4,5},{5,4},{6,7},{7,6},{8,9},{9,8},{10,11... | collective-permute-start | bytes 2027528 | tf_op jit(solution)/shard_map/ppermute | solution.py:47
  8.6 15.8 %collective-permute-start.1 = (bf16[1,272,1024]{2,1,0:T(8,128)(2,1)S(1)}, bf16[1,272,1024]{2,1,0:T(8,128)(2,1)S(1)}, u32[]{:S(2)}, u32[]{:S(2)}) collective-permute-start(bf16[1,272,1024]{2,1,0:T(8,128)(2,1)S(1)} %bitcast.10), channel_id=1, source_target_pairs={{0,4},{1,5},{2,6},{3,7},{4,0},{5,1},{6,2},{7,3},{8,12},{9,13},{10,... | collective-permute-start | bytes 1671176 | tf_op jit(solution)/shard_map/ppermute | solution.py:47
  11.2 27.6 %collective-permute-start.6 = (bf16[1,272,1024]{2,1,0:T(8,128)(2,1)S(1)}, bf16[1,272,1024]{2,1,0:T(8,128)(2,1)S(1)}, u32[]{:S(2)}, u32[]{:S(2)}) collective-permute-start(bf16[1,272,1024]{2,1,0:T(8,128)(2,1)S(1)} %bitcast.11), channel_id=1, source_target_pairs={{0,16},{1,17},{2,18},{3,19},{4,20},{5,21},{6,22},{7,23},{8,24},{9,... | collective-permute-start | bytes 1671176 | tf_op jit(solution)/shard_map/ppermute | solution.py:47
  13.8 25.2 %collective-permute-start.5 = (bf16[1,272,1024]{2,1,0:T(8,128)(2,1)S(1)}, bf16[1,272,1024]{2,1,0:T(8,128)(2,1)S(1)}, u32[]{:S(2)}, u32[]{:S(2)}) collective-permute-start(bf16[1,272,1024]{2,1,0:T(8,128)(2,1)S(1)} %bitcast.12), channel_id=1, source_target_pairs={{0,8},{1,9},{2,10},{3,11},{4,12},{5,13},{6,14},{7,15},{8,0},{9,1},... | collective-permute-start | bytes 1671176 | tf_op jit(solution)/shard_map/ppermute | solution.py:47
  25.1 7.6 %collective-permute-start.3 = (bf16[144,640]{1,0:T(8,128)(2,1)S(1)}, bf16[144,640]{1,0:T(8,128)(2,1)S(1)}, u32[]{:S(2)}, u32[]{:S(2)}) collective-permute-start(bf16[144,640]{1,0:T(8,128)(2,1)S(1)} %get-tuple-element.65), channel_id=1, source_target_pairs={{0,4},{1,5},{2,6},{3,7},{4,0},{5,1},{6,2},{7,3},{8,12},{9,13},{10,... | collective-permute-start | bytes 552968 | tf_op jit(solution)/shard_map/ppermute | solution.py:47
  26.9 9.7 %collective-permute-start.4 = (bf16[144,640]{1,0:T(8,128)(2,1)S(1)}, bf16[144,640]{1,0:T(8,128)(2,1)S(1)}, u32[]{:S(2)}, u32[]{:S(2)}) collective-permute-start(bf16[144,640]{1,0:T(8,128)(2,1)S(1)} %get-tuple-element.66), channel_id=1, source_target_pairs={{0,6},{1,7},{2,4},{3,5},{4,2},{5,3},{6,0},{7,1},{8,14},{9,15},{10,... | collective-permute-start | bytes 552968 | tf_op jit(solution)/shard_map/ppermute | solution.py:47
  28.4 9.6 %collective-permute-start.2 = (bf16[144,640]{1,0:T(8,128)(2,1)S(1)}, bf16[144,640]{1,0:T(8,128)(2,1)S(1)}, u32[]{:S(2)}, u32[]{:S(2)}) collective-permute-start(bf16[144,640]{1,0:T(8,128)(2,1)S(1)} %get-tuple-element.64.sent_ref), channel_id=1, source_target_pairs={{0,2},{1,3},{2,0},{3,1},{4,6},{5,7},{6,4},{7,5},{8,10},{9,11},{10,... | collective-permute-start | bytes 552968 | tf_op jit(solution)/shard_map/ppermute | solution.py:47
  38.0 32.3 %copy-start = (bf16[256,4096]{1,0:T(8,128)(2,1)S(1)}, bf16[256,4096]{1,0:T(8,128)(2,1)}, u32[]{:S(2)}) copy-start(bf16[256,4096]{1,0:T(8,128)(2,1)} %features_hbm.3) | copy-start | bytes 6291460
  39.0 9.3 %collective-permute-start.8 = (bf16[64,640]{1,0:T(8,128)(2,1)S(1)}, bf16[64,640]{1,0:T(8,128)(2,1)S(1)}, u32[]{:S(2)}, u32[]{:S(2)}) collective-permute-start(bf16[64,640]{1,0:T(8,128)(2,1)S(1)} %get-tuple-element.72), channel_id=1, source_target_pairs={{0,16},{1,17},{2,18},{3,19},{4,20},{5,21},{6,22},{7,23},{8,24},{9,... | collective-permute-start | bytes 245768 | tf_op jit(solution)/shard_map/ppermute | solution.py:47
  41.4 6.9 %collective-permute-start.9 = (bf16[64,640]{1,0:T(8,128)(2,1)S(1)}, bf16[64,640]{1,0:T(8,128)(2,1)S(1)}, u32[]{:S(2)}, u32[]{:S(2)}) collective-permute-start(bf16[64,640]{1,0:T(8,128)(2,1)S(1)} %get-tuple-element.73), channel_id=1, source_target_pairs={{0,24},{1,25},{2,26},{3,27},{4,28},{5,29},{6,30},{7,31},{8,16},{9,... | collective-permute-start | bytes 245768 | tf_op jit(solution)/shard_map/ppermute | solution.py:47
  42.8 5.8 %collective-permute-start.7 = (bf16[64,640]{1,0:T(8,128)(2,1)S(1)}, bf16[64,640]{1,0:T(8,128)(2,1)S(1)}, u32[]{:S(2)}, u32[]{:S(2)}) collective-permute-start(bf16[64,640]{1,0:T(8,128)(2,1)S(1)} %get-tuple-element.71.refs_0_), channel_id=1, source_target_pairs={{0,8},{1,9},{2,10},{3,11},{4,12},{5,13},{6,14},{7,15},{8,0},{9,1},... | collective-permute-start | bytes 245768 | tf_op jit(solution)/shard_map/ppermute | solution.py:47
  42.9 14.5 %collective-permute-start.13 = (bf16[1,272,1024]{2,1,0:T(8,128)(2,1)S(1)}, bf16[1,272,1024]{2,1,0:T(8,128)(2,1)S(1)}, u32[]{:S(2)}, u32[]{:S(2)}) collective-permute-start(bf16[1,272,1024]{2,1,0:T(8,128)(2,1)S(1)} %collective-permute-done.6.refs_4_), channel_id=1, source_target_pairs={{0,4},{1,5},{2,6},{3,7},{4,0},{5,1},{6,2},{7,3},{8,12},{9,13},{10,... | collective-permute-start | bytes 1671176 | tf_op jit(solution)/shard_map/ppermute | solution.py:47
  48.7 6.1 %collective-permute-start.12 = (bf16[32,640]{1,0:T(8,128)(2,1)S(1)}, bf16[32,640]{1,0:T(8,128)(2,1)S(1)}, u32[]{:S(2)}, u32[]{:S(2)}) collective-permute-start(bf16[32,640]{1,0:T(8,128)(2,1)S(1)} %add_convert_fusion), channel_id=1, source_target_pairs={{0,24},{1,25},{2,26},{3,27},{4,28},{5,29},{6,30},{7,31},{8,16},{9,... | collective-permute-start | bytes 122888 | tf_op jit(solution)/shard_map/ppermute | solution.py:47
  51.3 5.3 %collective-permute-start.11 = (bf16[32,640]{1,0:T(8,128)(2,1)S(1)}, bf16[32,640]{1,0:T(8,128)(2,1)S(1)}, u32[]{:S(2)}, u32[]{:S(2)}) collective-permute-start(bf16[32,640]{1,0:T(8,128)(2,1)S(1)} %add_convert_fusion), channel_id=1, source_target_pairs={{0,16},{1,17},{2,18},{3,19},{4,20},{5,21},{6,22},{7,23},{8,24},{9,... | collective-permute-start | bytes 122888 | tf_op jit(solution)/shard_map/ppermute | solution.py:47
  51.4 5.2 %collective-permute-start.10 = (bf16[32,640]{1,0:T(8,128)(2,1)S(1)}, bf16[32,640]{1,0:T(8,128)(2,1)S(1)}, u32[]{:S(2)}, u32[]{:S(2)}) collective-permute-start(bf16[32,640]{1,0:T(8,128)(2,1)S(1)} %add_convert_fusion), channel_id=1, source_target_pairs={{0,8},{1,9},{2,10},{3,11},{4,12},{5,13},{6,14},{7,15},{8,0},{9,1},... | collective-permute-start | bytes 122888 | tf_op jit(solution)/shard_map/ppermute | solution.py:47
  56.6 11.8 %collective-permute-start.17 = (bf16[1,272,1024]{2,1,0:T(8,128)(2,1)S(1)}, bf16[1,272,1024]{2,1,0:T(8,128)(2,1)S(1)}, u32[]{:S(2)}, u32[]{:S(2)}) collective-permute-start(bf16[1,272,1024]{2,1,0:T(8,128)(2,1)S(1)} %collective-permute-done.6.refs_4_), channel_id=1, source_target_pairs={{0,8},{1,9},{2,10},{3,11},{4,12},{5,13},{6,14},{7,15},{8,0},{9,1},... | collective-permute-start | bytes 1671176 | tf_op jit(solution)/shard_map/ppermute | solution.py:47
  57.4 6.6 %collective-permute-start.16 = (bf16[128,640]{1,0:T(8,128)(2,1)S(1)}, bf16[128,640]{1,0:T(8,128)(2,1)S(1)}, u32[]{:S(2)}, u32[]{:S(2)}) collective-permute-start(bf16[128,640]{1,0:T(8,128)(2,1)S(1)} %pad_maximum_fusion.1), channel_id=1, source_target_pairs={{0,6},{1,7},{2,4},{3,5},{4,2},{5,3},{6,0},{7,1},{8,14},{9,15},{10,... | collective-permute-start | bytes 491528 | tf_op jit(solution)/shard_map/ppermute | solution.py:47
  58.9 7.0 %collective-permute-start.15 = (bf16[128,640]{1,0:T(8,128)(2,1)S(1)}, bf16[128,640]{1,0:T(8,128)(2,1)S(1)}, u32[]{:S(2)}, u32[]{:S(2)}) collective-permute-start(bf16[128,640]{1,0:T(8,128)(2,1)S(1)} %pad_maximum_fusion.1), channel_id=1, source_target_pairs={{0,4},{1,5},{2,6},{3,7},{4,0},{5,1},{6,2},{7,3},{8,12},{9,13},{10,... | collective-permute-start | bytes 491528 | tf_op jit(solution)/shard_map/ppermute | solution.py:47
  60.1 5.8 %collective-permute-start.14 = (bf16[128,640]{1,0:T(8,128)(2,1)S(1)}, bf16[128,640]{1,0:T(8,128)(2,1)S(1)}, u32[]{:S(2)}, u32[]{:S(2)}) collective-permute-start(bf16[128,640]{1,0:T(8,128)(2,1)S(1)} %pad_maximum_fusion.1), channel_id=1, source_target_pairs={{0,2},{1,3},{2,0},{3,1},{4,6},{5,7},{6,4},{7,5},{8,10},{9,11},{10,... | collective-permute-start | bytes 491528 | tf_op jit(solution)/shard_map/ppermute | solution.py:47
  68.3 2.9 %collective-permute-start.18 = (bf16[16,32,640]{2,1,0:T(8,128)(2,1)S(1)}, bf16[16,32,640]{2,1,0:T(8,128)(2,1)S(1)}, u32[]{:S(2)}, u32[]{:S(2)}) collective-permute-start(bf16[16,32,640]{2,1,0:T(8,128)(2,1)S(1)} %bitcast.7), channel_id=1, source_target_pairs={{0,1},{1,0},{2,3},{3,2},{4,5},{5,4},{6,7},{7,6},{8,9},{9,8},{10,11... | collective-permute-start | bytes 1966088 | tf_op jit(solution)/shard_map/ppermute | solution.py:47
  68.3 17.5 %collective-permute-start.19 = (bf16[1,272,1024]{2,1,0:T(8,128)(2,1)S(1)}, bf16[1,272,1024]{2,1,0:T(8,128)(2,1)S(1)}, u32[]{:S(2)}, u32[]{:S(2)}) collective-permute-start(bf16[1,272,1024]{2,1,0:T(8,128)(2,1)S(1)} %collective-permute-done.5.refs_2_), channel_id=1, source_target_pairs={{0,4},{1,5},{2,6},{3,7},{4,0},{5,1},{6,2},{7,3},{8,12},{9,13},{10,... | collective-permute-start | bytes 1671176 | tf_op jit(solution)/shard_map/ppermute | solution.py:47
  68.6 32.6 %collective-permute-start.20 = (bf16[1,272,1024]{2,1,0:T(8,128)(2,1)S(1)}, bf16[1,272,1024]{2,1,0:T(8,128)(2,1)S(1)}, u32[]{:S(2)}, u32[]{:S(2)}) collective-permute-start(bf16[1,272,1024]{2,1,0:T(8,128)(2,1)S(1)} %collective-permute-done.17.refs_6_), channel_id=1, source_target_pairs={{0,4},{1,5},{2,6},{3,7},{4,0},{5,1},{6,2},{7,3},{8,12},{9,13},{10,... | collective-permute-start | bytes 1671176 | tf_op jit(solution)/shard_map/ppermute | solution.py:47
  71.2 15.4 %collective-permute-start.21 = (bf16[256,512]{1,0:T(8,128)(2,1)S(1)}, bf16[256,512]{1,0:T(8,128)(2,1)S(1)}, u32[]{:S(2)}, u32[]{:S(2)}) collective-permute-start(bf16[256,512]{1,0:T(8,128)(2,1)S(1)} %get-tuple-element.102), channel_id=1, source_target_pairs={{0,8},{1,9},{2,10},{3,11},{4,12},{5,13},{6,14},{7,15},{8,0},{9,1},... | collective-permute-start | bytes 786440 | tf_op jit(solution)/shard_map/ppermute | solution.py:47
  72.0 27.0 %collective-permute-start.22 = (bf16[256,512]{1,0:T(8,128)(2,1)S(1)}, bf16[256,512]{1,0:T(8,128)(2,1)S(1)}, u32[]{:S(2)}, u32[]{:S(2)}) collective-permute-start(bf16[256,512]{1,0:T(8,128)(2,1)S(1)} %get-tuple-element.105), channel_id=1, source_target_pairs={{0,16},{1,17},{2,18},{3,19},{4,20},{5,21},{6,22},{7,23},{8,24},{9,... | collective-permute-start | bytes 786440 | tf_op jit(solution)/shard_map/ppermute | solution.py:47
  73.8 48.8 %collective-permute-start.23 = (bf16[256,512]{1,0:T(8,128)(2,1)S(1)}, bf16[256,512]{1,0:T(8,128)(2,1)S(1)}, u32[]{:S(2)}, u32[]{:S(2)}) collective-permute-start(bf16[256,512]{1,0:T(8,128)(2,1)S(1)} %get-tuple-element.107), channel_id=1, source_target_pairs={{0,24},{1,25},{2,26},{3,27},{4,28},{5,29},{6,30},{7,31},{8,16},{9,... | collective-permute-start | bytes 786440 | tf_op jit(solution)/shard_map/ppermute | solution.py:47
  85.9 36.8 %collective-permute-start.24 = (bf16[256,512]{1,0:T(8,128)(2,1)S(1)}, bf16[256,512]{1,0:T(8,128)(2,1)S(1)}, u32[]{:S(2)}, u32[]{:S(2)}) collective-permute-start(bf16[256,512]{1,0:T(8,128)(2,1)S(1)} %get-tuple-element.108), channel_id=1, source_target_pairs={{0,20},{1,21},{2,22},{3,23},{4,16},{5,17},{6,18},{7,19},{8,28},{9,... | collective-permute-start | bytes 786440 | tf_op jit(solution)/shard_map/ppermute | solution.py:47
  86.6 36.1 %collective-permute-start.27 = (bf16[256,512]{1,0:T(8,128)(2,1)S(1)}, bf16[256,512]{1,0:T(8,128)(2,1)S(1)}, u32[]{:S(2)}, u32[]{:S(2)}) collective-permute-start(bf16[256,512]{1,0:T(8,128)(2,1)S(1)} %get-tuple-element.111), channel_id=1, source_target_pairs={{0,12},{1,13},{2,14},{3,15},{4,8},{5,9},{6,10},{7,11},{8,4},{9,5},... | collective-permute-start | bytes 786440 | tf_op jit(solution)/shard_map/ppermute | solution.py:47
  99.0 23.6 %collective-permute-start.25 = (bf16[256,512]{1,0:T(8,128)(2,1)S(1)}, bf16[256,512]{1,0:T(8,128)(2,1)S(1)}, u32[]{:S(2)}, u32[]{:S(2)}) collective-permute-start(bf16[256,512]{1,0:T(8,128)(2,1)S(1)} %get-tuple-element.109), channel_id=1, source_target_pairs={{0,28},{1,29},{2,30},{3,31},{4,24},{5,25},{6,26},{7,27},{8,20},{9,... | collective-permute-start | bytes 786440 | tf_op jit(solution)/shard_map/ppermute | solution.py:47
  101.2 21.5 %collective-permute-start.26 = (bf16[256,512]{1,0:T(8,128)(2,1)S(1)}, bf16[256,512]{1,0:T(8,128)(2,1)S(1)}, u32[]{:S(2)}, u32[]{:S(2)}) collective-permute-start(bf16[256,512]{1,0:T(8,128)(2,1)S(1)} %get-tuple-element.110), channel_id=1, source_target_pairs={{0,4},{1,5},{2,6},{3,7},{4,0},{5,1},{6,2},{7,3},{8,12},{9,13},{10,... | collective-permute-start | bytes 786440 | tf_op jit(solution)/shard_map/ppermute | solution.py:47
  124.5 2.5 %collective-permute-start.29 = (bf16[128,1024]{1,0:T(8,128)(2,1)S(1)}, bf16[128,1024]{1,0:T(8,128)(2,1)S(1)}, u32[]{:S(2)}, u32[]{:S(2)}) collective-permute-start(bf16[128,1024]{1,0:T(8,128)(2,1)S(1)} %get-tuple-element.115), channel_id=1, source_target_pairs={{0,1},{1,0},{2,3},{3,2},{4,5},{5,4},{6,7},{7,6},{8,9},{9,8},{10,11... | collective-permute-start | bytes 786440 | tf_op jit(solution)/shard_map/ppermute | solution.py:47
  126.4 3.0 %collective-permute-start.28 = (bf16[128,1024]{1,0:T(8,128)(2,1)S(1)}, bf16[128,1024]{1,0:T(8,128)(2,1)S(1)}, u32[]{:S(2)}, u32[]{:S(2)}) collective-permute-start(bf16[128,1024]{1,0:T(8,128)(2,1)S(1)} %get-tuple-element.113), channel_id=1, source_target_pairs={{0,1},{1,0},{2,3},{3,2},{4,5},{5,4},{6,7},{7,6},{8,9},{9,8},{10,11... | collective-permute-start | bytes 786440 | tf_op jit(solution)/shard_map/ppermute | solution.py:47
  127.1 8.9 %collective-permute-start.30 = (bf16[128,1024]{1,0:T(8,128)(2,1)S(1)}, bf16[128,1024]{1,0:T(8,128)(2,1)S(1)}, u32[]{:S(2)}, u32[]{:S(2)}) collective-permute-start(bf16[128,1024]{1,0:T(8,128)(2,1)S(1)} %join.1), channel_id=1, source_target_pairs={{0,2},{1,3},{2,0},{3,1},{4,6},{5,7},{6,4},{7,5},{8,10},{9,11},{10,... | collective-permute-start | bytes 786440 | tf_op jit(solution)/shard_map/ppermute | solution.py:47
